TPU v7x, 32 devices: a whole 2x2x4 slice. The times are simulated.
32 devices in a mesh: replica: 2 (over x), shard: 16 (over z, y, core).
Axes of the slice: x: 2, y: 2, z: 4, core: 2. Of those that a mesh axis runs over, the one named last changes fastest.
Arguments:
- latents: bfloat16 [2, 256, 32, 640], P('replica', 'shard'), may hold values from -6 to 6
- cotangent: float32 [2, 256, 32, 640], P('replica', 'shard'), may hold values from -20.4 to 20.4
- kernel: float32 [2, 640, 5760], P('replica', 'shard'), may hold values from -4 to 4
- conv_bias: float32 [2, 640], P('replica'), may hold values from -3 to 3
- gn_gain: float32 [2, 640], P('replica'), may hold values from 0.25 to 1.75
- gn_shift: float32 [2, 640], P('replica'), may hold values from -3 to 3
- step: int32 [1], replicated, may hold values from 0 to 999
Outputs:
- block_out: bfloat16 [2, 256, 32, 640], P('replica', 'shard')
- new_kernel: float32 [2, 640, 5760], P('replica', 'shard')
- new_bias: float32 [2, 640], P('replica')
- new_gain: float32 [2, 640], P('replica')
- new_shift: float32 [2, 640], P('replica')
All inputs are finite; a program needn't handle non-finite values.
Results may differ from a plain program's by a relative error of at most 0.005.
Values may be sent and summed in bfloat16 or wider, within the bound.
No kernel may reach another device: no remote copies, remote signals or barrier semaphores. Data moves between devices by JAX's collectives and lax.ppermute only.
A program may use at most 128 MiB of HBM per device.

v0:
```python
from functools import partial

import jax
import jax.numpy as jnp
from jax import lax
from jax.sharding import PartitionSpec as P

GROUPS = 32


eps = 1e-05
lr_kernel = 0.1
lr_vector = 0.01


def as_sent(x):
    return jax.tree.map(lambda a: a.astype(jnp.bfloat16) if a.dtype == jnp.float32 else a, x)


def from_behind(value, axis, steps):
    count = lax.axis_size(axis)
    pairs = [(source, (source + steps) % count) for source in range(count)]
    return lax.ppermute(value, axis, pairs)


def from_partner(value, axis, apart):
    mask = 2**apart
    pairs = [(source, source ^ mask) for source in range(lax.axis_size(axis))]
    return lax.ppermute(value, axis, pairs)


def params_from_peer(values, by):
    return jax.tree.map(
        lambda part, own: part.astype(own.dtype),
        from_behind(as_sent(values), "replica", by),
        values,
    )


def per_device(latents, cotangent, kernel, conv_bias, gn_gain, gn_shift, step):
    latent = latents[0]
    cotan = cotangent[0]
    half_rows, columns, channels = latent.shape
    kernel_shard = kernel[0]
    kernel_cols = kernel_shard.shape[1]
    weight_scale = kernel_cols ** (-0.5)
    group_width = channels // GROUPS
    row_count = half_rows * columns
    is_lower = lax.axis_index("shard") % 2 == 0
    levels = lax.axis_size("replica").bit_length() - 1
    peer_level = step[0] % levels
    kernel_rate = lr_kernel * (1.0 - (step[0] % 1000).astype(jnp.float32) / 2000.0)
    params = (kernel_shard, conv_bias[0], gn_gain[0], gn_shift[0])
    kernel_b = kernel_shard.astype(jnp.bfloat16)
    whole_kernel = lax.all_gather(kernel_b, "shard", axis=0, tiled=True)
    latent_float = latent.astype(jnp.float32)
    grouped = latent_float.reshape(row_count, GROUPS, group_width)
    part_sum = jnp.sum(grouped, axis=(0, 2))
    part_square = jnp.sum(grouped * grouped, axis=(0, 2))
    own_edge = jnp.where(is_lower, latent_float[-1], latent_float[0])
    far_edge, far_sum, far_square = (
        from_partner(own_edge.astype(jnp.bfloat16), "shard", 0).astype(own_edge.dtype),
        from_partner(part_sum.astype(jnp.bfloat16), "shard", 0).astype(part_sum.dtype),
        from_partner(part_square.astype(jnp.bfloat16), "shard", 0).astype(part_square.dtype),
    )
    elements = 2 * row_count * group_width
    group_mean = (part_sum + far_sum) / elements
    square = (part_square + far_square) / elements
    rstd = lax.rsqrt(square - group_mean * group_mean + eps)
    channel_means = jnp.repeat(group_mean, group_width)
    channel_inverse_deviation = jnp.repeat(rstd, group_width)
    norm_scale_vector = params[2]
    norm_offset_vector = params[3]
    normalized_input = (latent_float - channel_means) * channel_inverse_deviation
    preactivation = norm_scale_vector * normalized_input + norm_offset_vector
    act_mid = jax.nn.silu(preactivation)
    far_act = jax.nn.silu(
        norm_scale_vector * ((far_edge - channel_means) * channel_inverse_deviation)
        + norm_offset_vector
    )
    zero_row = jnp.zeros_like(far_act)
    stacked = jnp.concatenate(
        [
            jnp.where(is_lower, zero_row, far_act)[None],
            act_mid,
            jnp.where(is_lower, far_act, zero_row)[None],
        ],
        axis=0,
    ).astype(jnp.bfloat16)
    padded = jnp.pad(stacked, ((0, 0), (1, 1), (0, 0)))
    patches = jnp.concatenate(
        [
            padded[row_off : row_off + half_rows, col_off : col_off + columns].reshape(
                row_count, channels
            )
            for row_off in range(3)
            for col_off in range(3)
        ],
        axis=1,
    )
    cot_b = cotan.reshape(row_count, channels).astype(jnp.bfloat16)
    spread_init = jnp.zeros((half_rows + 2, columns + 2, channels), jnp.float32)
    conv_out = lax.dot_general(
        patches, whole_kernel, (((1,), (1,)), ((), ())), preferred_element_type=jnp.float32
    )
    running = spread_init
    cot_cols = cot_b
    for tap_index in range(9):
        row_off = tap_index // 3
        col_off = tap_index % 3
        contrib = jnp.dot(
            cot_cols,
            whole_kernel[:, tap_index * channels : (tap_index + 1) * channels],
            preferred_element_type=jnp.float32,
        )
        running = running.at[row_off : row_off + half_rows, col_off : col_off + columns].add(
            contrib.reshape(half_rows, columns, channels)
        )
    block = (
        weight_scale * conv_out + params[1] + latent_float.reshape(row_count, channels)
    ).astype(jnp.bfloat16)
    send_row = jnp.where(
        is_lower, running[half_rows + 1, 1 : columns + 1], running[0, 1 : columns + 1]
    )
    got_row = from_partner(send_row.astype(jnp.bfloat16), "shard", 0).astype(send_row.dtype)
    inner = running[1 : half_rows + 1, 1 : columns + 1]
    inner = inner.at[half_rows - 1].add(jnp.where(is_lower, got_row, jnp.zeros_like(got_row)))
    inner = inner.at[0].add(jnp.where(is_lower, jnp.zeros_like(got_row), got_row))
    act_grad = weight_scale * inner
    sigmoid_pre = jax.nn.sigmoid(preactivation)
    preactivation_gradient = act_grad * sigmoid_pre * (1.0 + preactivation * (1.0 - sigmoid_pre))
    partial_scale_vector = jnp.sum(preactivation_gradient * normalized_input, axis=(0, 1))
    part_shift = jnp.sum(preactivation_gradient, axis=(0, 1))
    part_bias = jnp.sum(cotan, axis=(0, 1))
    cot_cols = cot_b
    kernel_grad = lax.psum_scatter(
        (
            weight_scale
            * lax.dot_general(
                cot_cols, patches, (((0,), (0,)), ((), ())), preferred_element_type=jnp.float32
            )
        ).astype(jnp.bfloat16),
        "shard",
        scatter_dimension=0,
        tiled=True,
    ).astype(jnp.float32)
    bias_grad, scale_vector_gradient, shift_grad = lax.psum(
        (part_bias, partial_scale_vector, part_shift), "shard"
    )
    grads = (kernel_grad, bias_grad, scale_vector_gradient, shift_grad)
    rates = (kernel_rate, lr_vector, lr_vector, lr_vector)
    stepped = tuple((own - rate * own_grad for own, own_grad, rate in zip(params, grads, rates)))
    peer_values = lax.switch(
        peer_level, [partial(params_from_peer, by=1 << level) for level in range(levels)], stepped
    )
    results = [0.5 * (own + other) for own, other in zip(stepped, peer_values)]
    return (
        block.reshape(1, half_rows, columns, channels),
        results[0][None],
        results[1][None],
        results[2][None],
        results[3][None],
    )


def solution(mesh):
    return jax.shard_map(
        per_device,
        mesh=mesh,
        in_specs=(
            P("replica", "shard", None, None),
            P("replica", "shard", None, None),
            P("replica", "shard", None),
            P("replica", None),
            P("replica", None),
            P("replica", None),
            P(),
        ),
        out_specs=(
            P("replica", "shard", None, None),
            P("replica", "shard", None),
            P("replica", None),
            P("replica", None),
            P("replica", None),
        ),
        check_vma=False,
    )
```

profile of v0, /device:TPU:0, one launch (start us, length us, event | category | flops | bytes accessed | tf_op | source)
XLA Modules:
  0.0 332.7 jit_solution(14029467323952309036)
XLA Ops:
  7.2 2.1 bitcast_convert_fusion
  9.4 0.2 multiply_reduce_fusion.1
  9.8 0.5 collective-permute-start.2
  10.8 0.5 collective-permute-start
  11.4 0.6 fusion.43
  12.0 0.6 fusion.42
  12.6 0.7 and_reduce_fusion
  13.3 0.1 fusion.40
  13.9 68.1 %all-gather.2.cloned.1.call-done = bf16[640,5760]{1,0:T(8,128)(2,1)} async-done(((bf16[40,5760]{1,0:T(8,128)(2,1)}), bf16[640,5760]{1,0:T(8,128)(2,1)}) %all-gather.2.cloned.1.call-update) | async-done | bytes 7372816 | tf_op jit(solution)/shard_map/all_gather | solution.py:55
  82.0 1.9 fusion.13
  84.0 4.3 %convolution_add_fusion.6 = f32[16,32,640]{2,1,0:T(8,128)} fusion(s32[]{:T(128)} %bitcast.22, s32[]{:T(128)} %bitcast.23, bf16[640,5760]{1,0:T(8,128)(2,1)} %all-gather.2.cloned.1.call-done, bf16[1,16,32,640]{3,2,1,0:T(8,128)(2,1)S(1)} %get-tuple-element.157, f32[16,32,640]{2,1,0:T(8,128)S(1)} %fusion.13), kind=kOutput, calls=%fused_computation.14 | convolution fusion | flops 419758080 | bytes 4097024 | tf_op jit(solution)/shard_map/dot_general | solution.py:111
  88.3 6.4 %scatter-add.39 = f32[18,34,640]{2,1,0:T(8,128)S(1)} dynamic-update-slice(f32[18,34,640]{2,1,0:T(8,128)S(1)} %scatter-add.36, f32[16,32,640]{2,1,0:T(8,128)} %convolution_add_fusion.6, s32[]{:T(128)} %bitcast.22, s32[]{:T(128)} %bitcast.23, s32[]{:T(128)} %constant.358.clone.1) | dynamic-update-slice | bytes 2621444 | tf_op jit(solution)/shard_map/scatter-add | solution.py:116
  94.6 4.9 %add_select_fusion = f32[16,32,640]{2,1,0:T(8,128)} fusion(f32[18,34,640]{2,1,0:T(8,128)S(1)} %scatter-add.39, s32[]{:T(128)} %bitcast.25, s32[]{:T(128)} %bitcast.26, bf16[640,5760]{1,0:T(8,128)(2,1)} %all-gather.2.cloned.1.call-done, bf16[1,16,32,640]{3,2,1,0:T(8,128)(2,1)S(1)} %get-tuple-element.157, pred[]{:T(512)} %and_reduce_fusion), kind=kOutput, calls=%fused_computation.4 | convolution fusion | flops 420085760 | bytes 4097536 | tf_op jit(solution)/shard_map/dot_general | solution.py:111
  99.6 6.2 %scatter-add.40 = f32[18,34,640]{2,1,0:T(8,128)S(1)} dynamic-update-slice(f32[18,34,640]{2,1,0:T(8,128)S(1)} %scatter-add.39, f32[16,32,640]{2,1,0:T(8,128)} %add_select_fusion, s32[]{:T(128)} %bitcast.25, s32[]{:T(128)} %bitcast.26, s32[]{:T(128)} %constant.358.clone.1) | dynamic-update-slice | bytes 2621444 | tf_op jit(solution)/shard_map/scatter-add | solution.py:116
  105.8 1.9 fusion.3
  107.7 3.0 convolution_add_fusion.4
  110.7 4.9 %scatter-add.44 = f32[18,34,640]{2,1,0:T(8,128)S(1)} dynamic-update-slice(f32[18,34,640]{2,1,0:T(8,128)S(1)} %fusion.3, f32[16,32,640]{2,1,0:T(8,128)} %convolution_add_fusion.4, s32[]{:T(128)} %constant.359.clone.1, s32[]{:T(128)} %constant.359.clone.1, s32[]{:T(128)} %constant.358.clone.1) | dynamic-update-slice | bytes 2621444 | tf_op jit(solution)/shard_map/scatter-add | solution.py:116
  115.6 3.0 convolution_add_fusion.3
  118.6 4.9 %scatter-add.45 = f32[18,34,640]{2,1,0:T(8,128)S(1)} dynamic-update-slice(f32[18,34,640]{2,1,0:T(8,128)S(1)} %scatter-add.44, f32[16,32,640]{2,1,0:T(8,128)} %convolution_add_fusion.3, s32[]{:T(128)} %constant.359.clone.1, s32[]{:T(128)} %constant.360.clone.1, s32[]{:T(128)} %constant.358.clone.1) | dynamic-update-slice | bytes 2621444 | tf_op jit(solution)/shard_map/scatter-add | solution.py:116
  123.4 1.9 fusion.2
  125.4 3.0 convolution_add_fusion.1
  128.4 4.9 %scatter-add.49 = f32[18,34,640]{2,1,0:T(8,128)S(1)} dynamic-update-slice(f32[18,34,640]{2,1,0:T(8,128)S(1)} %fusion.2, f32[16,32,640]{2,1,0:T(8,128)} %convolution_add_fusion.1, s32[]{:T(128)} %constant.360.clone.1, s32[]{:T(128)} %constant.359.clone.1, s32[]{:T(128)} %constant.358.clone.1) | dynamic-update-slice | bytes 2621444 | tf_op jit(solution)/shard_map/scatter-add | solution.py:116
  133.3 3.0 convolution_add_fusion
  136.3 4.9 %scatter-add.50 = f32[18,34,640]{2,1,0:T(8,128)S(1)} dynamic-update-slice(f32[18,34,640]{2,1,0:T(8,128)S(1)} %scatter-add.49, f32[16,32,640]{2,1,0:T(8,128)} %convolution_add_fusion, s32[]{:T(128)} %constant.360.clone.1, s32[]{:T(128)} %constant.360.clone.1, s32[]{:T(128)} %constant.358.clone.1) | dynamic-update-slice | bytes 2621444 | tf_op jit(solution)/shard_map/scatter-add | solution.py:116
  141.2 0.3 collective-permute-start.5
  141.5 0.1 slice.443
  141.7 0.8 collective-permute-done.5
  142.5 0.7 add_multiply_fusion
  143.2 0.3 fusion.12
  143.7 0.4 fusion.41
  145.0 2.6 copy-done.4
  147.6 6.9 %fusion = bf16[640,5760]{0,1:T(8,128)(2,1)} fusion(bf16[512,5760]{1,0:T(8,128)(2,1)S(1)} %constant_dynamic-update-slice_fusion, bf16[512,640]{1,0:T(8,128)(2,1)S(1)} %bitcast.111), kind=kOutput, calls=%fused_computation.1 | convolution fusion | flops 3782246400 | bytes 13926400 | tf_op jit(solution)/shard_map/dot_general | solution.py:139
  155.3 0.6 dynamic-slice.89
  156.5 0.3 fusion.39
  156.8 62.1 %all-reduce.3 = (f32[640]{0:T(1024)S(1)}, f32[640]{0:T(1024)S(1)}, f32[640]{0:T(1024)S(1)}) all-reduce(f32[640]{0:T(1024)S(1)} %get-tuple-element.156, f32[640]{0:T(1024)S(1)} %get-tuple-element.148, f32[640]{0:T(1024)S(1)} %get-tuple-element.147), channel_id=1, replica_groups=mesh['replica'=2,'shard'=16] {'shard'}, use_global_device_ids=true, to_apply=%region_6.7 | all-reduce | flops 1920 | bytes 15360 | tf_op jit(solution)/shard_map/psum | solution.py:147
  218.9 1.4 collective-permute-start.7
  220.3 0.6 collective-permute-start.6
  220.9 1.4 collective-permute-start.4
  222.3 10.9 %fusion.6 = bf16[512,640]{1,0:T(8,128)(2,1)} fusion(f32[512,640]{1,0:T(8,128)} %bitcast.121, bf16[512,5760]{1,0:T(8,128)(2,1)} %copy-done.4, bf16[640,5760]{1,0:T(8,128)(2,1)} %all-gather.2.cloned.1.call-done, f32[640]{0:T(1024)S(1)} %reduce.34), kind=kOutput, calls=%fused_computation.18 | convolution fusion | flops 3776184320 | bytes 15239680 | tf_op jit(solution)/shard_map/dot_general | solution.py:103
  233.2 75.3 %all-reduce.6.cloned.1.call-done = bf16[640,5760]{0,1:T(8,128)(2,1)} async-done(((bf16[640,5760]{0,1:T(8,128)(2,1)}), bf16[640,5760]{0,1:T(8,128)(2,1)}) %all-reduce.6.cloned.1.call-update) | async-done | bytes 7372816
  308.6 2.4 constant_dynamic-slice_fusion
  310.9 1.4 copy.34
  312.5 1.5 collective-permute-start.3
  314.1 0.6 broadcast_in_dim.34
  314.6 0.6 broadcast_in_dim.33
  315.2 0.6 broadcast_in_dim.32
  315.8 9.0 %collective-permute-done.3 = bf16[40,5760]{1,0:T(8,128)(2,1)S(1)} collective-permute-done((bf16[40,5760]{1,0:T(8,128)(2,1)S(1)}, bf16[40,5760]{1,0:T(8,128)(2,1)S(1)}, u32[]{:S(2)}, u32[]{:S(2)}) %collective-permute-start.3) | collective-permute-done | bytes 460832 | tf_op jit(solution)/shard_map/ppermute | solution.py:23
  324.8 1.1 multiply_bitcast_fusion
  (70 shorter events, 2.6 us)
Async XLA Ops:
  7.2 2.2 copy-start
  7.2 74.8 %all-gather.2.cloned.1.call-start = ((), (), s32[]{:S(2)}) async-start(), calls=%async_computation | async-start | bytes 7833600 | tf_op jit(solution)/shard_map/all_gather | solution.py:55
  9.3 2.1 copy-start.5
  9.3 3.3 copy-start.8
  9.3 4.0 %copy-start.3 = (f32[1,16,32,640]{3,2,1,0:T(8,128)S(1)}, f32[1,16,32,640]{3,2,1,0:T(8,128)}, u32[]{:S(2)}) copy-start(f32[1,16,32,640]{3,2,1,0:T(8,128)} %param.30) | copy-start | bytes 3932164
  9.3 299.3 %all-reduce.6.cloned.1.call-start = ((), (), s32[]{:S(2)}) async-start(), calls=%async_computation.1 | async-start | bytes 14745600
  9.8 3.7 %collective-permute-start.2 = (bf16[32]{0:T(256)(128)(2,1)S(1)}, bf16[32]{0:T(256)(128)(2,1)S(1)}, u32[]{:S(2)}, u32[]{:S(2)}) collective-permute-start(bf16[32]{0:T(256)(128)(2,1)S(1)} %convert_element_type.115), channel_id=1, source_target_pairs={{0,1},{1,0},{2,3},{3,2},{4,5},{5,4},{6,7},{7,6},{8,9},{9,8},{10,11... | collective-permute-start | bytes 200 | tf_op jit(solution)/shard_map/ppermute | solution.py:29
  10.5 2.9 collective-permute-start.1
  10.7 2.8 copy-start.6
  10.8 1.8 copy-start.2
  10.8 130.6 %collective-permute-start = (bf16[32,640]{1,0:T(8,128)(2,1)S(1)}, bf16[32,640]{1,0:T(8,128)(2,1)S(1)}, u32[]{:S(2)}, u32[]{:S(2)}) collective-permute-start(bf16[32,640]{1,0:T(8,128)(2,1)S(1)} %fusion.34), channel_id=1, source_target_pairs={{0,1},{1,0},{2,3},{3,2},{4,5},{5,4},{6,7},{7,6},{8,9},{9,8},{10,11... | collective-permute-start | bytes 122888 | tf_op jit(solution)/shard_map/ppermute | solution.py:29
  141.2 1.3 collective-permute-start.5
  145.0 2.6 copy-start.4
  154.5 0.7 copy-start.7
  154.5 0.7 copy-start.9
  218.9 95.1 %collective-permute-start.7 = (bf16[640]{0:T(1024)(128)(2,1)S(1)}, bf16[640]{0:T(1024)(128)(2,1)S(1)}, u32[]{:S(2)}, u32[]{:S(2)}) collective-permute-start(bf16[640]{0:T(1024)(128)(2,1)S(1)} %fusion.38), channel_id=1, source_target_pairs={{0,16},{16,0},{1,17},{17,1},{2,18},{18,2},{3,19},{19,3},{4,20},{20... | collective-permute-start | bytes 3848 | tf_op jit(solution)/shard_map/ppermute | solution.py:23
  220.3 93.7 %collective-permute-start.6 = (bf16[640]{0:T(1024)(128)(2,1)S(1)}, bf16[640]{0:T(1024)(128)(2,1)S(1)}, u32[]{:S(2)}, u32[]{:S(2)}) collective-permute-start(bf16[640]{0:T(1024)(128)(2,1)S(1)} %fusion.37), channel_id=1, source_target_pairs={{0,16},{16,0},{1,17},{17,1},{2,18},{18,2},{3,19},{19,3},{4,20},{20... | collective-permute-start | bytes 3848 | tf_op jit(solution)/shard_map/ppermute | solution.py:23
  220.9 94.3 %collective-permute-start.4 = (bf16[640]{0:T(1024)(128)(2,1)S(1)}, bf16[640]{0:T(1024)(128)(2,1)S(1)}, u32[]{:S(2)}, u32[]{:S(2)}) collective-permute-start(bf16[640]{0:T(1024)(128)(2,1)S(1)} %fusion.36), channel_id=1, source_target_pairs={{0,16},{16,0},{1,17},{17,1},{2,18},{18,2},{3,19},{19,3},{4,20},{20... | collective-permute-start | bytes 3848 | tf_op jit(solution)/shard_map/ppermute | solution.py:23
  233.2 79.1 %copy-start.1 = (f32[1,40,5760]{2,1,0:T(8,128)S(1)}, f32[1,40,5760]{2,1,0:T(8,128)}, u32[]{:S(2)}) copy-start(f32[1,40,5760]{2,1,0:T(8,128)} %param.31) | copy-start | bytes 2764804
  312.5 12.3 %collective-permute-start.3 = (bf16[40,5760]{1,0:T(8,128)(2,1)S(1)}, bf16[40,5760]{1,0:T(8,128)(2,1)S(1)}, u32[]{:S(2)}, u32[]{:S(2)}) collective-permute-start(bf16[40,5760]{1,0:T(8,128)(2,1)S(1)} %fusion.23), channel_id=1, source_target_pairs={{0,16},{16,0},{1,17},{17,1},{2,18},{18,2},{3,19},{19,3},{4,20},{20... | collective-permute-start | bytes 1382408 | tf_op jit(solution)/shard_map/ppermute | solution.py:23
Sparse Core Ops, SparseCore 0:
  10.7 71.1 all-gather.1
  154.7 153.8 all-reduce.5
where the time goes:
time: 334 us; the launch traced here: 333 us
  waiting for transfers between devices  153 us (46%)
  blocking collectives  62.1 us (19%)
  matrix products  44.8 us (13%)
  local copies, waits for them, and re-layouts  43.9 us (13%)
  between operations  15.8 us (5%)
  starting transfers between devices  6.53 us (2%)
  other arithmetic  6.36 us (2%)
    unnamed x3, waiting for transfers between devices  75.4 us
    all_gather x1, waiting for transfers between devices, per_device(): whole_kernel = lax.all_gather(kernel_b, 'shard', axis=0, tiled=True)  68.1 us
    psum x1, blocking collectives, per_device(): lax.psum((part_bias, partial_scale_vector, part_shift), 'shard')  62.1 us
    scatter-add x7, local copies, waits for them, and re-layouts, per_device(): running.at[row_off:row_off + half_rows, col_off:col_off + columns]  32.1 us
    dot_general x9, matrix products, per_device(): jnp.dot(cot_cols, whole_kernel[:, tap_index * channels:(tap_index + 1) *...  27 us
    dot_general x1, matrix products, per_device(): lax.dot_general(patches, whole_kernel, (((1,), (1,)), ((), ())), preferre...  10.9 us
    ppermute x4, waiting for transfers between devices, from_behind(): return lax.ppermute(value, axis, pairs)  8.97 us
    dot_general x1, matrix products, per_device(): lax.dot_general(cot_cols, patches, (((0,), (0,)), ((), ())), preferred_el...  6.94 us
  transfers between devices with their start and end apart: 10, of which 4 were waited for; matrix products, arithmetic and copies ran while one was open for 24% of the time, Pallas kernels for 0%

commit v1 on v0

v1 whole, which is shorter than its diff:
```python
import jax
import jax.numpy as jnp
from jax import lax
from jax.sharding import Mesh, PartitionSpec as P

GROUPS = 32
EPS = 1e-05
LR_KERNEL = 0.1
LR_VECTOR = 0.01
BF16 = jnp.bfloat16
F32 = jnp.float32


def swap_cores(value):
    return lax.ppermute(value, "core", [(0, 1), (1, 0)])


def from_behind(value, steps):
    count = lax.axis_size("replica")
    return lax.ppermute(value, "replica", [(s, (s + steps) % count) for s in range(count)])


def from_peer(level, levels, value):
    if levels == 1:
        return from_behind(value, 1)
    return lax.switch(level, [lambda v, by=1 << k: from_behind(v, by) for k in range(levels)], value)


def column_shifts(rows):
    zero = jnp.zeros_like(rows[:, :1])
    return [
        jnp.concatenate([zero, rows[:, :-1]], axis=1),
        rows,
        jnp.concatenate([rows[:, 1:], zero], axis=1),
    ]


def per_device(latents, cotangent, kernel, conv_bias, gn_gain, gn_shift, step):
    latent, cotan, shard = latents[0], cotangent[0], kernel[0]
    bias, gain, shift = conv_bias[0], gn_gain[0], gn_shift[0]
    half, width, chans = latent.shape
    own_rows, taps_in = shard.shape
    cells = half * width
    nodes = lax.axis_size("node")
    core = lax.axis_index("core")
    lower = core == 0
    scale = taps_in ** (-0.5)
    group_width = chans // GROUPS
    levels = lax.axis_size("replica").bit_length() - 1
    level = step[0] % levels
    rate = LR_KERNEL * (1.0 - (step[0] % 1000).astype(F32) / 2000.0)

    own = lax.all_gather(shard.astype(BF16), "node", axis=0, tiled=False)

    cot_b = cotan.astype(BF16)
    edges = jnp.stack([
        jnp.where(lower, latent[-1], latent[0]),
        jnp.where(lower, cot_b[-1], cot_b[0]),
    ])
    far_lat, far_cot = swap_cores(edges)
    lat = latent.astype(F32)
    flat = lat.reshape(cells, chans)
    sums = jnp.stack([jnp.sum(flat, axis=0), jnp.sum(flat * flat, axis=0)])
    sums = sums.reshape(2, GROUPS, group_width).sum(axis=2)
    sums = (sums + swap_cores(sums)) / (2 * cells * group_width)
    rstd = lax.rsqrt(sums[1] - sums[0] * sums[0] + EPS)
    mean_c = jnp.repeat(sums[0], group_width)
    rstd_c = jnp.repeat(rstd, group_width)

    def pre_of(values):
        xhat = (values - mean_c) * rstd_c
        return xhat, gain * xhat + shift

    xhat, pre = pre_of(lat)
    act = jax.nn.silu(pre).astype(BF16)
    far_act = jax.nn.silu(pre_of(far_lat.astype(F32))[1]).astype(BF16)

    def with_halo(rows, far):
        zero = jnp.zeros_like(far)
        top = jnp.where(lower, zero, far)[None]
        bottom = jnp.where(lower, far, zero)[None]
        return jnp.concatenate([top, rows, bottom], axis=0)

    act_s = column_shifts(with_halo(act, far_act))
    cot_s = column_shifts(with_halo(cot_b, far_cot))
    patches = jnp.concatenate(
        [act_s[b][a:a + half].reshape(cells, chans) for a in range(3) for b in range(3)], axis=1
    )
    cot_flat = cot_b.reshape(cells, chans)
    grad = scale * lax.dot_general(
        cot_flat, patches, (((0,), (0,)), ((), ())), preferred_element_type=F32
    )
    grad = grad.astype(BF16).reshape(nodes, 2, own_rows, taps_in)
    keep = lax.dynamic_index_in_dim(grad, core, 1, keepdims=False)
    send = lax.dynamic_index_in_dim(grad, 1 - core, 1, keepdims=False)
    pair = (keep.astype(F32) + swap_cores(send).astype(F32)).astype(BF16)

    other = swap_cores(own)
    whole = jnp.where(
        lower, jnp.stack([own, other], axis=1), jnp.stack([other, own], axis=1)
    ).reshape(chans, taps_in)

    kernel_grad = lax.psum_scatter(pair, "node", scatter_dimension=0, tiled=False).astype(F32)

    conv = lax.dot_general(patches, whole, (((1,), (1,)), ((), ())), preferred_element_type=F32)
    block = (scale * conv + bias + flat).astype(BF16)

    back = jnp.zeros((cells, chans), F32)
    for a in range(3):
        for b in range(3):
            tap = (a * 3 + b) * chans
            shifted = cot_s[2 - b][2 - a:2 - a + half].reshape(cells, chans)
            back = back + jnp.dot(shifted, whole[:, tap:tap + chans], preferred_element_type=F32)
    act_grad = (scale * back).reshape(half, width, chans)
    sig = jax.nn.sigmoid(pre)
    pre_grad = act_grad * sig * (1.0 + pre * (1.0 - sig))
    vectors = jnp.stack([
        jnp.sum(cotan, axis=(0, 1)),
        jnp.sum(pre_grad * xhat, axis=(0, 1)),
        jnp.sum(pre_grad, axis=(0, 1)),
    ])
    vectors = lax.psum(vectors, ("node", "core"))
    stepped_v = jnp.stack([bias, gain, shift]) - LR_VECTOR * vectors
    peer_v = from_peer(level, levels, stepped_v.astype(BF16)).astype(F32)
    new_v = 0.5 * (stepped_v + peer_v)

    stepped = shard - rate * kernel_grad
    peer = from_peer(level, levels, stepped.astype(BF16)).astype(F32)
    new_kernel = 0.5 * (stepped + peer)
    return (
        block.reshape(1, half, width, chans),
        new_kernel[None],
        new_v[0][None],
        new_v[1][None],
        new_v[2][None],
    )


def solution(mesh):
    replicas, shards = mesh.shape["replica"], mesh.shape["shard"]
    split = Mesh(mesh.devices.reshape(replicas, shards // 2, 2), ("replica", "node", "core"))
    shard = ("node", "core")
    return jax.shard_map(
        per_device,
        mesh=split,
        in_specs=(
            P("replica", shard, None, None),
            P("replica", shard, None, None),
            P("replica", shard, None),
            P("replica", None),
            P("replica", None),
            P("replica", None),
            P(),
        ),
        out_specs=(
            P("replica", shard, None, None),
            P("replica", shard, None),
            P("replica", None),
            P("replica", None),
            P("replica", None),
        ),
        check_vma=False,
    )
```

time: 334 us -> 300 us (0.90)
  local copies, waits for them, and re-layouts: 43.9 us -> 9.36 us
  matrix products: 44.8 us -> 22.3 us
  other arithmetic: 6.36 us -> 21.5 us
  waiting for transfers between devices: 153 us -> 168 us
  blocking collectives: 62.1 us -> 58.6 us
    scatter-add x7 -> x0, local copies, waits for them, and re-layouts: 32.1 us -> none  [per_device(): running.at[row_off:row_off + half_rows, col_off:col_off + columns]]
    dot_general x11, matrix products: 44.8 us -> 22.3 us  [the longest x1 10.5 us: per_device(): lax.dot_general(patches, whole, (((1,), (1,)), ((), ())), preferred_eleme...]
    ppermute x8 -> x6, waiting for transfers between devices: 9.74 us -> 18.6 us  [the longest x2 10.9 us: from_behind(): lax.ppermute(value, 'replica', [(s, (s + steps) % count) for s in range(c...]
    unnamed x3, waiting for transfers between devices: 75.4 us -> 82.6 us
    convert_element_type x10 -> x4, other arithmetic: 2.35 us -> 8.35 us  [the longest x1 5.81 us: per_device(): pair = (keep.astype(F32) + swap_cores(send).astype(F32)).astype(BF16)]
    select_n x0 -> x4, other arithmetic: none -> 5.99 us  [the longest x1 5.29 us: per_device(): jnp.where(lower, jnp.stack([own, other], axis=1), jnp.stack([other, own],...]
    psum x1, blocking collectives: 62.1 us -> 58.6 us  [per_device(): vectors = lax.psum(vectors, ('node', 'core'))]
  transfers between devices with their start and end apart: 10 -> 8, of which waited for: 4 -> 5; matrix products, arithmetic and copies ran while one was open for 24% -> 6% of each run, Pallas kernels for 0% -> 0%
where the time goes in v1:
time: 300 us; the launch traced here: 299 us
  waiting for transfers between devices  168 us (56%)
  blocking collectives  58.6 us (20%)
  matrix products  22.3 us (7%)
  other arithmetic  21.5 us (7%)
  between operations  15.2 us (5%)
  local copies, waits for them, and re-layouts  9.36 us (3%)
  starting transfers between devices  4 us (1%)
    unnamed x3, waiting for transfers between devices  82.6 us
    all_gather x1, waiting for transfers between devices, per_device(): own = lax.all_gather(shard.astype(BF16), 'node', axis=0, tiled=False)  67.1 us
    psum x1, blocking collectives, per_device(): vectors = lax.psum(vectors, ('node', 'core'))  58.6 us
    ppermute x2, waiting for transfers between devices, from_behind(): lax.ppermute(value, 'replica', [(s, (s + steps) % count) for s in range(c...  10.9 us
    dot_general x1, matrix products, per_device(): lax.dot_general(patches, whole, (((1,), (1,)), ((), ())), preferred_eleme...  10.5 us
    ppermute x4, waiting for transfers between devices, swap_cores(): return lax.ppermute(value, 'core', [(0, 1), (1, 0)])  7.62 us
    dot_general x9, matrix products, per_device(): jnp.dot(shifted, whole[:, tap:tap + chans], preferred_element_type=F32)  7.23 us
  transfers between devices with their start and end apart: 8, of which 5 were waited for; matrix products, arithmetic and copies ran while one was open for 6% of the time, Pallas kernels for 0%

profile of v1, /device:TPU:0, one launch (start us, length us, event | category | flops | bytes accessed | tf_op | source)
XLA Modules:
  0.0 299.2 jit_solution(11433227639593594648)
XLA Ops:
  7.2 2.6 fusion.33
  9.9 0.5 collective-permute-start
  10.4 0.2 convert_reduce_fusion
  11.0 1.0 collective-permute-done.1
  12.1 0.1 mul.135
  12.4 0.5 multiply_convert_fusion.2
  12.9 0.7 broadcast_select_fusion.1
  13.6 0.1 pad_maximum_fusion
  13.7 0.1 pad_maximum_fusion.4
  13.8 0.3 fusion.35
  14.1 0.2 pad_slice_fusion.9
  14.4 0.2 pad_slice_fusion.6
  14.9 0.5 fusion.28
  15.8 4.6 %multiply_convert_fusion = bf16[5760,640]{0,1:T(8,128)(2,1)S(1)} fusion(bf16[512,5760]{1,0:T(8,128)(2,1)S(1)} %constant_dynamic-update-slice_fusion, bf16[512,640]{1,0:T(8,128)(2,1)S(1)} %bitcast.107), kind=kOutput, calls=%fused_computation | convolution fusion | flops 3782246400 | bytes 13926400 | tf_op jit(solution)/shard_map/dot_general | solution.py:90
  20.5 2.2 dynamic-slice_bitcast_fusion
  22.7 1.8 copy-done.1
  24.5 0.2 collective-permute-start.3
  24.7 6.6 %collective-permute-done.3 = bf16[8,40,5760]{2,1,0:T(8,128)(2,1)} collective-permute-done((bf16[8,40,5760]{2,1,0:T(8,128)(2,1)}, bf16[8,40,5760]{2,1,0:T(8,128)(2,1)}, u32[]{:S(2)}, u32[]{:S(2)}) %collective-permute-start.3) | collective-permute-done | bytes 3686432 | tf_op jit(solution)/shard_map/ppermute | solution.py:15
  31.3 5.8 %fusion = bf16[8,40,5760]{2,1,0:T(8,128)(2,1)} fusion(bf16[8,40,5760]{2,1,0:T(8,128)(2,1)} %collective-permute-done.3, bf16[8,2,40,5760]{3,2,1,0:T(8,128)(2,1)} %bitcast.112, s32[]{:T(128)S(6)} %select_n.86), kind=kLoop, calls=%fused_computation.3 | loop fusion | flops 7372800 | bytes 11059204 | tf_op jit(solution)/shard_map/convert_element_type | solution.py:96
  37.1 0.2 all-gather.2.cloned.1.call-start
  38.1 82.5 %reduce-scatter.4.cloned.1.call-done = bf16[1,40,5760]{2,1,0:T(8,128)(2,1)} async-done(((bf16[8,40,5760]{2,1,0:T(8,128)(2,1)}), bf16[1,40,5760]{2,1,0:T(8,128)(2,1)}) %reduce-scatter.4.cloned.1.call-update) | async-done | bytes 460816
  120.6 2.1 bitcast_convert_fusion
  122.7 67.1 %all-gather.2.cloned.1.call-done = bf16[8,40,5760]{2,1,0:T(8,128)(2,1)} async-done(((bf16[1,40,5760]{2,1,0:T(8,128)(2,1)}), bf16[8,40,5760]{2,1,0:T(8,128)(2,1)}) %all-gather.2.cloned.1.call-update) | async-done | bytes 3686416 | tf_op jit(solution)/shard_map/all_gather | solution.py:53
  189.8 1.3 stack.52
  191.1 1.3 reduce.7
  192.4 0.9 pad_maximum_fusion.1
  193.3 0.3 fusion.34
  193.6 0.7 copy-done.6
  194.3 1.5 collective-permute-start.4
  195.8 0.1 pad_maximum_fusion.2
  195.9 0.2 pad_slice_fusion.4
  196.1 0.2 pad_slice_fusion
  196.3 10.9 %collective-permute-done.4 = bf16[40,5760]{1,0:T(8,128)(2,1)S(1)} collective-permute-done((bf16[40,5760]{1,0:T(8,128)(2,1)S(1)}, bf16[40,5760]{1,0:T(8,128)(2,1)S(1)}, u32[]{:S(2)}, u32[]{:S(2)}) %collective-permute-start.4) | collective-permute-done | bytes 460832 | tf_op jit(solution)/shard_map/ppermute | solution.py:20
  207.3 1.1 fusion.15
  208.4 5.3 %maximum_select_fusion = bf16[8,2,40,5760]{3,2,1,0:T(8,128)(2,1)S(1)} fusion(bf16[8,1,40,5760]{3,2,1,0:T(8,128)(2,1)} %bitcast.15, bf16[8,1,40,5760]{3,2,1,0:T(8,128)(2,1)S(1)} %bitcast.114, pred[]{:T(512)S(6)} %eq.5), kind=kLoop, calls=%fused_computation.1 | loop fusion | flops 11059200 | bytes 14745601 | tf_op jit(solution)/shard_map/jit(_where)/select_n | solution.py:99
  213.7 0.7 fusion.25
  214.5 0.7 fusion.20
  215.2 0.7 fusion.18
  216.0 0.8 convolution_add_fusion.4
  216.8 0.8 convolution_add_fusion.3
  217.5 0.8 convolution_add_fusion.2
  218.3 0.8 fusion.6
  219.1 0.8 convolution_add_fusion.1
  219.9 1.1 multiply_reduce_fusion
  221.1 58.6 %psum.7 = f32[3,640]{1,0:T(4,128)S(1)} all-reduce(f32[3,640]{1,0:T(4,128)S(1)} %pad_maximum_fusion.7), channel_id=1, replica_groups=mesh['replica'=2,'node'=8,'core'=2] {'node','core'}, use_global_device_ids=true, to_apply=%region_7.8 | all-reduce | flops 1920 | bytes 15360 | tf_op jit(solution)/shard_map/psum | solution.py:122
  279.7 1.5 collective-permute-start.5
  281.2 10.5 %fusion.9 = bf16[512,640]{1,0:T(8,128)(2,1)} fusion(bf16[512,5760]{1,0:T(8,128)(2,1)} %copy-done.9, bf16[640,5760]{1,0:T(8,128)(2,1)} %bitcast.106, f32[640]{0:T(1024)S(1)} %copy-done.15, bf16[512,640]{1,0:T(8,128)(2,1)S(1)} %bitcast.113), kind=kOutput, calls=%fused_computation.20 | convolution fusion | flops 3776512000 | bytes 14584320 | tf_op jit(solution)/shard_map/dot_general | solution.py:105
  291.7 0.6 fusion.36
  (65 shorter events, 1.6 us)
Async XLA Ops:
  7.2 2.7 copy-start.2
  7.2 113.4 %reduce-scatter.4.cloned.1.call-start = ((), (), s32[]{:S(2)}) async-start(), calls=%async_computation.2 | async-start | bytes 4147200
  7.2 3.7 %copy-start.11 = (f32[1,640]{1,0:T(1,128)S(1)}, f32[1,640]{1,0:T(1,128)}, u32[]{:S(2)}) copy-start(f32[1,640]{1,0:T(1,128)} %param.11) | copy-start | bytes 7684
  7.2 3.7 %copy-start.10 = (f32[1,640]{1,0:T(1,128)S(1)}, f32[1,640]{1,0:T(1,128)}, u32[]{:S(2)}) copy-start(f32[1,640]{1,0:T(1,128)} %param.12) | copy-start | bytes 7684
  9.9 3.0 %collective-permute-start = (bf16[2,32,640]{2,1,0:T(8,128)(2,1)S(1)}, bf16[2,32,640]{2,1,0:T(8,128)(2,1)S(1)}, u32[]{:S(2)}, u32[]{:S(2)}) collective-permute-start(bf16[2,32,640]{2,1,0:T(8,128)(2,1)S(1)} %pad_maximum_fusion.6), channel_id=1, source_target_pairs={{0,1},{1,0},{2,3},{3,2},{4,5},{5,4},{6,7},{7,6},{8,9},{9,8},{10,11... | collective-permute-start | bytes 245768 | tf_op jit(solution)/shard_map/ppermute | solution.py:15
  10.9 1.1 collective-permute-start.1
  15.8 4.6 %copy-start.9 = (bf16[512,5760]{1,0:T(8,128)(2,1)}, bf16[512,5760]{1,0:T(8,128)(2,1)S(1)}, u32[]{:S(2)}) copy-start(bf16[512,5760]{1,0:T(8,128)(2,1)S(1)} %constant_dynamic-update-slice_fusion) | copy-start | bytes 17694724
  20.5 4.1 %copy-start.1 = (bf16[5760,640]{0,1:T(8,128)(2,1)}, bf16[5760,640]{0,1:T(8,128)(2,1)S(1)}, u32[]{:S(2)}) copy-start(bf16[5760,640]{0,1:T(8,128)(2,1)S(1)} %multiply_convert_fusion) | copy-start | bytes 22118404
  24.5 6.8 %collective-permute-start.3 = (bf16[8,40,5760]{2,1,0:T(8,128)(2,1)}, bf16[8,40,5760]{2,1,0:T(8,128)(2,1)}, u32[]{:S(2)}, u32[]{:S(2)}) collective-permute-start(bf16[8,40,5760]{2,1,0:T(8,128)(2,1)} %dynamic-slice_bitcast_fusion), channel_id=1, source_target_pairs={{0,1},{1,0},{2,3},{3,2},{4,5},{5,4},{6,7},{7,6},{8,9},{9,8},{10,11... | collective-permute-start | bytes 11059208 | tf_op jit(solution)/shard_map/ppermute | solution.py:15
  37.1 83.5 %copy-start.4 = (f32[1,40,5760]{2,1,0:T(8,128)S(1)}, f32[1,40,5760]{2,1,0:T(8,128)}, u32[]{:S(2)}) copy-start(f32[1,40,5760]{2,1,0:T(8,128)} %param.9) | copy-start | bytes 2764804
  37.1 152.7 %all-gather.2.cloned.1.call-start = ((), (), s32[]{:S(2)}) async-start(), calls=%async_computation.1 | async-start | bytes 4147200 | tf_op jit(solution)/shard_map/all_gather | solution.py:53
  189.8 18.6 %collective-permute-start.2 = (bf16[8,40,5760]{2,1,0:T(8,128)(2,1)}, bf16[8,40,5760]{2,1,0:T(8,128)(2,1)}, u32[]{:S(2)}, u32[]{:S(2)}) collective-permute-start(bf16[8,40,5760]{2,1,0:T(8,128)(2,1)} %all-gather.2.cloned.1.call-done), channel_id=1, source_target_pairs={{0,1},{1,0},{2,3},{3,2},{4,5},{5,4},{6,7},{7,6},{8,9},{9,8},{10,11... | collective-permute-start | bytes 11059208 | tf_op jit(solution)/shard_map/ppermute | solution.py:15
  193.3 1.0 copy-start.6
  193.3 2.5 copy-start.7
  193.3 2.5 copy-start.8
  194.3 13.0 %collective-permute-start.4 = (bf16[40,5760]{1,0:T(8,128)(2,1)S(1)}, bf16[40,5760]{1,0:T(8,128)(2,1)S(1)}, u32[]{:S(2)}, u32[]{:S(2)}) collective-permute-start(bf16[40,5760]{1,0:T(8,128)(2,1)S(1)} %copy-done.6), channel_id=1, source_target_pairs={{0,16},{16,0},{1,17},{17,1},{2,18},{18,2},{3,19},{19,3},{4,20},{20... | collective-permute-start | bytes 1382408 | tf_op jit(solution)/shard_map/ppermute | solution.py:20
  195.9 11.4 %copy-start.5 = (bf16[1,40,5760]{2,1,0:T(8,128)(2,1)S(1)}, bf16[1,40,5760]{2,1,0:T(8,128)(2,1)}, u32[]{:S(2)}) copy-start(bf16[1,40,5760]{2,1,0:T(8,128)(2,1)} %reduce-scatter.4.cloned.1.call-done) | copy-start | bytes 1382404
  196.1 12.3 %copy-start.3 = (bf16[8,40,5760]{2,1,0:T(8,128)(2,1)S(1)}, bf16[8,40,5760]{2,1,0:T(8,128)(2,1)}, u32[]{:S(2)}) copy-start(bf16[8,40,5760]{2,1,0:T(8,128)(2,1)} %all-gather.2.cloned.1.call-done) | copy-start | bytes 11059204
  213.7 6.2 %copy-start = (bf16[8,2,40,5760]{3,2,1,0:T(8,128)(2,1)}, bf16[8,2,40,5760]{3,2,1,0:T(8,128)(2,1)S(1)}, u32[]{:S(2)}) copy-start(bf16[8,2,40,5760]{3,2,1,0:T(8,128)(2,1)S(1)} %maximum_select_fusion) | copy-start | bytes 22118404
  219.9 1.2 copy-start.14
  219.9 59.8 %copy-start.12 = (f32[1,640]{1,0:T(1,128)S(1)}, f32[1,640]{1,0:T(1,128)}, u32[]{:S(2)}) copy-start(f32[1,640]{1,0:T(1,128)} %param.11) | copy-start | bytes 7684
  219.9 59.8 %copy-start.13 = (f32[1,640]{1,0:T(1,128)S(1)}, f32[1,640]{1,0:T(1,128)}, u32[]{:S(2)}) copy-start(f32[1,640]{1,0:T(1,128)} %param.10) | copy-start | bytes 7684
  219.9 61.3 %copy-start.15 = (f32[640]{0:T(1024)S(1)}, f32[640]{0:T(1024)}, u32[]{:S(2)}) copy-start(f32[640]{0:T(1024)} %reduce.7) | copy-start | bytes 7684
  279.7 12.0 %collective-permute-start.5 = (bf16[3,640]{1,0:T(4,128)(2,1)S(1)}, bf16[3,640]{1,0:T(4,128)(2,1)S(1)}, u32[]{:S(2)}, u32[]{:S(2)}) collective-permute-start(bf16[3,640]{1,0:T(4,128)(2,1)S(1)} %fusion.32), channel_id=1, source_target_pairs={{0,16},{16,0},{1,17},{17,1},{2,18},{18,2},{3,19},{19,3},{4,20},{20... | collective-permute-start | bytes 11528 | tf_op jit(solution)/shard_map/ppermute | solution.py:20
Sparse Core Ops, SparseCore 0:
  37.3 83.3 reduce-scatter.3
  123.4 66.3 all-gather.1

commit v2 on v1

v2 whole, which is shorter than its diff:
```python
from functools import partial

import jax
import jax.numpy as jnp
import numpy as np
from jax import lax
from jax.experimental import pallas as pl
from jax.experimental.pallas import tpu as pltpu
from jax.sharding import Mesh, PartitionSpec as P

GROUPS = 32
EPS = 1e-05
LR_KERNEL = 0.1
LR_VECTOR = 0.01
LANES = 128
BF16 = jnp.bfloat16
F32 = jnp.float32
VMEM_BYTES = 56 * 2**20

SMEM_SPEC = pl.BlockSpec(memory_space=pltpu.SMEM)
VMEM_SPEC = pl.BlockSpec(memory_space=pltpu.VMEM)
HBM_SPEC = pl.BlockSpec(memory_space=pl.ANY)


class Columns:
    def __init__(self, chans):
        tiles = 9 * chans // LANES
        self.total = 9 * chans
        self.lead = (tiles + 1) // 2 * LANES
        self.start = self.total - self.lead
        self.both = 2 * self.lead - self.total
        self.mid = self.lead - 4 * chans
        self.mid_start = chans - self.mid

    def tap(self, core, k, chans):
        tap = jnp.where(core == 0, k, 5 + k)
        return tap, pl.multiple_of(jnp.where(core == 0, k * chans, self.mid + k * chans), LANES)

    def middle(self, core, chans):
        place = jnp.where(core == 0, 4 * chans, 0)
        channel = jnp.where(core == 0, 0, self.mid_start)
        return pl.multiple_of(place, LANES), pl.multiple_of(channel, LANES)


def fill_shifts(shifts, row, values):
    width = values.shape[0]
    at = lax.broadcasted_iota(jnp.int32, values.shape, 0)
    left = jnp.where(at == 0, 0.0, pltpu.roll(values, 1, 0))
    right = jnp.where(at == width - 1, 0.0, pltpu.roll(values, width - 1, 0))
    shifts[0, row] = left.astype(BF16)
    shifts[1, row] = values.astype(BF16)
    shifts[2, row] = right.astype(BF16)


def clear_edges(shifts):
    zero = jnp.zeros(shifts.shape[2:], shifts.dtype)
    for b in range(3):
        shifts[b, 0] = zero
        shifts[b, shifts.shape[1] - 1] = zero


def grad_kernel(cols, zs, ys, info, lat_own, lat_far, cot_own, cot_far, gain, shift,
                act, stats, keep, send, acts, cot_t, grad):
    core, which, flip = info[0], info[1], info[2]
    half, width, chans = lat_own.shape
    rows = 2 * half
    cells = rows * width
    group_width = chans // GROUPS
    own_at = core * half
    far_at = half - own_at
    clear_edges(acts)

    def add_row(i, sums):
        total, square = sums
        a = lat_own[i].astype(F32)
        b = lat_far[i].astype(F32)
        return total + (a + b), square + (a * a + b * b)

    zero = jnp.zeros((width, chans), F32)
    total, square = lax.fori_loop(0, half, add_row, (zero, zero))
    sums = jnp.concatenate(
        [jnp.sum(total, axis=0, keepdims=True), jnp.sum(square, axis=0, keepdims=True),
         jnp.zeros((6, chans), F32)], axis=0
    )
    first = lax.broadcasted_iota(jnp.int32, (chans, chans), 0) // group_width
    second = lax.broadcasted_iota(jnp.int32, (chans, chans), 1) // group_width
    member = jnp.where(first == second, 1.0, 0.0)
    sums = jnp.dot(sums, member, precision=lax.Precision.HIGHEST, preferred_element_type=F32)
    sums = sums / (cells * group_width)
    mean = sums[0:1]
    rstd = lax.rsqrt(sums[1:2] - mean * mean + EPS)
    stats[0:1] = mean
    stats[1:2] = rstd
    gain_v, shift_v = gain[...], shift[...]

    def act_row(values):
        pre = gain_v * ((values.astype(F32) - mean) * rstd) + shift_v
        return pre / (1.0 + jnp.exp(-pre))

    def act_rows(i, _):
        for ref, base in ((lat_own, own_at), (lat_far, far_at)):
            value = act_row(ref[i])
            act[base + i] = value.astype(BF16)
            fill_shifts(acts, base + i + 1, value)
        return 0

    lax.fori_loop(0, half, act_rows, 0)

    chunk = LANES // width
    for ref, base in ((cot_own, own_at), (cot_far, far_at)):
        for i in range(half // chunk):
            piece = ref[i * chunk:(i + 1) * chunk].reshape(LANES, chans).astype(F32)
            place = pl.multiple_of(base * width + i * LANES, LANES)
            cot_t[:, pl.ds(place, LANES)] = piece.T.astype(BF16)

    scale = cols.total ** (-0.5)
    unit = chans // (zs * ys)
    part = unit // 2

    def emit(value, place, count):
        grad[:, :count] = value
        for z in range(zs):
            for y in range(ys):
                at = (z * ys + y) * unit
                first_half = (scale * grad[at:at + part, :count]).astype(BF16)
                second_half = (scale * grad[at + part:at + unit, :count]).astype(BF16)
                slot = info[3 + z]
                other = y ^ flip
                keep[slot, other, :, pl.ds(place, count)] = jnp.where(which == 0, first_half, second_half)
                send[slot, other, :, pl.ds(place, count)] = jnp.where(which == 0, second_half, first_half)

    def full_tap(k, _):
        tap, place = cols.tap(core, k, chans)
        window = acts[tap % 3, pl.ds(tap // 3, rows)].reshape(cells, chans)
        emit(jnp.dot(cot_t[...], window, preferred_element_type=F32), place, chans)
        return 0

    lax.fori_loop(0, 4, full_tap, 0)
    place, channel = cols.middle(core, chans)
    window = acts[1, 1:rows + 1, :, pl.ds(channel, cols.mid)].reshape(cells, cols.mid)
    emit(jnp.dot(cot_t[...], window, preferred_element_type=F32), place, cols.mid)


def load_blocks(info, blocks, whole, sems):
    copies = []
    for i, block in enumerate(blocks):
        count = block.shape[0]
        at = pl.multiple_of(info[8 + i] * count, count)
        copies.append(pltpu.make_async_copy(block, whole.at[pl.ds(at, count)], sems.at[i]))
    for copy in copies:
        copy.start()
    return copies


def split_halves(core, total, own, far):
    count = own.shape[0]
    own[...] = total[pl.ds(pl.multiple_of(core * count, count), count)]
    far[...] = total[pl.ds(pl.multiple_of((1 - core) * count, count), count)].astype(far.dtype)


def conv_kernel(cols, count, info, act, *refs):
    blocks, (own, far, whole, acts, total, sems) = refs[:count], refs[count:]
    core = info[0]
    rows, width, chans = act.shape
    cells = rows * width
    copies = load_blocks(info, blocks, whole, sems)
    clear_edges(acts)

    def shift_row(i, _):
        fill_shifts(acts, i + 1, act[i].astype(F32))
        return 0

    lax.fori_loop(0, rows, shift_row, 0)
    for copy in copies:
        copy.wait()
    nt = (((1,), (1,)), ((), ()))
    place, channel = cols.middle(core, chans)
    window = acts[1, 1:rows + 1, :, pl.ds(channel, cols.mid)].reshape(cells, cols.mid)
    lane = lax.broadcasted_iota(jnp.int32, window.shape, 1)
    window = jnp.where((core == 1) & (lane < cols.both), jnp.zeros_like(window), window)
    total[...] = lax.dot_general(window, whole[:, pl.ds(place, cols.mid)], nt, preferred_element_type=F32)

    def full_tap(k, _):
        tap, place = cols.tap(core, k, chans)
        window = acts[tap % 3, pl.ds(tap // 3, rows)].reshape(cells, chans)
        total[...] += lax.dot_general(window, whole[:, pl.ds(place, chans)], nt, preferred_element_type=F32)
        return 0

    lax.fori_loop(0, 4, full_tap, 0)
    split_halves(core, total, own, far)


def back_kernel(cols, count, info, cot_own, cot_far, *refs):
    blocks, (own, far, whole, cots, total, sems) = refs[:count], refs[count:]
    core = info[0]
    half, width, chans = cot_own.shape
    rows = 2 * half
    cells = rows * width
    copies = load_blocks(info, blocks, whole, sems)
    clear_edges(cots)

    def shift_row(i, _):
        fill_shifts(cots, core * half + i + 1, cot_own[i].astype(F32))
        fill_shifts(cots, (1 - core) * half + i + 1, cot_far[i].astype(F32))
        return 0

    lax.fori_loop(0, half, shift_row, 0)
    for copy in copies:
        copy.wait()
    total[...] = jnp.zeros_like(total)
    place, channel = cols.middle(core, chans)
    window = cots[1, 1:rows + 1].reshape(cells, chans)
    value = jnp.dot(window, whole[:, pl.ds(place, cols.mid)], preferred_element_type=F32)
    lane = lax.broadcasted_iota(jnp.int32, value.shape, 1)
    total[:, pl.ds(channel, cols.mid)] = jnp.where((core == 1) & (lane < cols.both), 0.0, value)

    def full_tap(k, _):
        tap, place = cols.tap(core, k, chans)
        window = cots[2 - tap % 3, pl.ds(2 - tap // 3, rows)].reshape(cells, chans)
        total[...] += jnp.dot(window, whole[:, pl.ds(place, chans)], preferred_element_type=F32)
        return 0

    lax.fori_loop(0, 4, full_tap, 0)
    split_halves(core, total, own, far)


def swap(value, axis):
    return lax.ppermute(value, axis, [(0, 1), (1, 0)])


def from_peer(level, value):
    count = lax.axis_size("replica")
    levels = count.bit_length() - 1
    moves = [[(s, (s + (1 << k)) % count) for s in range(count)] for k in range(levels)]
    if levels == 1:
        return lax.ppermute(value, "replica", moves[0])
    return lax.switch(level, [lambda v, m=m: lax.ppermute(v, "replica", m) for m in moves], value)


PAIRS = [(0, 1), (1, 0), (2, 3), (3, 2)]
MIDDLE = [(1, 2), (2, 1)]
INWARD = [(0, 1), (3, 2)]
OUTWARD = [(1, 0), (2, 3)]
GATHER_FROM = [[1, 2, 3], [0, 2, 3], [3, 1, 0], [2, 1, 0]]
SLOT_OF = [[3, 2, 1, 0], [2, 3, 1, 0], [0, 1, 3, 2], [0, 1, 2, 3]]


def gather_line(unit, inner):
    along = partial(lax.ppermute, axis_name="z")
    r1 = along(unit, perm=PAIRS)
    mid = along(unit, perm=MIDDLE)
    mid_far = along(r1, perm=MIDDLE)
    out = along(mid, perm=OUTWARD)
    out_far = along(mid_far, perm=OUTWARD)
    r2 = jnp.where(inner, mid, out)
    r3 = jnp.where(inner, mid_far, out_far)
    held = [unit, r1, r2, r3]
    return held + [swap(block, "y") for block in held]


def add(*values):
    total = values[0].astype(F32)
    for value in values[1:]:
        total = total + value.astype(F32)
    return total.astype(BF16)


def reduce_all(keep, send):
    slots = [add(keep[j], swap(send[j], "replica")) for j in range(4)]
    along = partial(lax.ppermute, axis_name="z")
    in1 = along(slots[0], perm=INWARD)
    mid2 = along(add(in1, slots[0]), perm=MIDDLE)
    in2 = along(slots[1], perm=INWARD)
    in3 = along(slots[2], perm=INWARD)
    mid3 = along(add(in2, slots[1]), perm=MIDDLE)
    out3 = along(add(mid2, slots[2]), perm=OUTWARD)
    line = add(slots[3], in3, mid3, out3)
    return add(line[0], swap(line[1], "y"))


def per_device(latents, cotangent, kernel, conv_bias, gn_gain, gn_shift, step):
    latent, cotan, shard = latents[0], cotangent[0], kernel[0]
    half, width, chans = latent.shape
    own_rows = shard.shape[0]
    cols = Columns(chans)
    cells = half * width
    zs, ys, replicas = lax.axis_size("z"), lax.axis_size("y"), lax.axis_size("replica")
    core, z, y, replica = (lax.axis_index(a) for a in ("core", "z", "y", "replica"))
    lower = core == 0
    paired = replicas == 2 and zs == 4 and ys == 2
    scale = cols.total ** (-0.5)
    level = step[0] % (replicas.bit_length() - 1)
    rate = LR_KERNEL * (1.0 - (step[0] % 1000).astype(F32) / 2000.0)
    params = jnp.stack([conv_bias[0], gn_gain[0], gn_shift[0]])

    kernel_b = shard.astype(BF16)
    mine = lax.dynamic_slice_in_dim(kernel_b, core * cols.start, cols.lead, 1)
    theirs = lax.dynamic_slice_in_dim(kernel_b, (1 - core) * cols.start, cols.lead, 1)
    got = swap(theirs, "core")
    unit = jnp.where(lower, jnp.concatenate([mine, got]), jnp.concatenate([got, mine]))
    cot_b = cotan.astype(BF16)
    lat_far = swap(latent, "core")
    cot_far = swap(cot_b, "core")

    if paired:
        blocks = gather_line(unit, (z == 1) | (z == 2))
        order = jnp.asarray(np.array(GATHER_FROM, np.int32))[z]
        nodes = jnp.concatenate([z[None], order]) * 2
        places = jnp.concatenate([nodes + y, nodes + 1 - y])
        slots = jnp.asarray(np.array(SLOT_OF, np.int32))[z]
        head = jnp.stack([core, replica, y, jnp.int32(0)])
        info = jnp.concatenate([head[:3], slots, head[3:], places])
    else:
        blocks = [lax.all_gather(unit, ("z", "y"), axis=0, tiled=True)]
        places = jnp.zeros((1,), jnp.int32)
        head = jnp.stack([core, jnp.int32(0), jnp.int32(0)])
        info = None
    count = len(blocks)
    if info is None:
        slots = jnp.arange(zs, dtype=jnp.int32)
        grad_info = jnp.concatenate([head, slots])
        info = jnp.concatenate([head, jnp.zeros((5,), jnp.int32), places])
    else:
        grad_info = info

    params_of = pltpu.CompilerParams(vmem_limit_bytes=VMEM_BYTES)
    flops = 2 * 2 * cells * chans * cols.lead
    pieces = jax.ShapeDtypeStruct((zs, ys, own_rows, cols.lead), BF16)
    act, stats, keep, send = pl.pallas_call(
        partial(grad_kernel, cols, zs, ys),
        out_shape=(
            jax.ShapeDtypeStruct((2 * half, width, chans), BF16),
            jax.ShapeDtypeStruct((2, chans), F32),
            pieces,
            pieces,
        ),
        in_specs=[SMEM_SPEC] + [VMEM_SPEC] * 6,
        out_specs=(VMEM_SPEC,) * 4,
        scratch_shapes=[
            pltpu.VMEM((3, 2 * half + 2, width, chans), BF16),
            pltpu.VMEM((chans, 2 * cells), BF16),
            pltpu.VMEM((chans, chans), F32),
        ],
        compiler_params=params_of,
        cost_estimate=pl.CostEstimate(flops=2 * flops, bytes_accessed=10 * 2**20, transcendentals=2 * cells * chans),
        name="act_and_kernel_grad",
    )(grad_info, latent, lat_far, cot_b, cot_far, params[1:2], params[2:3])

    if paired:
        peer_b = from_peer(level, kernel_b)
        total = reduce_all(keep, send)
        a = lax.ppermute(total, ("replica", "core"), [(1, 0), (2, 3), (0, 2), (3, 1)])
        b = lax.ppermute(total, ("replica", "core"), [(1, 2), (2, 1)])
        left = jnp.where(replica == core, jnp.where(lower, total, a), jnp.where(lower, a, b))
        right = jnp.where(replica == core, jnp.where(lower, a, total), jnp.where(lower, b, a))
    else:
        terms = jnp.stack([keep, send], axis=2).reshape(zs * ys, 2, own_rows, cols.lead)
        summed = lax.psum_scatter(terms, ("z", "y"), scatter_dimension=0, tiled=False)
        ours = lax.dynamic_index_in_dim(summed, core, 0, keepdims=False)
        got = swap(lax.dynamic_index_in_dim(summed, 1 - core, 0, keepdims=False), "core")
        left, right = jnp.where(lower, ours, got), jnp.where(lower, got, ours)
    kernel_grad = jnp.concatenate([left, right[:, cols.both:]], axis=1).astype(F32)
    if paired:
        new_kernel = 0.5 * (shard + peer_b.astype(F32)) - (0.5 * rate) * kernel_grad
    else:
        stepped = shard - rate * kernel_grad
        new_kernel = 0.5 * (stepped + from_peer(level, stepped.astype(BF16)).astype(F32))

    block_rows = blocks[0].shape[0]
    product = partial(
        pl.pallas_call,
        out_shape=(
            jax.ShapeDtypeStruct((cells, chans), F32),
            jax.ShapeDtypeStruct((cells, chans), BF16),
        ),
        out_specs=(VMEM_SPEC,) * 2,
        scratch_shapes=[
            pltpu.VMEM((chans, cols.lead), BF16),
            pltpu.VMEM((3, 2 * half + 2, width, chans), BF16),
            pltpu.VMEM((2 * cells, chans), F32),
            pltpu.SemaphoreType.DMA((count,)),
        ],
        compiler_params=params_of,
        cost_estimate=pl.CostEstimate(flops=2 * flops, bytes_accessed=8 * 2**20, transcendentals=0),
    )
    back_own, back_send = product(
        partial(back_kernel, cols, count),
        in_specs=[SMEM_SPEC] + [VMEM_SPEC] * 2 + [HBM_SPEC] * count,
        name="act_grad_part",
    )(info, cot_b, cot_far, *blocks)
    back = back_own + swap(back_send, "core").astype(F32)

    lat = latent.astype(F32).reshape(cells, chans)
    xhat = (lat - stats[0]) * stats[1]
    pre = params[1] * xhat + params[2]
    sig = jax.nn.sigmoid(pre)
    pre_grad = (scale * back) * sig * (1.0 + pre * (1.0 - sig))
    vectors = jnp.stack([
        jnp.sum(cotan, axis=(0, 1)),
        jnp.sum(pre_grad * xhat, axis=0),
        jnp.sum(pre_grad, axis=0),
    ])
    vectors = vectors + swap(vectors, "core")
    vectors = vectors + swap(vectors, "y")
    reach = 1
    while reach < zs:
        vectors = vectors + lax.ppermute(vectors, "z", [(s, s ^ reach) for s in range(zs)])
        reach *= 2
    stepped_v = params - LR_VECTOR * vectors
    new_v = 0.5 * (stepped_v + from_peer(level, stepped_v))

    conv_own, conv_send = product(
        partial(conv_kernel, cols, count),
        in_specs=[SMEM_SPEC] + [VMEM_SPEC] + [HBM_SPEC] * count,
        name="conv_part",
    )(info, act, *blocks)
    conv = conv_own + swap(conv_send, "core").astype(F32)
    block = (scale * conv + params[0] + lat).astype(BF16)
    return (
        block.reshape(1, half, width, chans),
        new_kernel[None],
        new_v[0][None],
        new_v[1][None],
        new_v[2][None],
    )


def solution(mesh):
    replicas, shards = mesh.shape["replica"], mesh.shape["shard"]
    split = Mesh(mesh.devices.reshape(replicas, shards // 4, 2, 2), ("replica", "z", "y", "core"))
    shard = ("z", "y", "core")
    return jax.shard_map(
        per_device,
        mesh=split,
        in_specs=(
            P("replica", shard, None, None),
            P("replica", shard, None, None),
            P("replica", shard, None),
            P("replica", None),
            P("replica", None),
            P("replica", None),
            P(),
        ),
        out_specs=(
            P("replica", shard, None, None),
            P("replica", shard, None),
            P("replica", None),
            P("replica", None),
            P("replica", None),
        ),
        check_vma=False,
    )
```

time: 300 us -> 167 us (0.56)
  waiting for transfers between devices: 168 us -> 73.1 us
  blocking collectives: 58.6 us -> 0 us
  Pallas kernels: 0 us -> 35.6 us
  starting transfers between devices: 4 us -> 37.4 us
  matrix products: 22.3 us -> 0 us
  between operations: 15.2 us -> 1.77 us
  other arithmetic: 21.5 us -> 11.3 us
    unnamed x3 -> x0, waiting for transfers between devices: 82.6 us -> none
    all_gather x1 -> x0, waiting for transfers between devices: 67.1 us -> none  [per_device(): own = lax.all_gather(shard.astype(BF16), 'node', axis=0, tiled=False)]
    psum x1 -> x0, blocking collectives: 58.6 us -> none  [per_device(): vectors = lax.psum(vectors, ('node', 'core'))]
    ppermute x6 -> x33, waiting for transfers between devices: 18.6 us -> 73.1 us  [the longest x16 26 us: swap(): return lax.ppermute(value, axis, [(0, 1), (1, 0)])]
    pallas_call x0 -> x3, Pallas kernels: none -> 35.6 us  [the longest x1 13.3 us: per_device(): pl.pallas_call(partial(grad_kernel, cols, zs, ys), out_shape=(jax.ShapeDt...]
    ppermute x6 -> x33, starting transfers between devices: 3.74 us -> 37.4 us  [the longest x16 15.3 us: swap(): return lax.ppermute(value, axis, [(0, 1), (1, 0)])]
    dot_general x11 -> x0, matrix products: 22.3 us -> none  [the longest x1 10.5 us: per_device(): lax.dot_general(patches, whole, (((1,), (1,)), ((), ())), preferred_eleme...]
    select_n x4 -> x5, other arithmetic: 5.99 us -> 1.07 us  [the longest x1 0.85 us: per_device(): jnp.where(lower, jnp.concatenate([mine, got]), jnp.concatenate([got, mine]))]
  transfers between devices with their start and end apart: 8 -> 33, of which waited for: 5 -> 14; matrix products, arithmetic and copies ran while one was open for 6% -> 8% of each run, Pallas kernels for 0% -> 21%
where the time goes in v2:
time: 167 us; the launch traced here: 166 us
  waiting for transfers between devices  73.1 us (44%)
  starting transfers between devices  37.4 us (22%)
  Pallas kernels  35.6 us (21%)
  other arithmetic  11.3 us (7%)
  local copies, waits for them, and re-layouts  7.15 us (4%)
  between operations  1.77 us (1%)
    ppermute x16, waiting for transfers between devices, swap(): return lax.ppermute(value, axis, [(0, 1), (1, 0)])  26 us
    ppermute x16, starting transfers between devices, swap(): return lax.ppermute(value, axis, [(0, 1), (1, 0)])  15.3 us
    pallas_call x1, Pallas kernels, per_device(): pl.pallas_call(partial(grad_kernel, cols, zs, ys), out_shape=(jax.ShapeDt...  13.3 us
    ppermute x1, waiting for transfers between devices, gather_line(): out = along(mid, perm=OUTWARD)  11.3 us
    pallas_call x1, Pallas kernels, per_device(): product(partial(back_kernel, cols, count), in_specs=[SMEM_SPEC] + [VMEM_S...  11.2 us
    pallas_call x1, Pallas kernels, per_device(): product(partial(conv_kernel, cols, count), in_specs=[SMEM_SPEC] + [VMEM_S...  11.1 us
    ppermute x1, waiting for transfers between devices, gather_line(): out_far = along(mid_far, perm=OUTWARD)  9.08 us
    ppermute x1, waiting for transfers between devices, reduce_all(): in2 = along(slots[1], perm=INWARD)  8.78 us
  transfers between devices with their start and end apart: 33, of which 14 were waited for; matrix products, arithmetic and copies ran while one was open for 8% of the time, Pallas kernels for 21%

profile of v2, /device:TPU:0, one launch (start us, length us, event | category | flops | bytes accessed | tf_op | source)
XLA Modules:
  0.0 166.3 jit_solution(2751040656484105815)
XLA Ops:
  0.6 1.3 bitcast_convert_fusion
  2.6 0.9 fusion.26
  4.0 0.7 fusion.23
  6.1 0.8 maximum_select_fusion.refs_0_
  7.0 2.7 %collective-permute-start.3 = (bf16[80,2944]{1,0:T(8,128)(2,1)}, bf16[80,2944]{1,0:T(8,128)(2,1)}, u32[]{:S(2)}, u32[]{:S(2)}) collective-permute-start(bf16[80,2944]{1,0:T(8,128)(2,1)} %maximum_select_fusion.refs_0_), channel_id=1, source_target_pairs={{0,4},{4,0},{8,12},{12,8},{1,5},{5,1},{9,13},{13,9},{2,6},{6,2},{1... | collective-permute-start | bytes 1413128 | tf_op jit(solution)/shard_map/ppermute | solution.py:250
  9.7 1.4 collective-permute-start.4
  11.1 0.8 copy-done.12
  12.0 0.8 copy-done.13
  12.8 13.3 %act_and_kernel_grad.1 = (bf16[32,32,640]{2,1,0:T(8,128)(2,1)}, f32[2,640]{1,0:T(2,128)}, bf16[4,2,40,2944]{3,2,1,0:T(8,128)(2,1)}, bf16[4,2,40,2944]{3,2,1,0:T(8,128)(2,1)}) custom-call(s32[16]{0:T(128)} %concatenate.16.info, bf16[16,32,640]{2,1,0:T(8,128)(2,1)} %bitcast.57, bf16[16,32,640]{2,1,0:T(8,128)(2,1)} %copy-done.13, ...), custom_call_target="tpu_custom_call" | custom-call | flops 7717519360 | bytes 10485760 | tf_op jit(solution)/shard_map/act_and_kernel_grad/pallas_call | solution.py:329
  26.1 2.6 %slice_bitcast_fusion.3 = (bf16[2,40,2944]{2,1,0:T(8,128)(2,1)S(1)}, bf16[2,40,2944]{2,1,0:T(8,128)(2,1)}, bf16[2,40,2944]{2,1,0:T(8,128)(2,1)}, bf16[2,40,2944]{2,1,0:T(8,128)(2,1)S(1)}) fusion(bf16[4,2,40,2944]{3,2,1,0:T(8,128)(2,1)} %get-tuple-element.17), kind=kLoop, calls=%fused_computation.39 | loop fusion | bytes 3768320 | tf_op jit(solution)/shard_map/squeeze | solution.py:269
  28.7 1.5 collective-permute-start.17
  30.9 1.6 collective-permute-start.8
  32.5 1.6 collective-permute-start.15
  34.7 7.9 %collective-permute-done.17 = bf16[2,40,2944]{2,1,0:T(8,128)(2,1)} collective-permute-done((bf16[2,40,2944]{2,1,0:T(8,128)(2,1)}, bf16[2,40,2944]{2,1,0:T(8,128)(2,1)}, u32[]{:S(2)}, u32[]{:S(2)}) %collective-permute-start.17) | collective-permute-done | bytes 471072 | tf_op jit(solution)/shard_map/ppermute | solution.py:228
  42.7 1.5 collective-permute-start.9
  44.2 8.6 %collective-permute-done.20 = bf16[2,40,2944]{2,1,0:T(8,128)(2,1)} collective-permute-done((bf16[2,40,2944]{2,1,0:T(8,128)(2,1)}, bf16[2,40,2944]{2,1,0:T(8,128)(2,1)}, u32[]{:S(2)}, u32[]{:S(2)}) %collective-permute-start.20) | collective-permute-done | bytes 471072 | tf_op jit(solution)/shard_map/ppermute | solution.py:228
  52.8 1.3 collective-permute-start.5
  54.1 1.4 fusion.14
  55.5 11.3 %collective-permute-done.5 = bf16[80,2944]{1,0:T(8,128)(2,1)S(1)} collective-permute-done((bf16[80,2944]{1,0:T(8,128)(2,1)}, bf16[80,2944]{1,0:T(8,128)(2,1)S(1)}, u32[]{:S(2)}, u32[]{:S(2)}) %collective-permute-start.5) | collective-permute-done | bytes 471072 | tf_op jit(solution)/shard_map/ppermute | solution.py:253
  66.8 1.6 collective-permute-start.18
  68.5 2.3 %collective-permute-start.21 = (bf16[2,40,2944]{2,1,0:T(8,128)(2,1)S(1)}, bf16[2,40,2944]{2,1,0:T(8,128)(2,1)S(1)}, u32[]{:S(2)}, u32[]{:S(2)}) collective-permute-start(bf16[2,40,2944]{2,1,0:T(8,128)(2,1)S(1)} %get-tuple-element.32), channel_id=1, source_target_pairs={{0,4},{12,8},{1,5},{13,9},{2,6},{14,10},{3,7},{15,11},{16,20},{28,... | collective-permute-start | bytes 1413128 | tf_op jit(solution)/shard_map/ppermute | solution.py:271
  70.8 8.8 %collective-permute-done.18 = bf16[2,40,2944]{2,1,0:T(8,128)(2,1)S(1)} collective-permute-done((bf16[2,40,2944]{2,1,0:T(8,128)(2,1)S(1)}, bf16[2,40,2944]{2,1,0:T(8,128)(2,1)S(1)}, u32[]{:S(2)}, u32[]{:S(2)}) %collective-permute-start.18) | collective-permute-done | bytes 471072 | tf_op jit(solution)/shard_map/ppermute | solution.py:273
  79.6 1.3 collective-permute-start.7
  81.0 9.1 %collective-permute-done.7 = bf16[80,2944]{1,0:T(8,128)(2,1)S(1)} collective-permute-done((bf16[80,2944]{1,0:T(8,128)(2,1)S(1)}, bf16[80,2944]{1,0:T(8,128)(2,1)S(1)}, u32[]{:S(2)}, u32[]{:S(2)}) %collective-permute-start.7) | collective-permute-done | bytes 471072 | tf_op jit(solution)/shard_map/ppermute | solution.py:254
  90.0 1.5 collective-permute-start.10
  92.4 1.6 collective-permute-start.14
  94.6 4.7 %collective-permute-done.10.refs_6_ = bf16[80,2944]{1,0:T(8,128)(2,1)S(1)} collective-permute-done((bf16[80,2944]{1,0:T(8,128)(2,1)S(1)}, bf16[80,2944]{1,0:T(8,128)(2,1)S(1)}, u32[]{:S(2)}, u32[]{:S(2)}) %collective-permute-start.10) | collective-permute-done | bytes 471072 | tf_op jit(solution)/shard_map/ppermute | solution.py:228
  99.3 1.5 collective-permute-start.22
  100.8 3.6 %collective-permute-done.11.refs_7_ = bf16[80,2944]{1,0:T(8,128)(2,1)} collective-permute-done((bf16[80,2944]{1,0:T(8,128)(2,1)S(1)}, bf16[80,2944]{1,0:T(8,128)(2,1)}, u32[]{:S(2)}, u32[]{:S(2)}) %collective-permute-start.11) | collective-permute-done | bytes 471072 | tf_op jit(solution)/shard_map/ppermute | solution.py:228
  104.5 11.2 %act_grad_part.1 = (f32[512,640]{1,0:T(8,128)}, bf16[512,640]{1,0:T(8,128)(2,1)}) custom-call(s32[16]{0:T(128)} %concatenate.16.info, bf16[16,32,640]{2,1,0:T(8,128)(2,1)} %get-tuple-element.34.cot_own, bf16[16,32,640]{2,1,0:T(8,128)(2,1)} %copy-done.12, bf16[80,2944]{1,0:T(8,128)(2,1)} %maximum_select_fusion.refs_0_, ...), custom_call_target="tpu_custom_call" | custom-call | flops 7717519360 | bytes 8388608 | tf_op jit(solution)/shard_map/act_grad_part/pallas_call | solution.py:386
  115.8 11.1 %conv_part.1 = (f32[512,640]{1,0:T(8,128)}, bf16[512,640]{1,0:T(8,128)(2,1)}) custom-call(s32[16]{0:T(128)} %concatenate.16.info, bf16[32,32,640]{2,1,0:T(8,128)(2,1)} %get-tuple-element.13.act, bf16[80,2944]{1,0:T(8,128)(2,1)} %maximum_select_fusion.refs_0_, bf16[80,2944]{1,0:T(8,128)(2,1)} %collective-permute-done.3.refs_1_, bf16[80,2944]{1,0:T(8,128)(2,1)} %copy-done.6, ...), custom_call_target="tpu_custom_call" | custom-call | flops 7717519360 | bytes 8388608 | tf_op jit(solution)/shard_map/conv_part/pallas_call | solution.py:412
  127.5 1.2 add_convert_fusion.1
  128.8 1.8 %collective-permute-start.16 = (bf16[2,40,2944]{2,1,0:T(8,128)(2,1)S(1)}, bf16[2,40,2944]{2,1,0:T(8,128)(2,1)S(1)}, u32[]{:S(2)}, u32[]{:S(2)}) collective-permute-start(bf16[2,40,2944]{2,1,0:T(8,128)(2,1)S(1)} %get-tuple-element.26), channel_id=1, source_target_pairs={{0,4},{12,8},{1,5},{13,9},{2,6},{14,10},{3,7},{15,11},{16,20},{28,... | collective-permute-start | bytes 1413128 | tf_op jit(solution)/shard_map/ppermute | solution.py:274
  130.6 1.5 collective-permute-start.23
  132.1 3.3 %fusion.12 = (f32[640]{0:T(1024)S(1)}, f32[640]{0:T(1024)S(1)}, bf16[512,640]{1,0:T(8,128)(2,1)}) fusion(bf16[1,16,32,640]{3,2,1,0:T(8,128)(2,1)S(1)} %copy-done.5, f32[640]{0:T(1024)S(1)} %get-tuple-element.24, f32[640]{0:T(1024)S(1)} %get-tuple-element.23, f32[640]{0:T(1024)S(1)} %reduce.1, f32[512,640]{1,0:T(8,128)} %get-tuple-element.14, ...), kind=kLoop, calls=%fused_computation.14 | loop fusion | flops 8190720 | bytes 5260800 | tf_op jit(solution)/shard_map/reduce_sum | solution.py:400
  135.5 1.2 collective-permute-done.28
  136.7 1.6 collective-permute-start.29
  138.3 2.6 %collective-permute-done.16 = bf16[2,40,2944]{2,1,0:T(8,128)(2,1)S(1)} collective-permute-done((bf16[2,40,2944]{2,1,0:T(8,128)(2,1)S(1)}, bf16[2,40,2944]{2,1,0:T(8,128)(2,1)S(1)}, u32[]{:S(2)}, u32[]{:S(2)}) %collective-permute-start.16) | collective-permute-done | bytes 471072 | tf_op jit(solution)/shard_map/ppermute | solution.py:274
  140.9 4.2 %collective-permute-done.23 = bf16[2,40,2944]{2,1,0:T(8,128)(2,1)S(1)} collective-permute-done((bf16[2,40,2944]{2,1,0:T(8,128)(2,1)S(1)}, bf16[2,40,2944]{2,1,0:T(8,128)(2,1)S(1)}, u32[]{:S(2)}, u32[]{:S(2)}) %collective-permute-start.23) | collective-permute-done | bytes 471072 | tf_op jit(solution)/shard_map/ppermute | solution.py:276
  145.5 1.6 collective-permute-start.24
  147.1 2.0 %collective-permute-done.30 = f32[3,640]{1,0:T(4,128)S(1)} collective-permute-done((f32[3,640]{1,0:T(4,128)S(1)}, f32[3,640]{1,0:T(4,128)S(1)}, u32[]{:S(2)}, u32[]{:S(2)}) %collective-permute-start.30) | collective-permute-done | bytes 7712 | tf_op jit(solution)/shard_map/ppermute | solution.py:407
  149.1 1.1 collective-permute-start.31
  150.2 1.5 collective-permute-start.13
  152.4 1.3 collective-permute-done.31
  153.7 1.6 collective-permute-start.32
  156.6 7.0 %collective-permute-done.32 = f32[3,640]{1,0:T(4,128)S(1)} collective-permute-done((f32[3,640]{1,0:T(4,128)S(1)}, f32[3,640]{1,0:T(4,128)S(1)}, u32[]{:S(2)}, u32[]{:S(2)}) %collective-permute-start.32) | collective-permute-done | bytes 7712 | tf_op jit(solution)/shard_map/ppermute | solution.py:236
  164.2 0.9 collective-permute-done.25
  165.2 1.1 fusion.19
  (91 shorter events, 8.6 us)
Async XLA Ops:
  0.6 1.9 %copy-start.2 = (f32[1,16,32,640]{3,2,1,0:T(8,128)S(1)}, f32[1,16,32,640]{3,2,1,0:T(8,128)}, u32[]{:S(2)}) copy-start(f32[1,16,32,640]{3,2,1,0:T(8,128)} %param.10) | copy-start | bytes 3932164
  2.0 1.6 copy-start.4
  2.1 4.1 %collective-permute-start.2 = (bf16[40,2944]{1,0:T(8,128)(2,1)S(1)}, bf16[40,2944]{1,0:T(8,128)(2,1)S(1)}, u32[]{:S(2)}, u32[]{:S(2)}) collective-permute-start(bf16[40,2944]{1,0:T(8,128)(2,1)S(1)} %get-tuple-element.37), channel_id=1, source_target_pairs={{0,1},{1,0},{2,3},{3,2},{4,5},{5,4},{6,7},{7,6},{8,9},{9,8},{10,11... | collective-permute-start | bytes 706568 | tf_op jit(solution)/shard_map/ppermute | solution.py:228
  3.5 7.6 %collective-permute-start.1 = (bf16[16,32,640]{2,1,0:T(8,128)(2,1)}, bf16[16,32,640]{2,1,0:T(8,128)(2,1)S(1)}, u32[]{:S(2)}, u32[]{:S(2)}) collective-permute-start(bf16[16,32,640]{2,1,0:T(8,128)(2,1)} %get-tuple-element.34.cot_own), channel_id=1, source_target_pairs={{0,1},{1,0},{2,3},{3,2},{4,5},{5,4},{6,7},{7,6},{8,9},{9,8},{10,11... | collective-permute-start | bytes 1966088 | tf_op jit(solution)/shard_map/ppermute | solution.py:228
  3.6 7.5 %collective-permute-start = (bf16[16,32,640]{2,1,0:T(8,128)(2,1)S(1)}, bf16[16,32,640]{2,1,0:T(8,128)(2,1)S(1)}, u32[]{:S(2)}, u32[]{:S(2)}) collective-permute-start(bf16[16,32,640]{2,1,0:T(8,128)(2,1)S(1)} %bitcast.58), channel_id=1, source_target_pairs={{0,1},{1,0},{2,3},{3,2},{4,5},{5,4},{6,7},{7,6},{8,9},{9,8},{10,11... | collective-permute-start | bytes 1966088 | tf_op jit(solution)/shard_map/ppermute | solution.py:228
  7.0 25.5 %collective-permute-start.3 = (bf16[80,2944]{1,0:T(8,128)(2,1)}, bf16[80,2944]{1,0:T(8,128)(2,1)}, u32[]{:S(2)}, u32[]{:S(2)}) collective-permute-start(bf16[80,2944]{1,0:T(8,128)(2,1)} %maximum_select_fusion.refs_0_), channel_id=1, source_target_pairs={{0,4},{4,0},{8,12},{12,8},{1,5},{5,1},{9,13},{13,9},{2,6},{6,2},{1... | collective-permute-start | bytes 1413128 | tf_op jit(solution)/shard_map/ppermute | solution.py:250
  9.7 24.4 %collective-permute-start.4 = (bf16[80,2944]{1,0:T(8,128)(2,1)}, bf16[80,2944]{1,0:T(8,128)(2,1)}, u32[]{:S(2)}, u32[]{:S(2)}) collective-permute-start(bf16[80,2944]{1,0:T(8,128)(2,1)} %maximum_select_fusion.refs_0_), channel_id=1, source_target_pairs={{4,8},{8,4},{5,9},{9,5},{6,10},{10,6},{7,11},{11,7},{20,24},{24,20... | collective-permute-start | bytes 1413128 | tf_op jit(solution)/shard_map/ppermute | solution.py:251
  26.1 4.7 %copy-start.8 = (f32[1,640]{1,0:T(1,128)S(1)}, f32[1,640]{1,0:T(1,128)}, u32[]{:S(2)}) copy-start(f32[1,640]{1,0:T(1,128)} %gain.1) | copy-start | bytes 7684
  26.1 4.7 %copy-start.9 = (f32[1,640]{1,0:T(1,128)S(1)}, f32[1,640]{1,0:T(1,128)}, u32[]{:S(2)}) copy-start(f32[1,640]{1,0:T(1,128)} %shift.1) | copy-start | bytes 7684
  26.1 4.8 %copy-start.10 = (f32[1,640]{1,0:T(1,128)S(1)}, f32[1,640]{1,0:T(1,128)}, u32[]{:S(2)}) copy-start(f32[1,640]{1,0:T(1,128)} %param.12) | copy-start | bytes 7684
  26.1 6.4 %copy-start.11 = (f32[2,640]{1,0:T(2,128)S(1)}, f32[2,640]{1,0:T(2,128)}, u32[]{:S(2)}) copy-start(f32[2,640]{1,0:T(2,128)} %get-tuple-element.20) | copy-start | bytes 15364
  26.1 28.0 %copy-start.1 = (bf16[4,2,40,2944]{3,2,1,0:T(8,128)(2,1)S(1)}, bf16[4,2,40,2944]{3,2,1,0:T(8,128)(2,1)}, u32[]{:S(2)}) copy-start(bf16[4,2,40,2944]{3,2,1,0:T(8,128)(2,1)} %get-tuple-element.16) | copy-start | bytes 5652484
  28.7 13.9 %collective-permute-start.17 = (bf16[2,40,2944]{2,1,0:T(8,128)(2,1)}, bf16[2,40,2944]{2,1,0:T(8,128)(2,1)}, u32[]{:S(2)}, u32[]{:S(2)}) collective-permute-start(bf16[2,40,2944]{2,1,0:T(8,128)(2,1)} %get-tuple-element.29), channel_id=1, source_target_pairs={{0,16},{16,0},{1,17},{17,1},{2,18},{18,2},{3,19},{19,3},{4,20},{20... | collective-permute-start | bytes 1413128 | tf_op jit(solution)/shard_map/ppermute | solution.py:228
  30.2 22.5 %collective-permute-start.20 = (bf16[2,40,2944]{2,1,0:T(8,128)(2,1)}, bf16[2,40,2944]{2,1,0:T(8,128)(2,1)}, u32[]{:S(2)}, u32[]{:S(2)}) collective-permute-start(bf16[2,40,2944]{2,1,0:T(8,128)(2,1)} %get-tuple-element.28), channel_id=1, source_target_pairs={{0,16},{16,0},{1,17},{17,1},{2,18},{18,2},{3,19},{19,3},{4,20},{20... | collective-permute-start | bytes 1413128 | tf_op jit(solution)/shard_map/ppermute | solution.py:228
  30.9 61.5 %collective-permute-start.8 = (bf16[80,2944]{1,0:T(8,128)(2,1)}, bf16[80,2944]{1,0:T(8,128)(2,1)S(1)}, u32[]{:S(2)}, u32[]{:S(2)}) collective-permute-start(bf16[80,2944]{1,0:T(8,128)(2,1)} %maximum_select_fusion.refs_0_), channel_id=1, source_target_pairs={{0,2},{2,0},{1,3},{3,1},{4,6},{6,4},{5,7},{7,5},{8,10},{10,8},{9,1... | collective-permute-start | bytes 1413128 | tf_op jit(solution)/shard_map/ppermute | solution.py:228
  32.5 94.5 %collective-permute-start.15 = (bf16[2,40,2944]{2,1,0:T(8,128)(2,1)S(1)}, bf16[2,40,2944]{2,1,0:T(8,128)(2,1)S(1)}, u32[]{:S(2)}, u32[]{:S(2)}) collective-permute-start(bf16[2,40,2944]{2,1,0:T(8,128)(2,1)S(1)} %get-tuple-element.30), channel_id=1, source_target_pairs={{0,16},{16,0},{1,17},{17,1},{2,18},{18,2},{3,19},{19,3},{4,20},{20... | collective-permute-start | bytes 1413128 | tf_op jit(solution)/shard_map/ppermute | solution.py:228
  34.1 34.4 %collective-permute-start.6 = (bf16[80,2944]{1,0:T(8,128)(2,1)}, bf16[80,2944]{1,0:T(8,128)(2,1)S(1)}, u32[]{:S(2)}, u32[]{:S(2)}) collective-permute-start(bf16[80,2944]{1,0:T(8,128)(2,1)} %collective-permute-done.3.refs_1_), channel_id=1, source_target_pairs={{4,8},{8,4},{5,9},{9,5},{6,10},{10,6},{7,11},{11,7},{20,24},{24,20... | collective-permute-start | bytes 1413128 | tf_op jit(solution)/shard_map/ppermute | solution.py:252
  42.7 51.2 %collective-permute-start.9 = (bf16[80,2944]{1,0:T(8,128)(2,1)}, bf16[80,2944]{1,0:T(8,128)(2,1)S(1)}, u32[]{:S(2)}, u32[]{:S(2)}) collective-permute-start(bf16[80,2944]{1,0:T(8,128)(2,1)} %collective-permute-done.3.refs_1_), channel_id=1, source_target_pairs={{0,2},{2,0},{1,3},{3,1},{4,6},{6,4},{5,7},{7,5},{8,10},{10,8},{9,1... | collective-permute-start | bytes 1413128 | tf_op jit(solution)/shard_map/ppermute | solution.py:228
  52.8 14.0 %collective-permute-start.5 = (bf16[80,2944]{1,0:T(8,128)(2,1)}, bf16[80,2944]{1,0:T(8,128)(2,1)S(1)}, u32[]{:S(2)}, u32[]{:S(2)}) collective-permute-start(bf16[80,2944]{1,0:T(8,128)(2,1)} %collective-permute-done.4), channel_id=1, source_target_pairs={{4,0},{8,12},{5,1},{9,13},{6,2},{10,14},{7,3},{11,15},{20,16},{24,... | collective-permute-start | bytes 1413128 | tf_op jit(solution)/shard_map/ppermute | solution.py:253
  66.8 12.8 %collective-permute-start.18 = (bf16[2,40,2944]{2,1,0:T(8,128)(2,1)S(1)}, bf16[2,40,2944]{2,1,0:T(8,128)(2,1)S(1)}, u32[]{:S(2)}, u32[]{:S(2)}) collective-permute-start(bf16[2,40,2944]{2,1,0:T(8,128)(2,1)S(1)} %get-tuple-element.31), channel_id=1, source_target_pairs={{0,4},{12,8},{1,5},{13,9},{2,6},{14,10},{3,7},{15,11},{16,20},{28,... | collective-permute-start | bytes 1413128 | tf_op jit(solution)/shard_map/ppermute | solution.py:273
  68.4 23.2 %copy-start.6 = (bf16[80,2944]{1,0:T(8,128)(2,1)}, bf16[80,2944]{1,0:T(8,128)(2,1)S(1)}, u32[]{:S(2)}) copy-start(bf16[80,2944]{1,0:T(8,128)(2,1)S(1)} %broadcast_select_fusion.1.refs_2_) | copy-start | bytes 1413124
  68.5 23.2 %collective-permute-start.21 = (bf16[2,40,2944]{2,1,0:T(8,128)(2,1)S(1)}, bf16[2,40,2944]{2,1,0:T(8,128)(2,1)S(1)}, u32[]{:S(2)}, u32[]{:S(2)}) collective-permute-start(bf16[2,40,2944]{2,1,0:T(8,128)(2,1)S(1)} %get-tuple-element.32), channel_id=1, source_target_pairs={{0,4},{12,8},{1,5},{13,9},{2,6},{14,10},{3,7},{15,11},{16,20},{28,... | collective-permute-start | bytes 1413128 | tf_op jit(solution)/shard_map/ppermute | solution.py:271
  79.6 10.5 %collective-permute-start.7 = (bf16[80,2944]{1,0:T(8,128)(2,1)S(1)}, bf16[80,2944]{1,0:T(8,128)(2,1)S(1)}, u32[]{:S(2)}, u32[]{:S(2)}) collective-permute-start(bf16[80,2944]{1,0:T(8,128)(2,1)S(1)} %collective-permute-done.6), channel_id=1, source_target_pairs={{4,0},{8,12},{5,1},{9,13},{6,2},{10,14},{7,3},{11,15},{20,16},{24,... | collective-permute-start | bytes 1413128 | tf_op jit(solution)/shard_map/ppermute | solution.py:254
  90.0 9.3 %collective-permute-start.10 = (bf16[80,2944]{1,0:T(8,128)(2,1)S(1)}, bf16[80,2944]{1,0:T(8,128)(2,1)S(1)}, u32[]{:S(2)}, u32[]{:S(2)}) collective-permute-start(bf16[80,2944]{1,0:T(8,128)(2,1)S(1)} %broadcast_select_fusion.1.refs_2_), channel_id=1, source_target_pairs={{0,2},{2,0},{1,3},{3,1},{4,6},{6,4},{5,7},{7,5},{8,10},{10,8},{9,1... | collective-permute-start | bytes 1413128 | tf_op jit(solution)/shard_map/ppermute | solution.py:228
  91.6 12.9 %copy-start.7 = (bf16[80,2944]{1,0:T(8,128)(2,1)}, bf16[80,2944]{1,0:T(8,128)(2,1)S(1)}, u32[]{:S(2)}) copy-start(bf16[80,2944]{1,0:T(8,128)(2,1)S(1)} %broadcast_select_fusion.refs_3_) | copy-start | bytes 1413124
  91.7 12.8 %collective-permute-start.11 = (bf16[80,2944]{1,0:T(8,128)(2,1)S(1)}, bf16[80,2944]{1,0:T(8,128)(2,1)}, u32[]{:S(2)}, u32[]{:S(2)}) collective-permute-start(bf16[80,2944]{1,0:T(8,128)(2,1)S(1)} %broadcast_select_fusion.refs_3_), channel_id=1, source_target_pairs={{0,2},{2,0},{1,3},{3,1},{4,6},{6,4},{5,7},{7,5},{8,10},{10,8},{9,1... | collective-permute-start | bytes 1413128 | tf_op jit(solution)/shard_map/ppermute | solution.py:228
  92.4 12.1 %copy-start.14 = (bf16[80,2944]{1,0:T(8,128)(2,1)}, bf16[80,2944]{1,0:T(8,128)(2,1)S(1)}, u32[]{:S(2)}) copy-start(bf16[80,2944]{1,0:T(8,128)(2,1)S(1)} %collective-permute-done.8.refs_4_) | copy-start | bytes 1413124
  92.4 45.9 %collective-permute-start.14 = (bf16[2,40,2944]{2,1,0:T(8,128)(2,1)S(1)}, bf16[2,40,2944]{2,1,0:T(8,128)(2,1)S(1)}, u32[]{:S(2)}, u32[]{:S(2)}) collective-permute-start(bf16[2,40,2944]{2,1,0:T(8,128)(2,1)S(1)} %get-tuple-element.27), channel_id=1, source_target_pairs={{0,16},{16,0},{1,17},{17,1},{2,18},{18,2},{3,19},{19,3},{4,20},{20... | collective-permute-start | bytes 1413128 | tf_op jit(solution)/shard_map/ppermute | solution.py:228
  93.9 6.9 %copy-start.15 = (bf16[80,2944]{1,0:T(8,128)(2,1)}, bf16[80,2944]{1,0:T(8,128)(2,1)S(1)}, u32[]{:S(2)}) copy-start(bf16[80,2944]{1,0:T(8,128)(2,1)S(1)} %collective-permute-done.9.refs_5_) | copy-start | bytes 1413124
  93.9 44.4 %collective-permute-start.19 = (bf16[2,40,2944]{2,1,0:T(8,128)(2,1)S(1)}, bf16[2,40,2944]{2,1,0:T(8,128)(2,1)S(1)}, u32[]{:S(2)}, u32[]{:S(2)}) collective-permute-start(bf16[2,40,2944]{2,1,0:T(8,128)(2,1)S(1)} %add_convert_fusion.3), channel_id=1, source_target_pairs={{4,8},{8,4},{5,9},{9,5},{6,10},{10,6},{7,11},{11,7},{20,24},{24,20... | collective-permute-start | bytes 1413128 | tf_op jit(solution)/shard_map/ppermute | solution.py:275
  99.3 1.5 copy-start.16
  99.3 28.2 %collective-permute-start.22 = (bf16[2,40,2944]{2,1,0:T(8,128)(2,1)S(1)}, bf16[2,40,2944]{2,1,0:T(8,128)(2,1)}, u32[]{:S(2)}, u32[]{:S(2)}) collective-permute-start(bf16[2,40,2944]{2,1,0:T(8,128)(2,1)S(1)} %add_convert_fusion.2), channel_id=1, source_target_pairs={{4,8},{8,4},{5,9},{9,5},{6,10},{10,6},{7,11},{11,7},{20,24},{24,20... | collective-permute-start | bytes 1413128 | tf_op jit(solution)/shard_map/ppermute | solution.py:272
  115.7 14.8 %collective-permute-start.27 = (bf16[512,640]{1,0:T(8,128)(2,1)}, bf16[512,640]{1,0:T(8,128)(2,1)S(1)}, u32[]{:S(2)}, u32[]{:S(2)}) collective-permute-start(bf16[512,640]{1,0:T(8,128)(2,1)} %get-tuple-element.19), channel_id=1, source_target_pairs={{0,1},{1,0},{2,3},{3,2},{4,5},{5,4},{6,7},{7,6},{8,9},{9,8},{10,11... | collective-permute-start | bytes 1966088 | tf_op jit(solution)/shard_map/ppermute | solution.py:228
  126.9 5.1 %copy-start.3 = (f32[512,640]{1,0:T(8,128)S(1)}, f32[512,640]{1,0:T(8,128)}, u32[]{:S(2)}) copy-start(f32[512,640]{1,0:T(8,128)} %get-tuple-element.18) | copy-start | bytes 3932164
  127.0 5.1 %copy-start.5 = (bf16[1,16,32,640]{3,2,1,0:T(8,128)(2,1)S(1)}, bf16[1,16,32,640]{3,2,1,0:T(8,128)(2,1)}, u32[]{:S(2)}) copy-start(bf16[1,16,32,640]{3,2,1,0:T(8,128)(2,1)} %param.9) | copy-start | bytes 1966084
  127.0 5.1 %collective-permute-start.12 = (bf16[512,640]{1,0:T(8,128)(2,1)}, bf16[512,640]{1,0:T(8,128)(2,1)S(1)}, u32[]{:S(2)}, u32[]{:S(2)}) collective-permute-start(bf16[512,640]{1,0:T(8,128)(2,1)} %get-tuple-element.15), channel_id=1, source_target_pairs={{0,1},{1,0},{2,3},{3,2},{4,5},{5,4},{6,7},{7,6},{8,9},{9,8},{10,11... | collective-permute-start | bytes 1966088 | tf_op jit(solution)/shard_map/ppermute | solution.py:228
  128.8 12.1 %collective-permute-start.16 = (bf16[2,40,2944]{2,1,0:T(8,128)(2,1)S(1)}, bf16[2,40,2944]{2,1,0:T(8,128)(2,1)S(1)}, u32[]{:S(2)}, u32[]{:S(2)}) collective-permute-start(bf16[2,40,2944]{2,1,0:T(8,128)(2,1)S(1)} %get-tuple-element.26), channel_id=1, source_target_pairs={{0,4},{12,8},{1,5},{13,9},{2,6},{14,10},{3,7},{15,11},{16,20},{28,... | collective-permute-start | bytes 1413128 | tf_op jit(solution)/shard_map/ppermute | solution.py:274
  130.6 14.4 %collective-permute-start.23 = (bf16[2,40,2944]{2,1,0:T(8,128)(2,1)S(1)}, bf16[2,40,2944]{2,1,0:T(8,128)(2,1)S(1)}, u32[]{:S(2)}, u32[]{:S(2)}) collective-permute-start(bf16[2,40,2944]{2,1,0:T(8,128)(2,1)S(1)} %get-tuple-element.25), channel_id=1, source_target_pairs={{4,0},{8,12},{5,1},{9,13},{6,2},{10,14},{7,3},{11,15},{20,16},{24,... | collective-permute-start | bytes 1413128 | tf_op jit(solution)/shard_map/ppermute | solution.py:276
  135.4 1.2 collective-permute-start.28
  136.7 8.7 %collective-permute-start.29 = (f32[3,640]{1,0:T(4,128)S(1)}, f32[3,640]{1,0:T(4,128)S(1)}, u32[]{:S(2)}, u32[]{:S(2)}) collective-permute-start(f32[3,640]{1,0:T(4,128)S(1)} %fusion.24), channel_id=1, source_target_pairs={{0,2},{2,0},{1,3},{3,1},{4,6},{6,4},{5,7},{7,5},{8,10},{10,8},{9,1... | collective-permute-start | bytes 23048 | tf_op jit(solution)/shard_map/ppermute | solution.py:228
  145.4 3.7 %collective-permute-start.30 = (f32[3,640]{1,0:T(4,128)S(1)}, f32[3,640]{1,0:T(4,128)S(1)}, u32[]{:S(2)}, u32[]{:S(2)}) collective-permute-start(f32[3,640]{1,0:T(4,128)S(1)} %fusion.28), channel_id=1, source_target_pairs={{0,4},{4,0},{8,12},{12,8},{1,5},{5,1},{9,13},{13,9},{2,6},{6,2},{1... | collective-permute-start | bytes 23048 | tf_op jit(solution)/shard_map/ppermute | solution.py:407
  145.5 9.8 %collective-permute-start.24 = (bf16[40,2944]{1,0:T(8,128)(2,1)S(1)}, bf16[40,2944]{1,0:T(8,128)(2,1)S(1)}, u32[]{:S(2)}, u32[]{:S(2)}) collective-permute-start(bf16[40,2944]{1,0:T(8,128)(2,1)S(1)} %slice_bitcast_fusion.4), channel_id=1, source_target_pairs={{0,2},{2,0},{1,3},{3,1},{4,6},{6,4},{5,7},{7,5},{8,10},{10,8},{9,1... | collective-permute-start | bytes 706568 | tf_op jit(solution)/shard_map/ppermute | solution.py:228
  149.1 4.6 %collective-permute-start.31 = (f32[3,640]{1,0:T(4,128)S(1)}, f32[3,640]{1,0:T(4,128)S(1)}, u32[]{:S(2)}, u32[]{:S(2)}) collective-permute-start(f32[3,640]{1,0:T(4,128)S(1)} %add.141), channel_id=1, source_target_pairs={{0,8},{4,12},{8,0},{12,4},{1,9},{5,13},{9,1},{13,5},{2,10},{6,14},... | collective-permute-start | bytes 23048 | tf_op jit(solution)/shard_map/ppermute | solution.py:407
  150.2 15.0 %collective-permute-start.13 = (bf16[40,5760]{1,0:T(8,128)(2,1)S(1)}, bf16[40,5760]{1,0:T(8,128)(2,1)S(1)}, u32[]{:S(2)}, u32[]{:S(2)}) collective-permute-start(bf16[40,5760]{1,0:T(8,128)(2,1)S(1)} %bitcast_convert_fusion), channel_id=1, source_target_pairs={{0,16},{16,0},{1,17},{17,1},{2,18},{18,2},{3,19},{19,3},{4,20},{20... | collective-permute-start | bytes 1382408 | tf_op jit(solution)/shard_map/ppermute | solution.py:236
  152.4 12.8 %copy-start = (f32[1,40,5760]{2,1,0:T(8,128)S(1)}, f32[1,40,5760]{2,1,0:T(8,128)}, u32[]{:S(2)}) copy-start(f32[1,40,5760]{2,1,0:T(8,128)} %param.11) | copy-start | bytes 2764804
  153.7 9.9 %collective-permute-start.32 = (f32[3,640]{1,0:T(4,128)S(1)}, f32[3,640]{1,0:T(4,128)S(1)}, u32[]{:S(2)}, u32[]{:S(2)}) collective-permute-start(f32[3,640]{1,0:T(4,128)S(1)} %maximum_subtract_fusion), channel_id=1, source_target_pairs={{0,16},{16,0},{1,17},{17,1},{2,18},{18,2},{3,19},{19,3},{4,20},{20... | collective-permute-start | bytes 23048 | tf_op jit(solution)/shard_map/ppermute | solution.py:236
  155.4 9.7 %collective-permute-start.25 = (bf16[40,2944]{1,0:T(8,128)(2,1)S(1)}, bf16[40,2944]{1,0:T(8,128)(2,1)S(1)}, u32[]{:S(2)}, u32[]{:S(2)}) collective-permute-start(bf16[40,2944]{1,0:T(8,128)(2,1)S(1)} %fusion.20), channel_id=1, source_target_pairs={{1,0},{16,17},{0,16},{17,1},{3,2},{18,19},{2,18},{19,3},{5,4},{20,... | collective-permute-start | bytes 706568 | tf_op jit(solution)/shard_map/ppermute | solution.py:352
  155.9 9.2 %collective-permute-start.26 = (bf16[40,2944]{1,0:T(8,128)(2,1)S(1)}, bf16[40,2944]{1,0:T(8,128)(2,1)S(1)}, u32[]{:S(2)}, u32[]{:S(2)}) collective-permute-start(bf16[40,2944]{1,0:T(8,128)(2,1)S(1)} %fusion.20), channel_id=1, source_target_pairs={{1,16},{16,1},{3,18},{18,3},{5,20},{20,5},{7,22},{22,7},{9,24},{24... | collective-permute-start | bytes 706568 | tf_op jit(solution)/shard_map/ppermute | solution.py:353
  (2 other events, 1.7 us)

commit v3 on v2

v3 whole, which is shorter than its diff:
```python
from functools import partial

import jax
import jax.numpy as jnp
import numpy as np
from jax import lax
from jax.experimental import pallas as pl
from jax.experimental.pallas import tpu as pltpu
from jax.sharding import Mesh, PartitionSpec as P

GROUPS = 32
EPS = 1e-05
LR_KERNEL = 0.1
LR_VECTOR = 0.01
LANES = 128
BF16 = jnp.bfloat16
F32 = jnp.float32

SMEM_SPEC = pl.BlockSpec(memory_space=pltpu.SMEM)
VMEM_SPEC = pl.BlockSpec(memory_space=pltpu.VMEM)


class Columns:
    def __init__(self, chans):
        tiles = 9 * chans // LANES
        self.total = 9 * chans
        self.lead = (tiles + 1) // 2 * LANES
        self.start = self.total - self.lead
        self.both = 2 * self.lead - self.total
        self.mid = self.lead - 4 * chans
        self.mid_start = chans - self.mid

    def tap(self, core, k, chans):
        tap = jnp.where(core == 0, k, 5 + k)
        return tap, pl.multiple_of(jnp.where(core == 0, k * chans, self.mid + k * chans), LANES)

    def middle(self, core, chans):
        place = jnp.where(core == 0, 4 * chans, 0)
        channel = jnp.where(core == 0, 0, self.mid_start)
        return pl.multiple_of(place, LANES), pl.multiple_of(channel, LANES)


def fill_shifts(shifts, row, values):
    width = values.shape[0]
    at = lax.broadcasted_iota(jnp.int32, values.shape, 0)
    left = jnp.where(at == 0, 0.0, pltpu.roll(values, 1, 0))
    right = jnp.where(at == width - 1, 0.0, pltpu.roll(values, width - 1, 0))
    shifts[0, row] = left.astype(BF16)
    shifts[1, row] = values.astype(BF16)
    shifts[2, row] = right.astype(BF16)


def clear_edges(shifts):
    zero = jnp.zeros(shifts.shape[2:], shifts.dtype)
    for b in range(3):
        shifts[b, 0] = zero
        shifts[b, shifts.shape[1] - 1] = zero


def act_kernel(order, dev, table, lat_own, lat_far, cot_own, cot_far, gain, shift,
               stats, acts, cot_t, cot_f):
    me = dev[0]
    core = me % 2
    half, width, chans = lat_own.shape
    cells = 2 * half * width
    group_width = chans // GROUPS
    own_at = core * half
    far_at = half - own_at
    clear_edges(acts)

    def add_row(i, sums):
        total, square = sums
        a = lat_own[i].astype(F32)
        b = lat_far[i].astype(F32)
        return total + (a + b), square + (a * a + b * b)

    zero = jnp.zeros((width, chans), F32)
    total, square = lax.fori_loop(0, half, add_row, (zero, zero))
    sums = jnp.concatenate(
        [jnp.sum(total, axis=0, keepdims=True), jnp.sum(square, axis=0, keepdims=True),
         jnp.zeros((6, chans), F32)], axis=0
    )
    first = lax.broadcasted_iota(jnp.int32, (chans, LANES), 0)
    start = lax.broadcasted_iota(jnp.int32, (chans, LANES), 1) * group_width
    member = jnp.where((first >= start) & (first < start + group_width), 1.0, 0.0)
    exact = partial(lax.dot_general, precision=lax.Precision.HIGHEST, preferred_element_type=F32)
    sums = exact(sums, member, (((1,), (0,)), ((), ()))) / (cells * group_width)
    sums = exact(sums, member, (((1,), (1,)), ((), ())))
    mean = sums[0:1]
    rstd = lax.rsqrt(sums[1:2] - mean * mean + EPS)
    stats[0:1] = mean
    stats[1:2] = rstd
    gain_v, shift_v = gain[...], shift[...]

    def act_rows(i, _):
        for ref, base in ((lat_own, own_at), (lat_far, far_at)):
            pre = gain_v * ((ref[i].astype(F32) - mean) * rstd) + shift_v
            fill_shifts(acts, base + i + 1, pre * (0.5 + 0.5 * jnp.tanh(0.5 * pre)))
        return 0

    lax.fori_loop(0, half, act_rows, 0)

    chunk = LANES // width
    for ref, base in ((cot_own, own_at), (cot_far, far_at)):
        for i in range(half // chunk):
            piece = ref[i * chunk:(i + 1) * chunk].reshape(LANES, chans).astype(F32)
            place = pl.multiple_of(base * width + i * LANES, LANES)
            if order is None:
                cot_t[:, pl.ds(place, LANES)] = piece.T.astype(BF16)
            else:
                cot_f[:, pl.ds(place, LANES)] = piece.T
    if order is not None:
        first_at, part, count = order
        for q in range(count // 2):
            pair = [
                cot_f[pl.ds(pl.multiple_of(table[me, first_at + 2 * q + i], 8), part)]
                for i in range(2)
            ]
            cot_t[2 * q * part:(2 * q + 2) * part] = jnp.concatenate(pair).astype(BF16)


def grad_kernel(cols, dev, acts, cot_t, *pieces):
    core = dev[0] % 2
    rows, width, chans = acts.shape[1] - 2, acts.shape[2], acts.shape[3]
    cells = rows * width
    count = pieces[0].shape[0]

    def emit(window, place, wide):
        value = jnp.dot(cot_t[...], window, preferred_element_type=F32)
        for q, piece in enumerate(pieces):
            piece[:, pl.ds(place, wide)] = value[q * count:(q + 1) * count].astype(BF16)

    def full_tap(k, _):
        tap, place = cols.tap(core, k, chans)
        emit(acts[tap % 3, pl.ds(tap // 3, rows)].reshape(cells, chans), place, chans)
        return 0

    lax.fori_loop(0, 4, full_tap, 0)
    place, channel = cols.middle(core, chans)
    emit(acts[1, 1:rows + 1, :, pl.ds(channel, cols.mid)].reshape(cells, cols.mid), place, cols.mid)


def slope_kernel(dev, stats, gain, shift, lat_own, lat_far, cot_own, cot_far, cots, slope, slope_x):
    core = dev[0] % 2
    half = lat_own.shape[0]
    clear_edges(cots)
    mean, rstd = stats[0:1], stats[1:2]
    gain_v, shift_v = gain[...], shift[...]

    def one_row(i, _):
        for lat, cot, base in ((lat_own, cot_own, core * half), (lat_far, cot_far, half - core * half)):
            fill_shifts(cots, base + i + 1, cot[i].astype(F32))
            xhat = (lat[i].astype(F32) - mean) * rstd
            pre = gain_v * xhat + shift_v
            sig = 0.5 + 0.5 * jnp.tanh(0.5 * pre)
            value = sig * (1.0 + pre * (1.0 - sig))
            slope[base + i] = value.astype(BF16)
            slope_x[base + i] = (value * xhat).astype(BF16)
        return 0

    lax.fori_loop(0, half, one_row, 0)


def place_blocks(first_at, me, table, blocks, whole):
    for i, block in enumerate(blocks):
        count = block.shape[0]
        at = pl.multiple_of(table[me, first_at + i] * count, count)
        whole[pl.ds(at, count)] = block[...]


def conv_kernel(cols, first_at, count, dev, table, acts, *refs):
    blocks, (own, far, whole, total) = refs[:count], refs[count:]
    me = dev[0]
    core = me % 2
    rows, width, chans = acts.shape[1] - 2, acts.shape[2], acts.shape[3]
    cells = rows * width
    place_blocks(first_at, me, table, blocks, whole)
    nt = (((1,), (1,)), ((), ()))
    place, channel = cols.middle(core, chans)
    window = acts[1, 1:rows + 1, :, pl.ds(channel, cols.mid)].reshape(cells, cols.mid)
    lane = lax.broadcasted_iota(jnp.int32, window.shape, 1)
    window = jnp.where((core == 1) & (lane < cols.both), jnp.zeros_like(window), window)
    total[...] = lax.dot_general(window, whole[:, pl.ds(place, cols.mid)], nt, preferred_element_type=F32)

    def full_tap(k, _):
        tap, place = cols.tap(core, k, chans)
        window = acts[tap % 3, pl.ds(tap // 3, rows)].reshape(cells, chans)
        total[...] += lax.dot_general(window, whole[:, pl.ds(place, chans)], nt, preferred_element_type=F32)
        return 0

    lax.fori_loop(0, 4, full_tap, 0)
    half = cells // 2
    own[...] = total[pl.ds(pl.multiple_of(core * half, half), half)]
    far[...] = total[pl.ds(pl.multiple_of((1 - core) * half, half), half)].astype(BF16)


def back_kernel(cols, first_at, count, dev, table, cots, slope, slope_x, *refs):
    blocks, (sums, whole, total) = refs[:count], refs[count:]
    me = dev[0]
    core = me % 2
    rows, width, chans = slope.shape
    cells = rows * width
    place_blocks(first_at, me, table, blocks, whole)
    total[...] = jnp.zeros_like(total)
    place, channel = cols.middle(core, chans)
    window = cots[1, 1:rows + 1].reshape(cells, chans)
    value = jnp.dot(window, whole[:, pl.ds(place, cols.mid)], preferred_element_type=F32)
    lane = lax.broadcasted_iota(jnp.int32, value.shape, 1)
    total[:, pl.ds(channel, cols.mid)] = jnp.where((core == 1) & (lane < cols.both), 0.0, value)

    def full_tap(k, _):
        tap, place = cols.tap(core, k, chans)
        window = cots[2 - tap % 3, pl.ds(2 - tap // 3, rows)].reshape(cells, chans)
        total[...] += jnp.dot(window, whole[:, pl.ds(place, chans)], preferred_element_type=F32)
        return 0

    lax.fori_loop(0, 4, full_tap, 0)

    def add_row(i, carry):
        gains, shifts = carry
        value = total[pl.ds(pl.multiple_of(i * width, width), width)]
        return gains + value * slope_x[i].astype(F32), shifts + value * slope[i].astype(F32)

    zero = jnp.zeros((width, chans), F32)
    gains, shifts = lax.fori_loop(0, rows, add_row, (zero, zero))
    scale = cols.total ** (-0.5)
    sums[0:1] = scale * jnp.sum(gains, axis=0, keepdims=True)
    sums[1:2] = scale * jnp.sum(shifts, axis=0, keepdims=True)


NODE = ("z", "y")


def swap(value, axis):
    return lax.ppermute(value, axis, [(0, 1), (1, 0)])


def from_peer(level, value):
    count = lax.axis_size("replica")
    levels = count.bit_length() - 1
    moves = [[(s, (s + (1 << k)) % count) for s in range(count)] for k in range(levels)]
    if levels == 1:
        return lax.ppermute(value, "replica", moves[0])
    return lax.switch(level, [lambda v, m=m: lax.ppermute(v, "replica", m) for m in moves], value)


class Ring:
    def __init__(self, zs):
        self.count = 2 * zs
        self.reach = zs
        self.nodes = [2 * z for z in range(zs)] + [2 * z + 1 for z in reversed(range(zs))]
        ahead = list(zip(self.nodes, self.nodes[1:] + self.nodes[:1]))
        self.ahead = ahead
        self.behind = [(b, a) for a, b in ahead]

    def node(self, at, offset):
        return self.nodes[(at + offset) % self.count]

    def up(self, value):
        return lax.ppermute(value, NODE, self.ahead)

    def down(self, value):
        return lax.ppermute(value, NODE, self.behind)

    def table(self, part):
        rows = np.zeros((2, self.count, 2, 3 * self.count), np.int32)
        for replica in range(2):
            for at, node in enumerate(self.nodes):
                line = [node]
                for k in range(1, self.reach + 1):
                    line.append(self.node(at, -k))
                    if k < self.reach:
                        line.append(self.node(at, k))
                for j in range(self.reach):
                    targets = [self.node(at, self.reach - j), self.node(at, j + 1 - self.reach)]
                    for which in (replica, 1 - replica):
                        line += [(2 * target + which) * part for target in targets]
                rows[replica, node, :] = line
        return rows.reshape(-1, 3 * self.count)


def add(*values):
    total = values[0].astype(F32)
    for value in values[1:]:
        total = total + value.astype(F32)
    return total.astype(BF16)


def tied(*values):
    return lax.optimization_barrier(values)


def per_device(latents, cotangent, kernel, conv_bias, gn_gain, gn_shift, step):
    latent, cotan, shard = latents[0], cotangent[0], kernel[0]
    half, width, chans = latent.shape
    part = shard.shape[0]
    cols = Columns(chans)
    cells = half * width
    zs, replicas = lax.axis_size("z"), lax.axis_size("replica")
    core, z, y, replica = (lax.axis_index(a) for a in ("core", "z", "y", "replica"))
    lower = core == 0
    paired = replicas == 2
    ring = Ring(zs)
    scale = cols.total ** (-0.5)
    level = step[0] % (replicas.bit_length() - 1)
    rate = LR_KERNEL * (1.0 - (step[0] % 1000).astype(F32) / 2000.0)
    dev = (((replica * zs + z) * 2 + y) * 2 + core).reshape(1)

    kernel_b = shard.astype(BF16)
    mine = lax.dynamic_slice_in_dim(kernel_b, core * cols.start, cols.lead, 1)
    theirs = lax.dynamic_slice_in_dim(kernel_b, (1 - core) * cols.start, cols.lead, 1)
    got = swap(theirs, "core")
    unit = jnp.where(lower, jnp.concatenate([mine, got]), jnp.concatenate([got, mine]))
    lat_far = swap(latent, "core")
    cot_b = cotan.astype(BF16)
    cot_far = swap(cot_b, "core")

    if paired:
        table = jnp.asarray(ring.table(part))
        order = (ring.count, part, 2 * ring.count)
        up1, down1 = ring.up(unit), ring.down(unit)
        peer_b = from_peer(level, kernel_b)
    else:
        table = jnp.zeros((replicas * zs * 4, 1), jnp.int32)
        order = None

    def call(body, outs, ins, scratch, megabytes, flops, extra=0):
        return pl.pallas_call(
            body,
            out_shape=outs,
            in_specs=ins,
            out_specs=jax.tree.map(lambda _: VMEM_SPEC, outs),
            scratch_shapes=scratch,
            compiler_params=pltpu.CompilerParams(vmem_limit_bytes=megabytes * 2**20),
            cost_estimate=pl.CostEstimate(flops=flops, bytes_accessed=8 * 2**20, transcendentals=extra),
        )

    image = (2 * half, width, chans)
    shifted = jax.ShapeDtypeStruct((3, 2 * half + 2, width, chans), BF16)
    flops = 2 * 2 * cells * chans * cols.lead
    stats, acts, cot_t = call(
        partial(act_kernel, order),
        (jax.ShapeDtypeStruct((2, chans), F32), shifted, jax.ShapeDtypeStruct((chans, 2 * cells), BF16)),
        [SMEM_SPEC] * 2 + [VMEM_SPEC] * 6,
        [pltpu.VMEM((chans, 2 * cells), F32)],
        24, flops, 2 * cells * chans,
    )(dev, table, latent, lat_far, cot_b, cot_far, gn_gain, gn_shift)
    if paired:
        up1, down1, acts = tied(up1, down1, acts)
        up2, down2 = ring.up(up1), ring.down(down1)

    pieces = call(
        partial(grad_kernel, cols),
        [jax.ShapeDtypeStruct((2 * part, cols.lead), BF16)] * (2 * zs),
        [SMEM_SPEC] + [VMEM_SPEC] * 2,
        [],
        24, 2 * flops,
    )(dev, acts, cot_t)
    cots, slope, slope_x = call(
        slope_kernel,
        (shifted, jax.ShapeDtypeStruct(image, BF16), jax.ShapeDtypeStruct(image, BF16)),
        [SMEM_SPEC] + [VMEM_SPEC] * 7,
        [],
        24, flops, 2 * cells * chans,
    )(dev, stats, gn_gain, gn_shift, latent, lat_far, cot_b, cot_far)

    if paired:
        blocks = [unit, up1, down1, up2, down2]
        ups, downs = [up1, up2], [down1, down2]
        for k in range(3, zs + 1):
            ups.append(ring.up(ups[-1]))
            blocks.append(ups[-1])
            if k < zs:
                downs.append(ring.down(downs[-1]))
                blocks.append(downs[-1])
        slots = [add(pieces[2 * j], swap(pieces[2 * j + 1], "replica")) for j in range(zs)]
        up_sum = down_sum = None
        for j in range(zs):
            ahead, behind = slots[j][:part], slots[j][part:]
            if j > 0:
                ahead, behind = add(ahead, up_sum), add(behind, down_sum)
            up_sum = ring.up(ahead)
            if j < zs - 1:
                down_sum = ring.down(behind)
        total = add(behind, up_sum)
        a = lax.ppermute(total, ("replica", "core"), [(1, 0), (2, 3), (0, 2), (3, 1)])
        b = lax.ppermute(total, ("replica", "core"), [(1, 2), (2, 1)])
        left = jnp.where(replica == core, jnp.where(lower, total, a), jnp.where(lower, a, b))
        right = jnp.where(replica == core, jnp.where(lower, a, total), jnp.where(lower, b, a))
    else:
        blocks = [lax.all_gather(unit, NODE, axis=0, tiled=True)]
        terms = jnp.concatenate(pieces).reshape(2 * zs, 2, part, cols.lead)
        summed = lax.psum_scatter(terms, NODE, scatter_dimension=0, tiled=False)
        ours = lax.dynamic_index_in_dim(summed, core, 0, keepdims=False)
        got = swap(lax.dynamic_index_in_dim(summed, 1 - core, 0, keepdims=False), "core")
        left, right = jnp.where(lower, ours, got), jnp.where(lower, got, ours)
    kernel_grad = jnp.concatenate([left, right[:, cols.both:]], axis=1).astype(F32)
    if paired:
        new_kernel = 0.5 * (shard + peer_b.astype(F32)) - (0.5 * scale * rate) * kernel_grad
    else:
        stepped = shard - (scale * rate) * kernel_grad
        new_kernel = 0.5 * (stepped + from_peer(level, stepped.astype(BF16)).astype(F32))

    count = len(blocks)
    whole = pltpu.VMEM((chans, cols.lead), BF16)
    total_f = pltpu.VMEM((2 * cells, chans), F32)
    sums = call(
        partial(back_kernel, cols, 0, count),
        jax.ShapeDtypeStruct((2, chans), F32),
        [SMEM_SPEC] * 2 + [VMEM_SPEC] * (3 + count),
        [whole, total_f],
        24, 2 * flops,
    )(dev, table, cots, slope, slope_x, *blocks)
    conv_own, conv_send = call(
        partial(conv_kernel, cols, 0, count),
        (jax.ShapeDtypeStruct((cells, chans), F32), jax.ShapeDtypeStruct((cells, chans), BF16)),
        [SMEM_SPEC] * 2 + [VMEM_SPEC] * (1 + count),
        [whole, total_f],
        24, 2 * flops,
    )(dev, table, acts, *blocks)

    vectors = jnp.concatenate([jnp.sum(cotan, axis=(0, 1))[None], sums])
    vectors = vectors + swap(vectors, "core")
    vectors = vectors + swap(vectors, "y")
    reach = 1
    while reach < zs:
        vectors = vectors + lax.ppermute(vectors, "z", [(s, s ^ reach) for s in range(zs)])
        reach *= 2
    stepped_v = jnp.concatenate([conv_bias, gn_gain, gn_shift]) - LR_VECTOR * vectors
    new_v = 0.5 * (stepped_v + from_peer(level, stepped_v))

    conv = conv_own + swap(conv_send, "core").astype(F32)
    block = (scale * conv + conv_bias + latent.astype(F32).reshape(cells, chans)).astype(BF16)
    return (
        block.reshape(1, half, width, chans),
        new_kernel[None],
        new_v[0][None],
        new_v[1][None],
        new_v[2][None],
    )


def solution(mesh):
    replicas, shards = mesh.shape["replica"], mesh.shape["shard"]
    split = Mesh(mesh.devices.reshape(replicas, shards // 4, 2, 2), ("replica", "z", "y", "core"))
    shard = ("z", "y", "core")
    return jax.shard_map(
        per_device,
        mesh=split,
        in_specs=(
            P("replica", shard, None, None),
            P("replica", shard, None, None),
            P("replica", shard, None),
            P("replica", None),
            P("replica", None),
            P("replica", None),
            P(),
        ),
        out_specs=(
            P("replica", shard, None, None),
            P("replica", shard, None),
            P("replica", None),
            P("replica", None),
            P("replica", None),
        ),
        check_vma=False,
    )
```

time: 167 us -> 131 us (0.78)
  waiting for transfers between devices: 73.1 us -> 51.9 us
  starting transfers between devices: 37.4 us -> 29.9 us
  Pallas kernels: 35.6 us -> 29.4 us
    ppermute x11 -> x14, waiting for transfers between devices: 35.9 us -> 17.8 us  [the longest x8 12 us: up(): return lax.ppermute(value, NODE, self.ahead)]
    ppermute x16 -> x10, starting transfers between devices: 15.3 us -> 7.18 us  [swap(): return lax.ppermute(value, axis, [(0, 1), (1, 0)])]
    ppermute x2, waiting for transfers between devices: 7.03 us -> 0.01 us  [from_peer(): return lax.ppermute(value, 'replica', moves[0])]
    ppermute x16 -> x10, waiting for transfers between devices: 26 us -> 32.6 us  [swap(): return lax.ppermute(value, axis, [(0, 1), (1, 0)])]
    pallas_call x3 -> x5, Pallas kernels: 35.6 us -> 29.4 us  [the longest x1 9.05 us: per_device(): call(partial(back_kernel, cols, 0, count), jax.ShapeDtypeStruct((2, chans...]
    squeeze x4 -> x0, local copies, waits for them, and re-layouts: 4.03 us -> none  [the longest x1 2.64 us: reduce_all(): slots = [add(keep[j], swap(send[j], 'replica')) for j in range(4)]]
    unnamed x34 -> x26, local copies, waits for them, and re-layouts: 1.75 us -> 4.31 us
    reduce_sum x2 -> x1, other arithmetic: 4.25 us -> 1.94 us  [per_device(): vectors = jnp.concatenate([jnp.sum(cotan, axis=(0, 1))[None], sums])]
  transfers between devices with their start and end apart: 33 -> 30, of which waited for: 14 -> 10; matrix products, arithmetic and copies ran while one was open for 8% -> 7% of each run, Pallas kernels for 21% -> 18%
where the time goes in v3:
time: 131 us; the launch traced here: 130 us
  waiting for transfers between devices  51.9 us (40%)
  starting transfers between devices  29.9 us (23%)
  Pallas kernels  29.4 us (22%)
  other arithmetic  11.2 us (9%)
  local copies, waits for them, and re-layouts  6.03 us (5%)
  between operations  1.61 us (1%)
    ppermute x10, waiting for transfers between devices, swap(): return lax.ppermute(value, axis, [(0, 1), (1, 0)])  32.6 us
    ppermute x8, starting transfers between devices, up(): return lax.ppermute(value, NODE, self.ahead)  12.9 us
    ppermute x8, waiting for transfers between devices, up(): return lax.ppermute(value, NODE, self.ahead)  12 us
    pallas_call x1, Pallas kernels, per_device(): call(partial(back_kernel, cols, 0, count), jax.ShapeDtypeStruct((2, chans...  9.05 us
    pallas_call x1, Pallas kernels, per_device(): call(partial(conv_kernel, cols, 0, count), (jax.ShapeDtypeStruct((cells,...  8.04 us
    ppermute x10, starting transfers between devices, swap(): return lax.ppermute(value, axis, [(0, 1), (1, 0)])  7.18 us
    ppermute x6, waiting for transfers between devices, down(): return lax.ppermute(value, NODE, self.behind)  5.83 us
    pallas_call x1, Pallas kernels, per_device(): call(partial(grad_kernel, cols), [jax.ShapeDtypeStruct((2 * part, cols.le...  5.62 us
  transfers between devices with their start and end apart: 30, of which 10 were waited for; matrix products, arithmetic and copies ran while one was open for 7% of the time, Pallas kernels for 18%

profile of v3, /device:TPU:0, one launch (start us, length us, event | category | flops | bytes accessed | tf_op | source)
XLA Modules:
  0.0 130.0 jit_solution(11909488854636181812)
XLA Ops:
  0.6 2.1 %bitcast_convert_fusion = bf16[40,5760]{1,0:T(8,128)(2,1)} fusion(f32[1,40,5760]{2,1,0:T(8,128)} %param.10), kind=kLoop, calls=%fused_computation.7 | loop fusion | flops 230400 | bytes 1382400 | tf_op jit(solution)/shard_map/convert_element_type | solution.py:309
  2.7 1.1 constant_dynamic-slice_fusion.1
  3.8 0.5 collective-permute-start
  4.5 1.9 %fusion.6 = (f32[640]{0:T(1024)S(1)}, bf16[16,32,640]{2,1,0:T(8,128)(2,1)S(1)}) fusion(f32[1,16,32,640]{3,2,1,0:T(8,128)} %param.9), kind=kLoop, calls=%fused_computation.30 | loop fusion | flops 654720 | bytes 1968640 | tf_op jit(solution)/shard_map/reduce_sum | solution.py:422
  6.4 0.5 collective-permute-start.4
  6.9 1.2 maximum_select_fusion.refs_0_
  8.1 2.7 %collective-permute-start.1 = (bf16[80,2944]{1,0:T(8,128)(2,1)S(1)}, bf16[80,2944]{1,0:T(8,128)(2,1)}, u32[]{:S(2)}, u32[]{:S(2)}) collective-permute-start(bf16[80,2944]{1,0:T(8,128)(2,1)S(1)} %maximum_select_fusion.refs_0_), channel_id=1, source_target_pairs={{0,4},{4,8},{8,12},{12,14},{14,10},{10,6},{6,2},{2,0},{1,5},{5,9},... | collective-permute-start | bytes 1413128 | tf_op jit(solution)/shard_map/ppermute | solution.py:260
  10.8 4.4 %shard_map.119 = (f32[2,640]{1,0:T(2,128)S(1)}, bf16[3,34,32,640]{3,2,1,0:T(8,128)(2,1)S(1)}, bf16[640,1024]{1,0:T(8,128)(2,1)S(1)}) custom-call(s32[1]{0:T(128)} %bitcast.dev, s32[32,24]{1,0:T(8,128)S(1)} %copy-done.7, bf16[16,32,640]{2,1,0:T(8,128)(2,1)S(1)} %bitcast.21, bf16[16,32,640]{2,1,0:T(8,128)(2,1)S(1)} %collective-permute-done.3.lat_far, ...), custom_call_target="tpu_custom_call" | custom-call | flops 3858759680 | bytes 8388608 | tf_op jit(solution)/shard_map/pallas_call | solution.py:341
  15.2 7.0 %collective-permute-done.1.refs_1_ = bf16[80,2944]{1,0:T(8,128)(2,1)} collective-permute-done((bf16[80,2944]{1,0:T(8,128)(2,1)S(1)}, bf16[80,2944]{1,0:T(8,128)(2,1)}, u32[]{:S(2)}, u32[]{:S(2)}) %collective-permute-start.1) | collective-permute-done | bytes 471072 | tf_op jit(solution)/shard_map/ppermute | solution.py:260
  22.2 1.5 %collective-permute-done.2.refs_2_ = bf16[80,2944]{1,0:T(8,128)(2,1)} collective-permute-done((bf16[80,2944]{1,0:T(8,128)(2,1)S(1)}, bf16[80,2944]{1,0:T(8,128)(2,1)}, u32[]{:S(2)}, u32[]{:S(2)}) %collective-permute-start.2) | collective-permute-done | bytes 471072 | tf_op jit(solution)/shard_map/ppermute | solution.py:263
  23.7 5.6 %shard_map.121 = (bf16[80,2944]{1,0:T(8,128)(2,1)S(1)}, bf16[80,2944]{1,0:T(8,128)(2,1)S(1)}, bf16[80,2944]{1,0:T(8,128)(2,1)S(1)}, bf16[80,2944]{1,0:T(8,128)(2...) custom-call(s32[1]{0:T(128)} %bitcast.dev, ...), custom_call_target="tpu_custom_call" | custom-call | flops 7717519360 | bytes 8388608 | tf_op jit(solution)/shard_map/pallas_call | solution.py:352
  29.4 1.6 %collective-permute-start.15 = (bf16[80,2944]{1,0:T(8,128)(2,1)S(1)}, bf16[80,2944]{1,0:T(8,128)(2,1)S(1)}, u32[]{:S(2)}, u32[]{:S(2)}) collective-permute-start(bf16[80,2944]{1,0:T(8,128)(2,1)S(1)} %get-tuple-element.38), channel_id=1, source_target_pairs={{0,16},{16,0},{1,17},{17,1},{2,18},{18,2},{3,19},{19,3},{4,20},{20... | collective-permute-start | bytes 1413128 | tf_op jit(solution)/shard_map/ppermute | solution.py:235
  30.9 2.3 %shard_map.122 = (bf16[3,34,32,640]{3,2,1,0:T(8,128)(2,1)S(1)}, bf16[32,32,640]{2,1,0:T(8,128)(2,1)S(1)}, bf16[32,32,640]{2,1,0:T(8,128)(2,1)S(1)}) custom-call(s32[1]{0:T(128)} %bitcast.dev, f32[2,640]{1,0:T(2,128)S(1)} %get-tuple-element.39.stats, f32[1,640]{1,0:T(1,128)S(1)} %copy-done.1, f32[1,640]{1,0:T(1,128)S(1)} %copy-done.2, ...), custom_call_target="tpu_custom_call" | custom-call | flops 3858759680 | bytes 8388608 | tf_op jit(solution)/shard_map/pallas_call | solution.py:359
  33.2 1.6 %collective-permute-start.5 = (bf16[80,2944]{1,0:T(8,128)(2,1)}, bf16[80,2944]{1,0:T(8,128)(2,1)S(1)}, u32[]{:S(2)}, u32[]{:S(2)}) collective-permute-start(bf16[80,2944]{1,0:T(8,128)(2,1)} %collective-permute-done.1.refs_1_), channel_id=1, source_target_pairs={{0,4},{4,8},{8,12},{12,14},{14,10},{10,6},{6,2},{2,0},{1,5},{5,9},... | collective-permute-start | bytes 1413128 | tf_op jit(solution)/shard_map/ppermute | solution.py:260
  34.8 0.4 collective-permute-start.6
  35.3 0.5 collective-permute-start.14
  35.8 1.5 %collective-permute-start.13 = (bf16[80,2944]{1,0:T(8,128)(2,1)S(1)}, bf16[80,2944]{1,0:T(8,128)(2,1)S(1)}, u32[]{:S(2)}, u32[]{:S(2)}) collective-permute-start(bf16[80,2944]{1,0:T(8,128)(2,1)S(1)} %get-tuple-element.34), channel_id=1, source_target_pairs={{0,16},{16,0},{1,17},{17,1},{2,18},{18,2},{3,19},{19,3},{4,20},{20... | collective-permute-start | bytes 1413128 | tf_op jit(solution)/shard_map/ppermute | solution.py:235
  37.3 5.8 %collective-permute-done.15 = bf16[80,2944]{1,0:T(8,128)(2,1)S(1)} collective-permute-done((bf16[80,2944]{1,0:T(8,128)(2,1)S(1)}, bf16[80,2944]{1,0:T(8,128)(2,1)S(1)}, u32[]{:S(2)}, u32[]{:S(2)}) %collective-permute-start.15) | collective-permute-done | bytes 471072 | tf_op jit(solution)/shard_map/ppermute | solution.py:235
  43.1 1.5 %collective-permute-start.12 = (bf16[80,2944]{1,0:T(8,128)(2,1)S(1)}, bf16[80,2944]{1,0:T(8,128)(2,1)S(1)}, u32[]{:S(2)}, u32[]{:S(2)}) collective-permute-start(bf16[80,2944]{1,0:T(8,128)(2,1)S(1)} %get-tuple-element.32), channel_id=1, source_target_pairs={{0,16},{16,0},{1,17},{17,1},{2,18},{18,2},{3,19},{19,3},{4,20},{20... | collective-permute-start | bytes 1413128 | tf_op jit(solution)/shard_map/ppermute | solution.py:235
  44.8 8.4 %collective-permute-done.14 = bf16[80,2944]{1,0:T(8,128)(2,1)S(1)} collective-permute-done((bf16[80,2944]{1,0:T(8,128)(2,1)S(1)}, bf16[80,2944]{1,0:T(8,128)(2,1)S(1)}, u32[]{:S(2)}, u32[]{:S(2)}) %collective-permute-start.14) | collective-permute-done | bytes 471072 | tf_op jit(solution)/shard_map/ppermute | solution.py:235
  53.6 1.8 %collective-permute-start.19 = (bf16[40,2944]{1,0:T(8,128)(2,1)S(1)}, bf16[40,2944]{1,0:T(8,128)(2,1)S(1)}, u32[]{:S(2)}, u32[]{:S(2)}) collective-permute-start(bf16[40,2944]{1,0:T(8,128)(2,1)S(1)} %get-tuple-element.50), channel_id=1, source_target_pairs={{0,4},{4,8},{8,12},{12,14},{14,10},{10,6},{6,2},{2,0},{1,5},{5,9},... | collective-permute-start | bytes 706568 | tf_op jit(solution)/shard_map/ppermute | solution.py:260
  55.5 1.6 %collective-permute-start.7 = (bf16[80,2944]{1,0:T(8,128)(2,1)S(1)}, bf16[80,2944]{1,0:T(8,128)(2,1)S(1)}, u32[]{:S(2)}, u32[]{:S(2)}) collective-permute-start(bf16[80,2944]{1,0:T(8,128)(2,1)S(1)} %collective-permute-done.5.refs_3_), channel_id=1, source_target_pairs={{0,4},{4,8},{8,12},{12,14},{14,10},{10,6},{6,2},{2,0},{1,5},{5,9},... | collective-permute-start | bytes 1413128 | tf_op jit(solution)/shard_map/ppermute | solution.py:260
  57.0 6.3 %collective-permute-done.13 = bf16[80,2944]{1,0:T(8,128)(2,1)S(1)} collective-permute-done((bf16[80,2944]{1,0:T(8,128)(2,1)S(1)}, bf16[80,2944]{1,0:T(8,128)(2,1)S(1)}, u32[]{:S(2)}, u32[]{:S(2)}) %collective-permute-start.13) | collective-permute-done | bytes 471072 | tf_op jit(solution)/shard_map/ppermute | solution.py:235
  63.9 1.8 %collective-permute-start.17 = (bf16[40,2944]{1,0:T(8,128)(2,1)S(1)}, bf16[40,2944]{1,0:T(8,128)(2,1)S(1)}, u32[]{:S(2)}, u32[]{:S(2)}) collective-permute-start(bf16[40,2944]{1,0:T(8,128)(2,1)S(1)} %get-tuple-element.47), channel_id=1, source_target_pairs={{4,0},{8,4},{12,8},{14,12},{10,14},{6,10},{2,6},{0,2},{5,1},{9,5},... | collective-permute-start | bytes 706568 | tf_op jit(solution)/shard_map/ppermute | solution.py:263
  65.9 5.8 %collective-permute-done.12 = bf16[80,2944]{1,0:T(8,128)(2,1)S(1)} collective-permute-done((bf16[80,2944]{1,0:T(8,128)(2,1)S(1)}, bf16[80,2944]{1,0:T(8,128)(2,1)S(1)}, u32[]{:S(2)}, u32[]{:S(2)}) %collective-permute-start.12) | collective-permute-done | bytes 471072 | tf_op jit(solution)/shard_map/ppermute | solution.py:235
  71.9 1.6 %collective-permute-start.9 = (bf16[80,2944]{1,0:T(8,128)(2,1)S(1)}, bf16[80,2944]{1,0:T(8,128)(2,1)S(1)}, u32[]{:S(2)}, u32[]{:S(2)}) collective-permute-start(bf16[80,2944]{1,0:T(8,128)(2,1)S(1)} %collective-permute-done.7.refs_5_), channel_id=1, source_target_pairs={{0,4},{4,8},{8,12},{12,14},{14,10},{10,6},{6,2},{2,0},{1,5},{5,9},... | collective-permute-start | bytes 1413128 | tf_op jit(solution)/shard_map/ppermute | solution.py:260
  73.5 4.3 %collective-permute-done.17 = bf16[40,2944]{1,0:T(8,128)(2,1)S(1)} collective-permute-done((bf16[40,2944]{1,0:T(8,128)(2,1)S(1)}, bf16[40,2944]{1,0:T(8,128)(2,1)S(1)}, u32[]{:S(2)}, u32[]{:S(2)}) %collective-permute-start.17) | collective-permute-done | bytes 235552 | tf_op jit(solution)/shard_map/ppermute | solution.py:263
  77.8 0.8 add_convert_fusion.9
  78.6 1.6 %collective-permute-start.21 = (bf16[40,2944]{1,0:T(8,128)(2,1)S(1)}, bf16[40,2944]{1,0:T(8,128)(2,1)S(1)}, u32[]{:S(2)}, u32[]{:S(2)}) collective-permute-start(bf16[40,2944]{1,0:T(8,128)(2,1)S(1)} %get-tuple-element.46), channel_id=1, source_target_pairs={{0,4},{4,8},{8,12},{12,14},{14,10},{10,6},{6,2},{2,0},{1,5},{5,9},... | collective-permute-start | bytes 706568 | tf_op jit(solution)/shard_map/ppermute | solution.py:260
  80.7 5.0 %collective-permute-done.9.refs_7_ = bf16[80,2944]{1,0:T(8,128)(2,1)S(1)} collective-permute-done((bf16[80,2944]{1,0:T(8,128)(2,1)S(1)}, bf16[80,2944]{1,0:T(8,128)(2,1)S(1)}, u32[]{:S(2)}, u32[]{:S(2)}) %collective-permute-start.9) | collective-permute-done | bytes 471072 | tf_op jit(solution)/shard_map/ppermute | solution.py:260
  85.7 9.0 %shard_map.123 = f32[2,640]{1,0:T(2,128)S(1)} custom-call(s32[1]{0:T(128)} %bitcast.dev, s32[32,24]{1,0:T(8,128)S(1)} %copy-done.7, bf16[3,34,32,640]{3,2,1,0:T(8,128)(2,1)S(1)} %get-tuple-element.40.cots, bf16[32,32,640]{2,1,0:T(8,128)(2,1)S(1)} %get-tuple-element.41.slope, bf16[32,32,640]{2,1,0:T(8,128)(2,1)S(1)} %get-tuple-element.42.slope_x, ...), custom_call_target="tpu_custom_call" | custom-call | flops 7717519360 | bytes 8388608 | tf_op jit(solution)/shard_map/pallas_call | solution.py:407
  94.9 1.7 %collective-permute-start.22 = (bf16[40,2944]{1,0:T(8,128)(2,1)S(1)}, bf16[40,2944]{1,0:T(8,128)(2,1)S(1)}, u32[]{:S(2)}, u32[]{:S(2)}) collective-permute-start(bf16[40,2944]{1,0:T(8,128)(2,1)S(1)} %add_convert_fusion.5), channel_id=1, source_target_pairs={{0,4},{4,8},{8,12},{12,14},{14,10},{10,6},{6,2},{2,0},{1,5},{5,9},... | collective-permute-start | bytes 706568 | tf_op jit(solution)/shard_map/ppermute | solution.py:260
  96.6 0.5 collective-permute-start.26
  97.1 6.2 %collective-permute-done.26 = f32[3,640]{1,0:T(4,128)S(1)} collective-permute-done((f32[3,640]{1,0:T(4,128)S(1)}, f32[3,640]{1,0:T(4,128)S(1)}, u32[]{:S(2)}, u32[]{:S(2)}) %collective-permute-start.26) | collective-permute-done | bytes 7712 | tf_op jit(solution)/shard_map/ppermute | solution.py:235
  103.3 1.6 %collective-permute-start.11 = (bf16[40,5760]{1,0:T(8,128)(2,1)}, bf16[40,5760]{1,0:T(8,128)(2,1)}, u32[]{:S(2)}, u32[]{:S(2)}) collective-permute-start(bf16[40,5760]{1,0:T(8,128)(2,1)} %bitcast_convert_fusion), channel_id=1, source_target_pairs={{0,16},{16,0},{1,17},{17,1},{2,18},{18,2},{3,19},{19,3},{4,20},{20... | collective-permute-start | bytes 1382408 | tf_op jit(solution)/shard_map/ppermute | solution.py:243
  105.6 1.4 %collective-permute-done.27 = f32[3,640]{1,0:T(4,128)S(1)} collective-permute-done((f32[3,640]{1,0:T(4,128)S(1)}, f32[3,640]{1,0:T(4,128)S(1)}, u32[]{:S(2)}, u32[]{:S(2)}) %collective-permute-start.27) | collective-permute-done | bytes 7712 | tf_op jit(solution)/shard_map/ppermute | solution.py:427
  107.0 0.8 collective-permute-start.28
  107.8 1.0 add_convert_fusion.4
  108.9 0.9 collective-permute-start.24
  109.7 2.1 %collective-permute-start.23 = (bf16[40,2944]{1,0:T(8,128)(2,1)S(1)}, bf16[40,2944]{1,0:T(8,128)(2,1)S(1)}, u32[]{:S(2)}, u32[]{:S(2)}) collective-permute-start(bf16[40,2944]{1,0:T(8,128)(2,1)S(1)} %add_convert_fusion.4), channel_id=1, source_target_pairs={{1,0},{16,17},{0,16},{17,1},{3,2},{18,19},{2,18},{19,3},{5,4},{20,... | collective-permute-start | bytes 706568 | tf_op jit(solution)/shard_map/ppermute | solution.py:386
  111.9 1.3 collective-permute-start.29
  113.2 1.0 copy-done.4
  114.2 1.0 copy-done.6
  115.2 2.2 %copy-done.9 = bf16[3,34,32,640]{3,2,1,0:T(8,128)(2,1)S(1)} copy-done((bf16[3,34,32,640]{3,2,1,0:T(8,128)(2,1)S(1)}, bf16[3,34,32,640]{3,2,1,0:T(8,128)(2,1)}, u32[]{:S(2)}) %copy-start.9) | copy-done | bytes 4177944
  117.4 8.0 %shard_map.120 = (f32[512,640]{1,0:T(8,128)S(1)}, bf16[512,640]{1,0:T(8,128)(2,1)S(1)}) custom-call(s32[1]{0:T(128)} %bitcast.dev, s32[32,24]{1,0:T(8,128)S(1)} %copy-done.7, bf16[3,34,32,640]{3,2,1,0:T(8,128)(2,1)S(1)} %copy-done.9, bf16[80,2944]{1,0:T(8,128)(2,1)S(1)} %maximum_select_fusion.refs_0_, bf16[80,2944]{1,0:T(8,128)(2,1)} %collective-permute-done.1.refs_1_, ...), custom_call_target="tpu_custom_call" | custom-call | flops 7717519360 | bytes 8388608 | tf_op jit(solution)/shard_map/pallas_call | solution.py:414
  125.9 0.6 fusion.8
  126.6 2.1 %fusion.3 = f32[1,40,5760]{2,1,0:T(8,128)} fusion(f32[1,40,5760]{2,1,0:T(8,128)S(1)} %copy-done.10, bf16[40,5760]{1,0:T(8,128)(2,1)} %collective-permute-done.11, bf16[40,2816]{1,0:T(8,128)(2,1)S(1)} %fusion.4, bf16[40,2944]{1,0:T(8,128)(2,1)S(1)} %select_select_fusion, f32[]{:T(128)S(6)} %mul_shard_map.4), kind=kLoop, calls=%fused_computation.10 | loop fusion | flops 2073600 | bytes 2764804 | tf_op jit(solution)/shard_map/broadcast_in_dim | solution.py:436
  128.8 1.2 fusion
  (69 shorter events, 2.9 us)
Async XLA Ops:
  0.6 3.7 %copy-start = (bf16[1,16,32,640]{3,2,1,0:T(8,128)(2,1)S(1)}, bf16[1,16,32,640]{3,2,1,0:T(8,128)(2,1)}, u32[]{:S(2)}) copy-start(bf16[1,16,32,640]{3,2,1,0:T(8,128)(2,1)} %param.8) | copy-start | bytes 1966084
  3.8 3.1 %collective-permute-start = (bf16[40,2944]{1,0:T(8,128)(2,1)S(1)}, bf16[40,2944]{1,0:T(8,128)(2,1)}, u32[]{:S(2)}, u32[]{:S(2)}) collective-permute-start(bf16[40,2944]{1,0:T(8,128)(2,1)S(1)} %get-tuple-element.52), channel_id=1, source_target_pairs={{0,1},{1,0},{2,3},{3,2},{4,5},{5,4},{6,7},{7,6},{8,9},{9,8},{10,11... | collective-permute-start | bytes 706568 | tf_op jit(solution)/shard_map/ppermute | solution.py:235
  4.3 6.4 %copy-start.1 = (f32[1,640]{1,0:T(1,128)S(1)}, f32[1,640]{1,0:T(1,128)}, u32[]{:S(2)}) copy-start(f32[1,640]{1,0:T(1,128)} %gain.3) | copy-start | bytes 7684
  4.3 6.4 %copy-start.2 = (f32[1,640]{1,0:T(1,128)S(1)}, f32[1,640]{1,0:T(1,128)}, u32[]{:S(2)}) copy-start(f32[1,640]{1,0:T(1,128)} %shift.3) | copy-start | bytes 7684
  4.3 6.5 %copy-start.7 = (s32[32,24]{1,0:T(8,128)S(1)}, s32[32,24]{1,0:T(8,128)}, u32[]{:S(2)}) copy-start(s32[32,24]{1,0:T(8,128)} %constant.58.clone.table) | copy-start | bytes 9220
  4.3 6.4 %collective-permute-start.3 = (bf16[16,32,640]{2,1,0:T(8,128)(2,1)S(1)}, bf16[16,32,640]{2,1,0:T(8,128)(2,1)S(1)}, u32[]{:S(2)}, u32[]{:S(2)}) collective-permute-start(bf16[16,32,640]{2,1,0:T(8,128)(2,1)S(1)} %bitcast.20), channel_id=1, source_target_pairs={{0,1},{1,0},{2,3},{3,2},{4,5},{5,4},{6,7},{7,6},{8,9},{9,8},{10,11... | collective-permute-start | bytes 1966088 | tf_op jit(solution)/shard_map/ppermute | solution.py:235
  6.4 4.4 %collective-permute-start.4 = (bf16[16,32,640]{2,1,0:T(8,128)(2,1)S(1)}, bf16[16,32,640]{2,1,0:T(8,128)(2,1)S(1)}, u32[]{:S(2)}, u32[]{:S(2)}) collective-permute-start(bf16[16,32,640]{2,1,0:T(8,128)(2,1)S(1)} %get-tuple-element.44.cot_own), channel_id=1, source_target_pairs={{0,1},{1,0},{2,3},{3,2},{4,5},{5,4},{6,7},{7,6},{8,9},{9,8},{10,11... | collective-permute-start | bytes 1966088 | tf_op jit(solution)/shard_map/ppermute | solution.py:235
  8.1 14.1 %collective-permute-start.1 = (bf16[80,2944]{1,0:T(8,128)(2,1)S(1)}, bf16[80,2944]{1,0:T(8,128)(2,1)}, u32[]{:S(2)}, u32[]{:S(2)}) collective-permute-start(bf16[80,2944]{1,0:T(8,128)(2,1)S(1)} %maximum_select_fusion.refs_0_), channel_id=1, source_target_pairs={{0,4},{4,8},{8,12},{12,14},{14,10},{10,6},{6,2},{2,0},{1,5},{5,9},... | collective-permute-start | bytes 1413128 | tf_op jit(solution)/shard_map/ppermute | solution.py:260
  10.7 13.0 %collective-permute-start.2 = (bf16[80,2944]{1,0:T(8,128)(2,1)S(1)}, bf16[80,2944]{1,0:T(8,128)(2,1)}, u32[]{:S(2)}, u32[]{:S(2)}) collective-permute-start(bf16[80,2944]{1,0:T(8,128)(2,1)S(1)} %maximum_select_fusion.refs_0_), channel_id=1, source_target_pairs={{4,0},{8,4},{12,8},{14,12},{10,14},{6,10},{2,6},{0,2},{5,1},{9,5},... | collective-permute-start | bytes 1413128 | tf_op jit(solution)/shard_map/ppermute | solution.py:263
  15.2 14.2 %copy-start.8 = (bf16[3,34,32,640]{3,2,1,0:T(8,128)(2,1)}, bf16[3,34,32,640]{3,2,1,0:T(8,128)(2,1)S(1)}, u32[]{:S(2)}) copy-start(bf16[3,34,32,640]{3,2,1,0:T(8,128)(2,1)S(1)} %get-tuple-element.25.acts) | copy-start | bytes 12533764
  29.4 13.8 %collective-permute-start.15 = (bf16[80,2944]{1,0:T(8,128)(2,1)S(1)}, bf16[80,2944]{1,0:T(8,128)(2,1)S(1)}, u32[]{:S(2)}, u32[]{:S(2)}) collective-permute-start(bf16[80,2944]{1,0:T(8,128)(2,1)S(1)} %get-tuple-element.38), channel_id=1, source_target_pairs={{0,16},{16,0},{1,17},{17,1},{2,18},{18,2},{3,19},{19,3},{4,20},{20... | collective-permute-start | bytes 1413128 | tf_op jit(solution)/shard_map/ppermute | solution.py:235
  33.2 20.4 %collective-permute-start.5 = (bf16[80,2944]{1,0:T(8,128)(2,1)}, bf16[80,2944]{1,0:T(8,128)(2,1)S(1)}, u32[]{:S(2)}, u32[]{:S(2)}) collective-permute-start(bf16[80,2944]{1,0:T(8,128)(2,1)} %collective-permute-done.1.refs_1_), channel_id=1, source_target_pairs={{0,4},{4,8},{8,12},{12,14},{14,10},{10,6},{6,2},{2,0},{1,5},{5,9},... | collective-permute-start | bytes 1413128 | tf_op jit(solution)/shard_map/ppermute | solution.py:260
  34.8 20.6 %collective-permute-start.6 = (bf16[80,2944]{1,0:T(8,128)(2,1)}, bf16[80,2944]{1,0:T(8,128)(2,1)S(1)}, u32[]{:S(2)}, u32[]{:S(2)}) collective-permute-start(bf16[80,2944]{1,0:T(8,128)(2,1)} %collective-permute-done.2.refs_2_), channel_id=1, source_target_pairs={{4,0},{8,4},{12,8},{14,12},{10,14},{6,10},{2,6},{0,2},{5,1},{9,5},... | collective-permute-start | bytes 1413128 | tf_op jit(solution)/shard_map/ppermute | solution.py:263
  35.3 18.0 %collective-permute-start.14 = (bf16[80,2944]{1,0:T(8,128)(2,1)S(1)}, bf16[80,2944]{1,0:T(8,128)(2,1)S(1)}, u32[]{:S(2)}, u32[]{:S(2)}) collective-permute-start(bf16[80,2944]{1,0:T(8,128)(2,1)S(1)} %get-tuple-element.36), channel_id=1, source_target_pairs={{0,16},{16,0},{1,17},{17,1},{2,18},{18,2},{3,19},{19,3},{4,20},{20... | collective-permute-start | bytes 1413128 | tf_op jit(solution)/shard_map/ppermute | solution.py:235
  35.8 27.5 %collective-permute-start.13 = (bf16[80,2944]{1,0:T(8,128)(2,1)S(1)}, bf16[80,2944]{1,0:T(8,128)(2,1)S(1)}, u32[]{:S(2)}, u32[]{:S(2)}) collective-permute-start(bf16[80,2944]{1,0:T(8,128)(2,1)S(1)} %get-tuple-element.34), channel_id=1, source_target_pairs={{0,16},{16,0},{1,17},{17,1},{2,18},{18,2},{3,19},{19,3},{4,20},{20... | collective-permute-start | bytes 1413128 | tf_op jit(solution)/shard_map/ppermute | solution.py:235
  43.1 28.6 %collective-permute-start.12 = (bf16[80,2944]{1,0:T(8,128)(2,1)S(1)}, bf16[80,2944]{1,0:T(8,128)(2,1)S(1)}, u32[]{:S(2)}, u32[]{:S(2)}) collective-permute-start(bf16[80,2944]{1,0:T(8,128)(2,1)S(1)} %get-tuple-element.32), channel_id=1, source_target_pairs={{0,16},{16,0},{1,17},{17,1},{2,18},{18,2},{3,19},{19,3},{4,20},{20... | collective-permute-start | bytes 1413128 | tf_op jit(solution)/shard_map/ppermute | solution.py:235
  53.2 10.5 %collective-permute-start.16 = (bf16[40,2944]{1,0:T(8,128)(2,1)S(1)}, bf16[40,2944]{1,0:T(8,128)(2,1)S(1)}, u32[]{:S(2)}, u32[]{:S(2)}) collective-permute-start(bf16[40,2944]{1,0:T(8,128)(2,1)S(1)} %get-tuple-element.49), channel_id=1, source_target_pairs={{4,0},{8,4},{12,8},{14,12},{10,14},{6,10},{2,6},{0,2},{5,1},{9,5},... | collective-permute-start | bytes 706568 | tf_op jit(solution)/shard_map/ppermute | solution.py:263
  53.6 10.1 %collective-permute-start.19 = (bf16[40,2944]{1,0:T(8,128)(2,1)S(1)}, bf16[40,2944]{1,0:T(8,128)(2,1)S(1)}, u32[]{:S(2)}, u32[]{:S(2)}) collective-permute-start(bf16[40,2944]{1,0:T(8,128)(2,1)S(1)} %get-tuple-element.50), channel_id=1, source_target_pairs={{0,4},{4,8},{8,12},{12,14},{14,10},{10,6},{6,2},{2,0},{1,5},{5,9},... | collective-permute-start | bytes 706568 | tf_op jit(solution)/shard_map/ppermute | solution.py:260
  55.5 16.4 %collective-permute-start.7 = (bf16[80,2944]{1,0:T(8,128)(2,1)S(1)}, bf16[80,2944]{1,0:T(8,128)(2,1)S(1)}, u32[]{:S(2)}, u32[]{:S(2)}) collective-permute-start(bf16[80,2944]{1,0:T(8,128)(2,1)S(1)} %collective-permute-done.5.refs_3_), channel_id=1, source_target_pairs={{0,4},{4,8},{8,12},{12,14},{14,10},{10,6},{6,2},{2,0},{1,5},{5,9},... | collective-permute-start | bytes 1413128 | tf_op jit(solution)/shard_map/ppermute | solution.py:260
  63.3 17.3 %collective-permute-start.8 = (bf16[80,2944]{1,0:T(8,128)(2,1)S(1)}, bf16[80,2944]{1,0:T(8,128)(2,1)S(1)}, u32[]{:S(2)}, u32[]{:S(2)}) collective-permute-start(bf16[80,2944]{1,0:T(8,128)(2,1)S(1)} %collective-permute-done.6.refs_4_), channel_id=1, source_target_pairs={{4,0},{8,4},{12,8},{14,12},{10,14},{6,10},{2,6},{0,2},{5,1},{9,5},... | collective-permute-start | bytes 1413128 | tf_op jit(solution)/shard_map/ppermute | solution.py:263
  63.9 14.0 %collective-permute-start.17 = (bf16[40,2944]{1,0:T(8,128)(2,1)S(1)}, bf16[40,2944]{1,0:T(8,128)(2,1)S(1)}, u32[]{:S(2)}, u32[]{:S(2)}) collective-permute-start(bf16[40,2944]{1,0:T(8,128)(2,1)S(1)} %get-tuple-element.47), channel_id=1, source_target_pairs={{4,0},{8,4},{12,8},{14,12},{10,14},{6,10},{2,6},{0,2},{5,1},{9,5},... | collective-permute-start | bytes 706568 | tf_op jit(solution)/shard_map/ppermute | solution.py:263
  65.6 12.2 %collective-permute-start.20 = (bf16[40,2944]{1,0:T(8,128)(2,1)S(1)}, bf16[40,2944]{1,0:T(8,128)(2,1)S(1)}, u32[]{:S(2)}, u32[]{:S(2)}) collective-permute-start(bf16[40,2944]{1,0:T(8,128)(2,1)S(1)} %get-tuple-element.48), channel_id=1, source_target_pairs={{0,4},{4,8},{8,12},{12,14},{14,10},{10,6},{6,2},{2,0},{1,5},{5,9},... | collective-permute-start | bytes 706568 | tf_op jit(solution)/shard_map/ppermute | solution.py:260
  71.9 23.0 %copy-start.11 = (bf16[80,2944]{1,0:T(8,128)(2,1)}, bf16[80,2944]{1,0:T(8,128)(2,1)S(1)}, u32[]{:S(2)}) copy-start(bf16[80,2944]{1,0:T(8,128)(2,1)S(1)} %add_convert_fusion.3) | copy-start | bytes 1413124
  71.9 13.8 %collective-permute-start.9 = (bf16[80,2944]{1,0:T(8,128)(2,1)S(1)}, bf16[80,2944]{1,0:T(8,128)(2,1)S(1)}, u32[]{:S(2)}, u32[]{:S(2)}) collective-permute-start(bf16[80,2944]{1,0:T(8,128)(2,1)S(1)} %collective-permute-done.7.refs_5_), channel_id=1, source_target_pairs={{0,4},{4,8},{8,12},{12,14},{14,10},{10,6},{6,2},{2,0},{1,5},{5,9},... | collective-permute-start | bytes 1413128 | tf_op jit(solution)/shard_map/ppermute | solution.py:260
  78.6 16.2 %collective-permute-start.21 = (bf16[40,2944]{1,0:T(8,128)(2,1)S(1)}, bf16[40,2944]{1,0:T(8,128)(2,1)S(1)}, u32[]{:S(2)}, u32[]{:S(2)}) collective-permute-start(bf16[40,2944]{1,0:T(8,128)(2,1)S(1)} %get-tuple-element.46), channel_id=1, source_target_pairs={{0,4},{4,8},{8,12},{12,14},{14,10},{10,6},{6,2},{2,0},{1,5},{5,9},... | collective-permute-start | bytes 706568 | tf_op jit(solution)/shard_map/ppermute | solution.py:260
  80.2 27.6 %collective-permute-start.18 = (bf16[40,2944]{1,0:T(8,128)(2,1)}, bf16[40,2944]{1,0:T(8,128)(2,1)S(1)}, u32[]{:S(2)}, u32[]{:S(2)}) collective-permute-start(bf16[40,2944]{1,0:T(8,128)(2,1)} %get-tuple-element.45), channel_id=1, source_target_pairs={{4,0},{8,4},{12,8},{14,12},{10,14},{6,10},{2,6},{0,2},{5,1},{9,5},... | collective-permute-start | bytes 706568 | tf_op jit(solution)/shard_map/ppermute | solution.py:263
  80.7 14.1 %copy-start.3 = (bf16[80,2944]{1,0:T(8,128)(2,1)}, bf16[80,2944]{1,0:T(8,128)(2,1)S(1)}, u32[]{:S(2)}) copy-start(bf16[80,2944]{1,0:T(8,128)(2,1)S(1)} %collective-permute-done.8.refs_6_) | copy-start | bytes 1413124
  85.7 9.1 %copy-start.5 = (bf16[80,2944]{1,0:T(8,128)(2,1)}, bf16[80,2944]{1,0:T(8,128)(2,1)S(1)}, u32[]{:S(2)}) copy-start(bf16[80,2944]{1,0:T(8,128)(2,1)S(1)} %collective-permute-done.9.refs_7_) | copy-start | bytes 1413124
  85.7 19.9 %copy-start.12 = (f32[1,640]{1,0:T(1,128)S(1)}, f32[1,640]{1,0:T(1,128)}, u32[]{:S(2)}) copy-start(f32[1,640]{1,0:T(1,128)} %param.11) | copy-start | bytes 7684
  94.8 1.8 %collective-permute-start.25 = (f32[3,640]{1,0:T(4,128)S(1)}, f32[3,640]{1,0:T(4,128)S(1)}, u32[]{:S(2)}, u32[]{:S(2)}) collective-permute-start(f32[3,640]{1,0:T(4,128)S(1)} %pad_maximum_fusion), channel_id=1, source_target_pairs={{0,1},{1,0},{2,3},{3,2},{4,5},{5,4},{6,7},{7,6},{8,9},{9,8},{10,11... | collective-permute-start | bytes 23048 | tf_op jit(solution)/shard_map/ppermute | solution.py:235
  94.9 12.9 %collective-permute-start.22 = (bf16[40,2944]{1,0:T(8,128)(2,1)S(1)}, bf16[40,2944]{1,0:T(8,128)(2,1)S(1)}, u32[]{:S(2)}, u32[]{:S(2)}) collective-permute-start(bf16[40,2944]{1,0:T(8,128)(2,1)S(1)} %add_convert_fusion.5), channel_id=1, source_target_pairs={{0,4},{4,8},{8,12},{12,14},{14,10},{10,6},{6,2},{2,0},{1,5},{5,9},... | collective-permute-start | bytes 706568 | tf_op jit(solution)/shard_map/ppermute | solution.py:260
  96.6 6.7 %collective-permute-start.26 = (f32[3,640]{1,0:T(4,128)S(1)}, f32[3,640]{1,0:T(4,128)S(1)}, u32[]{:S(2)}, u32[]{:S(2)}) collective-permute-start(f32[3,640]{1,0:T(4,128)S(1)} %fusion.5), channel_id=1, source_target_pairs={{0,2},{2,0},{1,3},{3,1},{4,6},{6,4},{5,7},{7,5},{8,10},{10,8},{9,1... | collective-permute-start | bytes 23048 | tf_op jit(solution)/shard_map/ppermute | solution.py:235
  103.3 3.7 %collective-permute-start.27 = (f32[3,640]{1,0:T(4,128)S(1)}, f32[3,640]{1,0:T(4,128)S(1)}, u32[]{:S(2)}, u32[]{:S(2)}) collective-permute-start(f32[3,640]{1,0:T(4,128)S(1)} %add.110), channel_id=1, source_target_pairs={{0,4},{4,0},{8,12},{12,8},{1,5},{5,1},{9,13},{13,9},{2,6},{6,2},{1... | collective-permute-start | bytes 23048 | tf_op jit(solution)/shard_map/ppermute | solution.py:427
  103.3 23.3 %collective-permute-start.11 = (bf16[40,5760]{1,0:T(8,128)(2,1)}, bf16[40,5760]{1,0:T(8,128)(2,1)}, u32[]{:S(2)}, u32[]{:S(2)}) collective-permute-start(bf16[40,5760]{1,0:T(8,128)(2,1)} %bitcast_convert_fusion), channel_id=1, source_target_pairs={{0,16},{16,0},{1,17},{17,1},{2,18},{18,2},{3,19},{19,3},{4,20},{20... | collective-permute-start | bytes 1382408 | tf_op jit(solution)/shard_map/ppermute | solution.py:243
  107.0 4.9 %collective-permute-start.28 = (f32[3,640]{1,0:T(4,128)S(1)}, f32[3,640]{1,0:T(4,128)S(1)}, u32[]{:S(2)}, u32[]{:S(2)}) collective-permute-start(f32[3,640]{1,0:T(4,128)S(1)} %add.111), channel_id=1, source_target_pairs={{0,8},{4,12},{8,0},{12,4},{1,9},{5,13},{9,1},{13,5},{2,10},{6,14},... | collective-permute-start | bytes 23048 | tf_op jit(solution)/shard_map/ppermute | solution.py:427
  108.9 17.6 %collective-permute-start.24 = (bf16[40,2944]{1,0:T(8,128)(2,1)S(1)}, bf16[40,2944]{1,0:T(8,128)(2,1)S(1)}, u32[]{:S(2)}, u32[]{:S(2)}) collective-permute-start(bf16[40,2944]{1,0:T(8,128)(2,1)S(1)} %add_convert_fusion.4), channel_id=1, source_target_pairs={{1,16},{16,1},{3,18},{18,3},{5,20},{20,5},{7,22},{22,7},{9,24},{24... | collective-permute-start | bytes 706568 | tf_op jit(solution)/shard_map/ppermute | solution.py:387
  109.7 16.7 %collective-permute-start.23 = (bf16[40,2944]{1,0:T(8,128)(2,1)S(1)}, bf16[40,2944]{1,0:T(8,128)(2,1)S(1)}, u32[]{:S(2)}, u32[]{:S(2)}) collective-permute-start(bf16[40,2944]{1,0:T(8,128)(2,1)S(1)} %add_convert_fusion.4), channel_id=1, source_target_pairs={{1,0},{16,17},{0,16},{17,1},{3,2},{18,19},{2,18},{19,3},{5,4},{20,... | collective-permute-start | bytes 706568 | tf_op jit(solution)/shard_map/ppermute | solution.py:386
  111.9 14.0 %collective-permute-start.29 = (f32[3,640]{1,0:T(4,128)S(1)}, f32[3,640]{1,0:T(4,128)S(1)}, u32[]{:S(2)}, u32[]{:S(2)}) collective-permute-start(f32[3,640]{1,0:T(4,128)S(1)} %maximum_subtract_fusion), channel_id=1, source_target_pairs={{0,16},{16,0},{1,17},{17,1},{2,18},{18,2},{3,19},{19,3},{4,20},{20... | collective-permute-start | bytes 23048 | tf_op jit(solution)/shard_map/ppermute | solution.py:243
  113.2 1.0 copy-start.4
  114.2 1.0 copy-start.6
  115.2 2.2 %copy-start.9 = (bf16[3,34,32,640]{3,2,1,0:T(8,128)(2,1)S(1)}, bf16[3,34,32,640]{3,2,1,0:T(8,128)(2,1)}, u32[]{:S(2)}) copy-start(bf16[3,34,32,640]{3,2,1,0:T(8,128)(2,1)} %copy-done.8) | copy-start | bytes 12533764
  125.5 1.2 copy-start.10
  125.5 3.3 %collective-permute-start.10 = (bf16[512,640]{1,0:T(8,128)(2,1)S(1)}, bf16[512,640]{1,0:T(8,128)(2,1)S(1)}, u32[]{:S(2)}, u32[]{:S(2)}) collective-permute-start(bf16[512,640]{1,0:T(8,128)(2,1)S(1)} %get-tuple-element.29), channel_id=1, source_target_pairs={{0,1},{1,0},{2,3},{3,2},{4,5},{5,4},{6,7},{7,6},{8,9},{9,8},{10,11... | collective-permute-start | bytes 1966088 | tf_op jit(solution)/shard_map/ppermute | solution.py:235

commit v4 on v3

--- a/solution.py
+++ b/solution.py
@@ -30,9 +30,10 @@
         self.mid = self.lead - 4 * chans
         self.mid_start = chans - self.mid
 
-    def tap(self, core, k, chans):
-        tap = jnp.where(core == 0, k, 5 + k)
-        return tap, pl.multiple_of(jnp.where(core == 0, k * chans, self.mid + k * chans), LANES)
+    def pair(self, core, k, chans):
+        first = jnp.where(core == 0, 2 * k, 5 + 2 * k)
+        place = jnp.where(core == 0, 2 * k * chans, self.mid + 2 * k * chans)
+        return (first, first + 1), pl.multiple_of(place, LANES)
 
     def middle(self, core, chans):
         place = jnp.where(core == 0, 4 * chans, 0)
@@ -130,12 +131,13 @@
         for q, piece in enumerate(pieces):
             piece[:, pl.ds(place, wide)] = value[q * count:(q + 1) * count].astype(BF16)
 
-    def full_tap(k, _):
-        tap, place = cols.tap(core, k, chans)
-        emit(acts[tap % 3, pl.ds(tap // 3, rows)].reshape(cells, chans), place, chans)
+    def two_taps(k, _):
+        taps, place = cols.pair(core, k, chans)
+        windows = [acts[t % 3, pl.ds(t // 3, rows)].reshape(cells, chans) for t in taps]
+        emit(jnp.concatenate(windows, axis=1), place, 2 * chans)
         return 0
 
-    lax.fori_loop(0, 4, full_tap, 0)
+    lax.fori_loop(0, 2, two_taps, 0)
     place, channel = cols.middle(core, chans)
     emit(acts[1, 1:rows + 1, :, pl.ds(channel, cols.mid)].reshape(cells, cols.mid), place, cols.mid)
 
@@ -161,46 +163,55 @@
     lax.fori_loop(0, half, one_row, 0)
 
 
-def place_blocks(first_at, me, table, blocks, whole):
+def place_kernel(dev, table, *refs):
+    blocks, whole = refs[:-1], refs[-1]
     for i, block in enumerate(blocks):
         count = block.shape[0]
-        at = pl.multiple_of(table[me, first_at + i] * count, count)
+        at = pl.multiple_of(table[dev[0], i] * count, count)
         whole[pl.ds(at, count)] = block[...]
 
 
-def conv_kernel(cols, first_at, count, dev, table, acts, *refs):
-    blocks, (own, far, whole, total) = refs[:count], refs[count:]
-    me = dev[0]
-    core = me % 2
-    rows, width, chans = acts.shape[1] - 2, acts.shape[2], acts.shape[3]
-    cells = rows * width
-    place_blocks(first_at, me, table, blocks, whole)
+def conv_sum(cols, core, first, half, acts, whole, total):
+    width, chans = acts.shape[2:]
+    cells = half * width
     nt = (((1,), (1,)), ((), ()))
     place, channel = cols.middle(core, chans)
-    window = acts[1, 1:rows + 1, :, pl.ds(channel, cols.mid)].reshape(cells, cols.mid)
+    window = acts[1, pl.ds(first + 1, half), :, pl.ds(channel, cols.mid)].reshape(cells, cols.mid)
     lane = lax.broadcasted_iota(jnp.int32, window.shape, 1)
     window = jnp.where((core == 1) & (lane < cols.both), jnp.zeros_like(window), window)
     total[...] = lax.dot_general(window, whole[:, pl.ds(place, cols.mid)], nt, preferred_element_type=F32)
 
-    def full_tap(k, _):
-        tap, place = cols.tap(core, k, chans)
-        window = acts[tap % 3, pl.ds(tap // 3, rows)].reshape(cells, chans)
-        total[...] += lax.dot_general(window, whole[:, pl.ds(place, chans)], nt, preferred_element_type=F32)
+    def two_taps(k, _):
+        taps, place = cols.pair(core, k, chans)
+        windows = [acts[t % 3, pl.ds(first + t // 3, half)].reshape(cells, chans) for t in taps]
+        total[...] += lax.dot_general(
+            jnp.concatenate(windows, axis=1), whole[:, pl.ds(place, 2 * chans)], nt, preferred_element_type=F32
+        )
         return 0
 
-    lax.fori_loop(0, 4, full_tap, 0)
-    half = cells // 2
-    own[...] = total[pl.ds(pl.multiple_of(core * half, half), half)]
-    far[...] = total[pl.ds(pl.multiple_of((1 - core) * half, half), half)].astype(BF16)
-
-
-def back_kernel(cols, first_at, count, dev, table, cots, slope, slope_x, *refs):
-    blocks, (sums, whole, total) = refs[:count], refs[count:]
-    me = dev[0]
-    core = me % 2
+    lax.fori_loop(0, 2, two_taps, 0)
+
+
+def conv_far_kernel(cols, dev, acts, whole, far, total):
+    core = dev[0] % 2
+    half = (acts.shape[1] - 2) // 2
+    conv_sum(cols, core, (1 - core) * half, half, acts, whole, total)
+    far[...] = total[...].astype(BF16)
+
+
+def conv_own_kernel(cols, dev, acts, whole, got, latent, bias, block, total):
+    core = dev[0] % 2
+    half, width, chans = latent.shape
+    conv_sum(cols, core, core * half, half, acts, whole, total)
+    scale = cols.total ** (-0.5)
+    conv = scale * (total[...] + got[...].astype(F32)) + bias[...]
+    block[...] = (conv.reshape(half, width, chans) + latent[...].astype(F32)).astype(BF16)
+
+
+def back_kernel(cols, dev, cots, slope, slope_x, whole, sums, total):
+    core = dev[0] % 2
     rows, width, chans = slope.shape
     cells = rows * width
-    place_blocks(first_at, me, table, blocks, whole)
     total[...] = jnp.zeros_like(total)
     place, channel = cols.middle(core, chans)
     window = cots[1, 1:rows + 1].reshape(cells, chans)
@@ -208,13 +219,17 @@
     lane = lax.broadcasted_iota(jnp.int32, value.shape, 1)
     total[:, pl.ds(channel, cols.mid)] = jnp.where((core == 1) & (lane < cols.both), 0.0, value)
 
-    def full_tap(k, _):
-        tap, place = cols.tap(core, k, chans)
-        window = cots[2 - tap % 3, pl.ds(2 - tap // 3, rows)].reshape(cells, chans)
-        total[...] += jnp.dot(window, whole[:, pl.ds(place, chans)], preferred_element_type=F32)
+    def two_taps(k, _):
+        taps, place = cols.pair(core, k, chans)
+        windows = [cots[2 - t % 3, pl.ds(2 - t // 3, rows)].reshape(cells, chans) for t in taps]
+        second = pl.multiple_of(place + chans, LANES)
+        kernels = [whole[:, pl.ds(place, chans)], whole[:, pl.ds(second, chans)]]
+        total[...] += jnp.dot(
+            jnp.concatenate(windows, axis=1), jnp.concatenate(kernels, axis=0), preferred_element_type=F32
+        )
         return 0
 
-    lax.fori_loop(0, 4, full_tap, 0)
+    lax.fori_loop(0, 2, two_taps, 0)
 
     def add_row(i, carry):
         gains, shifts = carry
@@ -306,9 +321,8 @@
     rate = LR_KERNEL * (1.0 - (step[0] % 1000).astype(F32) / 2000.0)
     dev = (((replica * zs + z) * 2 + y) * 2 + core).reshape(1)
 
-    kernel_b = shard.astype(BF16)
-    mine = lax.dynamic_slice_in_dim(kernel_b, core * cols.start, cols.lead, 1)
-    theirs = lax.dynamic_slice_in_dim(kernel_b, (1 - core) * cols.start, cols.lead, 1)
+    mine = lax.dynamic_slice_in_dim(shard, core * cols.start, cols.lead, 1).astype(BF16)
+    theirs = lax.dynamic_slice_in_dim(shard, (1 - core) * cols.start, cols.lead, 1).astype(BF16)
     got = swap(theirs, "core")
     unit = jnp.where(lower, jnp.concatenate([mine, got]), jnp.concatenate([got, mine]))
     lat_far = swap(latent, "core")
@@ -319,12 +333,11 @@
         table = jnp.asarray(ring.table(part))
         order = (ring.count, part, 2 * ring.count)
         up1, down1 = ring.up(unit), ring.down(unit)
-        peer_b = from_peer(level, kernel_b)
     else:
         table = jnp.zeros((replicas * zs * 4, 1), jnp.int32)
         order = None
 
-    def call(body, outs, ins, scratch, megabytes, flops, extra=0):
+    def call(body, outs, ins, scratch, megabytes, flops):
         return pl.pallas_call(
             body,
             out_shape=outs,
@@ -332,7 +345,7 @@
             out_specs=jax.tree.map(lambda _: VMEM_SPEC, outs),
             scratch_shapes=scratch,
             compiler_params=pltpu.CompilerParams(vmem_limit_bytes=megabytes * 2**20),
-            cost_estimate=pl.CostEstimate(flops=flops, bytes_accessed=8 * 2**20, transcendentals=extra),
+            cost_estimate=pl.CostEstimate(flops=flops, bytes_accessed=0, transcendentals=0),
         )
 
     image = (2 * half, width, chans)
@@ -343,52 +356,90 @@
         (jax.ShapeDtypeStruct((2, chans), F32), shifted, jax.ShapeDtypeStruct((chans, 2 * cells), BF16)),
         [SMEM_SPEC] * 2 + [VMEM_SPEC] * 6,
         [pltpu.VMEM((chans, 2 * cells), F32)],
-        24, flops, 2 * cells * chans,
+        24, flops // 4,
     )(dev, table, latent, lat_far, cot_b, cot_far, gn_gain, gn_shift)
-    if paired:
-        up1, down1, acts = tied(up1, down1, acts)
-        up2, down2 = ring.up(up1), ring.down(down1)
-
     pieces = call(
         partial(grad_kernel, cols),
         [jax.ShapeDtypeStruct((2 * part, cols.lead), BF16)] * (2 * zs),
         [SMEM_SPEC] + [VMEM_SPEC] * 2,
         [],
-        24, 2 * flops,
+        24, flops // 2,
     )(dev, acts, cot_t)
-    cots, slope, slope_x = call(
-        slope_kernel,
-        (shifted, jax.ShapeDtypeStruct(image, BF16), jax.ShapeDtypeStruct(image, BF16)),
-        [SMEM_SPEC] + [VMEM_SPEC] * 7,
-        [],
-        24, flops, 2 * cells * chans,
-    )(dev, stats, gn_gain, gn_shift, latent, lat_far, cot_b, cot_far)
+    def slopes_of(stats):
+        return call(
+            slope_kernel,
+            (shifted, jax.ShapeDtypeStruct(image, BF16), jax.ShapeDtypeStruct(image, BF16)),
+            [SMEM_SPEC] + [VMEM_SPEC] * 7,
+            [],
+            24, flops // 4,
+        )(dev, stats, gn_gain, gn_shift, latent, lat_far, cot_b, cot_far)
+
+    def back_of(blocks, slopes):
+        whole = call(
+            place_kernel, jax.ShapeDtypeStruct((chans, cols.lead), BF16),
+            [SMEM_SPEC] * 2 + [VMEM_SPEC] * len(blocks), [], 16, flops // 16,
+        )(dev, table, *blocks)
+        return whole, call(
+            partial(back_kernel, cols), jax.ShapeDtypeStruct((2, chans), F32),
+            [SMEM_SPEC] + [VMEM_SPEC] * 4, [pltpu.VMEM((2 * cells, chans), F32)], 24, flops // 2,
+        )(dev, *slopes, whole)
+
+    half_sum = [pltpu.VMEM((cells, chans), F32)]
+
+    def conv_far(whole):
+        return call(
+            partial(conv_far_kernel, cols), jax.ShapeDtypeStruct((cells, chans), BF16),
+            [SMEM_SPEC] + [VMEM_SPEC] * 2, half_sum, 24, flops // 4,
+        )(dev, acts, whole)
+
+    def chip_pair_sum(sums):
+        vectors = jnp.concatenate([jnp.sum(cotan, axis=(0, 1))[None], sums])
+        vectors = vectors + swap(vectors, "core")
+        return vectors + swap(vectors, "y")
 
     if paired:
-        blocks = [unit, up1, down1, up2, down2]
-        ups, downs = [up1, up2], [down1, down2]
-        for k in range(3, zs + 1):
-            ups.append(ring.up(ups[-1]))
-            blocks.append(ups[-1])
-            if k < zs:
-                downs.append(ring.down(downs[-1]))
-                blocks.append(downs[-1])
-        slots = [add(pieces[2 * j], swap(pieces[2 * j + 1], "replica")) for j in range(zs)]
-        up_sum = down_sum = None
+        pieces = list(pieces)
+        up, down, pieces[1] = tied(up1, down1, pieces[1])
+        blocks = [unit, up, down]
+        sums_in = [(), ()]
         for j in range(zs):
-            ahead, behind = slots[j][:part], slots[j][part:]
-            if j > 0:
-                ahead, behind = add(ahead, up_sum), add(behind, down_sum)
-            up_sum = ring.up(ahead)
+            crossed = swap(pieces[2 * j + 1], "replica")
             if j < zs - 1:
-                down_sum = ring.down(behind)
-        total = add(behind, up_sum)
+                up = ring.up(up)
+                blocks.append(up)
+            if j < zs - 2:
+                down = ring.down(down)
+                blocks.append(down)
+            if j == zs - 2:
+                slopes = slopes_of(tied(stats, blocks[-2])[0])
+                kernel_f = tied(shard, blocks[-2])[0]
+                up, crossed, slopes, *received = tied(up, crossed, slopes, *sums_in[0], *sums_in[1])
+            elif j < zs - 2:
+                up, down, crossed, *received = tied(up, down, crossed, *sums_in[0], *sums_in[1])
+            else:
+                whole, sums = back_of(blocks, slopes)
+                crossed, sums, *received = tied(crossed, sums, *sums_in[0], *sums_in[1])
+            if j < zs - 2:
+                blocks[-2:] = [up, down]
+            elif j == zs - 2:
+                blocks[-1] = up
+            sums_in = [tuple(received[:1]), tuple(received[1:])]
+            kept = pieces[2 * j]
+            ahead = add(kept[:part], crossed[:part], *sums_in[0])
+            behind = (kept[part:], crossed[part:], *sums_in[1])
+            sums_in = [(ring.up(ahead),), ()]
+            if j < zs - 1:
+                sums_in[1] = (ring.down(add(*behind)),)
+        last, conv_send, vectors = tied(*sums_in[0], conv_far(whole), chip_pair_sum(sums))
+        total = add(*behind, last)
+        peer_b = from_peer(level, kernel_f.astype(BF16))
         a = lax.ppermute(total, ("replica", "core"), [(1, 0), (2, 3), (0, 2), (3, 1)])
         b = lax.ppermute(total, ("replica", "core"), [(1, 2), (2, 1)])
         left = jnp.where(replica == core, jnp.where(lower, total, a), jnp.where(lower, a, b))
         right = jnp.where(replica == core, jnp.where(lower, a, total), jnp.where(lower, b, a))
     else:
-        blocks = [lax.all_gather(unit, NODE, axis=0, tiled=True)]
+        whole, sums = back_of([lax.all_gather(unit, NODE, axis=0, tiled=True)], slopes_of(stats))
+        conv_send, vectors = conv_far(whole), chip_pair_sum(sums)
         terms = jnp.concatenate(pieces).reshape(2 * zs, 2, part, cols.lead)
         summed = lax.psum_scatter(terms, NODE, scatter_dimension=0, tiled=False)
         ours = lax.dynamic_index_in_dim(summed, core, 0, keepdims=False)
@@ -401,27 +452,11 @@
         stepped = shard - (scale * rate) * kernel_grad
         new_kernel = 0.5 * (stepped + from_peer(level, stepped.astype(BF16)).astype(F32))
 
-    count = len(blocks)
-    whole = pltpu.VMEM((chans, cols.lead), BF16)
-    total_f = pltpu.VMEM((2 * cells, chans), F32)
-    sums = call(
-        partial(back_kernel, cols, 0, count),
-        jax.ShapeDtypeStruct((2, chans), F32),
-        [SMEM_SPEC] * 2 + [VMEM_SPEC] * (3 + count),
-        [whole, total_f],
-        24, 2 * flops,
-    )(dev, table, cots, slope, slope_x, *blocks)
-    conv_own, conv_send = call(
-        partial(conv_kernel, cols, 0, count),
-        (jax.ShapeDtypeStruct((cells, chans), F32), jax.ShapeDtypeStruct((cells, chans), BF16)),
-        [SMEM_SPEC] * 2 + [VMEM_SPEC] * (1 + count),
-        [whole, total_f],
-        24, 2 * flops,
-    )(dev, table, acts, *blocks)
-
-    vectors = jnp.concatenate([jnp.sum(cotan, axis=(0, 1))[None], sums])
-    vectors = vectors + swap(vectors, "core")
-    vectors = vectors + swap(vectors, "y")
+    block = call(
+        partial(conv_own_kernel, cols), jax.ShapeDtypeStruct((half, width, chans), BF16),
+        [SMEM_SPEC] + [VMEM_SPEC] * 5, half_sum, 24, flops // 4,
+    )(dev, acts, whole, swap(conv_send, "core"), latent, conv_bias)
+
     reach = 1
     while reach < zs:
         vectors = vectors + lax.ppermute(vectors, "z", [(s, s ^ reach) for s in range(zs)])
@@ -429,10 +464,8 @@
     stepped_v = jnp.concatenate([conv_bias, gn_gain, gn_shift]) - LR_VECTOR * vectors
     new_v = 0.5 * (stepped_v + from_peer(level, stepped_v))
 
-    conv = conv_own + swap(conv_send, "core").astype(F32)
-    block = (scale * conv + conv_bias + latent.astype(F32).reshape(cells, chans)).astype(BF16)
     return (
-        block.reshape(1, half, width, chans),
+        block[None],
         new_kernel[None],
         new_v[0][None],
         new_v[1][None],

time: 131 us -> 118 us (0.901)
  waiting for transfers between devices: 51.9 us -> 44 us
  other arithmetic: 11.2 us -> 4.05 us
  starting transfers between devices: 29.9 us -> 33.7 us
    ppermute x10, waiting for transfers between devices: 32.6 us -> 9.04 us  [swap(): return lax.ppermute(value, axis, [(0, 1), (1, 0)])]
    ppermute x8, waiting for transfers between devices: 12 us -> 21.5 us  [up(): return lax.ppermute(value, NODE, self.ahead)]
    ppermute x2, waiting for transfers between devices: 0.01 us -> 7.63 us  [from_peer(): return lax.ppermute(value, 'replica', moves[0])]
    ppermute x2, starting transfers between devices: 0.84 us -> 4.23 us  [per_device(): lax.ppermute(vectors, 'z', [(s, s ^ reach) for s in range(zs)])]
    convert_element_type x2 -> x1, other arithmetic: 3.28 us -> 0.05 us  [per_device(): peer_b = from_peer(level, kernel_f.astype(BF16))]
    ppermute x6, waiting for transfers between devices: 5.83 us -> 2.88 us  [down(): return lax.ppermute(value, NODE, self.behind)]
    ppermute x8, starting transfers between devices: 12.9 us -> 15.7 us  [up(): return lax.ppermute(value, NODE, self.ahead)]
    convert_element_type x8 -> x5, other arithmetic: 2.49 us -> 0.71 us  [add(): return total.astype(BF16)]
  transfers between devices with their start and end apart: 30 -> 30, of which waited for: 10 -> 12; matrix products, arithmetic and copies ran while one was open for 7% -> 4% of each run, Pallas kernels for 18% -> 20%
where the time goes in v4:
time: 118 us; the launch traced here: 117 us
  waiting for transfers between devices  44 us (37%)
  starting transfers between devices  33.7 us (29%)
  Pallas kernels  28.1 us (24%)
  local copies, waits for them, and re-layouts  5.97 us (5%)
  other arithmetic  4.05 us (3%)
  between operations  1.63 us (1%)
    ppermute x8, waiting for transfers between devices, up(): return lax.ppermute(value, NODE, self.ahead)  21.5 us
    ppermute x8, starting transfers between devices, up(): return lax.ppermute(value, NODE, self.ahead)  15.7 us
    ppermute x10, waiting for transfers between devices, swap(): return lax.ppermute(value, axis, [(0, 1), (1, 0)])  9.04 us
    ppermute x10, starting transfers between devices, swap(): return lax.ppermute(value, axis, [(0, 1), (1, 0)])  7.91 us
    ppermute x2, waiting for transfers between devices, from_peer(): return lax.ppermute(value, 'replica', moves[0])  7.63 us
    pallas_call x1, Pallas kernels, back_of(): call(partial(back_kernel, cols), jax.ShapeDtypeStruct((2, chans), F32), [...  6.57 us
    pallas_call x1, Pallas kernels, per_device(): call(partial(act_kernel, order), (jax.ShapeDtypeStruct((2, chans), F32),...  4.87 us
    pallas_call x1, Pallas kernels, per_device(): call(partial(grad_kernel, cols), [jax.ShapeDtypeStruct((2 * part, cols.le...  4.64 us
  transfers between devices with their start and end apart: 30, of which 12 were waited for; matrix products, arithmetic and copies ran while one was open for 4% of the time, Pallas kernels for 20%

profile of v4, /device:TPU:0, one launch (start us, length us, event | category | flops | bytes accessed | tf_op | source)
XLA Modules:
  0.0 117.4 jit_solution(324431511964455622)
XLA Ops:
  0.6 1.3 %fusion = (bf16[40,2944]{1,0:T(8,128)(2,1)S(1)}, bf16[40,2944]{1,0:T(8,128)(2,1)S(1)}) fusion(f32[1,40,5760]{2,1,0:T(8,128)} %param.10, s32[]{:T(128)S(6)} %select_n.52, s32[]{:T(128)S(6)} %select_n.53), kind=kLoop, calls=%fused_computation.13 | loop fusion | bytes 942088 | tf_op jit(solution)/shard_map/convert_element_type | solution.py:324
  2.0 0.5 collective-permute-start.2
  2.5 1.9 %fusion.4 = (f32[640]{0:T(1024)S(1)}, bf16[16,32,640]{2,1,0:T(8,128)(2,1)S(1)}) fusion(f32[1,16,32,640]{3,2,1,0:T(8,128)} %param.9), kind=kLoop, calls=%fused_computation.23 | loop fusion | flops 654720 | bytes 1968640 | tf_op jit(solution)/shard_map/reduce_sum | solution.py:396
  4.5 0.5 collective-permute-start
  5.1 2.7 %collective-permute-start.3 = (bf16[80,2944]{1,0:T(8,128)(2,1)S(1)}, bf16[80,2944]{1,0:T(8,128)(2,1)S(1)}, u32[]{:S(2)}, u32[]{:S(2)}) collective-permute-start(bf16[80,2944]{1,0:T(8,128)(2,1)S(1)} %maximum_select_fusion.refs_0_), channel_id=1, source_target_pairs={{0,4},{4,8},{8,12},{12,14},{14,10},{10,6},{6,2},{2,0},{1,5},{5,9},... | collective-permute-start | bytes 1413128 | tf_op jit(solution)/shard_map/ppermute | solution.py:275
  7.8 4.9 %shard_map.119 = (f32[2,640]{1,0:T(2,128)S(1)}, bf16[3,34,32,640]{3,2,1,0:T(8,128)(2,1)S(1)}, bf16[640,1024]{1,0:T(8,128)(2,1)S(1)}) custom-call(s32[1]{0:T(128)} %bitcast.dev, s32[32,24]{1,0:T(8,128)S(1)} %copy-done.5, bf16[16,32,640]{2,1,0:T(8,128)(2,1)S(1)} %bitcast.15, bf16[16,32,640]{2,1,0:T(8,128)(2,1)} %collective-permute-done.lat_far, ...), custom_call_target="tpu_custom_call" | custom-call | flops 964689920 | tf_op jit(solution)/shard_map/pallas_call | solution.py:354
  12.7 4.6 %shard_map.120 = (bf16[80,2944]{1,0:T(8,128)(2,1)S(1)}, bf16[80,2944]{1,0:T(8,128)(2,1)S(1)}, bf16[80,2944]{1,0:T(8,128)(2,1)S(1)}, bf16[80,2944]{1,0:T(8,128)(2...) custom-call(s32[1]{0:T(128)} %bitcast.dev, ...), custom_call_target="tpu_custom_call" | custom-call | flops 1929379840 | tf_op jit(solution)/shard_map/pallas_call | solution.py:361
  17.4 1.7 %collective-permute-done.3.refs_1_ = bf16[80,2944]{1,0:T(8,128)(2,1)S(1)} collective-permute-done((bf16[80,2944]{1,0:T(8,128)(2,1)S(1)}, bf16[80,2944]{1,0:T(8,128)(2,1)S(1)}, u32[]{:S(2)}, u32[]{:S(2)}) %collective-permute-start.3) | collective-permute-done | bytes 471072 | tf_op jit(solution)/shard_map/ppermute | solution.py:275
  19.1 1.5 %collective-permute-done.4.refs_2_ = bf16[80,2944]{1,0:T(8,128)(2,1)S(1)} collective-permute-done((bf16[80,2944]{1,0:T(8,128)(2,1)S(1)}, bf16[80,2944]{1,0:T(8,128)(2,1)S(1)}, u32[]{:S(2)}, u32[]{:S(2)}) %collective-permute-start.4) | collective-permute-done | bytes 471072 | tf_op jit(solution)/shard_map/ppermute | solution.py:278
  20.6 1.6 %collective-permute-start.5 = (bf16[80,2944]{1,0:T(8,128)(2,1)S(1)}, bf16[80,2944]{1,0:T(8,128)(2,1)S(1)}, u32[]{:S(2)}, u32[]{:S(2)}) collective-permute-start(bf16[80,2944]{1,0:T(8,128)(2,1)S(1)} %collective-permute-done.3.refs_1_), channel_id=1, source_target_pairs={{0,4},{4,8},{8,12},{12,14},{14,10},{10,6},{6,2},{2,0},{1,5},{5,9},... | collective-permute-start | bytes 1413128 | tf_op jit(solution)/shard_map/ppermute | solution.py:275
  22.7 1.5 %collective-permute-start.7 = (bf16[80,2944]{1,0:T(8,128)(2,1)S(1)}, bf16[80,2944]{1,0:T(8,128)(2,1)S(1)}, u32[]{:S(2)}, u32[]{:S(2)}) collective-permute-start(bf16[80,2944]{1,0:T(8,128)(2,1)S(1)} %get-tuple-element.51), channel_id=1, source_target_pairs={{0,16},{16,0},{1,17},{17,1},{2,18},{18,2},{3,19},{19,3},{4,20},{20... | collective-permute-start | bytes 1413128 | tf_op jit(solution)/shard_map/ppermute | solution.py:250
  24.2 0.5 collective-permute-start.10
  24.7 8.0 %collective-permute-done.5.refs_3_ = bf16[80,2944]{1,0:T(8,128)(2,1)S(1)} collective-permute-done((bf16[80,2944]{1,0:T(8,128)(2,1)S(1)}, bf16[80,2944]{1,0:T(8,128)(2,1)S(1)}, u32[]{:S(2)}, u32[]{:S(2)}) %collective-permute-start.5) | collective-permute-done | bytes 471072 | tf_op jit(solution)/shard_map/ppermute | solution.py:275
  32.7 1.3 %collective-permute-done.6.refs_4_ = bf16[80,2944]{1,0:T(8,128)(2,1)S(1)} collective-permute-done((bf16[80,2944]{1,0:T(8,128)(2,1)S(1)}, bf16[80,2944]{1,0:T(8,128)(2,1)S(1)}, u32[]{:S(2)}, u32[]{:S(2)}) %collective-permute-start.6) | collective-permute-done | bytes 471072 | tf_op jit(solution)/shard_map/ppermute | solution.py:278
  34.0 2.4 %collective-permute-done.7 = bf16[80,2944]{1,0:T(8,128)(2,1)S(1)} collective-permute-done((bf16[80,2944]{1,0:T(8,128)(2,1)S(1)}, bf16[80,2944]{1,0:T(8,128)(2,1)S(1)}, u32[]{:S(2)}, u32[]{:S(2)}) %collective-permute-start.7) | collective-permute-done | bytes 471072 | tf_op jit(solution)/shard_map/ppermute | solution.py:250
  36.4 1.6 %collective-permute-start.8 = (bf16[80,2944]{1,0:T(8,128)(2,1)S(1)}, bf16[80,2944]{1,0:T(8,128)(2,1)S(1)}, u32[]{:S(2)}, u32[]{:S(2)}) collective-permute-start(bf16[80,2944]{1,0:T(8,128)(2,1)S(1)} %collective-permute-done.5.refs_3_), channel_id=1, source_target_pairs={{0,4},{4,8},{8,12},{12,14},{14,10},{10,6},{6,2},{2,0},{1,5},{5,9},... | collective-permute-start | bytes 1413128 | tf_op jit(solution)/shard_map/ppermute | solution.py:275
  38.0 0.4 collective-permute-start.9
  38.5 1.6 %collective-permute-start.11 = (bf16[40,2944]{1,0:T(8,128)(2,1)S(1)}, bf16[40,2944]{1,0:T(8,128)(2,1)S(1)}, u32[]{:S(2)}, u32[]{:S(2)}) collective-permute-start(bf16[40,2944]{1,0:T(8,128)(2,1)S(1)} %get-tuple-element.94), channel_id=1, source_target_pairs={{0,4},{4,8},{8,12},{12,14},{14,10},{10,6},{6,2},{2,0},{1,5},{5,9},... | collective-permute-start | bytes 706568 | tf_op jit(solution)/shard_map/ppermute | solution.py:275
  40.6 3.6 %collective-permute-done.10 = bf16[80,2944]{1,0:T(8,128)(2,1)S(1)} collective-permute-done((bf16[80,2944]{1,0:T(8,128)(2,1)S(1)}, bf16[80,2944]{1,0:T(8,128)(2,1)S(1)}, u32[]{:S(2)}, u32[]{:S(2)}) %collective-permute-start.10) | collective-permute-done | bytes 471072 | tf_op jit(solution)/shard_map/ppermute | solution.py:250
  44.2 1.5 %collective-permute-start.14 = (bf16[80,2944]{1,0:T(8,128)(2,1)S(1)}, bf16[80,2944]{1,0:T(8,128)(2,1)S(1)}, u32[]{:S(2)}, u32[]{:S(2)}) collective-permute-start(bf16[80,2944]{1,0:T(8,128)(2,1)S(1)} %get-tuple-element.59), channel_id=1, source_target_pairs={{0,16},{16,0},{1,17},{17,1},{2,18},{18,2},{3,19},{19,3},{4,20},{20... | collective-permute-start | bytes 1413128 | tf_op jit(solution)/shard_map/ppermute | solution.py:250
  45.7 5.7 %collective-permute-done.11 = bf16[40,2944]{1,0:T(8,128)(2,1)S(1)} collective-permute-done((bf16[40,2944]{1,0:T(8,128)(2,1)S(1)}, bf16[40,2944]{1,0:T(8,128)(2,1)S(1)}, u32[]{:S(2)}, u32[]{:S(2)}) %collective-permute-start.11) | collective-permute-done | bytes 235552 | tf_op jit(solution)/shard_map/ppermute | solution.py:275
  51.4 2.0 %collective-permute-start.13 = (bf16[80,2944]{1,0:T(8,128)(2,1)S(1)}, bf16[80,2944]{1,0:T(8,128)(2,1)S(1)}, u32[]{:S(2)}, u32[]{:S(2)}) collective-permute-start(bf16[80,2944]{1,0:T(8,128)(2,1)S(1)} %collective-permute-done.8.refs_5_), channel_id=1, source_target_pairs={{0,4},{4,8},{8,12},{12,14},{14,10},{10,6},{6,2},{2,0},{1,5},{5,9},... | collective-permute-start | bytes 1413128 | tf_op jit(solution)/shard_map/ppermute | solution.py:275
  53.6 2.4 %collective-permute-start.15 = (bf16[40,2944]{1,0:T(8,128)(2,1)S(1)}, bf16[40,2944]{1,0:T(8,128)(2,1)S(1)}, u32[]{:S(2)}, u32[]{:S(2)}) collective-permute-start(bf16[40,2944]{1,0:T(8,128)(2,1)S(1)} %get-tuple-element.92), channel_id=1, source_target_pairs={{0,4},{4,8},{8,12},{12,14},{14,10},{10,6},{6,2},{2,0},{1,5},{5,9},... | collective-permute-start | bytes 706568 | tf_op jit(solution)/shard_map/ppermute | solution.py:275
  56.0 1.5 %collective-permute-start.17 = (bf16[80,2944]{1,0:T(8,128)(2,1)S(1)}, bf16[80,2944]{1,0:T(8,128)(2,1)S(1)}, u32[]{:S(2)}, u32[]{:S(2)}) collective-permute-start(bf16[80,2944]{1,0:T(8,128)(2,1)S(1)} %get-tuple-element.71), channel_id=1, source_target_pairs={{0,16},{16,0},{1,17},{17,1},{2,18},{18,2},{3,19},{19,3},{4,20},{20... | collective-permute-start | bytes 1413128 | tf_op jit(solution)/shard_map/ppermute | solution.py:250
  57.4 3.6 %shard_map.121 = (bf16[3,34,32,640]{3,2,1,0:T(8,128)(2,1)S(1)}, bf16[32,32,640]{2,1,0:T(8,128)(2,1)S(1)}, bf16[32,32,640]{2,1,0:T(8,128)(2,1)S(1)}) custom-call(s32[1]{0:T(128)} %bitcast.dev, f32[2,640]{1,0:T(2,128)S(1)} %get-tuple-element.61.stats, f32[1,640]{1,0:T(1,128)S(1)} %copy-done.7, f32[1,640]{1,0:T(1,128)S(1)} %copy-done.8, ...), custom_call_target="tpu_custom_call" | custom-call | flops 964689920 | tf_op jit(solution)/shard_map/pallas_call | solution.py:369
  61.0 6.2 %collective-permute-done.15 = bf16[40,2944]{1,0:T(8,128)(2,1)S(1)} collective-permute-done((bf16[40,2944]{1,0:T(8,128)(2,1)S(1)}, bf16[40,2944]{1,0:T(8,128)(2,1)S(1)}, u32[]{:S(2)}, u32[]{:S(2)}) %collective-permute-start.15) | collective-permute-done | bytes 235552 | tf_op jit(solution)/shard_map/ppermute | solution.py:275
  67.4 1.9 %collective-permute-start.18 = (bf16[40,2944]{1,0:T(8,128)(2,1)S(1)}, bf16[40,2944]{1,0:T(8,128)(2,1)S(1)}, u32[]{:S(2)}, u32[]{:S(2)}) collective-permute-start(bf16[40,2944]{1,0:T(8,128)(2,1)S(1)} %get-tuple-element.90), channel_id=1, source_target_pairs={{0,4},{4,8},{8,12},{12,14},{14,10},{10,6},{6,2},{2,0},{1,5},{5,9},... | collective-permute-start | bytes 706568 | tf_op jit(solution)/shard_map/ppermute | solution.py:275
  69.5 1.1 shard_map.122.whole
  70.5 6.6 %shard_map.123 = f32[2,640]{1,0:T(2,128)S(1)} custom-call(s32[1]{0:T(128)} %bitcast.dev, bf16[3,34,32,640]{3,2,1,0:T(8,128)(2,1)S(1)} %get-tuple-element.72.cots, bf16[32,32,640]{2,1,0:T(8,128)(2,1)S(1)} %get-tuple-element.73.slope, bf16[32,32,640]{2,1,0:T(8,128)(2,1)S(1)} %get-tuple-element.74.slope_x, bf16[640,2944]{1,0:T(8,128)(2,1)S(1)} %shard_map.122.whole), custom_call_target="tpu_custom_call" | custom-call | flops 1929379840 | tf_op jit(solution)/shard_map/pallas_call | solution.py:382
  77.4 1.9 %collective-permute-start.20 = (bf16[40,2944]{1,0:T(8,128)(2,1)S(1)}, bf16[40,2944]{1,0:T(8,128)(2,1)S(1)}, u32[]{:S(2)}, u32[]{:S(2)}) collective-permute-start(bf16[40,2944]{1,0:T(8,128)(2,1)S(1)} %add_convert_fusion.1), channel_id=1, source_target_pairs={{0,4},{4,8},{8,12},{12,14},{14,10},{10,6},{6,2},{2,0},{1,5},{5,9},... | collective-permute-start | bytes 706568 | tf_op jit(solution)/shard_map/ppermute | solution.py:275
  79.6 3.1 %shard_map.124 = bf16[512,640]{1,0:T(8,128)(2,1)S(1)} custom-call(s32[1]{0:T(128)} %bitcast.dev, bf16[3,34,32,640]{3,2,1,0:T(8,128)(2,1)S(1)} %get-tuple-element.46.acts, bf16[640,2944]{1,0:T(8,128)(2,1)S(1)} %shard_map.122.whole), custom_call_target="tpu_custom_call" | custom-call | flops 964689920 | tf_op jit(solution)/shard_map/pallas_call | solution.py:390
  82.8 3.0 %collective-permute-done.22 = f32[3,640]{1,0:T(4,128)S(1)} collective-permute-done((f32[3,640]{1,0:T(4,128)S(1)}, f32[3,640]{1,0:T(4,128)S(1)}, u32[]{:S(2)}, u32[]{:S(2)}) %collective-permute-start.22) | collective-permute-done | bytes 7712 | tf_op jit(solution)/shard_map/ppermute | solution.py:250
  85.8 0.7 copy-done.12
  86.5 1.6 %collective-permute-start.27 = (f32[3,640]{1,0:T(4,128)S(1)}, f32[3,640]{1,0:T(4,128)S(1)}, u32[]{:S(2)}, u32[]{:S(2)}) collective-permute-start(f32[3,640]{1,0:T(4,128)S(1)} %add.100), channel_id=1, source_target_pairs={{0,4},{4,0},{8,12},{12,8},{1,5},{5,1},{9,13},{13,9},{2,6},{6,2},{1... | collective-permute-start | bytes 23048 | tf_op jit(solution)/shard_map/ppermute | solution.py:462
  88.1 2.0 %collective-permute-done.27 = f32[3,640]{1,0:T(4,128)S(1)} collective-permute-done((f32[3,640]{1,0:T(4,128)S(1)}, f32[3,640]{1,0:T(4,128)S(1)}, u32[]{:S(2)}, u32[]{:S(2)}) %collective-permute-start.27) | collective-permute-done | bytes 7712 | tf_op jit(solution)/shard_map/ppermute | solution.py:462
  90.2 2.6 %collective-permute-start.28 = (f32[3,640]{1,0:T(4,128)S(1)}, f32[3,640]{1,0:T(4,128)S(1)}, u32[]{:S(2)}, u32[]{:S(2)}) collective-permute-start(f32[3,640]{1,0:T(4,128)S(1)} %add.106), channel_id=1, source_target_pairs={{0,8},{4,12},{8,0},{12,4},{1,9},{5,13},{9,1},{13,5},{2,10},{6,14},... | collective-permute-start | bytes 23048 | tf_op jit(solution)/shard_map/ppermute | solution.py:462
  93.5 1.6 %collective-permute-start.24 = (bf16[40,5760]{1,0:T(8,128)(2,1)S(1)}, bf16[40,5760]{1,0:T(8,128)(2,1)S(1)}, u32[]{:S(2)}, u32[]{:S(2)}) collective-permute-start(bf16[40,5760]{1,0:T(8,128)(2,1)S(1)} %convert_element_type.154), channel_id=1, source_target_pairs={{0,16},{16,0},{1,17},{17,1},{2,18},{18,2},{3,19},{19,3},{4,20},{20... | collective-permute-start | bytes 1382408 | tf_op jit(solution)/shard_map/ppermute | solution.py:258
  95.1 1.2 %collective-permute-start.29 = (f32[3,640]{1,0:T(4,128)S(1)}, f32[3,640]{1,0:T(4,128)S(1)}, u32[]{:S(2)}, u32[]{:S(2)}) collective-permute-start(f32[3,640]{1,0:T(4,128)S(1)} %maximum_subtract_fusion), channel_id=1, source_target_pairs={{0,16},{16,0},{1,17},{17,1},{2,18},{18,2},{3,19},{19,3},{4,20},{20... | collective-permute-start | bytes 23048 | tf_op jit(solution)/shard_map/ppermute | solution.py:258
  96.4 0.9 collective-permute-start.25
  97.3 0.7 collective-permute-start.26
  98.0 1.4 %collective-permute-start.23 = (bf16[512,640]{1,0:T(8,128)(2,1)S(1)}, bf16[512,640]{1,0:T(8,128)(2,1)S(1)}, u32[]{:S(2)}, u32[]{:S(2)}) collective-permute-start(bf16[512,640]{1,0:T(8,128)(2,1)S(1)} %shard_map.124), channel_id=1, source_target_pairs={{0,1},{1,0},{2,3},{3,2},{4,5},{5,4},{6,7},{7,6},{8,9},{9,8},{10,11... | collective-permute-start | bytes 1966088 | tf_op jit(solution)/shard_map/ppermute | solution.py:250
  99.5 7.6 %collective-permute-done.29 = f32[3,640]{1,0:T(4,128)S(1)} collective-permute-done((f32[3,640]{1,0:T(4,128)S(1)}, f32[3,640]{1,0:T(4,128)S(1)}, u32[]{:S(2)}, u32[]{:S(2)}) %collective-permute-start.29) | collective-permute-done | bytes 7712 | tf_op jit(solution)/shard_map/ppermute | solution.py:258
  107.1 0.6 fusion.5
  107.7 0.9 collective-permute-done.25
  108.7 1.1 subtract_bitcast_fusion
  109.9 1.2 copy-done.1
  111.0 2.2 %copy-done.3 = bf16[3,34,32,640]{3,2,1,0:T(8,128)(2,1)S(1)} copy-done((bf16[3,34,32,640]{3,2,1,0:T(8,128)(2,1)S(1)}, bf16[3,34,32,640]{3,2,1,0:T(8,128)(2,1)}, u32[]{:S(2)}) %copy-start.3) | copy-done | bytes 4177944
  113.2 4.2 %shard_map.125 = bf16[16,32,640]{2,1,0:T(8,128)(2,1)} custom-call(s32[1]{0:T(128)} %bitcast.dev, bf16[3,34,32,640]{3,2,1,0:T(8,128)(2,1)S(1)} %copy-done.3, bf16[640,2944]{1,0:T(8,128)(2,1)S(1)} %copy-done.1, bf16[512,640]{1,0:T(8,128)(2,1)S(1)} %collective-permute-done.23.got, bf16[16,32,640]{2,1,0:T(8,128)(2,1)S(1)} %bitcast.17, f32[1,640]{1,0:T(1,128)S(1)} %copy-done.6), custom_call_target="tpu_custom_call" | custom-call | flops 964689920 | tf_op jit(solution)/shard_map/pallas_call | solution.py:455
  (67 shorter events, 2.7 us)
Async XLA Ops:
  0.6 3.9 %copy-start.4 = (bf16[1,16,32,640]{3,2,1,0:T(8,128)(2,1)S(1)}, bf16[1,16,32,640]{3,2,1,0:T(8,128)(2,1)}, u32[]{:S(2)}) copy-start(bf16[1,16,32,640]{3,2,1,0:T(8,128)(2,1)} %param.8) | copy-start | bytes 1966084
  1.9 5.9 %copy-start.5 = (s32[32,24]{1,0:T(8,128)S(1)}, s32[32,24]{1,0:T(8,128)}, u32[]{:S(2)}) copy-start(s32[32,24]{1,0:T(8,128)} %constant.58.clone.table) | copy-start | bytes 9220
  1.9 5.9 %copy-start.7 = (f32[1,640]{1,0:T(1,128)S(1)}, f32[1,640]{1,0:T(1,128)}, u32[]{:S(2)}) copy-start(f32[1,640]{1,0:T(1,128)} %gain.3) | copy-start | bytes 7684
  2.0 5.9 %copy-start.8 = (f32[1,640]{1,0:T(1,128)S(1)}, f32[1,640]{1,0:T(1,128)}, u32[]{:S(2)}) copy-start(f32[1,640]{1,0:T(1,128)} %shift.3) | copy-start | bytes 7684
  2.0 3.0 %collective-permute-start.2 = (bf16[40,2944]{1,0:T(8,128)(2,1)S(1)}, bf16[40,2944]{1,0:T(8,128)(2,1)S(1)}, u32[]{:S(2)}, u32[]{:S(2)}) collective-permute-start(bf16[40,2944]{1,0:T(8,128)(2,1)S(1)} %get-tuple-element.96), channel_id=1, source_target_pairs={{0,1},{1,0},{2,3},{3,2},{4,5},{5,4},{6,7},{7,6},{8,9},{9,8},{10,11... | collective-permute-start | bytes 706568 | tf_op jit(solution)/shard_map/ppermute | solution.py:250
  4.4 3.4 %collective-permute-start.1 = (bf16[16,32,640]{2,1,0:T(8,128)(2,1)S(1)}, bf16[16,32,640]{2,1,0:T(8,128)(2,1)}, u32[]{:S(2)}, u32[]{:S(2)}) collective-permute-start(bf16[16,32,640]{2,1,0:T(8,128)(2,1)S(1)} %get-tuple-element.88.cot_own), channel_id=1, source_target_pairs={{0,1},{1,0},{2,3},{3,2},{4,5},{5,4},{6,7},{7,6},{8,9},{9,8},{10,11... | collective-permute-start | bytes 1966088 | tf_op jit(solution)/shard_map/ppermute | solution.py:250
  4.5 3.3 %collective-permute-start = (bf16[16,32,640]{2,1,0:T(8,128)(2,1)S(1)}, bf16[16,32,640]{2,1,0:T(8,128)(2,1)}, u32[]{:S(2)}, u32[]{:S(2)}) collective-permute-start(bf16[16,32,640]{2,1,0:T(8,128)(2,1)S(1)} %bitcast.14), channel_id=1, source_target_pairs={{0,1},{1,0},{2,3},{3,2},{4,5},{5,4},{6,7},{7,6},{8,9},{9,8},{10,11... | collective-permute-start | bytes 1966088 | tf_op jit(solution)/shard_map/ppermute | solution.py:250
  5.1 14.0 %collective-permute-start.3 = (bf16[80,2944]{1,0:T(8,128)(2,1)S(1)}, bf16[80,2944]{1,0:T(8,128)(2,1)S(1)}, u32[]{:S(2)}, u32[]{:S(2)}) collective-permute-start(bf16[80,2944]{1,0:T(8,128)(2,1)S(1)} %maximum_select_fusion.refs_0_), channel_id=1, source_target_pairs={{0,4},{4,8},{8,12},{12,14},{14,10},{10,6},{6,2},{2,0},{1,5},{5,9},... | collective-permute-start | bytes 1413128 | tf_op jit(solution)/shard_map/ppermute | solution.py:275
  7.8 12.8 %collective-permute-start.4 = (bf16[80,2944]{1,0:T(8,128)(2,1)S(1)}, bf16[80,2944]{1,0:T(8,128)(2,1)S(1)}, u32[]{:S(2)}, u32[]{:S(2)}) collective-permute-start(bf16[80,2944]{1,0:T(8,128)(2,1)S(1)} %maximum_select_fusion.refs_0_), channel_id=1, source_target_pairs={{4,0},{8,4},{12,8},{14,12},{10,14},{6,10},{2,6},{0,2},{5,1},{9,5},... | collective-permute-start | bytes 1413128 | tf_op jit(solution)/shard_map/ppermute | solution.py:278
  12.7 66.9 %copy-start.2 = (bf16[3,34,32,640]{3,2,1,0:T(8,128)(2,1)}, bf16[3,34,32,640]{3,2,1,0:T(8,128)(2,1)S(1)}, u32[]{:S(2)}) copy-start(bf16[3,34,32,640]{3,2,1,0:T(8,128)(2,1)S(1)} %get-tuple-element.46.acts) | copy-start | bytes 12533764
  20.6 12.0 %collective-permute-start.5 = (bf16[80,2944]{1,0:T(8,128)(2,1)S(1)}, bf16[80,2944]{1,0:T(8,128)(2,1)S(1)}, u32[]{:S(2)}, u32[]{:S(2)}) collective-permute-start(bf16[80,2944]{1,0:T(8,128)(2,1)S(1)} %collective-permute-done.3.refs_1_), channel_id=1, source_target_pairs={{0,4},{4,8},{8,12},{12,14},{14,10},{10,6},{6,2},{2,0},{1,5},{5,9},... | collective-permute-start | bytes 1413128 | tf_op jit(solution)/shard_map/ppermute | solution.py:275
  22.2 11.7 %collective-permute-start.6 = (bf16[80,2944]{1,0:T(8,128)(2,1)S(1)}, bf16[80,2944]{1,0:T(8,128)(2,1)S(1)}, u32[]{:S(2)}, u32[]{:S(2)}) collective-permute-start(bf16[80,2944]{1,0:T(8,128)(2,1)S(1)} %collective-permute-done.4.refs_2_), channel_id=1, source_target_pairs={{4,0},{8,4},{12,8},{14,12},{10,14},{6,10},{2,6},{0,2},{5,1},{9,5},... | collective-permute-start | bytes 1413128 | tf_op jit(solution)/shard_map/ppermute | solution.py:278
  22.7 13.7 %collective-permute-start.7 = (bf16[80,2944]{1,0:T(8,128)(2,1)S(1)}, bf16[80,2944]{1,0:T(8,128)(2,1)S(1)}, u32[]{:S(2)}, u32[]{:S(2)}) collective-permute-start(bf16[80,2944]{1,0:T(8,128)(2,1)S(1)} %get-tuple-element.51), channel_id=1, source_target_pairs={{0,16},{16,0},{1,17},{17,1},{2,18},{18,2},{3,19},{19,3},{4,20},{20... | collective-permute-start | bytes 1413128 | tf_op jit(solution)/shard_map/ppermute | solution.py:250
  24.2 20.1 %collective-permute-start.10 = (bf16[80,2944]{1,0:T(8,128)(2,1)S(1)}, bf16[80,2944]{1,0:T(8,128)(2,1)S(1)}, u32[]{:S(2)}, u32[]{:S(2)}) collective-permute-start(bf16[80,2944]{1,0:T(8,128)(2,1)S(1)} %get-tuple-element.54), channel_id=1, source_target_pairs={{0,16},{16,0},{1,17},{17,1},{2,18},{18,2},{3,19},{19,3},{4,20},{20... | collective-permute-start | bytes 1413128 | tf_op jit(solution)/shard_map/ppermute | solution.py:250
  36.4 15.0 %collective-permute-start.8 = (bf16[80,2944]{1,0:T(8,128)(2,1)S(1)}, bf16[80,2944]{1,0:T(8,128)(2,1)S(1)}, u32[]{:S(2)}, u32[]{:S(2)}) collective-permute-start(bf16[80,2944]{1,0:T(8,128)(2,1)S(1)} %collective-permute-done.5.refs_3_), channel_id=1, source_target_pairs={{0,4},{4,8},{8,12},{12,14},{14,10},{10,6},{6,2},{2,0},{1,5},{5,9},... | collective-permute-start | bytes 1413128 | tf_op jit(solution)/shard_map/ppermute | solution.py:275
  38.0 13.4 %collective-permute-start.9 = (bf16[80,2944]{1,0:T(8,128)(2,1)S(1)}, bf16[80,2944]{1,0:T(8,128)(2,1)S(1)}, u32[]{:S(2)}, u32[]{:S(2)}) collective-permute-start(bf16[80,2944]{1,0:T(8,128)(2,1)S(1)} %collective-permute-done.6.refs_4_), channel_id=1, source_target_pairs={{4,0},{8,4},{12,8},{14,12},{10,14},{6,10},{2,6},{0,2},{5,1},{9,5},... | collective-permute-start | bytes 1413128 | tf_op jit(solution)/shard_map/ppermute | solution.py:278
  38.5 12.8 %collective-permute-start.11 = (bf16[40,2944]{1,0:T(8,128)(2,1)S(1)}, bf16[40,2944]{1,0:T(8,128)(2,1)S(1)}, u32[]{:S(2)}, u32[]{:S(2)}) collective-permute-start(bf16[40,2944]{1,0:T(8,128)(2,1)S(1)} %get-tuple-element.94), channel_id=1, source_target_pairs={{0,4},{4,8},{8,12},{12,14},{14,10},{10,6},{6,2},{2,0},{1,5},{5,9},... | collective-permute-start | bytes 706568 | tf_op jit(solution)/shard_map/ppermute | solution.py:275
  40.2 11.2 %collective-permute-start.12 = (bf16[40,2944]{1,0:T(8,128)(2,1)S(1)}, bf16[40,2944]{1,0:T(8,128)(2,1)S(1)}, u32[]{:S(2)}, u32[]{:S(2)}) collective-permute-start(bf16[40,2944]{1,0:T(8,128)(2,1)S(1)} %get-tuple-element.93), channel_id=1, source_target_pairs={{4,0},{8,4},{12,8},{14,12},{10,14},{6,10},{2,6},{0,2},{5,1},{9,5},... | collective-permute-start | bytes 706568 | tf_op jit(solution)/shard_map/ppermute | solution.py:278
  44.2 16.8 %collective-permute-start.14 = (bf16[80,2944]{1,0:T(8,128)(2,1)S(1)}, bf16[80,2944]{1,0:T(8,128)(2,1)S(1)}, u32[]{:S(2)}, u32[]{:S(2)}) collective-permute-start(bf16[80,2944]{1,0:T(8,128)(2,1)S(1)} %get-tuple-element.59), channel_id=1, source_target_pairs={{0,16},{16,0},{1,17},{17,1},{2,18},{18,2},{3,19},{19,3},{4,20},{20... | collective-permute-start | bytes 1413128 | tf_op jit(solution)/shard_map/ppermute | solution.py:250
  51.4 15.8 %collective-permute-start.13 = (bf16[80,2944]{1,0:T(8,128)(2,1)S(1)}, bf16[80,2944]{1,0:T(8,128)(2,1)S(1)}, u32[]{:S(2)}, u32[]{:S(2)}) collective-permute-start(bf16[80,2944]{1,0:T(8,128)(2,1)S(1)} %collective-permute-done.8.refs_5_), channel_id=1, source_target_pairs={{0,4},{4,8},{8,12},{12,14},{14,10},{10,6},{6,2},{2,0},{1,5},{5,9},... | collective-permute-start | bytes 1413128 | tf_op jit(solution)/shard_map/ppermute | solution.py:275
  53.6 13.6 %collective-permute-start.15 = (bf16[40,2944]{1,0:T(8,128)(2,1)S(1)}, bf16[40,2944]{1,0:T(8,128)(2,1)S(1)}, u32[]{:S(2)}, u32[]{:S(2)}) collective-permute-start(bf16[40,2944]{1,0:T(8,128)(2,1)S(1)} %get-tuple-element.92), channel_id=1, source_target_pairs={{0,4},{4,8},{8,12},{12,14},{14,10},{10,6},{6,2},{2,0},{1,5},{5,9},... | collective-permute-start | bytes 706568 | tf_op jit(solution)/shard_map/ppermute | solution.py:275
  56.0 11.2 %collective-permute-start.16 = (bf16[40,2944]{1,0:T(8,128)(2,1)S(1)}, bf16[40,2944]{1,0:T(8,128)(2,1)S(1)}, u32[]{:S(2)}, u32[]{:S(2)}) collective-permute-start(bf16[40,2944]{1,0:T(8,128)(2,1)S(1)} %get-tuple-element.91), channel_id=1, source_target_pairs={{4,0},{8,4},{12,8},{14,12},{10,14},{6,10},{2,6},{0,2},{5,1},{9,5},... | collective-permute-start | bytes 706568 | tf_op jit(solution)/shard_map/ppermute | solution.py:278
  56.0 21.2 %collective-permute-start.17 = (bf16[80,2944]{1,0:T(8,128)(2,1)S(1)}, bf16[80,2944]{1,0:T(8,128)(2,1)S(1)}, u32[]{:S(2)}, u32[]{:S(2)}) collective-permute-start(bf16[80,2944]{1,0:T(8,128)(2,1)S(1)} %get-tuple-element.71), channel_id=1, source_target_pairs={{0,16},{16,0},{1,17},{17,1},{2,18},{18,2},{3,19},{19,3},{4,20},{20... | collective-permute-start | bytes 1413128 | tf_op jit(solution)/shard_map/ppermute | solution.py:250
  67.4 9.8 %collective-permute-start.18 = (bf16[40,2944]{1,0:T(8,128)(2,1)S(1)}, bf16[40,2944]{1,0:T(8,128)(2,1)S(1)}, u32[]{:S(2)}, u32[]{:S(2)}) collective-permute-start(bf16[40,2944]{1,0:T(8,128)(2,1)S(1)} %get-tuple-element.90), channel_id=1, source_target_pairs={{0,4},{4,8},{8,12},{12,14},{14,10},{10,6},{6,2},{2,0},{1,5},{5,9},... | collective-permute-start | bytes 706568 | tf_op jit(solution)/shard_map/ppermute | solution.py:275
  69.3 7.8 %collective-permute-start.19 = (bf16[40,2944]{1,0:T(8,128)(2,1)S(1)}, bf16[40,2944]{1,0:T(8,128)(2,1)S(1)}, u32[]{:S(2)}, u32[]{:S(2)}) collective-permute-start(bf16[40,2944]{1,0:T(8,128)(2,1)S(1)} %get-tuple-element.89), channel_id=1, source_target_pairs={{4,0},{8,4},{12,8},{14,12},{10,14},{6,10},{2,6},{0,2},{5,1},{9,5},... | collective-permute-start | bytes 706568 | tf_op jit(solution)/shard_map/ppermute | solution.py:278
  70.5 9.1 %copy-start = (bf16[640,2944]{1,0:T(8,128)(2,1)}, bf16[640,2944]{1,0:T(8,128)(2,1)S(1)}, u32[]{:S(2)}) copy-start(bf16[640,2944]{1,0:T(8,128)(2,1)S(1)} %shard_map.122.whole) | copy-start | bytes 11304964
  77.1 5.6 %copy-start.10 = (bf16[80,2944]{1,0:T(8,128)(2,1)}, bf16[80,2944]{1,0:T(8,128)(2,1)S(1)}, u32[]{:S(2)}) copy-start(bf16[80,2944]{1,0:T(8,128)(2,1)S(1)} %collective-permute-done.17) | copy-start | bytes 1413124
  77.2 2.1 %collective-permute-start.21 = (f32[3,640]{1,0:T(4,128)S(1)}, f32[3,640]{1,0:T(4,128)S(1)}, u32[]{:S(2)}, u32[]{:S(2)}) collective-permute-start(f32[3,640]{1,0:T(4,128)S(1)} %pad_maximum_fusion), channel_id=1, source_target_pairs={{0,1},{1,0},{2,3},{3,2},{4,5},{5,4},{6,7},{7,6},{8,9},{9,8},{10,11... | collective-permute-start | bytes 23048 | tf_op jit(solution)/shard_map/ppermute | solution.py:250
  77.4 8.4 %collective-permute-start.20 = (bf16[40,2944]{1,0:T(8,128)(2,1)S(1)}, bf16[40,2944]{1,0:T(8,128)(2,1)S(1)}, u32[]{:S(2)}, u32[]{:S(2)}) collective-permute-start(bf16[40,2944]{1,0:T(8,128)(2,1)S(1)} %add_convert_fusion.1), channel_id=1, source_target_pairs={{0,4},{4,8},{8,12},{12,14},{14,10},{10,6},{6,2},{2,0},{1,5},{5,9},... | collective-permute-start | bytes 706568 | tf_op jit(solution)/shard_map/ppermute | solution.py:275
  79.3 14.2 %copy-start.9 = (f32[1,40,5760]{2,1,0:T(8,128)S(1)}, f32[1,40,5760]{2,1,0:T(8,128)}, u32[]{:S(2)}) copy-start(f32[1,40,5760]{2,1,0:T(8,128)} %param.10) | copy-start | bytes 2764804
  79.3 6.5 %collective-permute-start.22 = (f32[3,640]{1,0:T(4,128)S(1)}, f32[3,640]{1,0:T(4,128)S(1)}, u32[]{:S(2)}, u32[]{:S(2)}) collective-permute-start(f32[3,640]{1,0:T(4,128)S(1)} %fusion.3), channel_id=1, source_target_pairs={{0,2},{2,0},{1,3},{3,1},{4,6},{6,4},{5,7},{7,5},{8,10},{10,8},{9,1... | collective-permute-start | bytes 23048 | tf_op jit(solution)/shard_map/ppermute | solution.py:250
  82.8 12.3 %copy-start.6 = (f32[1,640]{1,0:T(1,128)S(1)}, f32[1,640]{1,0:T(1,128)}, u32[]{:S(2)}) copy-start(f32[1,640]{1,0:T(1,128)} %bias.1) | copy-start | bytes 7684
  85.8 0.7 copy-start.12
  86.5 3.7 %collective-permute-start.27 = (f32[3,640]{1,0:T(4,128)S(1)}, f32[3,640]{1,0:T(4,128)S(1)}, u32[]{:S(2)}, u32[]{:S(2)}) collective-permute-start(f32[3,640]{1,0:T(4,128)S(1)} %add.100), channel_id=1, source_target_pairs={{0,4},{4,0},{8,12},{12,8},{1,5},{5,1},{9,13},{13,9},{2,6},{6,2},{1... | collective-permute-start | bytes 23048 | tf_op jit(solution)/shard_map/ppermute | solution.py:462
  90.2 4.9 %collective-permute-start.28 = (f32[3,640]{1,0:T(4,128)S(1)}, f32[3,640]{1,0:T(4,128)S(1)}, u32[]{:S(2)}, u32[]{:S(2)}) collective-permute-start(f32[3,640]{1,0:T(4,128)S(1)} %add.106), channel_id=1, source_target_pairs={{0,8},{4,12},{8,0},{12,4},{1,9},{5,13},{9,1},{13,5},{2,10},{6,14},... | collective-permute-start | bytes 23048 | tf_op jit(solution)/shard_map/ppermute | solution.py:462
  93.4 2.9 %copy-start.11 = (bf16[80,2944]{1,0:T(8,128)(2,1)S(1)}, bf16[80,2944]{1,0:T(8,128)(2,1)}, u32[]{:S(2)}) copy-start(bf16[80,2944]{1,0:T(8,128)(2,1)} %copy-done.10) | copy-start | bytes 1413124
  93.4 2.9 %copy-start.13 = (bf16[40,2944]{1,0:T(8,128)(2,1)S(1)}, bf16[40,2944]{1,0:T(8,128)(2,1)}, u32[]{:S(2)}) copy-start(bf16[40,2944]{1,0:T(8,128)(2,1)} %copy-done.12) | copy-start | bytes 706564
  93.5 15.2 %collective-permute-start.24 = (bf16[40,5760]{1,0:T(8,128)(2,1)S(1)}, bf16[40,5760]{1,0:T(8,128)(2,1)S(1)}, u32[]{:S(2)}, u32[]{:S(2)}) collective-permute-start(bf16[40,5760]{1,0:T(8,128)(2,1)S(1)} %convert_element_type.154), channel_id=1, source_target_pairs={{0,16},{16,0},{1,17},{17,1},{2,18},{18,2},{3,19},{19,3},{4,20},{20... | collective-permute-start | bytes 1382408 | tf_op jit(solution)/shard_map/ppermute | solution.py:258
  95.1 12.0 %collective-permute-start.29 = (f32[3,640]{1,0:T(4,128)S(1)}, f32[3,640]{1,0:T(4,128)S(1)}, u32[]{:S(2)}, u32[]{:S(2)}) collective-permute-start(f32[3,640]{1,0:T(4,128)S(1)} %maximum_subtract_fusion), channel_id=1, source_target_pairs={{0,16},{16,0},{1,17},{17,1},{2,18},{18,2},{3,19},{19,3},{4,20},{20... | collective-permute-start | bytes 23048 | tf_op jit(solution)/shard_map/ppermute | solution.py:258
  96.4 12.2 %collective-permute-start.25 = (bf16[40,2944]{1,0:T(8,128)(2,1)S(1)}, bf16[40,2944]{1,0:T(8,128)(2,1)S(1)}, u32[]{:S(2)}, u32[]{:S(2)}) collective-permute-start(bf16[40,2944]{1,0:T(8,128)(2,1)S(1)} %add_convert_fusion), channel_id=1, source_target_pairs={{1,0},{16,17},{0,16},{17,1},{3,2},{18,19},{2,18},{19,3},{5,4},{20,... | collective-permute-start | bytes 706568 | tf_op jit(solution)/shard_map/ppermute | solution.py:436
  97.3 11.3 %collective-permute-start.26 = (bf16[40,2944]{1,0:T(8,128)(2,1)S(1)}, bf16[40,2944]{1,0:T(8,128)(2,1)S(1)}, u32[]{:S(2)}, u32[]{:S(2)}) collective-permute-start(bf16[40,2944]{1,0:T(8,128)(2,1)S(1)} %add_convert_fusion), channel_id=1, source_target_pairs={{1,16},{16,1},{3,18},{18,3},{5,20},{20,5},{7,22},{22,7},{9,24},{24... | collective-permute-start | bytes 706568 | tf_op jit(solution)/shard_map/ppermute | solution.py:437
  98.0 11.8 %collective-permute-start.23 = (bf16[512,640]{1,0:T(8,128)(2,1)S(1)}, bf16[512,640]{1,0:T(8,128)(2,1)S(1)}, u32[]{:S(2)}, u32[]{:S(2)}) collective-permute-start(bf16[512,640]{1,0:T(8,128)(2,1)S(1)} %shard_map.124), channel_id=1, source_target_pairs={{0,1},{1,0},{2,3},{3,2},{4,5},{5,4},{6,7},{7,6},{8,9},{9,8},{10,11... | collective-permute-start | bytes 1966088 | tf_op jit(solution)/shard_map/ppermute | solution.py:250
  108.6 2.4 %copy-start.1 = (bf16[640,2944]{1,0:T(8,128)(2,1)S(1)}, bf16[640,2944]{1,0:T(8,128)(2,1)}, u32[]{:S(2)}) copy-start(bf16[640,2944]{1,0:T(8,128)(2,1)} %copy-done) | copy-start | bytes 11304964
  111.0 2.2 %copy-start.3 = (bf16[3,34,32,640]{3,2,1,0:T(8,128)(2,1)S(1)}, bf16[3,34,32,640]{3,2,1,0:T(8,128)(2,1)}, u32[]{:S(2)}) copy-start(bf16[3,34,32,640]{3,2,1,0:T(8,128)(2,1)} %copy-done.2) | copy-start | bytes 12533764

commit v5 on v4

--- a/solution.py
+++ b/solution.py
@@ -164,7 +164,9 @@
 
 
 def place_kernel(dev, table, *refs):
-    blocks, whole = refs[:-1], refs[-1]
+    blocks, whole = list(refs[:-1]), refs[-1]
+    if blocks[-1].shape != blocks[0].shape:
+        blocks[-2:] = [jnp.concatenate([blocks[-2][...], blocks[-1][...]])]
     for i, block in enumerate(blocks):
         count = block.shape[0]
         at = pl.multiple_of(table[dev[0], i] * count, count)
@@ -294,6 +296,14 @@
         return rows.reshape(-1, 3 * self.count)
 
 
+def sum_over(value, axes, masks):
+    count = lax.axis_size(axes)
+    for mask in (masks[0], masks[1], masks[0] | masks[1]):
+        value_in = lax.ppermute(value, axes, [(s, s ^ mask) for s in range(count)])
+        total = value_in if mask == masks[0] else total + value_in
+    return value + total
+
+
 def add(*values):
     total = values[0].astype(F32)
     for value in values[1:]:
@@ -318,6 +328,7 @@
     ring = Ring(zs)
     scale = cols.total ** (-0.5)
     level = step[0] % (replicas.bit_length() - 1)
+    params = jnp.concatenate([conv_bias, gn_gain, gn_shift])
     rate = LR_KERNEL * (1.0 - (step[0] % 1000).astype(F32) / 2000.0)
     dev = (((replica * zs + z) * 2 + y) * 2 + core).reshape(1)
 
@@ -333,6 +344,7 @@
         table = jnp.asarray(ring.table(part))
         order = (ring.count, part, 2 * ring.count)
         up1, down1 = ring.up(unit), ring.down(unit)
+        peer_b = from_peer(level, shard.astype(BF16))
     else:
         table = jnp.zeros((replicas * zs * 4, 1), jnp.int32)
         order = None
@@ -356,14 +368,14 @@
         (jax.ShapeDtypeStruct((2, chans), F32), shifted, jax.ShapeDtypeStruct((chans, 2 * cells), BF16)),
         [SMEM_SPEC] * 2 + [VMEM_SPEC] * 6,
         [pltpu.VMEM((chans, 2 * cells), F32)],
-        24, flops // 4,
+        16, flops // 4,
     )(dev, table, latent, lat_far, cot_b, cot_far, gn_gain, gn_shift)
     pieces = call(
         partial(grad_kernel, cols),
         [jax.ShapeDtypeStruct((2 * part, cols.lead), BF16)] * (2 * zs),
         [SMEM_SPEC] + [VMEM_SPEC] * 2,
         [],
-        24, flops // 2,
+        20, flops // 2,
     )(dev, acts, cot_t)
     def slopes_of(stats):
         return call(
@@ -371,13 +383,13 @@
             (shifted, jax.ShapeDtypeStruct(image, BF16), jax.ShapeDtypeStruct(image, BF16)),
             [SMEM_SPEC] + [VMEM_SPEC] * 7,
             [],
-            24, flops // 4,
+            12, flops // 4,
         )(dev, stats, gn_gain, gn_shift, latent, lat_far, cot_b, cot_far)
 
     def back_of(blocks, slopes):
         whole = call(
             place_kernel, jax.ShapeDtypeStruct((chans, cols.lead), BF16),
-            [SMEM_SPEC] * 2 + [VMEM_SPEC] * len(blocks), [], 16, flops // 16,
+            [SMEM_SPEC] * 2 + [VMEM_SPEC] * len(blocks), [], 10, flops // 16,
         )(dev, table, *blocks)
         return whole, call(
             partial(back_kernel, cols), jax.ShapeDtypeStruct((2, chans), F32),
@@ -389,57 +401,49 @@
     def conv_far(whole):
         return call(
             partial(conv_far_kernel, cols), jax.ShapeDtypeStruct((cells, chans), BF16),
-            [SMEM_SPEC] + [VMEM_SPEC] * 2, half_sum, 24, flops // 4,
+            [SMEM_SPEC] + [VMEM_SPEC] * 2, half_sum, 16, flops // 4,
         )(dev, acts, whole)
 
-    def chip_pair_sum(sums):
+    def chip_sum(sums):
         vectors = jnp.concatenate([jnp.sum(cotan, axis=(0, 1))[None], sums])
-        vectors = vectors + swap(vectors, "core")
-        return vectors + swap(vectors, "y")
+        vectors = params / (4 * zs) - LR_VECTOR * vectors
+        return vectors + swap(vectors, "core")
 
     if paired:
-        pieces = list(pieces)
-        up, down, pieces[1] = tied(up1, down1, pieces[1])
+        kept, sent = pieces[::2], pieces[1::2]
+        slopes = slopes_of(tied(stats, sent[0])[0])
+        up, down, peer_b, slopes = tied(up1, down1, peer_b, slopes)
         blocks = [unit, up, down]
-        sums_in = [(), ()]
+        crossed = [swap(piece, "replica") for piece in sent]
+        up_sum = down_sum = ()
         for j in range(zs):
-            crossed = swap(pieces[2 * j + 1], "replica")
+            if j < zs - 2:
+                up, down = ring.up(up), ring.down(down)
+                blocks += [up, down]
+                up, down, crossed[j], *received = tied(up, down, crossed[j], *up_sum, *down_sum)
+                up_sum, down_sum = tuple(received[:1]), tuple(received[1:])
+            elif j == zs - 2:
+                halves = ring.up(up[:part]), ring.down(down[part:])
+                *halves, crossed[j] = tied(*halves, crossed[j])
+                whole, sums = back_of(blocks + halves, slopes)
+            else:
+                crossed[j], sums, *received = tied(crossed[j], sums, *up_sum, *down_sum)
+                up_sum, down_sum = tuple(received[:1]), tuple(received[1:])
+            ahead = add(kept[j][:part], crossed[j][:part], *up_sum)
+            behind = (kept[j][part:], crossed[j][part:], *down_sum)
+            up_sum = (ring.up(ahead),)
             if j < zs - 1:
-                up = ring.up(up)
-                blocks.append(up)
-            if j < zs - 2:
-                down = ring.down(down)
-                blocks.append(down)
-            if j == zs - 2:
-                slopes = slopes_of(tied(stats, blocks[-2])[0])
-                kernel_f = tied(shard, blocks[-2])[0]
-                up, crossed, slopes, *received = tied(up, crossed, slopes, *sums_in[0], *sums_in[1])
-            elif j < zs - 2:
-                up, down, crossed, *received = tied(up, down, crossed, *sums_in[0], *sums_in[1])
-            else:
-                whole, sums = back_of(blocks, slopes)
-                crossed, sums, *received = tied(crossed, sums, *sums_in[0], *sums_in[1])
-            if j < zs - 2:
-                blocks[-2:] = [up, down]
-            elif j == zs - 2:
-                blocks[-1] = up
-            sums_in = [tuple(received[:1]), tuple(received[1:])]
-            kept = pieces[2 * j]
-            ahead = add(kept[:part], crossed[:part], *sums_in[0])
-            behind = (kept[part:], crossed[part:], *sums_in[1])
-            sums_in = [(ring.up(ahead),), ()]
-            if j < zs - 1:
-                sums_in[1] = (ring.down(add(*behind)),)
-        last, conv_send, vectors = tied(*sums_in[0], conv_far(whole), chip_pair_sum(sums))
+                down_sum = (ring.down(add(*behind)),)
+        vectors = sum_over(chip_sum(sums), ("z", "y"), (1, 2))
+        last, conv_got, vectors = tied(*up_sum, swap(conv_far(whole), "core"), vectors)
         total = add(*behind, last)
-        peer_b = from_peer(level, kernel_f.astype(BF16))
         a = lax.ppermute(total, ("replica", "core"), [(1, 0), (2, 3), (0, 2), (3, 1)])
         b = lax.ppermute(total, ("replica", "core"), [(1, 2), (2, 1)])
         left = jnp.where(replica == core, jnp.where(lower, total, a), jnp.where(lower, a, b))
         right = jnp.where(replica == core, jnp.where(lower, a, total), jnp.where(lower, b, a))
     else:
         whole, sums = back_of([lax.all_gather(unit, NODE, axis=0, tiled=True)], slopes_of(stats))
-        conv_send, vectors = conv_far(whole), chip_pair_sum(sums)
+        conv_got, vectors = swap(conv_far(whole), "core"), chip_sum(sums)
         terms = jnp.concatenate(pieces).reshape(2 * zs, 2, part, cols.lead)
         summed = lax.psum_scatter(terms, NODE, scatter_dimension=0, tiled=False)
         ours = lax.dynamic_index_in_dim(summed, core, 0, keepdims=False)
@@ -454,15 +458,14 @@
 
     block = call(
         partial(conv_own_kernel, cols), jax.ShapeDtypeStruct((half, width, chans), BF16),
-        [SMEM_SPEC] + [VMEM_SPEC] * 5, half_sum, 24, flops // 4,
-    )(dev, acts, whole, swap(conv_send, "core"), latent, conv_bias)
-
-    reach = 1
-    while reach < zs:
-        vectors = vectors + lax.ppermute(vectors, "z", [(s, s ^ reach) for s in range(zs)])
-        reach *= 2
-    stepped_v = jnp.concatenate([conv_bias, gn_gain, gn_shift]) - LR_VECTOR * vectors
-    new_v = 0.5 * (stepped_v + from_peer(level, stepped_v))
+        [SMEM_SPEC] + [VMEM_SPEC] * 5, half_sum, 16, flops // 4,
+    )(dev, acts, whole, conv_got, latent, conv_bias)
+
+    if paired:
+        new_v = 0.5 * sum_over(vectors, ("replica", "z"), (2, zs))
+    else:
+        stepped_v = lax.psum(vectors, NODE)
+        new_v = 0.5 * (stepped_v + from_peer(level, stepped_v))
 
     return (
         block[None],

time: 118 us -> 110 us (0.932)
  waiting for transfers between devices: 44 us -> 28.9 us
  other arithmetic: 4.05 us -> 7.87 us
  starting transfers between devices: 33.7 us -> 35.7 us
    ppermute x2 -> x1, waiting for transfers between devices: 7.63 us -> 0.01 us  [from_peer(): return lax.ppermute(value, 'replica', moves[0])]
    ppermute x8, waiting for transfers between devices: 21.5 us -> 16.5 us  [up(): return lax.ppermute(value, NODE, self.ahead)]
    ppermute x2 -> x6, starting transfers between devices: 4.23 us -> 8.01 us  [sum_over(): value_in = lax.ppermute(value, axes, [(s, s ^ mask) for s in range(count)])]
    ppermute x10 -> x9, waiting for transfers between devices: 9.04 us -> 6.5 us  [swap(): return lax.ppermute(value, axis, [(0, 1), (1, 0)])]
    convert_element_type x1, other arithmetic: 0.05 us -> 2 us  [per_device(): peer_b = from_peer(level, shard.astype(BF16))]
    convert_element_type x5, other arithmetic: 0.71 us -> 2.44 us  [add(): return total.astype(BF16)]
    ppermute x10 -> x9, starting transfers between devices: 7.91 us -> 6.41 us  [swap(): return lax.ppermute(value, axis, [(0, 1), (1, 0)])]
    ppermute x2 -> x1, starting transfers between devices: 2.76 us -> 1.93 us  [from_peer(): return lax.ppermute(value, 'replica', moves[0])]
  transfers between devices with their start and end apart: 30 -> 33, of which waited for: 12 -> 11; matrix products, arithmetic and copies ran while one was open for 4% -> 7% of each run, Pallas kernels for 20% -> 26%
where the time goes in v5:
time: 110 us; the launch traced here: 109 us
  starting transfers between devices  35.7 us (32%)
  waiting for transfers between devices  28.9 us (26%)
  Pallas kernels  28.2 us (26%)
  other arithmetic  7.87 us (7%)
  local copies, waits for them, and re-layouts  6.65 us (6%)
  between operations  1.64 us (1%)
    ppermute x8, waiting for transfers between devices, up(): return lax.ppermute(value, NODE, self.ahead)  16.5 us
    ppermute x8, starting transfers between devices, up(): return lax.ppermute(value, NODE, self.ahead)  15.2 us
    ppermute x6, starting transfers between devices, sum_over(): value_in = lax.ppermute(value, axes, [(s, s ^ mask) for s in range(count)])  8.01 us
    pallas_call x1, Pallas kernels, back_of(): call(partial(back_kernel, cols), jax.ShapeDtypeStruct((2, chans), F32), [...  6.56 us
    ppermute x9, waiting for transfers between devices, swap(): return lax.ppermute(value, axis, [(0, 1), (1, 0)])  6.5 us
    ppermute x9, starting transfers between devices, swap(): return lax.ppermute(value, axis, [(0, 1), (1, 0)])  6.41 us
    pallas_call x1, Pallas kernels, per_device(): call(partial(act_kernel, order), (jax.ShapeDtypeStruct((2, chans), F32),...  4.86 us
    unnamed x22, local copies, waits for them, and re-layouts  4.73 us
  transfers between devices with their start and end apart: 33, of which 11 were waited for; matrix products, arithmetic and copies ran while one was open for 7% of the time, Pallas kernels for 26%

profile of v5, /device:TPU:0, one launch (start us, length us, event | category | flops | bytes accessed | tf_op | source)
XLA Modules:
  0.0 108.9 jit_solution(1366808825872800399)
XLA Ops:
  0.6 1.3 %fusion.3 = (bf16[40,2944]{1,0:T(8,128)(2,1)S(1)}, bf16[40,2944]{1,0:T(8,128)(2,1)S(1)}) fusion(f32[1,40,5760]{2,1,0:T(8,128)} %param.10, s32[]{:T(128)S(6)} %select_n.52, s32[]{:T(128)S(6)} %select_n.53), kind=kLoop, calls=%fused_computation.17 | loop fusion | bytes 942088 | tf_op jit(solution)/shard_map/convert_element_type | solution.py:335
  1.9 0.5 collective-permute-start.2
  2.5 2.1 %fusion.7 = (f32[640]{0:T(1024)S(1)}, bf16[16,32,640]{2,1,0:T(8,128)(2,1)S(1)}) fusion(f32[1,16,32,640]{3,2,1,0:T(8,128)} %param.9), kind=kLoop, calls=%fused_computation.28 | loop fusion | flops 654720 | bytes 1968640 | tf_op jit(solution)/shard_map/reduce_sum | solution.py:408
  4.7 0.5 collective-permute-start
  5.2 2.7 %collective-permute-start.3 = (bf16[80,2944]{1,0:T(8,128)(2,1)S(1)}, bf16[80,2944]{1,0:T(8,128)(2,1)S(1)}, u32[]{:S(2)}, u32[]{:S(2)}) collective-permute-start(bf16[80,2944]{1,0:T(8,128)(2,1)S(1)} %maximum_select_fusion.refs_0_), channel_id=1, source_target_pairs={{0,4},{4,8},{8,12},{12,14},{14,10},{10,6},{6,2},{2,0},{1,5},{5,9},... | collective-permute-start | bytes 1413128 | tf_op jit(solution)/shard_map/ppermute | solution.py:277
  7.9 2.0 %bitcast_convert_fusion = bf16[40,5760]{1,0:T(8,128)(2,1)} fusion(f32[1,40,5760]{2,1,0:T(8,128)} %param.10), kind=kLoop, calls=%fused_computation.1 | loop fusion | flops 230400 | bytes 1382400 | tf_op jit(solution)/shard_map/convert_element_type | solution.py:347
  9.9 1.9 %collective-permute-start.5 = (bf16[40,5760]{1,0:T(8,128)(2,1)}, bf16[40,5760]{1,0:T(8,128)(2,1)S(1)}, u32[]{:S(2)}, u32[]{:S(2)}) collective-permute-start(bf16[40,5760]{1,0:T(8,128)(2,1)} %bitcast_convert_fusion), channel_id=1, source_target_pairs={{0,16},{16,0},{1,17},{17,1},{2,18},{18,2},{3,19},{19,3},{4,20},{20... | collective-permute-start | bytes 1382408 | tf_op jit(solution)/shard_map/ppermute | solution.py:260
  11.9 4.9 %shard_map.119 = (f32[2,640]{1,0:T(2,128)S(1)}, bf16[3,34,32,640]{3,2,1,0:T(8,128)(2,1)S(1)}, bf16[640,1024]{1,0:T(8,128)(2,1)S(1)}) custom-call(s32[1]{0:T(128)} %bitcast.dev, s32[32,24]{1,0:T(8,128)S(1)} %copy-done.6, bf16[16,32,640]{2,1,0:T(8,128)(2,1)S(1)} %bitcast.22, bf16[16,32,640]{2,1,0:T(8,128)(2,1)} %collective-permute-done.lat_far, ...), custom_call_target="tpu_custom_call" | custom-call | flops 964689920 | tf_op jit(solution)/shard_map/pallas_call | solution.py:366
  16.8 4.6 %shard_map.120 = (bf16[80,2944]{1,0:T(8,128)(2,1)S(1)}, bf16[80,2944]{1,0:T(8,128)(2,1)S(1)}, bf16[80,2944]{1,0:T(8,128)(2,1)S(1)}, bf16[80,2944]{1,0:T(8,128)(2...) custom-call(s32[1]{0:T(128)} %bitcast.dev, ...), custom_call_target="tpu_custom_call" | custom-call | flops 1929379840 | tf_op jit(solution)/shard_map/pallas_call | solution.py:373
  21.6 3.6 %shard_map.121 = (bf16[3,34,32,640]{3,2,1,0:T(8,128)(2,1)S(1)}, bf16[32,32,640]{2,1,0:T(8,128)(2,1)S(1)}, bf16[32,32,640]{2,1,0:T(8,128)(2,1)S(1)}) custom-call(s32[1]{0:T(128)} %bitcast.dev, f32[2,640]{1,0:T(2,128)S(1)} %get-tuple-element.48.stats, f32[1,640]{1,0:T(1,128)S(1)} %copy-done.7, f32[1,640]{1,0:T(1,128)S(1)} %copy-done.8, ...), custom_call_target="tpu_custom_call" | custom-call | flops 964689920 | tf_op jit(solution)/shard_map/pallas_call | solution.py:381
  25.2 2.1 %collective-permute-start.6 = (bf16[80,2944]{1,0:T(8,128)(2,1)S(1)}, bf16[80,2944]{1,0:T(8,128)(2,1)S(1)}, u32[]{:S(2)}, u32[]{:S(2)}) collective-permute-start(bf16[80,2944]{1,0:T(8,128)(2,1)S(1)} %collective-permute-done.3.refs_1_), channel_id=1, source_target_pairs={{0,4},{4,8},{8,12},{12,14},{14,10},{10,6},{6,2},{2,0},{1,5},{5,9},... | collective-permute-start | bytes 1413128 | tf_op jit(solution)/shard_map/ppermute | solution.py:277
  27.2 1.9 %collective-permute-start.11 = (bf16[80,2944]{1,0:T(8,128)(2,1)S(1)}, bf16[80,2944]{1,0:T(8,128)(2,1)S(1)}, u32[]{:S(2)}, u32[]{:S(2)}) collective-permute-start(bf16[80,2944]{1,0:T(8,128)(2,1)S(1)} %get-tuple-element.56), channel_id=1, source_target_pairs={{0,16},{16,0},{1,17},{17,1},{2,18},{18,2},{3,19},{19,3},{4,20},{20... | collective-permute-start | bytes 1413128 | tf_op jit(solution)/shard_map/ppermute | solution.py:252
  29.2 6.0 %collective-permute-done.8 = bf16[80,2944]{1,0:T(8,128)(2,1)S(1)} collective-permute-done((bf16[80,2944]{1,0:T(8,128)(2,1)S(1)}, bf16[80,2944]{1,0:T(8,128)(2,1)S(1)}, u32[]{:S(2)}, u32[]{:S(2)}) %collective-permute-start.8) | collective-permute-done | bytes 471072 | tf_op jit(solution)/shard_map/ppermute | solution.py:252
  35.2 2.3 %collective-permute-done.6.refs_3_ = bf16[80,2944]{1,0:T(8,128)(2,1)S(1)} collective-permute-done((bf16[80,2944]{1,0:T(8,128)(2,1)S(1)}, bf16[80,2944]{1,0:T(8,128)(2,1)S(1)}, u32[]{:S(2)}, u32[]{:S(2)}) %collective-permute-start.6) | collective-permute-done | bytes 471072 | tf_op jit(solution)/shard_map/ppermute | solution.py:277
  37.5 1.7 %collective-permute-done.7.refs_4_ = bf16[80,2944]{1,0:T(8,128)(2,1)S(1)} collective-permute-done((bf16[80,2944]{1,0:T(8,128)(2,1)}, bf16[80,2944]{1,0:T(8,128)(2,1)S(1)}, u32[]{:S(2)}, u32[]{:S(2)}) %collective-permute-start.7) | collective-permute-done | bytes 471072 | tf_op jit(solution)/shard_map/ppermute | solution.py:280
  39.5 1.7 %collective-permute-start.9 = (bf16[80,2944]{1,0:T(8,128)(2,1)S(1)}, bf16[80,2944]{1,0:T(8,128)(2,1)S(1)}, u32[]{:S(2)}, u32[]{:S(2)}) collective-permute-start(bf16[80,2944]{1,0:T(8,128)(2,1)S(1)} %collective-permute-done.6.refs_3_), channel_id=1, source_target_pairs={{0,4},{4,8},{8,12},{12,14},{14,10},{10,6},{6,2},{2,0},{1,5},{5,9},... | collective-permute-start | bytes 1413128 | tf_op jit(solution)/shard_map/ppermute | solution.py:277
  41.3 1.6 %collective-permute-start.12 = (bf16[40,2944]{1,0:T(8,128)(2,1)S(1)}, bf16[40,2944]{1,0:T(8,128)(2,1)S(1)}, u32[]{:S(2)}, u32[]{:S(2)}) collective-permute-start(bf16[40,2944]{1,0:T(8,128)(2,1)S(1)} %get-tuple-element.90), channel_id=1, source_target_pairs={{0,4},{4,8},{8,12},{12,14},{14,10},{10,6},{6,2},{2,0},{1,5},{5,9},... | collective-permute-start | bytes 706568 | tf_op jit(solution)/shard_map/ppermute | solution.py:277
  43.4 0.5 collective-permute-done.11
  43.9 1.0 collective-permute-start.16
  44.9 10.5 %collective-permute-done.12 = bf16[40,2944]{1,0:T(8,128)(2,1)S(1)} collective-permute-done((bf16[40,2944]{1,0:T(8,128)(2,1)S(1)}, bf16[40,2944]{1,0:T(8,128)(2,1)S(1)}, u32[]{:S(2)}, u32[]{:S(2)}) %collective-permute-start.12) | collective-permute-done | bytes 235552 | tf_op jit(solution)/shard_map/ppermute | solution.py:277
  55.4 1.7 %collective-permute-start.14 = (bf16[40,2944]{1,0:T(8,128)(2,1)S(1)}, bf16[40,2944]{1,0:T(8,128)(2,1)S(1)}, u32[]{:S(2)}, u32[]{:S(2)}) collective-permute-start(bf16[40,2944]{1,0:T(8,128)(2,1)S(1)} %slice.70), channel_id=1, source_target_pairs={{0,4},{4,8},{8,12},{12,14},{14,10},{10,6},{6,2},{2,0},{1,5},{5,9},... | collective-permute-start | bytes 706568 | tf_op jit(solution)/shard_map/ppermute | solution.py:277
  57.7 1.7 %collective-permute-start.18 = (bf16[40,2944]{1,0:T(8,128)(2,1)S(1)}, bf16[40,2944]{1,0:T(8,128)(2,1)S(1)}, u32[]{:S(2)}, u32[]{:S(2)}) collective-permute-start(bf16[40,2944]{1,0:T(8,128)(2,1)S(1)} %get-tuple-element.88), channel_id=1, source_target_pairs={{0,4},{4,8},{8,12},{12,14},{14,10},{10,6},{6,2},{2,0},{1,5},{5,9},... | collective-permute-start | bytes 706568 | tf_op jit(solution)/shard_map/ppermute | solution.py:277
  59.8 1.6 %collective-permute-start.17 = (bf16[80,2944]{1,0:T(8,128)(2,1)S(1)}, bf16[80,2944]{1,0:T(8,128)(2,1)S(1)}, u32[]{:S(2)}, u32[]{:S(2)}) collective-permute-start(bf16[80,2944]{1,0:T(8,128)(2,1)S(1)} %get-tuple-element.65), channel_id=1, source_target_pairs={{0,16},{16,0},{1,17},{17,1},{2,18},{18,2},{3,19},{19,3},{4,20},{20... | collective-permute-start | bytes 1413128 | tf_op jit(solution)/shard_map/ppermute | solution.py:252
  61.4 1.5 %collective-permute-done.14.refs_7_ = bf16[40,2944]{1,0:T(8,128)(2,1)S(1)} collective-permute-done((bf16[40,2944]{1,0:T(8,128)(2,1)S(1)}, bf16[40,2944]{1,0:T(8,128)(2,1)S(1)}, u32[]{:S(2)}, u32[]{:S(2)}) %collective-permute-start.14) | collective-permute-done | bytes 235552 | tf_op jit(solution)/shard_map/ppermute | solution.py:277
  62.9 0.9 collective-permute-done.15.refs_8_
  63.8 2.2 %collective-permute-done.18 = bf16[40,2944]{1,0:T(8,128)(2,1)S(1)} collective-permute-done((bf16[40,2944]{1,0:T(8,128)(2,1)S(1)}, bf16[40,2944]{1,0:T(8,128)(2,1)S(1)}, u32[]{:S(2)}, u32[]{:S(2)}) %collective-permute-start.18) | collective-permute-done | bytes 235552 | tf_op jit(solution)/shard_map/ppermute | solution.py:277
  66.0 0.5 collective-permute-done.20
  66.7 1.9 %collective-permute-start.19 = (bf16[40,2944]{1,0:T(8,128)(2,1)S(1)}, bf16[40,2944]{1,0:T(8,128)(2,1)S(1)}, u32[]{:S(2)}, u32[]{:S(2)}) collective-permute-start(bf16[40,2944]{1,0:T(8,128)(2,1)S(1)} %get-tuple-element.86), channel_id=1, source_target_pairs={{0,4},{4,8},{8,12},{12,14},{14,10},{10,6},{6,2},{2,0},{1,5},{5,9},... | collective-permute-start | bytes 706568 | tf_op jit(solution)/shard_map/ppermute | solution.py:277
  68.8 1.3 %shard_map.122.whole = bf16[640,2944]{1,0:T(8,128)(2,1)S(1)} custom-call(s32[1]{0:T(128)} %bitcast.dev, s32[32,24]{1,0:T(8,128)S(1)} %copy-done.6, bf16[80,2944]{1,0:T(8,128)(2,1)S(1)} %maximum_select_fusion.refs_0_, bf16[80,2944]{1,0:T(8,128)(2,1)S(1)} %collective-permute-done.3.refs_1_, bf16[80,2944]{1,0:T(8,128)(2,1)} %collective-permute-done.4.refs_2_, ...), custom_call_target="tpu_custom_call" | custom-call | flops 241172480 | tf_op jit(solution)/shard_map/pallas_call | solution.py:390
  70.1 3.1 %shard_map.124 = bf16[512,640]{1,0:T(8,128)(2,1)S(1)} custom-call(s32[1]{0:T(128)} %bitcast.dev, bf16[3,34,32,640]{3,2,1,0:T(8,128)(2,1)S(1)} %get-tuple-element.44.acts, bf16[640,2944]{1,0:T(8,128)(2,1)S(1)} %shard_map.122.whole), custom_call_target="tpu_custom_call" | custom-call | flops 964689920 | tf_op jit(solution)/shard_map/pallas_call | solution.py:402
  73.3 6.6 %shard_map.123 = f32[2,640]{1,0:T(2,128)S(1)} custom-call(s32[1]{0:T(128)} %bitcast.dev, bf16[3,34,32,640]{3,2,1,0:T(8,128)(2,1)S(1)} %get-tuple-element.66.cots, bf16[32,32,640]{2,1,0:T(8,128)(2,1)S(1)} %get-tuple-element.67.slope, bf16[32,32,640]{2,1,0:T(8,128)(2,1)S(1)} %get-tuple-element.68.slope_x, bf16[640,2944]{1,0:T(8,128)(2,1)S(1)} %shard_map.122.whole), custom_call_target="tpu_custom_call" | custom-call | flops 1929379840 | tf_op jit(solution)/shard_map/pallas_call | solution.py:394
  80.0 0.6 collective-permute-start.24
  80.5 0.8 add_convert_fusion.1
  81.3 1.8 %collective-permute-start.22 = (bf16[40,2944]{1,0:T(8,128)(2,1)}, bf16[40,2944]{1,0:T(8,128)(2,1)}, u32[]{:S(2)}, u32[]{:S(2)}) collective-permute-start(bf16[40,2944]{1,0:T(8,128)(2,1)} %add_convert_fusion.1), channel_id=1, source_target_pairs={{0,4},{4,8},{8,12},{12,14},{14,10},{10,6},{6,2},{2,0},{1,5},{5,9},... | collective-permute-start | bytes 706568 | tf_op jit(solution)/shard_map/ppermute | solution.py:277
  83.4 1.5 %collective-permute-start.26 = (f32[3,640]{1,0:T(4,128)S(1)}, f32[3,640]{1,0:T(4,128)S(1)}, u32[]{:S(2)}, u32[]{:S(2)}) collective-permute-start(f32[3,640]{1,0:T(4,128)S(1)} %fusion.9), channel_id=1, source_target_pairs={{0,4},{2,6},{4,0},{6,2},{8,12},{10,14},{12,8},{14,10},{1,5},{3,7},... | collective-permute-start | bytes 23048 | tf_op jit(solution)/shard_map/ppermute | solution.py:302
  84.9 1.8 %collective-permute-start.27 = (f32[3,640]{1,0:T(4,128)S(1)}, f32[3,640]{1,0:T(4,128)S(1)}, u32[]{:S(2)}, u32[]{:S(2)}) collective-permute-start(f32[3,640]{1,0:T(4,128)S(1)} %fusion.9), channel_id=1, source_target_pairs={{0,6},{2,4},{4,2},{6,0},{8,14},{10,12},{12,10},{14,8},{1,7},{3,5},... | collective-permute-start | bytes 23048 | tf_op jit(solution)/shard_map/ppermute | solution.py:302
  87.4 2.1 %collective-permute-done.25 = f32[3,640]{1,0:T(4,128)S(1)} collective-permute-done((f32[3,640]{1,0:T(4,128)S(1)}, f32[3,640]{1,0:T(4,128)S(1)}, u32[]{:S(2)}, u32[]{:S(2)}) %collective-permute-start.25) | collective-permute-done | bytes 7712 | tf_op jit(solution)/shard_map/ppermute | solution.py:302
  89.5 0.7 collective-permute-done.27
  90.2 2.8 %collective-permute-start.30 = (f32[3,640]{1,0:T(4,128)S(1)}, f32[3,640]{1,0:T(4,128)S(1)}, u32[]{:S(2)}, u32[]{:S(2)}) collective-permute-start(f32[3,640]{1,0:T(4,128)S(1)} %add_add_fusion), channel_id=1, source_target_pairs={{0,8},{4,12},{8,0},{12,4},{16,24},{20,28},{24,16},{28,20},{1,9},{5... | collective-permute-start | bytes 23048 | tf_op jit(solution)/shard_map/ppermute | solution.py:302
  93.0 1.5 %collective-permute-start.31 = (f32[3,640]{1,0:T(4,128)S(1)}, f32[3,640]{1,0:T(4,128)S(1)}, u32[]{:S(2)}, u32[]{:S(2)}) collective-permute-start(f32[3,640]{1,0:T(4,128)S(1)} %add_add_fusion), channel_id=1, source_target_pairs={{0,16},{4,20},{8,24},{12,28},{16,0},{20,4},{24,8},{28,12},{1,17},{... | collective-permute-start | bytes 23048 | tf_op jit(solution)/shard_map/ppermute | solution.py:302
  94.7 1.2 %add_convert_fusion = bf16[40,2944]{1,0:T(8,128)(2,1)S(1)} fusion(bf16[40,2944]{1,0:T(8,128)(2,1)} %collective-permute-done.22, bf16[40,2944]{1,0:T(8,128)(2,1)} %copy-done.10, bf16[80,2944]{1,0:T(8,128)(2,1)S(1)} %collective-permute-done.17, bf16[80,2944]{1,0:T(8,128)(2,1)S(1)} %get-tuple-element.64), kind=kLoop, calls=%fused_computation.7 | loop fusion | flops 942080 | bytes 1177600 | tf_op jit(solution)/shard_map/convert_element_type | solution.py:311
  95.9 1.7 %collective-permute-start.28 = (bf16[40,2944]{1,0:T(8,128)(2,1)S(1)}, bf16[40,2944]{1,0:T(8,128)(2,1)S(1)}, u32[]{:S(2)}, u32[]{:S(2)}) collective-permute-start(bf16[40,2944]{1,0:T(8,128)(2,1)S(1)} %add_convert_fusion), channel_id=1, source_target_pairs={{1,0},{16,17},{0,16},{17,1},{3,2},{18,19},{2,18},{19,3},{5,4},{20,... | collective-permute-start | bytes 706568 | tf_op jit(solution)/shard_map/ppermute | solution.py:440
  97.5 0.7 collective-permute-start.29
  98.2 2.1 %copy-done.1 = bf16[640,2944]{1,0:T(8,128)(2,1)S(1)} copy-done((bf16[640,2944]{1,0:T(8,128)(2,1)S(1)}, bf16[640,2944]{1,0:T(8,128)(2,1)}, u32[]{:S(2)}) %copy-start.1) | copy-done | bytes 3768344
  100.3 2.2 %copy-done.3 = bf16[3,34,32,640]{3,2,1,0:T(8,128)(2,1)S(1)} copy-done((bf16[3,34,32,640]{3,2,1,0:T(8,128)(2,1)S(1)}, bf16[3,34,32,640]{3,2,1,0:T(8,128)(2,1)}, u32[]{:S(2)}) %copy-start.3) | copy-done | bytes 4177944
  102.5 4.2 %shard_map.125 = bf16[16,32,640]{2,1,0:T(8,128)(2,1)} custom-call(s32[1]{0:T(128)} %bitcast.dev, bf16[3,34,32,640]{3,2,1,0:T(8,128)(2,1)S(1)} %copy-done.3, bf16[640,2944]{1,0:T(8,128)(2,1)S(1)} %copy-done.1, bf16[512,640]{1,0:T(8,128)(2,1)S(1)} %collective-permute-done.23.got, bf16[16,32,640]{2,1,0:T(8,128)(2,1)S(1)} %bitcast.24, f32[1,640]{1,0:T(1,128)S(1)} %copy-done.5), custom_call_target="tpu_custom_call" | custom-call | flops 964689920 | tf_op jit(solution)/shard_map/pallas_call | solution.py:459
  106.7 0.6 fusion.8
  107.8 1.1 %fusion.2 = f32[1,40,5760]{2,1,0:T(8,128)} fusion(f32[1,40,5760]{2,1,0:T(8,128)S(1)} %copy-done.9, bf16[40,5760]{1,0:T(8,128)(2,1)S(1)} %collective-permute-done.5, bf16[40,2816]{1,0:T(8,128)(2,1)S(1)} %fusion.5, bf16[40,2944]{1,0:T(8,128)(2,1)S(1)} %select_select_fusion, f32[]{:T(128)S(6)} %mul_shard_map.4), kind=kLoop, calls=%fused_computation.4 | loop fusion | flops 2073600 | bytes 2764804 | tf_op jit(solution)/shard_map/broadcast_in_dim | solution.py:472
  (67 shorter events, 3.9 us)
Async XLA Ops:
  0.6 4.0 %copy-start.4 = (bf16[1,16,32,640]{3,2,1,0:T(8,128)(2,1)S(1)}, bf16[1,16,32,640]{3,2,1,0:T(8,128)(2,1)}, u32[]{:S(2)}) copy-start(bf16[1,16,32,640]{3,2,1,0:T(8,128)(2,1)} %param.8) | copy-start | bytes 1966084
  1.9 3.2 %collective-permute-start.2 = (bf16[40,2944]{1,0:T(8,128)(2,1)S(1)}, bf16[40,2944]{1,0:T(8,128)(2,1)S(1)}, u32[]{:S(2)}, u32[]{:S(2)}) collective-permute-start(bf16[40,2944]{1,0:T(8,128)(2,1)S(1)} %get-tuple-element.92), channel_id=1, source_target_pairs={{0,1},{1,0},{2,3},{3,2},{4,5},{5,4},{6,7},{7,6},{8,9},{9,8},{10,11... | collective-permute-start | bytes 706568 | tf_op jit(solution)/shard_map/ppermute | solution.py:252
  4.5 7.4 %copy-start.6 = (s32[32,24]{1,0:T(8,128)S(1)}, s32[32,24]{1,0:T(8,128)}, u32[]{:S(2)}) copy-start(s32[32,24]{1,0:T(8,128)} %constant.61.clone.table) | copy-start | bytes 9220
  4.5 7.4 %copy-start.7 = (f32[1,640]{1,0:T(1,128)S(1)}, f32[1,640]{1,0:T(1,128)}, u32[]{:S(2)}) copy-start(f32[1,640]{1,0:T(1,128)} %gain.3) | copy-start | bytes 7684
  4.5 7.4 %copy-start.8 = (f32[1,640]{1,0:T(1,128)S(1)}, f32[1,640]{1,0:T(1,128)}, u32[]{:S(2)}) copy-start(f32[1,640]{1,0:T(1,128)} %shift.3) | copy-start | bytes 7684
  4.6 7.3 %collective-permute-start.1 = (bf16[16,32,640]{2,1,0:T(8,128)(2,1)S(1)}, bf16[16,32,640]{2,1,0:T(8,128)(2,1)}, u32[]{:S(2)}, u32[]{:S(2)}) collective-permute-start(bf16[16,32,640]{2,1,0:T(8,128)(2,1)S(1)} %get-tuple-element.84.cot_own), channel_id=1, source_target_pairs={{0,1},{1,0},{2,3},{3,2},{4,5},{5,4},{6,7},{7,6},{8,9},{9,8},{10,11... | collective-permute-start | bytes 1966088 | tf_op jit(solution)/shard_map/ppermute | solution.py:252
  4.7 7.2 %collective-permute-start = (bf16[16,32,640]{2,1,0:T(8,128)(2,1)S(1)}, bf16[16,32,640]{2,1,0:T(8,128)(2,1)}, u32[]{:S(2)}, u32[]{:S(2)}) collective-permute-start(bf16[16,32,640]{2,1,0:T(8,128)(2,1)S(1)} %bitcast.21), channel_id=1, source_target_pairs={{0,1},{1,0},{2,3},{3,2},{4,5},{5,4},{6,7},{7,6},{8,9},{9,8},{10,11... | collective-permute-start | bytes 1966088 | tf_op jit(solution)/shard_map/ppermute | solution.py:252
  5.2 19.9 %collective-permute-start.3 = (bf16[80,2944]{1,0:T(8,128)(2,1)S(1)}, bf16[80,2944]{1,0:T(8,128)(2,1)S(1)}, u32[]{:S(2)}, u32[]{:S(2)}) collective-permute-start(bf16[80,2944]{1,0:T(8,128)(2,1)S(1)} %maximum_select_fusion.refs_0_), channel_id=1, source_target_pairs={{0,4},{4,8},{8,12},{12,14},{14,10},{10,6},{6,2},{2,0},{1,5},{5,9},... | collective-permute-start | bytes 1413128 | tf_op jit(solution)/shard_map/ppermute | solution.py:277
  7.9 17.2 %collective-permute-start.4 = (bf16[80,2944]{1,0:T(8,128)(2,1)S(1)}, bf16[80,2944]{1,0:T(8,128)(2,1)}, u32[]{:S(2)}, u32[]{:S(2)}) collective-permute-start(bf16[80,2944]{1,0:T(8,128)(2,1)S(1)} %maximum_select_fusion.refs_0_), channel_id=1, source_target_pairs={{4,0},{8,4},{12,8},{14,12},{10,14},{6,10},{2,6},{0,2},{5,1},{9,5},... | collective-permute-start | bytes 1413128 | tf_op jit(solution)/shard_map/ppermute | solution.py:280
  9.9 15.2 %collective-permute-start.5 = (bf16[40,5760]{1,0:T(8,128)(2,1)}, bf16[40,5760]{1,0:T(8,128)(2,1)S(1)}, u32[]{:S(2)}, u32[]{:S(2)}) collective-permute-start(bf16[40,5760]{1,0:T(8,128)(2,1)} %bitcast_convert_fusion), channel_id=1, source_target_pairs={{0,16},{16,0},{1,17},{17,1},{2,18},{18,2},{3,19},{19,3},{4,20},{20... | collective-permute-start | bytes 1382408 | tf_op jit(solution)/shard_map/ppermute | solution.py:260
  16.8 53.3 %copy-start.2 = (bf16[3,34,32,640]{3,2,1,0:T(8,128)(2,1)}, bf16[3,34,32,640]{3,2,1,0:T(8,128)(2,1)S(1)}, u32[]{:S(2)}) copy-start(bf16[3,34,32,640]{3,2,1,0:T(8,128)(2,1)S(1)} %get-tuple-element.44.acts) | copy-start | bytes 12533764
  21.4 13.8 %collective-permute-start.8 = (bf16[80,2944]{1,0:T(8,128)(2,1)S(1)}, bf16[80,2944]{1,0:T(8,128)(2,1)S(1)}, u32[]{:S(2)}, u32[]{:S(2)}) collective-permute-start(bf16[80,2944]{1,0:T(8,128)(2,1)S(1)} %get-tuple-element.47), channel_id=1, source_target_pairs={{0,16},{16,0},{1,17},{17,1},{2,18},{18,2},{3,19},{19,3},{4,20},{20... | collective-permute-start | bytes 1413128 | tf_op jit(solution)/shard_map/ppermute | solution.py:252
  25.2 12.3 %collective-permute-start.6 = (bf16[80,2944]{1,0:T(8,128)(2,1)S(1)}, bf16[80,2944]{1,0:T(8,128)(2,1)S(1)}, u32[]{:S(2)}, u32[]{:S(2)}) collective-permute-start(bf16[80,2944]{1,0:T(8,128)(2,1)S(1)} %collective-permute-done.3.refs_1_), channel_id=1, source_target_pairs={{0,4},{4,8},{8,12},{12,14},{14,10},{10,6},{6,2},{2,0},{1,5},{5,9},... | collective-permute-start | bytes 1413128 | tf_op jit(solution)/shard_map/ppermute | solution.py:277
  27.2 11.9 %collective-permute-start.7 = (bf16[80,2944]{1,0:T(8,128)(2,1)}, bf16[80,2944]{1,0:T(8,128)(2,1)S(1)}, u32[]{:S(2)}, u32[]{:S(2)}) collective-permute-start(bf16[80,2944]{1,0:T(8,128)(2,1)} %collective-permute-done.4.refs_2_), channel_id=1, source_target_pairs={{4,0},{8,4},{12,8},{14,12},{10,14},{6,10},{2,6},{0,2},{5,1},{9,5},... | collective-permute-start | bytes 1413128 | tf_op jit(solution)/shard_map/ppermute | solution.py:280
  27.2 16.6 %collective-permute-start.11 = (bf16[80,2944]{1,0:T(8,128)(2,1)S(1)}, bf16[80,2944]{1,0:T(8,128)(2,1)S(1)}, u32[]{:S(2)}, u32[]{:S(2)}) collective-permute-start(bf16[80,2944]{1,0:T(8,128)(2,1)S(1)} %get-tuple-element.56), channel_id=1, source_target_pairs={{0,16},{16,0},{1,17},{17,1},{2,18},{18,2},{3,19},{19,3},{4,20},{20... | collective-permute-start | bytes 1413128 | tf_op jit(solution)/shard_map/ppermute | solution.py:252
  39.2 16.2 %collective-permute-start.10 = (bf16[80,2944]{1,0:T(8,128)(2,1)S(1)}, bf16[80,2944]{1,0:T(8,128)(2,1)S(1)}, u32[]{:S(2)}, u32[]{:S(2)}) collective-permute-start(bf16[80,2944]{1,0:T(8,128)(2,1)S(1)} %collective-permute-done.7.refs_4_), channel_id=1, source_target_pairs={{4,0},{8,4},{12,8},{14,12},{10,14},{6,10},{2,6},{0,2},{5,1},{9,5},... | collective-permute-start | bytes 1413128 | tf_op jit(solution)/shard_map/ppermute | solution.py:280
  39.5 15.9 %collective-permute-start.9 = (bf16[80,2944]{1,0:T(8,128)(2,1)S(1)}, bf16[80,2944]{1,0:T(8,128)(2,1)S(1)}, u32[]{:S(2)}, u32[]{:S(2)}) collective-permute-start(bf16[80,2944]{1,0:T(8,128)(2,1)S(1)} %collective-permute-done.6.refs_3_), channel_id=1, source_target_pairs={{0,4},{4,8},{8,12},{12,14},{14,10},{10,6},{6,2},{2,0},{1,5},{5,9},... | collective-permute-start | bytes 1413128 | tf_op jit(solution)/shard_map/ppermute | solution.py:277
  41.3 14.1 %collective-permute-start.12 = (bf16[40,2944]{1,0:T(8,128)(2,1)S(1)}, bf16[40,2944]{1,0:T(8,128)(2,1)S(1)}, u32[]{:S(2)}, u32[]{:S(2)}) collective-permute-start(bf16[40,2944]{1,0:T(8,128)(2,1)S(1)} %get-tuple-element.90), channel_id=1, source_target_pairs={{0,4},{4,8},{8,12},{12,14},{14,10},{10,6},{6,2},{2,0},{1,5},{5,9},... | collective-permute-start | bytes 706568 | tf_op jit(solution)/shard_map/ppermute | solution.py:277
  42.9 12.4 %collective-permute-start.13 = (bf16[40,2944]{1,0:T(8,128)(2,1)S(1)}, bf16[40,2944]{1,0:T(8,128)(2,1)S(1)}, u32[]{:S(2)}, u32[]{:S(2)}) collective-permute-start(bf16[40,2944]{1,0:T(8,128)(2,1)S(1)} %get-tuple-element.89), channel_id=1, source_target_pairs={{4,0},{8,4},{12,8},{14,12},{10,14},{6,10},{2,6},{0,2},{5,1},{9,5},... | collective-permute-start | bytes 706568 | tf_op jit(solution)/shard_map/ppermute | solution.py:280
  43.9 16.0 %collective-permute-start.16 = (bf16[80,2944]{1,0:T(8,128)(2,1)S(1)}, bf16[80,2944]{1,0:T(8,128)(2,1)S(1)}, u32[]{:S(2)}, u32[]{:S(2)}) collective-permute-start(bf16[80,2944]{1,0:T(8,128)(2,1)S(1)} %get-tuple-element.61), channel_id=1, source_target_pairs={{0,16},{16,0},{1,17},{17,1},{2,18},{18,2},{3,19},{19,3},{4,20},{20... | collective-permute-start | bytes 1413128 | tf_op jit(solution)/shard_map/ppermute | solution.py:252
  55.4 7.5 %collective-permute-start.14 = (bf16[40,2944]{1,0:T(8,128)(2,1)S(1)}, bf16[40,2944]{1,0:T(8,128)(2,1)S(1)}, u32[]{:S(2)}, u32[]{:S(2)}) collective-permute-start(bf16[40,2944]{1,0:T(8,128)(2,1)S(1)} %slice.70), channel_id=1, source_target_pairs={{0,4},{4,8},{8,12},{12,14},{14,10},{10,6},{6,2},{2,0},{1,5},{5,9},... | collective-permute-start | bytes 706568 | tf_op jit(solution)/shard_map/ppermute | solution.py:277
  57.1 6.7 %collective-permute-start.15 = (bf16[40,2944]{1,0:T(8,128)(2,1)S(1)}, bf16[40,2944]{1,0:T(8,128)(2,1)S(1)}, u32[]{:S(2)}, u32[]{:S(2)}) collective-permute-start(bf16[40,2944]{1,0:T(8,128)(2,1)S(1)} %slice.71), channel_id=1, source_target_pairs={{4,0},{8,4},{12,8},{14,12},{10,14},{6,10},{2,6},{0,2},{5,1},{9,5},... | collective-permute-start | bytes 706568 | tf_op jit(solution)/shard_map/ppermute | solution.py:280
  57.7 8.3 %collective-permute-start.18 = (bf16[40,2944]{1,0:T(8,128)(2,1)S(1)}, bf16[40,2944]{1,0:T(8,128)(2,1)S(1)}, u32[]{:S(2)}, u32[]{:S(2)}) collective-permute-start(bf16[40,2944]{1,0:T(8,128)(2,1)S(1)} %get-tuple-element.88), channel_id=1, source_target_pairs={{0,4},{4,8},{8,12},{12,14},{14,10},{10,6},{6,2},{2,0},{1,5},{5,9},... | collective-permute-start | bytes 706568 | tf_op jit(solution)/shard_map/ppermute | solution.py:277
  59.4 7.1 %collective-permute-start.20 = (bf16[40,2944]{1,0:T(8,128)(2,1)S(1)}, bf16[40,2944]{1,0:T(8,128)(2,1)S(1)}, u32[]{:S(2)}, u32[]{:S(2)}) collective-permute-start(bf16[40,2944]{1,0:T(8,128)(2,1)S(1)} %get-tuple-element.87), channel_id=1, source_target_pairs={{4,0},{8,4},{12,8},{14,12},{10,14},{6,10},{2,6},{0,2},{5,1},{9,5},... | collective-permute-start | bytes 706568 | tf_op jit(solution)/shard_map/ppermute | solution.py:280
  59.8 20.1 %collective-permute-start.17 = (bf16[80,2944]{1,0:T(8,128)(2,1)S(1)}, bf16[80,2944]{1,0:T(8,128)(2,1)S(1)}, u32[]{:S(2)}, u32[]{:S(2)}) collective-permute-start(bf16[80,2944]{1,0:T(8,128)(2,1)S(1)} %get-tuple-element.65), channel_id=1, source_target_pairs={{0,16},{16,0},{1,17},{17,1},{2,18},{18,2},{3,19},{19,3},{4,20},{20... | collective-permute-start | bytes 1413128 | tf_op jit(solution)/shard_map/ppermute | solution.py:252
  66.7 13.2 %collective-permute-start.19 = (bf16[40,2944]{1,0:T(8,128)(2,1)S(1)}, bf16[40,2944]{1,0:T(8,128)(2,1)S(1)}, u32[]{:S(2)}, u32[]{:S(2)}) collective-permute-start(bf16[40,2944]{1,0:T(8,128)(2,1)S(1)} %get-tuple-element.86), channel_id=1, source_target_pairs={{0,4},{4,8},{8,12},{12,14},{14,10},{10,6},{6,2},{2,0},{1,5},{5,9},... | collective-permute-start | bytes 706568 | tf_op jit(solution)/shard_map/ppermute | solution.py:277
  68.6 11.3 %collective-permute-start.21 = (bf16[40,2944]{1,0:T(8,128)(2,1)S(1)}, bf16[40,2944]{1,0:T(8,128)(2,1)S(1)}, u32[]{:S(2)}, u32[]{:S(2)}) collective-permute-start(bf16[40,2944]{1,0:T(8,128)(2,1)S(1)} %get-tuple-element.85), channel_id=1, source_target_pairs={{4,0},{8,4},{12,8},{14,12},{10,14},{6,10},{2,6},{0,2},{5,1},{9,5},... | collective-permute-start | bytes 706568 | tf_op jit(solution)/shard_map/ppermute | solution.py:280
  70.1 3.2 %copy-start = (bf16[640,2944]{1,0:T(8,128)(2,1)}, bf16[640,2944]{1,0:T(8,128)(2,1)S(1)}, u32[]{:S(2)}) copy-start(bf16[640,2944]{1,0:T(8,128)(2,1)S(1)} %shard_map.122.whole) | copy-start | bytes 11304964
  73.2 6.7 %copy-start.5 = (f32[1,640]{1,0:T(1,128)S(1)}, f32[1,640]{1,0:T(1,128)}, u32[]{:S(2)}) copy-start(f32[1,640]{1,0:T(1,128)} %bias.1) | copy-start | bytes 7684
  73.2 17.0 %collective-permute-start.23 = (bf16[512,640]{1,0:T(8,128)(2,1)S(1)}, bf16[512,640]{1,0:T(8,128)(2,1)S(1)}, u32[]{:S(2)}, u32[]{:S(2)}) collective-permute-start(bf16[512,640]{1,0:T(8,128)(2,1)S(1)} %shard_map.124), channel_id=1, source_target_pairs={{0,1},{1,0},{2,3},{3,2},{4,5},{5,4},{6,7},{7,6},{8,9},{9,8},{10,11... | collective-permute-start | bytes 1966088 | tf_op jit(solution)/shard_map/ppermute | solution.py:252
  79.9 3.2 %copy-start.10 = (bf16[40,2944]{1,0:T(8,128)(2,1)}, bf16[40,2944]{1,0:T(8,128)(2,1)S(1)}, u32[]{:S(2)}) copy-start(bf16[40,2944]{1,0:T(8,128)(2,1)S(1)} %collective-permute-done.21) | copy-start | bytes 706564
  80.0 3.2 %collective-permute-start.24 = (f32[3,640]{1,0:T(4,128)S(1)}, f32[3,640]{1,0:T(4,128)S(1)}, u32[]{:S(2)}, u32[]{:S(2)}) collective-permute-start(f32[3,640]{1,0:T(4,128)S(1)} %fusion.6), channel_id=1, source_target_pairs={{0,1},{1,0},{2,3},{3,2},{4,5},{5,4},{6,7},{7,6},{8,9},{9,8},{10,11... | collective-permute-start | bytes 23048 | tf_op jit(solution)/shard_map/ppermute | solution.py:252
  81.3 8.9 %collective-permute-start.22 = (bf16[40,2944]{1,0:T(8,128)(2,1)}, bf16[40,2944]{1,0:T(8,128)(2,1)}, u32[]{:S(2)}, u32[]{:S(2)}) collective-permute-start(bf16[40,2944]{1,0:T(8,128)(2,1)} %add_convert_fusion.1), channel_id=1, source_target_pairs={{0,4},{4,8},{8,12},{12,14},{14,10},{10,6},{6,2},{2,0},{1,5},{5,9},... | collective-permute-start | bytes 706568 | tf_op jit(solution)/shard_map/ppermute | solution.py:277
  83.2 6.3 %collective-permute-start.25 = (f32[3,640]{1,0:T(4,128)S(1)}, f32[3,640]{1,0:T(4,128)S(1)}, u32[]{:S(2)}, u32[]{:S(2)}) collective-permute-start(f32[3,640]{1,0:T(4,128)S(1)} %fusion.9), channel_id=1, source_target_pairs={{0,2},{2,0},{4,6},{6,4},{8,10},{10,8},{12,14},{14,12},{1,3},{3,1},... | collective-permute-start | bytes 23048 | tf_op jit(solution)/shard_map/ppermute | solution.py:302
  83.4 6.1 %collective-permute-start.26 = (f32[3,640]{1,0:T(4,128)S(1)}, f32[3,640]{1,0:T(4,128)S(1)}, u32[]{:S(2)}, u32[]{:S(2)}) collective-permute-start(f32[3,640]{1,0:T(4,128)S(1)} %fusion.9), channel_id=1, source_target_pairs={{0,4},{2,6},{4,0},{6,2},{8,12},{10,14},{12,8},{14,10},{1,5},{3,7},... | collective-permute-start | bytes 23048 | tf_op jit(solution)/shard_map/ppermute | solution.py:302
  84.9 5.3 %collective-permute-start.27 = (f32[3,640]{1,0:T(4,128)S(1)}, f32[3,640]{1,0:T(4,128)S(1)}, u32[]{:S(2)}, u32[]{:S(2)}) collective-permute-start(f32[3,640]{1,0:T(4,128)S(1)} %fusion.9), channel_id=1, source_target_pairs={{0,6},{2,4},{4,2},{6,0},{8,14},{10,12},{12,10},{14,8},{1,7},{3,5},... | collective-permute-start | bytes 23048 | tf_op jit(solution)/shard_map/ppermute | solution.py:302
  90.2 16.4 %collective-permute-start.30 = (f32[3,640]{1,0:T(4,128)S(1)}, f32[3,640]{1,0:T(4,128)S(1)}, u32[]{:S(2)}, u32[]{:S(2)}) collective-permute-start(f32[3,640]{1,0:T(4,128)S(1)} %add_add_fusion), channel_id=1, source_target_pairs={{0,8},{4,12},{8,0},{12,4},{16,24},{20,28},{24,16},{28,20},{1,9},{5... | collective-permute-start | bytes 23048 | tf_op jit(solution)/shard_map/ppermute | solution.py:302
  93.0 13.6 %collective-permute-start.31 = (f32[3,640]{1,0:T(4,128)S(1)}, f32[3,640]{1,0:T(4,128)S(1)}, u32[]{:S(2)}, u32[]{:S(2)}) collective-permute-start(f32[3,640]{1,0:T(4,128)S(1)} %add_add_fusion), channel_id=1, source_target_pairs={{0,16},{4,20},{8,24},{12,28},{16,0},{20,4},{24,8},{28,12},{1,17},{... | collective-permute-start | bytes 23048 | tf_op jit(solution)/shard_map/ppermute | solution.py:302
  94.5 12.1 %collective-permute-start.32 = (f32[3,640]{1,0:T(4,128)S(1)}, f32[3,640]{1,0:T(4,128)S(1)}, u32[]{:S(2)}, u32[]{:S(2)}) collective-permute-start(f32[3,640]{1,0:T(4,128)S(1)} %add_add_fusion), channel_id=1, source_target_pairs={{0,24},{4,28},{8,16},{12,20},{16,8},{20,12},{24,0},{28,4},{1,25},{... | collective-permute-start | bytes 23048 | tf_op jit(solution)/shard_map/ppermute | solution.py:302
  95.9 11.4 %collective-permute-start.28 = (bf16[40,2944]{1,0:T(8,128)(2,1)S(1)}, bf16[40,2944]{1,0:T(8,128)(2,1)S(1)}, u32[]{:S(2)}, u32[]{:S(2)}) collective-permute-start(bf16[40,2944]{1,0:T(8,128)(2,1)S(1)} %add_convert_fusion), channel_id=1, source_target_pairs={{1,0},{16,17},{0,16},{17,1},{3,2},{18,19},{2,18},{19,3},{5,4},{20,... | collective-permute-start | bytes 706568 | tf_op jit(solution)/shard_map/ppermute | solution.py:440
  97.5 9.7 %collective-permute-start.29 = (bf16[40,2944]{1,0:T(8,128)(2,1)S(1)}, bf16[40,2944]{1,0:T(8,128)(2,1)S(1)}, u32[]{:S(2)}, u32[]{:S(2)}) collective-permute-start(bf16[40,2944]{1,0:T(8,128)(2,1)S(1)} %add_convert_fusion), channel_id=1, source_target_pairs={{1,16},{16,1},{3,18},{18,3},{5,20},{20,5},{7,22},{22,7},{9,24},{24... | collective-permute-start | bytes 706568 | tf_op jit(solution)/shard_map/ppermute | solution.py:441
  98.2 2.1 %copy-start.1 = (bf16[640,2944]{1,0:T(8,128)(2,1)S(1)}, bf16[640,2944]{1,0:T(8,128)(2,1)}, u32[]{:S(2)}) copy-start(bf16[640,2944]{1,0:T(8,128)(2,1)} %copy-done) | copy-start | bytes 11304964
  100.3 2.2 %copy-start.3 = (bf16[3,34,32,640]{3,2,1,0:T(8,128)(2,1)S(1)}, bf16[3,34,32,640]{3,2,1,0:T(8,128)(2,1)}, u32[]{:S(2)}) copy-start(bf16[3,34,32,640]{3,2,1,0:T(8,128)(2,1)} %copy-done.2) | copy-start | bytes 12533764
  106.6 1.2 %copy-start.9 = (f32[1,40,5760]{2,1,0:T(8,128)S(1)}, f32[1,40,5760]{2,1,0:T(8,128)}, u32[]{:S(2)}) copy-start(f32[1,40,5760]{2,1,0:T(8,128)} %param.10) | copy-start | bytes 2764804

commit v6 on v5

--- a/solution.py
+++ b/solution.py
@@ -142,16 +142,60 @@
     emit(acts[1, 1:rows + 1, :, pl.ds(channel, cols.mid)].reshape(cells, cols.mid), place, cols.mid)
 
 
-def slope_kernel(dev, stats, gain, shift, lat_own, lat_far, cot_own, cot_far, cots, slope, slope_x):
-    core = dev[0] % 2
-    half = lat_own.shape[0]
+class Stages:
+    def __init__(self, counts, rows):
+        self.rows = rows
+        self.counts = counts
+        self.widths = [-(-n * rows // LANES) * LANES for n in counts]
+        self.starts = [sum(self.widths[:i]) for i in range(len(counts))]
+        self.width = sum(self.widths)
+
+    def lanes(self, stage):
+        return slice(self.starts[stage], self.starts[stage] + self.widths[stage])
+
+    def columns(self, stage, blocks, place, wide):
+        parts = [ref[:, pl.ds(place, wide)] for ref in blocks]
+        if len(parts) == self.counts[stage] + 1:
+            parts[-2:] = [jnp.concatenate(parts[-2:])]
+        spare = self.widths[stage] - self.counts[stage] * self.rows
+        if spare:
+            parts.append(jnp.zeros((spare, wide), BF16))
+        return jnp.concatenate(parts) if len(parts) > 1 else parts[0]
+
+    def order(self, me, table, order, chans):
+        lane = lax.broadcasted_iota(jnp.int32, (1, self.width), 1)
+        source = jnp.full((1, self.width), -1, jnp.int32)
+        at = 0
+        for start, count in zip(self.starts, self.counts):
+            for i in range(count):
+                first = start + i * self.rows
+                inside = (lane >= first) & (lane < first + self.rows)
+                source = jnp.where(inside, table[me, at] * self.rows + lane - first, source)
+                at += 1
+        channel = lax.broadcasted_iota(jnp.int32, (chans, self.width), 0)
+        order[...] = jnp.where(channel == source, 1.0, 0.0).astype(BF16)
+
+
+def slope_kernel(stages, dev, table, stats, gain, shift, lat_own, lat_far, cot_own, cot_far,
+                 cots, slope, slope_x, *refs):
+    me = dev[0]
+    core = me % 2
+    half, width, chans = lat_own.shape
     clear_edges(cots)
     mean, rstd = stats[0:1], stats[1:2]
     gain_v, shift_v = gain[...], shift[...]
+    far_at = half - core * half
+    if len(stages.counts) > 1:
+        order, placed = refs
+        stages.order(me, table, order, chans)
+        for ref, base in ((cot_own, core * half), (cot_far, far_at)):
+            value = jnp.dot(ref[...].reshape(half * width, chans), order[...], preferred_element_type=F32)
+            placed[pl.ds(base, half)] = value.reshape(half, width, stages.width)
 
     def one_row(i, _):
-        for lat, cot, base in ((lat_own, cot_own, core * half), (lat_far, cot_far, half - core * half)):
-            fill_shifts(cots, base + i + 1, cot[i].astype(F32))
+        for lat, cot, base in ((lat_own, cot_own, core * half), (lat_far, cot_far, far_at)):
+            value = placed[base + i] if len(stages.counts) > 1 else cot[i].astype(F32)
+            fill_shifts(cots, base + i + 1, value)
             xhat = (lat[i].astype(F32) - mean) * rstd
             pre = gain_v * xhat + shift_v
             sig = 0.5 + 0.5 * jnp.tanh(0.5 * pre)
@@ -163,17 +207,7 @@
     lax.fori_loop(0, half, one_row, 0)
 
 
-def place_kernel(dev, table, *refs):
-    blocks, whole = list(refs[:-1]), refs[-1]
-    if blocks[-1].shape != blocks[0].shape:
-        blocks[-2:] = [jnp.concatenate([blocks[-2][...], blocks[-1][...]])]
-    for i, block in enumerate(blocks):
-        count = block.shape[0]
-        at = pl.multiple_of(table[dev[0], i] * count, count)
-        whole[pl.ds(at, count)] = block[...]
-
-
-def conv_sum(cols, core, first, half, acts, whole, total):
+def conv_sum(cols, stages, stage, core, first, half, acts, blocks, total):
     width, chans = acts.shape[2:]
     cells = half * width
     nt = (((1,), (1,)), ((), ()))
@@ -181,68 +215,115 @@
     window = acts[1, pl.ds(first + 1, half), :, pl.ds(channel, cols.mid)].reshape(cells, cols.mid)
     lane = lax.broadcasted_iota(jnp.int32, window.shape, 1)
     window = jnp.where((core == 1) & (lane < cols.both), jnp.zeros_like(window), window)
-    total[...] = lax.dot_general(window, whole[:, pl.ds(place, cols.mid)], nt, preferred_element_type=F32)
+    kernel = stages.columns(stage, blocks, place, cols.mid)
+    total[...] = lax.dot_general(window, kernel, nt, preferred_element_type=F32)
 
     def two_taps(k, _):
         taps, place = cols.pair(core, k, chans)
         windows = [acts[t % 3, pl.ds(first + t // 3, half)].reshape(cells, chans) for t in taps]
+        kernel = stages.columns(stage, blocks, place, 2 * chans)
         total[...] += lax.dot_general(
-            jnp.concatenate(windows, axis=1), whole[:, pl.ds(place, 2 * chans)], nt, preferred_element_type=F32
+            jnp.concatenate(windows, axis=1), kernel, nt, preferred_element_type=F32
         )
         return 0
 
     lax.fori_loop(0, 2, two_taps, 0)
 
 
-def conv_far_kernel(cols, dev, acts, whole, far, total):
+def conv_both_kernel(cols, stages, stage, dev, acts, *refs):
+    blocks, (own, far, total) = refs[:-3], refs[-3:]
+    core = dev[0] % 2
+    rows = acts.shape[1] - 2
+    conv_sum(cols, stages, stage, core, 0, rows, acts, blocks, total)
+    half = own.shape[0]
+    own[...] = total[pl.ds(pl.multiple_of(core * half, half), half)]
+    far[...] = total[pl.ds(pl.multiple_of((1 - core) * half, half), half)].astype(BF16)
+
+
+def conv_far_kernel(cols, stages, stage, dev, acts, *refs):
+    blocks, (far, total) = refs[:-2], refs[-2:]
     core = dev[0] % 2
     half = (acts.shape[1] - 2) // 2
-    conv_sum(cols, core, (1 - core) * half, half, acts, whole, total)
+    conv_sum(cols, stages, stage, core, (1 - core) * half, half, acts, blocks, total)
     far[...] = total[...].astype(BF16)
 
 
-def conv_own_kernel(cols, dev, acts, whole, got, latent, bias, block, total):
+def conv_own_kernel(cols, stages, dev, acts, got, latent, bias, *refs):
     core = dev[0] % 2
     half, width, chans = latent.shape
-    conv_sum(cols, core, core * half, half, acts, whole, total)
     scale = cols.total ** (-0.5)
-    conv = scale * (total[...] + got[...].astype(F32)) + bias[...]
+    stage = len(stages.counts) - 1
+    before = 3 * stage
+    blocks, (block, total) = refs[before:-2], refs[-2:]
+    conv_sum(cols, stages, stage, core, core * half, half, acts, blocks, total)
+    conv = total[...] + got[...].astype(F32)
+    if stage:
+        first_own, first_got, order = refs[:before]
+        conv = jnp.concatenate([first_own[...] + first_got[...].astype(F32), conv], axis=1)
+        high = conv.astype(BF16)
+        low = (conv - high.astype(F32)).astype(BF16)
+        nt = (((1,), (1,)), ((), ()))
+        conv = sum(
+            lax.dot_general(value, order[...], nt, preferred_element_type=F32) for value in (low, high)
+        )
+    conv = scale * conv + bias[...]
     block[...] = (conv.reshape(half, width, chans) + latent[...].astype(F32)).astype(BF16)
 
 
-def back_kernel(cols, dev, cots, slope, slope_x, whole, sums, total):
+def back_kernel(cols, stages, stage, dev, cots, *refs):
+    last = stage == len(stages.counts) - 1
+    before = (1 if stage else 0) + (2 if last else 0)
+    blocks = refs[before:-2] if last else refs[before:-1]
+    total = refs[-1]
     core = dev[0] % 2
-    rows, width, chans = slope.shape
-    cells = rows * width
-    total[...] = jnp.zeros_like(total)
+    rows, width = cots.shape[1] - 2, cots.shape[2]
+    cells, chans = total.shape
+    lanes = stages.lanes(stage)
+
+    total[...] = refs[0][...] if stage else jnp.zeros_like(total)
     place, channel = cols.middle(core, chans)
-    window = cots[1, 1:rows + 1].reshape(cells, chans)
-    value = jnp.dot(window, whole[:, pl.ds(place, cols.mid)], preferred_element_type=F32)
+    window = cots[1, 1:rows + 1, :, lanes].reshape(cells, stages.widths[stage])
+    kernel = stages.columns(stage, blocks, place, cols.mid)
+    value = jnp.dot(window, kernel, preferred_element_type=F32)
     lane = lax.broadcasted_iota(jnp.int32, value.shape, 1)
-    total[:, pl.ds(channel, cols.mid)] = jnp.where((core == 1) & (lane < cols.both), 0.0, value)
+    total[:, pl.ds(channel, cols.mid)] += jnp.where((core == 1) & (lane < cols.both), 0.0, value)
+
+    def taps_from(first, place, count):
+        windows, kernels = [], []
+        for i in range(count):
+            tap = first + i
+            window = cots[2 - tap % 3, pl.ds(2 - tap // 3, rows), :, lanes]
+            windows.append(window.reshape(cells, stages.widths[stage]))
+            kernels.append(stages.columns(stage, blocks, pl.multiple_of(place + i * chans, LANES), chans))
+        total[...] += jnp.dot(
+            jnp.concatenate(windows, axis=1), jnp.concatenate(kernels), preferred_element_type=F32
+        )
 
     def two_taps(k, _):
         taps, place = cols.pair(core, k, chans)
-        windows = [cots[2 - t % 3, pl.ds(2 - t // 3, rows)].reshape(cells, chans) for t in taps]
-        second = pl.multiple_of(place + chans, LANES)
-        kernels = [whole[:, pl.ds(place, chans)], whole[:, pl.ds(second, chans)]]
-        total[...] += jnp.dot(
-            jnp.concatenate(windows, axis=1), jnp.concatenate(kernels, axis=0), preferred_element_type=F32
-        )
+        taps_from(taps[0], place, 2)
         return 0
 
-    lax.fori_loop(0, 2, two_taps, 0)
-
-    def add_row(i, carry):
-        gains, shifts = carry
-        value = total[pl.ds(pl.multiple_of(i * width, width), width)]
-        return gains + value * slope_x[i].astype(F32), shifts + value * slope[i].astype(F32)
-
-    zero = jnp.zeros((width, chans), F32)
-    gains, shifts = lax.fori_loop(0, rows, add_row, (zero, zero))
-    scale = cols.total ** (-0.5)
-    sums[0:1] = scale * jnp.sum(gains, axis=0, keepdims=True)
-    sums[1:2] = scale * jnp.sum(shifts, axis=0, keepdims=True)
+    if stage:
+        taps, place = cols.pair(core, 0, chans)
+        taps_from(taps[0], place, 4)
+    else:
+        lax.fori_loop(0, 2, two_taps, 0)
+
+    if last:
+        slope, slope_x = refs[before - 2:before]
+        sums = refs[-2]
+
+        def add_row(i, carry):
+            gains, shifts = carry
+            value = total[pl.ds(pl.multiple_of(i * width, width), width)]
+            return gains + value * slope_x[i].astype(F32), shifts + value * slope[i].astype(F32)
+
+        zero = jnp.zeros((width, chans), F32)
+        gains, shifts = lax.fori_loop(0, rows, add_row, (zero, zero))
+        scale = cols.total ** (-0.5)
+        sums[0:1] = scale * jnp.sum(gains, axis=0, keepdims=True)
+        sums[1:2] = scale * jnp.sum(shifts, axis=0, keepdims=True)
 
 
 NODE = ("z", "y")
@@ -344,7 +425,7 @@
         table = jnp.asarray(ring.table(part))
         order = (ring.count, part, 2 * ring.count)
         up1, down1 = ring.up(unit), ring.down(unit)
-        peer_b = from_peer(level, shard.astype(BF16))
+        peer = from_peer(level, mine), from_peer(level, theirs)
     else:
         table = jnp.zeros((replicas * zs * 4, 1), jnp.int32)
         order = None
@@ -377,32 +458,59 @@
         [],
         20, flops // 2,
     )(dev, acts, cot_t)
+    stages = Stages([2 * zs - 3, 3] if paired else [1], 2 * part if paired else chans)
+    staged = paired
+
     def slopes_of(stats):
+        extra = (jax.ShapeDtypeStruct((chans, stages.width), BF16),) if staged else ()
         return call(
-            slope_kernel,
-            (shifted, jax.ShapeDtypeStruct(image, BF16), jax.ShapeDtypeStruct(image, BF16)),
-            [SMEM_SPEC] + [VMEM_SPEC] * 7,
-            [],
-            12, flops // 4,
-        )(dev, stats, gn_gain, gn_shift, latent, lat_far, cot_b, cot_far)
-
-    def back_of(blocks, slopes):
-        whole = call(
-            place_kernel, jax.ShapeDtypeStruct((chans, cols.lead), BF16),
-            [SMEM_SPEC] * 2 + [VMEM_SPEC] * len(blocks), [], 10, flops // 16,
-        )(dev, table, *blocks)
-        return whole, call(
-            partial(back_kernel, cols), jax.ShapeDtypeStruct((2, chans), F32),
-            [SMEM_SPEC] + [VMEM_SPEC] * 4, [pltpu.VMEM((2 * cells, chans), F32)], 24, flops // 2,
-        )(dev, *slopes, whole)
-
-    half_sum = [pltpu.VMEM((cells, chans), F32)]
-
-    def conv_far(whole):
+            partial(slope_kernel, stages),
+            (jax.ShapeDtypeStruct((3, 2 * half + 2, width, stages.width), BF16),
+             jax.ShapeDtypeStruct(image, BF16), jax.ShapeDtypeStruct(image, BF16)) + extra,
+            [SMEM_SPEC] * 2 + [VMEM_SPEC] * 7,
+            [pltpu.VMEM((2 * half, width, stages.width), F32)] if staged else [],
+            18, flops // 4,
+        )(dev, table, stats, gn_gain, gn_shift, latent, lat_far, cot_b, cot_far)
+
+    total_of = jax.ShapeDtypeStruct((2 * cells, chans), F32)
+
+    def back_first(cots, blocks):
         return call(
-            partial(conv_far_kernel, cols), jax.ShapeDtypeStruct((cells, chans), BF16),
-            [SMEM_SPEC] + [VMEM_SPEC] * 2, half_sum, 16, flops // 4,
-        )(dev, acts, whole)
+            partial(back_kernel, cols, stages, 0), total_of,
+            [SMEM_SPEC] + [VMEM_SPEC] * (1 + len(blocks)), [], 20, flops // 4,
+        )(dev, cots, *blocks)
+
+    def back_last(cots, earlier, slopes, blocks):
+        return call(
+            partial(back_kernel, cols, stages, len(stages.counts) - 1), jax.ShapeDtypeStruct((2, chans), F32),
+            [SMEM_SPEC] + [VMEM_SPEC] * (3 + len(earlier) + len(blocks)),
+            [pltpu.VMEM(total_of.shape, F32)], 24, flops // 4,
+        )(dev, cots, *earlier, *slopes, *blocks)
+
+    def conv_first(blocks):
+        wide = stages.widths[0]
+        return call(
+            partial(conv_both_kernel, cols, stages, 0),
+            (jax.ShapeDtypeStruct((cells, wide), F32), jax.ShapeDtypeStruct((cells, wide), BF16)),
+            [SMEM_SPEC] + [VMEM_SPEC] * (1 + len(blocks)),
+            [pltpu.VMEM((2 * cells, wide), F32)], 18, flops // 4,
+        )(dev, acts, *blocks)
+
+    def conv_far(blocks):
+        wide = stages.widths[-1]
+        return call(
+            partial(conv_far_kernel, cols, stages, len(stages.counts) - 1),
+            jax.ShapeDtypeStruct((cells, wide), BF16),
+            [SMEM_SPEC] + [VMEM_SPEC] * (1 + len(blocks)),
+            [pltpu.VMEM((cells, wide), F32)], 16, flops // 8,
+        )(dev, acts, *blocks)
+
+    def conv_own(got, earlier, blocks):
+        return call(
+            partial(conv_own_kernel, cols, stages), jax.ShapeDtypeStruct((half, width, chans), BF16),
+            [SMEM_SPEC] + [VMEM_SPEC] * (4 + len(earlier) + len(blocks)),
+            [pltpu.VMEM((cells, stages.widths[-1]), F32)], 18, flops // 4,
+        )(dev, acts, got, latent, conv_bias, *earlier, *blocks)
 
     def chip_sum(sums):
         vectors = jnp.concatenate([jnp.sum(cotan, axis=(0, 1))[None], sums])
@@ -410,22 +518,34 @@
         return vectors + swap(vectors, "core")
 
     if paired:
-        kept, sent = pieces[::2], pieces[1::2]
-        slopes = slopes_of(tied(stats, sent[0])[0])
-        up, down, peer_b, slopes = tied(up1, down1, peer_b, slopes)
+        kept, sent = pieces[::2], list(pieces[1::2])
+        up, down, peer, sent[0] = tied(up1, down1, peer, sent[0])
         blocks = [unit, up, down]
         crossed = [swap(piece, "replica") for piece in sent]
         up_sum = down_sum = ()
         for j in range(zs):
             if j < zs - 2:
                 up, down = ring.up(up), ring.down(down)
-                blocks += [up, down]
-                up, down, crossed[j], *received = tied(up, down, crossed[j], *up_sum, *down_sum)
-                up_sum, down_sum = tuple(received[:1]), tuple(received[1:])
+                if j == zs - 3:
+                    total_first = back_first(cots, blocks)
+                    conv_first_own, conv_send = conv_first(blocks)
+                    up, down, crossed[j], total_first, conv_send = tied(
+                        up, down, crossed[j], total_first, conv_send
+                    )
+                    conv_first_got = swap(conv_send, "core")
+                    late = [up, down]
+                else:
+                    blocks += [up, down]
+                    up, down, crossed[j], cots, slope, slope_x, order = tied(
+                        up, down, crossed[j], *slopes_of(stats)
+                    )
+                    blocks[-2:] = [up, down]
             elif j == zs - 2:
                 halves = ring.up(up[:part]), ring.down(down[part:])
-                *halves, crossed[j] = tied(*halves, crossed[j])
-                whole, sums = back_of(blocks + halves, slopes)
+                *halves, crossed[j], conv_first_got = tied(*halves, crossed[j], conv_first_got)
+                late += halves
+                sums = back_last(cots, [total_first], [slope, slope_x], late)
+                conv_got = swap(conv_far(late), "core")
             else:
                 crossed[j], sums, *received = tied(crossed[j], sums, *up_sum, *down_sum)
                 up_sum, down_sum = tuple(received[:1]), tuple(received[1:])
@@ -435,32 +555,36 @@
             if j < zs - 1:
                 down_sum = (ring.down(add(*behind)),)
         vectors = sum_over(chip_sum(sums), ("z", "y"), (1, 2))
-        last, conv_got, vectors = tied(*up_sum, swap(conv_far(whole), "core"), vectors)
+        last, conv_got, vectors = tied(*up_sum, conv_got, vectors)
         total = add(*behind, last)
+        earlier = [conv_first_own, conv_first_got, order]
         a = lax.ppermute(total, ("replica", "core"), [(1, 0), (2, 3), (0, 2), (3, 1)])
         b = lax.ppermute(total, ("replica", "core"), [(1, 2), (2, 1)])
         left = jnp.where(replica == core, jnp.where(lower, total, a), jnp.where(lower, a, b))
         right = jnp.where(replica == core, jnp.where(lower, a, total), jnp.where(lower, b, a))
     else:
-        whole, sums = back_of([lax.all_gather(unit, NODE, axis=0, tiled=True)], slopes_of(stats))
-        conv_got, vectors = swap(conv_far(whole), "core"), chip_sum(sums)
+        late, earlier = [lax.all_gather(unit, NODE, axis=0, tiled=True)], []
+        cots, slope, slope_x = slopes_of(stats)
+        sums = back_last(cots, [], [slope, slope_x], late)
+        conv_got, vectors = swap(conv_far(late), "core"), chip_sum(sums)
         terms = jnp.concatenate(pieces).reshape(2 * zs, 2, part, cols.lead)
         summed = lax.psum_scatter(terms, NODE, scatter_dimension=0, tiled=False)
         ours = lax.dynamic_index_in_dim(summed, core, 0, keepdims=False)
         got = swap(lax.dynamic_index_in_dim(summed, 1 - core, 0, keepdims=False), "core")
         left, right = jnp.where(lower, ours, got), jnp.where(lower, got, ours)
-    kernel_grad = jnp.concatenate([left, right[:, cols.both:]], axis=1).astype(F32)
+
+    def all_columns(left, right):
+        return jnp.concatenate([left, right[:, cols.both:]], axis=1).astype(F32)
+
+    kernel_grad = all_columns(left, right)
     if paired:
-        new_kernel = 0.5 * (shard + peer_b.astype(F32)) - (0.5 * scale * rate) * kernel_grad
+        peer = all_columns(jnp.where(lower, *peer), jnp.where(lower, *peer[::-1]))
+        new_kernel = 0.5 * (shard + peer) - (0.5 * scale * rate) * kernel_grad
     else:
         stepped = shard - (scale * rate) * kernel_grad
         new_kernel = 0.5 * (stepped + from_peer(level, stepped.astype(BF16)).astype(F32))
 
-    block = call(
-        partial(conv_own_kernel, cols), jax.ShapeDtypeStruct((half, width, chans), BF16),
-        [SMEM_SPEC] + [VMEM_SPEC] * 5, half_sum, 16, flops // 4,
-    )(dev, acts, whole, conv_got, latent, conv_bias)
-
+    block = conv_own(conv_got, earlier, late)
     if paired:
         new_v = 0.5 * sum_over(vectors, ("replica", "z"), (2, zs))
     else:

time: 110 us -> 111 us (level)
  waiting for transfers between devices: 28.9 us -> 13.1 us
  local copies, waits for them, and re-layouts: 6.65 us -> 16.6 us
  Pallas kernels: 28.2 us -> 35.5 us
  starting transfers between devices: 35.7 us -> 34.3 us
    ppermute x8, waiting for transfers between devices: 16.5 us -> 2.27 us  [up(): return lax.ppermute(value, NODE, self.ahead)]
    unnamed x22 -> x70, local copies, waits for them, and re-layouts: 4.73 us -> 13.3 us
    pallas_call x5 -> x6, Pallas kernels: 18.7 us -> 26 us  [the longest x1 4.98 us: slopes_of(): call(partial(slope_kernel, stages), (jax.ShapeDtypeStruct((3, 2 * half +...]
    concatenate x0 -> x4, other arithmetic: none -> 2.05 us  [all_columns(): return jnp.concatenate([left, right[:, cols.both:]], axis=1).astype(F32)]
    convert_element_type x1 -> x0, other arithmetic: 2 us -> none  [per_device(): peer_b = from_peer(level, shard.astype(BF16))]
    slice x2, local copies, waits for them, and re-layouts: 0.04 us -> 1.47 us  [per_device(): halves = (ring.up(up[:part]), ring.down(down[part:]))]
    ppermute x8, starting transfers between devices: 15.2 us -> 13.9 us  [up(): return lax.ppermute(value, NODE, self.ahead)]
    ppermute x9 -> x10, waiting for transfers between devices: 6.5 us -> 5.18 us  [swap(): return lax.ppermute(value, axis, [(0, 1), (1, 0)])]
  transfers between devices with their start and end apart: 33 -> 35, of which waited for: 11 -> 7; matrix products, arithmetic and copies ran while one was open for 7% -> 8% of each run, Pallas kernels for 26% -> 32%
where the time goes in v6:
time: 111 us; the launch traced here: 110 us
  Pallas kernels  35.5 us (32%)
  starting transfers between devices  34.3 us (31%)
  local copies, waits for them, and re-layouts  16.6 us (15%)
  waiting for transfers between devices  13.1 us (12%)
  other arithmetic  8.41 us (8%)
  between operations  1.77 us (2%)
    ppermute x8, starting transfers between devices, up(): return lax.ppermute(value, NODE, self.ahead)  13.9 us
    unnamed x70, local copies, waits for them, and re-layouts  13.3 us
    ppermute x6, starting transfers between devices, sum_over(): value_in = lax.ppermute(value, axes, [(s, s ^ mask) for s in range(count)])  8.01 us
    ppermute x10, starting transfers between devices, swap(): return lax.ppermute(value, axis, [(0, 1), (1, 0)])  5.64 us
    ppermute x10, waiting for transfers between devices, swap(): return lax.ppermute(value, axis, [(0, 1), (1, 0)])  5.18 us
    pallas_call x1, Pallas kernels, slopes_of(): call(partial(slope_kernel, stages), (jax.ShapeDtypeStruct((3, 2 * half +...  4.98 us
    pallas_call x1, Pallas kernels, per_device(): call(partial(act_kernel, order), (jax.ShapeDtypeStruct((2, chans), F32),...  4.87 us
    pallas_call x1, Pallas kernels, conv_own(): call(partial(conv_own_kernel, cols, stages), jax.ShapeDtypeStruct((half,...  4.78 us
  transfers between devices with their start and end apart: 35, of which 7 were waited for; matrix products, arithmetic and copies ran while one was open for 8% of the time, Pallas kernels for 32%

profile of v6, /device:TPU:0, one launch (start us, length us, event | category | flops | bytes accessed | tf_op | source)
XLA Modules:
  0.0 109.7 jit_solution(5367586817668812243)
XLA Ops:
  0.6 1.3 %fusion = (bf16[40,2944]{1,0:T(8,128)(2,1)S(1)}, bf16[40,2944]{1,0:T(8,128)(2,1)S(1)}) fusion(f32[1,40,5760]{2,1,0:T(8,128)} %param.10, s32[]{:T(128)S(6)} %select_n.60, s32[]{:T(128)S(6)} %select_n.61), kind=kLoop, calls=%fused_computation.13 | loop fusion | bytes 942088 | tf_op jit(solution)/shard_map/convert_element_type | solution.py:416
  2.5 2.1 %fusion.6 = (f32[640]{0:T(1024)S(1)}, bf16[16,32,640]{2,1,0:T(8,128)(2,1)S(1)}) fusion(f32[1,16,32,640]{3,2,1,0:T(8,128)} %param.9), kind=kLoop, calls=%fused_computation.28 | loop fusion | flops 654720 | bytes 1968640 | tf_op jit(solution)/shard_map/reduce_sum | solution.py:516
  5.2 2.7 %collective-permute-start.4 = (bf16[80,2944]{1,0:T(8,128)(2,1)S(1)}, bf16[80,2944]{1,0:T(8,128)(2,1)S(1)}, u32[]{:S(2)}, u32[]{:S(2)}) collective-permute-start(bf16[80,2944]{1,0:T(8,128)(2,1)S(1)} %maximum_select_fusion.refs_0_), channel_id=1, source_target_pairs={{0,4},{4,8},{8,12},{12,14},{14,10},{10,6},{6,2},{2,0},{1,5},{5,9},... | collective-permute-start | bytes 1413128 | tf_op jit(solution)/shard_map/ppermute | solution.py:358
  8.0 1.9 %collective-permute-start.6 = (bf16[40,2944]{1,0:T(8,128)(2,1)S(1)}, bf16[40,2944]{1,0:T(8,128)(2,1)}, u32[]{:S(2)}, u32[]{:S(2)}) collective-permute-start(bf16[40,2944]{1,0:T(8,128)(2,1)S(1)} %get-tuple-element.103), channel_id=1, source_target_pairs={{0,16},{16,0},{1,17},{17,1},{2,18},{18,2},{3,19},{19,3},{4,20},{20... | collective-permute-start | bytes 706568 | tf_op jit(solution)/shard_map/ppermute | solution.py:341
  10.0 4.9 %shard_map.119 = (f32[2,640]{1,0:T(2,128)S(1)}, bf16[3,34,32,640]{3,2,1,0:T(8,128)(2,1)S(1)}, bf16[640,1024]{1,0:T(8,128)(2,1)S(1)}) custom-call(s32[1]{0:T(128)} %bitcast.dev, s32[32,24]{1,0:T(8,128)S(1)} %copy-done.30, bf16[16,32,640]{2,1,0:T(8,128)(2,1)S(1)} %bitcast.19, bf16[16,32,640]{2,1,0:T(8,128)(2,1)} %collective-permute-done.lat_far, ...), custom_call_target="tpu_custom_call" | custom-call | flops 964689920 | tf_op jit(solution)/shard_map/pallas_call | solution.py:447
  14.9 4.6 %shard_map.120 = (bf16[80,2944]{1,0:T(8,128)(2,1)S(1)}, bf16[80,2944]{1,0:T(8,128)(2,1)S(1)}, bf16[80,2944]{1,0:T(8,128)(2,1)S(1)}, bf16[80,2944]{1,0:T(8,128)(2...) custom-call(s32[1]{0:T(128)} %bitcast.dev, ...), custom_call_target="tpu_custom_call" | custom-call | flops 1929379840 | tf_op jit(solution)/shard_map/pallas_call | solution.py:454
  19.5 0.8 copy-done.23
  20.3 0.8 copy-done.24
  22.0 2.0 %collective-permute-start.10 = (bf16[80,2944]{1,0:T(8,128)(2,1)S(1)}, bf16[80,2944]{1,0:T(8,128)(2,1)S(1)}, u32[]{:S(2)}, u32[]{:S(2)}) collective-permute-start(bf16[80,2944]{1,0:T(8,128)(2,1)S(1)} %get-tuple-element.57), channel_id=1, source_target_pairs={{0,16},{16,0},{1,17},{17,1},{2,18},{18,2},{3,19},{19,3},{4,20},{20... | collective-permute-start | bytes 1413128 | tf_op jit(solution)/shard_map/ppermute | solution.py:333
  24.0 1.6 %collective-permute-start.8 = (bf16[80,2944]{1,0:T(8,128)(2,1)S(1)}, bf16[80,2944]{1,0:T(8,128)(2,1)S(1)}, u32[]{:S(2)}, u32[]{:S(2)}) collective-permute-start(bf16[80,2944]{1,0:T(8,128)(2,1)S(1)} %collective-permute-done.4.refs_1_), channel_id=1, source_target_pairs={{0,4},{4,8},{8,12},{12,14},{14,10},{10,6},{6,2},{2,0},{1,5},{5,9},... | collective-permute-start | bytes 1413128 | tf_op jit(solution)/shard_map/ppermute | solution.py:358
  26.1 5.0 %shard_map.121 = (bf16[3,34,32,768]{3,2,1,0:T(8,128)(2,1)S(1)}, bf16[32,32,640]{2,1,0:T(8,128)(2,1)S(1)}, bf16[32,32,640]{2,1,0:T(8,128)(2,1)S(1)}, bf16[640,768]{1,0:T(8,128)(2,1)S(1)}) custom-call(s32[1]{0:T(128)} %bitcast.dev, s32[32,24]{1,0:T(8,128)S(1)} %copy-done.30, f32[2,640]{1,0:T(2,128)S(1)} %get-tuple-element.58.stats, f32[1,640]{1,0:T(1,128)S(1)} %copy-done.27, ...), custom_call_target="tpu_custom_call" | custom-call | flops 964689920 | tf_op jit(solution)/shard_map/pallas_call | solution.py:466
  31.1 1.1 copy-done.15
  32.1 1.0 copy-done.19
  33.1 2.6 %collective-permute-done.10 = bf16[80,2944]{1,0:T(8,128)(2,1)S(1)} collective-permute-done((bf16[80,2944]{1,0:T(8,128)(2,1)S(1)}, bf16[80,2944]{1,0:T(8,128)(2,1)S(1)}, u32[]{:S(2)}, u32[]{:S(2)}) %collective-permute-start.10) | collective-permute-done | bytes 471072 | tf_op jit(solution)/shard_map/ppermute | solution.py:333
  35.7 1.2 %collective-permute-done.9.refs_4_ = bf16[80,2944]{1,0:T(8,128)(2,1)S(1)} collective-permute-done((bf16[80,2944]{1,0:T(8,128)(2,1)S(1)}, bf16[80,2944]{1,0:T(8,128)(2,1)S(1)}, u32[]{:S(2)}, u32[]{:S(2)}) %collective-permute-start.9) | collective-permute-done | bytes 471072 | tf_op jit(solution)/shard_map/ppermute | solution.py:361
  37.0 1.6 %collective-permute-start.11 = (bf16[80,2944]{1,0:T(8,128)(2,1)S(1)}, bf16[80,2944]{1,0:T(8,128)(2,1)S(1)}, u32[]{:S(2)}, u32[]{:S(2)}) collective-permute-start(bf16[80,2944]{1,0:T(8,128)(2,1)S(1)} %collective-permute-done.8.refs_3_), channel_id=1, source_target_pairs={{0,4},{4,8},{8,12},{12,14},{14,10},{10,6},{6,2},{2,0},{1,5},{5,9},... | collective-permute-start | bytes 1413128 | tf_op jit(solution)/shard_map/ppermute | solution.py:358
  39.1 1.6 %collective-permute-start.18 = (bf16[40,2944]{1,0:T(8,128)(2,1)S(1)}, bf16[40,2944]{1,0:T(8,128)(2,1)S(1)}, u32[]{:S(2)}, u32[]{:S(2)}) collective-permute-start(bf16[40,2944]{1,0:T(8,128)(2,1)S(1)} %get-tuple-element.102), channel_id=1, source_target_pairs={{0,4},{4,8},{8,12},{12,14},{14,10},{10,6},{6,2},{2,0},{1,5},{5,9},... | collective-permute-start | bytes 706568 | tf_op jit(solution)/shard_map/ppermute | solution.py:358
  41.2 4.8 %shard_map.123 = (f32[512,512]{1,0:T(8,128)S(1)}, bf16[512,512]{1,0:T(8,128)(2,1)}) custom-call(s32[1]{0:T(128)} %bitcast.dev, bf16[3,34,32,640]{3,2,1,0:T(8,128)(2,1)S(1)} %get-tuple-element.50.acts, bf16[80,2944]{1,0:T(8,128)(2,1)S(1)} %maximum_select_fusion.refs_0_, bf16[80,2944]{1,0:T(8,128)(2,1)S(1)} %collective-permute-done.4.refs_1_, ...), custom_call_target="tpu_custom_call" | custom-call | flops 964689920 | tf_op jit(solution)/shard_map/pallas_call | solution.py:492
  46.0 1.0 copy-done.17
  47.0 1.0 copy-done.8
  48.0 1.0 copy-done.10
  49.0 1.0 copy-done.12
  50.1 4.6 %shard_map.122.refs_0_ = f32[1024,640]{1,0:T(8,128)S(1)} custom-call(s32[1]{0:T(128)} %bitcast.dev, bf16[3,34,32,768]{3,2,1,0:T(8,128)(2,1)S(1)} %get-tuple-element.63.cots, bf16[80,2944]{1,0:T(8,128)(2,1)S(1)} %copy-done.8, bf16[80,2944]{1,0:T(8,128)(2,1)S(1)} %copy-done.10, bf16[80,2944]{1,0:T(8,128)(2,1)S(1)} %copy-done.12, ...), custom_call_target="tpu_custom_call" | custom-call | flops 964689920 | tf_op jit(solution)/shard_map/pallas_call | solution.py:478
  56.3 1.6 %collective-permute-start.14 = (bf16[40,2944]{1,0:T(8,128)(2,1)}, bf16[40,2944]{1,0:T(8,128)(2,1)S(1)}, u32[]{:S(2)}, u32[]{:S(2)}) collective-permute-start(bf16[40,2944]{1,0:T(8,128)(2,1)} %slice.70), channel_id=1, source_target_pairs={{0,4},{4,8},{8,12},{12,14},{14,10},{10,6},{6,2},{2,0},{1,5},{5,9},... | collective-permute-start | bytes 706568 | tf_op jit(solution)/shard_map/ppermute | solution.py:358
  59.1 1.0 add_convert_fusion.3
  60.0 1.6 %collective-permute-start.19 = (bf16[40,2944]{1,0:T(8,128)(2,1)}, bf16[40,2944]{1,0:T(8,128)(2,1)}, u32[]{:S(2)}, u32[]{:S(2)}) collective-permute-start(bf16[40,2944]{1,0:T(8,128)(2,1)} %get-tuple-element.100), channel_id=1, source_target_pairs={{0,4},{4,8},{8,12},{12,14},{14,10},{10,6},{6,2},{2,0},{1,5},{5,9},... | collective-permute-start | bytes 706568 | tf_op jit(solution)/shard_map/ppermute | solution.py:358
  61.6 2.5 %collective-permute-done.16 = bf16[80,2944]{1,0:T(8,128)(2,1)S(1)} collective-permute-done((bf16[80,2944]{1,0:T(8,128)(2,1)S(1)}, bf16[80,2944]{1,0:T(8,128)(2,1)S(1)}, u32[]{:S(2)}, u32[]{:S(2)}) %collective-permute-start.16) | collective-permute-done | bytes 471072 | tf_op jit(solution)/shard_map/ppermute | solution.py:333
  66.2 1.0 collective-permute-start.2
  67.5 2.3 %collective-permute-done.19 = bf16[40,2944]{1,0:T(8,128)(2,1)} collective-permute-done((bf16[40,2944]{1,0:T(8,128)(2,1)}, bf16[40,2944]{1,0:T(8,128)(2,1)}, u32[]{:S(2)}, u32[]{:S(2)}) %collective-permute-start.19) | collective-permute-done | bytes 235552 | tf_op jit(solution)/shard_map/ppermute | solution.py:358
  69.8 2.0 %collective-permute-done.22 = bf16[40,2944]{1,0:T(8,128)(2,1)} collective-permute-done((bf16[40,2944]{1,0:T(8,128)(2,1)}, bf16[40,2944]{1,0:T(8,128)(2,1)}, u32[]{:S(2)}, u32[]{:S(2)}) %collective-permute-start.22) | collective-permute-done | bytes 235552 | tf_op jit(solution)/shard_map/ppermute | solution.py:361
  71.8 1.7 %add_convert_fusion.2 = (bf16[40,2944]{1,0:T(8,128)(2,1)S(1)}, bf16[40,2944]{1,0:T(8,128)(2,1)S(1)}) fusion(bf16[40,2944]{1,0:T(8,128)(2,1)} %collective-permute-done.22, bf16[80,2944]{1,0:T(8,128)(2,1)} %copy-done.34, bf16[80,2944]{1,0:T(8,128)(2,1)} %copy-done.23, bf16[40,2944]{1,0:T(8,128)(2,1)} %collective-permute-done.19), kind=kLoop, calls=%fused_computation.5 | loop fusion | flops 1413120 | bytes 1884160 | tf_op jit(solution)/shard_map/convert_element_type | solution.py:392
  73.5 1.6 %collective-permute-start.20 = (bf16[40,2944]{1,0:T(8,128)(2,1)S(1)}, bf16[40,2944]{1,0:T(8,128)(2,1)S(1)}, u32[]{:S(2)}, u32[]{:S(2)}) collective-permute-start(bf16[40,2944]{1,0:T(8,128)(2,1)S(1)} %get-tuple-element.98), channel_id=1, source_target_pairs={{0,4},{4,8},{8,12},{12,14},{14,10},{10,6},{6,2},{2,0},{1,5},{5,9},... | collective-permute-start | bytes 706568 | tf_op jit(solution)/shard_map/ppermute | solution.py:358
  75.6 1.0 select_bitcast_fusion.1
  76.6 2.2 %copy-done.1 = bf16[3,34,32,640]{3,2,1,0:T(8,128)(2,1)S(1)} copy-done((bf16[3,34,32,640]{3,2,1,0:T(8,128)(2,1)S(1)}, bf16[3,34,32,640]{3,2,1,0:T(8,128)(2,1)}, u32[]{:S(2)}) %copy-start.1) | copy-done | bytes 4177944
  78.7 2.5 %shard_map.125 = bf16[512,256]{1,0:T(8,128)(2,1)S(1)} custom-call(s32[1]{0:T(128)} %bitcast.dev, bf16[3,34,32,640]{3,2,1,0:T(8,128)(2,1)S(1)} %copy-done.1, bf16[80,2944]{1,0:T(8,128)(2,1)S(1)} %collective-permute-done.11.refs_3_.refs_0_, bf16[80,2944]{1,0:T(8,128)(2,1)S(1)} %copy-done.6, bf16[40,2944]{1,0:T(8,128)(2,1)S(1)} %collective-permute-done.14.refs_5_.refs_2_, ...), custom_call_target="tpu_custom_call" | custom-call | flops 482344960 | tf_op jit(solution)/shard_map/pallas_call | solution.py:501
  81.4 1.3 %copy-done.16 = bf16[32,32,640]{2,1,0:T(8,128)(2,1)S(1)} copy-done((bf16[32,32,640]{2,1,0:T(8,128)(2,1)S(1)}, bf16[32,32,640]{2,1,0:T(8,128)(2,1)}, u32[]{:S(2)}) %copy-start.16) | copy-done | bytes 1310744
  82.7 4.4 %shard_map.124 = f32[2,640]{1,0:T(2,128)S(1)} custom-call(s32[1]{0:T(128)} %bitcast.dev, bf16[3,34,32,768]{3,2,1,0:T(8,128)(2,1)S(1)} %copy-done.4, f32[1024,640]{1,0:T(8,128)S(1)} %shard_map.122.refs_0_, bf16[32,32,640]{2,1,0:T(8,128)(2,1)S(1)} %copy-done.14, bf16[32,32,640]{2,1,0:T(8,128)(2,1)S(1)} %copy-done.16, ...), custom_call_target="tpu_custom_call" | custom-call | flops 964689920 | tf_op jit(solution)/shard_map/pallas_call | solution.py:484
  87.8 1.6 %collective-permute-start.24 = (bf16[40,2944]{1,0:T(8,128)(2,1)S(1)}, bf16[40,2944]{1,0:T(8,128)(2,1)S(1)}, u32[]{:S(2)}, u32[]{:S(2)}) collective-permute-start(bf16[40,2944]{1,0:T(8,128)(2,1)S(1)} %add_convert_fusion.1), channel_id=1, source_target_pairs={{0,4},{4,8},{8,12},{12,14},{14,10},{10,6},{6,2},{2,0},{1,5},{5,9},... | collective-permute-start | bytes 706568 | tf_op jit(solution)/shard_map/ppermute | solution.py:358
  89.9 1.2 %collective-permute-start.28 = (f32[3,640]{1,0:T(4,128)S(1)}, f32[3,640]{1,0:T(4,128)S(1)}, u32[]{:S(2)}, u32[]{:S(2)}) collective-permute-start(f32[3,640]{1,0:T(4,128)S(1)} %fusion.8), channel_id=1, source_target_pairs={{0,4},{2,6},{4,0},{6,2},{8,12},{10,14},{12,8},{14,10},{1,5},{3,7},... | collective-permute-start | bytes 23048 | tf_op jit(solution)/shard_map/ppermute | solution.py:383
  91.1 1.8 %collective-permute-start.29 = (f32[3,640]{1,0:T(4,128)S(1)}, f32[3,640]{1,0:T(4,128)S(1)}, u32[]{:S(2)}, u32[]{:S(2)}) collective-permute-start(f32[3,640]{1,0:T(4,128)S(1)} %fusion.8), channel_id=1, source_target_pairs={{0,6},{2,4},{4,2},{6,0},{8,14},{10,12},{12,10},{14,8},{1,7},{3,5},... | collective-permute-start | bytes 23048 | tf_op jit(solution)/shard_map/ppermute | solution.py:383
  93.0 1.0 fusion.4
  93.9 2.0 %collective-permute-done.27 = f32[3,640]{1,0:T(4,128)S(1)} collective-permute-done((f32[3,640]{1,0:T(4,128)S(1)}, f32[3,640]{1,0:T(4,128)S(1)}, u32[]{:S(2)}, u32[]{:S(2)}) %collective-permute-start.27) | collective-permute-done | bytes 7712 | tf_op jit(solution)/shard_map/ppermute | solution.py:383
  96.0 2.5 %collective-permute-start.32 = (f32[3,640]{1,0:T(4,128)S(1)}, f32[3,640]{1,0:T(4,128)S(1)}, u32[]{:S(2)}, u32[]{:S(2)}) collective-permute-start(f32[3,640]{1,0:T(4,128)S(1)} %add_add_fusion), channel_id=1, source_target_pairs={{0,8},{4,12},{8,0},{12,4},{16,24},{20,28},{24,16},{28,20},{1,9},{5... | collective-permute-start | bytes 23048 | tf_op jit(solution)/shard_map/ppermute | solution.py:383
  98.5 0.9 collective-permute-start.33
  99.4 1.1 collective-permute-start.34
  100.6 1.3 %collective-permute-start.30 = (bf16[40,2944]{1,0:T(8,128)(2,1)S(1)}, bf16[40,2944]{1,0:T(8,128)(2,1)S(1)}, u32[]{:S(2)}, u32[]{:S(2)}) collective-permute-start(bf16[40,2944]{1,0:T(8,128)(2,1)S(1)} %add_convert_fusion), channel_id=1, source_target_pairs={{1,0},{16,17},{0,16},{17,1},{3,2},{18,19},{2,18},{19,3},{5,4},{20,... | collective-permute-start | bytes 706568 | tf_op jit(solution)/shard_map/ppermute | solution.py:561
  102.6 4.8 %shard_map.126 = bf16[16,32,640]{2,1,0:T(8,128)(2,1)} custom-call(s32[1]{0:T(128)} %bitcast.dev, bf16[3,34,32,640]{3,2,1,0:T(8,128)(2,1)S(1)} %copy-done.2, bf16[512,256]{1,0:T(8,128)(2,1)S(1)} %collective-permute-done.25.got, bf16[16,32,640]{2,1,0:T(8,128)(2,1)S(1)} %bitcast.21, f32[1,640]{1,0:T(1,128)S(1)} %copy-done.26, f32[512,512]{1,0:T(8,128)S(1)} %copy-done.18, ...), custom_call_target="tpu_custom_call" | custom-call | flops 964689920 | tf_op jit(solution)/shard_map/pallas_call | solution.py:509
  108.6 1.1 %multiply_subtract_fusion = f32[1,40,5760]{2,1,0:T(8,128)} fusion(f32[1,40,5760]{2,1,0:T(8,128)S(1)} %copy-done.31, bf16[1,40,2816]{2,1,0:T(8,128)(2,1)S(1)} %fusion.4, bf16[1,40,2944]{2,1,0:T(8,128)(2,1)S(1)} %select_bitcast_fusion.1, bf16[1,40,2816]{2,1,0:T(8,128)(2,1)S(1)} %fusion.3, bf16[1,40,2944]{2,1,0:T(8,128)(2,1)S(1)} %select_bitcast_fusion, ...), kind=kLoop, calls=%fused_computation | loop fusion | flops 2764800 | bytes 2764804 | tf_op jit(solution)/shard_map/sub | solution.py:582
  (121 shorter events, 11.9 us)
Async XLA Ops:
  2.0 3.2 %collective-permute-start.3 = (bf16[40,2944]{1,0:T(8,128)(2,1)S(1)}, bf16[40,2944]{1,0:T(8,128)(2,1)S(1)}, u32[]{:S(2)}, u32[]{:S(2)}) collective-permute-start(bf16[40,2944]{1,0:T(8,128)(2,1)S(1)} %get-tuple-element.104), channel_id=1, source_target_pairs={{0,1},{1,0},{2,3},{3,2},{4,5},{5,4},{6,7},{7,6},{8,9},{9,8},{10,11... | collective-permute-start | bytes 706568 | tf_op jit(solution)/shard_map/ppermute | solution.py:333
  4.6 5.3 %collective-permute-start.1 = (bf16[16,32,640]{2,1,0:T(8,128)(2,1)S(1)}, bf16[16,32,640]{2,1,0:T(8,128)(2,1)}, u32[]{:S(2)}, u32[]{:S(2)}) collective-permute-start(bf16[16,32,640]{2,1,0:T(8,128)(2,1)S(1)} %get-tuple-element.96.cot_own), channel_id=1, source_target_pairs={{0,1},{1,0},{2,3},{3,2},{4,5},{5,4},{6,7},{7,6},{8,9},{9,8},{10,11... | collective-permute-start | bytes 1966088 | tf_op jit(solution)/shard_map/ppermute | solution.py:333
  4.7 5.3 %collective-permute-start = (bf16[16,32,640]{2,1,0:T(8,128)(2,1)S(1)}, bf16[16,32,640]{2,1,0:T(8,128)(2,1)}, u32[]{:S(2)}, u32[]{:S(2)}) collective-permute-start(bf16[16,32,640]{2,1,0:T(8,128)(2,1)S(1)} %bitcast.18), channel_id=1, source_target_pairs={{0,1},{1,0},{2,3},{3,2},{4,5},{5,4},{6,7},{7,6},{8,9},{9,8},{10,11... | collective-permute-start | bytes 1966088 | tf_op jit(solution)/shard_map/ppermute | solution.py:333
  5.2 36.0 %copy-start.7 = (bf16[80,2944]{1,0:T(8,128)(2,1)}, bf16[80,2944]{1,0:T(8,128)(2,1)S(1)}, u32[]{:S(2)}) copy-start(bf16[80,2944]{1,0:T(8,128)(2,1)S(1)} %maximum_select_fusion.refs_0_) | copy-start | bytes 1413124
  5.2 16.7 %collective-permute-start.4 = (bf16[80,2944]{1,0:T(8,128)(2,1)S(1)}, bf16[80,2944]{1,0:T(8,128)(2,1)S(1)}, u32[]{:S(2)}, u32[]{:S(2)}) collective-permute-start(bf16[80,2944]{1,0:T(8,128)(2,1)S(1)} %maximum_select_fusion.refs_0_), channel_id=1, source_target_pairs={{0,4},{4,8},{8,12},{12,14},{14,10},{10,6},{6,2},{2,0},{1,5},{5,9},... | collective-permute-start | bytes 1413128 | tf_op jit(solution)/shard_map/ppermute | solution.py:358
  8.0 14.0 %collective-permute-start.5 = (bf16[80,2944]{1,0:T(8,128)(2,1)S(1)}, bf16[80,2944]{1,0:T(8,128)(2,1)S(1)}, u32[]{:S(2)}, u32[]{:S(2)}) collective-permute-start(bf16[80,2944]{1,0:T(8,128)(2,1)S(1)} %maximum_select_fusion.refs_0_), channel_id=1, source_target_pairs={{4,0},{8,4},{12,8},{14,12},{10,14},{6,10},{2,6},{0,2},{5,1},{9,5},... | collective-permute-start | bytes 1413128 | tf_op jit(solution)/shard_map/ppermute | solution.py:361
  8.0 13.9 %collective-permute-start.6 = (bf16[40,2944]{1,0:T(8,128)(2,1)S(1)}, bf16[40,2944]{1,0:T(8,128)(2,1)}, u32[]{:S(2)}, u32[]{:S(2)}) collective-permute-start(bf16[40,2944]{1,0:T(8,128)(2,1)S(1)} %get-tuple-element.103), channel_id=1, source_target_pairs={{0,16},{16,0},{1,17},{17,1},{2,18},{18,2},{3,19},{19,3},{4,20},{20... | collective-permute-start | bytes 706568 | tf_op jit(solution)/shard_map/ppermute | solution.py:341
  9.9 12.0 %collective-permute-start.7 = (bf16[40,2944]{1,0:T(8,128)(2,1)S(1)}, bf16[40,2944]{1,0:T(8,128)(2,1)S(1)}, u32[]{:S(2)}, u32[]{:S(2)}) collective-permute-start(bf16[40,2944]{1,0:T(8,128)(2,1)S(1)} %get-tuple-element.104), channel_id=1, source_target_pairs={{0,16},{16,0},{1,17},{17,1},{2,18},{18,2},{3,19},{19,3},{4,20},{20... | collective-permute-start | bytes 706568 | tf_op jit(solution)/shard_map/ppermute | solution.py:341
  14.9 26.3 %copy-start = (bf16[3,34,32,640]{3,2,1,0:T(8,128)(2,1)}, bf16[3,34,32,640]{3,2,1,0:T(8,128)(2,1)S(1)}, u32[]{:S(2)}) copy-start(bf16[3,34,32,640]{3,2,1,0:T(8,128)(2,1)S(1)} %get-tuple-element.50.acts) | copy-start | bytes 12533764
  21.9 19.3 %copy-start.9 = (bf16[80,2944]{1,0:T(8,128)(2,1)}, bf16[80,2944]{1,0:T(8,128)(2,1)S(1)}, u32[]{:S(2)}) copy-start(bf16[80,2944]{1,0:T(8,128)(2,1)S(1)} %collective-permute-done.4.refs_1_) | copy-start | bytes 1413124
  22.0 19.3 %copy-start.11 = (bf16[80,2944]{1,0:T(8,128)(2,1)}, bf16[80,2944]{1,0:T(8,128)(2,1)S(1)}, u32[]{:S(2)}) copy-start(bf16[80,2944]{1,0:T(8,128)(2,1)S(1)} %collective-permute-done.5.refs_2_) | copy-start | bytes 1413124
  22.0 13.8 %collective-permute-start.10 = (bf16[80,2944]{1,0:T(8,128)(2,1)S(1)}, bf16[80,2944]{1,0:T(8,128)(2,1)S(1)}, u32[]{:S(2)}, u32[]{:S(2)}) collective-permute-start(bf16[80,2944]{1,0:T(8,128)(2,1)S(1)} %get-tuple-element.57), channel_id=1, source_target_pairs={{0,16},{16,0},{1,17},{17,1},{2,18},{18,2},{3,19},{19,3},{4,20},{20... | collective-permute-start | bytes 1413128 | tf_op jit(solution)/shard_map/ppermute | solution.py:333
  24.0 11.8 %collective-permute-start.8 = (bf16[80,2944]{1,0:T(8,128)(2,1)S(1)}, bf16[80,2944]{1,0:T(8,128)(2,1)S(1)}, u32[]{:S(2)}, u32[]{:S(2)}) collective-permute-start(bf16[80,2944]{1,0:T(8,128)(2,1)S(1)} %collective-permute-done.4.refs_1_), channel_id=1, source_target_pairs={{0,4},{4,8},{8,12},{12,14},{14,10},{10,6},{6,2},{2,0},{1,5},{5,9},... | collective-permute-start | bytes 1413128 | tf_op jit(solution)/shard_map/ppermute | solution.py:358
  25.5 11.4 %collective-permute-start.9 = (bf16[80,2944]{1,0:T(8,128)(2,1)S(1)}, bf16[80,2944]{1,0:T(8,128)(2,1)S(1)}, u32[]{:S(2)}, u32[]{:S(2)}) collective-permute-start(bf16[80,2944]{1,0:T(8,128)(2,1)S(1)} %collective-permute-done.5.refs_2_), channel_id=1, source_target_pairs={{4,0},{8,4},{12,8},{14,12},{10,14},{6,10},{2,6},{0,2},{5,1},{9,5},... | collective-permute-start | bytes 1413128 | tf_op jit(solution)/shard_map/ppermute | solution.py:361
  26.0 28.7 %collective-permute-start.13 = (bf16[80,2944]{1,0:T(8,128)(2,1)S(1)}, bf16[80,2944]{1,0:T(8,128)(2,1)S(1)}, u32[]{:S(2)}, u32[]{:S(2)}) collective-permute-start(bf16[80,2944]{1,0:T(8,128)(2,1)S(1)} %get-tuple-element.66), channel_id=1, source_target_pairs={{0,16},{16,0},{1,17},{17,1},{2,18},{18,2},{3,19},{19,3},{4,20},{20... | collective-permute-start | bytes 1413128 | tf_op jit(solution)/shard_map/ppermute | solution.py:333
  33.1 12.9 %copy-start.3 = (bf16[3,34,32,768]{3,2,1,0:T(8,128)(2,1)}, bf16[3,34,32,768]{3,2,1,0:T(8,128)(2,1)S(1)}, u32[]{:S(2)}) copy-start(bf16[3,34,32,768]{3,2,1,0:T(8,128)(2,1)S(1)} %get-tuple-element.63.cots) | copy-start | bytes 15040516
  33.1 12.9 %copy-start.13 = (bf16[32,32,640]{2,1,0:T(8,128)(2,1)}, bf16[32,32,640]{2,1,0:T(8,128)(2,1)S(1)}, u32[]{:S(2)}) copy-start(bf16[32,32,640]{2,1,0:T(8,128)(2,1)S(1)} %get-tuple-element.69.refs_1_) | copy-start | bytes 3932164
  37.0 18.5 %collective-permute-start.11 = (bf16[80,2944]{1,0:T(8,128)(2,1)S(1)}, bf16[80,2944]{1,0:T(8,128)(2,1)S(1)}, u32[]{:S(2)}, u32[]{:S(2)}) collective-permute-start(bf16[80,2944]{1,0:T(8,128)(2,1)S(1)} %collective-permute-done.8.refs_3_), channel_id=1, source_target_pairs={{0,4},{4,8},{8,12},{12,14},{14,10},{10,6},{6,2},{2,0},{1,5},{5,9},... | collective-permute-start | bytes 1413128 | tf_op jit(solution)/shard_map/ppermute | solution.py:358
  38.6 16.9 %collective-permute-start.12 = (bf16[80,2944]{1,0:T(8,128)(2,1)S(1)}, bf16[80,2944]{1,0:T(8,128)(2,1)S(1)}, u32[]{:S(2)}, u32[]{:S(2)}) collective-permute-start(bf16[80,2944]{1,0:T(8,128)(2,1)S(1)} %collective-permute-done.9.refs_4_), channel_id=1, source_target_pairs={{4,0},{8,4},{12,8},{14,12},{10,14},{6,10},{2,6},{0,2},{5,1},{9,5},... | collective-permute-start | bytes 1413128 | tf_op jit(solution)/shard_map/ppermute | solution.py:361
  39.1 19.5 %collective-permute-start.18 = (bf16[40,2944]{1,0:T(8,128)(2,1)S(1)}, bf16[40,2944]{1,0:T(8,128)(2,1)S(1)}, u32[]{:S(2)}, u32[]{:S(2)}) collective-permute-start(bf16[40,2944]{1,0:T(8,128)(2,1)S(1)} %get-tuple-element.102), channel_id=1, source_target_pairs={{0,4},{4,8},{8,12},{12,14},{14,10},{10,6},{6,2},{2,0},{1,5},{5,9},... | collective-permute-start | bytes 706568 | tf_op jit(solution)/shard_map/ppermute | solution.py:358
  40.8 18.3 %collective-permute-start.21 = (bf16[40,2944]{1,0:T(8,128)(2,1)S(1)}, bf16[40,2944]{1,0:T(8,128)(2,1)S(1)}, u32[]{:S(2)}, u32[]{:S(2)}) collective-permute-start(bf16[40,2944]{1,0:T(8,128)(2,1)S(1)} %get-tuple-element.101), channel_id=1, source_target_pairs={{4,0},{8,4},{12,8},{14,12},{10,14},{6,10},{2,6},{0,2},{5,1},{9,5},... | collective-permute-start | bytes 706568 | tf_op jit(solution)/shard_map/ppermute | solution.py:361
  54.7 9.5 %collective-permute-start.16 = (bf16[80,2944]{1,0:T(8,128)(2,1)S(1)}, bf16[80,2944]{1,0:T(8,128)(2,1)S(1)}, u32[]{:S(2)}, u32[]{:S(2)}) collective-permute-start(bf16[80,2944]{1,0:T(8,128)(2,1)S(1)} %get-tuple-element.73), channel_id=1, source_target_pairs={{0,16},{16,0},{1,17},{17,1},{2,18},{18,2},{3,19},{19,3},{4,20},{20... | collective-permute-start | bytes 1413128 | tf_op jit(solution)/shard_map/ppermute | solution.py:333
  55.5 12.0 %collective-permute-start.17 = (bf16[512,512]{1,0:T(8,128)(2,1)}, bf16[512,512]{1,0:T(8,128)(2,1)}, u32[]{:S(2)}, u32[]{:S(2)}) collective-permute-start(bf16[512,512]{1,0:T(8,128)(2,1)} %get-tuple-element.74), channel_id=1, source_target_pairs={{0,1},{1,0},{2,3},{3,2},{4,5},{5,4},{6,7},{7,6},{8,9},{9,8},{10,11... | collective-permute-start | bytes 1572872 | tf_op jit(solution)/shard_map/ppermute | solution.py:333
  56.3 9.8 %collective-permute-start.14 = (bf16[40,2944]{1,0:T(8,128)(2,1)}, bf16[40,2944]{1,0:T(8,128)(2,1)S(1)}, u32[]{:S(2)}, u32[]{:S(2)}) collective-permute-start(bf16[40,2944]{1,0:T(8,128)(2,1)} %slice.70), channel_id=1, source_target_pairs={{0,4},{4,8},{8,12},{12,14},{14,10},{10,6},{6,2},{2,0},{1,5},{5,9},... | collective-permute-start | bytes 706568 | tf_op jit(solution)/shard_map/ppermute | solution.py:358
  58.6 8.9 %collective-permute-start.15 = (bf16[40,2944]{1,0:T(8,128)(2,1)}, bf16[40,2944]{1,0:T(8,128)(2,1)}, u32[]{:S(2)}, u32[]{:S(2)}) collective-permute-start(bf16[40,2944]{1,0:T(8,128)(2,1)} %slice.71), channel_id=1, source_target_pairs={{4,0},{8,4},{12,8},{14,12},{10,14},{6,10},{2,6},{0,2},{5,1},{9,5},... | collective-permute-start | bytes 706568 | tf_op jit(solution)/shard_map/ppermute | solution.py:361
  60.0 9.7 %collective-permute-start.19 = (bf16[40,2944]{1,0:T(8,128)(2,1)}, bf16[40,2944]{1,0:T(8,128)(2,1)}, u32[]{:S(2)}, u32[]{:S(2)}) collective-permute-start(bf16[40,2944]{1,0:T(8,128)(2,1)} %get-tuple-element.100), channel_id=1, source_target_pairs={{0,4},{4,8},{8,12},{12,14},{14,10},{10,6},{6,2},{2,0},{1,5},{5,9},... | collective-permute-start | bytes 706568 | tf_op jit(solution)/shard_map/ppermute | solution.py:358
  64.9 6.8 %collective-permute-start.22 = (bf16[40,2944]{1,0:T(8,128)(2,1)}, bf16[40,2944]{1,0:T(8,128)(2,1)}, u32[]{:S(2)}, u32[]{:S(2)}) collective-permute-start(bf16[40,2944]{1,0:T(8,128)(2,1)} %get-tuple-element.99), channel_id=1, source_target_pairs={{4,0},{8,4},{12,8},{14,12},{10,14},{6,10},{2,6},{0,2},{5,1},{9,5},... | collective-permute-start | bytes 706568 | tf_op jit(solution)/shard_map/ppermute | solution.py:361
  66.1 9.4 %copy-start.33 = (bf16[40,2944]{1,0:T(8,128)(2,1)S(1)}, bf16[40,2944]{1,0:T(8,128)(2,1)}, u32[]{:S(2)}) copy-start(bf16[40,2944]{1,0:T(8,128)(2,1)} %copy-done.32) | copy-start | bytes 706564
  66.1 10.4 %copy-start.6 = (bf16[80,2944]{1,0:T(8,128)(2,1)S(1)}, bf16[80,2944]{1,0:T(8,128)(2,1)}, u32[]{:S(2)}) copy-start(bf16[80,2944]{1,0:T(8,128)(2,1)} %copy-done.5) | copy-start | bytes 1413124
  66.2 20.9 %collective-permute-start.2 = (bf16[80,2944]{1,0:T(8,128)(2,1)}, bf16[80,2944]{1,0:T(8,128)(2,1)S(1)}, u32[]{:S(2)}, u32[]{:S(2)}) collective-permute-start(bf16[80,2944]{1,0:T(8,128)(2,1)} %copy-done.29), channel_id=1, source_target_pairs={{0,16},{16,0},{1,17},{17,1},{2,18},{18,2},{3,19},{19,3},{4,20},{20... | collective-permute-start | bytes 1413128 | tf_op jit(solution)/shard_map/ppermute | solution.py:333
  71.8 9.6 %copy-start.14 = (bf16[32,32,640]{2,1,0:T(8,128)(2,1)S(1)}, bf16[32,32,640]{2,1,0:T(8,128)(2,1)}, u32[]{:S(2)}) copy-start(bf16[32,32,640]{2,1,0:T(8,128)(2,1)} %copy-done.13) | copy-start | bytes 3932164
  73.5 13.6 %collective-permute-start.20 = (bf16[40,2944]{1,0:T(8,128)(2,1)S(1)}, bf16[40,2944]{1,0:T(8,128)(2,1)S(1)}, u32[]{:S(2)}, u32[]{:S(2)}) collective-permute-start(bf16[40,2944]{1,0:T(8,128)(2,1)S(1)} %get-tuple-element.98), channel_id=1, source_target_pairs={{0,4},{4,8},{8,12},{12,14},{14,10},{10,6},{6,2},{2,0},{1,5},{5,9},... | collective-permute-start | bytes 706568 | tf_op jit(solution)/shard_map/ppermute | solution.py:358
  75.1 12.0 %collective-permute-start.23 = (bf16[40,2944]{1,0:T(8,128)(2,1)S(1)}, bf16[40,2944]{1,0:T(8,128)(2,1)S(1)}, u32[]{:S(2)}, u32[]{:S(2)}) collective-permute-start(bf16[40,2944]{1,0:T(8,128)(2,1)S(1)} %get-tuple-element.97), channel_id=1, source_target_pairs={{4,0},{8,4},{12,8},{14,12},{10,14},{6,10},{2,6},{0,2},{5,1},{9,5},... | collective-permute-start | bytes 706568 | tf_op jit(solution)/shard_map/ppermute | solution.py:361
  81.3 14.7 %collective-permute-start.25 = (bf16[512,256]{1,0:T(8,128)(2,1)S(1)}, bf16[512,256]{1,0:T(8,128)(2,1)S(1)}, u32[]{:S(2)}, u32[]{:S(2)}) collective-permute-start(bf16[512,256]{1,0:T(8,128)(2,1)S(1)} %shard_map.125), channel_id=1, source_target_pairs={{0,1},{1,0},{2,3},{3,2},{4,5},{5,4},{6,7},{7,6},{8,9},{9,8},{10,11... | collective-permute-start | bytes 786440 | tf_op jit(solution)/shard_map/ppermute | solution.py:333
  82.7 19.9 %copy-start.2 = (bf16[3,34,32,640]{3,2,1,0:T(8,128)(2,1)S(1)}, bf16[3,34,32,640]{3,2,1,0:T(8,128)(2,1)}, u32[]{:S(2)}) copy-start(bf16[3,34,32,640]{3,2,1,0:T(8,128)(2,1)} %copy-done) | copy-start | bytes 12533764
  87.1 2.3 %collective-permute-start.26 = (f32[3,640]{1,0:T(4,128)S(1)}, f32[3,640]{1,0:T(4,128)S(1)}, u32[]{:S(2)}, u32[]{:S(2)}) collective-permute-start(f32[3,640]{1,0:T(4,128)S(1)} %fusion.5), channel_id=1, source_target_pairs={{0,1},{1,0},{2,3},{3,2},{4,5},{5,4},{6,7},{7,6},{8,9},{9,8},{10,11... | collective-permute-start | bytes 23048 | tf_op jit(solution)/shard_map/ppermute | solution.py:333
  87.7 14.9 %copy-start.18 = (f32[512,512]{1,0:T(8,128)S(1)}, f32[512,512]{1,0:T(8,128)}, u32[]{:S(2)}) copy-start(f32[512,512]{1,0:T(8,128)} %copy-done.17) | copy-start | bytes 3145732
  87.7 14.9 %copy-start.20 = (bf16[640,768]{1,0:T(8,128)(2,1)S(1)}, bf16[640,768]{1,0:T(8,128)(2,1)}, u32[]{:S(2)}) copy-start(bf16[640,768]{1,0:T(8,128)(2,1)} %copy-done.19) | copy-start | bytes 2949124
  87.7 15.0 %copy-start.22 = (bf16[1,16,32,640]{3,2,1,0:T(8,128)(2,1)S(1)}, bf16[1,16,32,640]{3,2,1,0:T(8,128)(2,1)}, u32[]{:S(2)}) copy-start(bf16[1,16,32,640]{3,2,1,0:T(8,128)(2,1)} %param.8) | copy-start | bytes 1966084
  87.8 8.2 %collective-permute-start.24 = (bf16[40,2944]{1,0:T(8,128)(2,1)S(1)}, bf16[40,2944]{1,0:T(8,128)(2,1)S(1)}, u32[]{:S(2)}, u32[]{:S(2)}) collective-permute-start(bf16[40,2944]{1,0:T(8,128)(2,1)S(1)} %add_convert_fusion.1), channel_id=1, source_target_pairs={{0,4},{4,8},{8,12},{12,14},{14,10},{10,6},{6,2},{2,0},{1,5},{5,9},... | collective-permute-start | bytes 706568 | tf_op jit(solution)/shard_map/ppermute | solution.py:358
  89.4 6.5 %collective-permute-start.27 = (f32[3,640]{1,0:T(4,128)S(1)}, f32[3,640]{1,0:T(4,128)S(1)}, u32[]{:S(2)}, u32[]{:S(2)}) collective-permute-start(f32[3,640]{1,0:T(4,128)S(1)} %fusion.8), channel_id=1, source_target_pairs={{0,2},{2,0},{4,6},{6,4},{8,10},{10,8},{12,14},{14,12},{1,3},{3,1},... | collective-permute-start | bytes 23048 | tf_op jit(solution)/shard_map/ppermute | solution.py:383
  89.9 6.0 %collective-permute-start.28 = (f32[3,640]{1,0:T(4,128)S(1)}, f32[3,640]{1,0:T(4,128)S(1)}, u32[]{:S(2)}, u32[]{:S(2)}) collective-permute-start(f32[3,640]{1,0:T(4,128)S(1)} %fusion.8), channel_id=1, source_target_pairs={{0,4},{2,6},{4,0},{6,2},{8,12},{10,14},{12,8},{14,10},{1,5},{3,7},... | collective-permute-start | bytes 23048 | tf_op jit(solution)/shard_map/ppermute | solution.py:383
  91.1 4.8 %collective-permute-start.29 = (f32[3,640]{1,0:T(4,128)S(1)}, f32[3,640]{1,0:T(4,128)S(1)}, u32[]{:S(2)}, u32[]{:S(2)}) collective-permute-start(f32[3,640]{1,0:T(4,128)S(1)} %fusion.8), channel_id=1, source_target_pairs={{0,6},{2,4},{4,2},{6,0},{8,14},{10,12},{12,10},{14,8},{1,7},{3,5},... | collective-permute-start | bytes 23048 | tf_op jit(solution)/shard_map/ppermute | solution.py:383
  96.0 11.4 %collective-permute-start.32 = (f32[3,640]{1,0:T(4,128)S(1)}, f32[3,640]{1,0:T(4,128)S(1)}, u32[]{:S(2)}, u32[]{:S(2)}) collective-permute-start(f32[3,640]{1,0:T(4,128)S(1)} %add_add_fusion), channel_id=1, source_target_pairs={{0,8},{4,12},{8,0},{12,4},{16,24},{20,28},{24,16},{28,20},{1,9},{5... | collective-permute-start | bytes 23048 | tf_op jit(solution)/shard_map/ppermute | solution.py:383
  98.5 9.0 %collective-permute-start.33 = (f32[3,640]{1,0:T(4,128)S(1)}, f32[3,640]{1,0:T(4,128)S(1)}, u32[]{:S(2)}, u32[]{:S(2)}) collective-permute-start(f32[3,640]{1,0:T(4,128)S(1)} %add_add_fusion), channel_id=1, source_target_pairs={{0,16},{4,20},{8,24},{12,28},{16,0},{20,4},{24,8},{28,12},{1,17},{... | collective-permute-start | bytes 23048 | tf_op jit(solution)/shard_map/ppermute | solution.py:383
  99.4 8.1 %collective-permute-start.34 = (f32[3,640]{1,0:T(4,128)S(1)}, f32[3,640]{1,0:T(4,128)S(1)}, u32[]{:S(2)}, u32[]{:S(2)}) collective-permute-start(f32[3,640]{1,0:T(4,128)S(1)} %add_add_fusion), channel_id=1, source_target_pairs={{0,24},{4,28},{8,16},{12,20},{16,8},{20,12},{24,0},{28,4},{1,25},{... | collective-permute-start | bytes 23048 | tf_op jit(solution)/shard_map/ppermute | solution.py:383
  100.6 7.5 %collective-permute-start.30 = (bf16[40,2944]{1,0:T(8,128)(2,1)S(1)}, bf16[40,2944]{1,0:T(8,128)(2,1)S(1)}, u32[]{:S(2)}, u32[]{:S(2)}) collective-permute-start(bf16[40,2944]{1,0:T(8,128)(2,1)S(1)} %add_convert_fusion), channel_id=1, source_target_pairs={{1,0},{16,17},{0,16},{17,1},{3,2},{18,19},{2,18},{19,3},{5,4},{20,... | collective-permute-start | bytes 706568 | tf_op jit(solution)/shard_map/ppermute | solution.py:561
  101.9 6.1 %collective-permute-start.31 = (bf16[40,2944]{1,0:T(8,128)(2,1)S(1)}, bf16[40,2944]{1,0:T(8,128)(2,1)S(1)}, u32[]{:S(2)}, u32[]{:S(2)}) collective-permute-start(bf16[40,2944]{1,0:T(8,128)(2,1)S(1)} %add_convert_fusion), channel_id=1, source_target_pairs={{1,16},{16,1},{3,18},{18,3},{5,20},{20,5},{7,22},{22,7},{9,24},{24... | collective-permute-start | bytes 706568 | tf_op jit(solution)/shard_map/ppermute | solution.py:562
  (22 other events, 62.9 us)

commit v7 on v6

--- a/solution.py
+++ b/solution.py
@@ -449,14 +449,14 @@
         (jax.ShapeDtypeStruct((2, chans), F32), shifted, jax.ShapeDtypeStruct((chans, 2 * cells), BF16)),
         [SMEM_SPEC] * 2 + [VMEM_SPEC] * 6,
         [pltpu.VMEM((chans, 2 * cells), F32)],
-        16, flops // 4,
+        8, flops // 4,
     )(dev, table, latent, lat_far, cot_b, cot_far, gn_gain, gn_shift)
     pieces = call(
         partial(grad_kernel, cols),
         [jax.ShapeDtypeStruct((2 * part, cols.lead), BF16)] * (2 * zs),
         [SMEM_SPEC] + [VMEM_SPEC] * 2,
         [],
-        20, flops // 2,
+        4, flops // 2,
     )(dev, acts, cot_t)
     stages = Stages([2 * zs - 3, 3] if paired else [1], 2 * part if paired else chans)
     staged = paired
@@ -469,7 +469,7 @@
              jax.ShapeDtypeStruct(image, BF16), jax.ShapeDtypeStruct(image, BF16)) + extra,
             [SMEM_SPEC] * 2 + [VMEM_SPEC] * 7,
             [pltpu.VMEM((2 * half, width, stages.width), F32)] if staged else [],
-            18, flops // 4,
+            8, flops // 4,
         )(dev, table, stats, gn_gain, gn_shift, latent, lat_far, cot_b, cot_far)
 
     total_of = jax.ShapeDtypeStruct((2 * cells, chans), F32)
@@ -477,14 +477,14 @@
     def back_first(cots, blocks):
         return call(
             partial(back_kernel, cols, stages, 0), total_of,
-            [SMEM_SPEC] + [VMEM_SPEC] * (1 + len(blocks)), [], 20, flops // 4,
+            [SMEM_SPEC] + [VMEM_SPEC] * (1 + len(blocks)), [], 4, flops // 4,
         )(dev, cots, *blocks)
 
     def back_last(cots, earlier, slopes, blocks):
         return call(
             partial(back_kernel, cols, stages, len(stages.counts) - 1), jax.ShapeDtypeStruct((2, chans), F32),
             [SMEM_SPEC] + [VMEM_SPEC] * (3 + len(earlier) + len(blocks)),
-            [pltpu.VMEM(total_of.shape, F32)], 24, flops // 4,
+            [pltpu.VMEM(total_of.shape, F32)], 8, flops // 4,
         )(dev, cots, *earlier, *slopes, *blocks)
 
     def conv_first(blocks):
@@ -493,7 +493,7 @@
             partial(conv_both_kernel, cols, stages, 0),
             (jax.ShapeDtypeStruct((cells, wide), F32), jax.ShapeDtypeStruct((cells, wide), BF16)),
             [SMEM_SPEC] + [VMEM_SPEC] * (1 + len(blocks)),
-            [pltpu.VMEM((2 * cells, wide), F32)], 18, flops // 4,
+            [pltpu.VMEM((2 * cells, wide), F32)], 6, flops // 4,
         )(dev, acts, *blocks)
 
     def conv_far(blocks):
@@ -502,14 +502,14 @@
             partial(conv_far_kernel, cols, stages, len(stages.counts) - 1),
             jax.ShapeDtypeStruct((cells, wide), BF16),
             [SMEM_SPEC] + [VMEM_SPEC] * (1 + len(blocks)),
-            [pltpu.VMEM((cells, wide), F32)], 16, flops // 8,
+            [pltpu.VMEM((cells, wide), F32)], 4, flops // 8,
         )(dev, acts, *blocks)
 
     def conv_own(got, earlier, blocks):
         return call(
             partial(conv_own_kernel, cols, stages), jax.ShapeDtypeStruct((half, width, chans), BF16),
             [SMEM_SPEC] + [VMEM_SPEC] * (4 + len(earlier) + len(blocks)),
-            [pltpu.VMEM((cells, stages.widths[-1]), F32)], 18, flops // 4,
+            [pltpu.VMEM((cells, stages.widths[-1]), F32)], 8, flops // 4,
         )(dev, acts, got, latent, conv_bias, *earlier, *blocks)
 
     def chip_sum(sums):

time: 111 us -> 111 us (level)
  transfers between devices with their start and end apart: 35 -> 35, of which waited for: 7 -> 8; matrix products, arithmetic and copies ran while one was open for 8% -> 8% of each run, Pallas kernels for 32% -> 32%
where the time goes in v7:
time: 111 us; the launch traced here: 110 us
  Pallas kernels  35.5 us (32%)
  starting transfers between devices  34.3 us (31%)
  local copies, waits for them, and re-layouts  15.6 us (14%)
  waiting for transfers between devices  14.2 us (13%)
  other arithmetic  8.4 us (8%)
  between operations  1.78 us (2%)
    ppermute x8, starting transfers between devices, up(): return lax.ppermute(value, NODE, self.ahead)  13.9 us
    unnamed x70, local copies, waits for them, and re-layouts  12.2 us
    ppermute x6, starting transfers between devices, sum_over(): value_in = lax.ppermute(value, axes, [(s, s ^ mask) for s in range(count)])  8.01 us
    ppermute x10, waiting for transfers between devices, swap(): return lax.ppermute(value, axis, [(0, 1), (1, 0)])  6.28 us
    ppermute x10, starting transfers between devices, swap(): return lax.ppermute(value, axis, [(0, 1), (1, 0)])  5.64 us
    pallas_call x1, Pallas kernels, slopes_of(): call(partial(slope_kernel, stages), (jax.ShapeDtypeStruct((3, 2 * half +...  4.98 us
    pallas_call x1, Pallas kernels, per_device(): call(partial(act_kernel, order), (jax.ShapeDtypeStruct((2, chans), F32),...  4.87 us
    pallas_call x1, Pallas kernels, conv_own(): call(partial(conv_own_kernel, cols, stages), jax.ShapeDtypeStruct((half,...  4.79 us
  transfers between devices with their start and end apart: 35, of which 8 were waited for; matrix products, arithmetic and copies ran while one was open for 8% of the time, Pallas kernels for 32%

profile of v7, /device:TPU:0, one launch (start us, length us, event | category | flops | bytes accessed | tf_op | source)
XLA Modules:
  0.0 109.7 jit_solution(9867268119246602574)
XLA Ops:
  0.6 1.3 %fusion = (bf16[40,2944]{1,0:T(8,128)(2,1)S(1)}, bf16[40,2944]{1,0:T(8,128)(2,1)S(1)}) fusion(f32[1,40,5760]{2,1,0:T(8,128)} %param.10, s32[]{:T(128)S(6)} %select_n.60, s32[]{:T(128)S(6)} %select_n.61), kind=kLoop, calls=%fused_computation.13 | loop fusion | bytes 942088 | tf_op jit(solution)/shard_map/convert_element_type | solution.py:416
  2.5 2.1 %fusion.6 = (f32[640]{0:T(1024)S(1)}, bf16[16,32,640]{2,1,0:T(8,128)(2,1)S(1)}) fusion(f32[1,16,32,640]{3,2,1,0:T(8,128)} %param.9), kind=kLoop, calls=%fused_computation.28 | loop fusion | flops 654720 | bytes 1968640 | tf_op jit(solution)/shard_map/reduce_sum | solution.py:516
  5.2 2.7 %collective-permute-start.4 = (bf16[80,2944]{1,0:T(8,128)(2,1)S(1)}, bf16[80,2944]{1,0:T(8,128)(2,1)S(1)}, u32[]{:S(2)}, u32[]{:S(2)}) collective-permute-start(bf16[80,2944]{1,0:T(8,128)(2,1)S(1)} %maximum_select_fusion.refs_0_), channel_id=1, source_target_pairs={{0,4},{4,8},{8,12},{12,14},{14,10},{10,6},{6,2},{2,0},{1,5},{5,9},... | collective-permute-start | bytes 1413128 | tf_op jit(solution)/shard_map/ppermute | solution.py:358
  8.0 1.9 %collective-permute-start.6 = (bf16[40,2944]{1,0:T(8,128)(2,1)S(1)}, bf16[40,2944]{1,0:T(8,128)(2,1)}, u32[]{:S(2)}, u32[]{:S(2)}) collective-permute-start(bf16[40,2944]{1,0:T(8,128)(2,1)S(1)} %get-tuple-element.103), channel_id=1, source_target_pairs={{0,16},{16,0},{1,17},{17,1},{2,18},{18,2},{3,19},{19,3},{4,20},{20... | collective-permute-start | bytes 706568 | tf_op jit(solution)/shard_map/ppermute | solution.py:341
  10.0 4.9 %shard_map.119 = (f32[2,640]{1,0:T(2,128)S(1)}, bf16[3,34,32,640]{3,2,1,0:T(8,128)(2,1)S(1)}, bf16[640,1024]{1,0:T(8,128)(2,1)S(1)}) custom-call(s32[1]{0:T(128)} %bitcast.dev, s32[32,24]{1,0:T(8,128)S(1)} %copy-done.30, bf16[16,32,640]{2,1,0:T(8,128)(2,1)S(1)} %bitcast.19, bf16[16,32,640]{2,1,0:T(8,128)(2,1)} %collective-permute-done.lat_far, ...), custom_call_target="tpu_custom_call" | custom-call | flops 964689920 | tf_op jit(solution)/shard_map/pallas_call | solution.py:447
  14.9 4.6 %shard_map.120 = (bf16[80,2944]{1,0:T(8,128)(2,1)S(1)}, bf16[80,2944]{1,0:T(8,128)(2,1)S(1)}, bf16[80,2944]{1,0:T(8,128)(2,1)S(1)}, bf16[80,2944]{1,0:T(8,128)(2...) custom-call(s32[1]{0:T(128)} %bitcast.dev, ...), custom_call_target="tpu_custom_call" | custom-call | flops 1929379840 | tf_op jit(solution)/shard_map/pallas_call | solution.py:454
  19.6 0.8 copy-done.23
  20.3 0.8 copy-done.24
  22.0 2.0 %collective-permute-start.10 = (bf16[80,2944]{1,0:T(8,128)(2,1)S(1)}, bf16[80,2944]{1,0:T(8,128)(2,1)S(1)}, u32[]{:S(2)}, u32[]{:S(2)}) collective-permute-start(bf16[80,2944]{1,0:T(8,128)(2,1)S(1)} %get-tuple-element.57), channel_id=1, source_target_pairs={{0,16},{16,0},{1,17},{17,1},{2,18},{18,2},{3,19},{19,3},{4,20},{20... | collective-permute-start | bytes 1413128 | tf_op jit(solution)/shard_map/ppermute | solution.py:333
  24.0 1.6 %collective-permute-start.8 = (bf16[80,2944]{1,0:T(8,128)(2,1)S(1)}, bf16[80,2944]{1,0:T(8,128)(2,1)S(1)}, u32[]{:S(2)}, u32[]{:S(2)}) collective-permute-start(bf16[80,2944]{1,0:T(8,128)(2,1)S(1)} %collective-permute-done.4.refs_1_), channel_id=1, source_target_pairs={{0,4},{4,8},{8,12},{12,14},{14,10},{10,6},{6,2},{2,0},{1,5},{5,9},... | collective-permute-start | bytes 1413128 | tf_op jit(solution)/shard_map/ppermute | solution.py:358
  26.1 5.0 %shard_map.121 = (bf16[3,34,32,768]{3,2,1,0:T(8,128)(2,1)S(1)}, bf16[32,32,640]{2,1,0:T(8,128)(2,1)S(1)}, bf16[32,32,640]{2,1,0:T(8,128)(2,1)S(1)}, bf16[640,768]{1,0:T(8,128)(2,1)S(1)}) custom-call(s32[1]{0:T(128)} %bitcast.dev, s32[32,24]{1,0:T(8,128)S(1)} %copy-done.30, f32[2,640]{1,0:T(2,128)S(1)} %get-tuple-element.58.stats, f32[1,640]{1,0:T(1,128)S(1)} %copy-done.27, ...), custom_call_target="tpu_custom_call" | custom-call | flops 964689920 | tf_op jit(solution)/shard_map/pallas_call | solution.py:466
  31.1 1.0 copy-done.19
  32.0 3.7 %collective-permute-done.10 = bf16[80,2944]{1,0:T(8,128)(2,1)S(1)} collective-permute-done((bf16[80,2944]{1,0:T(8,128)(2,1)S(1)}, bf16[80,2944]{1,0:T(8,128)(2,1)S(1)}, u32[]{:S(2)}, u32[]{:S(2)}) %collective-permute-start.10) | collective-permute-done | bytes 471072 | tf_op jit(solution)/shard_map/ppermute | solution.py:333
  35.7 1.2 %collective-permute-done.9.refs_4_ = bf16[80,2944]{1,0:T(8,128)(2,1)S(1)} collective-permute-done((bf16[80,2944]{1,0:T(8,128)(2,1)S(1)}, bf16[80,2944]{1,0:T(8,128)(2,1)S(1)}, u32[]{:S(2)}, u32[]{:S(2)}) %collective-permute-start.9) | collective-permute-done | bytes 471072 | tf_op jit(solution)/shard_map/ppermute | solution.py:361
  37.0 1.6 %collective-permute-start.11 = (bf16[80,2944]{1,0:T(8,128)(2,1)S(1)}, bf16[80,2944]{1,0:T(8,128)(2,1)S(1)}, u32[]{:S(2)}, u32[]{:S(2)}) collective-permute-start(bf16[80,2944]{1,0:T(8,128)(2,1)S(1)} %collective-permute-done.8.refs_3_), channel_id=1, source_target_pairs={{0,4},{4,8},{8,12},{12,14},{14,10},{10,6},{6,2},{2,0},{1,5},{5,9},... | collective-permute-start | bytes 1413128 | tf_op jit(solution)/shard_map/ppermute | solution.py:358
  39.1 1.6 %collective-permute-start.18 = (bf16[40,2944]{1,0:T(8,128)(2,1)S(1)}, bf16[40,2944]{1,0:T(8,128)(2,1)S(1)}, u32[]{:S(2)}, u32[]{:S(2)}) collective-permute-start(bf16[40,2944]{1,0:T(8,128)(2,1)S(1)} %get-tuple-element.102), channel_id=1, source_target_pairs={{0,4},{4,8},{8,12},{12,14},{14,10},{10,6},{6,2},{2,0},{1,5},{5,9},... | collective-permute-start | bytes 706568 | tf_op jit(solution)/shard_map/ppermute | solution.py:358
  41.2 4.8 %shard_map.123 = (f32[512,512]{1,0:T(8,128)S(1)}, bf16[512,512]{1,0:T(8,128)(2,1)}) custom-call(s32[1]{0:T(128)} %bitcast.dev, bf16[3,34,32,640]{3,2,1,0:T(8,128)(2,1)S(1)} %get-tuple-element.50.acts, bf16[80,2944]{1,0:T(8,128)(2,1)S(1)} %maximum_select_fusion.refs_0_, bf16[80,2944]{1,0:T(8,128)(2,1)S(1)} %collective-permute-done.4.refs_1_, ...), custom_call_target="tpu_custom_call" | custom-call | flops 964689920 | tf_op jit(solution)/shard_map/pallas_call | solution.py:492
  46.0 1.0 copy-done.17
  47.0 1.0 copy-done.8
  48.0 1.0 copy-done.10
  49.1 1.0 copy-done.12
  50.1 4.6 %shard_map.122.refs_0_ = f32[1024,640]{1,0:T(8,128)S(1)} custom-call(s32[1]{0:T(128)} %bitcast.dev, bf16[3,34,32,768]{3,2,1,0:T(8,128)(2,1)S(1)} %get-tuple-element.63.cots, bf16[80,2944]{1,0:T(8,128)(2,1)S(1)} %copy-done.8, bf16[80,2944]{1,0:T(8,128)(2,1)S(1)} %copy-done.10, bf16[80,2944]{1,0:T(8,128)(2,1)S(1)} %copy-done.12, ...), custom_call_target="tpu_custom_call" | custom-call | flops 964689920 | tf_op jit(solution)/shard_map/pallas_call | solution.py:478
  56.3 1.6 %collective-permute-start.14 = (bf16[40,2944]{1,0:T(8,128)(2,1)}, bf16[40,2944]{1,0:T(8,128)(2,1)S(1)}, u32[]{:S(2)}, u32[]{:S(2)}) collective-permute-start(bf16[40,2944]{1,0:T(8,128)(2,1)} %slice.70), channel_id=1, source_target_pairs={{0,4},{4,8},{8,12},{12,14},{14,10},{10,6},{6,2},{2,0},{1,5},{5,9},... | collective-permute-start | bytes 706568 | tf_op jit(solution)/shard_map/ppermute | solution.py:358
  59.1 1.0 add_convert_fusion.3
  60.0 1.6 %collective-permute-start.19 = (bf16[40,2944]{1,0:T(8,128)(2,1)}, bf16[40,2944]{1,0:T(8,128)(2,1)}, u32[]{:S(2)}, u32[]{:S(2)}) collective-permute-start(bf16[40,2944]{1,0:T(8,128)(2,1)} %get-tuple-element.100), channel_id=1, source_target_pairs={{0,4},{4,8},{8,12},{12,14},{14,10},{10,6},{6,2},{2,0},{1,5},{5,9},... | collective-permute-start | bytes 706568 | tf_op jit(solution)/shard_map/ppermute | solution.py:358
  61.6 2.6 %collective-permute-done.16 = bf16[80,2944]{1,0:T(8,128)(2,1)S(1)} collective-permute-done((bf16[80,2944]{1,0:T(8,128)(2,1)S(1)}, bf16[80,2944]{1,0:T(8,128)(2,1)S(1)}, u32[]{:S(2)}, u32[]{:S(2)}) %collective-permute-start.16) | collective-permute-done | bytes 471072 | tf_op jit(solution)/shard_map/ppermute | solution.py:333
  64.2 0.8 copy-done.34
  66.2 1.0 collective-permute-start.2
  67.5 2.3 %collective-permute-done.19 = bf16[40,2944]{1,0:T(8,128)(2,1)} collective-permute-done((bf16[40,2944]{1,0:T(8,128)(2,1)}, bf16[40,2944]{1,0:T(8,128)(2,1)}, u32[]{:S(2)}, u32[]{:S(2)}) %collective-permute-start.19) | collective-permute-done | bytes 235552 | tf_op jit(solution)/shard_map/ppermute | solution.py:358
  69.8 2.0 %collective-permute-done.22 = bf16[40,2944]{1,0:T(8,128)(2,1)} collective-permute-done((bf16[40,2944]{1,0:T(8,128)(2,1)}, bf16[40,2944]{1,0:T(8,128)(2,1)}, u32[]{:S(2)}, u32[]{:S(2)}) %collective-permute-start.22) | collective-permute-done | bytes 235552 | tf_op jit(solution)/shard_map/ppermute | solution.py:361
  71.8 1.7 %add_convert_fusion.2 = (bf16[40,2944]{1,0:T(8,128)(2,1)S(1)}, bf16[40,2944]{1,0:T(8,128)(2,1)S(1)}) fusion(bf16[40,2944]{1,0:T(8,128)(2,1)} %collective-permute-done.22, bf16[80,2944]{1,0:T(8,128)(2,1)} %copy-done.34, bf16[80,2944]{1,0:T(8,128)(2,1)} %copy-done.23, bf16[40,2944]{1,0:T(8,128)(2,1)} %collective-permute-done.19), kind=kLoop, calls=%fused_computation.5 | loop fusion | flops 1413120 | bytes 1884160 | tf_op jit(solution)/shard_map/convert_element_type | solution.py:392
  73.5 1.6 %collective-permute-start.20 = (bf16[40,2944]{1,0:T(8,128)(2,1)S(1)}, bf16[40,2944]{1,0:T(8,128)(2,1)S(1)}, u32[]{:S(2)}, u32[]{:S(2)}) collective-permute-start(bf16[40,2944]{1,0:T(8,128)(2,1)S(1)} %get-tuple-element.98), channel_id=1, source_target_pairs={{0,4},{4,8},{8,12},{12,14},{14,10},{10,6},{6,2},{2,0},{1,5},{5,9},... | collective-permute-start | bytes 706568 | tf_op jit(solution)/shard_map/ppermute | solution.py:358
  75.6 1.0 select_bitcast_fusion.1
  76.6 2.2 %copy-done.1 = bf16[3,34,32,640]{3,2,1,0:T(8,128)(2,1)S(1)} copy-done((bf16[3,34,32,640]{3,2,1,0:T(8,128)(2,1)S(1)}, bf16[3,34,32,640]{3,2,1,0:T(8,128)(2,1)}, u32[]{:S(2)}) %copy-start.1) | copy-done | bytes 4177944
  78.7 2.5 %shard_map.125 = bf16[512,256]{1,0:T(8,128)(2,1)S(1)} custom-call(s32[1]{0:T(128)} %bitcast.dev, bf16[3,34,32,640]{3,2,1,0:T(8,128)(2,1)S(1)} %copy-done.1, bf16[80,2944]{1,0:T(8,128)(2,1)S(1)} %collective-permute-done.11.refs_3_.refs_0_, bf16[80,2944]{1,0:T(8,128)(2,1)S(1)} %copy-done.6, bf16[40,2944]{1,0:T(8,128)(2,1)S(1)} %collective-permute-done.14.refs_5_.refs_2_, ...), custom_call_target="tpu_custom_call" | custom-call | flops 482344960 | tf_op jit(solution)/shard_map/pallas_call | solution.py:501
  81.4 1.3 %copy-done.16 = bf16[32,32,640]{2,1,0:T(8,128)(2,1)S(1)} copy-done((bf16[32,32,640]{2,1,0:T(8,128)(2,1)S(1)}, bf16[32,32,640]{2,1,0:T(8,128)(2,1)}, u32[]{:S(2)}) %copy-start.16) | copy-done | bytes 1310744
  82.7 4.3 %shard_map.124 = f32[2,640]{1,0:T(2,128)S(1)} custom-call(s32[1]{0:T(128)} %bitcast.dev, bf16[3,34,32,768]{3,2,1,0:T(8,128)(2,1)S(1)} %copy-done.4, f32[1024,640]{1,0:T(8,128)S(1)} %shard_map.122.refs_0_, bf16[32,32,640]{2,1,0:T(8,128)(2,1)S(1)} %copy-done.14, bf16[32,32,640]{2,1,0:T(8,128)(2,1)S(1)} %copy-done.16, ...), custom_call_target="tpu_custom_call" | custom-call | flops 964689920 | tf_op jit(solution)/shard_map/pallas_call | solution.py:484
  87.8 1.6 %collective-permute-start.24 = (bf16[40,2944]{1,0:T(8,128)(2,1)S(1)}, bf16[40,2944]{1,0:T(8,128)(2,1)S(1)}, u32[]{:S(2)}, u32[]{:S(2)}) collective-permute-start(bf16[40,2944]{1,0:T(8,128)(2,1)S(1)} %add_convert_fusion.1), channel_id=1, source_target_pairs={{0,4},{4,8},{8,12},{12,14},{14,10},{10,6},{6,2},{2,0},{1,5},{5,9},... | collective-permute-start | bytes 706568 | tf_op jit(solution)/shard_map/ppermute | solution.py:358
  89.9 1.2 %collective-permute-start.28 = (f32[3,640]{1,0:T(4,128)S(1)}, f32[3,640]{1,0:T(4,128)S(1)}, u32[]{:S(2)}, u32[]{:S(2)}) collective-permute-start(f32[3,640]{1,0:T(4,128)S(1)} %fusion.8), channel_id=1, source_target_pairs={{0,4},{2,6},{4,0},{6,2},{8,12},{10,14},{12,8},{14,10},{1,5},{3,7},... | collective-permute-start | bytes 23048 | tf_op jit(solution)/shard_map/ppermute | solution.py:383
  91.2 1.8 %collective-permute-start.29 = (f32[3,640]{1,0:T(4,128)S(1)}, f32[3,640]{1,0:T(4,128)S(1)}, u32[]{:S(2)}, u32[]{:S(2)}) collective-permute-start(f32[3,640]{1,0:T(4,128)S(1)} %fusion.8), channel_id=1, source_target_pairs={{0,6},{2,4},{4,2},{6,0},{8,14},{10,12},{12,10},{14,8},{1,7},{3,5},... | collective-permute-start | bytes 23048 | tf_op jit(solution)/shard_map/ppermute | solution.py:383
  93.0 1.0 fusion.4
  94.0 1.9 %collective-permute-done.27 = f32[3,640]{1,0:T(4,128)S(1)} collective-permute-done((f32[3,640]{1,0:T(4,128)S(1)}, f32[3,640]{1,0:T(4,128)S(1)}, u32[]{:S(2)}, u32[]{:S(2)}) %collective-permute-start.27) | collective-permute-done | bytes 7712 | tf_op jit(solution)/shard_map/ppermute | solution.py:383
  96.0 2.5 %collective-permute-start.32 = (f32[3,640]{1,0:T(4,128)S(1)}, f32[3,640]{1,0:T(4,128)S(1)}, u32[]{:S(2)}, u32[]{:S(2)}) collective-permute-start(f32[3,640]{1,0:T(4,128)S(1)} %add_add_fusion), channel_id=1, source_target_pairs={{0,8},{4,12},{8,0},{12,4},{16,24},{20,28},{24,16},{28,20},{1,9},{5... | collective-permute-start | bytes 23048 | tf_op jit(solution)/shard_map/ppermute | solution.py:383
  98.5 0.9 collective-permute-start.33
  99.4 1.1 collective-permute-start.34
  100.6 1.3 %collective-permute-start.30 = (bf16[40,2944]{1,0:T(8,128)(2,1)S(1)}, bf16[40,2944]{1,0:T(8,128)(2,1)S(1)}, u32[]{:S(2)}, u32[]{:S(2)}) collective-permute-start(bf16[40,2944]{1,0:T(8,128)(2,1)S(1)} %add_convert_fusion), channel_id=1, source_target_pairs={{1,0},{16,17},{0,16},{17,1},{3,2},{18,19},{2,18},{19,3},{5,4},{20,... | collective-permute-start | bytes 706568 | tf_op jit(solution)/shard_map/ppermute | solution.py:561
  102.6 4.8 %shard_map.126 = bf16[16,32,640]{2,1,0:T(8,128)(2,1)} custom-call(s32[1]{0:T(128)} %bitcast.dev, bf16[3,34,32,640]{3,2,1,0:T(8,128)(2,1)S(1)} %copy-done.2, bf16[512,256]{1,0:T(8,128)(2,1)S(1)} %collective-permute-done.25.got, bf16[16,32,640]{2,1,0:T(8,128)(2,1)S(1)} %bitcast.21, f32[1,640]{1,0:T(1,128)S(1)} %copy-done.26, f32[512,512]{1,0:T(8,128)S(1)} %copy-done.18, ...), custom_call_target="tpu_custom_call" | custom-call | flops 964689920 | tf_op jit(solution)/shard_map/pallas_call | solution.py:509
  108.6 1.1 %multiply_subtract_fusion = f32[1,40,5760]{2,1,0:T(8,128)} fusion(f32[1,40,5760]{2,1,0:T(8,128)S(1)} %copy-done.31, bf16[1,40,2816]{2,1,0:T(8,128)(2,1)S(1)} %fusion.4, bf16[1,40,2944]{2,1,0:T(8,128)(2,1)S(1)} %select_bitcast_fusion.1, bf16[1,40,2816]{2,1,0:T(8,128)(2,1)S(1)} %fusion.3, bf16[1,40,2944]{2,1,0:T(8,128)(2,1)S(1)} %select_bitcast_fusion, ...), kind=kLoop, calls=%fused_computation | loop fusion | flops 2764800 | bytes 2764804 | tf_op jit(solution)/shard_map/sub | solution.py:582
  (121 shorter events, 11.2 us)
Async XLA Ops:
  2.0 3.2 %collective-permute-start.3 = (bf16[40,2944]{1,0:T(8,128)(2,1)S(1)}, bf16[40,2944]{1,0:T(8,128)(2,1)S(1)}, u32[]{:S(2)}, u32[]{:S(2)}) collective-permute-start(bf16[40,2944]{1,0:T(8,128)(2,1)S(1)} %get-tuple-element.104), channel_id=1, source_target_pairs={{0,1},{1,0},{2,3},{3,2},{4,5},{5,4},{6,7},{7,6},{8,9},{9,8},{10,11... | collective-permute-start | bytes 706568 | tf_op jit(solution)/shard_map/ppermute | solution.py:333
  4.6 5.3 %collective-permute-start.1 = (bf16[16,32,640]{2,1,0:T(8,128)(2,1)S(1)}, bf16[16,32,640]{2,1,0:T(8,128)(2,1)}, u32[]{:S(2)}, u32[]{:S(2)}) collective-permute-start(bf16[16,32,640]{2,1,0:T(8,128)(2,1)S(1)} %get-tuple-element.96.cot_own), channel_id=1, source_target_pairs={{0,1},{1,0},{2,3},{3,2},{4,5},{5,4},{6,7},{7,6},{8,9},{9,8},{10,11... | collective-permute-start | bytes 1966088 | tf_op jit(solution)/shard_map/ppermute | solution.py:333
  4.7 5.3 %collective-permute-start = (bf16[16,32,640]{2,1,0:T(8,128)(2,1)S(1)}, bf16[16,32,640]{2,1,0:T(8,128)(2,1)}, u32[]{:S(2)}, u32[]{:S(2)}) collective-permute-start(bf16[16,32,640]{2,1,0:T(8,128)(2,1)S(1)} %bitcast.18), channel_id=1, source_target_pairs={{0,1},{1,0},{2,3},{3,2},{4,5},{5,4},{6,7},{7,6},{8,9},{9,8},{10,11... | collective-permute-start | bytes 1966088 | tf_op jit(solution)/shard_map/ppermute | solution.py:333
  5.2 36.0 %copy-start.7 = (bf16[80,2944]{1,0:T(8,128)(2,1)}, bf16[80,2944]{1,0:T(8,128)(2,1)S(1)}, u32[]{:S(2)}) copy-start(bf16[80,2944]{1,0:T(8,128)(2,1)S(1)} %maximum_select_fusion.refs_0_) | copy-start | bytes 1413124
  5.2 16.7 %collective-permute-start.4 = (bf16[80,2944]{1,0:T(8,128)(2,1)S(1)}, bf16[80,2944]{1,0:T(8,128)(2,1)S(1)}, u32[]{:S(2)}, u32[]{:S(2)}) collective-permute-start(bf16[80,2944]{1,0:T(8,128)(2,1)S(1)} %maximum_select_fusion.refs_0_), channel_id=1, source_target_pairs={{0,4},{4,8},{8,12},{12,14},{14,10},{10,6},{6,2},{2,0},{1,5},{5,9},... | collective-permute-start | bytes 1413128 | tf_op jit(solution)/shard_map/ppermute | solution.py:358
  8.0 14.0 %collective-permute-start.5 = (bf16[80,2944]{1,0:T(8,128)(2,1)S(1)}, bf16[80,2944]{1,0:T(8,128)(2,1)S(1)}, u32[]{:S(2)}, u32[]{:S(2)}) collective-permute-start(bf16[80,2944]{1,0:T(8,128)(2,1)S(1)} %maximum_select_fusion.refs_0_), channel_id=1, source_target_pairs={{4,0},{8,4},{12,8},{14,12},{10,14},{6,10},{2,6},{0,2},{5,1},{9,5},... | collective-permute-start | bytes 1413128 | tf_op jit(solution)/shard_map/ppermute | solution.py:361
  8.0 14.0 %collective-permute-start.6 = (bf16[40,2944]{1,0:T(8,128)(2,1)S(1)}, bf16[40,2944]{1,0:T(8,128)(2,1)}, u32[]{:S(2)}, u32[]{:S(2)}) collective-permute-start(bf16[40,2944]{1,0:T(8,128)(2,1)S(1)} %get-tuple-element.103), channel_id=1, source_target_pairs={{0,16},{16,0},{1,17},{17,1},{2,18},{18,2},{3,19},{19,3},{4,20},{20... | collective-permute-start | bytes 706568 | tf_op jit(solution)/shard_map/ppermute | solution.py:341
  9.9 12.0 %collective-permute-start.7 = (bf16[40,2944]{1,0:T(8,128)(2,1)S(1)}, bf16[40,2944]{1,0:T(8,128)(2,1)S(1)}, u32[]{:S(2)}, u32[]{:S(2)}) collective-permute-start(bf16[40,2944]{1,0:T(8,128)(2,1)S(1)} %get-tuple-element.104), channel_id=1, source_target_pairs={{0,16},{16,0},{1,17},{17,1},{2,18},{18,2},{3,19},{19,3},{4,20},{20... | collective-permute-start | bytes 706568 | tf_op jit(solution)/shard_map/ppermute | solution.py:341
  14.9 26.3 %copy-start = (bf16[3,34,32,640]{3,2,1,0:T(8,128)(2,1)}, bf16[3,34,32,640]{3,2,1,0:T(8,128)(2,1)S(1)}, u32[]{:S(2)}) copy-start(bf16[3,34,32,640]{3,2,1,0:T(8,128)(2,1)S(1)} %get-tuple-element.50.acts) | copy-start | bytes 12533764
  21.9 19.3 %copy-start.9 = (bf16[80,2944]{1,0:T(8,128)(2,1)}, bf16[80,2944]{1,0:T(8,128)(2,1)S(1)}, u32[]{:S(2)}) copy-start(bf16[80,2944]{1,0:T(8,128)(2,1)S(1)} %collective-permute-done.4.refs_1_) | copy-start | bytes 1413124
  22.0 19.3 %copy-start.11 = (bf16[80,2944]{1,0:T(8,128)(2,1)}, bf16[80,2944]{1,0:T(8,128)(2,1)S(1)}, u32[]{:S(2)}) copy-start(bf16[80,2944]{1,0:T(8,128)(2,1)S(1)} %collective-permute-done.5.refs_2_) | copy-start | bytes 1413124
  22.0 13.8 %collective-permute-start.10 = (bf16[80,2944]{1,0:T(8,128)(2,1)S(1)}, bf16[80,2944]{1,0:T(8,128)(2,1)S(1)}, u32[]{:S(2)}, u32[]{:S(2)}) collective-permute-start(bf16[80,2944]{1,0:T(8,128)(2,1)S(1)} %get-tuple-element.57), channel_id=1, source_target_pairs={{0,16},{16,0},{1,17},{17,1},{2,18},{18,2},{3,19},{19,3},{4,20},{20... | collective-permute-start | bytes 1413128 | tf_op jit(solution)/shard_map/ppermute | solution.py:333
  24.0 11.8 %collective-permute-start.8 = (bf16[80,2944]{1,0:T(8,128)(2,1)S(1)}, bf16[80,2944]{1,0:T(8,128)(2,1)S(1)}, u32[]{:S(2)}, u32[]{:S(2)}) collective-permute-start(bf16[80,2944]{1,0:T(8,128)(2,1)S(1)} %collective-permute-done.4.refs_1_), channel_id=1, source_target_pairs={{0,4},{4,8},{8,12},{12,14},{14,10},{10,6},{6,2},{2,0},{1,5},{5,9},... | collective-permute-start | bytes 1413128 | tf_op jit(solution)/shard_map/ppermute | solution.py:358
  25.5 11.4 %collective-permute-start.9 = (bf16[80,2944]{1,0:T(8,128)(2,1)S(1)}, bf16[80,2944]{1,0:T(8,128)(2,1)S(1)}, u32[]{:S(2)}, u32[]{:S(2)}) collective-permute-start(bf16[80,2944]{1,0:T(8,128)(2,1)S(1)} %collective-permute-done.5.refs_2_), channel_id=1, source_target_pairs={{4,0},{8,4},{12,8},{14,12},{10,14},{6,10},{2,6},{0,2},{5,1},{9,5},... | collective-permute-start | bytes 1413128 | tf_op jit(solution)/shard_map/ppermute | solution.py:361
  26.0 28.7 %collective-permute-start.13 = (bf16[80,2944]{1,0:T(8,128)(2,1)S(1)}, bf16[80,2944]{1,0:T(8,128)(2,1)S(1)}, u32[]{:S(2)}, u32[]{:S(2)}) collective-permute-start(bf16[80,2944]{1,0:T(8,128)(2,1)S(1)} %get-tuple-element.66), channel_id=1, source_target_pairs={{0,16},{16,0},{1,17},{17,1},{2,18},{18,2},{3,19},{19,3},{4,20},{20... | collective-permute-start | bytes 1413128 | tf_op jit(solution)/shard_map/ppermute | solution.py:333
  32.0 13.9 %copy-start.3 = (bf16[3,34,32,768]{3,2,1,0:T(8,128)(2,1)}, bf16[3,34,32,768]{3,2,1,0:T(8,128)(2,1)S(1)}, u32[]{:S(2)}) copy-start(bf16[3,34,32,768]{3,2,1,0:T(8,128)(2,1)S(1)} %get-tuple-element.63.cots) | copy-start | bytes 15040516
  32.0 13.9 %copy-start.13 = (bf16[32,32,640]{2,1,0:T(8,128)(2,1)}, bf16[32,32,640]{2,1,0:T(8,128)(2,1)S(1)}, u32[]{:S(2)}) copy-start(bf16[32,32,640]{2,1,0:T(8,128)(2,1)S(1)} %get-tuple-element.69.refs_1_) | copy-start | bytes 3932164
  32.0 13.9 %copy-start.15 = (bf16[32,32,640]{2,1,0:T(8,128)(2,1)}, bf16[32,32,640]{2,1,0:T(8,128)(2,1)S(1)}, u32[]{:S(2)}) copy-start(bf16[32,32,640]{2,1,0:T(8,128)(2,1)S(1)} %get-tuple-element.70.refs_2_) | copy-start | bytes 3932164
  37.0 18.5 %collective-permute-start.11 = (bf16[80,2944]{1,0:T(8,128)(2,1)S(1)}, bf16[80,2944]{1,0:T(8,128)(2,1)S(1)}, u32[]{:S(2)}, u32[]{:S(2)}) collective-permute-start(bf16[80,2944]{1,0:T(8,128)(2,1)S(1)} %collective-permute-done.8.refs_3_), channel_id=1, source_target_pairs={{0,4},{4,8},{8,12},{12,14},{14,10},{10,6},{6,2},{2,0},{1,5},{5,9},... | collective-permute-start | bytes 1413128 | tf_op jit(solution)/shard_map/ppermute | solution.py:358
  38.6 16.9 %collective-permute-start.12 = (bf16[80,2944]{1,0:T(8,128)(2,1)S(1)}, bf16[80,2944]{1,0:T(8,128)(2,1)S(1)}, u32[]{:S(2)}, u32[]{:S(2)}) collective-permute-start(bf16[80,2944]{1,0:T(8,128)(2,1)S(1)} %collective-permute-done.9.refs_4_), channel_id=1, source_target_pairs={{4,0},{8,4},{12,8},{14,12},{10,14},{6,10},{2,6},{0,2},{5,1},{9,5},... | collective-permute-start | bytes 1413128 | tf_op jit(solution)/shard_map/ppermute | solution.py:361
  39.1 19.5 %collective-permute-start.18 = (bf16[40,2944]{1,0:T(8,128)(2,1)S(1)}, bf16[40,2944]{1,0:T(8,128)(2,1)S(1)}, u32[]{:S(2)}, u32[]{:S(2)}) collective-permute-start(bf16[40,2944]{1,0:T(8,128)(2,1)S(1)} %get-tuple-element.102), channel_id=1, source_target_pairs={{0,4},{4,8},{8,12},{12,14},{14,10},{10,6},{6,2},{2,0},{1,5},{5,9},... | collective-permute-start | bytes 706568 | tf_op jit(solution)/shard_map/ppermute | solution.py:358
  40.8 18.3 %collective-permute-start.21 = (bf16[40,2944]{1,0:T(8,128)(2,1)S(1)}, bf16[40,2944]{1,0:T(8,128)(2,1)S(1)}, u32[]{:S(2)}, u32[]{:S(2)}) collective-permute-start(bf16[40,2944]{1,0:T(8,128)(2,1)S(1)} %get-tuple-element.101), channel_id=1, source_target_pairs={{4,0},{8,4},{12,8},{14,12},{10,14},{6,10},{2,6},{0,2},{5,1},{9,5},... | collective-permute-start | bytes 706568 | tf_op jit(solution)/shard_map/ppermute | solution.py:361
  54.7 9.5 %collective-permute-start.16 = (bf16[80,2944]{1,0:T(8,128)(2,1)S(1)}, bf16[80,2944]{1,0:T(8,128)(2,1)S(1)}, u32[]{:S(2)}, u32[]{:S(2)}) collective-permute-start(bf16[80,2944]{1,0:T(8,128)(2,1)S(1)} %get-tuple-element.73), channel_id=1, source_target_pairs={{0,16},{16,0},{1,17},{17,1},{2,18},{18,2},{3,19},{19,3},{4,20},{20... | collective-permute-start | bytes 1413128 | tf_op jit(solution)/shard_map/ppermute | solution.py:333
  55.5 12.0 %collective-permute-start.17 = (bf16[512,512]{1,0:T(8,128)(2,1)}, bf16[512,512]{1,0:T(8,128)(2,1)}, u32[]{:S(2)}, u32[]{:S(2)}) collective-permute-start(bf16[512,512]{1,0:T(8,128)(2,1)} %get-tuple-element.74), channel_id=1, source_target_pairs={{0,1},{1,0},{2,3},{3,2},{4,5},{5,4},{6,7},{7,6},{8,9},{9,8},{10,11... | collective-permute-start | bytes 1572872 | tf_op jit(solution)/shard_map/ppermute | solution.py:333
  56.3 9.8 %collective-permute-start.14 = (bf16[40,2944]{1,0:T(8,128)(2,1)}, bf16[40,2944]{1,0:T(8,128)(2,1)S(1)}, u32[]{:S(2)}, u32[]{:S(2)}) collective-permute-start(bf16[40,2944]{1,0:T(8,128)(2,1)} %slice.70), channel_id=1, source_target_pairs={{0,4},{4,8},{8,12},{12,14},{14,10},{10,6},{6,2},{2,0},{1,5},{5,9},... | collective-permute-start | bytes 706568 | tf_op jit(solution)/shard_map/ppermute | solution.py:358
  58.6 8.9 %collective-permute-start.15 = (bf16[40,2944]{1,0:T(8,128)(2,1)}, bf16[40,2944]{1,0:T(8,128)(2,1)}, u32[]{:S(2)}, u32[]{:S(2)}) collective-permute-start(bf16[40,2944]{1,0:T(8,128)(2,1)} %slice.71), channel_id=1, source_target_pairs={{4,0},{8,4},{12,8},{14,12},{10,14},{6,10},{2,6},{0,2},{5,1},{9,5},... | collective-permute-start | bytes 706568 | tf_op jit(solution)/shard_map/ppermute | solution.py:361
  60.0 9.7 %collective-permute-start.19 = (bf16[40,2944]{1,0:T(8,128)(2,1)}, bf16[40,2944]{1,0:T(8,128)(2,1)}, u32[]{:S(2)}, u32[]{:S(2)}) collective-permute-start(bf16[40,2944]{1,0:T(8,128)(2,1)} %get-tuple-element.100), channel_id=1, source_target_pairs={{0,4},{4,8},{8,12},{12,14},{14,10},{10,6},{6,2},{2,0},{1,5},{5,9},... | collective-permute-start | bytes 706568 | tf_op jit(solution)/shard_map/ppermute | solution.py:358
  65.0 6.8 %collective-permute-start.22 = (bf16[40,2944]{1,0:T(8,128)(2,1)}, bf16[40,2944]{1,0:T(8,128)(2,1)}, u32[]{:S(2)}, u32[]{:S(2)}) collective-permute-start(bf16[40,2944]{1,0:T(8,128)(2,1)} %get-tuple-element.99), channel_id=1, source_target_pairs={{4,0},{8,4},{12,8},{14,12},{10,14},{6,10},{2,6},{0,2},{5,1},{9,5},... | collective-permute-start | bytes 706568 | tf_op jit(solution)/shard_map/ppermute | solution.py:361
  66.1 10.4 %copy-start.6 = (bf16[80,2944]{1,0:T(8,128)(2,1)S(1)}, bf16[80,2944]{1,0:T(8,128)(2,1)}, u32[]{:S(2)}) copy-start(bf16[80,2944]{1,0:T(8,128)(2,1)} %copy-done.5) | copy-start | bytes 1413124
  66.2 20.9 %collective-permute-start.2 = (bf16[80,2944]{1,0:T(8,128)(2,1)}, bf16[80,2944]{1,0:T(8,128)(2,1)S(1)}, u32[]{:S(2)}, u32[]{:S(2)}) collective-permute-start(bf16[80,2944]{1,0:T(8,128)(2,1)} %copy-done.29), channel_id=1, source_target_pairs={{0,16},{16,0},{1,17},{17,1},{2,18},{18,2},{3,19},{19,3},{4,20},{20... | collective-permute-start | bytes 1413128 | tf_op jit(solution)/shard_map/ppermute | solution.py:333
  71.8 9.6 %copy-start.14 = (bf16[32,32,640]{2,1,0:T(8,128)(2,1)S(1)}, bf16[32,32,640]{2,1,0:T(8,128)(2,1)}, u32[]{:S(2)}) copy-start(bf16[32,32,640]{2,1,0:T(8,128)(2,1)} %copy-done.13) | copy-start | bytes 3932164
  73.5 13.6 %collective-permute-start.20 = (bf16[40,2944]{1,0:T(8,128)(2,1)S(1)}, bf16[40,2944]{1,0:T(8,128)(2,1)S(1)}, u32[]{:S(2)}, u32[]{:S(2)}) collective-permute-start(bf16[40,2944]{1,0:T(8,128)(2,1)S(1)} %get-tuple-element.98), channel_id=1, source_target_pairs={{0,4},{4,8},{8,12},{12,14},{14,10},{10,6},{6,2},{2,0},{1,5},{5,9},... | collective-permute-start | bytes 706568 | tf_op jit(solution)/shard_map/ppermute | solution.py:358
  75.1 12.0 %collective-permute-start.23 = (bf16[40,2944]{1,0:T(8,128)(2,1)S(1)}, bf16[40,2944]{1,0:T(8,128)(2,1)S(1)}, u32[]{:S(2)}, u32[]{:S(2)}) collective-permute-start(bf16[40,2944]{1,0:T(8,128)(2,1)S(1)} %get-tuple-element.97), channel_id=1, source_target_pairs={{4,0},{8,4},{12,8},{14,12},{10,14},{6,10},{2,6},{0,2},{5,1},{9,5},... | collective-permute-start | bytes 706568 | tf_op jit(solution)/shard_map/ppermute | solution.py:361
  81.3 14.7 %collective-permute-start.25 = (bf16[512,256]{1,0:T(8,128)(2,1)S(1)}, bf16[512,256]{1,0:T(8,128)(2,1)S(1)}, u32[]{:S(2)}, u32[]{:S(2)}) collective-permute-start(bf16[512,256]{1,0:T(8,128)(2,1)S(1)} %shard_map.125), channel_id=1, source_target_pairs={{0,1},{1,0},{2,3},{3,2},{4,5},{5,4},{6,7},{7,6},{8,9},{9,8},{10,11... | collective-permute-start | bytes 786440 | tf_op jit(solution)/shard_map/ppermute | solution.py:333
  82.7 19.9 %copy-start.2 = (bf16[3,34,32,640]{3,2,1,0:T(8,128)(2,1)S(1)}, bf16[3,34,32,640]{3,2,1,0:T(8,128)(2,1)}, u32[]{:S(2)}) copy-start(bf16[3,34,32,640]{3,2,1,0:T(8,128)(2,1)} %copy-done) | copy-start | bytes 12533764
  87.1 2.3 %collective-permute-start.26 = (f32[3,640]{1,0:T(4,128)S(1)}, f32[3,640]{1,0:T(4,128)S(1)}, u32[]{:S(2)}, u32[]{:S(2)}) collective-permute-start(f32[3,640]{1,0:T(4,128)S(1)} %fusion.5), channel_id=1, source_target_pairs={{0,1},{1,0},{2,3},{3,2},{4,5},{5,4},{6,7},{7,6},{8,9},{9,8},{10,11... | collective-permute-start | bytes 23048 | tf_op jit(solution)/shard_map/ppermute | solution.py:333
  87.7 14.9 %copy-start.18 = (f32[512,512]{1,0:T(8,128)S(1)}, f32[512,512]{1,0:T(8,128)}, u32[]{:S(2)}) copy-start(f32[512,512]{1,0:T(8,128)} %copy-done.17) | copy-start | bytes 3145732
  87.7 14.9 %copy-start.20 = (bf16[640,768]{1,0:T(8,128)(2,1)S(1)}, bf16[640,768]{1,0:T(8,128)(2,1)}, u32[]{:S(2)}) copy-start(bf16[640,768]{1,0:T(8,128)(2,1)} %copy-done.19) | copy-start | bytes 2949124
  87.7 14.9 %copy-start.22 = (bf16[1,16,32,640]{3,2,1,0:T(8,128)(2,1)S(1)}, bf16[1,16,32,640]{3,2,1,0:T(8,128)(2,1)}, u32[]{:S(2)}) copy-start(bf16[1,16,32,640]{3,2,1,0:T(8,128)(2,1)} %param.8) | copy-start | bytes 1966084
  87.8 8.2 %collective-permute-start.24 = (bf16[40,2944]{1,0:T(8,128)(2,1)S(1)}, bf16[40,2944]{1,0:T(8,128)(2,1)S(1)}, u32[]{:S(2)}, u32[]{:S(2)}) collective-permute-start(bf16[40,2944]{1,0:T(8,128)(2,1)S(1)} %add_convert_fusion.1), channel_id=1, source_target_pairs={{0,4},{4,8},{8,12},{12,14},{14,10},{10,6},{6,2},{2,0},{1,5},{5,9},... | collective-permute-start | bytes 706568 | tf_op jit(solution)/shard_map/ppermute | solution.py:358
  89.4 6.4 %collective-permute-start.27 = (f32[3,640]{1,0:T(4,128)S(1)}, f32[3,640]{1,0:T(4,128)S(1)}, u32[]{:S(2)}, u32[]{:S(2)}) collective-permute-start(f32[3,640]{1,0:T(4,128)S(1)} %fusion.8), channel_id=1, source_target_pairs={{0,2},{2,0},{4,6},{6,4},{8,10},{10,8},{12,14},{14,12},{1,3},{3,1},... | collective-permute-start | bytes 23048 | tf_op jit(solution)/shard_map/ppermute | solution.py:383
  89.9 5.9 %collective-permute-start.28 = (f32[3,640]{1,0:T(4,128)S(1)}, f32[3,640]{1,0:T(4,128)S(1)}, u32[]{:S(2)}, u32[]{:S(2)}) collective-permute-start(f32[3,640]{1,0:T(4,128)S(1)} %fusion.8), channel_id=1, source_target_pairs={{0,4},{2,6},{4,0},{6,2},{8,12},{10,14},{12,8},{14,10},{1,5},{3,7},... | collective-permute-start | bytes 23048 | tf_op jit(solution)/shard_map/ppermute | solution.py:383
  91.2 4.8 %collective-permute-start.29 = (f32[3,640]{1,0:T(4,128)S(1)}, f32[3,640]{1,0:T(4,128)S(1)}, u32[]{:S(2)}, u32[]{:S(2)}) collective-permute-start(f32[3,640]{1,0:T(4,128)S(1)} %fusion.8), channel_id=1, source_target_pairs={{0,6},{2,4},{4,2},{6,0},{8,14},{10,12},{12,10},{14,8},{1,7},{3,5},... | collective-permute-start | bytes 23048 | tf_op jit(solution)/shard_map/ppermute | solution.py:383
  96.0 11.4 %collective-permute-start.32 = (f32[3,640]{1,0:T(4,128)S(1)}, f32[3,640]{1,0:T(4,128)S(1)}, u32[]{:S(2)}, u32[]{:S(2)}) collective-permute-start(f32[3,640]{1,0:T(4,128)S(1)} %add_add_fusion), channel_id=1, source_target_pairs={{0,8},{4,12},{8,0},{12,4},{16,24},{20,28},{24,16},{28,20},{1,9},{5... | collective-permute-start | bytes 23048 | tf_op jit(solution)/shard_map/ppermute | solution.py:383
  98.5 8.9 %collective-permute-start.33 = (f32[3,640]{1,0:T(4,128)S(1)}, f32[3,640]{1,0:T(4,128)S(1)}, u32[]{:S(2)}, u32[]{:S(2)}) collective-permute-start(f32[3,640]{1,0:T(4,128)S(1)} %add_add_fusion), channel_id=1, source_target_pairs={{0,16},{4,20},{8,24},{12,28},{16,0},{20,4},{24,8},{28,12},{1,17},{... | collective-permute-start | bytes 23048 | tf_op jit(solution)/shard_map/ppermute | solution.py:383
  99.4 8.1 %collective-permute-start.34 = (f32[3,640]{1,0:T(4,128)S(1)}, f32[3,640]{1,0:T(4,128)S(1)}, u32[]{:S(2)}, u32[]{:S(2)}) collective-permute-start(f32[3,640]{1,0:T(4,128)S(1)} %add_add_fusion), channel_id=1, source_target_pairs={{0,24},{4,28},{8,16},{12,20},{16,8},{20,12},{24,0},{28,4},{1,25},{... | collective-permute-start | bytes 23048 | tf_op jit(solution)/shard_map/ppermute | solution.py:383
  100.6 7.5 %collective-permute-start.30 = (bf16[40,2944]{1,0:T(8,128)(2,1)S(1)}, bf16[40,2944]{1,0:T(8,128)(2,1)S(1)}, u32[]{:S(2)}, u32[]{:S(2)}) collective-permute-start(bf16[40,2944]{1,0:T(8,128)(2,1)S(1)} %add_convert_fusion), channel_id=1, source_target_pairs={{1,0},{16,17},{0,16},{17,1},{3,2},{18,19},{2,18},{19,3},{5,4},{20,... | collective-permute-start | bytes 706568 | tf_op jit(solution)/shard_map/ppermute | solution.py:561
  101.9 6.1 %collective-permute-start.31 = (bf16[40,2944]{1,0:T(8,128)(2,1)S(1)}, bf16[40,2944]{1,0:T(8,128)(2,1)S(1)}, u32[]{:S(2)}, u32[]{:S(2)}) collective-permute-start(bf16[40,2944]{1,0:T(8,128)(2,1)S(1)} %add_convert_fusion), channel_id=1, source_target_pairs={{1,16},{16,1},{3,18},{18,3},{5,20},{20,5},{7,22},{22,7},{9,24},{24... | collective-permute-start | bytes 706568 | tf_op jit(solution)/shard_map/ppermute | solution.py:562
  (22 other events, 71.3 us)

commit v8 on v7

--- a/solution.py
+++ b/solution.py
@@ -270,23 +270,12 @@
     block[...] = (conv.reshape(half, width, chans) + latent[...].astype(F32)).astype(BF16)
 
 
-def back_kernel(cols, stages, stage, dev, cots, *refs):
-    last = stage == len(stages.counts) - 1
-    before = (1 if stage else 0) + (2 if last else 0)
-    blocks = refs[before:-2] if last else refs[before:-1]
-    total = refs[-1]
+def back_kernel(cols, stages, stage, dev, cots, slope, slope_x, *refs):
+    blocks, (sums, total) = refs[:-2], refs[-2:]
     core = dev[0] % 2
     rows, width = cots.shape[1] - 2, cots.shape[2]
     cells, chans = total.shape
     lanes = stages.lanes(stage)
-
-    total[...] = refs[0][...] if stage else jnp.zeros_like(total)
-    place, channel = cols.middle(core, chans)
-    window = cots[1, 1:rows + 1, :, lanes].reshape(cells, stages.widths[stage])
-    kernel = stages.columns(stage, blocks, place, cols.mid)
-    value = jnp.dot(window, kernel, preferred_element_type=F32)
-    lane = lax.broadcasted_iota(jnp.int32, value.shape, 1)
-    total[:, pl.ds(channel, cols.mid)] += jnp.where((core == 1) & (lane < cols.both), 0.0, value)
 
     def taps_from(first, place, count):
         windows, kernels = [], []
@@ -295,35 +284,58 @@
             window = cots[2 - tap % 3, pl.ds(2 - tap // 3, rows), :, lanes]
             windows.append(window.reshape(cells, stages.widths[stage]))
             kernels.append(stages.columns(stage, blocks, pl.multiple_of(place + i * chans, LANES), chans))
-        total[...] += jnp.dot(
+        return jnp.dot(
             jnp.concatenate(windows, axis=1), jnp.concatenate(kernels), preferred_element_type=F32
         )
 
-    def two_taps(k, _):
-        taps, place = cols.pair(core, k, chans)
-        taps_from(taps[0], place, 2)
-        return 0
-
-    if stage:
+    if stages.widths[stage] * 4 <= 2 * chans:
         taps, place = cols.pair(core, 0, chans)
-        taps_from(taps[0], place, 4)
+        total[...] = taps_from(taps[0], place, 4)
     else:
+        total[...] = jnp.zeros_like(total)
+
+        def two_taps(k, _):
+            taps, place = cols.pair(core, k, chans)
+            total[...] += taps_from(taps[0], place, 2)
+            return 0
+
         lax.fori_loop(0, 2, two_taps, 0)
 
-    if last:
-        slope, slope_x = refs[before - 2:before]
-        sums = refs[-2]
-
-        def add_row(i, carry):
-            gains, shifts = carry
-            value = total[pl.ds(pl.multiple_of(i * width, width), width)]
-            return gains + value * slope_x[i].astype(F32), shifts + value * slope[i].astype(F32)
-
-        zero = jnp.zeros((width, chans), F32)
-        gains, shifts = lax.fori_loop(0, rows, add_row, (zero, zero))
-        scale = cols.total ** (-0.5)
-        sums[0:1] = scale * jnp.sum(gains, axis=0, keepdims=True)
-        sums[1:2] = scale * jnp.sum(shifts, axis=0, keepdims=True)
+    place, channel = cols.middle(core, chans)
+    window = cots[1, 1:rows + 1, :, lanes].reshape(cells, stages.widths[stage])
+    kernel = stages.columns(stage, blocks, place, cols.mid)
+    value = jnp.dot(window, kernel, preferred_element_type=F32)
+    lane = lax.broadcasted_iota(jnp.int32, value.shape, 1)
+    total[:, pl.ds(channel, cols.mid)] += jnp.where((core == 1) & (lane < cols.both), 0.0, value)
+
+    def add_row(i, carry):
+        gains, shifts = carry
+        value = total[pl.ds(pl.multiple_of(i * width, width), width)]
+        return gains + value * slope_x[i].astype(F32), shifts + value * slope[i].astype(F32)
+
+    zero = jnp.zeros((width, chans), F32)
+    gains, shifts = lax.fori_loop(0, rows, add_row, (zero, zero))
+    scale = cols.total ** (-0.5)
+    sums[0:1] = scale * jnp.sum(gains, axis=0, keepdims=True)
+    sums[1:2] = scale * jnp.sum(shifts, axis=0, keepdims=True)
+
+
+def finish_kernel(cols, dev, step, shard, mine, theirs, total, across, aside, out):
+    me = dev[0]
+    core = me % 2
+    same = me // (dev[1] // 2) == core
+    lower = core == 0
+    rate = LR_KERNEL * (1.0 - (step[0] % 1000).astype(F32) / 2000.0)
+    factor = 0.5 * cols.total ** (-0.5) * rate
+    total, across, aside = (ref[...].astype(F32) for ref in (total, across, aside))
+    left = jnp.where(same, jnp.where(lower, total, across), jnp.where(lower, across, aside))
+    right = jnp.where(same, jnp.where(lower, across, total), jnp.where(lower, aside, across))
+    mine, theirs = mine[...].astype(F32), theirs[...].astype(F32)
+    peer_left, peer_right = jnp.where(lower, mine, theirs), jnp.where(lower, theirs, mine)
+    out[:, :cols.lead] = 0.5 * (shard[:, :cols.lead] + peer_left) - factor * left
+    out[:, cols.lead:] = (
+        0.5 * (shard[:, cols.lead:] + peer_right[:, cols.both:]) - factor * right[:, cols.both:]
+    )
 
 
 NODE = ("z", "y")
@@ -377,12 +389,9 @@
         return rows.reshape(-1, 3 * self.count)
 
 
-def sum_over(value, axes, masks):
-    count = lax.axis_size(axes)
-    for mask in (masks[0], masks[1], masks[0] | masks[1]):
-        value_in = lax.ppermute(value, axes, [(s, s ^ mask) for s in range(count)])
-        total = value_in if mask == masks[0] else total + value_in
-    return value + total
+def hop(value, axis, mask):
+    count = lax.axis_size(axis)
+    return value + lax.ppermute(value, axis, [(s, s ^ mask) for s in range(count)])
 
 
 def add(*values):
@@ -408,10 +417,10 @@
     paired = replicas == 2
     ring = Ring(zs)
     scale = cols.total ** (-0.5)
-    level = step[0] % (replicas.bit_length() - 1)
     params = jnp.concatenate([conv_bias, gn_gain, gn_shift])
-    rate = LR_KERNEL * (1.0 - (step[0] % 1000).astype(F32) / 2000.0)
-    dev = (((replica * zs + z) * 2 + y) * 2 + core).reshape(1)
+    me = ((replica * zs + z) * 2 + y) * 2 + core
+    core, lower, me = tied(core, lower, me)
+    dev = jnp.stack([me, jnp.int32(4 * zs * replicas)])
 
     mine = lax.dynamic_slice_in_dim(shard, core * cols.start, cols.lead, 1).astype(BF16)
     theirs = lax.dynamic_slice_in_dim(shard, (1 - core) * cols.start, cols.lead, 1).astype(BF16)
@@ -425,7 +434,7 @@
         table = jnp.asarray(ring.table(part))
         order = (ring.count, part, 2 * ring.count)
         up1, down1 = ring.up(unit), ring.down(unit)
-        peer = from_peer(level, mine), from_peer(level, theirs)
+        peer = swap(mine, "replica"), swap(theirs, "replica")
     else:
         table = jnp.zeros((replicas * zs * 4, 1), jnp.int32)
         order = None
@@ -472,20 +481,12 @@
             8, flops // 4,
         )(dev, table, stats, gn_gain, gn_shift, latent, lat_far, cot_b, cot_far)
 
-    total_of = jax.ShapeDtypeStruct((2 * cells, chans), F32)
-
-    def back_first(cots, blocks):
+    def back(stage, cots, slopes, blocks):
         return call(
-            partial(back_kernel, cols, stages, 0), total_of,
-            [SMEM_SPEC] + [VMEM_SPEC] * (1 + len(blocks)), [], 4, flops // 4,
-        )(dev, cots, *blocks)
-
-    def back_last(cots, earlier, slopes, blocks):
-        return call(
-            partial(back_kernel, cols, stages, len(stages.counts) - 1), jax.ShapeDtypeStruct((2, chans), F32),
-            [SMEM_SPEC] + [VMEM_SPEC] * (3 + len(earlier) + len(blocks)),
-            [pltpu.VMEM(total_of.shape, F32)], 8, flops // 4,
-        )(dev, cots, *earlier, *slopes, *blocks)
+            partial(back_kernel, cols, stages, stage), jax.ShapeDtypeStruct((2, chans), F32),
+            [SMEM_SPEC] + [VMEM_SPEC] * (3 + len(blocks)),
+            [pltpu.VMEM((2 * cells, chans), F32)], 8, flops // 4,
+        )(dev, cots, *slopes, *blocks)
 
     def conv_first(blocks):
         wide = stages.widths[0]
@@ -496,7 +497,7 @@
             [pltpu.VMEM((2 * cells, wide), F32)], 6, flops // 4,
         )(dev, acts, *blocks)
 
-    def conv_far(blocks):
+    def conv_far(acts, blocks):
         wide = stages.widths[-1]
         return call(
             partial(conv_far_kernel, cols, stages, len(stages.counts) - 1),
@@ -526,71 +527,64 @@
         for j in range(zs):
             if j < zs - 2:
                 up, down = ring.up(up), ring.down(down)
-                if j == zs - 3:
-                    total_first = back_first(cots, blocks)
+                if j < zs - 3:
+                    up, down, cots, *slopes, order = tied(up, down, *slopes_of(stats))
+                    blocks += [up, down]
+                    crossed[j] = tied(crossed[j], up)[0]
+                else:
+                    cots, crossed[j - 1] = tied(cots, crossed[j - 1])
+                    first_sums = back(0, cots, slopes, blocks)
                     conv_first_own, conv_send = conv_first(blocks)
-                    up, down, crossed[j], total_first, conv_send = tied(
-                        up, down, crossed[j], total_first, conv_send
+                    up, down, crossed[j], first_sums, conv_send = tied(
+                        up, down, crossed[j], first_sums, conv_send
                     )
                     conv_first_got = swap(conv_send, "core")
                     late = [up, down]
-                else:
-                    blocks += [up, down]
-                    up, down, crossed[j], cots, slope, slope_x, order = tied(
-                        up, down, crossed[j], *slopes_of(stats)
-                    )
-                    blocks[-2:] = [up, down]
             elif j == zs - 2:
                 halves = ring.up(up[:part]), ring.down(down[part:])
                 *halves, crossed[j], conv_first_got = tied(*halves, crossed[j], conv_first_got)
                 late += halves
-                sums = back_last(cots, [total_first], [slope, slope_x], late)
-                conv_got = swap(conv_far(late), "core")
+                sums = back(1, cots, slopes, late)
             else:
-                crossed[j], sums, *received = tied(crossed[j], sums, *up_sum, *down_sum)
+                crossed[j], sums, acts, *received = tied(crossed[j], sums, acts, *up_sum, *down_sum)
                 up_sum, down_sum = tuple(received[:1]), tuple(received[1:])
+                conv_got = swap(conv_far(acts, late), "core")
             ahead = add(kept[j][:part], crossed[j][:part], *up_sum)
             behind = (kept[j][part:], crossed[j][part:], *down_sum)
             up_sum = (ring.up(ahead),)
             if j < zs - 1:
                 down_sum = (ring.down(add(*behind)),)
-        vectors = sum_over(chip_sum(sums), ("z", "y"), (1, 2))
+        vectors = hop(hop(chip_sum(first_sums + sums), "y", 1), "z", 1)
         last, conv_got, vectors = tied(*up_sum, conv_got, vectors)
         total = add(*behind, last)
         earlier = [conv_first_own, conv_first_got, order]
-        a = lax.ppermute(total, ("replica", "core"), [(1, 0), (2, 3), (0, 2), (3, 1)])
-        b = lax.ppermute(total, ("replica", "core"), [(1, 2), (2, 1)])
-        left = jnp.where(replica == core, jnp.where(lower, total, a), jnp.where(lower, a, b))
-        right = jnp.where(replica == core, jnp.where(lower, a, total), jnp.where(lower, b, a))
+        across = lax.ppermute(total, ("replica", "core"), [(1, 0), (2, 3), (0, 2), (3, 1)])
+        aside = lax.ppermute(total, ("replica", "core"), [(1, 2), (2, 1)])
+        new_kernel = call(
+            partial(finish_kernel, cols), jax.ShapeDtypeStruct(shard.shape, F32),
+            [SMEM_SPEC] * 2 + [VMEM_SPEC] * 6, [], 8, flops // 16,
+        )(dev, step, shard, *peer, total, across, aside)
+        vectors = hop(vectors, "z", 2)
+        new_v = 0.5 * hop(vectors, "replica", 1)
     else:
         late, earlier = [lax.all_gather(unit, NODE, axis=0, tiled=True)], []
         cots, slope, slope_x = slopes_of(stats)
-        sums = back_last(cots, [], [slope, slope_x], late)
-        conv_got, vectors = swap(conv_far(late), "core"), chip_sum(sums)
+        sums = back(0, cots, [slope, slope_x], late)
+        conv_got, vectors = swap(conv_far(acts, late), "core"), chip_sum(sums)
         terms = jnp.concatenate(pieces).reshape(2 * zs, 2, part, cols.lead)
         summed = lax.psum_scatter(terms, NODE, scatter_dimension=0, tiled=False)
         ours = lax.dynamic_index_in_dim(summed, core, 0, keepdims=False)
         got = swap(lax.dynamic_index_in_dim(summed, 1 - core, 0, keepdims=False), "core")
         left, right = jnp.where(lower, ours, got), jnp.where(lower, got, ours)
-
-    def all_columns(left, right):
-        return jnp.concatenate([left, right[:, cols.both:]], axis=1).astype(F32)
-
-    kernel_grad = all_columns(left, right)
-    if paired:
-        peer = all_columns(jnp.where(lower, *peer), jnp.where(lower, *peer[::-1]))
-        new_kernel = 0.5 * (shard + peer) - (0.5 * scale * rate) * kernel_grad
-    else:
+        kernel_grad = jnp.concatenate([left, right[:, cols.both:]], axis=1).astype(F32)
+        level = step[0] % (replicas.bit_length() - 1)
+        rate = LR_KERNEL * (1.0 - (step[0] % 1000).astype(F32) / 2000.0)
         stepped = shard - (scale * rate) * kernel_grad
         new_kernel = 0.5 * (stepped + from_peer(level, stepped.astype(BF16)).astype(F32))
-
-    block = conv_own(conv_got, earlier, late)
-    if paired:
-        new_v = 0.5 * sum_over(vectors, ("replica", "z"), (2, zs))
-    else:
         stepped_v = lax.psum(vectors, NODE)
         new_v = 0.5 * (stepped_v + from_peer(level, stepped_v))
 
+    block = conv_own(conv_got, earlier, late)
     return (
         block[None],
         new_kernel[None],

time: 111 us -> 103 us (0.928)
  local copies, waits for them, and re-layouts: 15.6 us -> 1.95 us
  waiting for transfers between devices: 14.2 us -> 24.3 us
  other arithmetic: 8.4 us -> 2.92 us
  starting transfers between devices: 34.3 us -> 35.5 us
    unnamed x70 -> x12, local copies, waits for them, and re-layouts: 12.2 us -> 0.03 us
    ppermute x7, starting transfers between devices: 2.74 us -> 11.1 us  [down(): return lax.ppermute(value, NODE, self.behind)]
    ppermute x8, starting transfers between devices: 13.9 us -> 5.55 us  [up(): return lax.ppermute(value, NODE, self.ahead)]
    ppermute x9 -> x5, waiting for transfers between devices: 2.01 us -> 8.79 us  [the longest x4 8.78 us: hop(): lax.ppermute(value, axis, [(s, s ^ mask) for s in range(count)])]
    ppermute x9 -> x5, starting transfers between devices: 10.7 us -> 4.87 us  [the longest x4 4.19 us: hop(): lax.ppermute(value, axis, [(s, s ^ mask) for s in range(count)])]
    ppermute x8, waiting for transfers between devices: 2.27 us -> 7.09 us  [up(): return lax.ppermute(value, NODE, self.ahead)]
    ppermute x10 -> x12, starting transfers between devices: 5.64 us -> 9.45 us  [swap(): return lax.ppermute(value, axis, [(0, 1), (1, 0)])]
    ppermute x1, starting transfers between devices: 1.33 us -> 4.46 us  [per_device(): lax.ppermute(total, ('replica', 'core'), [(1, 0), (2, 3), (0, 2), (3, 1)])]
  transfers between devices with their start and end apart: 35 -> 33, of which waited for: 8 -> 11; matrix products, arithmetic and copies ran while one was open for 8% -> 3% of each run, Pallas kernels for 32% -> 34%
where the time goes in v8:
time: 103 us
  Pallas kernels  36.4 us (35%)
  starting transfers between devices  35.5 us (34%)
  waiting for transfers between devices  24.3 us (24%)
  other arithmetic  2.92 us (3%)
  local copies, waits for them, and re-layouts  1.95 us (2%)
  between operations  1.54 us (1%)
    ppermute x7, starting transfers between devices, down(): return lax.ppermute(value, NODE, self.behind)  11.1 us
    pallas_call x2, Pallas kernels, back(): call(partial(back_kernel, cols, stages, stage), jax.ShapeDtypeStruct((2,...  9.7 us
    ppermute x12, starting transfers between devices, swap(): return lax.ppermute(value, axis, [(0, 1), (1, 0)])  9.45 us
    ppermute x4, waiting for transfers between devices, hop(): lax.ppermute(value, axis, [(s, s ^ mask) for s in range(count)])  8.78 us
    ppermute x8, waiting for transfers between devices, up(): return lax.ppermute(value, NODE, self.ahead)  7.09 us
    ppermute x8, starting transfers between devices, up(): return lax.ppermute(value, NODE, self.ahead)  5.55 us
    ppermute x12, waiting for transfers between devices, swap(): return lax.ppermute(value, axis, [(0, 1), (1, 0)])  5.43 us
    pallas_call x1, Pallas kernels, per_device(): call(partial(grad_kernel, cols), [jax.ShapeDtypeStruct((2 * part, cols.le...  5.18 us
  transfers between devices with their start and end apart: 33, of which 11 were waited for; matrix products, arithmetic and copies ran while one was open for 3% of the time, Pallas kernels for 34%

profile of v8, /device:TPU:0, one launch (start us, length us, event | category | flops | bytes accessed | tf_op | source)
XLA Modules:
  0.0 102.5 jit_solution(16774026707652790806)
XLA Ops:
  0.7 1.3 %fusion = (bf16[40,2944]{1,0:T(8,128)(2,1)S(1)}, bf16[40,2944]{1,0:T(8,128)(2,1)S(1)}) fusion(f32[1,40,5760]{2,1,0:T(8,128)} %param.10, s32[]{:T(128)S(6)} %select_n.15, s32[]{:T(128)S(6)} %select_n.16), kind=kLoop, calls=%fused_computation.12 | loop fusion | bytes 942088 | tf_op jit(solution)/shard_map/convert_element_type | solution.py:425
  2.0 0.5 collective-permute-start.3
  2.5 2.0 %fusion.3 = (f32[640]{0:T(1024)S(1)}, bf16[16,32,640]{2,1,0:T(8,128)(2,1)S(1)}) fusion(f32[1,16,32,640]{3,2,1,0:T(8,128)} %param.9), kind=kLoop, calls=%fused_computation.19 | loop fusion | flops 654720 | bytes 1968640 | tf_op jit(solution)/shard_map/reduce_sum | solution.py:517
  4.6 0.5 collective-permute-start
  5.1 2.7 %collective-permute-start.5 = (bf16[80,2944]{1,0:T(8,128)(2,1)S(1)}, bf16[80,2944]{1,0:T(8,128)(2,1)S(1)}, u32[]{:S(2)}, u32[]{:S(2)}) collective-permute-start(bf16[80,2944]{1,0:T(8,128)(2,1)S(1)} %maximum_select_fusion.refs_0_), channel_id=1, source_target_pairs={{4,0},{8,4},{12,8},{14,12},{10,14},{6,10},{2,6},{0,2},{5,1},{9,5},... | collective-permute-start | bytes 1413128 | tf_op jit(solution)/shard_map/ppermute | solution.py:373
  7.9 1.9 %collective-permute-start.6 = (bf16[40,2944]{1,0:T(8,128)(2,1)S(1)}, bf16[40,2944]{1,0:T(8,128)(2,1)S(1)}, u32[]{:S(2)}, u32[]{:S(2)}) collective-permute-start(bf16[40,2944]{1,0:T(8,128)(2,1)S(1)} %get-tuple-element.113), channel_id=1, source_target_pairs={{0,16},{16,0},{1,17},{17,1},{2,18},{18,2},{3,19},{19,3},{4,20},{20... | collective-permute-start | bytes 706568 | tf_op jit(solution)/shard_map/ppermute | solution.py:345
  10.0 4.4 %shard_map.119 = (f32[2,640]{1,0:T(2,128)S(1)}, bf16[3,34,32,640]{3,2,1,0:T(8,128)(2,1)S(1)}, bf16[640,1024]{1,0:T(8,128)(2,1)S(1)}) custom-call(s32[2]{0:T(128)S(1)} %pad_add_fusion.dev, s32[32,24]{1,0:T(8,128)S(1)} %copy-done.5, bf16[16,32,640]{2,1,0:T(8,128)(2,1)S(1)} %bitcast.13, bf16[16,32,640]{2,1,0:T(8,128)(2,1)S(1)} %collective-permute-done.lat_far, ...), custom_call_target="tpu_custom_call" | custom-call | flops 964689920 | tf_op jit(solution)/shard_map/pallas_call | solution.py:456
  14.4 5.2 %shard_map.120 = (bf16[80,2944]{1,0:T(8,128)(2,1)S(1)}, bf16[80,2944]{1,0:T(8,128)(2,1)S(1)}, bf16[80,2944]{1,0:T(8,128)(2,1)S(1)}, bf16[80,2944]{1,0:T(8,128)(2...) custom-call(s32[2]{0:T(128)S(1)} %pad_add_fusion.dev, ...), custom_call_target="tpu_custom_call" | custom-call | flops 1929379840 | tf_op jit(solution)/shard_map/pallas_call | solution.py:463
  19.6 1.1 %collective-permute-done.7.theirs = bf16[40,2944]{1,0:T(8,128)(2,1)S(1)} collective-permute-done((bf16[40,2944]{1,0:T(8,128)(2,1)S(1)}, bf16[40,2944]{1,0:T(8,128)(2,1)S(1)}, u32[]{:S(2)}, u32[]{:S(2)}) %collective-permute-start.7) | collective-permute-done | bytes 235552 | tf_op jit(solution)/shard_map/ppermute | solution.py:345
  20.8 1.7 %collective-permute-start.8 = (bf16[80,2944]{1,0:T(8,128)(2,1)S(1)}, bf16[80,2944]{1,0:T(8,128)(2,1)S(1)}, u32[]{:S(2)}, u32[]{:S(2)}) collective-permute-start(bf16[80,2944]{1,0:T(8,128)(2,1)S(1)} %collective-permute-done.4.refs_1_), channel_id=1, source_target_pairs={{0,4},{4,8},{8,12},{12,14},{14,10},{10,6},{6,2},{2,0},{1,5},{5,9},... | collective-permute-start | bytes 1413128 | tf_op jit(solution)/shard_map/ppermute | solution.py:370
  22.4 0.3 collective-permute-start.9
  22.8 1.6 %collective-permute-start.10 = (bf16[80,2944]{1,0:T(8,128)(2,1)S(1)}, bf16[80,2944]{1,0:T(8,128)(2,1)S(1)}, u32[]{:S(2)}, u32[]{:S(2)}) collective-permute-start(bf16[80,2944]{1,0:T(8,128)(2,1)S(1)} %get-tuple-element.70), channel_id=1, source_target_pairs={{0,16},{16,0},{1,17},{17,1},{2,18},{18,2},{3,19},{19,3},{4,20},{20... | collective-permute-start | bytes 1413128 | tf_op jit(solution)/shard_map/ppermute | solution.py:345
  24.4 0.4 collective-permute-start.13
  24.8 4.5 %shard_map.121 = (bf16[3,34,32,768]{3,2,1,0:T(8,128)(2,1)S(1)}, bf16[32,32,640]{2,1,0:T(8,128)(2,1)S(1)}, bf16[32,32,640]{2,1,0:T(8,128)(2,1)S(1)}, bf16[640,768]{1,0:T(8,128)(2,1)S(1)}) custom-call(s32[2]{0:T(128)S(1)} %pad_add_fusion.dev, s32[32,24]{1,0:T(8,128)S(1)} %copy-done.5, f32[2,640]{1,0:T(2,128)S(1)} %get-tuple-element.64.stats, ...), custom_call_target="tpu_custom_call" | custom-call | flops 964689920 | tf_op jit(solution)/shard_map/pallas_call | solution.py:475
  29.3 3.5 %collective-permute-done.8.refs_3_ = bf16[80,2944]{1,0:T(8,128)(2,1)S(1)} collective-permute-done((bf16[80,2944]{1,0:T(8,128)(2,1)S(1)}, bf16[80,2944]{1,0:T(8,128)(2,1)S(1)}, u32[]{:S(2)}, u32[]{:S(2)}) %collective-permute-start.8) | collective-permute-done | bytes 471072 | tf_op jit(solution)/shard_map/ppermute | solution.py:370
  32.8 1.1 %collective-permute-done.9.refs_4_ = bf16[80,2944]{1,0:T(8,128)(2,1)S(1)} collective-permute-done((bf16[80,2944]{1,0:T(8,128)(2,1)S(1)}, bf16[80,2944]{1,0:T(8,128)(2,1)S(1)}, u32[]{:S(2)}, u32[]{:S(2)}) %collective-permute-start.9) | collective-permute-done | bytes 471072 | tf_op jit(solution)/shard_map/ppermute | solution.py:373
  33.9 1.6 %collective-permute-start.11 = (bf16[80,2944]{1,0:T(8,128)(2,1)S(1)}, bf16[80,2944]{1,0:T(8,128)(2,1)S(1)}, u32[]{:S(2)}, u32[]{:S(2)}) collective-permute-start(bf16[80,2944]{1,0:T(8,128)(2,1)S(1)} %collective-permute-done.8.refs_3_), channel_id=1, source_target_pairs={{0,4},{4,8},{8,12},{12,14},{14,10},{10,6},{6,2},{2,0},{1,5},{5,9},... | collective-permute-start | bytes 1413128 | tf_op jit(solution)/shard_map/ppermute | solution.py:370
  35.4 1.1 %collective-permute-done.10 = bf16[80,2944]{1,0:T(8,128)(2,1)S(1)} collective-permute-done((bf16[80,2944]{1,0:T(8,128)(2,1)S(1)}, bf16[80,2944]{1,0:T(8,128)(2,1)S(1)}, u32[]{:S(2)}, u32[]{:S(2)}) %collective-permute-start.10) | collective-permute-done | bytes 471072 | tf_op jit(solution)/shard_map/ppermute | solution.py:345
  36.5 1.6 %collective-permute-start.12 = (bf16[80,2944]{1,0:T(8,128)(2,1)S(1)}, bf16[80,2944]{1,0:T(8,128)(2,1)S(1)}, u32[]{:S(2)}, u32[]{:S(2)}) collective-permute-start(bf16[80,2944]{1,0:T(8,128)(2,1)S(1)} %collective-permute-done.9.refs_4_), channel_id=1, source_target_pairs={{4,0},{8,4},{12,8},{14,12},{10,14},{6,10},{2,6},{0,2},{5,1},{9,5},... | collective-permute-start | bytes 1413128 | tf_op jit(solution)/shard_map/ppermute | solution.py:373
  38.3 1.6 %collective-permute-start.21 = (bf16[40,2944]{1,0:T(8,128)(2,1)S(1)}, bf16[40,2944]{1,0:T(8,128)(2,1)S(1)}, u32[]{:S(2)}, u32[]{:S(2)}) collective-permute-start(bf16[40,2944]{1,0:T(8,128)(2,1)S(1)} %get-tuple-element.111), channel_id=1, source_target_pairs={{4,0},{8,4},{12,8},{14,12},{10,14},{6,10},{2,6},{0,2},{5,1},{9,5},... | collective-permute-start | bytes 706568 | tf_op jit(solution)/shard_map/ppermute | solution.py:373
  39.9 0.4 collective-permute-start.18
  40.3 4.5 %shard_map.123 = (f32[512,512]{1,0:T(8,128)S(1)}, bf16[512,512]{1,0:T(8,128)(2,1)S(1)}) custom-call(s32[2]{0:T(128)S(1)} %pad_add_fusion.dev, bf16[3,34,32,640]{3,2,1,0:T(8,128)(2,1)S(1)} %get-tuple-element.90.acts, bf16[80,2944]{1,0:T(8,128)(2,1)S(1)} %maximum_select_fusion.refs_0_, bf16[80,2944]{1,0:T(8,128)(2,1)S(1)} %collective-permute-done.4.refs_1_, ...), custom_call_target="tpu_custom_call" | custom-call | flops 964689920 | tf_op jit(solution)/shard_map/pallas_call | solution.py:493
  44.9 5.9 %shard_map.122 = f32[2,640]{1,0:T(2,128)S(1)} custom-call(s32[2]{0:T(128)S(1)} %pad_add_fusion.dev, bf16[3,34,32,768]{3,2,1,0:T(8,128)(2,1)S(1)} %get-tuple-element.73.cots, bf16[32,32,640]{2,1,0:T(8,128)(2,1)S(1)} %get-tuple-element.74.slope, bf16[32,32,640]{2,1,0:T(8,128)(2,1)S(1)} %get-tuple-element.75.slope_x, ...), custom_call_target="tpu_custom_call" | custom-call | flops 964689920 | tf_op jit(solution)/shard_map/pallas_call | solution.py:485
  50.8 1.6 %collective-permute-start.16 = (bf16[80,2944]{1,0:T(8,128)(2,1)S(1)}, bf16[80,2944]{1,0:T(8,128)(2,1)S(1)}, u32[]{:S(2)}, u32[]{:S(2)}) collective-permute-start(bf16[80,2944]{1,0:T(8,128)(2,1)S(1)} %get-tuple-element.81), channel_id=1, source_target_pairs={{0,16},{16,0},{1,17},{17,1},{2,18},{18,2},{3,19},{19,3},{4,20},{20... | collective-permute-start | bytes 1413128 | tf_op jit(solution)/shard_map/ppermute | solution.py:345
  52.4 1.6 %collective-permute-start.15 = (bf16[40,2944]{1,0:T(8,128)(2,1)S(1)}, bf16[40,2944]{1,0:T(8,128)(2,1)S(1)}, u32[]{:S(2)}, u32[]{:S(2)}) collective-permute-start(bf16[40,2944]{1,0:T(8,128)(2,1)S(1)} %slice.64), channel_id=1, source_target_pairs={{4,0},{8,4},{12,8},{14,12},{10,14},{6,10},{2,6},{0,2},{5,1},{9,5},... | collective-permute-start | bytes 706568 | tf_op jit(solution)/shard_map/ppermute | solution.py:373
  54.1 0.4 collective-permute-start.14
  54.7 1.6 %collective-permute-start.22 = (bf16[40,2944]{1,0:T(8,128)(2,1)S(1)}, bf16[40,2944]{1,0:T(8,128)(2,1)S(1)}, u32[]{:S(2)}, u32[]{:S(2)}) collective-permute-start(bf16[40,2944]{1,0:T(8,128)(2,1)S(1)} %get-tuple-element.109), channel_id=1, source_target_pairs={{4,0},{8,4},{12,8},{14,12},{10,14},{6,10},{2,6},{0,2},{5,1},{9,5},... | collective-permute-start | bytes 706568 | tf_op jit(solution)/shard_map/ppermute | solution.py:373
  56.4 3.2 %collective-permute-done.16 = bf16[80,2944]{1,0:T(8,128)(2,1)S(1)} collective-permute-done((bf16[80,2944]{1,0:T(8,128)(2,1)S(1)}, bf16[80,2944]{1,0:T(8,128)(2,1)S(1)}, u32[]{:S(2)}, u32[]{:S(2)}) %collective-permute-start.16) | collective-permute-done | bytes 471072 | tf_op jit(solution)/shard_map/ppermute | solution.py:345
  59.6 0.3 collective-permute-start.19
  59.9 2.1 %collective-permute-start.2 = (bf16[80,2944]{1,0:T(8,128)(2,1)S(1)}, bf16[80,2944]{1,0:T(8,128)(2,1)S(1)}, u32[]{:S(2)}, u32[]{:S(2)}) collective-permute-start(bf16[80,2944]{1,0:T(8,128)(2,1)S(1)} %get-tuple-element.58), channel_id=1, source_target_pairs={{0,16},{16,0},{1,17},{17,1},{2,18},{18,2},{3,19},{19,3},{4,20},{20... | collective-permute-start | bytes 1413128 | tf_op jit(solution)/shard_map/ppermute | solution.py:345
  62.0 1.6 %collective-permute-done.22 = bf16[40,2944]{1,0:T(8,128)(2,1)S(1)} collective-permute-done((bf16[40,2944]{1,0:T(8,128)(2,1)S(1)}, bf16[40,2944]{1,0:T(8,128)(2,1)S(1)}, u32[]{:S(2)}, u32[]{:S(2)}) %collective-permute-start.22) | collective-permute-done | bytes 235552 | tf_op jit(solution)/shard_map/ppermute | solution.py:373
  63.6 2.0 %collective-permute-done.19 = bf16[40,2944]{1,0:T(8,128)(2,1)S(1)} collective-permute-done((bf16[40,2944]{1,0:T(8,128)(2,1)S(1)}, bf16[40,2944]{1,0:T(8,128)(2,1)S(1)}, u32[]{:S(2)}, u32[]{:S(2)}) %collective-permute-start.19) | collective-permute-done | bytes 235552 | tf_op jit(solution)/shard_map/ppermute | solution.py:370
  65.9 1.6 %collective-permute-start.23 = (bf16[40,2944]{1,0:T(8,128)(2,1)S(1)}, bf16[40,2944]{1,0:T(8,128)(2,1)S(1)}, u32[]{:S(2)}, u32[]{:S(2)}) collective-permute-start(bf16[40,2944]{1,0:T(8,128)(2,1)S(1)} %get-tuple-element.107), channel_id=1, source_target_pairs={{4,0},{8,4},{12,8},{14,12},{10,14},{6,10},{2,6},{0,2},{5,1},{9,5},... | collective-permute-start | bytes 706568 | tf_op jit(solution)/shard_map/ppermute | solution.py:373
  67.5 0.4 collective-permute-start.20
  68.0 3.8 %shard_map.124 = f32[2,640]{1,0:T(2,128)S(1)} custom-call(s32[2]{0:T(128)S(1)} %pad_add_fusion.dev, bf16[3,34,32,768]{3,2,1,0:T(8,128)(2,1)S(1)} %get-tuple-element.73.cots, bf16[32,32,640]{2,1,0:T(8,128)(2,1)S(1)} %get-tuple-element.74.slope, bf16[32,32,640]{2,1,0:T(8,128)(2,1)S(1)} %get-tuple-element.75.slope_x, ...), custom_call_target="tpu_custom_call" | custom-call | flops 964689920 | tf_op jit(solution)/shard_map/pallas_call | solution.py:485
  72.0 1.6 %collective-permute-done.20 = bf16[40,2944]{1,0:T(8,128)(2,1)S(1)} collective-permute-done((bf16[40,2944]{1,0:T(8,128)(2,1)S(1)}, bf16[40,2944]{1,0:T(8,128)(2,1)S(1)}, u32[]{:S(2)}, u32[]{:S(2)}) %collective-permute-start.20) | collective-permute-done | bytes 235552 | tf_op jit(solution)/shard_map/ppermute | solution.py:370
  73.7 2.0 %shard_map.125 = bf16[512,256]{1,0:T(8,128)(2,1)S(1)} custom-call(s32[2]{0:T(128)S(1)} %pad_add_fusion.dev, bf16[3,34,32,640]{3,2,1,0:T(8,128)(2,1)S(1)} %get-tuple-element.90.acts, bf16[80,2944]{1,0:T(8,128)(2,1)S(1)} %collective-permute-done.11.refs_0_.refs_3_, bf16[80,2944]{1,0:T(8,128)(2,1)S(1)} %collective-permute-done.12.refs_1_.refs_4_, ...), custom_call_target="tpu_custom_call" | custom-call | flops 482344960 | tf_op jit(solution)/shard_map/pallas_call | solution.py:502
  75.7 0.6 collective-permute-start.25
  76.3 0.5 collective-permute-start.24
  76.9 1.6 %collective-permute-start.27 = (f32[3,640]{1,0:T(4,128)S(1)}, f32[3,640]{1,0:T(4,128)S(1)}, u32[]{:S(2)}, u32[]{:S(2)}) collective-permute-start(f32[3,640]{1,0:T(4,128)S(1)} %fusion.5), channel_id=1, source_target_pairs={{0,2},{2,0},{1,3},{3,1},{4,6},{6,4},{5,7},{7,5},{8,10},{10,8},{9,1... | collective-permute-start | bytes 23048 | tf_op jit(solution)/shard_map/ppermute | solution.py:394
  78.5 5.8 %collective-permute-done.27 = f32[3,640]{1,0:T(4,128)S(1)} collective-permute-done((f32[3,640]{1,0:T(4,128)S(1)}, f32[3,640]{1,0:T(4,128)S(1)}, u32[]{:S(2)}, u32[]{:S(2)}) %collective-permute-start.27) | collective-permute-done | bytes 7712 | tf_op jit(solution)/shard_map/ppermute | solution.py:394
  84.9 3.0 %collective-permute-done.28 = f32[3,640]{1,0:T(4,128)S(1)} collective-permute-done((f32[3,640]{1,0:T(4,128)S(1)}, f32[3,640]{1,0:T(4,128)S(1)}, u32[]{:S(2)}, u32[]{:S(2)}) %collective-permute-start.28) | collective-permute-done | bytes 7712 | tf_op jit(solution)/shard_map/ppermute | solution.py:394
  88.2 0.7 collective-permute-start.30
  88.9 4.5 %collective-permute-start.29 = (bf16[40,2944]{1,0:T(8,128)(2,1)S(1)}, bf16[40,2944]{1,0:T(8,128)(2,1)S(1)}, u32[]{:S(2)}, u32[]{:S(2)}) collective-permute-start(bf16[40,2944]{1,0:T(8,128)(2,1)S(1)} %add_convert_fusion.total), channel_id=1, source_target_pairs={{1,0},{16,17},{0,16},{17,1},{3,2},{18,19},{2,18},{19,3},{5,4},{20,... | collective-permute-start | bytes 706568 | tf_op jit(solution)/shard_map/ppermute | solution.py:561
  93.3 2.5 %collective-permute-start.32 = (f32[3,640]{1,0:T(4,128)S(1)}, f32[3,640]{1,0:T(4,128)S(1)}, u32[]{:S(2)}, u32[]{:S(2)}) collective-permute-start(f32[3,640]{1,0:T(4,128)S(1)} %add.102), channel_id=1, source_target_pairs={{0,16},{16,0},{1,17},{17,1},{2,18},{18,2},{3,19},{19,3},{4,20},{20... | collective-permute-start | bytes 23048 | tf_op jit(solution)/shard_map/ppermute | solution.py:394
  95.8 4.2 %shard_map.126 = bf16[16,32,640]{2,1,0:T(8,128)(2,1)} custom-call(s32[2]{0:T(128)S(1)} %pad_add_fusion.dev, bf16[3,34,32,640]{3,2,1,0:T(8,128)(2,1)S(1)} %get-tuple-element.90.acts, bf16[512,256]{1,0:T(8,128)(2,1)S(1)} %collective-permute-done.25.got, bf16[16,32,640]{2,1,0:T(8,128)(2,1)S(1)} %bitcast.15, f32[1,640]{1,0:T(1,128)S(1)} %copy-done.2, ...), custom_call_target="tpu_custom_call" | custom-call | flops 964689920 | tf_op jit(solution)/shard_map/pallas_call | solution.py:510
  100.0 0.6 fusion.4
  100.6 1.9 %shard_map.127 = f32[40,5760]{1,0:T(8,128)} custom-call(s32[2]{0:T(128)S(1)} %pad_add_fusion.dev, s32[1]{0:T(128)S(6)} %copy.13.step, f32[40,5760]{1,0:T(8,128)S(1)} %bitcast.11, bf16[40,2944]{1,0:T(8,128)(2,1)S(1)} %collective-permute-done.6.mine, bf16[40,2944]{1,0:T(8,128)(2,1)S(1)} %collective-permute-done.7.theirs, ...), custom_call_target="tpu_custom_call" | custom-call | flops 241172480 | tf_op jit(solution)/shard_map/pallas_call | solution.py:563
  (59 shorter events, 1.9 us)
Async XLA Ops:
  0.6 3.9 %copy-start.1 = (bf16[1,16,32,640]{3,2,1,0:T(8,128)(2,1)S(1)}, bf16[1,16,32,640]{3,2,1,0:T(8,128)(2,1)}, u32[]{:S(2)}) copy-start(bf16[1,16,32,640]{3,2,1,0:T(8,128)(2,1)} %param.8) | copy-start | bytes 1966084
  1.9 8.1 %copy-start.3 = (f32[1,640]{1,0:T(1,128)S(1)}, f32[1,640]{1,0:T(1,128)}, u32[]{:S(2)}) copy-start(f32[1,640]{1,0:T(1,128)} %gain.3) | copy-start | bytes 7684
  2.0 8.1 %copy-start.4 = (f32[1,640]{1,0:T(1,128)S(1)}, f32[1,640]{1,0:T(1,128)}, u32[]{:S(2)}) copy-start(f32[1,640]{1,0:T(1,128)} %shift.3) | copy-start | bytes 7684
  2.0 8.1 %copy-start.5 = (s32[32,24]{1,0:T(8,128)S(1)}, s32[32,24]{1,0:T(8,128)}, u32[]{:S(2)}) copy-start(s32[32,24]{1,0:T(8,128)} %constant.42.clone.table) | copy-start | bytes 9220
  2.0 3.1 %collective-permute-start.3 = (bf16[40,2944]{1,0:T(8,128)(2,1)S(1)}, bf16[40,2944]{1,0:T(8,128)(2,1)S(1)}, u32[]{:S(2)}, u32[]{:S(2)}) collective-permute-start(bf16[40,2944]{1,0:T(8,128)(2,1)S(1)} %get-tuple-element.114), channel_id=1, source_target_pairs={{0,1},{1,0},{2,3},{3,2},{4,5},{5,4},{6,7},{7,6},{8,9},{9,8},{10,11... | collective-permute-start | bytes 706568 | tf_op jit(solution)/shard_map/ppermute | solution.py:345
  4.5 5.4 %collective-permute-start.1 = (bf16[16,32,640]{2,1,0:T(8,128)(2,1)S(1)}, bf16[16,32,640]{2,1,0:T(8,128)(2,1)S(1)}, u32[]{:S(2)}, u32[]{:S(2)}) collective-permute-start(bf16[16,32,640]{2,1,0:T(8,128)(2,1)S(1)} %get-tuple-element.106.cot_own), channel_id=1, source_target_pairs={{0,1},{1,0},{2,3},{3,2},{4,5},{5,4},{6,7},{7,6},{8,9},{9,8},{10,11... | collective-permute-start | bytes 1966088 | tf_op jit(solution)/shard_map/ppermute | solution.py:345
  4.6 5.4 %collective-permute-start = (bf16[16,32,640]{2,1,0:T(8,128)(2,1)S(1)}, bf16[16,32,640]{2,1,0:T(8,128)(2,1)S(1)}, u32[]{:S(2)}, u32[]{:S(2)}) collective-permute-start(bf16[16,32,640]{2,1,0:T(8,128)(2,1)S(1)} %bitcast.12), channel_id=1, source_target_pairs={{0,1},{1,0},{2,3},{3,2},{4,5},{5,4},{6,7},{7,6},{8,9},{9,8},{10,11... | collective-permute-start | bytes 1966088 | tf_op jit(solution)/shard_map/ppermute | solution.py:345
  5.1 15.6 %collective-permute-start.5 = (bf16[80,2944]{1,0:T(8,128)(2,1)S(1)}, bf16[80,2944]{1,0:T(8,128)(2,1)S(1)}, u32[]{:S(2)}, u32[]{:S(2)}) collective-permute-start(bf16[80,2944]{1,0:T(8,128)(2,1)S(1)} %maximum_select_fusion.refs_0_), channel_id=1, source_target_pairs={{4,0},{8,4},{12,8},{14,12},{10,14},{6,10},{2,6},{0,2},{5,1},{9,5},... | collective-permute-start | bytes 1413128 | tf_op jit(solution)/shard_map/ppermute | solution.py:373
  7.8 13.0 %collective-permute-start.4 = (bf16[80,2944]{1,0:T(8,128)(2,1)S(1)}, bf16[80,2944]{1,0:T(8,128)(2,1)S(1)}, u32[]{:S(2)}, u32[]{:S(2)}) collective-permute-start(bf16[80,2944]{1,0:T(8,128)(2,1)S(1)} %maximum_select_fusion.refs_0_), channel_id=1, source_target_pairs={{0,4},{4,8},{8,12},{12,14},{14,10},{10,6},{6,2},{2,0},{1,5},{5,9},... | collective-permute-start | bytes 1413128 | tf_op jit(solution)/shard_map/ppermute | solution.py:370
  7.9 11.7 %collective-permute-start.6 = (bf16[40,2944]{1,0:T(8,128)(2,1)S(1)}, bf16[40,2944]{1,0:T(8,128)(2,1)S(1)}, u32[]{:S(2)}, u32[]{:S(2)}) collective-permute-start(bf16[40,2944]{1,0:T(8,128)(2,1)S(1)} %get-tuple-element.113), channel_id=1, source_target_pairs={{0,16},{16,0},{1,17},{17,1},{2,18},{18,2},{3,19},{19,3},{4,20},{20... | collective-permute-start | bytes 706568 | tf_op jit(solution)/shard_map/ppermute | solution.py:345
  9.9 10.9 %collective-permute-start.7 = (bf16[40,2944]{1,0:T(8,128)(2,1)S(1)}, bf16[40,2944]{1,0:T(8,128)(2,1)S(1)}, u32[]{:S(2)}, u32[]{:S(2)}) collective-permute-start(bf16[40,2944]{1,0:T(8,128)(2,1)S(1)} %get-tuple-element.114), channel_id=1, source_target_pairs={{0,16},{16,0},{1,17},{17,1},{2,18},{18,2},{3,19},{19,3},{4,20},{20... | collective-permute-start | bytes 706568 | tf_op jit(solution)/shard_map/ppermute | solution.py:345
  20.8 12.0 %collective-permute-start.8 = (bf16[80,2944]{1,0:T(8,128)(2,1)S(1)}, bf16[80,2944]{1,0:T(8,128)(2,1)S(1)}, u32[]{:S(2)}, u32[]{:S(2)}) collective-permute-start(bf16[80,2944]{1,0:T(8,128)(2,1)S(1)} %collective-permute-done.4.refs_1_), channel_id=1, source_target_pairs={{0,4},{4,8},{8,12},{12,14},{14,10},{10,6},{6,2},{2,0},{1,5},{5,9},... | collective-permute-start | bytes 1413128 | tf_op jit(solution)/shard_map/ppermute | solution.py:370
  22.4 11.4 %collective-permute-start.9 = (bf16[80,2944]{1,0:T(8,128)(2,1)S(1)}, bf16[80,2944]{1,0:T(8,128)(2,1)S(1)}, u32[]{:S(2)}, u32[]{:S(2)}) collective-permute-start(bf16[80,2944]{1,0:T(8,128)(2,1)S(1)} %collective-permute-done.5.refs_2_), channel_id=1, source_target_pairs={{4,0},{8,4},{12,8},{14,12},{10,14},{6,10},{2,6},{0,2},{5,1},{9,5},... | collective-permute-start | bytes 1413128 | tf_op jit(solution)/shard_map/ppermute | solution.py:373
  22.8 13.7 %collective-permute-start.10 = (bf16[80,2944]{1,0:T(8,128)(2,1)S(1)}, bf16[80,2944]{1,0:T(8,128)(2,1)S(1)}, u32[]{:S(2)}, u32[]{:S(2)}) collective-permute-start(bf16[80,2944]{1,0:T(8,128)(2,1)S(1)} %get-tuple-element.70), channel_id=1, source_target_pairs={{0,16},{16,0},{1,17},{17,1},{2,18},{18,2},{3,19},{19,3},{4,20},{20... | collective-permute-start | bytes 1413128 | tf_op jit(solution)/shard_map/ppermute | solution.py:345
  24.4 26.4 %collective-permute-start.13 = (bf16[80,2944]{1,0:T(8,128)(2,1)S(1)}, bf16[80,2944]{1,0:T(8,128)(2,1)S(1)}, u32[]{:S(2)}, u32[]{:S(2)}) collective-permute-start(bf16[80,2944]{1,0:T(8,128)(2,1)S(1)} %get-tuple-element.77), channel_id=1, source_target_pairs={{0,16},{16,0},{1,17},{17,1},{2,18},{18,2},{3,19},{19,3},{4,20},{20... | collective-permute-start | bytes 1413128 | tf_op jit(solution)/shard_map/ppermute | solution.py:345
  33.9 18.5 %collective-permute-start.11 = (bf16[80,2944]{1,0:T(8,128)(2,1)S(1)}, bf16[80,2944]{1,0:T(8,128)(2,1)S(1)}, u32[]{:S(2)}, u32[]{:S(2)}) collective-permute-start(bf16[80,2944]{1,0:T(8,128)(2,1)S(1)} %collective-permute-done.8.refs_3_), channel_id=1, source_target_pairs={{0,4},{4,8},{8,12},{12,14},{14,10},{10,6},{6,2},{2,0},{1,5},{5,9},... | collective-permute-start | bytes 1413128 | tf_op jit(solution)/shard_map/ppermute | solution.py:370
  36.5 15.9 %collective-permute-start.12 = (bf16[80,2944]{1,0:T(8,128)(2,1)S(1)}, bf16[80,2944]{1,0:T(8,128)(2,1)S(1)}, u32[]{:S(2)}, u32[]{:S(2)}) collective-permute-start(bf16[80,2944]{1,0:T(8,128)(2,1)S(1)} %collective-permute-done.9.refs_4_), channel_id=1, source_target_pairs={{4,0},{8,4},{12,8},{14,12},{10,14},{6,10},{2,6},{0,2},{5,1},{9,5},... | collective-permute-start | bytes 1413128 | tf_op jit(solution)/shard_map/ppermute | solution.py:373
  38.3 16.3 %collective-permute-start.21 = (bf16[40,2944]{1,0:T(8,128)(2,1)S(1)}, bf16[40,2944]{1,0:T(8,128)(2,1)S(1)}, u32[]{:S(2)}, u32[]{:S(2)}) collective-permute-start(bf16[40,2944]{1,0:T(8,128)(2,1)S(1)} %get-tuple-element.111), channel_id=1, source_target_pairs={{4,0},{8,4},{12,8},{14,12},{10,14},{6,10},{2,6},{0,2},{5,1},{9,5},... | collective-permute-start | bytes 706568 | tf_op jit(solution)/shard_map/ppermute | solution.py:373
  39.9 14.6 %collective-permute-start.18 = (bf16[40,2944]{1,0:T(8,128)(2,1)S(1)}, bf16[40,2944]{1,0:T(8,128)(2,1)S(1)}, u32[]{:S(2)}, u32[]{:S(2)}) collective-permute-start(bf16[40,2944]{1,0:T(8,128)(2,1)S(1)} %get-tuple-element.112), channel_id=1, source_target_pairs={{0,4},{4,8},{8,12},{12,14},{14,10},{10,6},{6,2},{2,0},{1,5},{5,9},... | collective-permute-start | bytes 706568 | tf_op jit(solution)/shard_map/ppermute | solution.py:370
  50.8 8.8 %collective-permute-start.16 = (bf16[80,2944]{1,0:T(8,128)(2,1)S(1)}, bf16[80,2944]{1,0:T(8,128)(2,1)S(1)}, u32[]{:S(2)}, u32[]{:S(2)}) collective-permute-start(bf16[80,2944]{1,0:T(8,128)(2,1)S(1)} %get-tuple-element.81), channel_id=1, source_target_pairs={{0,16},{16,0},{1,17},{17,1},{2,18},{18,2},{3,19},{19,3},{4,20},{20... | collective-permute-start | bytes 1413128 | tf_op jit(solution)/shard_map/ppermute | solution.py:345
  52.4 7.5 %collective-permute-start.15 = (bf16[40,2944]{1,0:T(8,128)(2,1)S(1)}, bf16[40,2944]{1,0:T(8,128)(2,1)S(1)}, u32[]{:S(2)}, u32[]{:S(2)}) collective-permute-start(bf16[40,2944]{1,0:T(8,128)(2,1)S(1)} %slice.64), channel_id=1, source_target_pairs={{4,0},{8,4},{12,8},{14,12},{10,14},{6,10},{2,6},{0,2},{5,1},{9,5},... | collective-permute-start | bytes 706568 | tf_op jit(solution)/shard_map/ppermute | solution.py:373
  54.1 8.0 %collective-permute-start.14 = (bf16[40,2944]{1,0:T(8,128)(2,1)S(1)}, bf16[40,2944]{1,0:T(8,128)(2,1)S(1)}, u32[]{:S(2)}, u32[]{:S(2)}) collective-permute-start(bf16[40,2944]{1,0:T(8,128)(2,1)S(1)} %slice.63), channel_id=1, source_target_pairs={{0,4},{4,8},{8,12},{12,14},{14,10},{10,6},{6,2},{2,0},{1,5},{5,9},... | collective-permute-start | bytes 706568 | tf_op jit(solution)/shard_map/ppermute | solution.py:370
  54.5 7.5 %collective-permute-start.17 = (bf16[512,512]{1,0:T(8,128)(2,1)S(1)}, bf16[512,512]{1,0:T(8,128)(2,1)S(1)}, u32[]{:S(2)}, u32[]{:S(2)}) collective-permute-start(bf16[512,512]{1,0:T(8,128)(2,1)S(1)} %get-tuple-element.82), channel_id=1, source_target_pairs={{0,1},{1,0},{2,3},{3,2},{4,5},{5,4},{6,7},{7,6},{8,9},{9,8},{10,11... | collective-permute-start | bytes 1572872 | tf_op jit(solution)/shard_map/ppermute | solution.py:345
  54.7 8.9 %collective-permute-start.22 = (bf16[40,2944]{1,0:T(8,128)(2,1)S(1)}, bf16[40,2944]{1,0:T(8,128)(2,1)S(1)}, u32[]{:S(2)}, u32[]{:S(2)}) collective-permute-start(bf16[40,2944]{1,0:T(8,128)(2,1)S(1)} %get-tuple-element.109), channel_id=1, source_target_pairs={{4,0},{8,4},{12,8},{14,12},{10,14},{6,10},{2,6},{0,2},{5,1},{9,5},... | collective-permute-start | bytes 706568 | tf_op jit(solution)/shard_map/ppermute | solution.py:373
  59.6 6.1 %collective-permute-start.19 = (bf16[40,2944]{1,0:T(8,128)(2,1)S(1)}, bf16[40,2944]{1,0:T(8,128)(2,1)S(1)}, u32[]{:S(2)}, u32[]{:S(2)}) collective-permute-start(bf16[40,2944]{1,0:T(8,128)(2,1)S(1)} %get-tuple-element.110), channel_id=1, source_target_pairs={{0,4},{4,8},{8,12},{12,14},{14,10},{10,6},{6,2},{2,0},{1,5},{5,9},... | collective-permute-start | bytes 706568 | tf_op jit(solution)/shard_map/ppermute | solution.py:370
  59.9 11.8 %collective-permute-start.2 = (bf16[80,2944]{1,0:T(8,128)(2,1)S(1)}, bf16[80,2944]{1,0:T(8,128)(2,1)S(1)}, u32[]{:S(2)}, u32[]{:S(2)}) collective-permute-start(bf16[80,2944]{1,0:T(8,128)(2,1)S(1)} %get-tuple-element.58), channel_id=1, source_target_pairs={{0,16},{16,0},{1,17},{17,1},{2,18},{18,2},{3,19},{19,3},{4,20},{20... | collective-permute-start | bytes 1413128 | tf_op jit(solution)/shard_map/ppermute | solution.py:345
  65.9 6.1 %collective-permute-start.23 = (bf16[40,2944]{1,0:T(8,128)(2,1)S(1)}, bf16[40,2944]{1,0:T(8,128)(2,1)S(1)}, u32[]{:S(2)}, u32[]{:S(2)}) collective-permute-start(bf16[40,2944]{1,0:T(8,128)(2,1)S(1)} %get-tuple-element.107), channel_id=1, source_target_pairs={{4,0},{8,4},{12,8},{14,12},{10,14},{6,10},{2,6},{0,2},{5,1},{9,5},... | collective-permute-start | bytes 706568 | tf_op jit(solution)/shard_map/ppermute | solution.py:373
  67.5 6.1 %collective-permute-start.20 = (bf16[40,2944]{1,0:T(8,128)(2,1)S(1)}, bf16[40,2944]{1,0:T(8,128)(2,1)S(1)}, u32[]{:S(2)}, u32[]{:S(2)}) collective-permute-start(bf16[40,2944]{1,0:T(8,128)(2,1)S(1)} %get-tuple-element.108), channel_id=1, source_target_pairs={{0,4},{4,8},{8,12},{12,14},{14,10},{10,6},{6,2},{2,0},{1,5},{5,9},... | collective-permute-start | bytes 706568 | tf_op jit(solution)/shard_map/ppermute | solution.py:370
  68.0 5.6 %copy-start.2 = (f32[1,640]{1,0:T(1,128)S(1)}, f32[1,640]{1,0:T(1,128)}, u32[]{:S(2)}) copy-start(f32[1,640]{1,0:T(1,128)} %bias.1) | copy-start | bytes 7684
  73.6 3.2 %collective-permute-start.26 = (f32[3,640]{1,0:T(4,128)S(1)}, f32[3,640]{1,0:T(4,128)S(1)}, u32[]{:S(2)}, u32[]{:S(2)}) collective-permute-start(f32[3,640]{1,0:T(4,128)S(1)} %fusion.2), channel_id=1, source_target_pairs={{0,1},{1,0},{2,3},{3,2},{4,5},{5,4},{6,7},{7,6},{8,9},{9,8},{10,11... | collective-permute-start | bytes 23048 | tf_op jit(solution)/shard_map/ppermute | solution.py:345
  75.7 12.3 %collective-permute-start.25 = (bf16[512,256]{1,0:T(8,128)(2,1)S(1)}, bf16[512,256]{1,0:T(8,128)(2,1)S(1)}, u32[]{:S(2)}, u32[]{:S(2)}) collective-permute-start(bf16[512,256]{1,0:T(8,128)(2,1)S(1)} %shard_map.125), channel_id=1, source_target_pairs={{0,1},{1,0},{2,3},{3,2},{4,5},{5,4},{6,7},{7,6},{8,9},{9,8},{10,11... | collective-permute-start | bytes 786440 | tf_op jit(solution)/shard_map/ppermute | solution.py:345
  76.3 11.6 %collective-permute-start.24 = (bf16[40,2944]{1,0:T(8,128)(2,1)S(1)}, bf16[40,2944]{1,0:T(8,128)(2,1)S(1)}, u32[]{:S(2)}, u32[]{:S(2)}) collective-permute-start(bf16[40,2944]{1,0:T(8,128)(2,1)S(1)} %add_convert_fusion.1), channel_id=1, source_target_pairs={{0,4},{4,8},{8,12},{12,14},{14,10},{10,6},{6,2},{2,0},{1,5},{5,9},... | collective-permute-start | bytes 706568 | tf_op jit(solution)/shard_map/ppermute | solution.py:370
  76.9 7.4 %collective-permute-start.27 = (f32[3,640]{1,0:T(4,128)S(1)}, f32[3,640]{1,0:T(4,128)S(1)}, u32[]{:S(2)}, u32[]{:S(2)}) collective-permute-start(f32[3,640]{1,0:T(4,128)S(1)} %fusion.5), channel_id=1, source_target_pairs={{0,2},{2,0},{1,3},{3,1},{4,6},{6,4},{5,7},{7,5},{8,10},{10,8},{9,1... | collective-permute-start | bytes 23048 | tf_op jit(solution)/shard_map/ppermute | solution.py:394
  84.3 3.7 %collective-permute-start.28 = (f32[3,640]{1,0:T(4,128)S(1)}, f32[3,640]{1,0:T(4,128)S(1)}, u32[]{:S(2)}, u32[]{:S(2)}) collective-permute-start(f32[3,640]{1,0:T(4,128)S(1)} %add.97), channel_id=1, source_target_pairs={{0,4},{4,0},{8,12},{12,8},{1,5},{5,1},{9,13},{13,9},{2,6},{6,2},{1... | collective-permute-start | bytes 23048 | tf_op jit(solution)/shard_map/ppermute | solution.py:394
  88.0 5.4 %collective-permute-start.31 = (f32[3,640]{1,0:T(4,128)S(1)}, f32[3,640]{1,0:T(4,128)S(1)}, u32[]{:S(2)}, u32[]{:S(2)}) collective-permute-start(f32[3,640]{1,0:T(4,128)S(1)} %add.98), channel_id=1, source_target_pairs={{0,8},{4,12},{8,0},{12,4},{1,9},{5,13},{9,1},{13,5},{2,10},{6,14},... | collective-permute-start | bytes 23048 | tf_op jit(solution)/shard_map/ppermute | solution.py:394
  88.2 12.4 %collective-permute-start.30 = (bf16[40,2944]{1,0:T(8,128)(2,1)S(1)}, bf16[40,2944]{1,0:T(8,128)(2,1)S(1)}, u32[]{:S(2)}, u32[]{:S(2)}) collective-permute-start(bf16[40,2944]{1,0:T(8,128)(2,1)S(1)} %add_convert_fusion.total), channel_id=1, source_target_pairs={{1,16},{16,1},{3,18},{18,3},{5,20},{20,5},{7,22},{22,7},{9,24},{24... | collective-permute-start | bytes 706568 | tf_op jit(solution)/shard_map/ppermute | solution.py:562
  88.9 11.8 %collective-permute-start.29 = (bf16[40,2944]{1,0:T(8,128)(2,1)S(1)}, bf16[40,2944]{1,0:T(8,128)(2,1)S(1)}, u32[]{:S(2)}, u32[]{:S(2)}) collective-permute-start(bf16[40,2944]{1,0:T(8,128)(2,1)S(1)} %add_convert_fusion.total), channel_id=1, source_target_pairs={{1,0},{16,17},{0,16},{17,1},{3,2},{18,19},{2,18},{19,3},{5,4},{20,... | collective-permute-start | bytes 706568 | tf_op jit(solution)/shard_map/ppermute | solution.py:561
  93.3 6.7 %collective-permute-start.32 = (f32[3,640]{1,0:T(4,128)S(1)}, f32[3,640]{1,0:T(4,128)S(1)}, u32[]{:S(2)}, u32[]{:S(2)}) collective-permute-start(f32[3,640]{1,0:T(4,128)S(1)} %add.102), channel_id=1, source_target_pairs={{0,16},{16,0},{1,17},{17,1},{2,18},{18,2},{3,19},{19,3},{4,20},{20... | collective-permute-start | bytes 23048 | tf_op jit(solution)/shard_map/ppermute | solution.py:394
  95.8 4.8 %copy-start = (f32[1,40,5760]{2,1,0:T(8,128)S(1)}, f32[1,40,5760]{2,1,0:T(8,128)}, u32[]{:S(2)}) copy-start(f32[1,40,5760]{2,1,0:T(8,128)} %param.10) | copy-start | bytes 2764804

commit v9 on v8

--- a/solution.py
+++ b/solution.py
@@ -124,12 +124,13 @@
     core = dev[0] % 2
     rows, width, chans = acts.shape[1] - 2, acts.shape[2], acts.shape[3]
     cells = rows * width
-    count = pieces[0].shape[0]
 
     def emit(window, place, wide):
         value = jnp.dot(cot_t[...], window, preferred_element_type=F32)
-        for q, piece in enumerate(pieces):
-            piece[:, pl.ds(place, wide)] = value[q * count:(q + 1) * count].astype(BF16)
+        at = 0
+        for piece in pieces:
+            piece[:, pl.ds(place, wide)] = value[at:at + piece.shape[0]].astype(BF16)
+            at += piece.shape[0]
 
     def two_taps(k, _):
         taps, place = cols.pair(core, k, chans)
@@ -320,22 +321,15 @@
     sums[1:2] = scale * jnp.sum(shifts, axis=0, keepdims=True)
 
 
-def finish_kernel(cols, dev, step, shard, mine, theirs, total, across, aside, out):
-    me = dev[0]
-    core = me % 2
-    same = me // (dev[1] // 2) == core
-    lower = core == 0
+def finish_kernel(cols, dev, step, shard, mine, theirs, ours, aside, out):
+    lower = dev[0] % 2 == 0
     rate = LR_KERNEL * (1.0 - (step[0] % 1000).astype(F32) / 2000.0)
     factor = 0.5 * cols.total ** (-0.5) * rate
-    total, across, aside = (ref[...].astype(F32) for ref in (total, across, aside))
-    left = jnp.where(same, jnp.where(lower, total, across), jnp.where(lower, across, aside))
-    right = jnp.where(same, jnp.where(lower, across, total), jnp.where(lower, aside, across))
-    mine, theirs = mine[...].astype(F32), theirs[...].astype(F32)
-    peer_left, peer_right = jnp.where(lower, mine, theirs), jnp.where(lower, theirs, mine)
-    out[:, :cols.lead] = 0.5 * (shard[:, :cols.lead] + peer_left) - factor * left
-    out[:, cols.lead:] = (
-        0.5 * (shard[:, cols.lead:] + peer_right[:, cols.both:]) - factor * right[:, cols.both:]
-    )
+    here = 0.5 * mine[...].astype(F32) - factor * ours[...].astype(F32)
+    there = 0.5 * theirs[...].astype(F32) - factor * aside[...].astype(F32)
+    left, right = jnp.where(lower, here, there), jnp.where(lower, there, here)
+    out[:, :cols.lead] = 0.5 * shard[:, :cols.lead] + left
+    out[:, cols.lead:] = 0.5 * shard[:, cols.lead:] + right[:, cols.both:]
 
 
 NODE = ("z", "y")
@@ -381,9 +375,9 @@
                     line.append(self.node(at, -k))
                     if k < self.reach:
                         line.append(self.node(at, k))
-                for j in range(self.reach):
-                    targets = [self.node(at, self.reach - j), self.node(at, j + 1 - self.reach)]
-                    for which in (replica, 1 - replica):
+                for which in (replica, 1 - replica):
+                    for j in range(self.reach):
+                        targets = [self.node(at, self.reach - j), self.node(at, j + 1 - self.reach)]
                         line += [(2 * target + which) * part for target in targets]
                 rows[replica, node, :] = line
         return rows.reshape(-1, 3 * self.count)
@@ -419,8 +413,8 @@
     scale = cols.total ** (-0.5)
     params = jnp.concatenate([conv_bias, gn_gain, gn_shift])
     me = ((replica * zs + z) * 2 + y) * 2 + core
-    core, lower, me = tied(core, lower, me)
-    dev = jnp.stack([me, jnp.int32(4 * zs * replicas)])
+    core, lower, same, me = tied(core, lower, replica == core, me)
+    dev = me.reshape(1)
 
     mine = lax.dynamic_slice_in_dim(shard, core * cols.start, cols.lead, 1).astype(BF16)
     theirs = lax.dynamic_slice_in_dim(shard, (1 - core) * cols.start, cols.lead, 1).astype(BF16)
@@ -460,9 +454,10 @@
         [pltpu.VMEM((chans, 2 * cells), F32)],
         8, flops // 4,
     )(dev, table, latent, lat_far, cot_b, cot_far, gn_gain, gn_shift)
+    counts = [zs, 1, zs - 2, 1] if paired else [2 * zs]
     pieces = call(
         partial(grad_kernel, cols),
-        [jax.ShapeDtypeStruct((2 * part, cols.lead), BF16)] * (2 * zs),
+        [jax.ShapeDtypeStruct((n * 2 * part, cols.lead), BF16) for n in counts],
         [SMEM_SPEC] + [VMEM_SPEC] * 2,
         [],
         4, flops // 2,
@@ -519,59 +514,71 @@
         return vectors + swap(vectors, "core")
 
     if paired:
-        kept, sent = pieces[::2], list(pieces[1::2])
-        up, down, peer, sent[0] = tied(up1, down1, peer, sent[0])
+        kept, *sent = pieces
+        up, down, sent[0], mine, theirs = tied(up1, down1, sent[0], *peer)
         blocks = [unit, up, down]
-        crossed = [swap(piece, "replica") for piece in sent]
-        up_sum = down_sum = ()
-        for j in range(zs):
-            if j < zs - 2:
-                up, down = ring.up(up), ring.down(down)
-                if j < zs - 3:
-                    up, down, cots, *slopes, order = tied(up, down, *slopes_of(stats))
-                    blocks += [up, down]
-                    crossed[j] = tied(crossed[j], up)[0]
-                else:
-                    cots, crossed[j - 1] = tied(cots, crossed[j - 1])
-                    first_sums = back(0, cots, slopes, blocks)
-                    conv_first_own, conv_send = conv_first(blocks)
-                    up, down, crossed[j], first_sums, conv_send = tied(
-                        up, down, crossed[j], first_sums, conv_send
-                    )
-                    conv_first_got = swap(conv_send, "core")
-                    late = [up, down]
-            elif j == zs - 2:
-                halves = ring.up(up[:part]), ring.down(down[part:])
-                *halves, crossed[j], conv_first_got = tied(*halves, crossed[j], conv_first_got)
-                late += halves
-                sums = back(1, cots, slopes, late)
-            else:
-                crossed[j], sums, acts, *received = tied(crossed[j], sums, acts, *up_sum, *down_sum)
-                up_sum, down_sum = tuple(received[:1]), tuple(received[1:])
-                conv_got = swap(conv_far(acts, late), "core")
-            ahead = add(kept[j][:part], crossed[j][:part], *up_sum)
-            behind = (kept[j][part:], crossed[j][part:], *down_sum)
-            up_sum = (ring.up(ahead),)
+        first, middle, final = (swap(piece, "replica") for piece in sent)
+        up, down = ring.up(up), ring.down(down)
+        up, down, cots, *slopes, order = tied(up, down, *slopes_of(stats))
+        blocks += [up, down]
+
+        def ring_step(j, crossed, *received):
+            rows = slice(2 * j * part, (2 * j + 2) * part)
+            parts = kept[rows], crossed
+            ahead, behind = (tuple(x[half] for x in parts) for half in (slice(part), slice(part, None)))
+            up_sum = ring.up(add(*ahead, *received[:1]))
             if j < zs - 1:
-                down_sum = (ring.down(add(*behind)),)
-        vectors = hop(hop(chip_sum(first_sums + sums), "y", 1), "z", 1)
-        last, conv_got, vectors = tied(*up_sum, conv_got, vectors)
+                return up_sum, ring.down(add(*behind, *received[1:]))
+            return up_sum, behind + tuple(received[1:])
+
+        up, down = ring.up(up), ring.down(down)
+        conv_first_own, conv_send = conv_first(blocks)
+        first, conv_send = tied(first, conv_send)
+        received = ring_step(0, first)
+        up, down, conv_send = tied(up, down, conv_send)
+        late = [up, down]
+
+        halves = ring.up(up[:part]), ring.down(down[part:])
+        conv_first_got = swap(conv_send, "core")
+        cots, conv_send = tied(cots, conv_send)
+        middle, first_sums = tied(middle, back(0, cots, slopes, blocks))
+        for j in range(1, zs - 2):
+            received = ring_step(j, middle[(2 * j - 2) * part:2 * j * part], *received)
+        *halves, conv_first_got = tied(*halves, conv_first_got)
+        late += halves
+
+        sums = back(1, cots, slopes, late)
+        middle, sums, *received = tied(middle, sums, *received)
+        acts_last, *_ = tied(acts, sums, *received)
+        received = ring_step(zs - 2, middle[(2 * zs - 6) * part:], *received)
+        conv_got = swap(conv_far(acts_last, late), "core")
+        vectors = hop(chip_sum(first_sums + sums), "replica", 1)
+        final, conv_got, *received = tied(final, conv_got, *received)
+        last, behind = ring_step(zs - 1, final, *received)
+        block = conv_own(conv_got, [conv_first_own, conv_first_got, order], late)
+        last, block, vectors = tied(last, block, vectors)
         total = add(*behind, last)
-        earlier = [conv_first_own, conv_first_got, order]
-        across = lax.ppermute(total, ("replica", "core"), [(1, 0), (2, 3), (0, 2), (3, 1)])
-        aside = lax.ppermute(total, ("replica", "core"), [(1, 2), (2, 1)])
+        across = swap(total, "replica")
+        ours, others = jnp.where(same, total, across), jnp.where(same, across, total)
+        aside = swap(others, "core")
         new_kernel = call(
             partial(finish_kernel, cols), jax.ShapeDtypeStruct(shard.shape, F32),
-            [SMEM_SPEC] * 2 + [VMEM_SPEC] * 6, [], 8, flops // 16,
-        )(dev, step, shard, *peer, total, across, aside)
-        vectors = hop(vectors, "z", 2)
-        new_v = 0.5 * hop(vectors, "replica", 1)
+            [SMEM_SPEC] * 2 + [VMEM_SPEC] * 5, [], 8, flops // 16,
+        )(dev, step, shard, mine, theirs, ours, aside)
+        vectors = hop(vectors, "z", 1)
+        vectors = hop(vectors, "y", 1)
+        reach = 2
+        while reach < zs:
+            vectors = hop(vectors, "z", reach)
+            reach *= 2
+        new_v = 0.5 * vectors
     else:
-        late, earlier = [lax.all_gather(unit, NODE, axis=0, tiled=True)], []
+        late = [lax.all_gather(unit, NODE, axis=0, tiled=True)]
         cots, slope, slope_x = slopes_of(stats)
         sums = back(0, cots, [slope, slope_x], late)
-        conv_got, vectors = swap(conv_far(acts, late), "core"), chip_sum(sums)
-        terms = jnp.concatenate(pieces).reshape(2 * zs, 2, part, cols.lead)
+        vectors = chip_sum(sums)
+        block = conv_own(swap(conv_far(acts, late), "core"), [], late)
+        terms = pieces[0].reshape(2 * zs, 2, part, cols.lead)
         summed = lax.psum_scatter(terms, NODE, scatter_dimension=0, tiled=False)
         ours = lax.dynamic_index_in_dim(summed, core, 0, keepdims=False)
         got = swap(lax.dynamic_index_in_dim(summed, 1 - core, 0, keepdims=False), "core")
@@ -584,7 +591,6 @@
         stepped_v = lax.psum(vectors, NODE)
         new_v = 0.5 * (stepped_v + from_peer(level, stepped_v))
 
-    block = conv_own(conv_got, earlier, late)
     return (
         block[None],
         new_kernel[None],

time: 103 us -> 103 us (level)
  waiting for transfers between devices: 24.3 us -> 34.8 us
  starting transfers between devices: 35.5 us -> 29 us
  Pallas kernels: 36.4 us -> 32.4 us
    ppermute x7, waiting for transfers between devices: 2.96 us -> 11.1 us  [down(): return lax.ppermute(value, NODE, self.behind)]
    ppermute x2 -> x0, starting transfers between devices: 5.13 us -> none  [the longest x1 4.46 us: per_device(): lax.ppermute(total, ('replica', 'core'), [(1, 0), (2, 3), (0, 2), (3, 1)])]
    ppermute x8, waiting for transfers between devices: 7.09 us -> 9.65 us  [up(): return lax.ppermute(value, NODE, self.ahead)]
    ppermute x7, starting transfers between devices: 11.1 us -> 8.79 us  [down(): return lax.ppermute(value, NODE, self.behind)]
    ppermute x8, starting transfers between devices: 5.55 us -> 6.85 us  [up(): return lax.ppermute(value, NODE, self.ahead)]
    ppermute x12 -> x13, starting transfers between devices: 9.45 us -> 8.25 us  [swap(): return lax.ppermute(value, axis, [(0, 1), (1, 0)])]
    ppermute x12 -> x13, waiting for transfers between devices: 5.43 us -> 4.25 us  [swap(): return lax.ppermute(value, axis, [(0, 1), (1, 0)])]
    pallas_call x2, Pallas kernels: 9.7 us -> 8.6 us  [back(): call(partial(back_kernel, cols, stages, stage), jax.ShapeDtypeStruct((2,...]
  transfers between devices with their start and end apart: 33 -> 32, of which waited for: 11 -> 15; matrix products, arithmetic and copies ran while one was open for 3% -> 3% of each run, Pallas kernels for 34% -> 30%
where the time goes in v9:
time: 103 us
  waiting for transfers between devices  34.8 us (34%)
  Pallas kernels  32.4 us (31%)
  starting transfers between devices  29 us (28%)
  other arithmetic  2.9 us (3%)
  local copies, waits for them, and re-layouts  1.94 us (2%)
  between operations  1.55 us (2%)
    ppermute x7, waiting for transfers between devices, down(): return lax.ppermute(value, NODE, self.behind)  11.1 us
    ppermute x4, waiting for transfers between devices, hop(): lax.ppermute(value, axis, [(s, s ^ mask) for s in range(count)])  9.8 us
    ppermute x8, waiting for transfers between devices, up(): return lax.ppermute(value, NODE, self.ahead)  9.65 us
    ppermute x7, starting transfers between devices, down(): return lax.ppermute(value, NODE, self.behind)  8.79 us
    pallas_call x2, Pallas kernels, back(): call(partial(back_kernel, cols, stages, stage), jax.ShapeDtypeStruct((2,...  8.6 us
    ppermute x13, starting transfers between devices, swap(): return lax.ppermute(value, axis, [(0, 1), (1, 0)])  8.25 us
    ppermute x8, starting transfers between devices, up(): return lax.ppermute(value, NODE, self.ahead)  6.85 us
    ppermute x4, starting transfers between devices, hop(): lax.ppermute(value, axis, [(s, s ^ mask) for s in range(count)])  5.08 us
  transfers between devices with their start and end apart: 32, of which 15 were waited for; matrix products, arithmetic and copies ran while one was open for 3% of the time, Pallas kernels for 30%

profile of v9, /device:TPU:0, one launch (start us, length us, event | category | flops | bytes accessed | tf_op | source)
XLA Modules:
  0.0 102.5 jit_solution(13422810725112886440)
XLA Ops:
  0.7 1.3 %fusion = (bf16[40,2944]{1,0:T(8,128)(2,1)S(1)}, bf16[40,2944]{1,0:T(8,128)(2,1)S(1)}) fusion(f32[1,40,5760]{2,1,0:T(8,128)} %param.10, s32[]{:T(128)S(6)} %select_n.27, s32[]{:T(128)S(6)} %select_n.28), kind=kLoop, calls=%fused_computation.12 | loop fusion | bytes 942088 | tf_op jit(solution)/shard_map/convert_element_type | solution.py:419
  2.0 0.5 collective-permute-start.4
  2.5 2.0 %fusion.3 = (f32[640]{0:T(1024)S(1)}, bf16[16,32,640]{2,1,0:T(8,128)(2,1)S(1)}) fusion(f32[1,16,32,640]{3,2,1,0:T(8,128)} %param.9), kind=kLoop, calls=%fused_computation.20 | loop fusion | flops 654720 | bytes 1968640 | tf_op jit(solution)/shard_map/reduce_sum | solution.py:512
  4.6 0.5 collective-permute-start
  5.1 2.7 %collective-permute-start.6 = (bf16[80,2944]{1,0:T(8,128)(2,1)S(1)}, bf16[80,2944]{1,0:T(8,128)(2,1)S(1)}, u32[]{:S(2)}, u32[]{:S(2)}) collective-permute-start(bf16[80,2944]{1,0:T(8,128)(2,1)S(1)} %maximum_select_fusion.refs_0_), channel_id=1, source_target_pairs={{4,0},{8,4},{12,8},{14,12},{10,14},{6,10},{2,6},{0,2},{5,1},{9,5},... | collective-permute-start | bytes 1413128 | tf_op jit(solution)/shard_map/ppermute | solution.py:367
  7.9 1.9 %collective-permute-start.7 = (bf16[40,2944]{1,0:T(8,128)(2,1)S(1)}, bf16[40,2944]{1,0:T(8,128)(2,1)S(1)}, u32[]{:S(2)}, u32[]{:S(2)}) collective-permute-start(bf16[40,2944]{1,0:T(8,128)(2,1)S(1)} %get-tuple-element.115), channel_id=1, source_target_pairs={{0,16},{16,0},{1,17},{17,1},{2,18},{18,2},{3,19},{19,3},{4,20},{20... | collective-permute-start | bytes 706568 | tf_op jit(solution)/shard_map/ppermute | solution.py:339
  10.0 4.4 %shard_map.119 = (f32[2,640]{1,0:T(2,128)S(1)}, bf16[3,34,32,640]{3,2,1,0:T(8,128)(2,1)S(1)}, bf16[640,1024]{1,0:T(8,128)(2,1)S(1)}) custom-call(s32[1]{0:T(128)} %bitcast.dev, s32[32,24]{1,0:T(8,128)S(1)} %copy-done.5, bf16[16,32,640]{2,1,0:T(8,128)(2,1)S(1)} %bitcast.13, bf16[16,32,640]{2,1,0:T(8,128)(2,1)S(1)} %collective-permute-done.lat_far, ...), custom_call_target="tpu_custom_call" | custom-call | flops 964689920 | tf_op jit(solution)/shard_map/pallas_call | solution.py:450
  14.3 4.6 %shard_map.120 = (bf16[320,2944]{1,0:T(8,128)(2,1)S(1)}, bf16[80,2944]{1,0:T(8,128)(2,1)S(1)}, bf16[160,2944]{1,0:T(8,128)(2,1)S(1)}, bf16[80,2944]{1,0:T(8,128)(2,1)S(1)}) custom-call(s32[1]{0:T(128)} %bitcast.dev, bf16[3,34,32,640]{3,2,1,0:T(8,128)(2,1)S(1)} %get-tuple-element.91.acts, bf16[640,1024]{1,0:T(8,128)(2,1)S(1)} %get-tuple-element.58.cot_t), custom_call_target="tpu_custom_call" | custom-call | flops 1929379840 | tf_op jit(solution)/shard_map/pallas_call | solution.py:458
  19.0 1.7 %collective-permute-done.8.theirs = bf16[40,2944]{1,0:T(8,128)(2,1)S(1)} collective-permute-done((bf16[40,2944]{1,0:T(8,128)(2,1)S(1)}, bf16[40,2944]{1,0:T(8,128)(2,1)S(1)}, u32[]{:S(2)}, u32[]{:S(2)}) %collective-permute-start.8) | collective-permute-done | bytes 235552 | tf_op jit(solution)/shard_map/ppermute | solution.py:339
  20.8 1.7 %collective-permute-start.9 = (bf16[80,2944]{1,0:T(8,128)(2,1)S(1)}, bf16[80,2944]{1,0:T(8,128)(2,1)S(1)}, u32[]{:S(2)}, u32[]{:S(2)}) collective-permute-start(bf16[80,2944]{1,0:T(8,128)(2,1)S(1)} %collective-permute-done.5.refs_1_), channel_id=1, source_target_pairs={{0,4},{4,8},{8,12},{12,14},{14,10},{10,6},{6,2},{2,0},{1,5},{5,9},... | collective-permute-start | bytes 1413128 | tf_op jit(solution)/shard_map/ppermute | solution.py:364
  22.8 1.6 %collective-permute-start.13 = (bf16[80,2944]{1,0:T(8,128)(2,1)S(1)}, bf16[80,2944]{1,0:T(8,128)(2,1)S(1)}, u32[]{:S(2)}, u32[]{:S(2)}) collective-permute-start(bf16[80,2944]{1,0:T(8,128)(2,1)S(1)} %get-tuple-element.75), channel_id=1, source_target_pairs={{0,16},{16,0},{1,17},{17,1},{2,18},{18,2},{3,19},{19,3},{4,20},{20... | collective-permute-start | bytes 1413128 | tf_op jit(solution)/shard_map/ppermute | solution.py:339
  24.8 4.5 %shard_map.121 = (bf16[3,34,32,768]{3,2,1,0:T(8,128)(2,1)S(1)}, bf16[32,32,640]{2,1,0:T(8,128)(2,1)S(1)}, bf16[32,32,640]{2,1,0:T(8,128)(2,1)S(1)}, bf16[640,768]{1,0:T(8,128)(2,1)S(1)}) custom-call(s32[1]{0:T(128)} %bitcast.dev, s32[32,24]{1,0:T(8,128)S(1)} %copy-done.5, f32[2,640]{1,0:T(2,128)S(1)} %get-tuple-element.67.stats, f32[1,640]{1,0:T(1,128)S(1)} %copy-done.3, ...), custom_call_target="tpu_custom_call" | custom-call | flops 964689920 | tf_op jit(solution)/shard_map/pallas_call | solution.py:470
  29.3 3.5 %collective-permute-done.9.refs_3_ = bf16[80,2944]{1,0:T(8,128)(2,1)S(1)} collective-permute-done((bf16[80,2944]{1,0:T(8,128)(2,1)S(1)}, bf16[80,2944]{1,0:T(8,128)(2,1)S(1)}, u32[]{:S(2)}, u32[]{:S(2)}) %collective-permute-start.9) | collective-permute-done | bytes 471072 | tf_op jit(solution)/shard_map/ppermute | solution.py:364
  32.8 1.1 %collective-permute-done.10.refs_4_ = bf16[80,2944]{1,0:T(8,128)(2,1)S(1)} collective-permute-done((bf16[80,2944]{1,0:T(8,128)(2,1)S(1)}, bf16[80,2944]{1,0:T(8,128)(2,1)S(1)}, u32[]{:S(2)}, u32[]{:S(2)}) %collective-permute-start.10) | collective-permute-done | bytes 471072 | tf_op jit(solution)/shard_map/ppermute | solution.py:367
  33.9 1.6 %collective-permute-start.11 = (bf16[80,2944]{1,0:T(8,128)(2,1)S(1)}, bf16[80,2944]{1,0:T(8,128)(2,1)S(1)}, u32[]{:S(2)}, u32[]{:S(2)}) collective-permute-start(bf16[80,2944]{1,0:T(8,128)(2,1)S(1)} %collective-permute-done.9.refs_3_), channel_id=1, source_target_pairs={{0,4},{4,8},{8,12},{12,14},{14,10},{10,6},{6,2},{2,0},{1,5},{5,9},... | collective-permute-start | bytes 1413128 | tf_op jit(solution)/shard_map/ppermute | solution.py:364
  35.4 0.4 collective-permute-start.12
  35.9 4.0 %shard_map.122 = (f32[512,512]{1,0:T(8,128)S(1)}, bf16[512,512]{1,0:T(8,128)(2,1)S(1)}) custom-call(s32[1]{0:T(128)} %bitcast.dev, bf16[3,34,32,640]{3,2,1,0:T(8,128)(2,1)S(1)} %get-tuple-element.91.acts, bf16[80,2944]{1,0:T(8,128)(2,1)S(1)} %maximum_select_fusion.refs_0_, bf16[80,2944]{1,0:T(8,128)(2,1)S(1)} %collective-permute-done.5.refs_1_, ...), custom_call_target="tpu_custom_call" | custom-call | flops 964689920 | tf_op jit(solution)/shard_map/pallas_call | solution.py:488
  40.0 0.7 collective-permute-start.19
  40.7 1.4 %collective-permute-start.17 = (bf16[40,2944]{1,0:T(8,128)(2,1)S(1)}, bf16[40,2944]{1,0:T(8,128)(2,1)S(1)}, u32[]{:S(2)}, u32[]{:S(2)}) collective-permute-start(bf16[40,2944]{1,0:T(8,128)(2,1)S(1)} %get-tuple-element.112), channel_id=1, source_target_pairs={{0,4},{4,8},{8,12},{12,14},{14,10},{10,6},{6,2},{2,0},{1,5},{5,9},... | collective-permute-start | bytes 706568 | tf_op jit(solution)/shard_map/ppermute | solution.py:364
  42.1 4.8 %collective-permute-done.11.refs_0_.refs_3_ = bf16[80,2944]{1,0:T(8,128)(2,1)S(1)} collective-permute-done((bf16[80,2944]{1,0:T(8,128)(2,1)S(1)}, bf16[80,2944]{1,0:T(8,128)(2,1)S(1)}, u32[]{:S(2)}, u32[]{:S(2)}) %collective-permute-start.11) | collective-permute-done | bytes 471072 | tf_op jit(solution)/shard_map/ppermute | solution.py:364
  46.9 1.3 %collective-permute-done.12.refs_1_.refs_4_ = bf16[80,2944]{1,0:T(8,128)(2,1)S(1)} collective-permute-done((bf16[80,2944]{1,0:T(8,128)(2,1)S(1)}, bf16[80,2944]{1,0:T(8,128)(2,1)S(1)}, u32[]{:S(2)}, u32[]{:S(2)}) %collective-permute-start.12) | collective-permute-done | bytes 471072 | tf_op jit(solution)/shard_map/ppermute | solution.py:367
  48.2 5.4 %shard_map.123 = f32[2,640]{1,0:T(2,128)S(1)} custom-call(s32[1]{0:T(128)} %bitcast.dev, bf16[3,34,32,768]{3,2,1,0:T(8,128)(2,1)S(1)} %get-tuple-element.79.cots, bf16[32,32,640]{2,1,0:T(8,128)(2,1)S(1)} %get-tuple-element.80.slope, bf16[32,32,640]{2,1,0:T(8,128)(2,1)S(1)} %get-tuple-element.81.slope_x, bf16[80,2944]{1,0:T(8,128)(2,1)S(1)} %maximum_select_fusion.refs_0_, ...), custom_call_target="tpu_custom_call" | custom-call | flops 964689920 | tf_op jit(solution)/shard_map/pallas_call | solution.py:480
  53.6 0.8 collective-permute-done.3
  54.5 1.5 %collective-permute-start.15 = (bf16[40,2944]{1,0:T(8,128)(2,1)S(1)}, bf16[40,2944]{1,0:T(8,128)(2,1)S(1)}, u32[]{:S(2)}, u32[]{:S(2)}) collective-permute-start(bf16[40,2944]{1,0:T(8,128)(2,1)S(1)} %slice.83), channel_id=1, source_target_pairs={{4,0},{8,4},{12,8},{14,12},{10,14},{6,10},{2,6},{0,2},{5,1},{9,5},... | collective-permute-start | bytes 706568 | tf_op jit(solution)/shard_map/ppermute | solution.py:367
  56.0 0.6 collective-permute-start.14
  56.8 1.5 %collective-permute-start.20 = (bf16[40,2944]{1,0:T(8,128)(2,1)S(1)}, bf16[40,2944]{1,0:T(8,128)(2,1)S(1)}, u32[]{:S(2)}, u32[]{:S(2)}) collective-permute-start(bf16[40,2944]{1,0:T(8,128)(2,1)S(1)} %get-tuple-element.109), channel_id=1, source_target_pairs={{4,0},{8,4},{12,8},{14,12},{10,14},{6,10},{2,6},{0,2},{5,1},{9,5},... | collective-permute-start | bytes 706568 | tf_op jit(solution)/shard_map/ppermute | solution.py:367
  58.2 0.6 collective-permute-start.18
  58.8 4.3 %collective-permute-done.15.refs_3_.refs_6_ = bf16[40,2944]{1,0:T(8,128)(2,1)S(1)} collective-permute-done((bf16[40,2944]{1,0:T(8,128)(2,1)S(1)}, bf16[40,2944]{1,0:T(8,128)(2,1)S(1)}, u32[]{:S(2)}, u32[]{:S(2)}) %collective-permute-start.15) | collective-permute-done | bytes 235552 | tf_op jit(solution)/shard_map/ppermute | solution.py:367
  63.2 1.3 %collective-permute-start.2 = (bf16[80,2944]{1,0:T(8,128)(2,1)S(1)}, bf16[80,2944]{1,0:T(8,128)(2,1)S(1)}, u32[]{:S(2)}, u32[]{:S(2)}) collective-permute-start(bf16[80,2944]{1,0:T(8,128)(2,1)S(1)} %get-tuple-element.60), channel_id=1, source_target_pairs={{0,16},{16,0},{1,17},{17,1},{2,18},{18,2},{3,19},{19,3},{4,20},{20... | collective-permute-start | bytes 1413128 | tf_op jit(solution)/shard_map/ppermute | solution.py:339
  64.6 3.2 %shard_map.124 = f32[2,640]{1,0:T(2,128)S(1)} custom-call(s32[1]{0:T(128)} %bitcast.dev, bf16[3,34,32,768]{3,2,1,0:T(8,128)(2,1)S(1)} %get-tuple-element.79.cots, bf16[32,32,640]{2,1,0:T(8,128)(2,1)S(1)} %get-tuple-element.80.slope, bf16[32,32,640]{2,1,0:T(8,128)(2,1)S(1)} %get-tuple-element.81.slope_x, ...), custom_call_target="tpu_custom_call" | custom-call | flops 964689920 | tf_op jit(solution)/shard_map/pallas_call | solution.py:480
  67.8 1.4 %shard_map.125 = bf16[512,256]{1,0:T(8,128)(2,1)S(1)} custom-call(s32[1]{0:T(128)} %bitcast.dev, bf16[3,34,32,640]{3,2,1,0:T(8,128)(2,1)S(1)} %get-tuple-element.91.acts, bf16[80,2944]{1,0:T(8,128)(2,1)S(1)} %collective-permute-done.11.refs_0_.refs_3_, bf16[80,2944]{1,0:T(8,128)(2,1)S(1)} %collective-permute-done.12.refs_1_.refs_4_, ...), custom_call_target="tpu_custom_call" | custom-call | flops 482344960 | tf_op jit(solution)/shard_map/pallas_call | solution.py:497
  69.6 1.6 %collective-permute-start.23 = (bf16[40,2944]{1,0:T(8,128)(2,1)S(1)}, bf16[40,2944]{1,0:T(8,128)(2,1)S(1)}, u32[]{:S(2)}, u32[]{:S(2)}) collective-permute-start(bf16[40,2944]{1,0:T(8,128)(2,1)S(1)} %get-tuple-element.107), channel_id=1, source_target_pairs={{4,0},{8,4},{12,8},{14,12},{10,14},{6,10},{2,6},{0,2},{5,1},{9,5},... | collective-permute-start | bytes 706568 | tf_op jit(solution)/shard_map/ppermute | solution.py:367
  71.8 1.6 %collective-permute-done.2 = bf16[80,2944]{1,0:T(8,128)(2,1)S(1)} collective-permute-done((bf16[80,2944]{1,0:T(8,128)(2,1)S(1)}, bf16[80,2944]{1,0:T(8,128)(2,1)S(1)}, u32[]{:S(2)}, u32[]{:S(2)}) %collective-permute-start.2) | collective-permute-done | bytes 471072 | tf_op jit(solution)/shard_map/ppermute | solution.py:339
  73.4 4.4 %collective-permute-done.23 = bf16[40,2944]{1,0:T(8,128)(2,1)S(1)} collective-permute-done((bf16[40,2944]{1,0:T(8,128)(2,1)S(1)}, bf16[40,2944]{1,0:T(8,128)(2,1)S(1)}, u32[]{:S(2)}, u32[]{:S(2)}) %collective-permute-start.23) | collective-permute-done | bytes 235552 | tf_op jit(solution)/shard_map/ppermute | solution.py:367
  77.8 1.3 %collective-permute-done.22 = bf16[40,2944]{1,0:T(8,128)(2,1)S(1)} collective-permute-done((bf16[40,2944]{1,0:T(8,128)(2,1)S(1)}, bf16[40,2944]{1,0:T(8,128)(2,1)S(1)}, u32[]{:S(2)}, u32[]{:S(2)}) %collective-permute-start.22) | collective-permute-done | bytes 235552 | tf_op jit(solution)/shard_map/ppermute | solution.py:364
  79.2 0.5 collective-permute-start.24
  79.7 1.6 %collective-permute-start.26 = (f32[3,640]{1,0:T(4,128)S(1)}, f32[3,640]{1,0:T(4,128)S(1)}, u32[]{:S(2)}, u32[]{:S(2)}) collective-permute-start(f32[3,640]{1,0:T(4,128)S(1)} %fusion.5), channel_id=1, source_target_pairs={{0,16},{16,0},{1,17},{17,1},{2,18},{18,2},{3,19},{19,3},{4,20},{20... | collective-permute-start | bytes 23048 | tf_op jit(solution)/shard_map/ppermute | solution.py:388
  81.3 2.2 %collective-permute-done.26 = f32[3,640]{1,0:T(4,128)S(1)} collective-permute-done((f32[3,640]{1,0:T(4,128)S(1)}, f32[3,640]{1,0:T(4,128)S(1)}, u32[]{:S(2)}, u32[]{:S(2)}) %collective-permute-start.26) | collective-permute-done | bytes 7712 | tf_op jit(solution)/shard_map/ppermute | solution.py:388
  83.4 3.7 %shard_map.126 = bf16[16,32,640]{2,1,0:T(8,128)(2,1)} custom-call(s32[1]{0:T(128)} %bitcast.dev, bf16[3,34,32,640]{3,2,1,0:T(8,128)(2,1)S(1)} %get-tuple-element.91.acts, bf16[512,256]{1,0:T(8,128)(2,1)S(1)} %collective-permute-done.21.got, bf16[16,32,640]{2,1,0:T(8,128)(2,1)S(1)} %bitcast.15, f32[1,640]{1,0:T(1,128)S(1)} %copy-done.2, ...), custom_call_target="tpu_custom_call" | custom-call | flops 964689920 | tf_op jit(solution)/shard_map/pallas_call | solution.py:505
  87.2 1.6 %collective-permute-start.27 = (bf16[40,2944]{1,0:T(8,128)(2,1)S(1)}, bf16[40,2944]{1,0:T(8,128)(2,1)S(1)}, u32[]{:S(2)}, u32[]{:S(2)}) collective-permute-start(bf16[40,2944]{1,0:T(8,128)(2,1)S(1)} %add_convert_fusion), channel_id=1, source_target_pairs={{0,16},{16,0},{1,17},{17,1},{2,18},{18,2},{3,19},{19,3},{4,20},{20... | collective-permute-start | bytes 706568 | tf_op jit(solution)/shard_map/ppermute | solution.py:339
  88.8 0.9 collective-permute-start.29
  89.6 2.8 %collective-permute-done.29 = f32[3,640]{1,0:T(4,128)S(1)} collective-permute-done((f32[3,640]{1,0:T(4,128)S(1)}, f32[3,640]{1,0:T(4,128)S(1)}, u32[]{:S(2)}, u32[]{:S(2)}) %collective-permute-start.29) | collective-permute-done | bytes 7712 | tf_op jit(solution)/shard_map/ppermute | solution.py:388
  92.5 0.8 collective-permute-start.30
  93.9 2.2 %collective-permute-done.30 = f32[3,640]{1,0:T(4,128)S(1)} collective-permute-done((f32[3,640]{1,0:T(4,128)S(1)}, f32[3,640]{1,0:T(4,128)S(1)}, u32[]{:S(2)}, u32[]{:S(2)}) %collective-permute-start.30) | collective-permute-done | bytes 7712 | tf_op jit(solution)/shard_map/ppermute | solution.py:388
  96.1 1.9 %collective-permute-start.31 = (f32[3,640]{1,0:T(4,128)S(1)}, f32[3,640]{1,0:T(4,128)S(1)}, u32[]{:S(2)}, u32[]{:S(2)}) collective-permute-start(f32[3,640]{1,0:T(4,128)S(1)} %add.102), channel_id=1, source_target_pairs={{0,8},{4,12},{8,0},{12,4},{1,9},{5,13},{9,1},{13,5},{2,10},{6,14},... | collective-permute-start | bytes 23048 | tf_op jit(solution)/shard_map/ppermute | solution.py:388
  98.1 2.6 %collective-permute-done.31 = f32[3,640]{1,0:T(4,128)S(1)} collective-permute-done((f32[3,640]{1,0:T(4,128)S(1)}, f32[3,640]{1,0:T(4,128)S(1)}, u32[]{:S(2)}, u32[]{:S(2)}) %collective-permute-start.31) | collective-permute-done | bytes 7712 | tf_op jit(solution)/shard_map/ppermute | solution.py:388
  100.7 0.6 fusion.4
  101.3 1.2 %shard_map.127 = f32[40,5760]{1,0:T(8,128)} custom-call(s32[1]{0:T(128)} %bitcast.dev, s32[1]{0:T(128)S(6)} %copy.13.step, f32[40,5760]{1,0:T(8,128)S(1)} %bitcast.11, bf16[40,2944]{1,0:T(8,128)(2,1)S(1)} %collective-permute-done.7.mine, bf16[40,2944]{1,0:T(8,128)(2,1)S(1)} %collective-permute-done.8.theirs, bf16[40,2944]{1,0:T(8,128)(2,1)S(1)} %get-tuple-element.118.ours, ...), custom_call_target="tpu_custom_call" | custom-call | flops 241172480 | tf_op jit(solution)/shard_map/pallas_call | solution.py:564
  (57 shorter events, 2.9 us)
Async XLA Ops:
  0.6 4.0 %copy-start.1 = (bf16[1,16,32,640]{3,2,1,0:T(8,128)(2,1)S(1)}, bf16[1,16,32,640]{3,2,1,0:T(8,128)(2,1)}, u32[]{:S(2)}) copy-start(bf16[1,16,32,640]{3,2,1,0:T(8,128)(2,1)} %param.8) | copy-start | bytes 1966084
  0.7 9.3 %copy-start.3 = (f32[1,640]{1,0:T(1,128)S(1)}, f32[1,640]{1,0:T(1,128)}, u32[]{:S(2)}) copy-start(f32[1,640]{1,0:T(1,128)} %gain.3) | copy-start | bytes 7684
  0.7 9.3 %copy-start.4 = (f32[1,640]{1,0:T(1,128)S(1)}, f32[1,640]{1,0:T(1,128)}, u32[]{:S(2)}) copy-start(f32[1,640]{1,0:T(1,128)} %shift.3) | copy-start | bytes 7684
  0.7 9.3 %copy-start.5 = (s32[32,24]{1,0:T(8,128)S(1)}, s32[32,24]{1,0:T(8,128)}, u32[]{:S(2)}) copy-start(s32[32,24]{1,0:T(8,128)} %constant.40.clone.table) | copy-start | bytes 9220
  2.0 3.1 %collective-permute-start.4 = (bf16[40,2944]{1,0:T(8,128)(2,1)S(1)}, bf16[40,2944]{1,0:T(8,128)(2,1)S(1)}, u32[]{:S(2)}, u32[]{:S(2)}) collective-permute-start(bf16[40,2944]{1,0:T(8,128)(2,1)S(1)} %get-tuple-element.116), channel_id=1, source_target_pairs={{0,1},{1,0},{2,3},{3,2},{4,5},{5,4},{6,7},{7,6},{8,9},{9,8},{10,11... | collective-permute-start | bytes 706568 | tf_op jit(solution)/shard_map/ppermute | solution.py:339
  4.5 5.3 %collective-permute-start.1 = (bf16[16,32,640]{2,1,0:T(8,128)(2,1)S(1)}, bf16[16,32,640]{2,1,0:T(8,128)(2,1)S(1)}, u32[]{:S(2)}, u32[]{:S(2)}) collective-permute-start(bf16[16,32,640]{2,1,0:T(8,128)(2,1)S(1)} %get-tuple-element.114.cot_own), channel_id=1, source_target_pairs={{0,1},{1,0},{2,3},{3,2},{4,5},{5,4},{6,7},{7,6},{8,9},{9,8},{10,11... | collective-permute-start | bytes 1966088 | tf_op jit(solution)/shard_map/ppermute | solution.py:339
  4.6 5.4 %collective-permute-start = (bf16[16,32,640]{2,1,0:T(8,128)(2,1)S(1)}, bf16[16,32,640]{2,1,0:T(8,128)(2,1)S(1)}, u32[]{:S(2)}, u32[]{:S(2)}) collective-permute-start(bf16[16,32,640]{2,1,0:T(8,128)(2,1)S(1)} %bitcast.12), channel_id=1, source_target_pairs={{0,1},{1,0},{2,3},{3,2},{4,5},{5,4},{6,7},{7,6},{8,9},{9,8},{10,11... | collective-permute-start | bytes 1966088 | tf_op jit(solution)/shard_map/ppermute | solution.py:339
  5.1 15.6 %collective-permute-start.6 = (bf16[80,2944]{1,0:T(8,128)(2,1)S(1)}, bf16[80,2944]{1,0:T(8,128)(2,1)S(1)}, u32[]{:S(2)}, u32[]{:S(2)}) collective-permute-start(bf16[80,2944]{1,0:T(8,128)(2,1)S(1)} %maximum_select_fusion.refs_0_), channel_id=1, source_target_pairs={{4,0},{8,4},{12,8},{14,12},{10,14},{6,10},{2,6},{0,2},{5,1},{9,5},... | collective-permute-start | bytes 1413128 | tf_op jit(solution)/shard_map/ppermute | solution.py:367
  7.8 13.0 %collective-permute-start.5 = (bf16[80,2944]{1,0:T(8,128)(2,1)S(1)}, bf16[80,2944]{1,0:T(8,128)(2,1)S(1)}, u32[]{:S(2)}, u32[]{:S(2)}) collective-permute-start(bf16[80,2944]{1,0:T(8,128)(2,1)S(1)} %maximum_select_fusion.refs_0_), channel_id=1, source_target_pairs={{0,4},{4,8},{8,12},{12,14},{14,10},{10,6},{6,2},{2,0},{1,5},{5,9},... | collective-permute-start | bytes 1413128 | tf_op jit(solution)/shard_map/ppermute | solution.py:364
  7.9 11.1 %collective-permute-start.7 = (bf16[40,2944]{1,0:T(8,128)(2,1)S(1)}, bf16[40,2944]{1,0:T(8,128)(2,1)S(1)}, u32[]{:S(2)}, u32[]{:S(2)}) collective-permute-start(bf16[40,2944]{1,0:T(8,128)(2,1)S(1)} %get-tuple-element.115), channel_id=1, source_target_pairs={{0,16},{16,0},{1,17},{17,1},{2,18},{18,2},{3,19},{19,3},{4,20},{20... | collective-permute-start | bytes 706568 | tf_op jit(solution)/shard_map/ppermute | solution.py:339
  9.8 11.0 %collective-permute-start.8 = (bf16[40,2944]{1,0:T(8,128)(2,1)S(1)}, bf16[40,2944]{1,0:T(8,128)(2,1)S(1)}, u32[]{:S(2)}, u32[]{:S(2)}) collective-permute-start(bf16[40,2944]{1,0:T(8,128)(2,1)S(1)} %get-tuple-element.116), channel_id=1, source_target_pairs={{0,16},{16,0},{1,17},{17,1},{2,18},{18,2},{3,19},{19,3},{4,20},{20... | collective-permute-start | bytes 706568 | tf_op jit(solution)/shard_map/ppermute | solution.py:339
  20.8 12.0 %collective-permute-start.9 = (bf16[80,2944]{1,0:T(8,128)(2,1)S(1)}, bf16[80,2944]{1,0:T(8,128)(2,1)S(1)}, u32[]{:S(2)}, u32[]{:S(2)}) collective-permute-start(bf16[80,2944]{1,0:T(8,128)(2,1)S(1)} %collective-permute-done.5.refs_1_), channel_id=1, source_target_pairs={{0,4},{4,8},{8,12},{12,14},{14,10},{10,6},{6,2},{2,0},{1,5},{5,9},... | collective-permute-start | bytes 1413128 | tf_op jit(solution)/shard_map/ppermute | solution.py:364
  22.4 11.4 %collective-permute-start.10 = (bf16[80,2944]{1,0:T(8,128)(2,1)S(1)}, bf16[80,2944]{1,0:T(8,128)(2,1)S(1)}, u32[]{:S(2)}, u32[]{:S(2)}) collective-permute-start(bf16[80,2944]{1,0:T(8,128)(2,1)S(1)} %collective-permute-done.6.refs_2_), channel_id=1, source_target_pairs={{4,0},{8,4},{12,8},{14,12},{10,14},{6,10},{2,6},{0,2},{5,1},{9,5},... | collective-permute-start | bytes 1413128 | tf_op jit(solution)/shard_map/ppermute | solution.py:367
  22.8 17.1 %collective-permute-start.13 = (bf16[80,2944]{1,0:T(8,128)(2,1)S(1)}, bf16[80,2944]{1,0:T(8,128)(2,1)S(1)}, u32[]{:S(2)}, u32[]{:S(2)}) collective-permute-start(bf16[80,2944]{1,0:T(8,128)(2,1)S(1)} %get-tuple-element.75), channel_id=1, source_target_pairs={{0,16},{16,0},{1,17},{17,1},{2,18},{18,2},{3,19},{19,3},{4,20},{20... | collective-permute-start | bytes 1413128 | tf_op jit(solution)/shard_map/ppermute | solution.py:339
  24.4 30.1 %collective-permute-start.3 = (bf16[160,2944]{1,0:T(8,128)(2,1)S(1)}, bf16[160,2944]{1,0:T(8,128)(2,1)S(1)}, u32[]{:S(2)}, u32[]{:S(2)}) collective-permute-start(bf16[160,2944]{1,0:T(8,128)(2,1)S(1)} %get-tuple-element.61), channel_id=1, source_target_pairs={{0,16},{16,0},{1,17},{17,1},{2,18},{18,2},{3,19},{19,3},{4,20},{20... | collective-permute-start | bytes 2826248 | tf_op jit(solution)/shard_map/ppermute | solution.py:339
  33.9 13.0 %collective-permute-start.11 = (bf16[80,2944]{1,0:T(8,128)(2,1)S(1)}, bf16[80,2944]{1,0:T(8,128)(2,1)S(1)}, u32[]{:S(2)}, u32[]{:S(2)}) collective-permute-start(bf16[80,2944]{1,0:T(8,128)(2,1)S(1)} %collective-permute-done.9.refs_3_), channel_id=1, source_target_pairs={{0,4},{4,8},{8,12},{12,14},{14,10},{10,6},{6,2},{2,0},{1,5},{5,9},... | collective-permute-start | bytes 1413128 | tf_op jit(solution)/shard_map/ppermute | solution.py:364
  35.4 12.7 %collective-permute-start.12 = (bf16[80,2944]{1,0:T(8,128)(2,1)S(1)}, bf16[80,2944]{1,0:T(8,128)(2,1)S(1)}, u32[]{:S(2)}, u32[]{:S(2)}) collective-permute-start(bf16[80,2944]{1,0:T(8,128)(2,1)S(1)} %collective-permute-done.10.refs_4_), channel_id=1, source_target_pairs={{4,0},{8,4},{12,8},{14,12},{10,14},{6,10},{2,6},{0,2},{5,1},{9,5},... | collective-permute-start | bytes 1413128 | tf_op jit(solution)/shard_map/ppermute | solution.py:367
  40.0 16.6 %collective-permute-start.19 = (bf16[40,2944]{1,0:T(8,128)(2,1)S(1)}, bf16[40,2944]{1,0:T(8,128)(2,1)S(1)}, u32[]{:S(2)}, u32[]{:S(2)}) collective-permute-start(bf16[40,2944]{1,0:T(8,128)(2,1)S(1)} %get-tuple-element.111), channel_id=1, source_target_pairs={{4,0},{8,4},{12,8},{14,12},{10,14},{6,10},{2,6},{0,2},{5,1},{9,5},... | collective-permute-start | bytes 706568 | tf_op jit(solution)/shard_map/ppermute | solution.py:367
  40.7 15.8 %collective-permute-start.17 = (bf16[40,2944]{1,0:T(8,128)(2,1)S(1)}, bf16[40,2944]{1,0:T(8,128)(2,1)S(1)}, u32[]{:S(2)}, u32[]{:S(2)}) collective-permute-start(bf16[40,2944]{1,0:T(8,128)(2,1)S(1)} %get-tuple-element.112), channel_id=1, source_target_pairs={{0,4},{4,8},{8,12},{12,14},{14,10},{10,6},{6,2},{2,0},{1,5},{5,9},... | collective-permute-start | bytes 706568 | tf_op jit(solution)/shard_map/ppermute | solution.py:364
  48.2 16.4 %collective-permute-start.16 = (bf16[512,512]{1,0:T(8,128)(2,1)S(1)}, bf16[512,512]{1,0:T(8,128)(2,1)S(1)}, u32[]{:S(2)}, u32[]{:S(2)}) collective-permute-start(bf16[512,512]{1,0:T(8,128)(2,1)S(1)} %get-tuple-element.78), channel_id=1, source_target_pairs={{0,1},{1,0},{2,3},{3,2},{4,5},{5,4},{6,7},{7,6},{8,9},{9,8},{10,11... | collective-permute-start | bytes 1572872 | tf_op jit(solution)/shard_map/ppermute | solution.py:339
  54.5 8.7 %collective-permute-start.15 = (bf16[40,2944]{1,0:T(8,128)(2,1)S(1)}, bf16[40,2944]{1,0:T(8,128)(2,1)S(1)}, u32[]{:S(2)}, u32[]{:S(2)}) collective-permute-start(bf16[40,2944]{1,0:T(8,128)(2,1)S(1)} %slice.83), channel_id=1, source_target_pairs={{4,0},{8,4},{12,8},{14,12},{10,14},{6,10},{2,6},{0,2},{5,1},{9,5},... | collective-permute-start | bytes 706568 | tf_op jit(solution)/shard_map/ppermute | solution.py:367
  56.0 8.6 %collective-permute-start.14 = (bf16[40,2944]{1,0:T(8,128)(2,1)S(1)}, bf16[40,2944]{1,0:T(8,128)(2,1)S(1)}, u32[]{:S(2)}, u32[]{:S(2)}) collective-permute-start(bf16[40,2944]{1,0:T(8,128)(2,1)S(1)} %slice.82), channel_id=1, source_target_pairs={{0,4},{4,8},{8,12},{12,14},{14,10},{10,6},{6,2},{2,0},{1,5},{5,9},... | collective-permute-start | bytes 706568 | tf_op jit(solution)/shard_map/ppermute | solution.py:364
  56.8 11.0 %collective-permute-start.20 = (bf16[40,2944]{1,0:T(8,128)(2,1)S(1)}, bf16[40,2944]{1,0:T(8,128)(2,1)S(1)}, u32[]{:S(2)}, u32[]{:S(2)}) collective-permute-start(bf16[40,2944]{1,0:T(8,128)(2,1)S(1)} %get-tuple-element.109), channel_id=1, source_target_pairs={{4,0},{8,4},{12,8},{14,12},{10,14},{6,10},{2,6},{0,2},{5,1},{9,5},... | collective-permute-start | bytes 706568 | tf_op jit(solution)/shard_map/ppermute | solution.py:367
  58.2 9.6 %collective-permute-start.18 = (bf16[40,2944]{1,0:T(8,128)(2,1)S(1)}, bf16[40,2944]{1,0:T(8,128)(2,1)S(1)}, u32[]{:S(2)}, u32[]{:S(2)}) collective-permute-start(bf16[40,2944]{1,0:T(8,128)(2,1)S(1)} %get-tuple-element.110), channel_id=1, source_target_pairs={{0,4},{4,8},{8,12},{12,14},{14,10},{10,6},{6,2},{2,0},{1,5},{5,9},... | collective-permute-start | bytes 706568 | tf_op jit(solution)/shard_map/ppermute | solution.py:364
  63.2 10.2 %collective-permute-start.2 = (bf16[80,2944]{1,0:T(8,128)(2,1)S(1)}, bf16[80,2944]{1,0:T(8,128)(2,1)S(1)}, u32[]{:S(2)}, u32[]{:S(2)}) collective-permute-start(bf16[80,2944]{1,0:T(8,128)(2,1)S(1)} %get-tuple-element.60), channel_id=1, source_target_pairs={{0,16},{16,0},{1,17},{17,1},{2,18},{18,2},{3,19},{19,3},{4,20},{20... | collective-permute-start | bytes 1413128 | tf_op jit(solution)/shard_map/ppermute | solution.py:339
  69.3 2.4 %copy-start.2 = (f32[1,640]{1,0:T(1,128)S(1)}, f32[1,640]{1,0:T(1,128)}, u32[]{:S(2)}) copy-start(f32[1,640]{1,0:T(1,128)} %bias.1) | copy-start | bytes 7684
  69.3 9.8 %collective-permute-start.21 = (bf16[512,256]{1,0:T(8,128)(2,1)S(1)}, bf16[512,256]{1,0:T(8,128)(2,1)S(1)}, u32[]{:S(2)}, u32[]{:S(2)}) collective-permute-start(bf16[512,256]{1,0:T(8,128)(2,1)S(1)} %shard_map.125), channel_id=1, source_target_pairs={{0,1},{1,0},{2,3},{3,2},{4,5},{5,4},{6,7},{7,6},{8,9},{9,8},{10,11... | collective-permute-start | bytes 786440 | tf_op jit(solution)/shard_map/ppermute | solution.py:339
  69.6 8.2 %collective-permute-start.23 = (bf16[40,2944]{1,0:T(8,128)(2,1)S(1)}, bf16[40,2944]{1,0:T(8,128)(2,1)S(1)}, u32[]{:S(2)}, u32[]{:S(2)}) collective-permute-start(bf16[40,2944]{1,0:T(8,128)(2,1)S(1)} %get-tuple-element.107), channel_id=1, source_target_pairs={{4,0},{8,4},{12,8},{14,12},{10,14},{6,10},{2,6},{0,2},{5,1},{9,5},... | collective-permute-start | bytes 706568 | tf_op jit(solution)/shard_map/ppermute | solution.py:367
  71.2 7.9 %collective-permute-start.22 = (bf16[40,2944]{1,0:T(8,128)(2,1)S(1)}, bf16[40,2944]{1,0:T(8,128)(2,1)S(1)}, u32[]{:S(2)}, u32[]{:S(2)}) collective-permute-start(bf16[40,2944]{1,0:T(8,128)(2,1)S(1)} %get-tuple-element.108), channel_id=1, source_target_pairs={{0,4},{4,8},{8,12},{12,14},{14,10},{10,6},{6,2},{2,0},{1,5},{5,9},... | collective-permute-start | bytes 706568 | tf_op jit(solution)/shard_map/ppermute | solution.py:364
  71.7 8.0 %collective-permute-start.25 = (f32[3,640]{1,0:T(4,128)S(1)}, f32[3,640]{1,0:T(4,128)S(1)}, u32[]{:S(2)}, u32[]{:S(2)}) collective-permute-start(f32[3,640]{1,0:T(4,128)S(1)} %fusion.2), channel_id=1, source_target_pairs={{0,1},{1,0},{2,3},{3,2},{4,5},{5,4},{6,7},{7,6},{8,9},{9,8},{10,11... | collective-permute-start | bytes 23048 | tf_op jit(solution)/shard_map/ppermute | solution.py:339
  79.2 7.9 %collective-permute-start.24 = (bf16[40,2944]{1,0:T(8,128)(2,1)S(1)}, bf16[40,2944]{1,0:T(8,128)(2,1)S(1)}, u32[]{:S(2)}, u32[]{:S(2)}) collective-permute-start(bf16[40,2944]{1,0:T(8,128)(2,1)S(1)} %add_convert_fusion.1), channel_id=1, source_target_pairs={{0,4},{4,8},{8,12},{12,14},{14,10},{10,6},{6,2},{2,0},{1,5},{5,9},... | collective-permute-start | bytes 706568 | tf_op jit(solution)/shard_map/ppermute | solution.py:364
  79.7 3.7 %collective-permute-start.26 = (f32[3,640]{1,0:T(4,128)S(1)}, f32[3,640]{1,0:T(4,128)S(1)}, u32[]{:S(2)}, u32[]{:S(2)}) collective-permute-start(f32[3,640]{1,0:T(4,128)S(1)} %fusion.5), channel_id=1, source_target_pairs={{0,16},{16,0},{1,17},{17,1},{2,18},{18,2},{3,19},{19,3},{4,20},{20... | collective-permute-start | bytes 23048 | tf_op jit(solution)/shard_map/ppermute | solution.py:388
  87.1 14.2 %copy-start = (f32[1,40,5760]{2,1,0:T(8,128)S(1)}, f32[1,40,5760]{2,1,0:T(8,128)}, u32[]{:S(2)}) copy-start(f32[1,40,5760]{2,1,0:T(8,128)} %param.10) | copy-start | bytes 2764804
  87.2 10.8 %collective-permute-start.27 = (bf16[40,2944]{1,0:T(8,128)(2,1)S(1)}, bf16[40,2944]{1,0:T(8,128)(2,1)S(1)}, u32[]{:S(2)}, u32[]{:S(2)}) collective-permute-start(bf16[40,2944]{1,0:T(8,128)(2,1)S(1)} %add_convert_fusion), channel_id=1, source_target_pairs={{0,16},{16,0},{1,17},{17,1},{2,18},{18,2},{3,19},{19,3},{4,20},{20... | collective-permute-start | bytes 706568 | tf_op jit(solution)/shard_map/ppermute | solution.py:339
  88.8 3.7 %collective-permute-start.29 = (f32[3,640]{1,0:T(4,128)S(1)}, f32[3,640]{1,0:T(4,128)S(1)}, u32[]{:S(2)}, u32[]{:S(2)}) collective-permute-start(f32[3,640]{1,0:T(4,128)S(1)} %add.97), channel_id=1, source_target_pairs={{0,4},{4,0},{8,12},{12,8},{1,5},{5,1},{9,13},{13,9},{2,6},{6,2},{1... | collective-permute-start | bytes 23048 | tf_op jit(solution)/shard_map/ppermute | solution.py:388
  92.5 3.7 %collective-permute-start.30 = (f32[3,640]{1,0:T(4,128)S(1)}, f32[3,640]{1,0:T(4,128)S(1)}, u32[]{:S(2)}, u32[]{:S(2)}) collective-permute-start(f32[3,640]{1,0:T(4,128)S(1)} %add.101), channel_id=1, source_target_pairs={{0,2},{2,0},{1,3},{3,1},{4,6},{6,4},{5,7},{7,5},{8,10},{10,8},{9,1... | collective-permute-start | bytes 23048 | tf_op jit(solution)/shard_map/ppermute | solution.py:388
  96.1 4.6 %collective-permute-start.31 = (f32[3,640]{1,0:T(4,128)S(1)}, f32[3,640]{1,0:T(4,128)S(1)}, u32[]{:S(2)}, u32[]{:S(2)}) collective-permute-start(f32[3,640]{1,0:T(4,128)S(1)} %add.102), channel_id=1, source_target_pairs={{0,8},{4,12},{8,0},{12,4},{1,9},{5,13},{9,1},{13,5},{2,10},{6,14},... | collective-permute-start | bytes 23048 | tf_op jit(solution)/shard_map/ppermute | solution.py:388
  98.1 3.3 %collective-permute-start.28 = (bf16[40,2944]{1,0:T(8,128)(2,1)S(1)}, bf16[40,2944]{1,0:T(8,128)(2,1)S(1)}, u32[]{:S(2)}, u32[]{:S(2)}) collective-permute-start(bf16[40,2944]{1,0:T(8,128)(2,1)S(1)} %get-tuple-element.117), channel_id=1, source_target_pairs={{0,1},{1,0},{2,3},{3,2},{4,5},{5,4},{6,7},{7,6},{8,9},{9,8},{10,11... | collective-permute-start | bytes 706568 | tf_op jit(solution)/shard_map/ppermute | solution.py:339

commit v10 on v9

--- a/solution.py
+++ b/solution.py
@@ -454,7 +454,7 @@
         [pltpu.VMEM((chans, 2 * cells), F32)],
         8, flops // 4,
     )(dev, table, latent, lat_far, cot_b, cot_far, gn_gain, gn_shift)
-    counts = [zs, 1, zs - 2, 1] if paired else [2 * zs]
+    counts = [zs] + [1] * zs if paired else [2 * zs]
     pieces = call(
         partial(grad_kernel, cols),
         [jax.ShapeDtypeStruct((n * 2 * part, cols.lead), BF16) for n in counts],
@@ -517,14 +517,13 @@
         kept, *sent = pieces
         up, down, sent[0], mine, theirs = tied(up1, down1, sent[0], *peer)
         blocks = [unit, up, down]
-        first, middle, final = (swap(piece, "replica") for piece in sent)
+        crossed = [swap(piece, "replica") for piece in sent]
         up, down = ring.up(up), ring.down(down)
         up, down, cots, *slopes, order = tied(up, down, *slopes_of(stats))
         blocks += [up, down]
 
-        def ring_step(j, crossed, *received):
-            rows = slice(2 * j * part, (2 * j + 2) * part)
-            parts = kept[rows], crossed
+        def ring_step(j, *received):
+            parts = kept[2 * j * part:(2 * j + 2) * part], crossed[j]
             ahead, behind = (tuple(x[half] for x in parts) for half in (slice(part), slice(part, None)))
             up_sum = ring.up(add(*ahead, *received[:1]))
             if j < zs - 1:
@@ -533,29 +532,30 @@
 
         up, down = ring.up(up), ring.down(down)
         conv_first_own, conv_send = conv_first(blocks)
-        first, conv_send = tied(first, conv_send)
-        received = ring_step(0, first)
-        up, down, conv_send = tied(up, down, conv_send)
+        crossed[0], conv_send = tied(crossed[0], conv_send)
+        received = ring_step(0)
+        cots, conv_send = tied(cots, conv_send)
+        first_sums = back(0, cots, slopes, blocks)
+        up, down, first_sums, crossed[1] = tied(up, down, first_sums, crossed[1])
         late = [up, down]
 
         halves = ring.up(up[:part]), ring.down(down[part:])
+        conv_send, *received = tied(conv_send, *received)
         conv_first_got = swap(conv_send, "core")
-        cots, conv_send = tied(cots, conv_send)
-        middle, first_sums = tied(middle, back(0, cots, slopes, blocks))
         for j in range(1, zs - 2):
-            received = ring_step(j, middle[(2 * j - 2) * part:2 * j * part], *received)
-        *halves, conv_first_got = tied(*halves, conv_first_got)
+            received = ring_step(j, *received)
         late += halves
 
         sums = back(1, cots, slopes, late)
-        middle, sums, *received = tied(middle, sums, *received)
+        crossed[-2], sums, *received = tied(crossed[-2], sums, *received)
         acts_last, *_ = tied(acts, sums, *received)
-        received = ring_step(zs - 2, middle[(2 * zs - 6) * part:], *received)
+        received = ring_step(zs - 2, *received)
         conv_got = swap(conv_far(acts_last, late), "core")
         vectors = hop(chip_sum(first_sums + sums), "replica", 1)
-        final, conv_got, *received = tied(final, conv_got, *received)
-        last, behind = ring_step(zs - 1, final, *received)
+        crossed[-1], conv_got, vectors, *received = tied(crossed[-1], conv_got, vectors, *received)
+        last, behind = ring_step(zs - 1, *received)
         block = conv_own(conv_got, [conv_first_own, conv_first_got, order], late)
+        vectors = hop(vectors, "z", 1)
         last, block, vectors = tied(last, block, vectors)
         total = add(*behind, last)
         across = swap(total, "replica")
@@ -565,7 +565,6 @@
             partial(finish_kernel, cols), jax.ShapeDtypeStruct(shard.shape, F32),
             [SMEM_SPEC] * 2 + [VMEM_SPEC] * 5, [], 8, flops // 16,
         )(dev, step, shard, mine, theirs, ours, aside)
-        vectors = hop(vectors, "z", 1)
         vectors = hop(vectors, "y", 1)
         reach = 2
         while reach < zs:

time: 103 us -> 92.5 us (0.90)
  waiting for transfers between devices: 34.8 us -> 20.1 us
  starting transfers between devices: 29 us -> 33.5 us
    ppermute x7, waiting for transfers between devices: 11.1 us -> 4.63 us  [down(): return lax.ppermute(value, NODE, self.behind)]
    ppermute x4, waiting for transfers between devices: 9.8 us -> 5.57 us  [hop(): lax.ppermute(value, axis, [(s, s ^ mask) for s in range(count)])]
    ppermute x8, waiting for transfers between devices: 9.65 us -> 7.34 us  [up(): return lax.ppermute(value, NODE, self.ahead)]
    ppermute x8, starting transfers between devices: 6.85 us -> 9.16 us  [up(): return lax.ppermute(value, NODE, self.ahead)]
    ppermute x4, starting transfers between devices: 5.08 us -> 7 us  [hop(): lax.ppermute(value, axis, [(s, s ^ mask) for s in range(count)])]
    ppermute x13 -> x14, starting transfers between devices: 8.25 us -> 9.92 us  [swap(): return lax.ppermute(value, axis, [(0, 1), (1, 0)])]
    ppermute x13 -> x14, waiting for transfers between devices: 4.25 us -> 2.59 us  [swap(): return lax.ppermute(value, axis, [(0, 1), (1, 0)])]
    ppermute x7, starting transfers between devices: 8.79 us -> 7.41 us  [down(): return lax.ppermute(value, NODE, self.behind)]
  transfers between devices with their start and end apart: 32 -> 33, of which waited for: 15 -> 13; matrix products, arithmetic and copies ran while one was open for 3% -> 4% of each run, Pallas kernels for 30% -> 34%
where the time goes in v10:
time: 92.5 us; the launch traced here: 92.4 us
  starting transfers between devices  33.5 us (36%)
  Pallas kernels  32.4 us (35%)
  waiting for transfers between devices  20.1 us (22%)
  other arithmetic  2.88 us (3%)
  local copies, waits for them, and re-layouts  1.94 us (2%)
  between operations  1.55 us (2%)
    ppermute x14, starting transfers between devices, swap(): return lax.ppermute(value, axis, [(0, 1), (1, 0)])  9.92 us
    ppermute x8, starting transfers between devices, up(): return lax.ppermute(value, NODE, self.ahead)  9.16 us
    pallas_call x2, Pallas kernels, back(): call(partial(back_kernel, cols, stages, stage), jax.ShapeDtypeStruct((2,...  8.6 us
    ppermute x7, starting transfers between devices, down(): return lax.ppermute(value, NODE, self.behind)  7.41 us
    ppermute x8, waiting for transfers between devices, up(): return lax.ppermute(value, NODE, self.ahead)  7.34 us
    ppermute x4, starting transfers between devices, hop(): lax.ppermute(value, axis, [(s, s ^ mask) for s in range(count)])  7 us
    ppermute x4, waiting for transfers between devices, hop(): lax.ppermute(value, axis, [(s, s ^ mask) for s in range(count)])  5.57 us
    pallas_call x1, Pallas kernels, per_device(): call(partial(grad_kernel, cols), [jax.ShapeDtypeStruct((n * 2 * part, col...  4.64 us
  transfers between devices with their start and end apart: 33, of which 13 were waited for; matrix products, arithmetic and copies ran while one was open for 4% of the time, Pallas kernels for 34%

profile of v10, /device:TPU:0, one launch (start us, length us, event | category | flops | bytes accessed | tf_op | source)
XLA Modules:
  0.0 92.4 jit_solution(9101859017029833440)
XLA Ops:
  0.7 1.3 %fusion = (bf16[40,2944]{1,0:T(8,128)(2,1)S(1)}, bf16[40,2944]{1,0:T(8,128)(2,1)S(1)}) fusion(f32[1,40,5760]{2,1,0:T(8,128)} %param.10, s32[]{:T(128)S(6)} %select_n.27, s32[]{:T(128)S(6)} %select_n.28), kind=kLoop, calls=%fused_computation.12 | loop fusion | bytes 942088 | tf_op jit(solution)/shard_map/convert_element_type | solution.py:419
  2.0 0.5 collective-permute-start.4
  2.5 2.0 %fusion.3 = (f32[640]{0:T(1024)S(1)}, bf16[16,32,640]{2,1,0:T(8,128)(2,1)S(1)}) fusion(f32[1,16,32,640]{3,2,1,0:T(8,128)} %param.9), kind=kLoop, calls=%fused_computation.20 | loop fusion | flops 654720 | bytes 1968640 | tf_op jit(solution)/shard_map/reduce_sum | solution.py:512
  4.6 0.5 collective-permute-start
  5.1 2.7 %collective-permute-start.5 = (bf16[80,2944]{1,0:T(8,128)(2,1)S(1)}, bf16[80,2944]{1,0:T(8,128)(2,1)S(1)}, u32[]{:S(2)}, u32[]{:S(2)}) collective-permute-start(bf16[80,2944]{1,0:T(8,128)(2,1)S(1)} %maximum_select_fusion.refs_0_), channel_id=1, source_target_pairs={{0,4},{4,8},{8,12},{12,14},{14,10},{10,6},{6,2},{2,0},{1,5},{5,9},... | collective-permute-start | bytes 1413128 | tf_op jit(solution)/shard_map/ppermute | solution.py:364
  7.8 1.9 %collective-permute-start.7 = (bf16[40,2944]{1,0:T(8,128)(2,1)S(1)}, bf16[40,2944]{1,0:T(8,128)(2,1)S(1)}, u32[]{:S(2)}, u32[]{:S(2)}) collective-permute-start(bf16[40,2944]{1,0:T(8,128)(2,1)S(1)} %get-tuple-element.119), channel_id=1, source_target_pairs={{0,16},{16,0},{1,17},{17,1},{2,18},{18,2},{3,19},{19,3},{4,20},{20... | collective-permute-start | bytes 706568 | tf_op jit(solution)/shard_map/ppermute | solution.py:339
  9.9 4.4 %shard_map.119 = (f32[2,640]{1,0:T(2,128)S(1)}, bf16[3,34,32,640]{3,2,1,0:T(8,128)(2,1)S(1)}, bf16[640,1024]{1,0:T(8,128)(2,1)S(1)}) custom-call(s32[1]{0:T(128)} %bitcast.dev, s32[32,24]{1,0:T(8,128)S(1)} %copy-done.5, bf16[16,32,640]{2,1,0:T(8,128)(2,1)S(1)} %bitcast.13, bf16[16,32,640]{2,1,0:T(8,128)(2,1)S(1)} %collective-permute-done.lat_far, ...), custom_call_target="tpu_custom_call" | custom-call | flops 964689920 | tf_op jit(solution)/shard_map/pallas_call | solution.py:450
  14.3 4.6 %shard_map.120 = (bf16[320,2944]{1,0:T(8,128)(2,1)S(1)}, bf16[80,2944]{1,0:T(8,128)(2,1)S(1)}, bf16[80,2944]{1,0:T(8,128)(2,1)S(1)}, bf16[80,2944]{1,0:T(8,128)(2,1)S(1)}, bf16[80,2944]{1,0:T(8,128)(2,1)S(1)}) custom-call(s32[1]{0:T(128)} %bitcast.dev, bf16[3,34,32,640]{3,2,1,0:T(8,128)(2,1)S(1)} %get-tuple-element.94.acts, ...), custom_call_target="tpu_custom_call" | custom-call | flops 1929379840 | tf_op jit(solution)/shard_map/pallas_call | solution.py:458
  19.0 1.7 %collective-permute-done.8.theirs = bf16[40,2944]{1,0:T(8,128)(2,1)S(1)} collective-permute-done((bf16[40,2944]{1,0:T(8,128)(2,1)S(1)}, bf16[40,2944]{1,0:T(8,128)(2,1)S(1)}, u32[]{:S(2)}, u32[]{:S(2)}) %collective-permute-start.8) | collective-permute-done | bytes 235552 | tf_op jit(solution)/shard_map/ppermute | solution.py:339
  20.7 1.7 %collective-permute-start.10 = (bf16[80,2944]{1,0:T(8,128)(2,1)S(1)}, bf16[80,2944]{1,0:T(8,128)(2,1)S(1)}, u32[]{:S(2)}, u32[]{:S(2)}) collective-permute-start(bf16[80,2944]{1,0:T(8,128)(2,1)S(1)} %collective-permute-done.6.refs_2_), channel_id=1, source_target_pairs={{4,0},{8,4},{12,8},{14,12},{10,14},{6,10},{2,6},{0,2},{5,1},{9,5},... | collective-permute-start | bytes 1413128 | tf_op jit(solution)/shard_map/ppermute | solution.py:367
  22.7 1.7 %collective-permute-start.11 = (bf16[80,2944]{1,0:T(8,128)(2,1)S(1)}, bf16[80,2944]{1,0:T(8,128)(2,1)S(1)}, u32[]{:S(2)}, u32[]{:S(2)}) collective-permute-start(bf16[80,2944]{1,0:T(8,128)(2,1)S(1)} %get-tuple-element.75), channel_id=1, source_target_pairs={{0,16},{16,0},{1,17},{17,1},{2,18},{18,2},{3,19},{19,3},{4,20},{20... | collective-permute-start | bytes 1413128 | tf_op jit(solution)/shard_map/ppermute | solution.py:339
  24.7 4.5 %shard_map.121 = (bf16[3,34,32,768]{3,2,1,0:T(8,128)(2,1)S(1)}, bf16[32,32,640]{2,1,0:T(8,128)(2,1)S(1)}, bf16[32,32,640]{2,1,0:T(8,128)(2,1)S(1)}, bf16[640,768]{1,0:T(8,128)(2,1)S(1)}) custom-call(s32[1]{0:T(128)} %bitcast.dev, s32[32,24]{1,0:T(8,128)S(1)} %copy-done.5, f32[2,640]{1,0:T(2,128)S(1)} %get-tuple-element.69.stats, f32[1,640]{1,0:T(1,128)S(1)} %copy-done.3, ...), custom_call_target="tpu_custom_call" | custom-call | flops 964689920 | tf_op jit(solution)/shard_map/pallas_call | solution.py:470
  29.2 3.5 %collective-permute-done.10.refs_4_ = bf16[80,2944]{1,0:T(8,128)(2,1)S(1)} collective-permute-done((bf16[80,2944]{1,0:T(8,128)(2,1)S(1)}, bf16[80,2944]{1,0:T(8,128)(2,1)S(1)}, u32[]{:S(2)}, u32[]{:S(2)}) %collective-permute-start.10) | collective-permute-done | bytes 471072 | tf_op jit(solution)/shard_map/ppermute | solution.py:367
  32.7 1.1 %collective-permute-done.9.refs_3_ = bf16[80,2944]{1,0:T(8,128)(2,1)S(1)} collective-permute-done((bf16[80,2944]{1,0:T(8,128)(2,1)S(1)}, bf16[80,2944]{1,0:T(8,128)(2,1)S(1)}, u32[]{:S(2)}, u32[]{:S(2)}) %collective-permute-start.9) | collective-permute-done | bytes 471072 | tf_op jit(solution)/shard_map/ppermute | solution.py:364
  33.8 0.7 collective-permute-start.12
  34.5 1.4 %collective-permute-start.13 = (bf16[80,2944]{1,0:T(8,128)(2,1)S(1)}, bf16[80,2944]{1,0:T(8,128)(2,1)S(1)}, u32[]{:S(2)}, u32[]{:S(2)}) collective-permute-start(bf16[80,2944]{1,0:T(8,128)(2,1)S(1)} %collective-permute-done.10.refs_4_), channel_id=1, source_target_pairs={{4,0},{8,4},{12,8},{14,12},{10,14},{6,10},{2,6},{0,2},{5,1},{9,5},... | collective-permute-start | bytes 1413128 | tf_op jit(solution)/shard_map/ppermute | solution.py:367
  35.8 4.0 %shard_map.122 = (f32[512,512]{1,0:T(8,128)S(1)}, bf16[512,512]{1,0:T(8,128)(2,1)S(1)}) custom-call(s32[1]{0:T(128)} %bitcast.dev, bf16[3,34,32,640]{3,2,1,0:T(8,128)(2,1)S(1)} %get-tuple-element.94.acts, bf16[80,2944]{1,0:T(8,128)(2,1)S(1)} %maximum_select_fusion.refs_0_, bf16[80,2944]{1,0:T(8,128)(2,1)S(1)} %collective-permute-done.5.refs_1_, ...), custom_call_target="tpu_custom_call" | custom-call | flops 964689920 | tf_op jit(solution)/shard_map/pallas_call | solution.py:488
  39.9 0.7 collective-permute-start.17
  40.7 1.4 %collective-permute-start.18 = (bf16[40,2944]{1,0:T(8,128)(2,1)S(1)}, bf16[40,2944]{1,0:T(8,128)(2,1)S(1)}, u32[]{:S(2)}, u32[]{:S(2)}) collective-permute-start(bf16[40,2944]{1,0:T(8,128)(2,1)S(1)} %get-tuple-element.115), channel_id=1, source_target_pairs={{4,0},{8,4},{12,8},{14,12},{10,14},{6,10},{2,6},{0,2},{5,1},{9,5},... | collective-permute-start | bytes 706568 | tf_op jit(solution)/shard_map/ppermute | solution.py:367
  42.0 5.4 %shard_map.123 = f32[2,640]{1,0:T(2,128)S(1)} custom-call(s32[1]{0:T(128)} %bitcast.dev, bf16[3,34,32,768]{3,2,1,0:T(8,128)(2,1)S(1)} %get-tuple-element.80.cots, bf16[32,32,640]{2,1,0:T(8,128)(2,1)S(1)} %get-tuple-element.81.slope, bf16[32,32,640]{2,1,0:T(8,128)(2,1)S(1)} %get-tuple-element.82.slope_x, bf16[80,2944]{1,0:T(8,128)(2,1)S(1)} %maximum_select_fusion.refs_0_, ...), custom_call_target="tpu_custom_call" | custom-call | flops 964689920 | tf_op jit(solution)/shard_map/pallas_call | solution.py:480
  47.4 1.9 %collective-permute-done.17 = bf16[40,2944]{1,0:T(8,128)(2,1)S(1)} collective-permute-done((bf16[40,2944]{1,0:T(8,128)(2,1)S(1)}, bf16[40,2944]{1,0:T(8,128)(2,1)S(1)}, u32[]{:S(2)}, u32[]{:S(2)}) %collective-permute-start.17) | collective-permute-done | bytes 235552 | tf_op jit(solution)/shard_map/ppermute | solution.py:364
  49.3 1.5 %collective-permute-start.3 = (bf16[80,2944]{1,0:T(8,128)(2,1)S(1)}, bf16[80,2944]{1,0:T(8,128)(2,1)S(1)}, u32[]{:S(2)}, u32[]{:S(2)}) collective-permute-start(bf16[80,2944]{1,0:T(8,128)(2,1)S(1)} %get-tuple-element.63), channel_id=1, source_target_pairs={{0,16},{16,0},{1,17},{17,1},{2,18},{18,2},{3,19},{19,3},{4,20},{20... | collective-permute-start | bytes 1413128 | tf_op jit(solution)/shard_map/ppermute | solution.py:339
  50.9 0.9 %collective-permute-start.15 = (bf16[40,2944]{1,0:T(8,128)(2,1)S(1)}, bf16[40,2944]{1,0:T(8,128)(2,1)S(1)}, u32[]{:S(2)}, u32[]{:S(2)}) collective-permute-start(bf16[40,2944]{1,0:T(8,128)(2,1)S(1)} %slice.76), channel_id=1, source_target_pairs={{0,4},{4,8},{8,12},{12,14},{14,10},{10,6},{6,2},{2,0},{1,5},{5,9},... | collective-permute-start | bytes 706568 | tf_op jit(solution)/shard_map/ppermute | solution.py:364
  51.9 1.2 %collective-permute-start.16 = (bf16[40,2944]{1,0:T(8,128)(2,1)S(1)}, bf16[40,2944]{1,0:T(8,128)(2,1)S(1)}, u32[]{:S(2)}, u32[]{:S(2)}) collective-permute-start(bf16[40,2944]{1,0:T(8,128)(2,1)S(1)} %slice.77), channel_id=1, source_target_pairs={{4,0},{8,4},{12,8},{14,12},{10,14},{6,10},{2,6},{0,2},{5,1},{9,5},... | collective-permute-start | bytes 706568 | tf_op jit(solution)/shard_map/ppermute | solution.py:367
  53.2 0.9 %collective-permute-start.19 = (bf16[40,2944]{1,0:T(8,128)(2,1)S(1)}, bf16[40,2944]{1,0:T(8,128)(2,1)S(1)}, u32[]{:S(2)}, u32[]{:S(2)}) collective-permute-start(bf16[40,2944]{1,0:T(8,128)(2,1)S(1)} %get-tuple-element.114), channel_id=1, source_target_pairs={{0,4},{4,8},{8,12},{12,14},{14,10},{10,6},{6,2},{2,0},{1,5},{5,9},... | collective-permute-start | bytes 706568 | tf_op jit(solution)/shard_map/ppermute | solution.py:364
  54.2 1.1 %collective-permute-start.20 = (bf16[40,2944]{1,0:T(8,128)(2,1)S(1)}, bf16[40,2944]{1,0:T(8,128)(2,1)S(1)}, u32[]{:S(2)}, u32[]{:S(2)}) collective-permute-start(bf16[40,2944]{1,0:T(8,128)(2,1)S(1)} %get-tuple-element.113), channel_id=1, source_target_pairs={{4,0},{8,4},{12,8},{14,12},{10,14},{6,10},{2,6},{0,2},{5,1},{9,5},... | collective-permute-start | bytes 706568 | tf_op jit(solution)/shard_map/ppermute | solution.py:367
  55.3 2.4 %collective-permute-done.15.refs_2_.refs_5_ = bf16[40,2944]{1,0:T(8,128)(2,1)S(1)} collective-permute-done((bf16[40,2944]{1,0:T(8,128)(2,1)S(1)}, bf16[40,2944]{1,0:T(8,128)(2,1)S(1)}, u32[]{:S(2)}, u32[]{:S(2)}) %collective-permute-start.15) | collective-permute-done | bytes 235552 | tf_op jit(solution)/shard_map/ppermute | solution.py:364
  57.7 0.9 collective-permute-start.2
  58.7 3.2 %shard_map.124 = f32[2,640]{1,0:T(2,128)S(1)} custom-call(s32[1]{0:T(128)} %bitcast.dev, bf16[3,34,32,768]{3,2,1,0:T(8,128)(2,1)S(1)} %get-tuple-element.80.cots, bf16[32,32,640]{2,1,0:T(8,128)(2,1)S(1)} %get-tuple-element.81.slope, bf16[32,32,640]{2,1,0:T(8,128)(2,1)S(1)} %get-tuple-element.82.slope_x, ...), custom_call_target="tpu_custom_call" | custom-call | flops 964689920 | tf_op jit(solution)/shard_map/pallas_call | solution.py:480
  61.9 0.8 collective-permute-done.3
  62.8 1.4 %shard_map.125 = bf16[512,256]{1,0:T(8,128)(2,1)S(1)} custom-call(s32[1]{0:T(128)} %bitcast.dev, bf16[3,34,32,640]{3,2,1,0:T(8,128)(2,1)S(1)} %get-tuple-element.94.acts, bf16[80,2944]{1,0:T(8,128)(2,1)S(1)} %collective-permute-done.12.refs_0_.refs_3_, bf16[80,2944]{1,0:T(8,128)(2,1)S(1)} %collective-permute-done.13.refs_1_.refs_4_, ...), custom_call_target="tpu_custom_call" | custom-call | flops 482344960 | tf_op jit(solution)/shard_map/pallas_call | solution.py:497
  64.3 0.6 collective-permute-start.21
  65.0 1.4 %collective-permute-start.24 = (bf16[40,2944]{1,0:T(8,128)(2,1)S(1)}, bf16[40,2944]{1,0:T(8,128)(2,1)S(1)}, u32[]{:S(2)}, u32[]{:S(2)}) collective-permute-start(bf16[40,2944]{1,0:T(8,128)(2,1)S(1)} %get-tuple-element.112), channel_id=1, source_target_pairs={{0,4},{4,8},{8,12},{12,14},{14,10},{10,6},{6,2},{2,0},{1,5},{5,9},... | collective-permute-start | bytes 706568 | tf_op jit(solution)/shard_map/ppermute | solution.py:364
  66.4 0.7 collective-permute-start.25
  67.1 1.9 %collective-permute-start.23 = (f32[3,640]{1,0:T(4,128)S(1)}, f32[3,640]{1,0:T(4,128)S(1)}, u32[]{:S(2)}, u32[]{:S(2)}) collective-permute-start(f32[3,640]{1,0:T(4,128)S(1)} %fusion.5), channel_id=1, source_target_pairs={{0,16},{16,0},{1,17},{17,1},{2,18},{18,2},{3,19},{19,3},{4,20},{20... | collective-permute-start | bytes 23048 | tf_op jit(solution)/shard_map/ppermute | solution.py:388
  69.1 1.8 %collective-permute-done.23 = f32[3,640]{1,0:T(4,128)S(1)} collective-permute-done((f32[3,640]{1,0:T(4,128)S(1)}, f32[3,640]{1,0:T(4,128)S(1)}, u32[]{:S(2)}, u32[]{:S(2)}) %collective-permute-start.23) | collective-permute-done | bytes 7712 | tf_op jit(solution)/shard_map/ppermute | solution.py:388
  70.9 1.8 %collective-permute-done.24 = bf16[40,2944]{1,0:T(8,128)(2,1)S(1)} collective-permute-done((bf16[40,2944]{1,0:T(8,128)(2,1)S(1)}, bf16[40,2944]{1,0:T(8,128)(2,1)S(1)}, u32[]{:S(2)}, u32[]{:S(2)}) %collective-permute-start.24) | collective-permute-done | bytes 235552 | tf_op jit(solution)/shard_map/ppermute | solution.py:364
  72.7 1.1 %collective-permute-done.25 = bf16[40,2944]{1,0:T(8,128)(2,1)S(1)} collective-permute-done((bf16[40,2944]{1,0:T(8,128)(2,1)S(1)}, bf16[40,2944]{1,0:T(8,128)(2,1)S(1)}, u32[]{:S(2)}, u32[]{:S(2)}) %collective-permute-start.25) | collective-permute-done | bytes 235552 | tf_op jit(solution)/shard_map/ppermute | solution.py:367
  73.9 1.4 %collective-permute-start.26 = (bf16[40,2944]{1,0:T(8,128)(2,1)S(1)}, bf16[40,2944]{1,0:T(8,128)(2,1)S(1)}, u32[]{:S(2)}, u32[]{:S(2)}) collective-permute-start(bf16[40,2944]{1,0:T(8,128)(2,1)S(1)} %add_convert_fusion.1), channel_id=1, source_target_pairs={{0,4},{4,8},{8,12},{12,14},{14,10},{10,6},{6,2},{2,0},{1,5},{5,9},... | collective-permute-start | bytes 706568 | tf_op jit(solution)/shard_map/ppermute | solution.py:364
  75.3 1.4 %collective-permute-start.28 = (f32[3,640]{1,0:T(4,128)S(1)}, f32[3,640]{1,0:T(4,128)S(1)}, u32[]{:S(2)}, u32[]{:S(2)}) collective-permute-start(f32[3,640]{1,0:T(4,128)S(1)} %add.91), channel_id=1, source_target_pairs={{0,4},{4,0},{8,12},{12,8},{1,5},{5,1},{9,13},{13,9},{2,6},{6,2},{1... | collective-permute-start | bytes 23048 | tf_op jit(solution)/shard_map/ppermute | solution.py:388
  76.7 3.7 %shard_map.126 = bf16[16,32,640]{2,1,0:T(8,128)(2,1)} custom-call(s32[1]{0:T(128)} %bitcast.dev, bf16[3,34,32,640]{3,2,1,0:T(8,128)(2,1)S(1)} %get-tuple-element.94.acts, bf16[512,256]{1,0:T(8,128)(2,1)S(1)} %collective-permute-done.21.got, bf16[16,32,640]{2,1,0:T(8,128)(2,1)S(1)} %bitcast.15, f32[1,640]{1,0:T(1,128)S(1)} %copy-done.2, ...), custom_call_target="tpu_custom_call" | custom-call | flops 964689920 | tf_op jit(solution)/shard_map/pallas_call | solution.py:505
  80.6 1.7 %collective-permute-start.29 = (bf16[40,2944]{1,0:T(8,128)(2,1)S(1)}, bf16[40,2944]{1,0:T(8,128)(2,1)S(1)}, u32[]{:S(2)}, u32[]{:S(2)}) collective-permute-start(bf16[40,2944]{1,0:T(8,128)(2,1)S(1)} %add_convert_fusion), channel_id=1, source_target_pairs={{0,16},{16,0},{1,17},{17,1},{2,18},{18,2},{3,19},{19,3},{4,20},{20... | collective-permute-start | bytes 706568 | tf_op jit(solution)/shard_map/ppermute | solution.py:339
  82.3 1.4 %collective-permute-start.31 = (f32[3,640]{1,0:T(4,128)S(1)}, f32[3,640]{1,0:T(4,128)S(1)}, u32[]{:S(2)}, u32[]{:S(2)}) collective-permute-start(f32[3,640]{1,0:T(4,128)S(1)} %add.98), channel_id=1, source_target_pairs={{0,2},{2,0},{1,3},{3,1},{4,6},{6,4},{5,7},{7,5},{8,10},{10,8},{9,1... | collective-permute-start | bytes 23048 | tf_op jit(solution)/shard_map/ppermute | solution.py:388
  84.3 1.6 %collective-permute-done.31 = f32[3,640]{1,0:T(4,128)S(1)} collective-permute-done((f32[3,640]{1,0:T(4,128)S(1)}, f32[3,640]{1,0:T(4,128)S(1)}, u32[]{:S(2)}, u32[]{:S(2)}) %collective-permute-start.31) | collective-permute-done | bytes 7712 | tf_op jit(solution)/shard_map/ppermute | solution.py:388
  86.0 2.4 %collective-permute-start.32 = (f32[3,640]{1,0:T(4,128)S(1)}, f32[3,640]{1,0:T(4,128)S(1)}, u32[]{:S(2)}, u32[]{:S(2)}) collective-permute-start(f32[3,640]{1,0:T(4,128)S(1)} %add.102), channel_id=1, source_target_pairs={{0,8},{4,12},{8,0},{12,4},{1,9},{5,13},{9,1},{13,5},{2,10},{6,14},... | collective-permute-start | bytes 23048 | tf_op jit(solution)/shard_map/ppermute | solution.py:388
  88.5 2.1 %collective-permute-done.32 = f32[3,640]{1,0:T(4,128)S(1)} collective-permute-done((f32[3,640]{1,0:T(4,128)S(1)}, f32[3,640]{1,0:T(4,128)S(1)}, u32[]{:S(2)}, u32[]{:S(2)}) %collective-permute-start.32) | collective-permute-done | bytes 7712 | tf_op jit(solution)/shard_map/ppermute | solution.py:388
  90.6 0.6 fusion.4
  91.2 1.2 %shard_map.127 = f32[40,5760]{1,0:T(8,128)} custom-call(s32[1]{0:T(128)} %bitcast.dev, s32[1]{0:T(128)S(6)} %copy.13.step, f32[40,5760]{1,0:T(8,128)S(1)} %bitcast.11, bf16[40,2944]{1,0:T(8,128)(2,1)S(1)} %collective-permute-done.7.mine, bf16[40,2944]{1,0:T(8,128)(2,1)S(1)} %collective-permute-done.8.theirs, bf16[40,2944]{1,0:T(8,128)(2,1)S(1)} %get-tuple-element.122.ours, ...), custom_call_target="tpu_custom_call" | custom-call | flops 241172480 | tf_op jit(solution)/shard_map/pallas_call | solution.py:564
  (59 shorter events, 2.3 us)
Async XLA Ops:
  0.6 3.9 %copy-start.1 = (bf16[1,16,32,640]{3,2,1,0:T(8,128)(2,1)S(1)}, bf16[1,16,32,640]{3,2,1,0:T(8,128)(2,1)}, u32[]{:S(2)}) copy-start(bf16[1,16,32,640]{3,2,1,0:T(8,128)(2,1)} %param.8) | copy-start | bytes 1966084
  0.7 9.2 %copy-start.3 = (f32[1,640]{1,0:T(1,128)S(1)}, f32[1,640]{1,0:T(1,128)}, u32[]{:S(2)}) copy-start(f32[1,640]{1,0:T(1,128)} %gain.3) | copy-start | bytes 7684
  0.7 9.2 %copy-start.4 = (f32[1,640]{1,0:T(1,128)S(1)}, f32[1,640]{1,0:T(1,128)}, u32[]{:S(2)}) copy-start(f32[1,640]{1,0:T(1,128)} %shift.3) | copy-start | bytes 7684
  0.7 9.2 %copy-start.5 = (s32[32,24]{1,0:T(8,128)S(1)}, s32[32,24]{1,0:T(8,128)}, u32[]{:S(2)}) copy-start(s32[32,24]{1,0:T(8,128)} %constant.40.clone.table) | copy-start | bytes 9220
  2.0 3.1 %collective-permute-start.4 = (bf16[40,2944]{1,0:T(8,128)(2,1)S(1)}, bf16[40,2944]{1,0:T(8,128)(2,1)S(1)}, u32[]{:S(2)}, u32[]{:S(2)}) collective-permute-start(bf16[40,2944]{1,0:T(8,128)(2,1)S(1)} %get-tuple-element.120), channel_id=1, source_target_pairs={{0,1},{1,0},{2,3},{3,2},{4,5},{5,4},{6,7},{7,6},{8,9},{9,8},{10,11... | collective-permute-start | bytes 706568 | tf_op jit(solution)/shard_map/ppermute | solution.py:339
  4.5 5.3 %collective-permute-start.1 = (bf16[16,32,640]{2,1,0:T(8,128)(2,1)S(1)}, bf16[16,32,640]{2,1,0:T(8,128)(2,1)S(1)}, u32[]{:S(2)}, u32[]{:S(2)}) collective-permute-start(bf16[16,32,640]{2,1,0:T(8,128)(2,1)S(1)} %get-tuple-element.118.cot_own), channel_id=1, source_target_pairs={{0,1},{1,0},{2,3},{3,2},{4,5},{5,4},{6,7},{7,6},{8,9},{9,8},{10,11... | collective-permute-start | bytes 1966088 | tf_op jit(solution)/shard_map/ppermute | solution.py:339
  4.6 5.3 %collective-permute-start = (bf16[16,32,640]{2,1,0:T(8,128)(2,1)S(1)}, bf16[16,32,640]{2,1,0:T(8,128)(2,1)S(1)}, u32[]{:S(2)}, u32[]{:S(2)}) collective-permute-start(bf16[16,32,640]{2,1,0:T(8,128)(2,1)S(1)} %bitcast.12), channel_id=1, source_target_pairs={{0,1},{1,0},{2,3},{3,2},{4,5},{5,4},{6,7},{7,6},{8,9},{9,8},{10,11... | collective-permute-start | bytes 1966088 | tf_op jit(solution)/shard_map/ppermute | solution.py:339
  5.1 15.6 %collective-permute-start.5 = (bf16[80,2944]{1,0:T(8,128)(2,1)S(1)}, bf16[80,2944]{1,0:T(8,128)(2,1)S(1)}, u32[]{:S(2)}, u32[]{:S(2)}) collective-permute-start(bf16[80,2944]{1,0:T(8,128)(2,1)S(1)} %maximum_select_fusion.refs_0_), channel_id=1, source_target_pairs={{0,4},{4,8},{8,12},{12,14},{14,10},{10,6},{6,2},{2,0},{1,5},{5,9},... | collective-permute-start | bytes 1413128 | tf_op jit(solution)/shard_map/ppermute | solution.py:364
  7.8 12.9 %collective-permute-start.6 = (bf16[80,2944]{1,0:T(8,128)(2,1)S(1)}, bf16[80,2944]{1,0:T(8,128)(2,1)S(1)}, u32[]{:S(2)}, u32[]{:S(2)}) collective-permute-start(bf16[80,2944]{1,0:T(8,128)(2,1)S(1)} %maximum_select_fusion.refs_0_), channel_id=1, source_target_pairs={{4,0},{8,4},{12,8},{14,12},{10,14},{6,10},{2,6},{0,2},{5,1},{9,5},... | collective-permute-start | bytes 1413128 | tf_op jit(solution)/shard_map/ppermute | solution.py:367
  7.8 11.1 %collective-permute-start.7 = (bf16[40,2944]{1,0:T(8,128)(2,1)S(1)}, bf16[40,2944]{1,0:T(8,128)(2,1)S(1)}, u32[]{:S(2)}, u32[]{:S(2)}) collective-permute-start(bf16[40,2944]{1,0:T(8,128)(2,1)S(1)} %get-tuple-element.119), channel_id=1, source_target_pairs={{0,16},{16,0},{1,17},{17,1},{2,18},{18,2},{3,19},{19,3},{4,20},{20... | collective-permute-start | bytes 706568 | tf_op jit(solution)/shard_map/ppermute | solution.py:339
  9.8 10.9 %collective-permute-start.8 = (bf16[40,2944]{1,0:T(8,128)(2,1)S(1)}, bf16[40,2944]{1,0:T(8,128)(2,1)S(1)}, u32[]{:S(2)}, u32[]{:S(2)}) collective-permute-start(bf16[40,2944]{1,0:T(8,128)(2,1)S(1)} %get-tuple-element.120), channel_id=1, source_target_pairs={{0,16},{16,0},{1,17},{17,1},{2,18},{18,2},{3,19},{19,3},{4,20},{20... | collective-permute-start | bytes 706568 | tf_op jit(solution)/shard_map/ppermute | solution.py:339
  20.7 12.0 %collective-permute-start.10 = (bf16[80,2944]{1,0:T(8,128)(2,1)S(1)}, bf16[80,2944]{1,0:T(8,128)(2,1)S(1)}, u32[]{:S(2)}, u32[]{:S(2)}) collective-permute-start(bf16[80,2944]{1,0:T(8,128)(2,1)S(1)} %collective-permute-done.6.refs_2_), channel_id=1, source_target_pairs={{4,0},{8,4},{12,8},{14,12},{10,14},{6,10},{2,6},{0,2},{5,1},{9,5},... | collective-permute-start | bytes 1413128 | tf_op jit(solution)/shard_map/ppermute | solution.py:367
  22.4 11.4 %collective-permute-start.9 = (bf16[80,2944]{1,0:T(8,128)(2,1)S(1)}, bf16[80,2944]{1,0:T(8,128)(2,1)S(1)}, u32[]{:S(2)}, u32[]{:S(2)}) collective-permute-start(bf16[80,2944]{1,0:T(8,128)(2,1)S(1)} %collective-permute-done.5.refs_1_), channel_id=1, source_target_pairs={{0,4},{4,8},{8,12},{12,14},{14,10},{10,6},{6,2},{2,0},{1,5},{5,9},... | collective-permute-start | bytes 1413128 | tf_op jit(solution)/shard_map/ppermute | solution.py:364
  22.7 17.1 %collective-permute-start.11 = (bf16[80,2944]{1,0:T(8,128)(2,1)S(1)}, bf16[80,2944]{1,0:T(8,128)(2,1)S(1)}, u32[]{:S(2)}, u32[]{:S(2)}) collective-permute-start(bf16[80,2944]{1,0:T(8,128)(2,1)S(1)} %get-tuple-element.75), channel_id=1, source_target_pairs={{0,16},{16,0},{1,17},{17,1},{2,18},{18,2},{3,19},{19,3},{4,20},{20... | collective-permute-start | bytes 1413128 | tf_op jit(solution)/shard_map/ppermute | solution.py:339
  24.4 26.5 %collective-permute-start.14 = (bf16[80,2944]{1,0:T(8,128)(2,1)S(1)}, bf16[80,2944]{1,0:T(8,128)(2,1)S(1)}, u32[]{:S(2)}, u32[]{:S(2)}) collective-permute-start(bf16[80,2944]{1,0:T(8,128)(2,1)S(1)} %get-tuple-element.83), channel_id=1, source_target_pairs={{0,16},{16,0},{1,17},{17,1},{2,18},{18,2},{3,19},{19,3},{4,20},{20... | collective-permute-start | bytes 1413128 | tf_op jit(solution)/shard_map/ppermute | solution.py:339
  33.8 17.0 %collective-permute-start.12 = (bf16[80,2944]{1,0:T(8,128)(2,1)S(1)}, bf16[80,2944]{1,0:T(8,128)(2,1)S(1)}, u32[]{:S(2)}, u32[]{:S(2)}) collective-permute-start(bf16[80,2944]{1,0:T(8,128)(2,1)S(1)} %collective-permute-done.9.refs_3_), channel_id=1, source_target_pairs={{0,4},{4,8},{8,12},{12,14},{14,10},{10,6},{6,2},{2,0},{1,5},{5,9},... | collective-permute-start | bytes 1413128 | tf_op jit(solution)/shard_map/ppermute | solution.py:364
  34.5 16.4 %collective-permute-start.13 = (bf16[80,2944]{1,0:T(8,128)(2,1)S(1)}, bf16[80,2944]{1,0:T(8,128)(2,1)S(1)}, u32[]{:S(2)}, u32[]{:S(2)}) collective-permute-start(bf16[80,2944]{1,0:T(8,128)(2,1)S(1)} %collective-permute-done.10.refs_4_), channel_id=1, source_target_pairs={{4,0},{8,4},{12,8},{14,12},{10,14},{6,10},{2,6},{0,2},{5,1},{9,5},... | collective-permute-start | bytes 1413128 | tf_op jit(solution)/shard_map/ppermute | solution.py:367
  39.9 9.4 %collective-permute-start.17 = (bf16[40,2944]{1,0:T(8,128)(2,1)S(1)}, bf16[40,2944]{1,0:T(8,128)(2,1)S(1)}, u32[]{:S(2)}, u32[]{:S(2)}) collective-permute-start(bf16[40,2944]{1,0:T(8,128)(2,1)S(1)} %get-tuple-element.116), channel_id=1, source_target_pairs={{0,4},{4,8},{8,12},{12,14},{14,10},{10,6},{6,2},{2,0},{1,5},{5,9},... | collective-permute-start | bytes 706568 | tf_op jit(solution)/shard_map/ppermute | solution.py:364
  40.7 10.2 %collective-permute-start.18 = (bf16[40,2944]{1,0:T(8,128)(2,1)S(1)}, bf16[40,2944]{1,0:T(8,128)(2,1)S(1)}, u32[]{:S(2)}, u32[]{:S(2)}) collective-permute-start(bf16[40,2944]{1,0:T(8,128)(2,1)S(1)} %get-tuple-element.115), channel_id=1, source_target_pairs={{4,0},{8,4},{12,8},{14,12},{10,14},{6,10},{2,6},{0,2},{5,1},{9,5},... | collective-permute-start | bytes 706568 | tf_op jit(solution)/shard_map/ppermute | solution.py:367
  49.3 13.4 %collective-permute-start.3 = (bf16[80,2944]{1,0:T(8,128)(2,1)S(1)}, bf16[80,2944]{1,0:T(8,128)(2,1)S(1)}, u32[]{:S(2)}, u32[]{:S(2)}) collective-permute-start(bf16[80,2944]{1,0:T(8,128)(2,1)S(1)} %get-tuple-element.63), channel_id=1, source_target_pairs={{0,16},{16,0},{1,17},{17,1},{2,18},{18,2},{3,19},{19,3},{4,20},{20... | collective-permute-start | bytes 1413128 | tf_op jit(solution)/shard_map/ppermute | solution.py:339
  50.9 6.8 %collective-permute-start.15 = (bf16[40,2944]{1,0:T(8,128)(2,1)S(1)}, bf16[40,2944]{1,0:T(8,128)(2,1)S(1)}, u32[]{:S(2)}, u32[]{:S(2)}) collective-permute-start(bf16[40,2944]{1,0:T(8,128)(2,1)S(1)} %slice.76), channel_id=1, source_target_pairs={{0,4},{4,8},{8,12},{12,14},{14,10},{10,6},{6,2},{2,0},{1,5},{5,9},... | collective-permute-start | bytes 706568 | tf_op jit(solution)/shard_map/ppermute | solution.py:364
  51.9 6.8 %collective-permute-start.16 = (bf16[40,2944]{1,0:T(8,128)(2,1)S(1)}, bf16[40,2944]{1,0:T(8,128)(2,1)S(1)}, u32[]{:S(2)}, u32[]{:S(2)}) collective-permute-start(bf16[40,2944]{1,0:T(8,128)(2,1)S(1)} %slice.77), channel_id=1, source_target_pairs={{4,0},{8,4},{12,8},{14,12},{10,14},{6,10},{2,6},{0,2},{5,1},{9,5},... | collective-permute-start | bytes 706568 | tf_op jit(solution)/shard_map/ppermute | solution.py:367
  53.2 9.5 %collective-permute-start.19 = (bf16[40,2944]{1,0:T(8,128)(2,1)S(1)}, bf16[40,2944]{1,0:T(8,128)(2,1)S(1)}, u32[]{:S(2)}, u32[]{:S(2)}) collective-permute-start(bf16[40,2944]{1,0:T(8,128)(2,1)S(1)} %get-tuple-element.114), channel_id=1, source_target_pairs={{0,4},{4,8},{8,12},{12,14},{14,10},{10,6},{6,2},{2,0},{1,5},{5,9},... | collective-permute-start | bytes 706568 | tf_op jit(solution)/shard_map/ppermute | solution.py:364
  54.2 8.5 %collective-permute-start.20 = (bf16[40,2944]{1,0:T(8,128)(2,1)S(1)}, bf16[40,2944]{1,0:T(8,128)(2,1)S(1)}, u32[]{:S(2)}, u32[]{:S(2)}) collective-permute-start(bf16[40,2944]{1,0:T(8,128)(2,1)S(1)} %get-tuple-element.113), channel_id=1, source_target_pairs={{4,0},{8,4},{12,8},{14,12},{10,14},{6,10},{2,6},{0,2},{5,1},{9,5},... | collective-permute-start | bytes 706568 | tf_op jit(solution)/shard_map/ppermute | solution.py:367
  57.7 5.0 %copy-start.2 = (f32[1,640]{1,0:T(1,128)S(1)}, f32[1,640]{1,0:T(1,128)}, u32[]{:S(2)}) copy-start(f32[1,640]{1,0:T(1,128)} %bias.1) | copy-start | bytes 7684
  57.7 13.2 %collective-permute-start.2 = (bf16[80,2944]{1,0:T(8,128)(2,1)S(1)}, bf16[80,2944]{1,0:T(8,128)(2,1)S(1)}, u32[]{:S(2)}, u32[]{:S(2)}) collective-permute-start(bf16[80,2944]{1,0:T(8,128)(2,1)S(1)} %get-tuple-element.62), channel_id=1, source_target_pairs={{0,16},{16,0},{1,17},{17,1},{2,18},{18,2},{3,19},{19,3},{4,20},{20... | collective-permute-start | bytes 1413128 | tf_op jit(solution)/shard_map/ppermute | solution.py:339
  62.7 4.4 %collective-permute-start.22 = (f32[3,640]{1,0:T(4,128)S(1)}, f32[3,640]{1,0:T(4,128)S(1)}, u32[]{:S(2)}, u32[]{:S(2)}) collective-permute-start(f32[3,640]{1,0:T(4,128)S(1)} %fusion.2), channel_id=1, source_target_pairs={{0,1},{1,0},{2,3},{3,2},{4,5},{5,4},{6,7},{7,6},{8,9},{9,8},{10,11... | collective-permute-start | bytes 23048 | tf_op jit(solution)/shard_map/ppermute | solution.py:339
  64.3 9.5 %collective-permute-start.21 = (bf16[512,256]{1,0:T(8,128)(2,1)S(1)}, bf16[512,256]{1,0:T(8,128)(2,1)S(1)}, u32[]{:S(2)}, u32[]{:S(2)}) collective-permute-start(bf16[512,256]{1,0:T(8,128)(2,1)S(1)} %shard_map.125), channel_id=1, source_target_pairs={{0,1},{1,0},{2,3},{3,2},{4,5},{5,4},{6,7},{7,6},{8,9},{9,8},{10,11... | collective-permute-start | bytes 786440 | tf_op jit(solution)/shard_map/ppermute | solution.py:339
  65.0 7.7 %collective-permute-start.24 = (bf16[40,2944]{1,0:T(8,128)(2,1)S(1)}, bf16[40,2944]{1,0:T(8,128)(2,1)S(1)}, u32[]{:S(2)}, u32[]{:S(2)}) collective-permute-start(bf16[40,2944]{1,0:T(8,128)(2,1)S(1)} %get-tuple-element.112), channel_id=1, source_target_pairs={{0,4},{4,8},{8,12},{12,14},{14,10},{10,6},{6,2},{2,0},{1,5},{5,9},... | collective-permute-start | bytes 706568 | tf_op jit(solution)/shard_map/ppermute | solution.py:364
  66.4 7.4 %collective-permute-start.25 = (bf16[40,2944]{1,0:T(8,128)(2,1)S(1)}, bf16[40,2944]{1,0:T(8,128)(2,1)S(1)}, u32[]{:S(2)}, u32[]{:S(2)}) collective-permute-start(bf16[40,2944]{1,0:T(8,128)(2,1)S(1)} %get-tuple-element.111), channel_id=1, source_target_pairs={{4,0},{8,4},{12,8},{14,12},{10,14},{6,10},{2,6},{0,2},{5,1},{9,5},... | collective-permute-start | bytes 706568 | tf_op jit(solution)/shard_map/ppermute | solution.py:367
  67.1 3.7 %collective-permute-start.23 = (f32[3,640]{1,0:T(4,128)S(1)}, f32[3,640]{1,0:T(4,128)S(1)}, u32[]{:S(2)}, u32[]{:S(2)}) collective-permute-start(f32[3,640]{1,0:T(4,128)S(1)} %fusion.5), channel_id=1, source_target_pairs={{0,16},{16,0},{1,17},{17,1},{2,18},{18,2},{3,19},{19,3},{4,20},{20... | collective-permute-start | bytes 23048 | tf_op jit(solution)/shard_map/ppermute | solution.py:388
  70.9 5.8 %collective-permute-start.27 = (bf16[512,512]{1,0:T(8,128)(2,1)S(1)}, bf16[512,512]{1,0:T(8,128)(2,1)S(1)}, u32[]{:S(2)}, u32[]{:S(2)}) collective-permute-start(bf16[512,512]{1,0:T(8,128)(2,1)S(1)} %get-tuple-element.101), channel_id=1, source_target_pairs={{0,1},{1,0},{2,3},{3,2},{4,5},{5,4},{6,7},{7,6},{8,9},{9,8},{10,11... | collective-permute-start | bytes 1572872 | tf_op jit(solution)/shard_map/ppermute | solution.py:339
  73.9 6.5 %collective-permute-start.26 = (bf16[40,2944]{1,0:T(8,128)(2,1)S(1)}, bf16[40,2944]{1,0:T(8,128)(2,1)S(1)}, u32[]{:S(2)}, u32[]{:S(2)}) collective-permute-start(bf16[40,2944]{1,0:T(8,128)(2,1)S(1)} %add_convert_fusion.1), channel_id=1, source_target_pairs={{0,4},{4,8},{8,12},{12,14},{14,10},{10,6},{6,2},{2,0},{1,5},{5,9},... | collective-permute-start | bytes 706568 | tf_op jit(solution)/shard_map/ppermute | solution.py:364
  75.3 5.0 %collective-permute-start.28 = (f32[3,640]{1,0:T(4,128)S(1)}, f32[3,640]{1,0:T(4,128)S(1)}, u32[]{:S(2)}, u32[]{:S(2)}) collective-permute-start(f32[3,640]{1,0:T(4,128)S(1)} %add.91), channel_id=1, source_target_pairs={{0,4},{4,0},{8,12},{12,8},{1,5},{5,1},{9,13},{13,9},{2,6},{6,2},{1... | collective-permute-start | bytes 23048 | tf_op jit(solution)/shard_map/ppermute | solution.py:388
  80.3 10.8 %copy-start = (f32[1,40,5760]{2,1,0:T(8,128)S(1)}, f32[1,40,5760]{2,1,0:T(8,128)}, u32[]{:S(2)}) copy-start(f32[1,40,5760]{2,1,0:T(8,128)} %param.10) | copy-start | bytes 2764804
  80.6 7.8 %collective-permute-start.29 = (bf16[40,2944]{1,0:T(8,128)(2,1)S(1)}, bf16[40,2944]{1,0:T(8,128)(2,1)S(1)}, u32[]{:S(2)}, u32[]{:S(2)}) collective-permute-start(bf16[40,2944]{1,0:T(8,128)(2,1)S(1)} %add_convert_fusion), channel_id=1, source_target_pairs={{0,16},{16,0},{1,17},{17,1},{2,18},{18,2},{3,19},{19,3},{4,20},{20... | collective-permute-start | bytes 706568 | tf_op jit(solution)/shard_map/ppermute | solution.py:339
  82.3 3.7 %collective-permute-start.31 = (f32[3,640]{1,0:T(4,128)S(1)}, f32[3,640]{1,0:T(4,128)S(1)}, u32[]{:S(2)}, u32[]{:S(2)}) collective-permute-start(f32[3,640]{1,0:T(4,128)S(1)} %add.98), channel_id=1, source_target_pairs={{0,2},{2,0},{1,3},{3,1},{4,6},{6,4},{5,7},{7,5},{8,10},{10,8},{9,1... | collective-permute-start | bytes 23048 | tf_op jit(solution)/shard_map/ppermute | solution.py:388
  86.0 4.6 %collective-permute-start.32 = (f32[3,640]{1,0:T(4,128)S(1)}, f32[3,640]{1,0:T(4,128)S(1)}, u32[]{:S(2)}, u32[]{:S(2)}) collective-permute-start(f32[3,640]{1,0:T(4,128)S(1)} %add.102), channel_id=1, source_target_pairs={{0,8},{4,12},{8,0},{12,4},{1,9},{5,13},{9,1},{13,5},{2,10},{6,14},... | collective-permute-start | bytes 23048 | tf_op jit(solution)/shard_map/ppermute | solution.py:388
  88.4 2.8 %collective-permute-start.30 = (bf16[40,2944]{1,0:T(8,128)(2,1)S(1)}, bf16[40,2944]{1,0:T(8,128)(2,1)S(1)}, u32[]{:S(2)}, u32[]{:S(2)}) collective-permute-start(bf16[40,2944]{1,0:T(8,128)(2,1)S(1)} %get-tuple-element.121), channel_id=1, source_target_pairs={{0,1},{1,0},{2,3},{3,2},{4,5},{5,4},{6,7},{7,6},{8,9},{9,8},{10,11... | collective-permute-start | bytes 706568 | tf_op jit(solution)/shard_map/ppermute | solution.py:339

commit v11 on v10

--- a/solution.py
+++ b/solution.py
@@ -321,7 +321,7 @@
     sums[1:2] = scale * jnp.sum(shifts, axis=0, keepdims=True)
 
 
-def finish_kernel(cols, dev, step, shard, mine, theirs, ours, aside, out):
+def finish_kernel(cols, dev, step, shard, mine, theirs, ours, aside, vectors, out, new_bias, new_gain, new_shift):
     lower = dev[0] % 2 == 0
     rate = LR_KERNEL * (1.0 - (step[0] % 1000).astype(F32) / 2000.0)
     factor = 0.5 * cols.total ** (-0.5) * rate
@@ -330,6 +330,8 @@
     left, right = jnp.where(lower, here, there), jnp.where(lower, there, here)
     out[:, :cols.lead] = 0.5 * shard[:, :cols.lead] + left
     out[:, cols.lead:] = 0.5 * shard[:, cols.lead:] + right[:, cols.both:]
+    for i, new in enumerate((new_bias, new_gain, new_shift)):
+        new[...] = 0.5 * vectors[i:i + 1]
 
 
 NODE = ("z", "y")
@@ -546,31 +548,33 @@
             received = ring_step(j, *received)
         late += halves
 
+        conv_send = conv_far(acts, late)
+        cots, conv_send = tied(cots, conv_send)
+        conv_got = swap(conv_send, "core")
         sums = back(1, cots, slopes, late)
         crossed[-2], sums, *received = tied(crossed[-2], sums, *received)
-        acts_last, *_ = tied(acts, sums, *received)
         received = ring_step(zs - 2, *received)
-        conv_got = swap(conv_far(acts_last, late), "core")
         vectors = hop(chip_sum(first_sums + sums), "replica", 1)
+        vectors = hop(vectors, "z", 1)
         crossed[-1], conv_got, vectors, *received = tied(crossed[-1], conv_got, vectors, *received)
         last, behind = ring_step(zs - 1, *received)
         block = conv_own(conv_got, [conv_first_own, conv_first_got, order], late)
-        vectors = hop(vectors, "z", 1)
+        vectors = hop(vectors, "y", 1)
         last, block, vectors = tied(last, block, vectors)
         total = add(*behind, last)
-        across = swap(total, "replica")
-        ours, others = jnp.where(same, total, across), jnp.where(same, across, total)
-        aside = swap(others, "core")
-        new_kernel = call(
-            partial(finish_kernel, cols), jax.ShapeDtypeStruct(shard.shape, F32),
-            [SMEM_SPEC] * 2 + [VMEM_SPEC] * 5, [], 8, flops // 16,
-        )(dev, step, shard, mine, theirs, ours, aside)
-        vectors = hop(vectors, "y", 1)
         reach = 2
         while reach < zs:
             vectors = hop(vectors, "z", reach)
             reach *= 2
-        new_v = 0.5 * vectors
+        across, vectors = tied(swap(total, "replica"), vectors)
+        ours, others = jnp.where(same, total, across), jnp.where(same, across, total)
+        aside = swap(others, "core")
+        vector = jax.ShapeDtypeStruct((1, chans), F32)
+        new_kernel, *new_v = call(
+            partial(finish_kernel, cols),
+            (jax.ShapeDtypeStruct(shard.shape, F32), vector, vector, vector),
+            [SMEM_SPEC] * 2 + [VMEM_SPEC] * 6, [], 8, flops // 16,
+        )(dev, step, shard, mine, theirs, ours, aside, vectors)
     else:
         late = [lax.all_gather(unit, NODE, axis=0, tiled=True)]
         cots, slope, slope_x = slopes_of(stats)
@@ -588,14 +592,14 @@
         stepped = shard - (scale * rate) * kernel_grad
         new_kernel = 0.5 * (stepped + from_peer(level, stepped.astype(BF16)).astype(F32))
         stepped_v = lax.psum(vectors, NODE)
-        new_v = 0.5 * (stepped_v + from_peer(level, stepped_v))
+        new_v = jnp.split(0.5 * (stepped_v + from_peer(level, stepped_v)), 3)
 
     return (
         block[None],
         new_kernel[None],
-        new_v[0][None],
-        new_v[1][None],
-        new_v[2][None],
+        new_v[0],
+        new_v[1],
+        new_v[2],
     )
 
 

time: 92.5 us -> 93.7 us (1.013)
  waiting for transfers between devices: 20.1 us -> 24 us
  starting transfers between devices: 33.5 us -> 31.3 us
    ppermute x4, waiting for transfers between devices: 5.57 us -> 10.3 us  [hop(): lax.ppermute(value, axis, [(s, s ^ mask) for s in range(count)])]
    ppermute x8, starting transfers between devices: 9.16 us -> 13.8 us  [up(): return lax.ppermute(value, NODE, self.ahead)]
    ppermute x7, starting transfers between devices: 7.41 us -> 2.77 us  [down(): return lax.ppermute(value, NODE, self.behind)]
    ppermute x7, waiting for transfers between devices: 4.63 us -> 1.37 us  [down(): return lax.ppermute(value, NODE, self.behind)]
    ppermute x4, starting transfers between devices: 7 us -> 4.97 us  [hop(): lax.ppermute(value, axis, [(s, s ^ mask) for s in range(count)])]
    ppermute x14, waiting for transfers between devices: 2.59 us -> 4.26 us  [swap(): return lax.ppermute(value, axis, [(0, 1), (1, 0)])]
  transfers between devices with their start and end apart: 33 -> 33, of which waited for: 13 -> 12; matrix products, arithmetic and copies ran while one was open for 4% -> 3% of each run, Pallas kernels for 34% -> 33%
where the time goes in v11:
time: 93.7 us; the launch traced here: 93.6 us
  Pallas kernels  32.4 us (35%)
  starting transfers between devices  31.3 us (33%)
  waiting for transfers between devices  24 us (26%)
  other arithmetic  2.87 us (3%)
  between operations  1.6 us (2%)
  local copies, waits for them, and re-layouts  1.34 us (1%)
    ppermute x8, starting transfers between devices, up(): return lax.ppermute(value, NODE, self.ahead)  13.8 us
    ppermute x4, waiting for transfers between devices, hop(): lax.ppermute(value, axis, [(s, s ^ mask) for s in range(count)])  10.3 us
    ppermute x14, starting transfers between devices, swap(): return lax.ppermute(value, axis, [(0, 1), (1, 0)])  9.73 us
    pallas_call x2, Pallas kernels, back(): call(partial(back_kernel, cols, stages, stage), jax.ShapeDtypeStruct((2,...  8.62 us
    ppermute x8, waiting for transfers between devices, up(): return lax.ppermute(value, NODE, self.ahead)  8.08 us
    ppermute x4, starting transfers between devices, hop(): lax.ppermute(value, axis, [(s, s ^ mask) for s in range(count)])  4.97 us
    pallas_call x1, Pallas kernels, per_device(): call(partial(grad_kernel, cols), [jax.ShapeDtypeStruct((n * 2 * part, col...  4.64 us
    pallas_call x1, Pallas kernels, slopes_of(): call(partial(slope_kernel, stages), (jax.ShapeDtypeStruct((3, 2 * half +...  4.48 us
  transfers between devices with their start and end apart: 33, of which 12 were waited for; matrix products, arithmetic and copies ran while one was open for 3% of the time, Pallas kernels for 33%

profile of v11, /device:TPU:0, one launch (start us, length us, event | category | flops | bytes accessed | tf_op | source)
XLA Modules:
  0.0 93.6 jit_solution(4371831684477082564)
XLA Ops:
  0.7 1.3 %fusion = (bf16[40,2944]{1,0:T(8,128)(2,1)S(1)}, bf16[40,2944]{1,0:T(8,128)(2,1)S(1)}) fusion(f32[1,40,5760]{2,1,0:T(8,128)} %param.10, s32[]{:T(128)S(6)} %select_n.27, s32[]{:T(128)S(6)} %select_n.28), kind=kLoop, calls=%fused_computation.12 | loop fusion | bytes 942088 | tf_op jit(solution)/shard_map/convert_element_type | solution.py:421
  2.0 0.5 collective-permute-start.3
  2.5 2.0 %fusion.3 = (f32[640]{0:T(1024)S(1)}, bf16[16,32,640]{2,1,0:T(8,128)(2,1)S(1)}) fusion(f32[1,16,32,640]{3,2,1,0:T(8,128)} %param.9), kind=kLoop, calls=%fused_computation.19 | loop fusion | flops 654720 | bytes 1968640 | tf_op jit(solution)/shard_map/reduce_sum | solution.py:514
  4.6 0.5 collective-permute-start
  5.1 2.7 %collective-permute-start.4 = (bf16[80,2944]{1,0:T(8,128)(2,1)S(1)}, bf16[80,2944]{1,0:T(8,128)(2,1)S(1)}, u32[]{:S(2)}, u32[]{:S(2)}) collective-permute-start(bf16[80,2944]{1,0:T(8,128)(2,1)S(1)} %maximum_select_fusion.refs_0_), channel_id=1, source_target_pairs={{0,4},{4,8},{8,12},{12,14},{14,10},{10,6},{6,2},{2,0},{1,5},{5,9},... | collective-permute-start | bytes 1413128 | tf_op jit(solution)/shard_map/ppermute | solution.py:366
  7.8 1.9 %collective-permute-start.6 = (bf16[40,2944]{1,0:T(8,128)(2,1)S(1)}, bf16[40,2944]{1,0:T(8,128)(2,1)S(1)}, u32[]{:S(2)}, u32[]{:S(2)}) collective-permute-start(bf16[40,2944]{1,0:T(8,128)(2,1)S(1)} %get-tuple-element.133), channel_id=1, source_target_pairs={{0,16},{16,0},{1,17},{17,1},{2,18},{18,2},{3,19},{19,3},{4,20},{20... | collective-permute-start | bytes 706568 | tf_op jit(solution)/shard_map/ppermute | solution.py:341
  9.9 4.4 %shard_map.119 = (f32[2,640]{1,0:T(2,128)S(1)}, bf16[3,34,32,640]{3,2,1,0:T(8,128)(2,1)S(1)}, bf16[640,1024]{1,0:T(8,128)(2,1)S(1)}) custom-call(s32[1]{0:T(128)} %bitcast.dev, s32[32,24]{1,0:T(8,128)S(1)} %copy-done.5, bf16[16,32,640]{2,1,0:T(8,128)(2,1)S(1)} %bitcast.13, bf16[16,32,640]{2,1,0:T(8,128)(2,1)S(1)} %collective-permute-done.lat_far, ...), custom_call_target="tpu_custom_call" | custom-call | flops 964689920 | tf_op jit(solution)/shard_map/pallas_call | solution.py:452
  14.3 4.6 %shard_map.120 = (bf16[320,2944]{1,0:T(8,128)(2,1)S(1)}, bf16[80,2944]{1,0:T(8,128)(2,1)S(1)}, bf16[80,2944]{1,0:T(8,128)(2,1)S(1)}, bf16[80,2944]{1,0:T(8,128)(2,1)S(1)}, bf16[80,2944]{1,0:T(8,128)(2,1)S(1)}) custom-call(s32[1]{0:T(128)} %bitcast.dev, bf16[3,34,32,640]{3,2,1,0:T(8,128)(2,1)S(1)} %get-tuple-element.66.acts, ...), custom_call_target="tpu_custom_call" | custom-call | flops 1929379840 | tf_op jit(solution)/shard_map/pallas_call | solution.py:460
  19.0 1.7 %collective-permute-done.7.theirs = bf16[40,2944]{1,0:T(8,128)(2,1)S(1)} collective-permute-done((bf16[40,2944]{1,0:T(8,128)(2,1)S(1)}, bf16[40,2944]{1,0:T(8,128)(2,1)S(1)}, u32[]{:S(2)}, u32[]{:S(2)}) %collective-permute-start.7) | collective-permute-done | bytes 235552 | tf_op jit(solution)/shard_map/ppermute | solution.py:341
  20.7 1.7 %collective-permute-start.8 = (bf16[80,2944]{1,0:T(8,128)(2,1)S(1)}, bf16[80,2944]{1,0:T(8,128)(2,1)S(1)}, u32[]{:S(2)}, u32[]{:S(2)}) collective-permute-start(bf16[80,2944]{1,0:T(8,128)(2,1)S(1)} %collective-permute-done.4.refs_1_), channel_id=1, source_target_pairs={{0,4},{4,8},{8,12},{12,14},{14,10},{10,6},{6,2},{2,0},{1,5},{5,9},... | collective-permute-start | bytes 1413128 | tf_op jit(solution)/shard_map/ppermute | solution.py:366
  22.7 1.7 %collective-permute-start.10 = (bf16[80,2944]{1,0:T(8,128)(2,1)S(1)}, bf16[80,2944]{1,0:T(8,128)(2,1)S(1)}, u32[]{:S(2)}, u32[]{:S(2)}) collective-permute-start(bf16[80,2944]{1,0:T(8,128)(2,1)S(1)} %get-tuple-element.81), channel_id=1, source_target_pairs={{0,16},{16,0},{1,17},{17,1},{2,18},{18,2},{3,19},{19,3},{4,20},{20... | collective-permute-start | bytes 1413128 | tf_op jit(solution)/shard_map/ppermute | solution.py:341
  24.4 0.4 collective-permute-start.13
  24.7 4.5 %shard_map.121 = (bf16[3,34,32,768]{3,2,1,0:T(8,128)(2,1)S(1)}, bf16[32,32,640]{2,1,0:T(8,128)(2,1)S(1)}, bf16[32,32,640]{2,1,0:T(8,128)(2,1)S(1)}, bf16[640,768]{1,0:T(8,128)(2,1)S(1)}) custom-call(s32[1]{0:T(128)} %bitcast.dev, s32[32,24]{1,0:T(8,128)S(1)} %copy-done.5, f32[2,640]{1,0:T(2,128)S(1)} %get-tuple-element.75.stats, f32[1,640]{1,0:T(1,128)S(1)} %copy-done.3, ...), custom_call_target="tpu_custom_call" | custom-call | flops 964689920 | tf_op jit(solution)/shard_map/pallas_call | solution.py:472
  29.2 3.5 %collective-permute-done.8.refs_3_ = bf16[80,2944]{1,0:T(8,128)(2,1)S(1)} collective-permute-done((bf16[80,2944]{1,0:T(8,128)(2,1)S(1)}, bf16[80,2944]{1,0:T(8,128)(2,1)S(1)}, u32[]{:S(2)}, u32[]{:S(2)}) %collective-permute-start.8) | collective-permute-done | bytes 471072 | tf_op jit(solution)/shard_map/ppermute | solution.py:366
  32.7 1.3 %collective-permute-done.9.refs_4_ = bf16[80,2944]{1,0:T(8,128)(2,1)S(1)} collective-permute-done((bf16[80,2944]{1,0:T(8,128)(2,1)S(1)}, bf16[80,2944]{1,0:T(8,128)(2,1)S(1)}, u32[]{:S(2)}, u32[]{:S(2)}) %collective-permute-start.9) | collective-permute-done | bytes 471072 | tf_op jit(solution)/shard_map/ppermute | solution.py:369
  34.0 1.6 %collective-permute-start.11 = (bf16[80,2944]{1,0:T(8,128)(2,1)S(1)}, bf16[80,2944]{1,0:T(8,128)(2,1)S(1)}, u32[]{:S(2)}, u32[]{:S(2)}) collective-permute-start(bf16[80,2944]{1,0:T(8,128)(2,1)S(1)} %collective-permute-done.8.refs_3_), channel_id=1, source_target_pairs={{0,4},{4,8},{8,12},{12,14},{14,10},{10,6},{6,2},{2,0},{1,5},{5,9},... | collective-permute-start | bytes 1413128 | tf_op jit(solution)/shard_map/ppermute | solution.py:366
  35.6 0.4 collective-permute-start.12
  36.0 4.0 %shard_map.122 = (f32[512,512]{1,0:T(8,128)S(1)}, bf16[512,512]{1,0:T(8,128)(2,1)S(1)}) custom-call(s32[1]{0:T(128)} %bitcast.dev, bf16[3,34,32,640]{3,2,1,0:T(8,128)(2,1)S(1)} %get-tuple-element.66.acts, bf16[80,2944]{1,0:T(8,128)(2,1)S(1)} %maximum_select_fusion.refs_0_, bf16[80,2944]{1,0:T(8,128)(2,1)S(1)} %collective-permute-done.4.refs_1_, ...), custom_call_target="tpu_custom_call" | custom-call | flops 964689920 | tf_op jit(solution)/shard_map/pallas_call | solution.py:490
  40.1 1.6 %collective-permute-start.18 = (bf16[40,2944]{1,0:T(8,128)(2,1)S(1)}, bf16[40,2944]{1,0:T(8,128)(2,1)S(1)}, u32[]{:S(2)}, u32[]{:S(2)}) collective-permute-start(bf16[40,2944]{1,0:T(8,128)(2,1)S(1)} %get-tuple-element.130), channel_id=1, source_target_pairs={{0,4},{4,8},{8,12},{12,14},{14,10},{10,6},{6,2},{2,0},{1,5},{5,9},... | collective-permute-start | bytes 706568 | tf_op jit(solution)/shard_map/ppermute | solution.py:366
  41.8 0.5 collective-permute-start.19
  42.2 5.4 %shard_map.123 = f32[2,640]{1,0:T(2,128)S(1)} custom-call(s32[1]{0:T(128)} %bitcast.dev, bf16[3,34,32,768]{3,2,1,0:T(8,128)(2,1)S(1)} %get-tuple-element.95.cots, bf16[32,32,640]{2,1,0:T(8,128)(2,1)S(1)} %get-tuple-element.87.slope, bf16[32,32,640]{2,1,0:T(8,128)(2,1)S(1)} %get-tuple-element.88.slope_x, bf16[80,2944]{1,0:T(8,128)(2,1)S(1)} %maximum_select_fusion.refs_0_, ...), custom_call_target="tpu_custom_call" | custom-call | flops 964689920 | tf_op jit(solution)/shard_map/pallas_call | solution.py:482
  47.6 2.0 %collective-permute-done.18 = bf16[40,2944]{1,0:T(8,128)(2,1)S(1)} collective-permute-done((bf16[40,2944]{1,0:T(8,128)(2,1)S(1)}, bf16[40,2944]{1,0:T(8,128)(2,1)S(1)}, u32[]{:S(2)}, u32[]{:S(2)}) %collective-permute-start.18) | collective-permute-done | bytes 235552 | tf_op jit(solution)/shard_map/ppermute | solution.py:366
  49.7 1.5 %collective-permute-start.17 = (bf16[80,2944]{1,0:T(8,128)(2,1)S(1)}, bf16[80,2944]{1,0:T(8,128)(2,1)S(1)}, u32[]{:S(2)}, u32[]{:S(2)}) collective-permute-start(bf16[80,2944]{1,0:T(8,128)(2,1)S(1)} %get-tuple-element.94), channel_id=1, source_target_pairs={{0,16},{16,0},{1,17},{17,1},{2,18},{18,2},{3,19},{19,3},{4,20},{20... | collective-permute-start | bytes 1413128 | tf_op jit(solution)/shard_map/ppermute | solution.py:341
  51.2 1.6 %collective-permute-start.14 = (bf16[40,2944]{1,0:T(8,128)(2,1)S(1)}, bf16[40,2944]{1,0:T(8,128)(2,1)S(1)}, u32[]{:S(2)}, u32[]{:S(2)}) collective-permute-start(bf16[40,2944]{1,0:T(8,128)(2,1)S(1)} %slice.67), channel_id=1, source_target_pairs={{0,4},{4,8},{8,12},{12,14},{14,10},{10,6},{6,2},{2,0},{1,5},{5,9},... | collective-permute-start | bytes 706568 | tf_op jit(solution)/shard_map/ppermute | solution.py:366
  52.9 0.5 collective-permute-start.15
  53.6 1.6 %collective-permute-start.20 = (bf16[40,2944]{1,0:T(8,128)(2,1)S(1)}, bf16[40,2944]{1,0:T(8,128)(2,1)S(1)}, u32[]{:S(2)}, u32[]{:S(2)}) collective-permute-start(bf16[40,2944]{1,0:T(8,128)(2,1)S(1)} %get-tuple-element.128), channel_id=1, source_target_pairs={{0,4},{4,8},{8,12},{12,14},{14,10},{10,6},{6,2},{2,0},{1,5},{5,9},... | collective-permute-start | bytes 706568 | tf_op jit(solution)/shard_map/ppermute | solution.py:366
  55.2 0.5 collective-permute-start.21
  55.6 2.5 %collective-permute-done.14.refs_2_.refs_5_ = bf16[40,2944]{1,0:T(8,128)(2,1)S(1)} collective-permute-done((bf16[40,2944]{1,0:T(8,128)(2,1)S(1)}, bf16[40,2944]{1,0:T(8,128)(2,1)S(1)}, u32[]{:S(2)}, u32[]{:S(2)}) %collective-permute-start.14) | collective-permute-done | bytes 235552 | tf_op jit(solution)/shard_map/ppermute | solution.py:366
  58.2 1.3 %collective-permute-start.2 = (bf16[80,2944]{1,0:T(8,128)(2,1)S(1)}, bf16[80,2944]{1,0:T(8,128)(2,1)S(1)}, u32[]{:S(2)}, u32[]{:S(2)}) collective-permute-start(bf16[80,2944]{1,0:T(8,128)(2,1)S(1)} %get-tuple-element.69), channel_id=1, source_target_pairs={{0,16},{16,0},{1,17},{17,1},{2,18},{18,2},{3,19},{19,3},{4,20},{20... | collective-permute-start | bytes 1413128 | tf_op jit(solution)/shard_map/ppermute | solution.py:341
  59.6 1.4 %shard_map.124 = bf16[512,256]{1,0:T(8,128)(2,1)S(1)} custom-call(s32[1]{0:T(128)} %bitcast.dev, bf16[3,34,32,640]{3,2,1,0:T(8,128)(2,1)S(1)} %get-tuple-element.66.acts, bf16[80,2944]{1,0:T(8,128)(2,1)S(1)} %collective-permute-done.11.refs_0_.refs_3_, bf16[80,2944]{1,0:T(8,128)(2,1)S(1)} %collective-permute-done.12.refs_1_.refs_4_, ...), custom_call_target="tpu_custom_call" | custom-call | flops 482344960 | tf_op jit(solution)/shard_map/pallas_call | solution.py:499
  61.0 3.2 %shard_map.125 = f32[2,640]{1,0:T(2,128)S(1)} custom-call(s32[1]{0:T(128)} %bitcast.dev, bf16[3,34,32,768]{3,2,1,0:T(8,128)(2,1)S(1)} %get-tuple-element.95.cots, bf16[32,32,640]{2,1,0:T(8,128)(2,1)S(1)} %get-tuple-element.87.slope, bf16[32,32,640]{2,1,0:T(8,128)(2,1)S(1)} %get-tuple-element.88.slope_x, ...), custom_call_target="tpu_custom_call" | custom-call | flops 964689920 | tf_op jit(solution)/shard_map/pallas_call | solution.py:482
  64.4 0.5 collective-permute-start.16
  65.1 1.5 %collective-permute-start.25 = (bf16[40,2944]{1,0:T(8,128)(2,1)S(1)}, bf16[40,2944]{1,0:T(8,128)(2,1)S(1)}, u32[]{:S(2)}, u32[]{:S(2)}) collective-permute-start(bf16[40,2944]{1,0:T(8,128)(2,1)S(1)} %get-tuple-element.126), channel_id=1, source_target_pairs={{0,4},{4,8},{8,12},{12,14},{14,10},{10,6},{6,2},{2,0},{1,5},{5,9},... | collective-permute-start | bytes 706568 | tf_op jit(solution)/shard_map/ppermute | solution.py:366
  66.5 0.6 collective-permute-start.26
  67.2 1.2 %collective-permute-start.23 = (f32[3,640]{1,0:T(4,128)S(1)}, f32[3,640]{1,0:T(4,128)S(1)}, u32[]{:S(2)}, u32[]{:S(2)}) collective-permute-start(f32[3,640]{1,0:T(4,128)S(1)} %fusion.4), channel_id=1, source_target_pairs={{0,16},{16,0},{1,17},{17,1},{2,18},{18,2},{3,19},{19,3},{4,20},{20... | collective-permute-start | bytes 23048 | tf_op jit(solution)/shard_map/ppermute | solution.py:390
  68.4 2.6 %collective-permute-done.23 = f32[3,640]{1,0:T(4,128)S(1)} collective-permute-done((f32[3,640]{1,0:T(4,128)S(1)}, f32[3,640]{1,0:T(4,128)S(1)}, u32[]{:S(2)}, u32[]{:S(2)}) %collective-permute-start.23) | collective-permute-done | bytes 7712 | tf_op jit(solution)/shard_map/ppermute | solution.py:390
  70.9 1.4 %collective-permute-start.24 = (f32[3,640]{1,0:T(4,128)S(1)}, f32[3,640]{1,0:T(4,128)S(1)}, u32[]{:S(2)}, u32[]{:S(2)}) collective-permute-start(f32[3,640]{1,0:T(4,128)S(1)} %add.91), channel_id=1, source_target_pairs={{0,4},{4,0},{8,12},{12,8},{1,5},{5,1},{9,13},{13,9},{2,6},{6,2},{1... | collective-permute-start | bytes 23048 | tf_op jit(solution)/shard_map/ppermute | solution.py:390
  72.3 2.3 %collective-permute-done.24 = f32[3,640]{1,0:T(4,128)S(1)} collective-permute-done((f32[3,640]{1,0:T(4,128)S(1)}, f32[3,640]{1,0:T(4,128)S(1)}, u32[]{:S(2)}, u32[]{:S(2)}) %collective-permute-start.24) | collective-permute-done | bytes 7712 | tf_op jit(solution)/shard_map/ppermute | solution.py:390
  74.7 1.5 %collective-permute-start.27 = (bf16[40,2944]{1,0:T(8,128)(2,1)S(1)}, bf16[40,2944]{1,0:T(8,128)(2,1)S(1)}, u32[]{:S(2)}, u32[]{:S(2)}) collective-permute-start(bf16[40,2944]{1,0:T(8,128)(2,1)S(1)} %add_convert_fusion.1), channel_id=1, source_target_pairs={{0,4},{4,8},{8,12},{12,14},{14,10},{10,6},{6,2},{2,0},{1,5},{5,9},... | collective-permute-start | bytes 706568 | tf_op jit(solution)/shard_map/ppermute | solution.py:366
  76.2 0.6 collective-permute-start.29
  76.8 3.7 %shard_map.126 = bf16[16,32,640]{2,1,0:T(8,128)(2,1)} custom-call(s32[1]{0:T(128)} %bitcast.dev, bf16[3,34,32,640]{3,2,1,0:T(8,128)(2,1)S(1)} %get-tuple-element.66.acts, bf16[512,256]{1,0:T(8,128)(2,1)S(1)} %collective-permute-done.16.got, bf16[16,32,640]{2,1,0:T(8,128)(2,1)S(1)} %bitcast.15, f32[1,640]{1,0:T(1,128)S(1)} %copy-done.2, ...), custom_call_target="tpu_custom_call" | custom-call | flops 964689920 | tf_op jit(solution)/shard_map/pallas_call | solution.py:507
  80.5 2.7 %collective-permute-done.29 = f32[3,640]{1,0:T(4,128)S(1)} collective-permute-done((f32[3,640]{1,0:T(4,128)S(1)}, f32[3,640]{1,0:T(4,128)S(1)}, u32[]{:S(2)}, u32[]{:S(2)}) %collective-permute-start.29) | collective-permute-done | bytes 7712 | tf_op jit(solution)/shard_map/ppermute | solution.py:390
  83.3 1.2 %collective-permute-start.30 = (bf16[40,2944]{1,0:T(8,128)(2,1)S(1)}, bf16[40,2944]{1,0:T(8,128)(2,1)S(1)}, u32[]{:S(2)}, u32[]{:S(2)}) collective-permute-start(bf16[40,2944]{1,0:T(8,128)(2,1)S(1)} %add_convert_fusion), channel_id=1, source_target_pairs={{0,16},{16,0},{1,17},{17,1},{2,18},{18,2},{3,19},{19,3},{4,20},{20... | collective-permute-start | bytes 706568 | tf_op jit(solution)/shard_map/ppermute | solution.py:341
  84.5 1.8 %collective-permute-start.31 = (f32[3,640]{1,0:T(4,128)S(1)}, f32[3,640]{1,0:T(4,128)S(1)}, u32[]{:S(2)}, u32[]{:S(2)}) collective-permute-start(f32[3,640]{1,0:T(4,128)S(1)} %add.99), channel_id=1, source_target_pairs={{0,8},{4,12},{8,0},{12,4},{1,9},{5,13},{9,1},{13,5},{2,10},{6,14},... | collective-permute-start | bytes 23048 | tf_op jit(solution)/shard_map/ppermute | solution.py:390
  86.2 2.8 %collective-permute-done.31 = f32[3,640]{1,0:T(4,128)S(1)} collective-permute-done((f32[3,640]{1,0:T(4,128)S(1)}, f32[3,640]{1,0:T(4,128)S(1)}, u32[]{:S(2)}, u32[]{:S(2)}) %collective-permute-start.31) | collective-permute-done | bytes 7712 | tf_op jit(solution)/shard_map/ppermute | solution.py:390
  89.1 1.7 %collective-permute-done.30 = bf16[40,2944]{1,0:T(8,128)(2,1)S(1)} collective-permute-done((bf16[40,2944]{1,0:T(8,128)(2,1)S(1)}, bf16[40,2944]{1,0:T(8,128)(2,1)S(1)}, u32[]{:S(2)}, u32[]{:S(2)}) %collective-permute-start.30) | collective-permute-done | bytes 235552 | tf_op jit(solution)/shard_map/ppermute | solution.py:341
  91.5 0.8 collective-permute-done.32.aside
  92.3 1.2 %shard_map.127 = (f32[40,5760]{1,0:T(8,128)}, f32[1,640]{1,0:T(1,128)}, f32[1,640]{1,0:T(1,128)}, f32[1,640]{1,0:T(1,128)}) custom-call(s32[1]{0:T(128)} %bitcast.dev, s32[1]{0:T(128)S(6)} %copy.13.step, f32[40,5760]{1,0:T(8,128)S(1)} %bitcast.11, bf16[40,2944]{1,0:T(8,128)(2,1)S(1)} %collective-permute-done.6.mine, ...), custom_call_target="tpu_custom_call" | custom-call | flops 241172480 | tf_op jit(solution)/shard_map/pallas_call | solution.py:573
  (58 shorter events, 1.8 us)
Async XLA Ops:
  0.6 3.9 %copy-start.1 = (bf16[1,16,32,640]{3,2,1,0:T(8,128)(2,1)S(1)}, bf16[1,16,32,640]{3,2,1,0:T(8,128)(2,1)}, u32[]{:S(2)}) copy-start(bf16[1,16,32,640]{3,2,1,0:T(8,128)(2,1)} %param.8) | copy-start | bytes 1966084
  0.7 9.2 %copy-start.3 = (f32[1,640]{1,0:T(1,128)S(1)}, f32[1,640]{1,0:T(1,128)}, u32[]{:S(2)}) copy-start(f32[1,640]{1,0:T(1,128)} %gain.3) | copy-start | bytes 7684
  0.7 9.2 %copy-start.4 = (f32[1,640]{1,0:T(1,128)S(1)}, f32[1,640]{1,0:T(1,128)}, u32[]{:S(2)}) copy-start(f32[1,640]{1,0:T(1,128)} %shift.3) | copy-start | bytes 7684
  0.7 9.2 %copy-start.5 = (s32[32,24]{1,0:T(8,128)S(1)}, s32[32,24]{1,0:T(8,128)}, u32[]{:S(2)}) copy-start(s32[32,24]{1,0:T(8,128)} %constant.38.clone.table) | copy-start | bytes 9220
  2.0 3.1 %collective-permute-start.3 = (bf16[40,2944]{1,0:T(8,128)(2,1)S(1)}, bf16[40,2944]{1,0:T(8,128)(2,1)S(1)}, u32[]{:S(2)}, u32[]{:S(2)}) collective-permute-start(bf16[40,2944]{1,0:T(8,128)(2,1)S(1)} %get-tuple-element.134), channel_id=1, source_target_pairs={{0,1},{1,0},{2,3},{3,2},{4,5},{5,4},{6,7},{7,6},{8,9},{9,8},{10,11... | collective-permute-start | bytes 706568 | tf_op jit(solution)/shard_map/ppermute | solution.py:341
  4.5 5.3 %collective-permute-start.1 = (bf16[16,32,640]{2,1,0:T(8,128)(2,1)S(1)}, bf16[16,32,640]{2,1,0:T(8,128)(2,1)S(1)}, u32[]{:S(2)}, u32[]{:S(2)}) collective-permute-start(bf16[16,32,640]{2,1,0:T(8,128)(2,1)S(1)} %get-tuple-element.132.cot_own), channel_id=1, source_target_pairs={{0,1},{1,0},{2,3},{3,2},{4,5},{5,4},{6,7},{7,6},{8,9},{9,8},{10,11... | collective-permute-start | bytes 1966088 | tf_op jit(solution)/shard_map/ppermute | solution.py:341
  4.6 5.3 %collective-permute-start = (bf16[16,32,640]{2,1,0:T(8,128)(2,1)S(1)}, bf16[16,32,640]{2,1,0:T(8,128)(2,1)S(1)}, u32[]{:S(2)}, u32[]{:S(2)}) collective-permute-start(bf16[16,32,640]{2,1,0:T(8,128)(2,1)S(1)} %bitcast.12), channel_id=1, source_target_pairs={{0,1},{1,0},{2,3},{3,2},{4,5},{5,4},{6,7},{7,6},{8,9},{9,8},{10,11... | collective-permute-start | bytes 1966088 | tf_op jit(solution)/shard_map/ppermute | solution.py:341
  5.1 15.6 %collective-permute-start.4 = (bf16[80,2944]{1,0:T(8,128)(2,1)S(1)}, bf16[80,2944]{1,0:T(8,128)(2,1)S(1)}, u32[]{:S(2)}, u32[]{:S(2)}) collective-permute-start(bf16[80,2944]{1,0:T(8,128)(2,1)S(1)} %maximum_select_fusion.refs_0_), channel_id=1, source_target_pairs={{0,4},{4,8},{8,12},{12,14},{14,10},{10,6},{6,2},{2,0},{1,5},{5,9},... | collective-permute-start | bytes 1413128 | tf_op jit(solution)/shard_map/ppermute | solution.py:366
  7.8 12.9 %collective-permute-start.5 = (bf16[80,2944]{1,0:T(8,128)(2,1)S(1)}, bf16[80,2944]{1,0:T(8,128)(2,1)S(1)}, u32[]{:S(2)}, u32[]{:S(2)}) collective-permute-start(bf16[80,2944]{1,0:T(8,128)(2,1)S(1)} %maximum_select_fusion.refs_0_), channel_id=1, source_target_pairs={{4,0},{8,4},{12,8},{14,12},{10,14},{6,10},{2,6},{0,2},{5,1},{9,5},... | collective-permute-start | bytes 1413128 | tf_op jit(solution)/shard_map/ppermute | solution.py:369
  7.8 11.1 %collective-permute-start.6 = (bf16[40,2944]{1,0:T(8,128)(2,1)S(1)}, bf16[40,2944]{1,0:T(8,128)(2,1)S(1)}, u32[]{:S(2)}, u32[]{:S(2)}) collective-permute-start(bf16[40,2944]{1,0:T(8,128)(2,1)S(1)} %get-tuple-element.133), channel_id=1, source_target_pairs={{0,16},{16,0},{1,17},{17,1},{2,18},{18,2},{3,19},{19,3},{4,20},{20... | collective-permute-start | bytes 706568 | tf_op jit(solution)/shard_map/ppermute | solution.py:341
  9.8 10.9 %collective-permute-start.7 = (bf16[40,2944]{1,0:T(8,128)(2,1)S(1)}, bf16[40,2944]{1,0:T(8,128)(2,1)S(1)}, u32[]{:S(2)}, u32[]{:S(2)}) collective-permute-start(bf16[40,2944]{1,0:T(8,128)(2,1)S(1)} %get-tuple-element.134), channel_id=1, source_target_pairs={{0,16},{16,0},{1,17},{17,1},{2,18},{18,2},{3,19},{19,3},{4,20},{20... | collective-permute-start | bytes 706568 | tf_op jit(solution)/shard_map/ppermute | solution.py:341
  20.7 12.0 %collective-permute-start.8 = (bf16[80,2944]{1,0:T(8,128)(2,1)S(1)}, bf16[80,2944]{1,0:T(8,128)(2,1)S(1)}, u32[]{:S(2)}, u32[]{:S(2)}) collective-permute-start(bf16[80,2944]{1,0:T(8,128)(2,1)S(1)} %collective-permute-done.4.refs_1_), channel_id=1, source_target_pairs={{0,4},{4,8},{8,12},{12,14},{14,10},{10,6},{6,2},{2,0},{1,5},{5,9},... | collective-permute-start | bytes 1413128 | tf_op jit(solution)/shard_map/ppermute | solution.py:366
  22.4 11.6 %collective-permute-start.9 = (bf16[80,2944]{1,0:T(8,128)(2,1)S(1)}, bf16[80,2944]{1,0:T(8,128)(2,1)S(1)}, u32[]{:S(2)}, u32[]{:S(2)}) collective-permute-start(bf16[80,2944]{1,0:T(8,128)(2,1)S(1)} %collective-permute-done.5.refs_2_), channel_id=1, source_target_pairs={{4,0},{8,4},{12,8},{14,12},{10,14},{6,10},{2,6},{0,2},{5,1},{9,5},... | collective-permute-start | bytes 1413128 | tf_op jit(solution)/shard_map/ppermute | solution.py:369
  22.7 17.3 %collective-permute-start.10 = (bf16[80,2944]{1,0:T(8,128)(2,1)S(1)}, bf16[80,2944]{1,0:T(8,128)(2,1)S(1)}, u32[]{:S(2)}, u32[]{:S(2)}) collective-permute-start(bf16[80,2944]{1,0:T(8,128)(2,1)S(1)} %get-tuple-element.81), channel_id=1, source_target_pairs={{0,16},{16,0},{1,17},{17,1},{2,18},{18,2},{3,19},{19,3},{4,20},{20... | collective-permute-start | bytes 1413128 | tf_op jit(solution)/shard_map/ppermute | solution.py:341
  24.4 26.8 %collective-permute-start.13 = (bf16[80,2944]{1,0:T(8,128)(2,1)S(1)}, bf16[80,2944]{1,0:T(8,128)(2,1)S(1)}, u32[]{:S(2)}, u32[]{:S(2)}) collective-permute-start(bf16[80,2944]{1,0:T(8,128)(2,1)S(1)} %get-tuple-element.89), channel_id=1, source_target_pairs={{0,16},{16,0},{1,17},{17,1},{2,18},{18,2},{3,19},{19,3},{4,20},{20... | collective-permute-start | bytes 1413128 | tf_op jit(solution)/shard_map/ppermute | solution.py:341
  34.0 17.2 %collective-permute-start.11 = (bf16[80,2944]{1,0:T(8,128)(2,1)S(1)}, bf16[80,2944]{1,0:T(8,128)(2,1)S(1)}, u32[]{:S(2)}, u32[]{:S(2)}) collective-permute-start(bf16[80,2944]{1,0:T(8,128)(2,1)S(1)} %collective-permute-done.8.refs_3_), channel_id=1, source_target_pairs={{0,4},{4,8},{8,12},{12,14},{14,10},{10,6},{6,2},{2,0},{1,5},{5,9},... | collective-permute-start | bytes 1413128 | tf_op jit(solution)/shard_map/ppermute | solution.py:366
  35.6 15.6 %collective-permute-start.12 = (bf16[80,2944]{1,0:T(8,128)(2,1)S(1)}, bf16[80,2944]{1,0:T(8,128)(2,1)S(1)}, u32[]{:S(2)}, u32[]{:S(2)}) collective-permute-start(bf16[80,2944]{1,0:T(8,128)(2,1)S(1)} %collective-permute-done.9.refs_4_), channel_id=1, source_target_pairs={{4,0},{8,4},{12,8},{14,12},{10,14},{6,10},{2,6},{0,2},{5,1},{9,5},... | collective-permute-start | bytes 1413128 | tf_op jit(solution)/shard_map/ppermute | solution.py:369
  40.1 9.5 %collective-permute-start.18 = (bf16[40,2944]{1,0:T(8,128)(2,1)S(1)}, bf16[40,2944]{1,0:T(8,128)(2,1)S(1)}, u32[]{:S(2)}, u32[]{:S(2)}) collective-permute-start(bf16[40,2944]{1,0:T(8,128)(2,1)S(1)} %get-tuple-element.130), channel_id=1, source_target_pairs={{0,4},{4,8},{8,12},{12,14},{14,10},{10,6},{6,2},{2,0},{1,5},{5,9},... | collective-permute-start | bytes 706568 | tf_op jit(solution)/shard_map/ppermute | solution.py:366
  41.8 9.4 %collective-permute-start.19 = (bf16[40,2944]{1,0:T(8,128)(2,1)S(1)}, bf16[40,2944]{1,0:T(8,128)(2,1)S(1)}, u32[]{:S(2)}, u32[]{:S(2)}) collective-permute-start(bf16[40,2944]{1,0:T(8,128)(2,1)S(1)} %get-tuple-element.129), channel_id=1, source_target_pairs={{4,0},{8,4},{12,8},{14,12},{10,14},{6,10},{2,6},{0,2},{5,1},{9,5},... | collective-permute-start | bytes 706568 | tf_op jit(solution)/shard_map/ppermute | solution.py:369
  49.7 14.6 %collective-permute-start.17 = (bf16[80,2944]{1,0:T(8,128)(2,1)S(1)}, bf16[80,2944]{1,0:T(8,128)(2,1)S(1)}, u32[]{:S(2)}, u32[]{:S(2)}) collective-permute-start(bf16[80,2944]{1,0:T(8,128)(2,1)S(1)} %get-tuple-element.94), channel_id=1, source_target_pairs={{0,16},{16,0},{1,17},{17,1},{2,18},{18,2},{3,19},{19,3},{4,20},{20... | collective-permute-start | bytes 1413128 | tf_op jit(solution)/shard_map/ppermute | solution.py:341
  51.2 7.0 %collective-permute-start.14 = (bf16[40,2944]{1,0:T(8,128)(2,1)S(1)}, bf16[40,2944]{1,0:T(8,128)(2,1)S(1)}, u32[]{:S(2)}, u32[]{:S(2)}) collective-permute-start(bf16[40,2944]{1,0:T(8,128)(2,1)S(1)} %slice.67), channel_id=1, source_target_pairs={{0,4},{4,8},{8,12},{12,14},{14,10},{10,6},{6,2},{2,0},{1,5},{5,9},... | collective-permute-start | bytes 706568 | tf_op jit(solution)/shard_map/ppermute | solution.py:366
  52.9 6.7 %collective-permute-start.15 = (bf16[40,2944]{1,0:T(8,128)(2,1)S(1)}, bf16[40,2944]{1,0:T(8,128)(2,1)S(1)}, u32[]{:S(2)}, u32[]{:S(2)}) collective-permute-start(bf16[40,2944]{1,0:T(8,128)(2,1)S(1)} %slice.68), channel_id=1, source_target_pairs={{4,0},{8,4},{12,8},{14,12},{10,14},{6,10},{2,6},{0,2},{5,1},{9,5},... | collective-permute-start | bytes 706568 | tf_op jit(solution)/shard_map/ppermute | solution.py:369
  53.6 10.7 %collective-permute-start.20 = (bf16[40,2944]{1,0:T(8,128)(2,1)S(1)}, bf16[40,2944]{1,0:T(8,128)(2,1)S(1)}, u32[]{:S(2)}, u32[]{:S(2)}) collective-permute-start(bf16[40,2944]{1,0:T(8,128)(2,1)S(1)} %get-tuple-element.128), channel_id=1, source_target_pairs={{0,4},{4,8},{8,12},{12,14},{14,10},{10,6},{6,2},{2,0},{1,5},{5,9},... | collective-permute-start | bytes 706568 | tf_op jit(solution)/shard_map/ppermute | solution.py:366
  55.2 9.1 %collective-permute-start.21 = (bf16[40,2944]{1,0:T(8,128)(2,1)S(1)}, bf16[40,2944]{1,0:T(8,128)(2,1)S(1)}, u32[]{:S(2)}, u32[]{:S(2)}) collective-permute-start(bf16[40,2944]{1,0:T(8,128)(2,1)S(1)} %get-tuple-element.127), channel_id=1, source_target_pairs={{4,0},{8,4},{12,8},{14,12},{10,14},{6,10},{2,6},{0,2},{5,1},{9,5},... | collective-permute-start | bytes 706568 | tf_op jit(solution)/shard_map/ppermute | solution.py:369
  58.2 16.4 %collective-permute-start.2 = (bf16[80,2944]{1,0:T(8,128)(2,1)S(1)}, bf16[80,2944]{1,0:T(8,128)(2,1)S(1)}, u32[]{:S(2)}, u32[]{:S(2)}) collective-permute-start(bf16[80,2944]{1,0:T(8,128)(2,1)S(1)} %get-tuple-element.69), channel_id=1, source_target_pairs={{0,16},{16,0},{1,17},{17,1},{2,18},{18,2},{3,19},{19,3},{4,20},{20... | collective-permute-start | bytes 1413128 | tf_op jit(solution)/shard_map/ppermute | solution.py:341
  61.0 3.3 %copy-start.2 = (f32[1,640]{1,0:T(1,128)S(1)}, f32[1,640]{1,0:T(1,128)}, u32[]{:S(2)}) copy-start(f32[1,640]{1,0:T(1,128)} %bias.1) | copy-start | bytes 7684
  64.3 2.8 %collective-permute-start.22 = (f32[3,640]{1,0:T(4,128)S(1)}, f32[3,640]{1,0:T(4,128)S(1)}, u32[]{:S(2)}, u32[]{:S(2)}) collective-permute-start(f32[3,640]{1,0:T(4,128)S(1)} %fusion.2), channel_id=1, source_target_pairs={{0,1},{1,0},{2,3},{3,2},{4,5},{5,4},{6,7},{7,6},{8,9},{9,8},{10,11... | collective-permute-start | bytes 23048 | tf_op jit(solution)/shard_map/ppermute | solution.py:341
  64.4 10.3 %collective-permute-start.16 = (bf16[512,256]{1,0:T(8,128)(2,1)S(1)}, bf16[512,256]{1,0:T(8,128)(2,1)S(1)}, u32[]{:S(2)}, u32[]{:S(2)}) collective-permute-start(bf16[512,256]{1,0:T(8,128)(2,1)S(1)} %shard_map.124), channel_id=1, source_target_pairs={{0,1},{1,0},{2,3},{3,2},{4,5},{5,4},{6,7},{7,6},{8,9},{9,8},{10,11... | collective-permute-start | bytes 786440 | tf_op jit(solution)/shard_map/ppermute | solution.py:341
  65.1 9.5 %collective-permute-start.25 = (bf16[40,2944]{1,0:T(8,128)(2,1)S(1)}, bf16[40,2944]{1,0:T(8,128)(2,1)S(1)}, u32[]{:S(2)}, u32[]{:S(2)}) collective-permute-start(bf16[40,2944]{1,0:T(8,128)(2,1)S(1)} %get-tuple-element.126), channel_id=1, source_target_pairs={{0,4},{4,8},{8,12},{12,14},{14,10},{10,6},{6,2},{2,0},{1,5},{5,9},... | collective-permute-start | bytes 706568 | tf_op jit(solution)/shard_map/ppermute | solution.py:366
  66.5 8.1 %collective-permute-start.26 = (bf16[40,2944]{1,0:T(8,128)(2,1)S(1)}, bf16[40,2944]{1,0:T(8,128)(2,1)S(1)}, u32[]{:S(2)}, u32[]{:S(2)}) collective-permute-start(bf16[40,2944]{1,0:T(8,128)(2,1)S(1)} %get-tuple-element.125), channel_id=1, source_target_pairs={{4,0},{8,4},{12,8},{14,12},{10,14},{6,10},{2,6},{0,2},{5,1},{9,5},... | collective-permute-start | bytes 706568 | tf_op jit(solution)/shard_map/ppermute | solution.py:369
  67.2 3.7 %collective-permute-start.23 = (f32[3,640]{1,0:T(4,128)S(1)}, f32[3,640]{1,0:T(4,128)S(1)}, u32[]{:S(2)}, u32[]{:S(2)}) collective-permute-start(f32[3,640]{1,0:T(4,128)S(1)} %fusion.4), channel_id=1, source_target_pairs={{0,16},{16,0},{1,17},{17,1},{2,18},{18,2},{3,19},{19,3},{4,20},{20... | collective-permute-start | bytes 23048 | tf_op jit(solution)/shard_map/ppermute | solution.py:390
  70.9 3.7 %collective-permute-start.24 = (f32[3,640]{1,0:T(4,128)S(1)}, f32[3,640]{1,0:T(4,128)S(1)}, u32[]{:S(2)}, u32[]{:S(2)}) collective-permute-start(f32[3,640]{1,0:T(4,128)S(1)} %add.91), channel_id=1, source_target_pairs={{0,4},{4,0},{8,12},{12,8},{1,5},{5,1},{9,13},{13,9},{2,6},{6,2},{1... | collective-permute-start | bytes 23048 | tf_op jit(solution)/shard_map/ppermute | solution.py:390
  74.6 2.2 %collective-permute-start.28 = (bf16[512,512]{1,0:T(8,128)(2,1)S(1)}, bf16[512,512]{1,0:T(8,128)(2,1)S(1)}, u32[]{:S(2)}, u32[]{:S(2)}) collective-permute-start(bf16[512,512]{1,0:T(8,128)(2,1)S(1)} %get-tuple-element.109), channel_id=1, source_target_pairs={{0,1},{1,0},{2,3},{3,2},{4,5},{5,4},{6,7},{7,6},{8,9},{9,8},{10,11... | collective-permute-start | bytes 1572872 | tf_op jit(solution)/shard_map/ppermute | solution.py:341
  74.7 8.4 %collective-permute-start.27 = (bf16[40,2944]{1,0:T(8,128)(2,1)S(1)}, bf16[40,2944]{1,0:T(8,128)(2,1)S(1)}, u32[]{:S(2)}, u32[]{:S(2)}) collective-permute-start(bf16[40,2944]{1,0:T(8,128)(2,1)S(1)} %add_convert_fusion.1), channel_id=1, source_target_pairs={{0,4},{4,8},{8,12},{12,14},{14,10},{10,6},{6,2},{2,0},{1,5},{5,9},... | collective-permute-start | bytes 706568 | tf_op jit(solution)/shard_map/ppermute | solution.py:366
  76.2 7.0 %collective-permute-start.29 = (f32[3,640]{1,0:T(4,128)S(1)}, f32[3,640]{1,0:T(4,128)S(1)}, u32[]{:S(2)}, u32[]{:S(2)}) collective-permute-start(f32[3,640]{1,0:T(4,128)S(1)} %add.92), channel_id=1, source_target_pairs={{0,2},{2,0},{1,3},{3,1},{4,6},{6,4},{5,7},{7,5},{8,10},{10,8},{9,1... | collective-permute-start | bytes 23048 | tf_op jit(solution)/shard_map/ppermute | solution.py:390
  80.5 11.8 %copy-start = (f32[1,40,5760]{2,1,0:T(8,128)S(1)}, f32[1,40,5760]{2,1,0:T(8,128)}, u32[]{:S(2)}) copy-start(f32[1,40,5760]{2,1,0:T(8,128)} %param.10) | copy-start | bytes 2764804
  83.3 7.4 %collective-permute-start.30 = (bf16[40,2944]{1,0:T(8,128)(2,1)S(1)}, bf16[40,2944]{1,0:T(8,128)(2,1)S(1)}, u32[]{:S(2)}, u32[]{:S(2)}) collective-permute-start(bf16[40,2944]{1,0:T(8,128)(2,1)S(1)} %add_convert_fusion), channel_id=1, source_target_pairs={{0,16},{16,0},{1,17},{17,1},{2,18},{18,2},{3,19},{19,3},{4,20},{20... | collective-permute-start | bytes 706568 | tf_op jit(solution)/shard_map/ppermute | solution.py:341
  84.5 4.6 %collective-permute-start.31 = (f32[3,640]{1,0:T(4,128)S(1)}, f32[3,640]{1,0:T(4,128)S(1)}, u32[]{:S(2)}, u32[]{:S(2)}) collective-permute-start(f32[3,640]{1,0:T(4,128)S(1)} %add.99), channel_id=1, source_target_pairs={{0,8},{4,12},{8,0},{12,4},{1,9},{5,13},{9,1},{13,5},{2,10},{6,14},... | collective-permute-start | bytes 23048 | tf_op jit(solution)/shard_map/ppermute | solution.py:390
  90.8 1.6 %collective-permute-start.32 = (bf16[40,2944]{1,0:T(8,128)(2,1)S(1)}, bf16[40,2944]{1,0:T(8,128)(2,1)S(1)}, u32[]{:S(2)}, u32[]{:S(2)}) collective-permute-start(bf16[40,2944]{1,0:T(8,128)(2,1)S(1)} %get-tuple-element.135), channel_id=1, source_target_pairs={{0,1},{1,0},{2,3},{3,2},{4,5},{5,4},{6,7},{7,6},{8,9},{9,8},{10,11... | collective-permute-start | bytes 706568 | tf_op jit(solution)/shard_map/ppermute | solution.py:341

commit v12 on v11

--- a/solution.py
+++ b/solution.py
@@ -120,7 +120,7 @@
             cot_t[2 * q * part:(2 * q + 2) * part] = jnp.concatenate(pair).astype(BF16)
 
 
-def grad_kernel(cols, dev, acts, cot_t, *pieces):
+def grad_kernel(cols, carrier, dev, acts, cot_t, mine, theirs, *pieces):
     core = dev[0] % 2
     rows, width, chans = acts.shape[1] - 2, acts.shape[2], acts.shape[3]
     cells = rows * width
@@ -128,9 +128,10 @@
     def emit(window, place, wide):
         value = jnp.dot(cot_t[...], window, preferred_element_type=F32)
         at = 0
-        for piece in pieces:
-            piece[:, pl.ds(place, wide)] = value[at:at + piece.shape[0]].astype(BF16)
-            at += piece.shape[0]
+        for i, piece in enumerate(pieces):
+            count = piece.shape[0] - (2 * mine.shape[0] if i == carrier else 0)
+            piece[:count, pl.ds(place, wide)] = value[at:at + count].astype(BF16)
+            at += count
 
     def two_taps(k, _):
         taps, place = cols.pair(core, k, chans)
@@ -141,6 +142,8 @@
     lax.fori_loop(0, 2, two_taps, 0)
     place, channel = cols.middle(core, chans)
     emit(acts[1, 1:rows + 1, :, pl.ds(channel, cols.mid)].reshape(cells, cols.mid), place, cols.mid)
+    if carrier is not None:
+        pieces[carrier][-2 * mine.shape[0]:] = jnp.concatenate([mine[...], theirs[...]])
 
 
 class Stages:
@@ -321,12 +324,15 @@
     sums[1:2] = scale * jnp.sum(shifts, axis=0, keepdims=True)
 
 
-def finish_kernel(cols, dev, step, shard, mine, theirs, ours, aside, vectors, out, new_bias, new_gain, new_shift):
+def finish_kernel(cols, dev, step, shard, carried, ours, aside, vectors, out, new_bias, new_gain, new_shift):
     lower = dev[0] % 2 == 0
     rate = LR_KERNEL * (1.0 - (step[0] % 1000).astype(F32) / 2000.0)
     factor = 0.5 * cols.total ** (-0.5) * rate
-    here = 0.5 * mine[...].astype(F32) - factor * ours[...].astype(F32)
-    there = 0.5 * theirs[...].astype(F32) - factor * aside[...].astype(F32)
+    part = shard.shape[0]
+    peer = carried[-2 * part:].astype(F32)
+    mine, theirs = peer[:part], peer[part:]
+    here = 0.5 * mine - factor * ours[...].astype(F32)
+    there = 0.5 * theirs - factor * aside[...].astype(F32)
     left, right = jnp.where(lower, here, there), jnp.where(lower, there, here)
     out[:, :cols.lead] = 0.5 * shard[:, :cols.lead] + left
     out[:, cols.lead:] = 0.5 * shard[:, cols.lead:] + right[:, cols.both:]
@@ -430,7 +436,6 @@
         table = jnp.asarray(ring.table(part))
         order = (ring.count, part, 2 * ring.count)
         up1, down1 = ring.up(unit), ring.down(unit)
-        peer = swap(mine, "replica"), swap(theirs, "replica")
     else:
         table = jnp.zeros((replicas * zs * 4, 1), jnp.int32)
         order = None
@@ -456,14 +461,14 @@
         [pltpu.VMEM((chans, 2 * cells), F32)],
         8, flops // 4,
     )(dev, table, latent, lat_far, cot_b, cot_far, gn_gain, gn_shift)
-    counts = [zs] + [1] * zs if paired else [2 * zs]
+    counts = [zs, 1, 2] + [1] * (zs - 2) if paired else [2 * zs]
     pieces = call(
-        partial(grad_kernel, cols),
+        partial(grad_kernel, cols, 2 if paired else None),
         [jax.ShapeDtypeStruct((n * 2 * part, cols.lead), BF16) for n in counts],
-        [SMEM_SPEC] + [VMEM_SPEC] * 2,
+        [SMEM_SPEC] + [VMEM_SPEC] * 4,
         [],
         4, flops // 2,
-    )(dev, acts, cot_t)
+    )(dev, acts, cot_t, mine, theirs)
     stages = Stages([2 * zs - 3, 3] if paired else [1], 2 * part if paired else chans)
     staged = paired
 
@@ -517,35 +522,39 @@
 
     if paired:
         kept, *sent = pieces
-        up, down, sent[0], mine, theirs = tied(up1, down1, sent[0], *peer)
+        crossed = [swap(piece, "replica") for piece in sent]
+
+        def ring_sums(j, *received):
+            parts = kept[2 * j * part:(2 * j + 2) * part], crossed[j]
+            ahead, behind = (tuple(x[at:at + part] for x in parts) for at in (0, part))
+            ahead = add(*ahead, *received[:1])
+            behind = behind + tuple(received[1:])
+            return ahead, add(*behind) if j < zs - 1 else behind
+
+        def ring_step(ahead, behind):
+            return ring.up(ahead), ring.down(behind)
+
+        up, down, _ = tied(up1, down1, sent[0])
         blocks = [unit, up, down]
-        crossed = [swap(piece, "replica") for piece in sent]
         up, down = ring.up(up), ring.down(down)
-        up, down, cots, *slopes, order = tied(up, down, *slopes_of(stats))
+        cots, *slopes, order = slopes_of(stats)
+        up, down, cots, *slopes, order = tied(up, down, cots, *slopes, order)
         blocks += [up, down]
-
-        def ring_step(j, *received):
-            parts = kept[2 * j * part:(2 * j + 2) * part], crossed[j]
-            ahead, behind = (tuple(x[half] for x in parts) for half in (slice(part), slice(part, None)))
-            up_sum = ring.up(add(*ahead, *received[:1]))
-            if j < zs - 1:
-                return up_sum, ring.down(add(*behind, *received[1:]))
-            return up_sum, behind + tuple(received[1:])
 
         up, down = ring.up(up), ring.down(down)
         conv_first_own, conv_send = conv_first(blocks)
         crossed[0], conv_send = tied(crossed[0], conv_send)
-        received = ring_step(0)
+        received = ring_step(*ring_sums(0))
         cots, conv_send = tied(cots, conv_send)
         first_sums = back(0, cots, slopes, blocks)
-        up, down, first_sums, crossed[1] = tied(up, down, first_sums, crossed[1])
+        up, down, first_sums = tied(up, down, first_sums)
         late = [up, down]
 
         halves = ring.up(up[:part]), ring.down(down[part:])
         conv_send, *received = tied(conv_send, *received)
         conv_first_got = swap(conv_send, "core")
         for j in range(1, zs - 2):
-            received = ring_step(j, *received)
+            received = ring_step(*ring_sums(j, *received))
         late += halves
 
         conv_send = conv_far(acts, late)
@@ -553,28 +562,30 @@
         conv_got = swap(conv_send, "core")
         sums = back(1, cots, slopes, late)
         crossed[-2], sums, *received = tied(crossed[-2], sums, *received)
-        received = ring_step(zs - 2, *received)
-        vectors = hop(chip_sum(first_sums + sums), "replica", 1)
-        vectors = hop(vectors, "z", 1)
-        crossed[-1], conv_got, vectors, *received = tied(crossed[-1], conv_got, vectors, *received)
-        last, behind = ring_step(zs - 1, *received)
+        received = ring_step(*ring_sums(zs - 2, *received))
+        vectors = chip_sum(first_sums + sums)
+        conv_got, vectors = tied(conv_got, vectors)
         block = conv_own(conv_got, [conv_first_own, conv_first_got, order], late)
+        vectors = hop(hop(vectors, "replica", 1), "z", 1)
+        crossed[-1], block, vectors, *received = tied(crossed[-1], block, vectors, *received)
+        ahead, behind = ring_sums(zs - 1, *received)
+        last = ring.up(ahead)
         vectors = hop(vectors, "y", 1)
-        last, block, vectors = tied(last, block, vectors)
-        total = add(*behind, last)
         reach = 2
         while reach < zs:
             vectors = hop(vectors, "z", reach)
             reach *= 2
-        across, vectors = tied(swap(total, "replica"), vectors)
+        last, vectors = tied(last, vectors)
+        total = add(*behind, last)
+        across = swap(total, "replica")
         ours, others = jnp.where(same, total, across), jnp.where(same, across, total)
         aside = swap(others, "core")
         vector = jax.ShapeDtypeStruct((1, chans), F32)
         new_kernel, *new_v = call(
             partial(finish_kernel, cols),
             (jax.ShapeDtypeStruct(shard.shape, F32), vector, vector, vector),
-            [SMEM_SPEC] * 2 + [VMEM_SPEC] * 6, [], 8, flops // 16,
-        )(dev, step, shard, mine, theirs, ours, aside, vectors)
+            [SMEM_SPEC] * 2 + [VMEM_SPEC] * 5, [], 8, flops // 16,
+        )(dev, step, shard, crossed[1], ours, aside, vectors)
     else:
         late = [lax.all_gather(unit, NODE, axis=0, tiled=True)]
         cots, slope, slope_x = slopes_of(stats)

time: 93.7 us -> 99.8 us (1.065)
  waiting for transfers between devices: 24 us -> 33.9 us
  starting transfers between devices: 31.3 us -> 27.5 us
    ppermute x8, starting transfers between devices: 13.8 us -> 6.59 us  [up(): return lax.ppermute(value, NODE, self.ahead)]
    ppermute x7, starting transfers between devices: 2.77 us -> 9.9 us  [down(): return lax.ppermute(value, NODE, self.behind)]
    ppermute x7, waiting for transfers between devices: 1.37 us -> 7.5 us  [down(): return lax.ppermute(value, NODE, self.behind)]
    ppermute x14 -> x12, waiting for transfers between devices: 4.26 us -> 9.28 us  [swap(): return lax.ppermute(value, axis, [(0, 1), (1, 0)])]
    ppermute x8, waiting for transfers between devices: 8.08 us -> 4.91 us  [up(): return lax.ppermute(value, NODE, self.ahead)]
    ppermute x14 -> x12, starting transfers between devices: 9.73 us -> 7.49 us  [swap(): return lax.ppermute(value, axis, [(0, 1), (1, 0)])]
    ppermute x4, waiting for transfers between devices: 10.3 us -> 12.2 us  [hop(): lax.ppermute(value, axis, [(s, s ^ mask) for s in range(count)])]
    ppermute x4, starting transfers between devices: 4.97 us -> 3.53 us  [hop(): lax.ppermute(value, axis, [(s, s ^ mask) for s in range(count)])]
  transfers between devices with their start and end apart: 33 -> 31, of which waited for: 12 -> 13; matrix products, arithmetic and copies ran while one was open for 3% -> 3% of each run, Pallas kernels for 33% -> 31%
where the time goes in v12:
time: 99.8 us; the launch traced here: 99.7 us
  waiting for transfers between devices  33.9 us (34%)
  Pallas kernels  32.4 us (32%)
  starting transfers between devices  27.5 us (28%)
  other arithmetic  2.92 us (3%)
  between operations  1.56 us (2%)
  local copies, waits for them, and re-layouts  1.35 us (1%)
    ppermute x4, waiting for transfers between devices, hop(): lax.ppermute(value, axis, [(s, s ^ mask) for s in range(count)])  12.2 us
    ppermute x7, starting transfers between devices, down(): return lax.ppermute(value, NODE, self.behind)  9.9 us
    ppermute x12, waiting for transfers between devices, swap(): return lax.ppermute(value, axis, [(0, 1), (1, 0)])  9.28 us
    pallas_call x2, Pallas kernels, back(): call(partial(back_kernel, cols, stages, stage), jax.ShapeDtypeStruct((2,...  8.62 us
    ppermute x7, waiting for transfers between devices, down(): return lax.ppermute(value, NODE, self.behind)  7.5 us
    ppermute x12, starting transfers between devices, swap(): return lax.ppermute(value, axis, [(0, 1), (1, 0)])  7.49 us
    ppermute x8, starting transfers between devices, up(): return lax.ppermute(value, NODE, self.ahead)  6.59 us
    ppermute x8, waiting for transfers between devices, up(): return lax.ppermute(value, NODE, self.ahead)  4.91 us
  transfers between devices with their start and end apart: 31, of which 13 were waited for; matrix products, arithmetic and copies ran while one was open for 3% of the time, Pallas kernels for 31%

profile of v12, /device:TPU:0, one launch (start us, length us, event | category | flops | bytes accessed | tf_op | source)
XLA Modules:
  0.0 99.7 jit_solution(4732546644509069202)
XLA Ops:
  0.7 1.3 %fusion.1 = (bf16[40,2944]{1,0:T(8,128)(2,1)S(1)}, bf16[40,2944]{1,0:T(8,128)(2,1)S(1)}) fusion(f32[1,40,5760]{2,1,0:T(8,128)} %param.10, s32[]{:T(128)S(6)} %select_n.27, s32[]{:T(128)S(6)} %select_n.26), kind=kLoop, calls=%fused_computation.13 | loop fusion | bytes 942088 | tf_op jit(solution)/shard_map/convert_element_type | solution.py:428
  2.0 0.5 collective-permute-start.3
  2.5 2.0 %fusion.3 = (f32[640]{0:T(1024)S(1)}, bf16[16,32,640]{2,1,0:T(8,128)(2,1)S(1)}) fusion(f32[1,16,32,640]{3,2,1,0:T(8,128)} %param.9), kind=kLoop, calls=%fused_computation.19 | loop fusion | flops 654720 | bytes 1968640 | tf_op jit(solution)/shard_map/reduce_sum | solution.py:519
  4.6 0.5 collective-permute-start
  5.1 2.7 %collective-permute-start.5 = (bf16[80,2944]{1,0:T(8,128)(2,1)S(1)}, bf16[80,2944]{1,0:T(8,128)(2,1)S(1)}, u32[]{:S(2)}, u32[]{:S(2)}) collective-permute-start(bf16[80,2944]{1,0:T(8,128)(2,1)S(1)} %maximum_select_fusion.refs_0_), channel_id=1, source_target_pairs={{4,0},{8,4},{12,8},{14,12},{10,14},{6,10},{2,6},{0,2},{5,1},{9,5},... | collective-permute-start | bytes 1413128 | tf_op jit(solution)/shard_map/ppermute | solution.py:375
  7.9 4.4 %shard_map.119 = (f32[2,640]{1,0:T(2,128)S(1)}, bf16[3,34,32,640]{3,2,1,0:T(8,128)(2,1)S(1)}, bf16[640,1024]{1,0:T(8,128)(2,1)S(1)}) custom-call(s32[1]{0:T(128)} %bitcast.dev, s32[32,24]{1,0:T(8,128)S(1)} %copy-done.5, bf16[16,32,640]{2,1,0:T(8,128)(2,1)S(1)} %bitcast.13, bf16[16,32,640]{2,1,0:T(8,128)(2,1)S(1)} %collective-permute-done.lat_far, ...), custom_call_target="tpu_custom_call" | custom-call | flops 964689920 | tf_op jit(solution)/shard_map/pallas_call | solution.py:457
  12.3 4.7 %shard_map.120 = (bf16[320,2944]{1,0:T(8,128)(2,1)S(1)}, bf16[80,2944]{1,0:T(8,128)(2,1)S(1)}, bf16[160,2944]{1,0:T(8,128)(2,1)S(1)}, bf16[80,2944]{1,0:T(8,128)(2,1)S(1)}, bf16[80,2944]{1,0:T(8,128)(2,1)S(1)}) custom-call(s32[1]{0:T(128)} %bitcast.dev, bf16[3,34,32,640]{3,2,1,0:T(8,128)(2,1)S(1)} %get-tuple-element.61.acts, ...), custom_call_target="tpu_custom_call" | custom-call | flops 1929379840 | tf_op jit(solution)/shard_map/pallas_call | solution.py:465
  17.0 2.2 %collective-permute-done.5.refs_2_ = bf16[80,2944]{1,0:T(8,128)(2,1)S(1)} collective-permute-done((bf16[80,2944]{1,0:T(8,128)(2,1)S(1)}, bf16[80,2944]{1,0:T(8,128)(2,1)S(1)}, u32[]{:S(2)}, u32[]{:S(2)}) %collective-permute-start.5) | collective-permute-done | bytes 471072 | tf_op jit(solution)/shard_map/ppermute | solution.py:375
  19.2 1.4 %collective-permute-done.4.refs_1_ = bf16[80,2944]{1,0:T(8,128)(2,1)S(1)} collective-permute-done((bf16[80,2944]{1,0:T(8,128)(2,1)S(1)}, bf16[80,2944]{1,0:T(8,128)(2,1)S(1)}, u32[]{:S(2)}, u32[]{:S(2)}) %collective-permute-start.4) | collective-permute-done | bytes 471072 | tf_op jit(solution)/shard_map/ppermute | solution.py:372
  21.0 1.6 %collective-permute-start.7 = (bf16[80,2944]{1,0:T(8,128)(2,1)S(1)}, bf16[80,2944]{1,0:T(8,128)(2,1)S(1)}, u32[]{:S(2)}, u32[]{:S(2)}) collective-permute-start(bf16[80,2944]{1,0:T(8,128)(2,1)S(1)} %collective-permute-done.5.refs_2_), channel_id=1, source_target_pairs={{4,0},{8,4},{12,8},{14,12},{10,14},{6,10},{2,6},{0,2},{5,1},{9,5},... | collective-permute-start | bytes 1413128 | tf_op jit(solution)/shard_map/ppermute | solution.py:375
  22.6 1.5 %collective-permute-start.8 = (bf16[80,2944]{1,0:T(8,128)(2,1)S(1)}, bf16[80,2944]{1,0:T(8,128)(2,1)S(1)}, u32[]{:S(2)}, u32[]{:S(2)}) collective-permute-start(bf16[80,2944]{1,0:T(8,128)(2,1)S(1)} %get-tuple-element.66), channel_id=1, source_target_pairs={{0,16},{16,0},{1,17},{17,1},{2,18},{18,2},{3,19},{19,3},{4,20},{20... | collective-permute-start | bytes 1413128 | tf_op jit(solution)/shard_map/ppermute | solution.py:347
  24.1 0.5 collective-permute-start.15
  24.7 4.5 %shard_map.121 = (bf16[3,34,32,768]{3,2,1,0:T(8,128)(2,1)S(1)}, bf16[32,32,640]{2,1,0:T(8,128)(2,1)S(1)}, bf16[32,32,640]{2,1,0:T(8,128)(2,1)S(1)}, bf16[640,768]{1,0:T(8,128)(2,1)S(1)}) custom-call(s32[1]{0:T(128)} %bitcast.dev, s32[32,24]{1,0:T(8,128)S(1)} %copy-done.5, f32[2,640]{1,0:T(2,128)S(1)} %get-tuple-element.69.stats, f32[1,640]{1,0:T(1,128)S(1)} %copy-done.3, ...), custom_call_target="tpu_custom_call" | custom-call | flops 964689920 | tf_op jit(solution)/shard_map/pallas_call | solution.py:477
  29.2 3.5 %collective-permute-done.6.refs_3_ = bf16[80,2944]{1,0:T(8,128)(2,1)S(1)} collective-permute-done((bf16[80,2944]{1,0:T(8,128)(2,1)S(1)}, bf16[80,2944]{1,0:T(8,128)(2,1)S(1)}, u32[]{:S(2)}, u32[]{:S(2)}) %collective-permute-start.6) | collective-permute-done | bytes 471072 | tf_op jit(solution)/shard_map/ppermute | solution.py:372
  32.6 0.4 collective-permute-done.7.refs_4_
  33.1 1.5 %collective-permute-start.9 = (bf16[80,2944]{1,0:T(8,128)(2,1)S(1)}, bf16[80,2944]{1,0:T(8,128)(2,1)S(1)}, u32[]{:S(2)}, u32[]{:S(2)}) collective-permute-start(bf16[80,2944]{1,0:T(8,128)(2,1)S(1)} %collective-permute-done.6.refs_3_), channel_id=1, source_target_pairs={{0,4},{4,8},{8,12},{12,14},{14,10},{10,6},{6,2},{2,0},{1,5},{5,9},... | collective-permute-start | bytes 1413128 | tf_op jit(solution)/shard_map/ppermute | solution.py:372
  34.6 0.5 collective-permute-start.10
  35.1 4.0 %shard_map.122 = (f32[512,512]{1,0:T(8,128)S(1)}, bf16[512,512]{1,0:T(8,128)(2,1)S(1)}) custom-call(s32[1]{0:T(128)} %bitcast.dev, bf16[3,34,32,640]{3,2,1,0:T(8,128)(2,1)S(1)} %get-tuple-element.61.acts, bf16[80,2944]{1,0:T(8,128)(2,1)S(1)} %maximum_select_fusion.refs_0_, bf16[80,2944]{1,0:T(8,128)(2,1)S(1)} %collective-permute-done.4.refs_1_, ...), custom_call_target="tpu_custom_call" | custom-call | flops 964689920 | tf_op jit(solution)/shard_map/pallas_call | solution.py:495
  39.2 1.4 %collective-permute-start.17 = (bf16[40,2944]{1,0:T(8,128)(2,1)S(1)}, bf16[40,2944]{1,0:T(8,128)(2,1)S(1)}, u32[]{:S(2)}, u32[]{:S(2)}) collective-permute-start(bf16[40,2944]{1,0:T(8,128)(2,1)S(1)} %get-tuple-element.119), channel_id=1, source_target_pairs={{4,0},{8,4},{12,8},{14,12},{10,14},{6,10},{2,6},{0,2},{5,1},{9,5},... | collective-permute-start | bytes 706568 | tf_op jit(solution)/shard_map/ppermute | solution.py:375
  40.6 0.7 collective-permute-start.16
  41.3 5.4 %shard_map.123 = f32[2,640]{1,0:T(2,128)S(1)} custom-call(s32[1]{0:T(128)} %bitcast.dev, bf16[3,34,32,768]{3,2,1,0:T(8,128)(2,1)S(1)} %get-tuple-element.87.cots, bf16[32,32,640]{2,1,0:T(8,128)(2,1)S(1)} %get-tuple-element.80.slope, bf16[32,32,640]{2,1,0:T(8,128)(2,1)S(1)} %get-tuple-element.81.slope_x, bf16[80,2944]{1,0:T(8,128)(2,1)S(1)} %maximum_select_fusion.refs_0_, ...), custom_call_target="tpu_custom_call" | custom-call | flops 964689920 | tf_op jit(solution)/shard_map/pallas_call | solution.py:487
  46.7 3.6 %collective-permute-done.17 = bf16[40,2944]{1,0:T(8,128)(2,1)S(1)} collective-permute-done((bf16[40,2944]{1,0:T(8,128)(2,1)S(1)}, bf16[40,2944]{1,0:T(8,128)(2,1)S(1)}, u32[]{:S(2)}, u32[]{:S(2)}) %collective-permute-start.17) | collective-permute-done | bytes 235552 | tf_op jit(solution)/shard_map/ppermute | solution.py:375
  50.3 1.5 %collective-permute-start.14 = (bf16[80,2944]{1,0:T(8,128)(2,1)S(1)}, bf16[80,2944]{1,0:T(8,128)(2,1)S(1)}, u32[]{:S(2)}, u32[]{:S(2)}) collective-permute-start(bf16[80,2944]{1,0:T(8,128)(2,1)S(1)} %get-tuple-element.86), channel_id=1, source_target_pairs={{0,16},{16,0},{1,17},{17,1},{2,18},{18,2},{3,19},{19,3},{4,20},{20... | collective-permute-start | bytes 1413128 | tf_op jit(solution)/shard_map/ppermute | solution.py:347
  51.9 0.5 collective-permute-start.12
  52.4 1.6 %collective-permute-start.11 = (bf16[40,2944]{1,0:T(8,128)(2,1)S(1)}, bf16[40,2944]{1,0:T(8,128)(2,1)S(1)}, u32[]{:S(2)}, u32[]{:S(2)}) collective-permute-start(bf16[40,2944]{1,0:T(8,128)(2,1)S(1)} %slice.66), channel_id=1, source_target_pairs={{0,4},{4,8},{8,12},{12,14},{14,10},{10,6},{6,2},{2,0},{1,5},{5,9},... | collective-permute-start | bytes 706568 | tf_op jit(solution)/shard_map/ppermute | solution.py:372
  54.0 2.6 %collective-permute-done.15.carried = bf16[160,2944]{1,0:T(8,128)(2,1)S(1)} collective-permute-done((bf16[160,2944]{1,0:T(8,128)(2,1)S(1)}, bf16[160,2944]{1,0:T(8,128)(2,1)S(1)}, u32[]{:S(2)}, u32[]{:S(2)}) %collective-permute-start.15) | collective-permute-done | bytes 942112 | tf_op jit(solution)/shard_map/ppermute | solution.py:347
  56.8 1.6 %collective-permute-start.19 = (bf16[40,2944]{1,0:T(8,128)(2,1)S(1)}, bf16[40,2944]{1,0:T(8,128)(2,1)S(1)}, u32[]{:S(2)}, u32[]{:S(2)}) collective-permute-start(bf16[40,2944]{1,0:T(8,128)(2,1)S(1)} %get-tuple-element.115), channel_id=1, source_target_pairs={{4,0},{8,4},{12,8},{14,12},{10,14},{6,10},{2,6},{0,2},{5,1},{9,5},... | collective-permute-start | bytes 706568 | tf_op jit(solution)/shard_map/ppermute | solution.py:375
  58.4 0.5 collective-permute-start.18
  58.8 1.2 %collective-permute-done.12.refs_3_.refs_6_ = bf16[40,2944]{1,0:T(8,128)(2,1)S(1)} collective-permute-done((bf16[40,2944]{1,0:T(8,128)(2,1)S(1)}, bf16[40,2944]{1,0:T(8,128)(2,1)S(1)}, u32[]{:S(2)}, u32[]{:S(2)}) %collective-permute-start.12) | collective-permute-done | bytes 235552 | tf_op jit(solution)/shard_map/ppermute | solution.py:375
  60.0 0.7 collective-permute-start.2
  60.7 1.4 %shard_map.124 = bf16[512,256]{1,0:T(8,128)(2,1)S(1)} custom-call(s32[1]{0:T(128)} %bitcast.dev, bf16[3,34,32,640]{3,2,1,0:T(8,128)(2,1)S(1)} %get-tuple-element.61.acts, bf16[80,2944]{1,0:T(8,128)(2,1)S(1)} %collective-permute-done.9.refs_0_.refs_3_, bf16[80,2944]{1,0:T(8,128)(2,1)S(1)} %collective-permute-done.10.refs_1_.refs_4_, ...), custom_call_target="tpu_custom_call" | custom-call | flops 482344960 | tf_op jit(solution)/shard_map/pallas_call | solution.py:504
  62.2 3.2 %shard_map.125 = f32[2,640]{1,0:T(2,128)S(1)} custom-call(s32[1]{0:T(128)} %bitcast.dev, bf16[3,34,32,768]{3,2,1,0:T(8,128)(2,1)S(1)} %get-tuple-element.87.cots, bf16[32,32,640]{2,1,0:T(8,128)(2,1)S(1)} %get-tuple-element.80.slope, bf16[32,32,640]{2,1,0:T(8,128)(2,1)S(1)} %get-tuple-element.81.slope_x, ...), custom_call_target="tpu_custom_call" | custom-call | flops 964689920 | tf_op jit(solution)/shard_map/pallas_call | solution.py:487
  65.4 1.2 %collective-permute-done.14 = bf16[80,2944]{1,0:T(8,128)(2,1)S(1)} collective-permute-done((bf16[80,2944]{1,0:T(8,128)(2,1)S(1)}, bf16[80,2944]{1,0:T(8,128)(2,1)S(1)}, u32[]{:S(2)}, u32[]{:S(2)}) %collective-permute-start.14) | collective-permute-done | bytes 471072 | tf_op jit(solution)/shard_map/ppermute | solution.py:347
  66.7 0.6 collective-permute-start.20
  67.5 1.6 %collective-permute-start.25 = (bf16[40,2944]{1,0:T(8,128)(2,1)S(1)}, bf16[40,2944]{1,0:T(8,128)(2,1)S(1)}, u32[]{:S(2)}, u32[]{:S(2)}) collective-permute-start(bf16[40,2944]{1,0:T(8,128)(2,1)S(1)} %get-tuple-element.117), channel_id=1, source_target_pairs={{4,0},{8,4},{12,8},{14,12},{10,14},{6,10},{2,6},{0,2},{5,1},{9,5},... | collective-permute-start | bytes 706568 | tf_op jit(solution)/shard_map/ppermute | solution.py:375
  69.1 0.5 collective-permute-start.24
  69.6 1.6 %collective-permute-start.22 = (f32[3,640]{1,0:T(4,128)S(1)}, f32[3,640]{1,0:T(4,128)S(1)}, u32[]{:S(2)}, u32[]{:S(2)}) collective-permute-start(f32[3,640]{1,0:T(4,128)S(1)} %fusion.4), channel_id=1, source_target_pairs={{0,16},{16,0},{1,17},{17,1},{2,18},{18,2},{3,19},{19,3},{4,20},{20... | collective-permute-start | bytes 23048 | tf_op jit(solution)/shard_map/ppermute | solution.py:396
  71.1 3.6 %collective-permute-done.22 = f32[3,640]{1,0:T(4,128)S(1)} collective-permute-done((f32[3,640]{1,0:T(4,128)S(1)}, f32[3,640]{1,0:T(4,128)S(1)}, u32[]{:S(2)}, u32[]{:S(2)}) %collective-permute-start.22) | collective-permute-done | bytes 7712 | tf_op jit(solution)/shard_map/ppermute | solution.py:396
  74.7 0.7 collective-permute-start.23
  75.4 3.7 %shard_map.126 = bf16[16,32,640]{2,1,0:T(8,128)(2,1)} custom-call(s32[1]{0:T(128)} %bitcast.dev, bf16[3,34,32,640]{3,2,1,0:T(8,128)(2,1)S(1)} %get-tuple-element.61.acts, bf16[512,256]{1,0:T(8,128)(2,1)S(1)} %collective-permute-done.13.got, bf16[16,32,640]{2,1,0:T(8,128)(2,1)S(1)} %bitcast.15, f32[1,640]{1,0:T(1,128)S(1)} %copy-done.2, ...), custom_call_target="tpu_custom_call" | custom-call | flops 964689920 | tf_op jit(solution)/shard_map/pallas_call | solution.py:512
  79.3 1.4 %collective-permute-start.26 = (bf16[40,2944]{1,0:T(8,128)(2,1)S(1)}, bf16[40,2944]{1,0:T(8,128)(2,1)S(1)}, u32[]{:S(2)}, u32[]{:S(2)}) collective-permute-start(bf16[40,2944]{1,0:T(8,128)(2,1)S(1)} %add_convert_fusion.1), channel_id=1, source_target_pairs={{0,4},{4,8},{8,12},{12,14},{14,10},{10,6},{6,2},{2,0},{1,5},{5,9},... | collective-permute-start | bytes 706568 | tf_op jit(solution)/shard_map/ppermute | solution.py:372
  80.6 1.2 %collective-permute-start.27 = (f32[3,640]{1,0:T(4,128)S(1)}, f32[3,640]{1,0:T(4,128)S(1)}, u32[]{:S(2)}, u32[]{:S(2)}) collective-permute-start(f32[3,640]{1,0:T(4,128)S(1)} %add.92), channel_id=1, source_target_pairs={{0,2},{2,0},{1,3},{3,1},{4,6},{6,4},{5,7},{7,5},{8,10},{10,8},{9,1... | collective-permute-start | bytes 23048 | tf_op jit(solution)/shard_map/ppermute | solution.py:396
  81.8 4.1 %collective-permute-done.27 = f32[3,640]{1,0:T(4,128)S(1)} collective-permute-done((f32[3,640]{1,0:T(4,128)S(1)}, f32[3,640]{1,0:T(4,128)S(1)}, u32[]{:S(2)}, u32[]{:S(2)}) %collective-permute-start.27) | collective-permute-done | bytes 7712 | tf_op jit(solution)/shard_map/ppermute | solution.py:396
  86.0 4.5 %collective-permute-done.28 = f32[3,640]{1,0:T(4,128)S(1)} collective-permute-done((f32[3,640]{1,0:T(4,128)S(1)}, f32[3,640]{1,0:T(4,128)S(1)}, u32[]{:S(2)}, u32[]{:S(2)}) %collective-permute-start.28) | collective-permute-done | bytes 7712 | tf_op jit(solution)/shard_map/ppermute | solution.py:396
  90.7 1.6 %collective-permute-start.29 = (bf16[40,2944]{1,0:T(8,128)(2,1)S(1)}, bf16[40,2944]{1,0:T(8,128)(2,1)S(1)}, u32[]{:S(2)}, u32[]{:S(2)}) collective-permute-start(bf16[40,2944]{1,0:T(8,128)(2,1)S(1)} %add_convert_fusion), channel_id=1, source_target_pairs={{0,16},{16,0},{1,17},{17,1},{2,18},{18,2},{3,19},{19,3},{4,20},{20... | collective-permute-start | bytes 706568 | tf_op jit(solution)/shard_map/ppermute | solution.py:347
  92.2 4.6 %collective-permute-done.29 = bf16[40,2944]{1,0:T(8,128)(2,1)S(1)} collective-permute-done((bf16[40,2944]{1,0:T(8,128)(2,1)S(1)}, bf16[40,2944]{1,0:T(8,128)(2,1)S(1)}, u32[]{:S(2)}, u32[]{:S(2)}) %collective-permute-start.29) | collective-permute-done | bytes 235552 | tf_op jit(solution)/shard_map/ppermute | solution.py:347
  97.6 0.8 collective-permute-done.30.aside
  98.4 1.2 %shard_map.127 = (f32[40,5760]{1,0:T(8,128)}, f32[1,640]{1,0:T(1,128)}, f32[1,640]{1,0:T(1,128)}, f32[1,640]{1,0:T(1,128)}) custom-call(s32[1]{0:T(128)} %bitcast.dev, s32[1]{0:T(128)S(6)} %copy.13.step, f32[40,5760]{1,0:T(8,128)S(1)} %bitcast.11, bf16[160,2944]{1,0:T(8,128)(2,1)S(1)} %collective-permute-done.15.carried, ...), custom_call_target="tpu_custom_call" | custom-call | flops 241172480 | tf_op jit(solution)/shard_map/pallas_call | solution.py:584
  (54 shorter events, 1.8 us)
Async XLA Ops:
  0.6 3.9 %copy-start.1 = (bf16[1,16,32,640]{3,2,1,0:T(8,128)(2,1)S(1)}, bf16[1,16,32,640]{3,2,1,0:T(8,128)(2,1)}, u32[]{:S(2)}) copy-start(bf16[1,16,32,640]{3,2,1,0:T(8,128)(2,1)} %param.8) | copy-start | bytes 1966084
  0.7 7.2 %copy-start.3 = (f32[1,640]{1,0:T(1,128)S(1)}, f32[1,640]{1,0:T(1,128)}, u32[]{:S(2)}) copy-start(f32[1,640]{1,0:T(1,128)} %gain.3) | copy-start | bytes 7684
  0.7 7.2 %copy-start.4 = (f32[1,640]{1,0:T(1,128)S(1)}, f32[1,640]{1,0:T(1,128)}, u32[]{:S(2)}) copy-start(f32[1,640]{1,0:T(1,128)} %shift.3) | copy-start | bytes 7684
  0.7 7.2 %copy-start.5 = (s32[32,24]{1,0:T(8,128)S(1)}, s32[32,24]{1,0:T(8,128)}, u32[]{:S(2)}) copy-start(s32[32,24]{1,0:T(8,128)} %constant.38.clone.table) | copy-start | bytes 9220
  2.0 3.1 %collective-permute-start.3 = (bf16[40,2944]{1,0:T(8,128)(2,1)S(1)}, bf16[40,2944]{1,0:T(8,128)(2,1)S(1)}, u32[]{:S(2)}, u32[]{:S(2)}) collective-permute-start(bf16[40,2944]{1,0:T(8,128)(2,1)S(1)} %get-tuple-element.123.theirs), channel_id=1, source_target_pairs={{0,1},{1,0},{2,3},{3,2},{4,5},{5,4},{6,7},{7,6},{8,9},{9,8},{10,11... | collective-permute-start | bytes 706568 | tf_op jit(solution)/shard_map/ppermute | solution.py:347
  4.5 3.4 %collective-permute-start.1 = (bf16[16,32,640]{2,1,0:T(8,128)(2,1)S(1)}, bf16[16,32,640]{2,1,0:T(8,128)(2,1)S(1)}, u32[]{:S(2)}, u32[]{:S(2)}) collective-permute-start(bf16[16,32,640]{2,1,0:T(8,128)(2,1)S(1)} %get-tuple-element.122.cot_own), channel_id=1, source_target_pairs={{0,1},{1,0},{2,3},{3,2},{4,5},{5,4},{6,7},{7,6},{8,9},{9,8},{10,11... | collective-permute-start | bytes 1966088 | tf_op jit(solution)/shard_map/ppermute | solution.py:347
  4.6 3.3 %collective-permute-start = (bf16[16,32,640]{2,1,0:T(8,128)(2,1)S(1)}, bf16[16,32,640]{2,1,0:T(8,128)(2,1)S(1)}, u32[]{:S(2)}, u32[]{:S(2)}) collective-permute-start(bf16[16,32,640]{2,1,0:T(8,128)(2,1)S(1)} %bitcast.12), channel_id=1, source_target_pairs={{0,1},{1,0},{2,3},{3,2},{4,5},{5,4},{6,7},{7,6},{8,9},{9,8},{10,11... | collective-permute-start | bytes 1966088 | tf_op jit(solution)/shard_map/ppermute | solution.py:347
  5.1 14.1 %collective-permute-start.5 = (bf16[80,2944]{1,0:T(8,128)(2,1)S(1)}, bf16[80,2944]{1,0:T(8,128)(2,1)S(1)}, u32[]{:S(2)}, u32[]{:S(2)}) collective-permute-start(bf16[80,2944]{1,0:T(8,128)(2,1)S(1)} %maximum_select_fusion.refs_0_), channel_id=1, source_target_pairs={{4,0},{8,4},{12,8},{14,12},{10,14},{6,10},{2,6},{0,2},{5,1},{9,5},... | collective-permute-start | bytes 1413128 | tf_op jit(solution)/shard_map/ppermute | solution.py:375
  7.8 12.8 %collective-permute-start.4 = (bf16[80,2944]{1,0:T(8,128)(2,1)S(1)}, bf16[80,2944]{1,0:T(8,128)(2,1)S(1)}, u32[]{:S(2)}, u32[]{:S(2)}) collective-permute-start(bf16[80,2944]{1,0:T(8,128)(2,1)S(1)} %maximum_select_fusion.refs_0_), channel_id=1, source_target_pairs={{0,4},{4,8},{8,12},{12,14},{14,10},{10,6},{6,2},{2,0},{1,5},{5,9},... | collective-permute-start | bytes 1413128 | tf_op jit(solution)/shard_map/ppermute | solution.py:372
  20.6 12.0 %collective-permute-start.6 = (bf16[80,2944]{1,0:T(8,128)(2,1)S(1)}, bf16[80,2944]{1,0:T(8,128)(2,1)S(1)}, u32[]{:S(2)}, u32[]{:S(2)}) collective-permute-start(bf16[80,2944]{1,0:T(8,128)(2,1)S(1)} %collective-permute-done.4.refs_1_), channel_id=1, source_target_pairs={{0,4},{4,8},{8,12},{12,14},{14,10},{10,6},{6,2},{2,0},{1,5},{5,9},... | collective-permute-start | bytes 1413128 | tf_op jit(solution)/shard_map/ppermute | solution.py:372
  21.0 12.1 %collective-permute-start.7 = (bf16[80,2944]{1,0:T(8,128)(2,1)S(1)}, bf16[80,2944]{1,0:T(8,128)(2,1)S(1)}, u32[]{:S(2)}, u32[]{:S(2)}) collective-permute-start(bf16[80,2944]{1,0:T(8,128)(2,1)S(1)} %collective-permute-done.5.refs_2_), channel_id=1, source_target_pairs={{4,0},{8,4},{12,8},{14,12},{10,14},{6,10},{2,6},{0,2},{5,1},{9,5},... | collective-permute-start | bytes 1413128 | tf_op jit(solution)/shard_map/ppermute | solution.py:375
  22.6 16.4 %collective-permute-start.8 = (bf16[80,2944]{1,0:T(8,128)(2,1)S(1)}, bf16[80,2944]{1,0:T(8,128)(2,1)S(1)}, u32[]{:S(2)}, u32[]{:S(2)}) collective-permute-start(bf16[80,2944]{1,0:T(8,128)(2,1)S(1)} %get-tuple-element.66), channel_id=1, source_target_pairs={{0,16},{16,0},{1,17},{17,1},{2,18},{18,2},{3,19},{19,3},{4,20},{20... | collective-permute-start | bytes 1413128 | tf_op jit(solution)/shard_map/ppermute | solution.py:347
  24.1 32.4 %collective-permute-start.15 = (bf16[160,2944]{1,0:T(8,128)(2,1)S(1)}, bf16[160,2944]{1,0:T(8,128)(2,1)S(1)}, u32[]{:S(2)}, u32[]{:S(2)}) collective-permute-start(bf16[160,2944]{1,0:T(8,128)(2,1)S(1)} %get-tuple-element.89), channel_id=1, source_target_pairs={{0,16},{16,0},{1,17},{17,1},{2,18},{18,2},{3,19},{19,3},{4,20},{20... | collective-permute-start | bytes 2826248 | tf_op jit(solution)/shard_map/ppermute | solution.py:347
  33.1 18.8 %collective-permute-start.9 = (bf16[80,2944]{1,0:T(8,128)(2,1)S(1)}, bf16[80,2944]{1,0:T(8,128)(2,1)S(1)}, u32[]{:S(2)}, u32[]{:S(2)}) collective-permute-start(bf16[80,2944]{1,0:T(8,128)(2,1)S(1)} %collective-permute-done.6.refs_3_), channel_id=1, source_target_pairs={{0,4},{4,8},{8,12},{12,14},{14,10},{10,6},{6,2},{2,0},{1,5},{5,9},... | collective-permute-start | bytes 1413128 | tf_op jit(solution)/shard_map/ppermute | solution.py:372
  34.6 17.2 %collective-permute-start.10 = (bf16[80,2944]{1,0:T(8,128)(2,1)S(1)}, bf16[80,2944]{1,0:T(8,128)(2,1)S(1)}, u32[]{:S(2)}, u32[]{:S(2)}) collective-permute-start(bf16[80,2944]{1,0:T(8,128)(2,1)S(1)} %collective-permute-done.7.refs_4_), channel_id=1, source_target_pairs={{4,0},{8,4},{12,8},{14,12},{10,14},{6,10},{2,6},{0,2},{5,1},{9,5},... | collective-permute-start | bytes 1413128 | tf_op jit(solution)/shard_map/ppermute | solution.py:375
  39.2 11.1 %collective-permute-start.17 = (bf16[40,2944]{1,0:T(8,128)(2,1)S(1)}, bf16[40,2944]{1,0:T(8,128)(2,1)S(1)}, u32[]{:S(2)}, u32[]{:S(2)}) collective-permute-start(bf16[40,2944]{1,0:T(8,128)(2,1)S(1)} %get-tuple-element.119), channel_id=1, source_target_pairs={{4,0},{8,4},{12,8},{14,12},{10,14},{6,10},{2,6},{0,2},{5,1},{9,5},... | collective-permute-start | bytes 706568 | tf_op jit(solution)/shard_map/ppermute | solution.py:375
  40.6 11.2 %collective-permute-start.16 = (bf16[40,2944]{1,0:T(8,128)(2,1)S(1)}, bf16[40,2944]{1,0:T(8,128)(2,1)S(1)}, u32[]{:S(2)}, u32[]{:S(2)}) collective-permute-start(bf16[40,2944]{1,0:T(8,128)(2,1)S(1)} %get-tuple-element.120), channel_id=1, source_target_pairs={{0,4},{4,8},{8,12},{12,14},{14,10},{10,6},{6,2},{2,0},{1,5},{5,9},... | collective-permute-start | bytes 706568 | tf_op jit(solution)/shard_map/ppermute | solution.py:372
  50.3 16.3 %collective-permute-start.14 = (bf16[80,2944]{1,0:T(8,128)(2,1)S(1)}, bf16[80,2944]{1,0:T(8,128)(2,1)S(1)}, u32[]{:S(2)}, u32[]{:S(2)}) collective-permute-start(bf16[80,2944]{1,0:T(8,128)(2,1)S(1)} %get-tuple-element.86), channel_id=1, source_target_pairs={{0,16},{16,0},{1,17},{17,1},{2,18},{18,2},{3,19},{19,3},{4,20},{20... | collective-permute-start | bytes 1413128 | tf_op jit(solution)/shard_map/ppermute | solution.py:347
  51.9 8.1 %collective-permute-start.12 = (bf16[40,2944]{1,0:T(8,128)(2,1)S(1)}, bf16[40,2944]{1,0:T(8,128)(2,1)S(1)}, u32[]{:S(2)}, u32[]{:S(2)}) collective-permute-start(bf16[40,2944]{1,0:T(8,128)(2,1)S(1)} %slice.67), channel_id=1, source_target_pairs={{4,0},{8,4},{12,8},{14,12},{10,14},{6,10},{2,6},{0,2},{5,1},{9,5},... | collective-permute-start | bytes 706568 | tf_op jit(solution)/shard_map/ppermute | solution.py:375
  52.4 8.3 %collective-permute-start.11 = (bf16[40,2944]{1,0:T(8,128)(2,1)S(1)}, bf16[40,2944]{1,0:T(8,128)(2,1)S(1)}, u32[]{:S(2)}, u32[]{:S(2)}) collective-permute-start(bf16[40,2944]{1,0:T(8,128)(2,1)S(1)} %slice.66), channel_id=1, source_target_pairs={{0,4},{4,8},{8,12},{12,14},{14,10},{10,6},{6,2},{2,0},{1,5},{5,9},... | collective-permute-start | bytes 706568 | tf_op jit(solution)/shard_map/ppermute | solution.py:372
  56.8 9.9 %collective-permute-start.19 = (bf16[40,2944]{1,0:T(8,128)(2,1)S(1)}, bf16[40,2944]{1,0:T(8,128)(2,1)S(1)}, u32[]{:S(2)}, u32[]{:S(2)}) collective-permute-start(bf16[40,2944]{1,0:T(8,128)(2,1)S(1)} %get-tuple-element.115), channel_id=1, source_target_pairs={{4,0},{8,4},{12,8},{14,12},{10,14},{6,10},{2,6},{0,2},{5,1},{9,5},... | collective-permute-start | bytes 706568 | tf_op jit(solution)/shard_map/ppermute | solution.py:375
  58.4 8.3 %collective-permute-start.18 = (bf16[40,2944]{1,0:T(8,128)(2,1)S(1)}, bf16[40,2944]{1,0:T(8,128)(2,1)S(1)}, u32[]{:S(2)}, u32[]{:S(2)}) collective-permute-start(bf16[40,2944]{1,0:T(8,128)(2,1)S(1)} %get-tuple-element.116), channel_id=1, source_target_pairs={{0,4},{4,8},{8,12},{12,14},{14,10},{10,6},{6,2},{2,0},{1,5},{5,9},... | collective-permute-start | bytes 706568 | tf_op jit(solution)/shard_map/ppermute | solution.py:372
  60.0 19.1 %collective-permute-start.2 = (bf16[80,2944]{1,0:T(8,128)(2,1)S(1)}, bf16[80,2944]{1,0:T(8,128)(2,1)S(1)}, u32[]{:S(2)}, u32[]{:S(2)}) collective-permute-start(bf16[80,2944]{1,0:T(8,128)(2,1)S(1)} %get-tuple-element.64), channel_id=1, source_target_pairs={{0,16},{16,0},{1,17},{17,1},{2,18},{18,2},{3,19},{19,3},{4,20},{20... | collective-permute-start | bytes 1413128 | tf_op jit(solution)/shard_map/ppermute | solution.py:347
  60.7 14.7 %collective-permute-start.21 = (bf16[512,512]{1,0:T(8,128)(2,1)S(1)}, bf16[512,512]{1,0:T(8,128)(2,1)S(1)}, u32[]{:S(2)}, u32[]{:S(2)}) collective-permute-start(bf16[512,512]{1,0:T(8,128)(2,1)S(1)} %get-tuple-element.97), channel_id=1, source_target_pairs={{0,1},{1,0},{2,3},{3,2},{4,5},{5,4},{6,7},{7,6},{8,9},{9,8},{10,11... | collective-permute-start | bytes 1572872 | tf_op jit(solution)/shard_map/ppermute | solution.py:347
  62.2 4.5 %copy-start.2 = (f32[1,640]{1,0:T(1,128)S(1)}, f32[1,640]{1,0:T(1,128)}, u32[]{:S(2)}) copy-start(f32[1,640]{1,0:T(1,128)} %bias.1) | copy-start | bytes 7684
  66.6 2.9 %collective-permute-start.13 = (bf16[512,256]{1,0:T(8,128)(2,1)S(1)}, bf16[512,256]{1,0:T(8,128)(2,1)S(1)}, u32[]{:S(2)}, u32[]{:S(2)}) collective-permute-start(bf16[512,256]{1,0:T(8,128)(2,1)S(1)} %shard_map.124), channel_id=1, source_target_pairs={{0,1},{1,0},{2,3},{3,2},{4,5},{5,4},{6,7},{7,6},{8,9},{9,8},{10,11... | collective-permute-start | bytes 786440 | tf_op jit(solution)/shard_map/ppermute | solution.py:347
  66.7 2.4 %collective-permute-start.20 = (f32[3,640]{1,0:T(4,128)S(1)}, f32[3,640]{1,0:T(4,128)S(1)}, u32[]{:S(2)}, u32[]{:S(2)}) collective-permute-start(f32[3,640]{1,0:T(4,128)S(1)} %fusion.2), channel_id=1, source_target_pairs={{0,1},{1,0},{2,3},{3,2},{4,5},{5,4},{6,7},{7,6},{8,9},{9,8},{10,11... | collective-permute-start | bytes 23048 | tf_op jit(solution)/shard_map/ppermute | solution.py:347
  67.5 11.7 %collective-permute-start.25 = (bf16[40,2944]{1,0:T(8,128)(2,1)S(1)}, bf16[40,2944]{1,0:T(8,128)(2,1)S(1)}, u32[]{:S(2)}, u32[]{:S(2)}) collective-permute-start(bf16[40,2944]{1,0:T(8,128)(2,1)S(1)} %get-tuple-element.117), channel_id=1, source_target_pairs={{4,0},{8,4},{12,8},{14,12},{10,14},{6,10},{2,6},{0,2},{5,1},{9,5},... | collective-permute-start | bytes 706568 | tf_op jit(solution)/shard_map/ppermute | solution.py:375
  69.1 10.0 %collective-permute-start.24 = (bf16[40,2944]{1,0:T(8,128)(2,1)S(1)}, bf16[40,2944]{1,0:T(8,128)(2,1)S(1)}, u32[]{:S(2)}, u32[]{:S(2)}) collective-permute-start(bf16[40,2944]{1,0:T(8,128)(2,1)S(1)} %get-tuple-element.118), channel_id=1, source_target_pairs={{0,4},{4,8},{8,12},{12,14},{14,10},{10,6},{6,2},{2,0},{1,5},{5,9},... | collective-permute-start | bytes 706568 | tf_op jit(solution)/shard_map/ppermute | solution.py:372
  69.6 5.1 %collective-permute-start.22 = (f32[3,640]{1,0:T(4,128)S(1)}, f32[3,640]{1,0:T(4,128)S(1)}, u32[]{:S(2)}, u32[]{:S(2)}) collective-permute-start(f32[3,640]{1,0:T(4,128)S(1)} %fusion.4), channel_id=1, source_target_pairs={{0,16},{16,0},{1,17},{17,1},{2,18},{18,2},{3,19},{19,3},{4,20},{20... | collective-permute-start | bytes 23048 | tf_op jit(solution)/shard_map/ppermute | solution.py:396
  74.7 4.4 %collective-permute-start.23 = (f32[3,640]{1,0:T(4,128)S(1)}, f32[3,640]{1,0:T(4,128)S(1)}, u32[]{:S(2)}, u32[]{:S(2)}) collective-permute-start(f32[3,640]{1,0:T(4,128)S(1)} %add.91), channel_id=1, source_target_pairs={{0,4},{4,0},{8,12},{12,8},{1,5},{5,1},{9,13},{13,9},{2,6},{6,2},{1... | collective-permute-start | bytes 23048 | tf_op jit(solution)/shard_map/ppermute | solution.py:396
  79.1 19.3 %copy-start = (f32[1,40,5760]{2,1,0:T(8,128)S(1)}, f32[1,40,5760]{2,1,0:T(8,128)}, u32[]{:S(2)}) copy-start(f32[1,40,5760]{2,1,0:T(8,128)} %param.10) | copy-start | bytes 2764804
  79.3 11.3 %collective-permute-start.26 = (bf16[40,2944]{1,0:T(8,128)(2,1)S(1)}, bf16[40,2944]{1,0:T(8,128)(2,1)S(1)}, u32[]{:S(2)}, u32[]{:S(2)}) collective-permute-start(bf16[40,2944]{1,0:T(8,128)(2,1)S(1)} %add_convert_fusion.1), channel_id=1, source_target_pairs={{0,4},{4,8},{8,12},{12,14},{14,10},{10,6},{6,2},{2,0},{1,5},{5,9},... | collective-permute-start | bytes 706568 | tf_op jit(solution)/shard_map/ppermute | solution.py:372
  80.6 5.3 %collective-permute-start.27 = (f32[3,640]{1,0:T(4,128)S(1)}, f32[3,640]{1,0:T(4,128)S(1)}, u32[]{:S(2)}, u32[]{:S(2)}) collective-permute-start(f32[3,640]{1,0:T(4,128)S(1)} %add.92), channel_id=1, source_target_pairs={{0,2},{2,0},{1,3},{3,1},{4,6},{6,4},{5,7},{7,5},{8,10},{10,8},{9,1... | collective-permute-start | bytes 23048 | tf_op jit(solution)/shard_map/ppermute | solution.py:396
  85.9 4.6 %collective-permute-start.28 = (f32[3,640]{1,0:T(4,128)S(1)}, f32[3,640]{1,0:T(4,128)S(1)}, u32[]{:S(2)}, u32[]{:S(2)}) collective-permute-start(f32[3,640]{1,0:T(4,128)S(1)} %add.101), channel_id=1, source_target_pairs={{0,8},{4,12},{8,0},{12,4},{1,9},{5,13},{9,1},{13,5},{2,10},{6,14},... | collective-permute-start | bytes 23048 | tf_op jit(solution)/shard_map/ppermute | solution.py:396
  90.7 6.2 %collective-permute-start.29 = (bf16[40,2944]{1,0:T(8,128)(2,1)S(1)}, bf16[40,2944]{1,0:T(8,128)(2,1)S(1)}, u32[]{:S(2)}, u32[]{:S(2)}) collective-permute-start(bf16[40,2944]{1,0:T(8,128)(2,1)S(1)} %add_convert_fusion), channel_id=1, source_target_pairs={{0,16},{16,0},{1,17},{17,1},{2,18},{18,2},{3,19},{19,3},{4,20},{20... | collective-permute-start | bytes 706568 | tf_op jit(solution)/shard_map/ppermute | solution.py:347
  96.9 1.6 %collective-permute-start.30 = (bf16[40,2944]{1,0:T(8,128)(2,1)S(1)}, bf16[40,2944]{1,0:T(8,128)(2,1)S(1)}, u32[]{:S(2)}, u32[]{:S(2)}) collective-permute-start(bf16[40,2944]{1,0:T(8,128)(2,1)S(1)} %get-tuple-element.125), channel_id=1, source_target_pairs={{0,1},{1,0},{2,3},{3,2},{4,5},{5,4},{6,7},{7,6},{8,9},{9,8},{10,11... | collective-permute-start | bytes 706568 | tf_op jit(solution)/shard_map/ppermute | solution.py:347

commit v13 on v11

--- a/solution.py
+++ b/solution.py
@@ -549,20 +549,18 @@
         late += halves
 
         conv_send = conv_far(acts, late)
-        cots, conv_send = tied(cots, conv_send)
+        crossed[-2], cots, conv_send = tied(crossed[-2], cots, conv_send)
         conv_got = swap(conv_send, "core")
+        received = ring_step(zs - 2, *received)
         sums = back(1, cots, slopes, late)
-        crossed[-2], sums, *received = tied(crossed[-2], sums, *received)
-        received = ring_step(zs - 2, *received)
-        vectors = hop(chip_sum(first_sums + sums), "replica", 1)
-        vectors = hop(vectors, "z", 1)
-        crossed[-1], conv_got, vectors, *received = tied(crossed[-1], conv_got, vectors, *received)
+        crossed[-1], conv_got, sums, *received = tied(crossed[-1], conv_got, sums, *received)
         last, behind = ring_step(zs - 1, *received)
         block = conv_own(conv_got, [conv_first_own, conv_first_got, order], late)
-        vectors = hop(vectors, "y", 1)
+        vectors = hop(chip_sum(first_sums + sums), "replica", 1)
         last, block, vectors = tied(last, block, vectors)
         total = add(*behind, last)
-        reach = 2
+        vectors = hop(vectors, "y", 1)
+        reach = 1
         while reach < zs:
             vectors = hop(vectors, "z", reach)
             reach *= 2

time: 93.7 us -> 97.2 us (1.037)
  waiting for transfers between devices: 24 us -> 26.1 us
  starting transfers between devices: 31.3 us -> 32.7 us
    ppermute x8, starting transfers between devices: 13.8 us -> 9.16 us  [up(): return lax.ppermute(value, NODE, self.ahead)]
    ppermute x7, starting transfers between devices: 2.77 us -> 7.4 us  [down(): return lax.ppermute(value, NODE, self.behind)]
    ppermute x4, waiting for transfers between devices: 10.3 us -> 6.57 us  [hop(): lax.ppermute(value, axis, [(s, s ^ mask) for s in range(count)])]
    ppermute x7, waiting for transfers between devices: 1.37 us -> 4.64 us  [down(): return lax.ppermute(value, NODE, self.behind)]
    ppermute x4, starting transfers between devices: 4.97 us -> 7.03 us  [hop(): lax.ppermute(value, axis, [(s, s ^ mask) for s in range(count)])]
    ppermute x14, waiting for transfers between devices: 4.26 us -> 5.99 us  [swap(): return lax.ppermute(value, axis, [(0, 1), (1, 0)])]
  transfers between devices with their start and end apart: 33 -> 33, of which waited for: 12 -> 15; matrix products, arithmetic and copies ran while one was open for 3% -> 3% of each run, Pallas kernels for 33% -> 32%
where the time goes in v13:
time: 97.2 us; the launch traced here: 97 us
  starting transfers between devices  32.7 us (34%)
  Pallas kernels  32.4 us (33%)
  waiting for transfers between devices  26.1 us (27%)
  other arithmetic  2.88 us (3%)
  between operations  1.54 us (2%)
  local copies, waits for them, and re-layouts  1.34 us (1%)
    ppermute x8, starting transfers between devices, up(): return lax.ppermute(value, NODE, self.ahead)  9.16 us
    ppermute x14, starting transfers between devices, swap(): return lax.ppermute(value, axis, [(0, 1), (1, 0)])  9.13 us
    ppermute x8, waiting for transfers between devices, up(): return lax.ppermute(value, NODE, self.ahead)  8.89 us
    pallas_call x2, Pallas kernels, back(): call(partial(back_kernel, cols, stages, stage), jax.ShapeDtypeStruct((2,...  8.6 us
    ppermute x7, starting transfers between devices, down(): return lax.ppermute(value, NODE, self.behind)  7.4 us
    ppermute x4, starting transfers between devices, hop(): lax.ppermute(value, axis, [(s, s ^ mask) for s in range(count)])  7.03 us
    ppermute x4, waiting for transfers between devices, hop(): lax.ppermute(value, axis, [(s, s ^ mask) for s in range(count)])  6.57 us
    ppermute x14, waiting for transfers between devices, swap(): return lax.ppermute(value, axis, [(0, 1), (1, 0)])  5.99 us
  transfers between devices with their start and end apart: 33, of which 15 were waited for; matrix products, arithmetic and copies ran while one was open for 3% of the time, Pallas kernels for 32%

profile of v13, /device:TPU:0, one launch (start us, length us, event | category | flops | bytes accessed | tf_op | source)
XLA Modules:
  0.0 97.0 jit_solution(8018471281392441200)
XLA Ops:
  0.7 1.3 %fusion = (bf16[40,2944]{1,0:T(8,128)(2,1)S(1)}, bf16[40,2944]{1,0:T(8,128)(2,1)S(1)}) fusion(f32[1,40,5760]{2,1,0:T(8,128)} %param.10, s32[]{:T(128)S(6)} %select_n.27, s32[]{:T(128)S(6)} %select_n.28), kind=kLoop, calls=%fused_computation.12 | loop fusion | bytes 942088 | tf_op jit(solution)/shard_map/convert_element_type | solution.py:421
  2.0 0.5 collective-permute-start.4
  2.5 2.0 %fusion.3 = (f32[640]{0:T(1024)S(1)}, bf16[16,32,640]{2,1,0:T(8,128)(2,1)S(1)}) fusion(f32[1,16,32,640]{3,2,1,0:T(8,128)} %param.9), kind=kLoop, calls=%fused_computation.19 | loop fusion | flops 654720 | bytes 1968640 | tf_op jit(solution)/shard_map/reduce_sum | solution.py:514
  5.1 2.7 %collective-permute-start.5 = (bf16[80,2944]{1,0:T(8,128)(2,1)S(1)}, bf16[80,2944]{1,0:T(8,128)(2,1)S(1)}, u32[]{:S(2)}, u32[]{:S(2)}) collective-permute-start(bf16[80,2944]{1,0:T(8,128)(2,1)S(1)} %maximum_select_fusion.refs_0_), channel_id=1, source_target_pairs={{0,4},{4,8},{8,12},{12,14},{14,10},{10,6},{6,2},{2,0},{1,5},{5,9},... | collective-permute-start | bytes 1413128 | tf_op jit(solution)/shard_map/ppermute | solution.py:366
  7.8 1.9 %collective-permute-start.7 = (bf16[40,2944]{1,0:T(8,128)(2,1)S(1)}, bf16[40,2944]{1,0:T(8,128)(2,1)S(1)}, u32[]{:S(2)}, u32[]{:S(2)}) collective-permute-start(bf16[40,2944]{1,0:T(8,128)(2,1)S(1)} %get-tuple-element.127), channel_id=1, source_target_pairs={{0,16},{16,0},{1,17},{17,1},{2,18},{18,2},{3,19},{19,3},{4,20},{20... | collective-permute-start | bytes 706568 | tf_op jit(solution)/shard_map/ppermute | solution.py:341
  9.9 4.4 %shard_map.119 = (f32[2,640]{1,0:T(2,128)S(1)}, bf16[3,34,32,640]{3,2,1,0:T(8,128)(2,1)S(1)}, bf16[640,1024]{1,0:T(8,128)(2,1)S(1)}) custom-call(s32[1]{0:T(128)} %bitcast.dev, s32[32,24]{1,0:T(8,128)S(1)} %copy-done.5, bf16[16,32,640]{2,1,0:T(8,128)(2,1)S(1)} %bitcast.13, bf16[16,32,640]{2,1,0:T(8,128)(2,1)S(1)} %collective-permute-done.lat_far, ...), custom_call_target="tpu_custom_call" | custom-call | flops 964689920 | tf_op jit(solution)/shard_map/pallas_call | solution.py:452
  14.3 4.6 %shard_map.120 = (bf16[320,2944]{1,0:T(8,128)(2,1)S(1)}, bf16[80,2944]{1,0:T(8,128)(2,1)S(1)}, bf16[80,2944]{1,0:T(8,128)(2,1)S(1)}, bf16[80,2944]{1,0:T(8,128)(2,1)S(1)}, bf16[80,2944]{1,0:T(8,128)(2,1)S(1)}) custom-call(s32[1]{0:T(128)} %bitcast.dev, bf16[3,34,32,640]{3,2,1,0:T(8,128)(2,1)S(1)} %get-tuple-element.63.acts, ...), custom_call_target="tpu_custom_call" | custom-call | flops 1929379840 | tf_op jit(solution)/shard_map/pallas_call | solution.py:460
  19.0 1.7 %collective-permute-done.8.theirs = bf16[40,2944]{1,0:T(8,128)(2,1)S(1)} collective-permute-done((bf16[40,2944]{1,0:T(8,128)(2,1)S(1)}, bf16[40,2944]{1,0:T(8,128)(2,1)S(1)}, u32[]{:S(2)}, u32[]{:S(2)}) %collective-permute-start.8) | collective-permute-done | bytes 235552 | tf_op jit(solution)/shard_map/ppermute | solution.py:341
  20.7 1.7 %collective-permute-start.10 = (bf16[80,2944]{1,0:T(8,128)(2,1)S(1)}, bf16[80,2944]{1,0:T(8,128)(2,1)S(1)}, u32[]{:S(2)}, u32[]{:S(2)}) collective-permute-start(bf16[80,2944]{1,0:T(8,128)(2,1)S(1)} %collective-permute-done.6.refs_2_), channel_id=1, source_target_pairs={{4,0},{8,4},{12,8},{14,12},{10,14},{6,10},{2,6},{0,2},{5,1},{9,5},... | collective-permute-start | bytes 1413128 | tf_op jit(solution)/shard_map/ppermute | solution.py:369
  22.7 1.7 %collective-permute-start.11 = (bf16[80,2944]{1,0:T(8,128)(2,1)S(1)}, bf16[80,2944]{1,0:T(8,128)(2,1)S(1)}, u32[]{:S(2)}, u32[]{:S(2)}) collective-permute-start(bf16[80,2944]{1,0:T(8,128)(2,1)S(1)} %get-tuple-element.79), channel_id=1, source_target_pairs={{0,16},{16,0},{1,17},{17,1},{2,18},{18,2},{3,19},{19,3},{4,20},{20... | collective-permute-start | bytes 1413128 | tf_op jit(solution)/shard_map/ppermute | solution.py:341
  24.7 4.5 %shard_map.121 = (bf16[3,34,32,768]{3,2,1,0:T(8,128)(2,1)S(1)}, bf16[32,32,640]{2,1,0:T(8,128)(2,1)S(1)}, bf16[32,32,640]{2,1,0:T(8,128)(2,1)S(1)}, bf16[640,768]{1,0:T(8,128)(2,1)S(1)}) custom-call(s32[1]{0:T(128)} %bitcast.dev, s32[32,24]{1,0:T(8,128)S(1)} %copy-done.5, f32[2,640]{1,0:T(2,128)S(1)} %get-tuple-element.73.stats, f32[1,640]{1,0:T(1,128)S(1)} %copy-done.3, ...), custom_call_target="tpu_custom_call" | custom-call | flops 964689920 | tf_op jit(solution)/shard_map/pallas_call | solution.py:472
  29.2 3.5 %collective-permute-done.10.refs_4_ = bf16[80,2944]{1,0:T(8,128)(2,1)S(1)} collective-permute-done((bf16[80,2944]{1,0:T(8,128)(2,1)S(1)}, bf16[80,2944]{1,0:T(8,128)(2,1)S(1)}, u32[]{:S(2)}, u32[]{:S(2)}) %collective-permute-start.10) | collective-permute-done | bytes 471072 | tf_op jit(solution)/shard_map/ppermute | solution.py:369
  32.7 1.1 %collective-permute-done.9.refs_3_ = bf16[80,2944]{1,0:T(8,128)(2,1)S(1)} collective-permute-done((bf16[80,2944]{1,0:T(8,128)(2,1)S(1)}, bf16[80,2944]{1,0:T(8,128)(2,1)S(1)}, u32[]{:S(2)}, u32[]{:S(2)}) %collective-permute-start.9) | collective-permute-done | bytes 471072 | tf_op jit(solution)/shard_map/ppermute | solution.py:366
  33.8 0.7 collective-permute-start.12
  34.5 1.4 %collective-permute-start.13 = (bf16[80,2944]{1,0:T(8,128)(2,1)S(1)}, bf16[80,2944]{1,0:T(8,128)(2,1)S(1)}, u32[]{:S(2)}, u32[]{:S(2)}) collective-permute-start(bf16[80,2944]{1,0:T(8,128)(2,1)S(1)} %collective-permute-done.10.refs_4_), channel_id=1, source_target_pairs={{4,0},{8,4},{12,8},{14,12},{10,14},{6,10},{2,6},{0,2},{5,1},{9,5},... | collective-permute-start | bytes 1413128 | tf_op jit(solution)/shard_map/ppermute | solution.py:369
  35.8 4.0 %shard_map.122 = (f32[512,512]{1,0:T(8,128)S(1)}, bf16[512,512]{1,0:T(8,128)(2,1)S(1)}) custom-call(s32[1]{0:T(128)} %bitcast.dev, bf16[3,34,32,640]{3,2,1,0:T(8,128)(2,1)S(1)} %get-tuple-element.63.acts, bf16[80,2944]{1,0:T(8,128)(2,1)S(1)} %maximum_select_fusion.refs_0_, bf16[80,2944]{1,0:T(8,128)(2,1)S(1)} %collective-permute-done.5.refs_1_, ...), custom_call_target="tpu_custom_call" | custom-call | flops 964689920 | tf_op jit(solution)/shard_map/pallas_call | solution.py:490
  39.9 0.7 collective-permute-start.18
  40.7 1.4 %collective-permute-start.19 = (bf16[40,2944]{1,0:T(8,128)(2,1)S(1)}, bf16[40,2944]{1,0:T(8,128)(2,1)S(1)}, u32[]{:S(2)}, u32[]{:S(2)}) collective-permute-start(bf16[40,2944]{1,0:T(8,128)(2,1)S(1)} %get-tuple-element.123), channel_id=1, source_target_pairs={{4,0},{8,4},{12,8},{14,12},{10,14},{6,10},{2,6},{0,2},{5,1},{9,5},... | collective-permute-start | bytes 706568 | tf_op jit(solution)/shard_map/ppermute | solution.py:369
  42.0 5.4 %shard_map.123 = f32[2,640]{1,0:T(2,128)S(1)} custom-call(s32[1]{0:T(128)} %bitcast.dev, bf16[3,34,32,768]{3,2,1,0:T(8,128)(2,1)S(1)} %get-tuple-element.91.cots, bf16[32,32,640]{2,1,0:T(8,128)(2,1)S(1)} %get-tuple-element.85.slope, bf16[32,32,640]{2,1,0:T(8,128)(2,1)S(1)} %get-tuple-element.86.slope_x, bf16[80,2944]{1,0:T(8,128)(2,1)S(1)} %maximum_select_fusion.refs_0_, ...), custom_call_target="tpu_custom_call" | custom-call | flops 964689920 | tf_op jit(solution)/shard_map/pallas_call | solution.py:482
  47.4 1.9 %collective-permute-done.18 = bf16[40,2944]{1,0:T(8,128)(2,1)S(1)} collective-permute-done((bf16[40,2944]{1,0:T(8,128)(2,1)S(1)}, bf16[40,2944]{1,0:T(8,128)(2,1)S(1)}, u32[]{:S(2)}, u32[]{:S(2)}) %collective-permute-start.18) | collective-permute-done | bytes 235552 | tf_op jit(solution)/shard_map/ppermute | solution.py:366
  49.3 1.5 %collective-permute-start.3 = (bf16[80,2944]{1,0:T(8,128)(2,1)S(1)}, bf16[80,2944]{1,0:T(8,128)(2,1)S(1)}, u32[]{:S(2)}, u32[]{:S(2)}) collective-permute-start(bf16[80,2944]{1,0:T(8,128)(2,1)S(1)} %get-tuple-element.67), channel_id=1, source_target_pairs={{0,16},{16,0},{1,17},{17,1},{2,18},{18,2},{3,19},{19,3},{4,20},{20... | collective-permute-start | bytes 1413128 | tf_op jit(solution)/shard_map/ppermute | solution.py:341
  50.9 0.9 collective-permute-start.15
  51.9 1.2 %collective-permute-start.16 = (bf16[40,2944]{1,0:T(8,128)(2,1)S(1)}, bf16[40,2944]{1,0:T(8,128)(2,1)S(1)}, u32[]{:S(2)}, u32[]{:S(2)}) collective-permute-start(bf16[40,2944]{1,0:T(8,128)(2,1)S(1)} %slice.68), channel_id=1, source_target_pairs={{4,0},{8,4},{12,8},{14,12},{10,14},{6,10},{2,6},{0,2},{5,1},{9,5},... | collective-permute-start | bytes 706568 | tf_op jit(solution)/shard_map/ppermute | solution.py:369
  53.2 0.9 collective-permute-start.20
  54.2 1.1 %collective-permute-start.22 = (bf16[40,2944]{1,0:T(8,128)(2,1)S(1)}, bf16[40,2944]{1,0:T(8,128)(2,1)S(1)}, u32[]{:S(2)}, u32[]{:S(2)}) collective-permute-start(bf16[40,2944]{1,0:T(8,128)(2,1)S(1)} %get-tuple-element.121), channel_id=1, source_target_pairs={{4,0},{8,4},{12,8},{14,12},{10,14},{6,10},{2,6},{0,2},{5,1},{9,5},... | collective-permute-start | bytes 706568 | tf_op jit(solution)/shard_map/ppermute | solution.py:369
  55.3 2.4 %collective-permute-done.15.refs_2_.refs_5_ = bf16[40,2944]{1,0:T(8,128)(2,1)S(1)} collective-permute-done((bf16[40,2944]{1,0:T(8,128)(2,1)S(1)}, bf16[40,2944]{1,0:T(8,128)(2,1)S(1)}, u32[]{:S(2)}, u32[]{:S(2)}) %collective-permute-start.15) | collective-permute-done | bytes 235552 | tf_op jit(solution)/shard_map/ppermute | solution.py:366
  57.7 0.9 collective-permute-start.2
  58.7 1.4 %shard_map.124 = bf16[512,256]{1,0:T(8,128)(2,1)S(1)} custom-call(s32[1]{0:T(128)} %bitcast.dev, bf16[3,34,32,640]{3,2,1,0:T(8,128)(2,1)S(1)} %get-tuple-element.63.acts, bf16[80,2944]{1,0:T(8,128)(2,1)S(1)} %collective-permute-done.12.refs_0_.refs_3_, bf16[80,2944]{1,0:T(8,128)(2,1)S(1)} %collective-permute-done.13.refs_1_.refs_4_, ...), custom_call_target="tpu_custom_call" | custom-call | flops 482344960 | tf_op jit(solution)/shard_map/pallas_call | solution.py:499
  60.1 2.6 %collective-permute-done.3 = bf16[80,2944]{1,0:T(8,128)(2,1)S(1)} collective-permute-done((bf16[80,2944]{1,0:T(8,128)(2,1)S(1)}, bf16[80,2944]{1,0:T(8,128)(2,1)S(1)}, u32[]{:S(2)}, u32[]{:S(2)}) %collective-permute-start.3) | collective-permute-done | bytes 471072 | tf_op jit(solution)/shard_map/ppermute | solution.py:341
  62.9 1.4 %collective-permute-start.21 = (bf16[40,2944]{1,0:T(8,128)(2,1)S(1)}, bf16[40,2944]{1,0:T(8,128)(2,1)S(1)}, u32[]{:S(2)}, u32[]{:S(2)}) collective-permute-start(bf16[40,2944]{1,0:T(8,128)(2,1)S(1)} %get-tuple-element.120), channel_id=1, source_target_pairs={{0,4},{4,8},{8,12},{12,14},{14,10},{10,6},{6,2},{2,0},{1,5},{5,9},... | collective-permute-start | bytes 706568 | tf_op jit(solution)/shard_map/ppermute | solution.py:366
  64.3 0.7 collective-permute-start.23
  65.0 3.2 %shard_map.125 = f32[2,640]{1,0:T(2,128)S(1)} custom-call(s32[1]{0:T(128)} %bitcast.dev, bf16[3,34,32,768]{3,2,1,0:T(8,128)(2,1)S(1)} %get-tuple-element.91.cots, bf16[32,32,640]{2,1,0:T(8,128)(2,1)S(1)} %get-tuple-element.85.slope, bf16[32,32,640]{2,1,0:T(8,128)(2,1)S(1)} %get-tuple-element.86.slope_x, ...), custom_call_target="tpu_custom_call" | custom-call | flops 964689920 | tf_op jit(solution)/shard_map/pallas_call | solution.py:482
  68.2 0.8 collective-permute-done.2
  69.0 2.1 %collective-permute-done.21 = bf16[40,2944]{1,0:T(8,128)(2,1)S(1)} collective-permute-done((bf16[40,2944]{1,0:T(8,128)(2,1)S(1)}, bf16[40,2944]{1,0:T(8,128)(2,1)S(1)}, u32[]{:S(2)}, u32[]{:S(2)}) %collective-permute-start.21) | collective-permute-done | bytes 235552 | tf_op jit(solution)/shard_map/ppermute | solution.py:366
  71.1 1.1 %collective-permute-done.23 = bf16[40,2944]{1,0:T(8,128)(2,1)S(1)} collective-permute-done((bf16[40,2944]{1,0:T(8,128)(2,1)S(1)}, bf16[40,2944]{1,0:T(8,128)(2,1)S(1)}, u32[]{:S(2)}, u32[]{:S(2)}) %collective-permute-start.23) | collective-permute-done | bytes 235552 | tf_op jit(solution)/shard_map/ppermute | solution.py:369
  72.4 1.4 %collective-permute-start.24 = (bf16[40,2944]{1,0:T(8,128)(2,1)S(1)}, bf16[40,2944]{1,0:T(8,128)(2,1)S(1)}, u32[]{:S(2)}, u32[]{:S(2)}) collective-permute-start(bf16[40,2944]{1,0:T(8,128)(2,1)S(1)} %add_convert_fusion.1), channel_id=1, source_target_pairs={{0,4},{4,8},{8,12},{12,14},{14,10},{10,6},{6,2},{2,0},{1,5},{5,9},... | collective-permute-start | bytes 706568 | tf_op jit(solution)/shard_map/ppermute | solution.py:366
  73.8 1.7 %collective-permute-start.27 = (f32[3,640]{1,0:T(4,128)S(1)}, f32[3,640]{1,0:T(4,128)S(1)}, u32[]{:S(2)}, u32[]{:S(2)}) collective-permute-start(f32[3,640]{1,0:T(4,128)S(1)} %fusion.4), channel_id=1, source_target_pairs={{0,16},{16,0},{1,17},{17,1},{2,18},{18,2},{3,19},{19,3},{4,20},{20... | collective-permute-start | bytes 23048 | tf_op jit(solution)/shard_map/ppermute | solution.py:390
  75.5 3.7 %shard_map.126 = bf16[16,32,640]{2,1,0:T(8,128)(2,1)} custom-call(s32[1]{0:T(128)} %bitcast.dev, bf16[3,34,32,640]{3,2,1,0:T(8,128)(2,1)S(1)} %get-tuple-element.63.acts, bf16[512,256]{1,0:T(8,128)(2,1)S(1)} %collective-permute-done.17.got, bf16[16,32,640]{2,1,0:T(8,128)(2,1)S(1)} %bitcast.15, f32[1,640]{1,0:T(1,128)S(1)} %copy-done.2, ...), custom_call_target="tpu_custom_call" | custom-call | flops 964689920 | tf_op jit(solution)/shard_map/pallas_call | solution.py:507
  79.2 1.4 %collective-permute-done.24 = bf16[40,2944]{1,0:T(8,128)(2,1)S(1)} collective-permute-done((bf16[40,2944]{1,0:T(8,128)(2,1)S(1)}, bf16[40,2944]{1,0:T(8,128)(2,1)S(1)}, u32[]{:S(2)}, u32[]{:S(2)}) %collective-permute-start.24) | collective-permute-done | bytes 235552 | tf_op jit(solution)/shard_map/ppermute | solution.py:366
  80.7 1.5 %collective-permute-start.28 = (bf16[40,2944]{1,0:T(8,128)(2,1)S(1)}, bf16[40,2944]{1,0:T(8,128)(2,1)S(1)}, u32[]{:S(2)}, u32[]{:S(2)}) collective-permute-start(bf16[40,2944]{1,0:T(8,128)(2,1)S(1)} %add_convert_fusion), channel_id=1, source_target_pairs={{0,16},{16,0},{1,17},{17,1},{2,18},{18,2},{3,19},{19,3},{4,20},{20... | collective-permute-start | bytes 706568 | tf_op jit(solution)/shard_map/ppermute | solution.py:341
  82.2 1.3 %collective-permute-start.29 = (f32[3,640]{1,0:T(4,128)S(1)}, f32[3,640]{1,0:T(4,128)S(1)}, u32[]{:S(2)}, u32[]{:S(2)}) collective-permute-start(f32[3,640]{1,0:T(4,128)S(1)} %add.97), channel_id=1, source_target_pairs={{0,2},{2,0},{1,3},{3,1},{4,6},{6,4},{5,7},{7,5},{8,10},{10,8},{9,1... | collective-permute-start | bytes 23048 | tf_op jit(solution)/shard_map/ppermute | solution.py:390
  83.5 2.4 %collective-permute-done.29 = f32[3,640]{1,0:T(4,128)S(1)} collective-permute-done((f32[3,640]{1,0:T(4,128)S(1)}, f32[3,640]{1,0:T(4,128)S(1)}, u32[]{:S(2)}, u32[]{:S(2)}) %collective-permute-start.29) | collective-permute-done | bytes 7712 | tf_op jit(solution)/shard_map/ppermute | solution.py:390
  85.9 1.6 %collective-permute-start.30 = (f32[3,640]{1,0:T(4,128)S(1)}, f32[3,640]{1,0:T(4,128)S(1)}, u32[]{:S(2)}, u32[]{:S(2)}) collective-permute-start(f32[3,640]{1,0:T(4,128)S(1)} %add.101), channel_id=1, source_target_pairs={{0,4},{4,0},{8,12},{12,8},{1,5},{5,1},{9,13},{13,9},{2,6},{6,2},{1... | collective-permute-start | bytes 23048 | tf_op jit(solution)/shard_map/ppermute | solution.py:390
  87.4 2.1 %collective-permute-done.30 = f32[3,640]{1,0:T(4,128)S(1)} collective-permute-done((f32[3,640]{1,0:T(4,128)S(1)}, f32[3,640]{1,0:T(4,128)S(1)}, u32[]{:S(2)}, u32[]{:S(2)}) %collective-permute-start.30) | collective-permute-done | bytes 7712 | tf_op jit(solution)/shard_map/ppermute | solution.py:390
  89.5 2.5 %collective-permute-start.31 = (f32[3,640]{1,0:T(4,128)S(1)}, f32[3,640]{1,0:T(4,128)S(1)}, u32[]{:S(2)}, u32[]{:S(2)}) collective-permute-start(f32[3,640]{1,0:T(4,128)S(1)} %add.102), channel_id=1, source_target_pairs={{0,8},{4,12},{8,0},{12,4},{1,9},{5,13},{9,1},{13,5},{2,10},{6,14},... | collective-permute-start | bytes 23048 | tf_op jit(solution)/shard_map/ppermute | solution.py:390
  92.0 2.1 %collective-permute-done.31 = f32[3,640]{1,0:T(4,128)S(1)} collective-permute-done((f32[3,640]{1,0:T(4,128)S(1)}, f32[3,640]{1,0:T(4,128)S(1)}, u32[]{:S(2)}, u32[]{:S(2)}) %collective-permute-start.31) | collective-permute-done | bytes 7712 | tf_op jit(solution)/shard_map/ppermute | solution.py:390
  94.9 0.8 collective-permute-done.32.aside
  95.7 1.2 %shard_map.127 = (f32[40,5760]{1,0:T(8,128)}, f32[1,640]{1,0:T(1,128)}, f32[1,640]{1,0:T(1,128)}, f32[1,640]{1,0:T(1,128)}) custom-call(s32[1]{0:T(128)} %bitcast.dev, s32[1]{0:T(128)S(6)} %copy.13.step, f32[40,5760]{1,0:T(8,128)S(1)} %bitcast.11, bf16[40,2944]{1,0:T(8,128)(2,1)S(1)} %collective-permute-done.7.mine, ...), custom_call_target="tpu_custom_call" | custom-call | flops 241172480 | tf_op jit(solution)/shard_map/pallas_call | solution.py:571
  (58 shorter events, 2.7 us)
Async XLA Ops:
  0.6 3.9 %copy-start.1 = (bf16[1,16,32,640]{3,2,1,0:T(8,128)(2,1)S(1)}, bf16[1,16,32,640]{3,2,1,0:T(8,128)(2,1)}, u32[]{:S(2)}) copy-start(bf16[1,16,32,640]{3,2,1,0:T(8,128)(2,1)} %param.8) | copy-start | bytes 1966084
  0.7 9.2 %copy-start.3 = (f32[1,640]{1,0:T(1,128)S(1)}, f32[1,640]{1,0:T(1,128)}, u32[]{:S(2)}) copy-start(f32[1,640]{1,0:T(1,128)} %gain.3) | copy-start | bytes 7684
  0.7 9.2 %copy-start.4 = (f32[1,640]{1,0:T(1,128)S(1)}, f32[1,640]{1,0:T(1,128)}, u32[]{:S(2)}) copy-start(f32[1,640]{1,0:T(1,128)} %shift.3) | copy-start | bytes 7684
  0.7 9.2 %copy-start.5 = (s32[32,24]{1,0:T(8,128)S(1)}, s32[32,24]{1,0:T(8,128)}, u32[]{:S(2)}) copy-start(s32[32,24]{1,0:T(8,128)} %constant.38.clone.table) | copy-start | bytes 9220
  2.0 3.1 %collective-permute-start.4 = (bf16[40,2944]{1,0:T(8,128)(2,1)S(1)}, bf16[40,2944]{1,0:T(8,128)(2,1)S(1)}, u32[]{:S(2)}, u32[]{:S(2)}) collective-permute-start(bf16[40,2944]{1,0:T(8,128)(2,1)S(1)} %get-tuple-element.128), channel_id=1, source_target_pairs={{0,1},{1,0},{2,3},{3,2},{4,5},{5,4},{6,7},{7,6},{8,9},{9,8},{10,11... | collective-permute-start | bytes 706568 | tf_op jit(solution)/shard_map/ppermute | solution.py:341
  4.5 5.3 %collective-permute-start.1 = (bf16[16,32,640]{2,1,0:T(8,128)(2,1)S(1)}, bf16[16,32,640]{2,1,0:T(8,128)(2,1)S(1)}, u32[]{:S(2)}, u32[]{:S(2)}) collective-permute-start(bf16[16,32,640]{2,1,0:T(8,128)(2,1)S(1)} %get-tuple-element.126.cot_own), channel_id=1, source_target_pairs={{0,1},{1,0},{2,3},{3,2},{4,5},{5,4},{6,7},{7,6},{8,9},{9,8},{10,11... | collective-permute-start | bytes 1966088 | tf_op jit(solution)/shard_map/ppermute | solution.py:341
  4.6 5.3 %collective-permute-start = (bf16[16,32,640]{2,1,0:T(8,128)(2,1)S(1)}, bf16[16,32,640]{2,1,0:T(8,128)(2,1)S(1)}, u32[]{:S(2)}, u32[]{:S(2)}) collective-permute-start(bf16[16,32,640]{2,1,0:T(8,128)(2,1)S(1)} %bitcast.12), channel_id=1, source_target_pairs={{0,1},{1,0},{2,3},{3,2},{4,5},{5,4},{6,7},{7,6},{8,9},{9,8},{10,11... | collective-permute-start | bytes 1966088 | tf_op jit(solution)/shard_map/ppermute | solution.py:341
  5.1 15.6 %collective-permute-start.5 = (bf16[80,2944]{1,0:T(8,128)(2,1)S(1)}, bf16[80,2944]{1,0:T(8,128)(2,1)S(1)}, u32[]{:S(2)}, u32[]{:S(2)}) collective-permute-start(bf16[80,2944]{1,0:T(8,128)(2,1)S(1)} %maximum_select_fusion.refs_0_), channel_id=1, source_target_pairs={{0,4},{4,8},{8,12},{12,14},{14,10},{10,6},{6,2},{2,0},{1,5},{5,9},... | collective-permute-start | bytes 1413128 | tf_op jit(solution)/shard_map/ppermute | solution.py:366
  7.8 12.9 %collective-permute-start.6 = (bf16[80,2944]{1,0:T(8,128)(2,1)S(1)}, bf16[80,2944]{1,0:T(8,128)(2,1)S(1)}, u32[]{:S(2)}, u32[]{:S(2)}) collective-permute-start(bf16[80,2944]{1,0:T(8,128)(2,1)S(1)} %maximum_select_fusion.refs_0_), channel_id=1, source_target_pairs={{4,0},{8,4},{12,8},{14,12},{10,14},{6,10},{2,6},{0,2},{5,1},{9,5},... | collective-permute-start | bytes 1413128 | tf_op jit(solution)/shard_map/ppermute | solution.py:369
  7.8 11.1 %collective-permute-start.7 = (bf16[40,2944]{1,0:T(8,128)(2,1)S(1)}, bf16[40,2944]{1,0:T(8,128)(2,1)S(1)}, u32[]{:S(2)}, u32[]{:S(2)}) collective-permute-start(bf16[40,2944]{1,0:T(8,128)(2,1)S(1)} %get-tuple-element.127), channel_id=1, source_target_pairs={{0,16},{16,0},{1,17},{17,1},{2,18},{18,2},{3,19},{19,3},{4,20},{20... | collective-permute-start | bytes 706568 | tf_op jit(solution)/shard_map/ppermute | solution.py:341
  9.8 10.9 %collective-permute-start.8 = (bf16[40,2944]{1,0:T(8,128)(2,1)S(1)}, bf16[40,2944]{1,0:T(8,128)(2,1)S(1)}, u32[]{:S(2)}, u32[]{:S(2)}) collective-permute-start(bf16[40,2944]{1,0:T(8,128)(2,1)S(1)} %get-tuple-element.128), channel_id=1, source_target_pairs={{0,16},{16,0},{1,17},{17,1},{2,18},{18,2},{3,19},{19,3},{4,20},{20... | collective-permute-start | bytes 706568 | tf_op jit(solution)/shard_map/ppermute | solution.py:341
  20.7 12.0 %collective-permute-start.10 = (bf16[80,2944]{1,0:T(8,128)(2,1)S(1)}, bf16[80,2944]{1,0:T(8,128)(2,1)S(1)}, u32[]{:S(2)}, u32[]{:S(2)}) collective-permute-start(bf16[80,2944]{1,0:T(8,128)(2,1)S(1)} %collective-permute-done.6.refs_2_), channel_id=1, source_target_pairs={{4,0},{8,4},{12,8},{14,12},{10,14},{6,10},{2,6},{0,2},{5,1},{9,5},... | collective-permute-start | bytes 1413128 | tf_op jit(solution)/shard_map/ppermute | solution.py:369
  22.4 11.4 %collective-permute-start.9 = (bf16[80,2944]{1,0:T(8,128)(2,1)S(1)}, bf16[80,2944]{1,0:T(8,128)(2,1)S(1)}, u32[]{:S(2)}, u32[]{:S(2)}) collective-permute-start(bf16[80,2944]{1,0:T(8,128)(2,1)S(1)} %collective-permute-done.5.refs_1_), channel_id=1, source_target_pairs={{0,4},{4,8},{8,12},{12,14},{14,10},{10,6},{6,2},{2,0},{1,5},{5,9},... | collective-permute-start | bytes 1413128 | tf_op jit(solution)/shard_map/ppermute | solution.py:366
  22.7 17.1 %collective-permute-start.11 = (bf16[80,2944]{1,0:T(8,128)(2,1)S(1)}, bf16[80,2944]{1,0:T(8,128)(2,1)S(1)}, u32[]{:S(2)}, u32[]{:S(2)}) collective-permute-start(bf16[80,2944]{1,0:T(8,128)(2,1)S(1)} %get-tuple-element.79), channel_id=1, source_target_pairs={{0,16},{16,0},{1,17},{17,1},{2,18},{18,2},{3,19},{19,3},{4,20},{20... | collective-permute-start | bytes 1413128 | tf_op jit(solution)/shard_map/ppermute | solution.py:341
  24.4 26.5 %collective-permute-start.14 = (bf16[80,2944]{1,0:T(8,128)(2,1)S(1)}, bf16[80,2944]{1,0:T(8,128)(2,1)S(1)}, u32[]{:S(2)}, u32[]{:S(2)}) collective-permute-start(bf16[80,2944]{1,0:T(8,128)(2,1)S(1)} %get-tuple-element.87), channel_id=1, source_target_pairs={{0,16},{16,0},{1,17},{17,1},{2,18},{18,2},{3,19},{19,3},{4,20},{20... | collective-permute-start | bytes 1413128 | tf_op jit(solution)/shard_map/ppermute | solution.py:341
  33.8 17.0 %collective-permute-start.12 = (bf16[80,2944]{1,0:T(8,128)(2,1)S(1)}, bf16[80,2944]{1,0:T(8,128)(2,1)S(1)}, u32[]{:S(2)}, u32[]{:S(2)}) collective-permute-start(bf16[80,2944]{1,0:T(8,128)(2,1)S(1)} %collective-permute-done.9.refs_3_), channel_id=1, source_target_pairs={{0,4},{4,8},{8,12},{12,14},{14,10},{10,6},{6,2},{2,0},{1,5},{5,9},... | collective-permute-start | bytes 1413128 | tf_op jit(solution)/shard_map/ppermute | solution.py:366
  34.5 16.4 %collective-permute-start.13 = (bf16[80,2944]{1,0:T(8,128)(2,1)S(1)}, bf16[80,2944]{1,0:T(8,128)(2,1)S(1)}, u32[]{:S(2)}, u32[]{:S(2)}) collective-permute-start(bf16[80,2944]{1,0:T(8,128)(2,1)S(1)} %collective-permute-done.10.refs_4_), channel_id=1, source_target_pairs={{4,0},{8,4},{12,8},{14,12},{10,14},{6,10},{2,6},{0,2},{5,1},{9,5},... | collective-permute-start | bytes 1413128 | tf_op jit(solution)/shard_map/ppermute | solution.py:369
  39.9 9.4 %collective-permute-start.18 = (bf16[40,2944]{1,0:T(8,128)(2,1)S(1)}, bf16[40,2944]{1,0:T(8,128)(2,1)S(1)}, u32[]{:S(2)}, u32[]{:S(2)}) collective-permute-start(bf16[40,2944]{1,0:T(8,128)(2,1)S(1)} %get-tuple-element.124), channel_id=1, source_target_pairs={{0,4},{4,8},{8,12},{12,14},{14,10},{10,6},{6,2},{2,0},{1,5},{5,9},... | collective-permute-start | bytes 706568 | tf_op jit(solution)/shard_map/ppermute | solution.py:366
  40.7 10.2 %collective-permute-start.19 = (bf16[40,2944]{1,0:T(8,128)(2,1)S(1)}, bf16[40,2944]{1,0:T(8,128)(2,1)S(1)}, u32[]{:S(2)}, u32[]{:S(2)}) collective-permute-start(bf16[40,2944]{1,0:T(8,128)(2,1)S(1)} %get-tuple-element.123), channel_id=1, source_target_pairs={{4,0},{8,4},{12,8},{14,12},{10,14},{6,10},{2,6},{0,2},{5,1},{9,5},... | collective-permute-start | bytes 706568 | tf_op jit(solution)/shard_map/ppermute | solution.py:369
  49.3 13.4 %collective-permute-start.3 = (bf16[80,2944]{1,0:T(8,128)(2,1)S(1)}, bf16[80,2944]{1,0:T(8,128)(2,1)S(1)}, u32[]{:S(2)}, u32[]{:S(2)}) collective-permute-start(bf16[80,2944]{1,0:T(8,128)(2,1)S(1)} %get-tuple-element.67), channel_id=1, source_target_pairs={{0,16},{16,0},{1,17},{17,1},{2,18},{18,2},{3,19},{19,3},{4,20},{20... | collective-permute-start | bytes 1413128 | tf_op jit(solution)/shard_map/ppermute | solution.py:341
  50.9 6.8 %collective-permute-start.15 = (bf16[40,2944]{1,0:T(8,128)(2,1)S(1)}, bf16[40,2944]{1,0:T(8,128)(2,1)S(1)}, u32[]{:S(2)}, u32[]{:S(2)}) collective-permute-start(bf16[40,2944]{1,0:T(8,128)(2,1)S(1)} %slice.67), channel_id=1, source_target_pairs={{0,4},{4,8},{8,12},{12,14},{14,10},{10,6},{6,2},{2,0},{1,5},{5,9},... | collective-permute-start | bytes 706568 | tf_op jit(solution)/shard_map/ppermute | solution.py:366
  51.9 6.8 %collective-permute-start.16 = (bf16[40,2944]{1,0:T(8,128)(2,1)S(1)}, bf16[40,2944]{1,0:T(8,128)(2,1)S(1)}, u32[]{:S(2)}, u32[]{:S(2)}) collective-permute-start(bf16[40,2944]{1,0:T(8,128)(2,1)S(1)} %slice.68), channel_id=1, source_target_pairs={{4,0},{8,4},{12,8},{14,12},{10,14},{6,10},{2,6},{0,2},{5,1},{9,5},... | collective-permute-start | bytes 706568 | tf_op jit(solution)/shard_map/ppermute | solution.py:369
  53.2 9.5 %collective-permute-start.20 = (bf16[40,2944]{1,0:T(8,128)(2,1)S(1)}, bf16[40,2944]{1,0:T(8,128)(2,1)S(1)}, u32[]{:S(2)}, u32[]{:S(2)}) collective-permute-start(bf16[40,2944]{1,0:T(8,128)(2,1)S(1)} %get-tuple-element.122), channel_id=1, source_target_pairs={{0,4},{4,8},{8,12},{12,14},{14,10},{10,6},{6,2},{2,0},{1,5},{5,9},... | collective-permute-start | bytes 706568 | tf_op jit(solution)/shard_map/ppermute | solution.py:366
  54.2 8.5 %collective-permute-start.22 = (bf16[40,2944]{1,0:T(8,128)(2,1)S(1)}, bf16[40,2944]{1,0:T(8,128)(2,1)S(1)}, u32[]{:S(2)}, u32[]{:S(2)}) collective-permute-start(bf16[40,2944]{1,0:T(8,128)(2,1)S(1)} %get-tuple-element.121), channel_id=1, source_target_pairs={{4,0},{8,4},{12,8},{14,12},{10,14},{6,10},{2,6},{0,2},{5,1},{9,5},... | collective-permute-start | bytes 706568 | tf_op jit(solution)/shard_map/ppermute | solution.py:369
  57.7 11.3 %collective-permute-start.2 = (bf16[80,2944]{1,0:T(8,128)(2,1)S(1)}, bf16[80,2944]{1,0:T(8,128)(2,1)S(1)}, u32[]{:S(2)}, u32[]{:S(2)}) collective-permute-start(bf16[80,2944]{1,0:T(8,128)(2,1)S(1)} %get-tuple-element.66), channel_id=1, source_target_pairs={{0,16},{16,0},{1,17},{17,1},{2,18},{18,2},{3,19},{19,3},{4,20},{20... | collective-permute-start | bytes 1413128 | tf_op jit(solution)/shard_map/ppermute | solution.py:341
  62.7 9.5 %collective-permute-start.17 = (bf16[512,256]{1,0:T(8,128)(2,1)S(1)}, bf16[512,256]{1,0:T(8,128)(2,1)S(1)}, u32[]{:S(2)}, u32[]{:S(2)}) collective-permute-start(bf16[512,256]{1,0:T(8,128)(2,1)S(1)} %shard_map.124), channel_id=1, source_target_pairs={{0,1},{1,0},{2,3},{3,2},{4,5},{5,4},{6,7},{7,6},{8,9},{9,8},{10,11... | collective-permute-start | bytes 786440 | tf_op jit(solution)/shard_map/ppermute | solution.py:341
  62.9 8.2 %collective-permute-start.21 = (bf16[40,2944]{1,0:T(8,128)(2,1)S(1)}, bf16[40,2944]{1,0:T(8,128)(2,1)S(1)}, u32[]{:S(2)}, u32[]{:S(2)}) collective-permute-start(bf16[40,2944]{1,0:T(8,128)(2,1)S(1)} %get-tuple-element.120), channel_id=1, source_target_pairs={{0,4},{4,8},{8,12},{12,14},{14,10},{10,6},{6,2},{2,0},{1,5},{5,9},... | collective-permute-start | bytes 706568 | tf_op jit(solution)/shard_map/ppermute | solution.py:366
  64.3 7.9 %collective-permute-start.23 = (bf16[40,2944]{1,0:T(8,128)(2,1)S(1)}, bf16[40,2944]{1,0:T(8,128)(2,1)S(1)}, u32[]{:S(2)}, u32[]{:S(2)}) collective-permute-start(bf16[40,2944]{1,0:T(8,128)(2,1)S(1)} %get-tuple-element.119), channel_id=1, source_target_pairs={{4,0},{8,4},{12,8},{14,12},{10,14},{6,10},{2,6},{0,2},{5,1},{9,5},... | collective-permute-start | bytes 706568 | tf_op jit(solution)/shard_map/ppermute | solution.py:369
  65.0 7.2 %copy-start.2 = (f32[1,640]{1,0:T(1,128)S(1)}, f32[1,640]{1,0:T(1,128)}, u32[]{:S(2)}) copy-start(f32[1,640]{1,0:T(1,128)} %bias.1) | copy-start | bytes 7684
  65.0 10.5 %collective-permute-start.25 = (bf16[512,512]{1,0:T(8,128)(2,1)S(1)}, bf16[512,512]{1,0:T(8,128)(2,1)S(1)}, u32[]{:S(2)}, u32[]{:S(2)}) collective-permute-start(bf16[512,512]{1,0:T(8,128)(2,1)S(1)} %get-tuple-element.102), channel_id=1, source_target_pairs={{0,1},{1,0},{2,3},{3,2},{4,5},{5,4},{6,7},{7,6},{8,9},{9,8},{10,11... | collective-permute-start | bytes 1572872 | tf_op jit(solution)/shard_map/ppermute | solution.py:341
  72.2 1.6 %collective-permute-start.26 = (f32[3,640]{1,0:T(4,128)S(1)}, f32[3,640]{1,0:T(4,128)S(1)}, u32[]{:S(2)}, u32[]{:S(2)}) collective-permute-start(f32[3,640]{1,0:T(4,128)S(1)} %fusion.2), channel_id=1, source_target_pairs={{0,1},{1,0},{2,3},{3,2},{4,5},{5,4},{6,7},{7,6},{8,9},{9,8},{10,11... | collective-permute-start | bytes 23048 | tf_op jit(solution)/shard_map/ppermute | solution.py:341
  72.4 8.2 %collective-permute-start.24 = (bf16[40,2944]{1,0:T(8,128)(2,1)S(1)}, bf16[40,2944]{1,0:T(8,128)(2,1)S(1)}, u32[]{:S(2)}, u32[]{:S(2)}) collective-permute-start(bf16[40,2944]{1,0:T(8,128)(2,1)S(1)} %add_convert_fusion.1), channel_id=1, source_target_pairs={{0,4},{4,8},{8,12},{12,14},{14,10},{10,6},{6,2},{2,0},{1,5},{5,9},... | collective-permute-start | bytes 706568 | tf_op jit(solution)/shard_map/ppermute | solution.py:366
  73.8 5.4 %collective-permute-start.27 = (f32[3,640]{1,0:T(4,128)S(1)}, f32[3,640]{1,0:T(4,128)S(1)}, u32[]{:S(2)}, u32[]{:S(2)}) collective-permute-start(f32[3,640]{1,0:T(4,128)S(1)} %fusion.4), channel_id=1, source_target_pairs={{0,16},{16,0},{1,17},{17,1},{2,18},{18,2},{3,19},{19,3},{4,20},{20... | collective-permute-start | bytes 23048 | tf_op jit(solution)/shard_map/ppermute | solution.py:390
  79.2 16.6 %copy-start = (f32[1,40,5760]{2,1,0:T(8,128)S(1)}, f32[1,40,5760]{2,1,0:T(8,128)}, u32[]{:S(2)}) copy-start(f32[1,40,5760]{2,1,0:T(8,128)} %param.10) | copy-start | bytes 2764804
  80.7 13.4 %collective-permute-start.28 = (bf16[40,2944]{1,0:T(8,128)(2,1)S(1)}, bf16[40,2944]{1,0:T(8,128)(2,1)S(1)}, u32[]{:S(2)}, u32[]{:S(2)}) collective-permute-start(bf16[40,2944]{1,0:T(8,128)(2,1)S(1)} %add_convert_fusion), channel_id=1, source_target_pairs={{0,16},{16,0},{1,17},{17,1},{2,18},{18,2},{3,19},{19,3},{4,20},{20... | collective-permute-start | bytes 706568 | tf_op jit(solution)/shard_map/ppermute | solution.py:341
  82.2 3.7 %collective-permute-start.29 = (f32[3,640]{1,0:T(4,128)S(1)}, f32[3,640]{1,0:T(4,128)S(1)}, u32[]{:S(2)}, u32[]{:S(2)}) collective-permute-start(f32[3,640]{1,0:T(4,128)S(1)} %add.97), channel_id=1, source_target_pairs={{0,2},{2,0},{1,3},{3,1},{4,6},{6,4},{5,7},{7,5},{8,10},{10,8},{9,1... | collective-permute-start | bytes 23048 | tf_op jit(solution)/shard_map/ppermute | solution.py:390
  85.9 3.7 %collective-permute-start.30 = (f32[3,640]{1,0:T(4,128)S(1)}, f32[3,640]{1,0:T(4,128)S(1)}, u32[]{:S(2)}, u32[]{:S(2)}) collective-permute-start(f32[3,640]{1,0:T(4,128)S(1)} %add.101), channel_id=1, source_target_pairs={{0,4},{4,0},{8,12},{12,8},{1,5},{5,1},{9,13},{13,9},{2,6},{6,2},{1... | collective-permute-start | bytes 23048 | tf_op jit(solution)/shard_map/ppermute | solution.py:390
  89.5 4.6 %collective-permute-start.31 = (f32[3,640]{1,0:T(4,128)S(1)}, f32[3,640]{1,0:T(4,128)S(1)}, u32[]{:S(2)}, u32[]{:S(2)}) collective-permute-start(f32[3,640]{1,0:T(4,128)S(1)} %add.102), channel_id=1, source_target_pairs={{0,8},{4,12},{8,0},{12,4},{1,9},{5,13},{9,1},{13,5},{2,10},{6,14},... | collective-permute-start | bytes 23048 | tf_op jit(solution)/shard_map/ppermute | solution.py:390
  94.2 1.6 %collective-permute-start.32 = (bf16[40,2944]{1,0:T(8,128)(2,1)S(1)}, bf16[40,2944]{1,0:T(8,128)(2,1)S(1)}, u32[]{:S(2)}, u32[]{:S(2)}) collective-permute-start(bf16[40,2944]{1,0:T(8,128)(2,1)S(1)} %get-tuple-element.129), channel_id=1, source_target_pairs={{0,1},{1,0},{2,3},{3,2},{4,5},{5,4},{6,7},{7,6},{8,9},{9,8},{10,11... | collective-permute-start | bytes 706568 | tf_op jit(solution)/shard_map/ppermute | solution.py:341

commit v14 on v12

--- a/solution.py
+++ b/solution.py
@@ -120,7 +120,7 @@
             cot_t[2 * q * part:(2 * q + 2) * part] = jnp.concatenate(pair).astype(BF16)
 
 
-def grad_kernel(cols, carrier, dev, acts, cot_t, mine, theirs, *pieces):
+def grad_kernel(cols, carrier, dev, acts, cot_t, theirs, *pieces):
     core = dev[0] % 2
     rows, width, chans = acts.shape[1] - 2, acts.shape[2], acts.shape[3]
     cells = rows * width
@@ -129,7 +129,7 @@
         value = jnp.dot(cot_t[...], window, preferred_element_type=F32)
         at = 0
         for i, piece in enumerate(pieces):
-            count = piece.shape[0] - (2 * mine.shape[0] if i == carrier else 0)
+            count = piece.shape[0] - (theirs.shape[0] if i == carrier else 0)
             piece[:count, pl.ds(place, wide)] = value[at:at + count].astype(BF16)
             at += count
 
@@ -143,7 +143,7 @@
     place, channel = cols.middle(core, chans)
     emit(acts[1, 1:rows + 1, :, pl.ds(channel, cols.mid)].reshape(cells, cols.mid), place, cols.mid)
     if carrier is not None:
-        pieces[carrier][-2 * mine.shape[0]:] = jnp.concatenate([mine[...], theirs[...]])
+        pieces[carrier][-theirs.shape[0]:] = theirs[...]
 
 
 class Stages:
@@ -158,7 +158,7 @@
         return slice(self.starts[stage], self.starts[stage] + self.widths[stage])
 
     def columns(self, stage, blocks, place, wide):
-        parts = [ref[:, pl.ds(place, wide)] for ref in blocks]
+        parts = [ref[:min(self.rows, ref.shape[0]), pl.ds(place, wide)] for ref in blocks]
         if len(parts) == self.counts[stage] + 1:
             parts[-2:] = [jnp.concatenate(parts[-2:])]
         spare = self.widths[stage] - self.counts[stage] * self.rows
@@ -324,14 +324,13 @@
     sums[1:2] = scale * jnp.sum(shifts, axis=0, keepdims=True)
 
 
-def finish_kernel(cols, dev, step, shard, carried, ours, aside, vectors, out, new_bias, new_gain, new_shift):
+def finish_kernel(cols, dev, step, shard, mine, carried, ours, aside, vectors, out, new_bias, new_gain, new_shift):
     lower = dev[0] % 2 == 0
     rate = LR_KERNEL * (1.0 - (step[0] % 1000).astype(F32) / 2000.0)
     factor = 0.5 * cols.total ** (-0.5) * rate
     part = shard.shape[0]
-    peer = carried[-2 * part:].astype(F32)
-    mine, theirs = peer[:part], peer[part:]
-    here = 0.5 * mine - factor * ours[...].astype(F32)
+    theirs = carried[-part:].astype(F32)
+    here = 0.5 * mine[...].astype(F32) - factor * ours[...].astype(F32)
     there = 0.5 * theirs - factor * aside[...].astype(F32)
     left, right = jnp.where(lower, here, there), jnp.where(lower, there, here)
     out[:, :cols.lead] = 0.5 * shard[:, :cols.lead] + left
@@ -436,6 +435,7 @@
         table = jnp.asarray(ring.table(part))
         order = (ring.count, part, 2 * ring.count)
         up1, down1 = ring.up(unit), ring.down(unit)
+        peer = swap(mine, "replica")
     else:
         table = jnp.zeros((replicas * zs * 4, 1), jnp.int32)
         order = None
@@ -448,7 +448,7 @@
             out_specs=jax.tree.map(lambda _: VMEM_SPEC, outs),
             scratch_shapes=scratch,
             compiler_params=pltpu.CompilerParams(vmem_limit_bytes=megabytes * 2**20),
-            cost_estimate=pl.CostEstimate(flops=flops, bytes_accessed=0, transcendentals=0),
+            cost_estimate=pl.CostEstimate(flops=flops * 4, bytes_accessed=0, transcendentals=0),
         )
 
     image = (2 * half, width, chans)
@@ -461,14 +461,16 @@
         [pltpu.VMEM((chans, 2 * cells), F32)],
         8, flops // 4,
     )(dev, table, latent, lat_far, cot_b, cot_far, gn_gain, gn_shift)
-    counts = [zs, 1, 2] + [1] * (zs - 2) if paired else [2 * zs]
+    if paired:
+        peer, acts = tied(peer, acts)
+    counts = [2 * zs, 2, 3] + [2] * (zs - 2) if paired else [4 * zs]
     pieces = call(
         partial(grad_kernel, cols, 2 if paired else None),
-        [jax.ShapeDtypeStruct((n * 2 * part, cols.lead), BF16) for n in counts],
-        [SMEM_SPEC] + [VMEM_SPEC] * 4,
+        [jax.ShapeDtypeStruct((n * part, cols.lead), BF16) for n in counts],
+        [SMEM_SPEC] + [VMEM_SPEC] * 3,
         [],
         4, flops // 2,
-    )(dev, acts, cot_t, mine, theirs)
+    )(dev, acts, cot_t, theirs)
     stages = Stages([2 * zs - 3, 3] if paired else [1], 2 * part if paired else chans)
     staged = paired
 
@@ -523,6 +525,7 @@
     if paired:
         kept, *sent = pieces
         crossed = [swap(piece, "replica") for piece in sent]
+        theirs = crossed[1]
 
         def ring_sums(j, *received):
             parts = kept[2 * j * part:(2 * j + 2) * part], crossed[j]
@@ -534,58 +537,54 @@
         def ring_step(ahead, behind):
             return ring.up(ahead), ring.down(behind)
 
-        up, down, _ = tied(up1, down1, sent[0])
+        up, down, stats, _ = tied(up1, down1, stats, sent[0])
         blocks = [unit, up, down]
         up, down = ring.up(up), ring.down(down)
-        cots, *slopes, order = slopes_of(stats)
-        up, down, cots, *slopes, order = tied(up, down, cots, *slopes, order)
+        up, down, cots, *slopes, order = tied(up, down, *slopes_of(stats))
         blocks += [up, down]
 
-        up, down = ring.up(up), ring.down(down)
+        ahead, behind = ring_sums(0)
+        up = ring.up(jnp.concatenate([up, ahead]))
+        down = ring.down(jnp.concatenate([down, behind]))
         conv_first_own, conv_send = conv_first(blocks)
-        crossed[0], conv_send = tied(crossed[0], conv_send)
-        received = ring_step(*ring_sums(0))
         cots, conv_send = tied(cots, conv_send)
         first_sums = back(0, cots, slopes, blocks)
-        up, down, first_sums = tied(up, down, first_sums)
+        up, down, first_sums, crossed[1] = tied(up, down, first_sums, crossed[1])
         late = [up, down]
-
-        halves = ring.up(up[:part]), ring.down(down[part:])
-        conv_send, *received = tied(conv_send, *received)
+        received = up[2 * part:], down[2 * part:]
+
+        halves = ring.up(up[:part]), ring.down(down[part:2 * part])
         conv_first_got = swap(conv_send, "core")
         for j in range(1, zs - 2):
             received = ring_step(*ring_sums(j, *received))
         late += halves
 
         conv_send = conv_far(acts, late)
-        cots, conv_send = tied(cots, conv_send)
+        crossed[2], cots, conv_send = tied(crossed[2], cots, conv_send)
         conv_got = swap(conv_send, "core")
+        received = ring_step(*ring_sums(zs - 2, *received))
         sums = back(1, cots, slopes, late)
-        crossed[-2], sums, *received = tied(crossed[-2], sums, *received)
-        received = ring_step(*ring_sums(zs - 2, *received))
-        vectors = chip_sum(first_sums + sums)
-        conv_got, vectors = tied(conv_got, vectors)
-        block = conv_own(conv_got, [conv_first_own, conv_first_got, order], late)
-        vectors = hop(hop(vectors, "replica", 1), "z", 1)
-        crossed[-1], block, vectors, *received = tied(crossed[-1], block, vectors, *received)
+        crossed[3], conv_got, sums, *received = tied(crossed[3], conv_got, sums, *received)
         ahead, behind = ring_sums(zs - 1, *received)
         last = ring.up(ahead)
+        block = conv_own(conv_got, [conv_first_own, conv_first_got, order], late)
+        vectors = hop(hop(chip_sum(first_sums + sums), "replica", 1), "z", 1)
+        last, block, vectors = tied(last, block, vectors)
+        total = add(*behind, last)
         vectors = hop(vectors, "y", 1)
         reach = 2
         while reach < zs:
             vectors = hop(vectors, "z", reach)
             reach *= 2
-        last, vectors = tied(last, vectors)
-        total = add(*behind, last)
-        across = swap(total, "replica")
+        across, vectors = tied(swap(total, "replica"), vectors)
         ours, others = jnp.where(same, total, across), jnp.where(same, across, total)
         aside = swap(others, "core")
         vector = jax.ShapeDtypeStruct((1, chans), F32)
         new_kernel, *new_v = call(
             partial(finish_kernel, cols),
             (jax.ShapeDtypeStruct(shard.shape, F32), vector, vector, vector),
-            [SMEM_SPEC] * 2 + [VMEM_SPEC] * 5, [], 8, flops // 16,
-        )(dev, step, shard, crossed[1], ours, aside, vectors)
+            [SMEM_SPEC] * 2 + [VMEM_SPEC] * 6, [], 8, flops // 16,
+        )(dev, step, shard, peer, theirs, ours, aside, vectors)
     else:
         late = [lax.all_gather(unit, NODE, axis=0, tiled=True)]
         cots, slope, slope_x = slopes_of(stats)

time: 99.8 us -> 93.9 us (0.941)
  waiting for transfers between devices: 33.9 us -> 25.8 us
  starting transfers between devices: 27.5 us -> 30.9 us
  local copies, waits for them, and re-layouts: 1.35 us -> 0.13 us
    ppermute x7 -> x6, starting transfers between devices: 9.9 us -> 2.38 us  [down(): return lax.ppermute(value, NODE, self.behind)]
    ppermute x4, waiting for transfers between devices: 12.2 us -> 6.32 us  [hop(): lax.ppermute(value, axis, [(s, s ^ mask) for s in range(count)])]
    ppermute x8 -> x7, starting transfers between devices: 6.59 us -> 12.4 us  [up(): return lax.ppermute(value, NODE, self.ahead)]
    ppermute x12 -> x13, waiting for transfers between devices: 9.28 us -> 5.21 us  [swap(): return lax.ppermute(value, axis, [(0, 1), (1, 0)])]
    ppermute x12 -> x13, starting transfers between devices: 7.49 us -> 10.5 us  [swap(): return lax.ppermute(value, axis, [(0, 1), (1, 0)])]
    ppermute x8 -> x7, waiting for transfers between devices: 4.91 us -> 7.14 us  [up(): return lax.ppermute(value, NODE, self.ahead)]
    ppermute x4, starting transfers between devices: 3.53 us -> 5.61 us  [hop(): lax.ppermute(value, axis, [(s, s ^ mask) for s in range(count)])]
    convert_element_type x1, local copies, waits for them, and re-layouts: 1.28 us -> 0.07 us  [per_device(): lax.dynamic_slice_in_dim(shard, (1 - core) * cols.start, cols.lead, 1)]
  transfers between devices with their start and end apart: 31 -> 30, of which waited for: 13 -> 16; matrix products, arithmetic and copies ran while one was open for 3% -> 1% of each run, Pallas kernels for 31% -> 33%
where the time goes in v14:
time: 93.9 us; the launch traced here: 93.8 us
  Pallas kernels  32.4 us (35%)
  starting transfers between devices  30.9 us (33%)
  waiting for transfers between devices  25.8 us (27%)
  other arithmetic  3.03 us (3%)
  between operations  1.52 us (2%)
    ppermute x7, starting transfers between devices, up(): return lax.ppermute(value, NODE, self.ahead)  12.4 us
    ppermute x13, starting transfers between devices, swap(): return lax.ppermute(value, axis, [(0, 1), (1, 0)])  10.5 us
    pallas_call x2, Pallas kernels, back(): call(partial(back_kernel, cols, stages, stage), jax.ShapeDtypeStruct((2,...  8.61 us
    ppermute x6, waiting for transfers between devices, down(): return lax.ppermute(value, NODE, self.behind)  7.14 us
    ppermute x7, waiting for transfers between devices, up(): return lax.ppermute(value, NODE, self.ahead)  7.14 us
    ppermute x4, waiting for transfers between devices, hop(): lax.ppermute(value, axis, [(s, s ^ mask) for s in range(count)])  6.32 us
    ppermute x4, starting transfers between devices, hop(): lax.ppermute(value, axis, [(s, s ^ mask) for s in range(count)])  5.61 us
    ppermute x13, waiting for transfers between devices, swap(): return lax.ppermute(value, axis, [(0, 1), (1, 0)])  5.21 us
  transfers between devices with their start and end apart: 30, of which 16 were waited for; matrix products, arithmetic and copies ran while one was open for 1% of the time, Pallas kernels for 33%

profile of v14, /device:TPU:0, one launch (start us, length us, event | category | flops | bytes accessed | tf_op | source)
XLA Modules:
  0.0 93.8 jit_solution(15169305383026812143)
XLA Ops:
  0.7 2.0 %fusion.3 = (f32[640]{0:T(1024)S(1)}, bf16[16,32,640]{2,1,0:T(8,128)(2,1)S(1)}) fusion(f32[1,16,32,640]{3,2,1,0:T(8,128)} %param.9), kind=kLoop, calls=%fused_computation.21 | loop fusion | flops 654720 | bytes 1968640 | tf_op jit(solution)/shard_map/reduce_sum | solution.py:521
  2.7 0.5 collective-permute-start.2
  3.4 0.5 collective-permute-start.5
  3.9 2.6 %collective-permute-start = (bf16[40,2944]{1,0:T(8,128)(2,1)S(1)}, bf16[40,2944]{1,0:T(8,128)(2,1)S(1)}, u32[]{:S(2)}, u32[]{:S(2)}) collective-permute-start(bf16[40,2944]{1,0:T(8,128)(2,1)S(1)} %get-tuple-element.118), channel_id=1, source_target_pairs={{0,16},{16,0},{1,17},{17,1},{2,18},{18,2},{3,19},{19,3},{4,20},{20... | collective-permute-start | bytes 706568 | tf_op jit(solution)/shard_map/ppermute | solution.py:346
  6.5 2.8 %collective-permute-start.6 = (bf16[80,2944]{1,0:T(8,128)(2,1)S(1)}, bf16[80,2944]{1,0:T(8,128)(2,1)S(1)}, u32[]{:S(2)}, u32[]{:S(2)}) collective-permute-start(bf16[80,2944]{1,0:T(8,128)(2,1)S(1)} %maximum_select_fusion.refs_0_), channel_id=1, source_target_pairs={{0,4},{4,8},{8,12},{12,14},{14,10},{10,6},{6,2},{2,0},{1,5},{5,9},... | collective-permute-start | bytes 1413128 | tf_op jit(solution)/shard_map/ppermute | solution.py:371
  9.3 4.4 %shard_map.119 = (f32[2,640]{1,0:T(2,128)S(1)}, bf16[3,34,32,640]{3,2,1,0:T(8,128)(2,1)S(1)}, bf16[640,1024]{1,0:T(8,128)(2,1)S(1)}) custom-call(s32[1]{0:T(128)} %bitcast.dev, s32[32,24]{1,0:T(8,128)S(1)} %copy-done.5, bf16[16,32,640]{2,1,0:T(8,128)(2,1)S(1)} %bitcast.13, bf16[16,32,640]{2,1,0:T(8,128)(2,1)S(1)} %collective-permute-done.1.lat_far, ...), custom_call_target="tpu_custom_call" | custom-call | flops 3858759680 | tf_op jit(solution)/shard_map/pallas_call | solution.py:457
  13.7 4.6 %shard_map.120 = (bf16[320,2944]{1,0:T(8,128)(2,1)S(1)}, bf16[80,2944]{1,0:T(8,128)(2,1)S(1)}, bf16[120,2944]{1,0:T(8,128)(2,1)S(1)}, bf16[80,2944]{1,0:T(8,128)(2,1)S(1)}, bf16[80,2944]{1,0:T(8,128)(2,1)S(1)}) custom-call(s32[1]{0:T(128)} %bitcast.dev, bf16[3,34,32,640]{3,2,1,0:T(8,128)(2,1)S(1)} %get-tuple-element.60.acts, ...), custom_call_target="tpu_custom_call" | custom-call | flops 7717519360 | tf_op jit(solution)/shard_map/pallas_call | solution.py:467
  18.4 2.0 %collective-permute-start.10 = (bf16[80,2944]{1,0:T(8,128)(2,1)S(1)}, bf16[80,2944]{1,0:T(8,128)(2,1)S(1)}, u32[]{:S(2)}, u32[]{:S(2)}) collective-permute-start(bf16[80,2944]{1,0:T(8,128)(2,1)S(1)} %get-tuple-element.67), channel_id=1, source_target_pairs={{0,16},{16,0},{1,17},{17,1},{2,18},{18,2},{3,19},{19,3},{4,20},{20... | collective-permute-start | bytes 1413128 | tf_op jit(solution)/shard_map/ppermute | solution.py:346
  20.5 1.9 %collective-permute-start.4 = (bf16[80,2944]{1,0:T(8,128)(2,1)S(1)}, bf16[80,2944]{1,0:T(8,128)(2,1)S(1)}, u32[]{:S(2)}, u32[]{:S(2)}) collective-permute-start(bf16[80,2944]{1,0:T(8,128)(2,1)S(1)} %get-tuple-element.64), channel_id=1, source_target_pairs={{0,16},{16,0},{1,17},{17,1},{2,18},{18,2},{3,19},{19,3},{4,20},{20... | collective-permute-start | bytes 1413128 | tf_op jit(solution)/shard_map/ppermute | solution.py:346
  22.4 1.6 %collective-permute-start.8 = (bf16[80,2944]{1,0:T(8,128)(2,1)S(1)}, bf16[80,2944]{1,0:T(8,128)(2,1)S(1)}, u32[]{:S(2)}, u32[]{:S(2)}) collective-permute-start(bf16[80,2944]{1,0:T(8,128)(2,1)S(1)} %collective-permute-done.6.refs_1_), channel_id=1, source_target_pairs={{0,4},{4,8},{8,12},{12,14},{14,10},{10,6},{6,2},{2,0},{1,5},{5,9},... | collective-permute-start | bytes 1413128 | tf_op jit(solution)/shard_map/ppermute | solution.py:371
  24.4 4.5 %shard_map.121 = (bf16[3,34,32,768]{3,2,1,0:T(8,128)(2,1)S(1)}, bf16[32,32,640]{2,1,0:T(8,128)(2,1)S(1)}, bf16[32,32,640]{2,1,0:T(8,128)(2,1)S(1)}, bf16[640,768]{1,0:T(8,128)(2,1)S(1)}) custom-call(s32[1]{0:T(128)} %bitcast.dev, s32[32,24]{1,0:T(8,128)S(1)} %copy-done.5, f32[2,640]{1,0:T(2,128)S(1)} %get-tuple-element.70.stats, f32[1,640]{1,0:T(1,128)S(1)} %copy-done.1, ...), custom_call_target="tpu_custom_call" | custom-call | flops 3858759680 | tf_op jit(solution)/shard_map/pallas_call | solution.py:479
  28.9 3.2 %collective-permute-done.10 = bf16[80,2944]{1,0:T(8,128)(2,1)S(1)} collective-permute-done((bf16[80,2944]{1,0:T(8,128)(2,1)S(1)}, bf16[80,2944]{1,0:T(8,128)(2,1)S(1)}, u32[]{:S(2)}, u32[]{:S(2)}) %collective-permute-start.10) | collective-permute-done | bytes 471072 | tf_op jit(solution)/shard_map/ppermute | solution.py:346
  32.2 1.6 %collective-permute-done.8.refs_3_ = bf16[80,2944]{1,0:T(8,128)(2,1)S(1)} collective-permute-done((bf16[80,2944]{1,0:T(8,128)(2,1)S(1)}, bf16[80,2944]{1,0:T(8,128)(2,1)S(1)}, u32[]{:S(2)}, u32[]{:S(2)}) %collective-permute-start.8) | collective-permute-done | bytes 471072 | tf_op jit(solution)/shard_map/ppermute | solution.py:371
  33.8 1.3 %collective-permute-done.9.refs_4_ = bf16[80,2944]{1,0:T(8,128)(2,1)S(1)} collective-permute-done((bf16[80,2944]{1,0:T(8,128)(2,1)S(1)}, bf16[80,2944]{1,0:T(8,128)(2,1)S(1)}, u32[]{:S(2)}, u32[]{:S(2)}) %collective-permute-start.9) | collective-permute-done | bytes 471072 | tf_op jit(solution)/shard_map/ppermute | solution.py:374
  35.2 0.5 collective-permute-start.12
  35.7 1.6 %collective-permute-start.11 = (bf16[120,2944]{1,0:T(8,128)(2,1)S(1)}, bf16[120,2944]{1,0:T(8,128)(2,1)S(1)}, u32[]{:S(2)}, u32[]{:S(2)}) collective-permute-start(bf16[120,2944]{1,0:T(8,128)(2,1)S(1)} %pad_maximum_fusion), channel_id=1, source_target_pairs={{0,4},{4,8},{8,12},{12,14},{14,10},{10,6},{6,2},{2,0},{1,5},{5,9},... | collective-permute-start | bytes 2119688 | tf_op jit(solution)/shard_map/ppermute | solution.py:371
  37.4 4.0 %shard_map.122 = (f32[512,512]{1,0:T(8,128)S(1)}, bf16[512,512]{1,0:T(8,128)(2,1)S(1)}) custom-call(s32[1]{0:T(128)} %bitcast.dev, bf16[3,34,32,640]{3,2,1,0:T(8,128)(2,1)S(1)} %get-tuple-element.60.acts, bf16[80,2944]{1,0:T(8,128)(2,1)S(1)} %maximum_select_fusion.refs_0_, bf16[80,2944]{1,0:T(8,128)(2,1)S(1)} %collective-permute-done.6.refs_1_, ...), custom_call_target="tpu_custom_call" | custom-call | flops 3858759680 | tf_op jit(solution)/shard_map/pallas_call | solution.py:497
  41.4 5.4 %shard_map.123 = f32[2,640]{1,0:T(2,128)S(1)} custom-call(s32[1]{0:T(128)} %bitcast.dev, bf16[3,34,32,768]{3,2,1,0:T(8,128)(2,1)S(1)} %get-tuple-element.86.cots, bf16[32,32,640]{2,1,0:T(8,128)(2,1)S(1)} %get-tuple-element.80.slope, bf16[32,32,640]{2,1,0:T(8,128)(2,1)S(1)} %get-tuple-element.81.slope_x, bf16[80,2944]{1,0:T(8,128)(2,1)S(1)} %maximum_select_fusion.refs_0_, ...), custom_call_target="tpu_custom_call" | custom-call | flops 3858759680 | tf_op jit(solution)/shard_map/pallas_call | solution.py:489
  46.7 0.5 collective-permute-done.13.carried
  47.3 3.2 %collective-permute-done.12.refs_1_.refs_4_ = bf16[120,2944]{1,0:T(8,128)(2,1)S(1)} collective-permute-done((bf16[120,2944]{1,0:T(8,128)(2,1)S(1)}, bf16[120,2944]{1,0:T(8,128)(2,1)S(1)}, u32[]{:S(2)}, u32[]{:S(2)}) %collective-permute-start.12) | collective-permute-done | bytes 706592 | tf_op jit(solution)/shard_map/ppermute | solution.py:374
  50.5 1.2 %collective-permute-done.11.refs_0_.refs_3_ = bf16[120,2944]{1,0:T(8,128)(2,1)S(1)} collective-permute-done((bf16[120,2944]{1,0:T(8,128)(2,1)S(1)}, bf16[120,2944]{1,0:T(8,128)(2,1)S(1)}, u32[]{:S(2)}, u32[]{:S(2)}) %collective-permute-start.11) | collective-permute-done | bytes 706592 | tf_op jit(solution)/shard_map/ppermute | solution.py:371
  51.7 1.6 %collective-permute-start.14 = (bf16[40,2944]{1,0:T(8,128)(2,1)S(1)}, bf16[40,2944]{1,0:T(8,128)(2,1)S(1)}, u32[]{:S(2)}, u32[]{:S(2)}) collective-permute-start(bf16[40,2944]{1,0:T(8,128)(2,1)S(1)} %slice.77), channel_id=1, source_target_pairs={{0,4},{4,8},{8,12},{12,14},{14,10},{10,6},{6,2},{2,0},{1,5},{5,9},... | collective-permute-start | bytes 706568 | tf_op jit(solution)/shard_map/ppermute | solution.py:371
  53.4 0.5 collective-permute-start.15
  54.1 1.6 %collective-permute-start.17 = (bf16[40,2944]{1,0:T(8,128)(2,1)S(1)}, bf16[40,2944]{1,0:T(8,128)(2,1)S(1)}, u32[]{:S(2)}, u32[]{:S(2)}) collective-permute-start(bf16[40,2944]{1,0:T(8,128)(2,1)S(1)} %get-tuple-element.110), channel_id=1, source_target_pairs={{0,4},{4,8},{8,12},{12,14},{14,10},{10,6},{6,2},{2,0},{1,5},{5,9},... | collective-permute-start | bytes 706568 | tf_op jit(solution)/shard_map/ppermute | solution.py:371
  55.7 0.5 collective-permute-start.19
  56.2 2.3 %collective-permute-done.14.refs_2_.refs_5_ = bf16[40,2944]{1,0:T(8,128)(2,1)S(1)} collective-permute-done((bf16[40,2944]{1,0:T(8,128)(2,1)S(1)}, bf16[40,2944]{1,0:T(8,128)(2,1)S(1)}, u32[]{:S(2)}, u32[]{:S(2)}) %collective-permute-start.14) | collective-permute-done | bytes 235552 | tf_op jit(solution)/shard_map/ppermute | solution.py:371
  58.4 1.4 %collective-permute-start.3 = (bf16[80,2944]{1,0:T(8,128)(2,1)S(1)}, bf16[80,2944]{1,0:T(8,128)(2,1)S(1)}, u32[]{:S(2)}, u32[]{:S(2)}) collective-permute-start(bf16[80,2944]{1,0:T(8,128)(2,1)S(1)} %get-tuple-element.63), channel_id=1, source_target_pairs={{0,16},{16,0},{1,17},{17,1},{2,18},{18,2},{3,19},{19,3},{4,20},{20... | collective-permute-start | bytes 1413128 | tf_op jit(solution)/shard_map/ppermute | solution.py:346
  59.8 1.4 %shard_map.124 = bf16[512,256]{1,0:T(8,128)(2,1)S(1)} custom-call(s32[1]{0:T(128)} %bitcast.dev, bf16[3,34,32,640]{3,2,1,0:T(8,128)(2,1)S(1)} %get-tuple-element.60.acts, bf16[120,2944]{1,0:T(8,128)(2,1)S(1)} %collective-permute-done.11.refs_0_.refs_3_, bf16[120,2944]{1,0:T(8,128)(2,1)S(1)} %collective-permute-done.12.refs_1_.refs_4_, ...), custom_call_target="tpu_custom_call" | custom-call | flops 1929379840 | tf_op jit(solution)/shard_map/pallas_call | solution.py:506
  61.2 1.3 %collective-permute-done.17 = bf16[40,2944]{1,0:T(8,128)(2,1)S(1)} collective-permute-done((bf16[40,2944]{1,0:T(8,128)(2,1)S(1)}, bf16[40,2944]{1,0:T(8,128)(2,1)S(1)}, u32[]{:S(2)}, u32[]{:S(2)}) %collective-permute-start.17) | collective-permute-done | bytes 235552 | tf_op jit(solution)/shard_map/ppermute | solution.py:371
  62.5 1.0 %collective-permute-done.19 = bf16[40,2944]{1,0:T(8,128)(2,1)S(1)} collective-permute-done((bf16[40,2944]{1,0:T(8,128)(2,1)S(1)}, bf16[40,2944]{1,0:T(8,128)(2,1)S(1)}, u32[]{:S(2)}, u32[]{:S(2)}) %collective-permute-start.19) | collective-permute-done | bytes 235552 | tf_op jit(solution)/shard_map/ppermute | solution.py:374
  63.7 1.6 %collective-permute-start.18 = (bf16[40,2944]{1,0:T(8,128)(2,1)S(1)}, bf16[40,2944]{1,0:T(8,128)(2,1)S(1)}, u32[]{:S(2)}, u32[]{:S(2)}) collective-permute-start(bf16[40,2944]{1,0:T(8,128)(2,1)S(1)} %get-tuple-element.112), channel_id=1, source_target_pairs={{0,4},{4,8},{8,12},{12,14},{14,10},{10,6},{6,2},{2,0},{1,5},{5,9},... | collective-permute-start | bytes 706568 | tf_op jit(solution)/shard_map/ppermute | solution.py:371
  65.8 3.2 %shard_map.125 = f32[2,640]{1,0:T(2,128)S(1)} custom-call(s32[1]{0:T(128)} %bitcast.dev, bf16[3,34,32,768]{3,2,1,0:T(8,128)(2,1)S(1)} %get-tuple-element.86.cots, bf16[32,32,640]{2,1,0:T(8,128)(2,1)S(1)} %get-tuple-element.80.slope, bf16[32,32,640]{2,1,0:T(8,128)(2,1)S(1)} %get-tuple-element.81.slope_x, ...), custom_call_target="tpu_custom_call" | custom-call | flops 3858759680 | tf_op jit(solution)/shard_map/pallas_call | solution.py:489
  69.0 0.8 collective-permute-done.18
  69.8 1.6 %collective-permute-done.20 = bf16[40,2944]{1,0:T(8,128)(2,1)S(1)} collective-permute-done((bf16[40,2944]{1,0:T(8,128)(2,1)S(1)}, bf16[40,2944]{1,0:T(8,128)(2,1)S(1)}, u32[]{:S(2)}, u32[]{:S(2)}) %collective-permute-start.20) | collective-permute-done | bytes 235552 | tf_op jit(solution)/shard_map/ppermute | solution.py:374
  71.5 0.5 collective-permute-start.22
  72.0 0.7 collective-permute-done.23
  72.7 0.8 collective-permute-start.24
  73.6 1.6 %collective-permute-start.21 = (bf16[40,2944]{1,0:T(8,128)(2,1)S(1)}, bf16[40,2944]{1,0:T(8,128)(2,1)S(1)}, u32[]{:S(2)}, u32[]{:S(2)}) collective-permute-start(bf16[40,2944]{1,0:T(8,128)(2,1)S(1)} %add_convert_fusion.1), channel_id=1, source_target_pairs={{0,4},{4,8},{8,12},{12,14},{14,10},{10,6},{6,2},{2,0},{1,5},{5,9},... | collective-permute-start | bytes 706568 | tf_op jit(solution)/shard_map/ppermute | solution.py:371
  75.1 1.3 %collective-permute-done.24 = f32[3,640]{1,0:T(4,128)S(1)} collective-permute-done((f32[3,640]{1,0:T(4,128)S(1)}, f32[3,640]{1,0:T(4,128)S(1)}, u32[]{:S(2)}, u32[]{:S(2)}) %collective-permute-start.24) | collective-permute-done | bytes 7712 | tf_op jit(solution)/shard_map/ppermute | solution.py:395
  76.5 1.6 %collective-permute-start.25 = (f32[3,640]{1,0:T(4,128)S(1)}, f32[3,640]{1,0:T(4,128)S(1)}, u32[]{:S(2)}, u32[]{:S(2)}) collective-permute-start(f32[3,640]{1,0:T(4,128)S(1)} %add.97), channel_id=1, source_target_pairs={{0,4},{4,0},{8,12},{12,8},{1,5},{5,1},{9,13},{13,9},{2,6},{6,2},{1... | collective-permute-start | bytes 23048 | tf_op jit(solution)/shard_map/ppermute | solution.py:395
  78.1 3.7 %shard_map.126 = bf16[16,32,640]{2,1,0:T(8,128)(2,1)} custom-call(s32[1]{0:T(128)} %bitcast.dev, bf16[3,34,32,640]{3,2,1,0:T(8,128)(2,1)S(1)} %get-tuple-element.60.acts, bf16[512,256]{1,0:T(8,128)(2,1)S(1)} %collective-permute-done.16.got, bf16[16,32,640]{2,1,0:T(8,128)(2,1)S(1)} %bitcast.15, f32[1,640]{1,0:T(1,128)S(1)} %copy-done.3, ...), custom_call_target="tpu_custom_call" | custom-call | flops 3858759680 | tf_op jit(solution)/shard_map/pallas_call | solution.py:514
  81.9 0.8 collective-permute-start.26
  82.7 0.7 collective-permute-start.27
  83.4 3.0 %collective-permute-done.27 = f32[3,640]{1,0:T(4,128)S(1)} collective-permute-done((f32[3,640]{1,0:T(4,128)S(1)}, f32[3,640]{1,0:T(4,128)S(1)}, u32[]{:S(2)}, u32[]{:S(2)}) %collective-permute-start.27) | collective-permute-done | bytes 7712 | tf_op jit(solution)/shard_map/ppermute | solution.py:395
  86.4 2.6 %collective-permute-start.28 = (f32[3,640]{1,0:T(4,128)S(1)}, f32[3,640]{1,0:T(4,128)S(1)}, u32[]{:S(2)}, u32[]{:S(2)}) collective-permute-start(f32[3,640]{1,0:T(4,128)S(1)} %add.102), channel_id=1, source_target_pairs={{0,8},{4,12},{8,0},{12,4},{1,9},{5,13},{9,1},{13,5},{2,10},{6,14},... | collective-permute-start | bytes 23048 | tf_op jit(solution)/shard_map/ppermute | solution.py:395
  88.9 2.0 %collective-permute-done.28 = f32[3,640]{1,0:T(4,128)S(1)} collective-permute-done((f32[3,640]{1,0:T(4,128)S(1)}, f32[3,640]{1,0:T(4,128)S(1)}, u32[]{:S(2)}, u32[]{:S(2)}) %collective-permute-start.28) | collective-permute-done | bytes 7712 | tf_op jit(solution)/shard_map/ppermute | solution.py:395
  91.7 0.8 collective-permute-done.29.aside
  92.6 1.2 %shard_map.127 = (f32[40,5760]{1,0:T(8,128)}, f32[1,640]{1,0:T(1,128)}, f32[1,640]{1,0:T(1,128)}, f32[1,640]{1,0:T(1,128)}) custom-call(s32[1]{0:T(128)} %bitcast.dev, s32[1]{0:T(128)S(6)} %copy.13.step, f32[40,5760]{1,0:T(8,128)S(1)} %bitcast.11, bf16[40,2944]{1,0:T(8,128)(2,1)S(1)} %collective-permute-done.mine, ...), custom_call_target="tpu_custom_call" | custom-call | flops 964689920 | tf_op jit(solution)/shard_map/pallas_call | solution.py:583
  (54 shorter events, 2.4 us)
Async XLA Ops:
  0.6 2.6 %copy-start.4 = (bf16[1,16,32,640]{3,2,1,0:T(8,128)(2,1)S(1)}, bf16[1,16,32,640]{3,2,1,0:T(8,128)(2,1)}, u32[]{:S(2)}) copy-start(bf16[1,16,32,640]{3,2,1,0:T(8,128)(2,1)} %param.8) | copy-start | bytes 1966084
  0.6 2.7 %copy-start = (f32[1,40,5760]{2,1,0:T(8,128)S(1)}, f32[1,40,5760]{2,1,0:T(8,128)}, u32[]{:S(2)}) copy-start(f32[1,40,5760]{2,1,0:T(8,128)} %param.10) | copy-start | bytes 2764804
  2.7 6.6 %copy-start.1 = (f32[1,640]{1,0:T(1,128)S(1)}, f32[1,640]{1,0:T(1,128)}, u32[]{:S(2)}) copy-start(f32[1,640]{1,0:T(1,128)} %gain.3) | copy-start | bytes 7684
  2.7 6.6 %copy-start.2 = (f32[1,640]{1,0:T(1,128)S(1)}, f32[1,640]{1,0:T(1,128)}, u32[]{:S(2)}) copy-start(f32[1,640]{1,0:T(1,128)} %shift.3) | copy-start | bytes 7684
  2.7 6.6 %collective-permute-start.2 = (bf16[16,32,640]{2,1,0:T(8,128)(2,1)S(1)}, bf16[16,32,640]{2,1,0:T(8,128)(2,1)S(1)}, u32[]{:S(2)}, u32[]{:S(2)}) collective-permute-start(bf16[16,32,640]{2,1,0:T(8,128)(2,1)S(1)} %get-tuple-element.116.cot_own), channel_id=1, source_target_pairs={{0,1},{1,0},{2,3},{3,2},{4,5},{5,4},{6,7},{7,6},{8,9},{9,8},{10,11... | collective-permute-start | bytes 1966088 | tf_op jit(solution)/shard_map/ppermute | solution.py:346
  3.2 6.1 %collective-permute-start.1 = (bf16[16,32,640]{2,1,0:T(8,128)(2,1)S(1)}, bf16[16,32,640]{2,1,0:T(8,128)(2,1)S(1)}, u32[]{:S(2)}, u32[]{:S(2)}) collective-permute-start(bf16[16,32,640]{2,1,0:T(8,128)(2,1)S(1)} %bitcast.12), channel_id=1, source_target_pairs={{0,1},{1,0},{2,3},{3,2},{4,5},{5,4},{6,7},{7,6},{8,9},{9,8},{10,11... | collective-permute-start | bytes 1966088 | tf_op jit(solution)/shard_map/ppermute | solution.py:346
  3.3 6.0 %copy-start.5 = (s32[32,24]{1,0:T(8,128)S(1)}, s32[32,24]{1,0:T(8,128)}, u32[]{:S(2)}) copy-start(s32[32,24]{1,0:T(8,128)} %constant.38.clone.table) | copy-start | bytes 9220
  3.4 3.1 %collective-permute-start.5 = (bf16[40,2944]{1,0:T(8,128)(2,1)S(1)}, bf16[40,2944]{1,0:T(8,128)(2,1)S(1)}, u32[]{:S(2)}, u32[]{:S(2)}) collective-permute-start(bf16[40,2944]{1,0:T(8,128)(2,1)S(1)} %get-tuple-element.117.theirs), channel_id=1, source_target_pairs={{0,1},{1,0},{2,3},{3,2},{4,5},{5,4},{6,7},{7,6},{8,9},{9,8},{10,11... | collective-permute-start | bytes 706568 | tf_op jit(solution)/shard_map/ppermute | solution.py:346
  3.9 9.9 %collective-permute-start = (bf16[40,2944]{1,0:T(8,128)(2,1)S(1)}, bf16[40,2944]{1,0:T(8,128)(2,1)S(1)}, u32[]{:S(2)}, u32[]{:S(2)}) collective-permute-start(bf16[40,2944]{1,0:T(8,128)(2,1)S(1)} %get-tuple-element.118), channel_id=1, source_target_pairs={{0,16},{16,0},{1,17},{17,1},{2,18},{18,2},{3,19},{19,3},{4,20},{20... | collective-permute-start | bytes 706568 | tf_op jit(solution)/shard_map/ppermute | solution.py:346
  6.5 15.9 %collective-permute-start.6 = (bf16[80,2944]{1,0:T(8,128)(2,1)S(1)}, bf16[80,2944]{1,0:T(8,128)(2,1)S(1)}, u32[]{:S(2)}, u32[]{:S(2)}) collective-permute-start(bf16[80,2944]{1,0:T(8,128)(2,1)S(1)} %maximum_select_fusion.refs_0_), channel_id=1, source_target_pairs={{0,4},{4,8},{8,12},{12,14},{14,10},{10,6},{6,2},{2,0},{1,5},{5,9},... | collective-permute-start | bytes 1413128 | tf_op jit(solution)/shard_map/ppermute | solution.py:371
  9.3 13.1 %collective-permute-start.7 = (bf16[80,2944]{1,0:T(8,128)(2,1)S(1)}, bf16[80,2944]{1,0:T(8,128)(2,1)S(1)}, u32[]{:S(2)}, u32[]{:S(2)}) collective-permute-start(bf16[80,2944]{1,0:T(8,128)(2,1)S(1)} %maximum_select_fusion.refs_0_), channel_id=1, source_target_pairs={{4,0},{8,4},{12,8},{14,12},{10,14},{6,10},{2,6},{0,2},{5,1},{9,5},... | collective-permute-start | bytes 1413128 | tf_op jit(solution)/shard_map/ppermute | solution.py:374
  18.4 13.7 %collective-permute-start.10 = (bf16[80,2944]{1,0:T(8,128)(2,1)S(1)}, bf16[80,2944]{1,0:T(8,128)(2,1)S(1)}, u32[]{:S(2)}, u32[]{:S(2)}) collective-permute-start(bf16[80,2944]{1,0:T(8,128)(2,1)S(1)} %get-tuple-element.67), channel_id=1, source_target_pairs={{0,16},{16,0},{1,17},{17,1},{2,18},{18,2},{3,19},{19,3},{4,20},{20... | collective-permute-start | bytes 1413128 | tf_op jit(solution)/shard_map/ppermute | solution.py:346
  20.4 26.9 %collective-permute-start.13 = (bf16[120,2944]{1,0:T(8,128)(2,1)S(1)}, bf16[120,2944]{1,0:T(8,128)(2,1)S(1)}, u32[]{:S(2)}, u32[]{:S(2)}) collective-permute-start(bf16[120,2944]{1,0:T(8,128)(2,1)S(1)} %get-tuple-element.82), channel_id=1, source_target_pairs={{0,16},{16,0},{1,17},{17,1},{2,18},{18,2},{3,19},{19,3},{4,20},{20... | collective-permute-start | bytes 2119688 | tf_op jit(solution)/shard_map/ppermute | solution.py:346
  20.5 40.7 %collective-permute-start.4 = (bf16[80,2944]{1,0:T(8,128)(2,1)S(1)}, bf16[80,2944]{1,0:T(8,128)(2,1)S(1)}, u32[]{:S(2)}, u32[]{:S(2)}) collective-permute-start(bf16[80,2944]{1,0:T(8,128)(2,1)S(1)} %get-tuple-element.64), channel_id=1, source_target_pairs={{0,16},{16,0},{1,17},{17,1},{2,18},{18,2},{3,19},{19,3},{4,20},{20... | collective-permute-start | bytes 1413128 | tf_op jit(solution)/shard_map/ppermute | solution.py:346
  22.4 11.4 %collective-permute-start.8 = (bf16[80,2944]{1,0:T(8,128)(2,1)S(1)}, bf16[80,2944]{1,0:T(8,128)(2,1)S(1)}, u32[]{:S(2)}, u32[]{:S(2)}) collective-permute-start(bf16[80,2944]{1,0:T(8,128)(2,1)S(1)} %collective-permute-done.6.refs_1_), channel_id=1, source_target_pairs={{0,4},{4,8},{8,12},{12,14},{14,10},{10,6},{6,2},{2,0},{1,5},{5,9},... | collective-permute-start | bytes 1413128 | tf_op jit(solution)/shard_map/ppermute | solution.py:371
  24.0 11.1 %collective-permute-start.9 = (bf16[80,2944]{1,0:T(8,128)(2,1)S(1)}, bf16[80,2944]{1,0:T(8,128)(2,1)S(1)}, u32[]{:S(2)}, u32[]{:S(2)}) collective-permute-start(bf16[80,2944]{1,0:T(8,128)(2,1)S(1)} %collective-permute-done.7.refs_2_), channel_id=1, source_target_pairs={{4,0},{8,4},{12,8},{14,12},{10,14},{6,10},{2,6},{0,2},{5,1},{9,5},... | collective-permute-start | bytes 1413128 | tf_op jit(solution)/shard_map/ppermute | solution.py:374
  35.2 15.3 %collective-permute-start.12 = (bf16[120,2944]{1,0:T(8,128)(2,1)S(1)}, bf16[120,2944]{1,0:T(8,128)(2,1)S(1)}, u32[]{:S(2)}, u32[]{:S(2)}) collective-permute-start(bf16[120,2944]{1,0:T(8,128)(2,1)S(1)} %pad_maximum_fusion.1), channel_id=1, source_target_pairs={{4,0},{8,4},{12,8},{14,12},{10,14},{6,10},{2,6},{0,2},{5,1},{9,5},... | collective-permute-start | bytes 2119688 | tf_op jit(solution)/shard_map/ppermute | solution.py:374
  35.7 16.0 %collective-permute-start.11 = (bf16[120,2944]{1,0:T(8,128)(2,1)S(1)}, bf16[120,2944]{1,0:T(8,128)(2,1)S(1)}, u32[]{:S(2)}, u32[]{:S(2)}) collective-permute-start(bf16[120,2944]{1,0:T(8,128)(2,1)S(1)} %pad_maximum_fusion), channel_id=1, source_target_pairs={{0,4},{4,8},{8,12},{12,14},{14,10},{10,6},{6,2},{2,0},{1,5},{5,9},... | collective-permute-start | bytes 2119688 | tf_op jit(solution)/shard_map/ppermute | solution.py:371
  51.7 6.7 %collective-permute-start.14 = (bf16[40,2944]{1,0:T(8,128)(2,1)S(1)}, bf16[40,2944]{1,0:T(8,128)(2,1)S(1)}, u32[]{:S(2)}, u32[]{:S(2)}) collective-permute-start(bf16[40,2944]{1,0:T(8,128)(2,1)S(1)} %slice.77), channel_id=1, source_target_pairs={{0,4},{4,8},{8,12},{12,14},{14,10},{10,6},{6,2},{2,0},{1,5},{5,9},... | collective-permute-start | bytes 706568 | tf_op jit(solution)/shard_map/ppermute | solution.py:371
  53.4 6.4 %collective-permute-start.15 = (bf16[40,2944]{1,0:T(8,128)(2,1)S(1)}, bf16[40,2944]{1,0:T(8,128)(2,1)S(1)}, u32[]{:S(2)}, u32[]{:S(2)}) collective-permute-start(bf16[40,2944]{1,0:T(8,128)(2,1)S(1)} %slice.78), channel_id=1, source_target_pairs={{4,0},{8,4},{12,8},{14,12},{10,14},{6,10},{2,6},{0,2},{5,1},{9,5},... | collective-permute-start | bytes 706568 | tf_op jit(solution)/shard_map/ppermute | solution.py:374
  54.1 8.4 %collective-permute-start.17 = (bf16[40,2944]{1,0:T(8,128)(2,1)S(1)}, bf16[40,2944]{1,0:T(8,128)(2,1)S(1)}, u32[]{:S(2)}, u32[]{:S(2)}) collective-permute-start(bf16[40,2944]{1,0:T(8,128)(2,1)S(1)} %get-tuple-element.110), channel_id=1, source_target_pairs={{0,4},{4,8},{8,12},{12,14},{14,10},{10,6},{6,2},{2,0},{1,5},{5,9},... | collective-permute-start | bytes 706568 | tf_op jit(solution)/shard_map/ppermute | solution.py:371
  55.7 7.8 %collective-permute-start.19 = (bf16[40,2944]{1,0:T(8,128)(2,1)S(1)}, bf16[40,2944]{1,0:T(8,128)(2,1)S(1)}, u32[]{:S(2)}, u32[]{:S(2)}) collective-permute-start(bf16[40,2944]{1,0:T(8,128)(2,1)S(1)} %get-tuple-element.109), channel_id=1, source_target_pairs={{4,0},{8,4},{12,8},{14,12},{10,14},{6,10},{2,6},{0,2},{5,1},{9,5},... | collective-permute-start | bytes 706568 | tf_op jit(solution)/shard_map/ppermute | solution.py:374
  58.4 10.6 %collective-permute-start.3 = (bf16[80,2944]{1,0:T(8,128)(2,1)S(1)}, bf16[80,2944]{1,0:T(8,128)(2,1)S(1)}, u32[]{:S(2)}, u32[]{:S(2)}) collective-permute-start(bf16[80,2944]{1,0:T(8,128)(2,1)S(1)} %get-tuple-element.63), channel_id=1, source_target_pairs={{0,16},{16,0},{1,17},{17,1},{2,18},{18,2},{3,19},{19,3},{4,20},{20... | collective-permute-start | bytes 1413128 | tf_op jit(solution)/shard_map/ppermute | solution.py:346
  63.7 6.1 %collective-permute-start.18 = (bf16[40,2944]{1,0:T(8,128)(2,1)S(1)}, bf16[40,2944]{1,0:T(8,128)(2,1)S(1)}, u32[]{:S(2)}, u32[]{:S(2)}) collective-permute-start(bf16[40,2944]{1,0:T(8,128)(2,1)S(1)} %get-tuple-element.112), channel_id=1, source_target_pairs={{0,4},{4,8},{8,12},{12,14},{14,10},{10,6},{6,2},{2,0},{1,5},{5,9},... | collective-permute-start | bytes 706568 | tf_op jit(solution)/shard_map/ppermute | solution.py:371
  65.3 6.1 %copy-start.3 = (f32[1,640]{1,0:T(1,128)S(1)}, f32[1,640]{1,0:T(1,128)}, u32[]{:S(2)}) copy-start(f32[1,640]{1,0:T(1,128)} %bias.1) | copy-start | bytes 7684
  65.3 6.1 %collective-permute-start.20 = (bf16[40,2944]{1,0:T(8,128)(2,1)S(1)}, bf16[40,2944]{1,0:T(8,128)(2,1)S(1)}, u32[]{:S(2)}, u32[]{:S(2)}) collective-permute-start(bf16[40,2944]{1,0:T(8,128)(2,1)S(1)} %get-tuple-element.111), channel_id=1, source_target_pairs={{4,0},{8,4},{12,8},{14,12},{10,14},{6,10},{2,6},{0,2},{5,1},{9,5},... | collective-permute-start | bytes 706568 | tf_op jit(solution)/shard_map/ppermute | solution.py:374
  65.8 5.6 %collective-permute-start.16 = (bf16[512,256]{1,0:T(8,128)(2,1)S(1)}, bf16[512,256]{1,0:T(8,128)(2,1)S(1)}, u32[]{:S(2)}, u32[]{:S(2)}) collective-permute-start(bf16[512,256]{1,0:T(8,128)(2,1)S(1)} %shard_map.124), channel_id=1, source_target_pairs={{0,1},{1,0},{2,3},{3,2},{4,5},{5,4},{6,7},{7,6},{8,9},{9,8},{10,11... | collective-permute-start | bytes 786440 | tf_op jit(solution)/shard_map/ppermute | solution.py:346
  71.5 1.2 %collective-permute-start.23 = (f32[3,640]{1,0:T(4,128)S(1)}, f32[3,640]{1,0:T(4,128)S(1)}, u32[]{:S(2)}, u32[]{:S(2)}) collective-permute-start(f32[3,640]{1,0:T(4,128)S(1)} %fusion.2), channel_id=1, source_target_pairs={{0,1},{1,0},{2,3},{3,2},{4,5},{5,4},{6,7},{7,6},{8,9},{9,8},{10,11... | collective-permute-start | bytes 23048 | tf_op jit(solution)/shard_map/ppermute | solution.py:346
  71.5 6.5 %collective-permute-start.22 = (bf16[512,512]{1,0:T(8,128)(2,1)S(1)}, bf16[512,512]{1,0:T(8,128)(2,1)S(1)}, u32[]{:S(2)}, u32[]{:S(2)}) collective-permute-start(bf16[512,512]{1,0:T(8,128)(2,1)S(1)} %get-tuple-element.93), channel_id=1, source_target_pairs={{0,1},{1,0},{2,3},{3,2},{4,5},{5,4},{6,7},{7,6},{8,9},{9,8},{10,11... | collective-permute-start | bytes 1572872 | tf_op jit(solution)/shard_map/ppermute | solution.py:346
  72.7 3.7 %collective-permute-start.24 = (f32[3,640]{1,0:T(4,128)S(1)}, f32[3,640]{1,0:T(4,128)S(1)}, u32[]{:S(2)}, u32[]{:S(2)}) collective-permute-start(f32[3,640]{1,0:T(4,128)S(1)} %fusion.4), channel_id=1, source_target_pairs={{0,16},{16,0},{1,17},{17,1},{2,18},{18,2},{3,19},{19,3},{4,20},{20... | collective-permute-start | bytes 23048 | tf_op jit(solution)/shard_map/ppermute | solution.py:395
  73.6 8.2 %collective-permute-start.21 = (bf16[40,2944]{1,0:T(8,128)(2,1)S(1)}, bf16[40,2944]{1,0:T(8,128)(2,1)S(1)}, u32[]{:S(2)}, u32[]{:S(2)}) collective-permute-start(bf16[40,2944]{1,0:T(8,128)(2,1)S(1)} %add_convert_fusion.1), channel_id=1, source_target_pairs={{0,4},{4,8},{8,12},{12,14},{14,10},{10,6},{6,2},{2,0},{1,5},{5,9},... | collective-permute-start | bytes 706568 | tf_op jit(solution)/shard_map/ppermute | solution.py:371
  76.5 5.3 %collective-permute-start.25 = (f32[3,640]{1,0:T(4,128)S(1)}, f32[3,640]{1,0:T(4,128)S(1)}, u32[]{:S(2)}, u32[]{:S(2)}) collective-permute-start(f32[3,640]{1,0:T(4,128)S(1)} %add.97), channel_id=1, source_target_pairs={{0,4},{4,0},{8,12},{12,8},{1,5},{5,1},{9,13},{13,9},{2,6},{6,2},{1... | collective-permute-start | bytes 23048 | tf_op jit(solution)/shard_map/ppermute | solution.py:395
  81.9 9.0 %collective-permute-start.26 = (bf16[40,2944]{1,0:T(8,128)(2,1)S(1)}, bf16[40,2944]{1,0:T(8,128)(2,1)S(1)}, u32[]{:S(2)}, u32[]{:S(2)}) collective-permute-start(bf16[40,2944]{1,0:T(8,128)(2,1)S(1)} %add_convert_fusion), channel_id=1, source_target_pairs={{0,16},{16,0},{1,17},{17,1},{2,18},{18,2},{3,19},{19,3},{4,20},{20... | collective-permute-start | bytes 706568 | tf_op jit(solution)/shard_map/ppermute | solution.py:346
  82.7 3.7 %collective-permute-start.27 = (f32[3,640]{1,0:T(4,128)S(1)}, f32[3,640]{1,0:T(4,128)S(1)}, u32[]{:S(2)}, u32[]{:S(2)}) collective-permute-start(f32[3,640]{1,0:T(4,128)S(1)} %add.98), channel_id=1, source_target_pairs={{0,2},{2,0},{1,3},{3,1},{4,6},{6,4},{5,7},{7,5},{8,10},{10,8},{9,1... | collective-permute-start | bytes 23048 | tf_op jit(solution)/shard_map/ppermute | solution.py:395
  86.4 4.6 %collective-permute-start.28 = (f32[3,640]{1,0:T(4,128)S(1)}, f32[3,640]{1,0:T(4,128)S(1)}, u32[]{:S(2)}, u32[]{:S(2)}) collective-permute-start(f32[3,640]{1,0:T(4,128)S(1)} %add.102), channel_id=1, source_target_pairs={{0,8},{4,12},{8,0},{12,4},{1,9},{5,13},{9,1},{13,5},{2,10},{6,14},... | collective-permute-start | bytes 23048 | tf_op jit(solution)/shard_map/ppermute | solution.py:395
  91.0 1.6 %collective-permute-start.29 = (bf16[40,2944]{1,0:T(8,128)(2,1)S(1)}, bf16[40,2944]{1,0:T(8,128)(2,1)S(1)}, u32[]{:S(2)}, u32[]{:S(2)}) collective-permute-start(bf16[40,2944]{1,0:T(8,128)(2,1)S(1)} %get-tuple-element.119), channel_id=1, source_target_pairs={{0,1},{1,0},{2,3},{3,2},{4,5},{5,4},{6,7},{7,6},{8,9},{9,8},{10,11... | collective-permute-start | bytes 706568 | tf_op jit(solution)/shard_map/ppermute | solution.py:346

commit v15 on v14

--- a/solution.py
+++ b/solution.py
@@ -524,7 +524,9 @@
 
     if paired:
         kept, *sent = pieces
-        crossed = [swap(piece, "replica") for piece in sent]
+        crossed = [swap(sent[0], "replica")]
+        up, down, stats, *sent[:3] = tied(up1, down1, stats, *sent[:3])
+        crossed += [swap(piece, "replica") for piece in sent[1:3]]
         theirs = crossed[1]
 
         def ring_sums(j, *received):
@@ -537,38 +539,39 @@
         def ring_step(ahead, behind):
             return ring.up(ahead), ring.down(behind)
 
-        up, down, stats, _ = tied(up1, down1, stats, sent[0])
         blocks = [unit, up, down]
         up, down = ring.up(up), ring.down(down)
         up, down, cots, *slopes, order = tied(up, down, *slopes_of(stats))
         blocks += [up, down]
 
-        ahead, behind = ring_sums(0)
-        up = ring.up(jnp.concatenate([up, ahead]))
-        down = ring.down(jnp.concatenate([down, behind]))
+        up, down = ring.up(up), ring.down(down)
         conv_first_own, conv_send = conv_first(blocks)
+        crossed[0], conv_send = tied(crossed[0], conv_send)
+        received = ring_step(*ring_sums(0))
         cots, conv_send = tied(cots, conv_send)
         first_sums = back(0, cots, slopes, blocks)
-        up, down, first_sums, crossed[1] = tied(up, down, first_sums, crossed[1])
+        up, down, first_sums, sent[3] = tied(up, down, first_sums, sent[3])
+        crossed.append(swap(sent[3], "replica"))
         late = [up, down]
-        received = up[2 * part:], down[2 * part:]
-
-        halves = ring.up(up[:part]), ring.down(down[part:2 * part])
+
+        halves = ring.up(up[:part]), ring.down(down[part:])
         conv_first_got = swap(conv_send, "core")
         for j in range(1, zs - 2):
             received = ring_step(*ring_sums(j, *received))
         late += halves
 
         conv_send = conv_far(acts, late)
-        crossed[2], cots, conv_send = tied(crossed[2], cots, conv_send)
+        cots, conv_send = tied(cots, conv_send)
         conv_got = swap(conv_send, "core")
+        sums = back(1, cots, slopes, late)
+        crossed[2], sums, *received = tied(crossed[2], sums, *received)
         received = ring_step(*ring_sums(zs - 2, *received))
-        sums = back(1, cots, slopes, late)
-        crossed[3], conv_got, sums, *received = tied(crossed[3], conv_got, sums, *received)
+        vectors = hop(chip_sum(first_sums + sums), "replica", 1)
+        crossed[3], conv_got, vectors, *received = tied(crossed[3], conv_got, vectors, *received)
         ahead, behind = ring_sums(zs - 1, *received)
         last = ring.up(ahead)
         block = conv_own(conv_got, [conv_first_own, conv_first_got, order], late)
-        vectors = hop(hop(chip_sum(first_sums + sums), "replica", 1), "z", 1)
+        vectors = hop(vectors, "z", 1)
         last, block, vectors = tied(last, block, vectors)
         total = add(*behind, last)
         vectors = hop(vectors, "y", 1)

time: 93.9 us -> 94.2 us (level)
    ppermute x7 -> x8, waiting for transfers between devices: 7.14 us -> 11.7 us  [up(): return lax.ppermute(value, NODE, self.ahead)]
    ppermute x13, waiting for transfers between devices: 5.21 us -> 1.55 us  [swap(): return lax.ppermute(value, axis, [(0, 1), (1, 0)])]
    ppermute x6 -> x7, waiting for transfers between devices: 7.14 us -> 4.07 us  [down(): return lax.ppermute(value, NODE, self.behind)]
    ppermute x4, waiting for transfers between devices: 6.32 us -> 8.82 us  [hop(): lax.ppermute(value, axis, [(s, s ^ mask) for s in range(count)])]
    ppermute x6 -> x7, starting transfers between devices: 2.38 us -> 3.15 us  [down(): return lax.ppermute(value, NODE, self.behind)]
    ppermute x7 -> x8, starting transfers between devices: 12.4 us -> 12.7 us  [up(): return lax.ppermute(value, NODE, self.ahead)]
  transfers between devices with their start and end apart: 30 -> 32, of which waited for: 16 -> 13; matrix products, arithmetic and copies ran while one was open for 1% -> 1% of each run, Pallas kernels for 33% -> 33%
where the time goes in v15:
time: 94.2 us; the launch traced here: 94.1 us
  Pallas kernels  32.4 us (34%)
  starting transfers between devices  30.9 us (33%)
  waiting for transfers between devices  26.1 us (28%)
  other arithmetic  2.92 us (3%)
  between operations  1.56 us (2%)
    ppermute x8, starting transfers between devices, up(): return lax.ppermute(value, NODE, self.ahead)  12.7 us
    ppermute x8, waiting for transfers between devices, up(): return lax.ppermute(value, NODE, self.ahead)  11.7 us
    ppermute x13, starting transfers between devices, swap(): return lax.ppermute(value, axis, [(0, 1), (1, 0)])  10.3 us
    ppermute x4, waiting for transfers between devices, hop(): lax.ppermute(value, axis, [(s, s ^ mask) for s in range(count)])  8.82 us
    pallas_call x2, Pallas kernels, back(): call(partial(back_kernel, cols, stages, stage), jax.ShapeDtypeStruct((2,...  8.61 us
    ppermute x4, starting transfers between devices, hop(): lax.ppermute(value, axis, [(s, s ^ mask) for s in range(count)])  4.7 us
    pallas_call x1, Pallas kernels, per_device(): call(partial(grad_kernel, cols, 2 if paired else None), [jax.ShapeDtypeSt...  4.63 us
    pallas_call x1, Pallas kernels, slopes_of(): call(partial(slope_kernel, stages), (jax.ShapeDtypeStruct((3, 2 * half +...  4.5 us
  transfers between devices with their start and end apart: 32, of which 13 were waited for; matrix products, arithmetic and copies ran while one was open for 1% of the time, Pallas kernels for 33%

profile of v15, /device:TPU:0, one launch (start us, length us, event | category | flops | bytes accessed | tf_op | source)
XLA Modules:
  0.0 94.1 jit_solution(8011442037744561713)
XLA Ops:
  0.7 2.0 %fusion.3 = (f32[640]{0:T(1024)S(1)}, bf16[16,32,640]{2,1,0:T(8,128)(2,1)S(1)}) fusion(f32[1,16,32,640]{3,2,1,0:T(8,128)} %param.9), kind=kLoop, calls=%fused_computation.19 | loop fusion | flops 654720 | bytes 1968640 | tf_op jit(solution)/shard_map/reduce_sum | solution.py:521
  2.7 0.5 collective-permute-start.2
  3.4 0.5 collective-permute-start.3
  3.8 2.6 %collective-permute-start = (bf16[40,2944]{1,0:T(8,128)(2,1)S(1)}, bf16[40,2944]{1,0:T(8,128)(2,1)S(1)}, u32[]{:S(2)}, u32[]{:S(2)}) collective-permute-start(bf16[40,2944]{1,0:T(8,128)(2,1)S(1)} %get-tuple-element.131), channel_id=1, source_target_pairs={{0,16},{16,0},{1,17},{17,1},{2,18},{18,2},{3,19},{19,3},{4,20},{20... | collective-permute-start | bytes 706568 | tf_op jit(solution)/shard_map/ppermute | solution.py:346
  6.5 2.8 %collective-permute-start.4 = (bf16[80,2944]{1,0:T(8,128)(2,1)S(1)}, bf16[80,2944]{1,0:T(8,128)(2,1)S(1)}, u32[]{:S(2)}, u32[]{:S(2)}) collective-permute-start(bf16[80,2944]{1,0:T(8,128)(2,1)S(1)} %maximum_select_fusion.refs_0_), channel_id=1, source_target_pairs={{0,4},{4,8},{8,12},{12,14},{14,10},{10,6},{6,2},{2,0},{1,5},{5,9},... | collective-permute-start | bytes 1413128 | tf_op jit(solution)/shard_map/ppermute | solution.py:371
  9.3 4.4 %shard_map.119 = (f32[2,640]{1,0:T(2,128)S(1)}, bf16[3,34,32,640]{3,2,1,0:T(8,128)(2,1)S(1)}, bf16[640,1024]{1,0:T(8,128)(2,1)S(1)}) custom-call(s32[1]{0:T(128)} %bitcast.dev, s32[32,24]{1,0:T(8,128)S(1)} %copy-done.5, bf16[16,32,640]{2,1,0:T(8,128)(2,1)S(1)} %bitcast.13, bf16[16,32,640]{2,1,0:T(8,128)(2,1)S(1)} %collective-permute-done.1.lat_far, ...), custom_call_target="tpu_custom_call" | custom-call | flops 3858759680 | tf_op jit(solution)/shard_map/pallas_call | solution.py:457
  13.7 4.6 %shard_map.120 = (bf16[320,2944]{1,0:T(8,128)(2,1)S(1)}, bf16[80,2944]{1,0:T(8,128)(2,1)S(1)}, bf16[120,2944]{1,0:T(8,128)(2,1)S(1)}, bf16[80,2944]{1,0:T(8,128)(2,1)S(1)}, bf16[80,2944]{1,0:T(8,128)(2,1)S(1)}) custom-call(s32[1]{0:T(128)} %bitcast.dev, bf16[3,34,32,640]{3,2,1,0:T(8,128)(2,1)S(1)} %get-tuple-element.67.acts, ...), custom_call_target="tpu_custom_call" | custom-call | flops 7717519360 | tf_op jit(solution)/shard_map/pallas_call | solution.py:467
  18.4 1.9 %collective-permute-done.4.refs_1_ = bf16[80,2944]{1,0:T(8,128)(2,1)S(1)} collective-permute-done((bf16[80,2944]{1,0:T(8,128)(2,1)S(1)}, bf16[80,2944]{1,0:T(8,128)(2,1)S(1)}, u32[]{:S(2)}, u32[]{:S(2)}) %collective-permute-start.4) | collective-permute-done | bytes 471072 | tf_op jit(solution)/shard_map/ppermute | solution.py:371
  20.3 1.5 %collective-permute-done.5.refs_2_ = bf16[80,2944]{1,0:T(8,128)(2,1)S(1)} collective-permute-done((bf16[80,2944]{1,0:T(8,128)(2,1)S(1)}, bf16[80,2944]{1,0:T(8,128)(2,1)S(1)}, u32[]{:S(2)}, u32[]{:S(2)}) %collective-permute-start.5) | collective-permute-done | bytes 471072 | tf_op jit(solution)/shard_map/ppermute | solution.py:374
  21.8 1.6 %collective-permute-start.6 = (bf16[80,2944]{1,0:T(8,128)(2,1)S(1)}, bf16[80,2944]{1,0:T(8,128)(2,1)S(1)}, u32[]{:S(2)}, u32[]{:S(2)}) collective-permute-start(bf16[80,2944]{1,0:T(8,128)(2,1)S(1)} %collective-permute-done.4.refs_1_), channel_id=1, source_target_pairs={{0,4},{4,8},{8,12},{12,14},{14,10},{10,6},{6,2},{2,0},{1,5},{5,9},... | collective-permute-start | bytes 1413128 | tf_op jit(solution)/shard_map/ppermute | solution.py:371
  23.4 0.4 collective-permute-start.7
  23.9 1.5 %collective-permute-start.10 = (bf16[80,2944]{1,0:T(8,128)(2,1)S(1)}, bf16[80,2944]{1,0:T(8,128)(2,1)S(1)}, u32[]{:S(2)}, u32[]{:S(2)}) collective-permute-start(bf16[80,2944]{1,0:T(8,128)(2,1)S(1)} %get-tuple-element.72), channel_id=1, source_target_pairs={{0,16},{16,0},{1,17},{17,1},{2,18},{18,2},{3,19},{19,3},{4,20},{20... | collective-permute-start | bytes 1413128 | tf_op jit(solution)/shard_map/ppermute | solution.py:346
  25.3 0.5 collective-permute-start.16
  25.9 4.5 %shard_map.121 = (bf16[3,34,32,768]{3,2,1,0:T(8,128)(2,1)S(1)}, bf16[32,32,640]{2,1,0:T(8,128)(2,1)S(1)}, bf16[32,32,640]{2,1,0:T(8,128)(2,1)S(1)}, bf16[640,768]{1,0:T(8,128)(2,1)S(1)}) custom-call(s32[1]{0:T(128)} %bitcast.dev, s32[32,24]{1,0:T(8,128)S(1)} %copy-done.5, f32[2,640]{1,0:T(2,128)S(1)} %get-tuple-element.77.stats, f32[1,640]{1,0:T(1,128)S(1)} %copy-done.1, ...), custom_call_target="tpu_custom_call" | custom-call | flops 3858759680 | tf_op jit(solution)/shard_map/pallas_call | solution.py:479
  30.4 3.1 %collective-permute-done.6.refs_3_ = bf16[80,2944]{1,0:T(8,128)(2,1)S(1)} collective-permute-done((bf16[80,2944]{1,0:T(8,128)(2,1)S(1)}, bf16[80,2944]{1,0:T(8,128)(2,1)S(1)}, u32[]{:S(2)}, u32[]{:S(2)}) %collective-permute-start.6) | collective-permute-done | bytes 471072 | tf_op jit(solution)/shard_map/ppermute | solution.py:371
  33.5 1.3 %collective-permute-done.7.refs_4_ = bf16[80,2944]{1,0:T(8,128)(2,1)S(1)} collective-permute-done((bf16[80,2944]{1,0:T(8,128)(2,1)S(1)}, bf16[80,2944]{1,0:T(8,128)(2,1)S(1)}, u32[]{:S(2)}, u32[]{:S(2)}) %collective-permute-start.7) | collective-permute-done | bytes 471072 | tf_op jit(solution)/shard_map/ppermute | solution.py:374
  34.8 1.6 %collective-permute-start.8 = (bf16[80,2944]{1,0:T(8,128)(2,1)S(1)}, bf16[80,2944]{1,0:T(8,128)(2,1)S(1)}, u32[]{:S(2)}, u32[]{:S(2)}) collective-permute-start(bf16[80,2944]{1,0:T(8,128)(2,1)S(1)} %collective-permute-done.6.refs_3_), channel_id=1, source_target_pairs={{0,4},{4,8},{8,12},{12,14},{14,10},{10,6},{6,2},{2,0},{1,5},{5,9},... | collective-permute-start | bytes 1413128 | tf_op jit(solution)/shard_map/ppermute | solution.py:371
  36.4 0.4 collective-permute-start.9
  36.8 4.0 %shard_map.122 = (f32[512,512]{1,0:T(8,128)S(1)}, bf16[512,512]{1,0:T(8,128)(2,1)S(1)}) custom-call(s32[1]{0:T(128)} %bitcast.dev, bf16[3,34,32,640]{3,2,1,0:T(8,128)(2,1)S(1)} %get-tuple-element.67.acts, bf16[80,2944]{1,0:T(8,128)(2,1)S(1)} %maximum_select_fusion.refs_0_, bf16[80,2944]{1,0:T(8,128)(2,1)S(1)} %collective-permute-done.4.refs_1_, ...), custom_call_target="tpu_custom_call" | custom-call | flops 3858759680 | tf_op jit(solution)/shard_map/pallas_call | solution.py:497
  40.9 1.6 %collective-permute-start.17 = (bf16[40,2944]{1,0:T(8,128)(2,1)S(1)}, bf16[40,2944]{1,0:T(8,128)(2,1)S(1)}, u32[]{:S(2)}, u32[]{:S(2)}) collective-permute-start(bf16[40,2944]{1,0:T(8,128)(2,1)S(1)} %get-tuple-element.128), channel_id=1, source_target_pairs={{0,4},{4,8},{8,12},{12,14},{14,10},{10,6},{6,2},{2,0},{1,5},{5,9},... | collective-permute-start | bytes 706568 | tf_op jit(solution)/shard_map/ppermute | solution.py:371
  43.0 5.4 %shard_map.123 = f32[2,640]{1,0:T(2,128)S(1)} custom-call(s32[1]{0:T(128)} %bitcast.dev, bf16[3,34,32,768]{3,2,1,0:T(8,128)(2,1)S(1)} %get-tuple-element.97.cots, bf16[32,32,640]{2,1,0:T(8,128)(2,1)S(1)} %get-tuple-element.88.slope, bf16[32,32,640]{2,1,0:T(8,128)(2,1)S(1)} %get-tuple-element.89.slope_x, bf16[80,2944]{1,0:T(8,128)(2,1)S(1)} %maximum_select_fusion.refs_0_, ...), custom_call_target="tpu_custom_call" | custom-call | flops 3858759680 | tf_op jit(solution)/shard_map/pallas_call | solution.py:489
  48.4 1.6 %collective-permute-start.15 = (bf16[80,2944]{1,0:T(8,128)(2,1)S(1)}, bf16[80,2944]{1,0:T(8,128)(2,1)S(1)}, u32[]{:S(2)}, u32[]{:S(2)}) collective-permute-start(bf16[80,2944]{1,0:T(8,128)(2,1)S(1)} %get-tuple-element.96), channel_id=1, source_target_pairs={{0,16},{16,0},{1,17},{17,1},{2,18},{18,2},{3,19},{19,3},{4,20},{20... | collective-permute-start | bytes 1413128 | tf_op jit(solution)/shard_map/ppermute | solution.py:346
  50.0 1.6 %collective-permute-start.12 = (bf16[40,2944]{1,0:T(8,128)(2,1)S(1)}, bf16[40,2944]{1,0:T(8,128)(2,1)S(1)}, u32[]{:S(2)}, u32[]{:S(2)}) collective-permute-start(bf16[40,2944]{1,0:T(8,128)(2,1)S(1)} %slice.67), channel_id=1, source_target_pairs={{0,4},{4,8},{8,12},{12,14},{14,10},{10,6},{6,2},{2,0},{1,5},{5,9},... | collective-permute-start | bytes 706568 | tf_op jit(solution)/shard_map/ppermute | solution.py:371
  51.7 0.7 collective-permute-done.16.carried
  52.4 0.6 collective-permute-start.13
  53.2 1.4 %collective-permute-start.18 = (bf16[40,2944]{1,0:T(8,128)(2,1)S(1)}, bf16[40,2944]{1,0:T(8,128)(2,1)S(1)}, u32[]{:S(2)}, u32[]{:S(2)}) collective-permute-start(bf16[40,2944]{1,0:T(8,128)(2,1)S(1)} %get-tuple-element.124), channel_id=1, source_target_pairs={{0,4},{4,8},{8,12},{12,14},{14,10},{10,6},{6,2},{2,0},{1,5},{5,9},... | collective-permute-start | bytes 706568 | tf_op jit(solution)/shard_map/ppermute | solution.py:371
  54.6 0.6 collective-permute-start.20
  55.3 2.6 %collective-permute-done.12.refs_2_.refs_5_ = bf16[40,2944]{1,0:T(8,128)(2,1)S(1)} collective-permute-done((bf16[40,2944]{1,0:T(8,128)(2,1)S(1)}, bf16[40,2944]{1,0:T(8,128)(2,1)S(1)}, u32[]{:S(2)}, u32[]{:S(2)}) %collective-permute-start.12) | collective-permute-done | bytes 235552 | tf_op jit(solution)/shard_map/ppermute | solution.py:371
  57.9 1.4 %collective-permute-start.11 = (bf16[80,2944]{1,0:T(8,128)(2,1)S(1)}, bf16[80,2944]{1,0:T(8,128)(2,1)S(1)}, u32[]{:S(2)}, u32[]{:S(2)}) collective-permute-start(bf16[80,2944]{1,0:T(8,128)(2,1)S(1)} %get-tuple-element.91), channel_id=1, source_target_pairs={{0,16},{16,0},{1,17},{17,1},{2,18},{18,2},{3,19},{19,3},{4,20},{20... | collective-permute-start | bytes 1413128 | tf_op jit(solution)/shard_map/ppermute | solution.py:346
  59.3 1.4 %shard_map.124 = bf16[512,256]{1,0:T(8,128)(2,1)S(1)} custom-call(s32[1]{0:T(128)} %bitcast.dev, bf16[3,34,32,640]{3,2,1,0:T(8,128)(2,1)S(1)} %get-tuple-element.67.acts, bf16[80,2944]{1,0:T(8,128)(2,1)S(1)} %collective-permute-done.8.refs_0_.refs_3_, bf16[80,2944]{1,0:T(8,128)(2,1)S(1)} %collective-permute-done.9.refs_1_.refs_4_, ...), custom_call_target="tpu_custom_call" | custom-call | flops 1929379840 | tf_op jit(solution)/shard_map/pallas_call | solution.py:506
  60.8 3.2 %shard_map.125 = f32[2,640]{1,0:T(2,128)S(1)} custom-call(s32[1]{0:T(128)} %bitcast.dev, bf16[3,34,32,768]{3,2,1,0:T(8,128)(2,1)S(1)} %get-tuple-element.97.cots, bf16[32,32,640]{2,1,0:T(8,128)(2,1)S(1)} %get-tuple-element.88.slope, bf16[32,32,640]{2,1,0:T(8,128)(2,1)S(1)} %get-tuple-element.89.slope_x, ...), custom_call_target="tpu_custom_call" | custom-call | flops 3858759680 | tf_op jit(solution)/shard_map/pallas_call | solution.py:489
  64.2 0.5 collective-permute-start.14
  64.9 1.6 %collective-permute-start.23 = (bf16[40,2944]{1,0:T(8,128)(2,1)S(1)}, bf16[40,2944]{1,0:T(8,128)(2,1)S(1)}, u32[]{:S(2)}, u32[]{:S(2)}) collective-permute-start(bf16[40,2944]{1,0:T(8,128)(2,1)S(1)} %get-tuple-element.126), channel_id=1, source_target_pairs={{0,4},{4,8},{8,12},{12,14},{14,10},{10,6},{6,2},{2,0},{1,5},{5,9},... | collective-permute-start | bytes 706568 | tf_op jit(solution)/shard_map/ppermute | solution.py:371
  66.4 0.5 collective-permute-start.24
  67.0 1.4 %collective-permute-start.22 = (f32[3,640]{1,0:T(4,128)S(1)}, f32[3,640]{1,0:T(4,128)S(1)}, u32[]{:S(2)}, u32[]{:S(2)}) collective-permute-start(f32[3,640]{1,0:T(4,128)S(1)} %fusion.4), channel_id=1, source_target_pairs={{0,16},{16,0},{1,17},{17,1},{2,18},{18,2},{3,19},{19,3},{4,20},{20... | collective-permute-start | bytes 23048 | tf_op jit(solution)/shard_map/ppermute | solution.py:395
  68.4 2.3 %collective-permute-done.22 = f32[3,640]{1,0:T(4,128)S(1)} collective-permute-done((f32[3,640]{1,0:T(4,128)S(1)}, f32[3,640]{1,0:T(4,128)S(1)}, u32[]{:S(2)}, u32[]{:S(2)}) %collective-permute-start.22) | collective-permute-done | bytes 7712 | tf_op jit(solution)/shard_map/ppermute | solution.py:395
  70.7 1.9 %collective-permute-done.23 = bf16[40,2944]{1,0:T(8,128)(2,1)S(1)} collective-permute-done((bf16[40,2944]{1,0:T(8,128)(2,1)S(1)}, bf16[40,2944]{1,0:T(8,128)(2,1)S(1)}, u32[]{:S(2)}, u32[]{:S(2)}) %collective-permute-start.23) | collective-permute-done | bytes 235552 | tf_op jit(solution)/shard_map/ppermute | solution.py:371
  72.6 1.2 %collective-permute-done.24 = bf16[40,2944]{1,0:T(8,128)(2,1)S(1)} collective-permute-done((bf16[40,2944]{1,0:T(8,128)(2,1)S(1)}, bf16[40,2944]{1,0:T(8,128)(2,1)S(1)}, u32[]{:S(2)}, u32[]{:S(2)}) %collective-permute-start.24) | collective-permute-done | bytes 235552 | tf_op jit(solution)/shard_map/ppermute | solution.py:374
  73.9 1.5 %collective-permute-start.27 = (f32[3,640]{1,0:T(4,128)S(1)}, f32[3,640]{1,0:T(4,128)S(1)}, u32[]{:S(2)}, u32[]{:S(2)}) collective-permute-start(f32[3,640]{1,0:T(4,128)S(1)} %add.91), channel_id=1, source_target_pairs={{0,4},{4,0},{8,12},{12,8},{1,5},{5,1},{9,13},{13,9},{2,6},{6,2},{1... | collective-permute-start | bytes 23048 | tf_op jit(solution)/shard_map/ppermute | solution.py:395
  75.5 0.5 collective-permute-start.25
  76.1 3.7 %shard_map.126 = bf16[16,32,640]{2,1,0:T(8,128)(2,1)} custom-call(s32[1]{0:T(128)} %bitcast.dev, bf16[3,34,32,640]{3,2,1,0:T(8,128)(2,1)S(1)} %get-tuple-element.67.acts, bf16[512,256]{1,0:T(8,128)(2,1)S(1)} %collective-permute-done.14.got, bf16[16,32,640]{2,1,0:T(8,128)(2,1)S(1)} %bitcast.15, f32[1,640]{1,0:T(1,128)S(1)} %copy-done.3, ...), custom_call_target="tpu_custom_call" | custom-call | flops 3858759680 | tf_op jit(solution)/shard_map/pallas_call | solution.py:514
  79.8 2.1 %collective-permute-done.25 = bf16[40,2944]{1,0:T(8,128)(2,1)S(1)} collective-permute-done((bf16[40,2944]{1,0:T(8,128)(2,1)S(1)}, bf16[40,2944]{1,0:T(8,128)(2,1)S(1)}, u32[]{:S(2)}, u32[]{:S(2)}) %collective-permute-start.25) | collective-permute-done | bytes 235552 | tf_op jit(solution)/shard_map/ppermute | solution.py:371
  82.0 1.0 %collective-permute-start.28 = (bf16[40,2944]{1,0:T(8,128)(2,1)S(1)}, bf16[40,2944]{1,0:T(8,128)(2,1)S(1)}, u32[]{:S(2)}, u32[]{:S(2)}) collective-permute-start(bf16[40,2944]{1,0:T(8,128)(2,1)S(1)} %add_convert_fusion), channel_id=1, source_target_pairs={{0,16},{16,0},{1,17},{17,1},{2,18},{18,2},{3,19},{19,3},{4,20},{20... | collective-permute-start | bytes 706568 | tf_op jit(solution)/shard_map/ppermute | solution.py:346
  83.0 3.7 %collective-permute-done.29 = f32[3,640]{1,0:T(4,128)S(1)} collective-permute-done((f32[3,640]{1,0:T(4,128)S(1)}, f32[3,640]{1,0:T(4,128)S(1)}, u32[]{:S(2)}, u32[]{:S(2)}) %collective-permute-start.29) | collective-permute-done | bytes 7712 | tf_op jit(solution)/shard_map/ppermute | solution.py:395
  86.7 1.7 %collective-permute-start.30 = (f32[3,640]{1,0:T(4,128)S(1)}, f32[3,640]{1,0:T(4,128)S(1)}, u32[]{:S(2)}, u32[]{:S(2)}) collective-permute-start(f32[3,640]{1,0:T(4,128)S(1)} %add.102), channel_id=1, source_target_pairs={{0,8},{4,12},{8,0},{12,4},{1,9},{5,13},{9,1},{13,5},{2,10},{6,14},... | collective-permute-start | bytes 23048 | tf_op jit(solution)/shard_map/ppermute | solution.py:395
  88.4 2.8 %collective-permute-done.30 = f32[3,640]{1,0:T(4,128)S(1)} collective-permute-done((f32[3,640]{1,0:T(4,128)S(1)}, f32[3,640]{1,0:T(4,128)S(1)}, u32[]{:S(2)}, u32[]{:S(2)}) %collective-permute-start.30) | collective-permute-done | bytes 7712 | tf_op jit(solution)/shard_map/ppermute | solution.py:395
  92.0 0.8 collective-permute-done.31.aside
  92.8 1.2 %shard_map.127 = (f32[40,5760]{1,0:T(8,128)}, f32[1,640]{1,0:T(1,128)}, f32[1,640]{1,0:T(1,128)}, f32[1,640]{1,0:T(1,128)}) custom-call(s32[1]{0:T(128)} %bitcast.dev, s32[1]{0:T(128)S(6)} %copy.13.step, f32[40,5760]{1,0:T(8,128)S(1)} %bitcast.11, bf16[40,2944]{1,0:T(8,128)(2,1)S(1)} %collective-permute-done.mine, ...), custom_call_target="tpu_custom_call" | custom-call | flops 964689920 | tf_op jit(solution)/shard_map/pallas_call | solution.py:586
  (56 shorter events, 1.8 us)
Async XLA Ops:
  0.6 2.6 %copy-start.4 = (bf16[1,16,32,640]{3,2,1,0:T(8,128)(2,1)S(1)}, bf16[1,16,32,640]{3,2,1,0:T(8,128)(2,1)}, u32[]{:S(2)}) copy-start(bf16[1,16,32,640]{3,2,1,0:T(8,128)(2,1)} %param.8) | copy-start | bytes 1966084
  0.6 2.6 %copy-start = (f32[1,40,5760]{2,1,0:T(8,128)S(1)}, f32[1,40,5760]{2,1,0:T(8,128)}, u32[]{:S(2)}) copy-start(f32[1,40,5760]{2,1,0:T(8,128)} %param.10) | copy-start | bytes 2764804
  0.7 8.6 %copy-start.1 = (f32[1,640]{1,0:T(1,128)S(1)}, f32[1,640]{1,0:T(1,128)}, u32[]{:S(2)}) copy-start(f32[1,640]{1,0:T(1,128)} %gain.3) | copy-start | bytes 7684
  0.7 8.6 %copy-start.2 = (f32[1,640]{1,0:T(1,128)S(1)}, f32[1,640]{1,0:T(1,128)}, u32[]{:S(2)}) copy-start(f32[1,640]{1,0:T(1,128)} %shift.3) | copy-start | bytes 7684
  2.7 6.6 %collective-permute-start.2 = (bf16[16,32,640]{2,1,0:T(8,128)(2,1)S(1)}, bf16[16,32,640]{2,1,0:T(8,128)(2,1)S(1)}, u32[]{:S(2)}, u32[]{:S(2)}) collective-permute-start(bf16[16,32,640]{2,1,0:T(8,128)(2,1)S(1)} %get-tuple-element.130.cot_own), channel_id=1, source_target_pairs={{0,1},{1,0},{2,3},{3,2},{4,5},{5,4},{6,7},{7,6},{8,9},{9,8},{10,11... | collective-permute-start | bytes 1966088 | tf_op jit(solution)/shard_map/ppermute | solution.py:346
  3.2 6.1 %collective-permute-start.1 = (bf16[16,32,640]{2,1,0:T(8,128)(2,1)S(1)}, bf16[16,32,640]{2,1,0:T(8,128)(2,1)S(1)}, u32[]{:S(2)}, u32[]{:S(2)}) collective-permute-start(bf16[16,32,640]{2,1,0:T(8,128)(2,1)S(1)} %bitcast.12), channel_id=1, source_target_pairs={{0,1},{1,0},{2,3},{3,2},{4,5},{5,4},{6,7},{7,6},{8,9},{9,8},{10,11... | collective-permute-start | bytes 1966088 | tf_op jit(solution)/shard_map/ppermute | solution.py:346
  3.3 6.0 %copy-start.5 = (s32[32,24]{1,0:T(8,128)S(1)}, s32[32,24]{1,0:T(8,128)}, u32[]{:S(2)}) copy-start(s32[32,24]{1,0:T(8,128)} %constant.38.clone.table) | copy-start | bytes 9220
  3.4 3.1 %collective-permute-start.3 = (bf16[40,2944]{1,0:T(8,128)(2,1)S(1)}, bf16[40,2944]{1,0:T(8,128)(2,1)S(1)}, u32[]{:S(2)}, u32[]{:S(2)}) collective-permute-start(bf16[40,2944]{1,0:T(8,128)(2,1)S(1)} %get-tuple-element.132.theirs), channel_id=1, source_target_pairs={{0,1},{1,0},{2,3},{3,2},{4,5},{5,4},{6,7},{7,6},{8,9},{9,8},{10,11... | collective-permute-start | bytes 706568 | tf_op jit(solution)/shard_map/ppermute | solution.py:346
  3.8 9.9 %collective-permute-start = (bf16[40,2944]{1,0:T(8,128)(2,1)S(1)}, bf16[40,2944]{1,0:T(8,128)(2,1)S(1)}, u32[]{:S(2)}, u32[]{:S(2)}) collective-permute-start(bf16[40,2944]{1,0:T(8,128)(2,1)S(1)} %get-tuple-element.131), channel_id=1, source_target_pairs={{0,16},{16,0},{1,17},{17,1},{2,18},{18,2},{3,19},{19,3},{4,20},{20... | collective-permute-start | bytes 706568 | tf_op jit(solution)/shard_map/ppermute | solution.py:346
  6.5 13.8 %collective-permute-start.4 = (bf16[80,2944]{1,0:T(8,128)(2,1)S(1)}, bf16[80,2944]{1,0:T(8,128)(2,1)S(1)}, u32[]{:S(2)}, u32[]{:S(2)}) collective-permute-start(bf16[80,2944]{1,0:T(8,128)(2,1)S(1)} %maximum_select_fusion.refs_0_), channel_id=1, source_target_pairs={{0,4},{4,8},{8,12},{12,14},{14,10},{10,6},{6,2},{2,0},{1,5},{5,9},... | collective-permute-start | bytes 1413128 | tf_op jit(solution)/shard_map/ppermute | solution.py:371
  9.3 12.5 %collective-permute-start.5 = (bf16[80,2944]{1,0:T(8,128)(2,1)S(1)}, bf16[80,2944]{1,0:T(8,128)(2,1)S(1)}, u32[]{:S(2)}, u32[]{:S(2)}) collective-permute-start(bf16[80,2944]{1,0:T(8,128)(2,1)S(1)} %maximum_select_fusion.refs_0_), channel_id=1, source_target_pairs={{4,0},{8,4},{12,8},{14,12},{10,14},{6,10},{2,6},{0,2},{5,1},{9,5},... | collective-permute-start | bytes 1413128 | tf_op jit(solution)/shard_map/ppermute | solution.py:374
  21.8 11.7 %collective-permute-start.6 = (bf16[80,2944]{1,0:T(8,128)(2,1)S(1)}, bf16[80,2944]{1,0:T(8,128)(2,1)S(1)}, u32[]{:S(2)}, u32[]{:S(2)}) collective-permute-start(bf16[80,2944]{1,0:T(8,128)(2,1)S(1)} %collective-permute-done.4.refs_1_), channel_id=1, source_target_pairs={{0,4},{4,8},{8,12},{12,14},{14,10},{10,6},{6,2},{2,0},{1,5},{5,9},... | collective-permute-start | bytes 1413128 | tf_op jit(solution)/shard_map/ppermute | solution.py:371
  23.4 11.4 %collective-permute-start.7 = (bf16[80,2944]{1,0:T(8,128)(2,1)S(1)}, bf16[80,2944]{1,0:T(8,128)(2,1)S(1)}, u32[]{:S(2)}, u32[]{:S(2)}) collective-permute-start(bf16[80,2944]{1,0:T(8,128)(2,1)S(1)} %collective-permute-done.5.refs_2_), channel_id=1, source_target_pairs={{4,0},{8,4},{12,8},{14,12},{10,14},{6,10},{2,6},{0,2},{5,1},{9,5},... | collective-permute-start | bytes 1413128 | tf_op jit(solution)/shard_map/ppermute | solution.py:374
  23.9 17.0 %collective-permute-start.10 = (bf16[80,2944]{1,0:T(8,128)(2,1)S(1)}, bf16[80,2944]{1,0:T(8,128)(2,1)S(1)}, u32[]{:S(2)}, u32[]{:S(2)}) collective-permute-start(bf16[80,2944]{1,0:T(8,128)(2,1)S(1)} %get-tuple-element.72), channel_id=1, source_target_pairs={{0,16},{16,0},{1,17},{17,1},{2,18},{18,2},{3,19},{19,3},{4,20},{20... | collective-permute-start | bytes 1413128 | tf_op jit(solution)/shard_map/ppermute | solution.py:346
  25.3 27.0 %collective-permute-start.16 = (bf16[120,2944]{1,0:T(8,128)(2,1)S(1)}, bf16[120,2944]{1,0:T(8,128)(2,1)S(1)}, u32[]{:S(2)}, u32[]{:S(2)}) collective-permute-start(bf16[120,2944]{1,0:T(8,128)(2,1)S(1)} %get-tuple-element.98), channel_id=1, source_target_pairs={{0,16},{16,0},{1,17},{17,1},{2,18},{18,2},{3,19},{19,3},{4,20},{20... | collective-permute-start | bytes 2119688 | tf_op jit(solution)/shard_map/ppermute | solution.py:346
  34.8 13.6 %collective-permute-start.8 = (bf16[80,2944]{1,0:T(8,128)(2,1)S(1)}, bf16[80,2944]{1,0:T(8,128)(2,1)S(1)}, u32[]{:S(2)}, u32[]{:S(2)}) collective-permute-start(bf16[80,2944]{1,0:T(8,128)(2,1)S(1)} %collective-permute-done.6.refs_3_), channel_id=1, source_target_pairs={{0,4},{4,8},{8,12},{12,14},{14,10},{10,6},{6,2},{2,0},{1,5},{5,9},... | collective-permute-start | bytes 1413128 | tf_op jit(solution)/shard_map/ppermute | solution.py:371
  36.4 13.6 %collective-permute-start.9 = (bf16[80,2944]{1,0:T(8,128)(2,1)S(1)}, bf16[80,2944]{1,0:T(8,128)(2,1)S(1)}, u32[]{:S(2)}, u32[]{:S(2)}) collective-permute-start(bf16[80,2944]{1,0:T(8,128)(2,1)S(1)} %collective-permute-done.7.refs_4_), channel_id=1, source_target_pairs={{4,0},{8,4},{12,8},{14,12},{10,14},{6,10},{2,6},{0,2},{5,1},{9,5},... | collective-permute-start | bytes 1413128 | tf_op jit(solution)/shard_map/ppermute | solution.py:374
  40.9 12.1 %collective-permute-start.17 = (bf16[40,2944]{1,0:T(8,128)(2,1)S(1)}, bf16[40,2944]{1,0:T(8,128)(2,1)S(1)}, u32[]{:S(2)}, u32[]{:S(2)}) collective-permute-start(bf16[40,2944]{1,0:T(8,128)(2,1)S(1)} %get-tuple-element.128), channel_id=1, source_target_pairs={{0,4},{4,8},{8,12},{12,14},{14,10},{10,6},{6,2},{2,0},{1,5},{5,9},... | collective-permute-start | bytes 706568 | tf_op jit(solution)/shard_map/ppermute | solution.py:371
  42.6 10.4 %collective-permute-start.19 = (bf16[40,2944]{1,0:T(8,128)(2,1)S(1)}, bf16[40,2944]{1,0:T(8,128)(2,1)S(1)}, u32[]{:S(2)}, u32[]{:S(2)}) collective-permute-start(bf16[40,2944]{1,0:T(8,128)(2,1)S(1)} %get-tuple-element.127), channel_id=1, source_target_pairs={{4,0},{8,4},{12,8},{14,12},{10,14},{6,10},{2,6},{0,2},{5,1},{9,5},... | collective-permute-start | bytes 706568 | tf_op jit(solution)/shard_map/ppermute | solution.py:374
  48.4 15.6 %collective-permute-start.15 = (bf16[80,2944]{1,0:T(8,128)(2,1)S(1)}, bf16[80,2944]{1,0:T(8,128)(2,1)S(1)}, u32[]{:S(2)}, u32[]{:S(2)}) collective-permute-start(bf16[80,2944]{1,0:T(8,128)(2,1)S(1)} %get-tuple-element.96), channel_id=1, source_target_pairs={{0,16},{16,0},{1,17},{17,1},{2,18},{18,2},{3,19},{19,3},{4,20},{20... | collective-permute-start | bytes 1413128 | tf_op jit(solution)/shard_map/ppermute | solution.py:346
  50.0 7.9 %collective-permute-start.12 = (bf16[40,2944]{1,0:T(8,128)(2,1)S(1)}, bf16[40,2944]{1,0:T(8,128)(2,1)S(1)}, u32[]{:S(2)}, u32[]{:S(2)}) collective-permute-start(bf16[40,2944]{1,0:T(8,128)(2,1)S(1)} %slice.67), channel_id=1, source_target_pairs={{0,4},{4,8},{8,12},{12,14},{14,10},{10,6},{6,2},{2,0},{1,5},{5,9},... | collective-permute-start | bytes 706568 | tf_op jit(solution)/shard_map/ppermute | solution.py:371
  52.4 7.0 %collective-permute-start.13 = (bf16[40,2944]{1,0:T(8,128)(2,1)S(1)}, bf16[40,2944]{1,0:T(8,128)(2,1)S(1)}, u32[]{:S(2)}, u32[]{:S(2)}) collective-permute-start(bf16[40,2944]{1,0:T(8,128)(2,1)S(1)} %slice.68), channel_id=1, source_target_pairs={{4,0},{8,4},{12,8},{14,12},{10,14},{6,10},{2,6},{0,2},{5,1},{9,5},... | collective-permute-start | bytes 706568 | tf_op jit(solution)/shard_map/ppermute | solution.py:374
  53.2 10.8 %collective-permute-start.18 = (bf16[40,2944]{1,0:T(8,128)(2,1)S(1)}, bf16[40,2944]{1,0:T(8,128)(2,1)S(1)}, u32[]{:S(2)}, u32[]{:S(2)}) collective-permute-start(bf16[40,2944]{1,0:T(8,128)(2,1)S(1)} %get-tuple-element.124), channel_id=1, source_target_pairs={{0,4},{4,8},{8,12},{12,14},{14,10},{10,6},{6,2},{2,0},{1,5},{5,9},... | collective-permute-start | bytes 706568 | tf_op jit(solution)/shard_map/ppermute | solution.py:371
  54.6 9.4 %collective-permute-start.20 = (bf16[40,2944]{1,0:T(8,128)(2,1)S(1)}, bf16[40,2944]{1,0:T(8,128)(2,1)S(1)}, u32[]{:S(2)}, u32[]{:S(2)}) collective-permute-start(bf16[40,2944]{1,0:T(8,128)(2,1)S(1)} %get-tuple-element.123), channel_id=1, source_target_pairs={{4,0},{8,4},{12,8},{14,12},{10,14},{6,10},{2,6},{0,2},{5,1},{9,5},... | collective-permute-start | bytes 706568 | tf_op jit(solution)/shard_map/ppermute | solution.py:374
  57.9 16.0 %collective-permute-start.11 = (bf16[80,2944]{1,0:T(8,128)(2,1)S(1)}, bf16[80,2944]{1,0:T(8,128)(2,1)S(1)}, u32[]{:S(2)}, u32[]{:S(2)}) collective-permute-start(bf16[80,2944]{1,0:T(8,128)(2,1)S(1)} %get-tuple-element.91), channel_id=1, source_target_pairs={{0,16},{16,0},{1,17},{17,1},{2,18},{18,2},{3,19},{19,3},{4,20},{20... | collective-permute-start | bytes 1413128 | tf_op jit(solution)/shard_map/ppermute | solution.py:346
  60.8 3.3 %copy-start.3 = (f32[1,640]{1,0:T(1,128)S(1)}, f32[1,640]{1,0:T(1,128)}, u32[]{:S(2)}) copy-start(f32[1,640]{1,0:T(1,128)} %bias.1) | copy-start | bytes 7684
  64.1 2.9 %collective-permute-start.21 = (f32[3,640]{1,0:T(4,128)S(1)}, f32[3,640]{1,0:T(4,128)S(1)}, u32[]{:S(2)}, u32[]{:S(2)}) collective-permute-start(f32[3,640]{1,0:T(4,128)S(1)} %fusion.2), channel_id=1, source_target_pairs={{0,1},{1,0},{2,3},{3,2},{4,5},{5,4},{6,7},{7,6},{8,9},{9,8},{10,11... | collective-permute-start | bytes 23048 | tf_op jit(solution)/shard_map/ppermute | solution.py:346
  64.2 9.7 %collective-permute-start.14 = (bf16[512,256]{1,0:T(8,128)(2,1)S(1)}, bf16[512,256]{1,0:T(8,128)(2,1)S(1)}, u32[]{:S(2)}, u32[]{:S(2)}) collective-permute-start(bf16[512,256]{1,0:T(8,128)(2,1)S(1)} %shard_map.124), channel_id=1, source_target_pairs={{0,1},{1,0},{2,3},{3,2},{4,5},{5,4},{6,7},{7,6},{8,9},{9,8},{10,11... | collective-permute-start | bytes 786440 | tf_op jit(solution)/shard_map/ppermute | solution.py:346
  64.9 7.8 %collective-permute-start.23 = (bf16[40,2944]{1,0:T(8,128)(2,1)S(1)}, bf16[40,2944]{1,0:T(8,128)(2,1)S(1)}, u32[]{:S(2)}, u32[]{:S(2)}) collective-permute-start(bf16[40,2944]{1,0:T(8,128)(2,1)S(1)} %get-tuple-element.126), channel_id=1, source_target_pairs={{0,4},{4,8},{8,12},{12,14},{14,10},{10,6},{6,2},{2,0},{1,5},{5,9},... | collective-permute-start | bytes 706568 | tf_op jit(solution)/shard_map/ppermute | solution.py:371
  66.4 7.4 %collective-permute-start.24 = (bf16[40,2944]{1,0:T(8,128)(2,1)S(1)}, bf16[40,2944]{1,0:T(8,128)(2,1)S(1)}, u32[]{:S(2)}, u32[]{:S(2)}) collective-permute-start(bf16[40,2944]{1,0:T(8,128)(2,1)S(1)} %get-tuple-element.125), channel_id=1, source_target_pairs={{4,0},{8,4},{12,8},{14,12},{10,14},{6,10},{2,6},{0,2},{5,1},{9,5},... | collective-permute-start | bytes 706568 | tf_op jit(solution)/shard_map/ppermute | solution.py:374
  67.0 3.7 %collective-permute-start.22 = (f32[3,640]{1,0:T(4,128)S(1)}, f32[3,640]{1,0:T(4,128)S(1)}, u32[]{:S(2)}, u32[]{:S(2)}) collective-permute-start(f32[3,640]{1,0:T(4,128)S(1)} %fusion.4), channel_id=1, source_target_pairs={{0,16},{16,0},{1,17},{17,1},{2,18},{18,2},{3,19},{19,3},{4,20},{20... | collective-permute-start | bytes 23048 | tf_op jit(solution)/shard_map/ppermute | solution.py:395
  70.7 5.4 %collective-permute-start.26 = (bf16[512,512]{1,0:T(8,128)(2,1)S(1)}, bf16[512,512]{1,0:T(8,128)(2,1)S(1)}, u32[]{:S(2)}, u32[]{:S(2)}) collective-permute-start(bf16[512,512]{1,0:T(8,128)(2,1)S(1)} %get-tuple-element.108), channel_id=1, source_target_pairs={{0,1},{1,0},{2,3},{3,2},{4,5},{5,4},{6,7},{7,6},{8,9},{9,8},{10,11... | collective-permute-start | bytes 1572872 | tf_op jit(solution)/shard_map/ppermute | solution.py:346
  73.9 5.9 %collective-permute-start.27 = (f32[3,640]{1,0:T(4,128)S(1)}, f32[3,640]{1,0:T(4,128)S(1)}, u32[]{:S(2)}, u32[]{:S(2)}) collective-permute-start(f32[3,640]{1,0:T(4,128)S(1)} %add.91), channel_id=1, source_target_pairs={{0,4},{4,0},{8,12},{12,8},{1,5},{5,1},{9,13},{13,9},{2,6},{6,2},{1... | collective-permute-start | bytes 23048 | tf_op jit(solution)/shard_map/ppermute | solution.py:395
  75.5 6.3 %collective-permute-start.25 = (bf16[40,2944]{1,0:T(8,128)(2,1)S(1)}, bf16[40,2944]{1,0:T(8,128)(2,1)S(1)}, u32[]{:S(2)}, u32[]{:S(2)}) collective-permute-start(bf16[40,2944]{1,0:T(8,128)(2,1)S(1)} %add_convert_fusion.1), channel_id=1, source_target_pairs={{0,4},{4,8},{8,12},{12,14},{14,10},{10,6},{6,2},{2,0},{1,5},{5,9},... | collective-permute-start | bytes 706568 | tf_op jit(solution)/shard_map/ppermute | solution.py:371
  82.0 9.3 %collective-permute-start.28 = (bf16[40,2944]{1,0:T(8,128)(2,1)S(1)}, bf16[40,2944]{1,0:T(8,128)(2,1)S(1)}, u32[]{:S(2)}, u32[]{:S(2)}) collective-permute-start(bf16[40,2944]{1,0:T(8,128)(2,1)S(1)} %add_convert_fusion), channel_id=1, source_target_pairs={{0,16},{16,0},{1,17},{17,1},{2,18},{18,2},{3,19},{19,3},{4,20},{20... | collective-permute-start | bytes 706568 | tf_op jit(solution)/shard_map/ppermute | solution.py:346
  83.0 3.7 %collective-permute-start.29 = (f32[3,640]{1,0:T(4,128)S(1)}, f32[3,640]{1,0:T(4,128)S(1)}, u32[]{:S(2)}, u32[]{:S(2)}) collective-permute-start(f32[3,640]{1,0:T(4,128)S(1)} %add.98), channel_id=1, source_target_pairs={{0,2},{2,0},{1,3},{3,1},{4,6},{6,4},{5,7},{7,5},{8,10},{10,8},{9,1... | collective-permute-start | bytes 23048 | tf_op jit(solution)/shard_map/ppermute | solution.py:395
  86.7 4.6 %collective-permute-start.30 = (f32[3,640]{1,0:T(4,128)S(1)}, f32[3,640]{1,0:T(4,128)S(1)}, u32[]{:S(2)}, u32[]{:S(2)}) collective-permute-start(f32[3,640]{1,0:T(4,128)S(1)} %add.102), channel_id=1, source_target_pairs={{0,8},{4,12},{8,0},{12,4},{1,9},{5,13},{9,1},{13,5},{2,10},{6,14},... | collective-permute-start | bytes 23048 | tf_op jit(solution)/shard_map/ppermute | solution.py:395
  91.3 1.6 %collective-permute-start.31 = (bf16[40,2944]{1,0:T(8,128)(2,1)S(1)}, bf16[40,2944]{1,0:T(8,128)(2,1)S(1)}, u32[]{:S(2)}, u32[]{:S(2)}) collective-permute-start(bf16[40,2944]{1,0:T(8,128)(2,1)S(1)} %get-tuple-element.133), channel_id=1, source_target_pairs={{0,1},{1,0},{2,3},{3,2},{4,5},{5,4},{6,7},{7,6},{8,9},{9,8},{10,11... | collective-permute-start | bytes 706568 | tf_op jit(solution)/shard_map/ppermute | solution.py:346

commit v16 on v15

--- a/solution.py
+++ b/solution.py
@@ -435,7 +435,7 @@
         table = jnp.asarray(ring.table(part))
         order = (ring.count, part, 2 * ring.count)
         up1, down1 = ring.up(unit), ring.down(unit)
-        peer = swap(mine, "replica")
+        peer = swap(tied(mine, unit)[0], "replica")
     else:
         table = jnp.zeros((replicas * zs * 4, 1), jnp.int32)
         order = None
@@ -566,15 +566,15 @@
         sums = back(1, cots, slopes, late)
         crossed[2], sums, *received = tied(crossed[2], sums, *received)
         received = ring_step(*ring_sums(zs - 2, *received))
-        vectors = hop(chip_sum(first_sums + sums), "replica", 1)
+        vectors = hop(hop(chip_sum(first_sums + sums), "replica", 1), "z", 1)
         crossed[3], conv_got, vectors, *received = tied(crossed[3], conv_got, vectors, *received)
         ahead, behind = ring_sums(zs - 1, *received)
         last = ring.up(ahead)
         block = conv_own(conv_got, [conv_first_own, conv_first_got, order], late)
-        vectors = hop(vectors, "z", 1)
+        block, vectors = tied(block, vectors)
+        vectors = hop(vectors, "y", 1)
         last, block, vectors = tied(last, block, vectors)
         total = add(*behind, last)
-        vectors = hop(vectors, "y", 1)
         reach = 2
         while reach < zs:
             vectors = hop(vectors, "z", reach)

time: 94.2 us -> 93.7 us (level)
  waiting for transfers between devices: 26.1 us -> 22 us
  starting transfers between devices: 30.9 us -> 34.5 us
    ppermute x8, waiting for transfers between devices: 11.7 us -> 4.8 us  [up(): return lax.ppermute(value, NODE, self.ahead)]
    ppermute x13, waiting for transfers between devices: 1.55 us -> 6.12 us  [swap(): return lax.ppermute(value, axis, [(0, 1), (1, 0)])]
    ppermute x7, waiting for transfers between devices: 4.07 us -> 1.72 us  [down(): return lax.ppermute(value, NODE, self.behind)]
    ppermute x7, starting transfers between devices: 3.15 us -> 5 us  [down(): return lax.ppermute(value, NODE, self.behind)]
    ppermute x4, starting transfers between devices: 4.7 us -> 6.32 us  [hop(): lax.ppermute(value, axis, [(s, s ^ mask) for s in range(count)])]
  transfers between devices with their start and end apart: 32 -> 32, of which waited for: 13 -> 14; matrix products, arithmetic and copies ran while one was open for 1% -> 1% of each run, Pallas kernels for 33% -> 33%
where the time goes in v16:
time: 93.7 us; the launch traced here: 93.5 us
  starting transfers between devices  34.5 us (37%)
  Pallas kernels  32.4 us (35%)
  waiting for transfers between devices  22 us (23%)
  other arithmetic  2.91 us (3%)
  between operations  1.58 us (2%)
    ppermute x8, starting transfers between devices, up(): return lax.ppermute(value, NODE, self.ahead)  13.1 us
    ppermute x13, starting transfers between devices, swap(): return lax.ppermute(value, axis, [(0, 1), (1, 0)])  10.1 us
    ppermute x4, waiting for transfers between devices, hop(): lax.ppermute(value, axis, [(s, s ^ mask) for s in range(count)])  9.34 us
    pallas_call x2, Pallas kernels, back(): call(partial(back_kernel, cols, stages, stage), jax.ShapeDtypeStruct((2,...  8.61 us
    ppermute x4, starting transfers between devices, hop(): lax.ppermute(value, axis, [(s, s ^ mask) for s in range(count)])  6.32 us
    ppermute x13, waiting for transfers between devices, swap(): return lax.ppermute(value, axis, [(0, 1), (1, 0)])  6.12 us
    ppermute x7, starting transfers between devices, down(): return lax.ppermute(value, NODE, self.behind)  5 us
    ppermute x8, waiting for transfers between devices, up(): return lax.ppermute(value, NODE, self.ahead)  4.8 us
  transfers between devices with their start and end apart: 32, of which 14 were waited for; matrix products, arithmetic and copies ran while one was open for 1% of the time, Pallas kernels for 33%

profile of v16, /device:TPU:0, one launch (start us, length us, event | category | flops | bytes accessed | tf_op | source)
XLA Modules:
  0.0 93.5 jit_solution(14541919211941158762)
XLA Ops:
  0.7 2.0 %fusion.3 = (f32[640]{0:T(1024)S(1)}, bf16[16,32,640]{2,1,0:T(8,128)(2,1)S(1)}) fusion(f32[1,16,32,640]{3,2,1,0:T(8,128)} %param.9), kind=kLoop, calls=%fused_computation.19 | loop fusion | flops 654720 | bytes 1968640 | tf_op jit(solution)/shard_map/reduce_sum | solution.py:521
  2.7 0.5 collective-permute-start.3
  3.4 0.5 collective-permute-start
  3.8 2.3 %collective-permute-done = bf16[40,2944]{1,0:T(8,128)(2,1)S(1)} collective-permute-done((bf16[40,2944]{1,0:T(8,128)(2,1)S(1)}, bf16[40,2944]{1,0:T(8,128)(2,1)S(1)}, u32[]{:S(2)}, u32[]{:S(2)}) %collective-permute-start) | collective-permute-done | bytes 235552 | tf_op jit(solution)/shard_map/ppermute | solution.py:346
  6.3 3.0 %collective-permute-start.4 = (bf16[80,2944]{1,0:T(8,128)(2,1)S(1)}, bf16[80,2944]{1,0:T(8,128)(2,1)S(1)}, u32[]{:S(2)}, u32[]{:S(2)}) collective-permute-start(bf16[80,2944]{1,0:T(8,128)(2,1)S(1)} %maximum_select_fusion.refs_0_), channel_id=1, source_target_pairs={{0,4},{4,8},{8,12},{12,14},{14,10},{10,6},{6,2},{2,0},{1,5},{5,9},... | collective-permute-start | bytes 1413128 | tf_op jit(solution)/shard_map/ppermute | solution.py:371
  9.3 1.9 %collective-permute-start.1 = (bf16[40,2944]{1,0:T(8,128)(2,1)S(1)}, bf16[40,2944]{1,0:T(8,128)(2,1)S(1)}, u32[]{:S(2)}, u32[]{:S(2)}) collective-permute-start(bf16[40,2944]{1,0:T(8,128)(2,1)S(1)} %get-tuple-element.70), channel_id=1, source_target_pairs={{0,16},{16,0},{1,17},{17,1},{2,18},{18,2},{3,19},{19,3},{4,20},{20... | collective-permute-start | bytes 706568 | tf_op jit(solution)/shard_map/ppermute | solution.py:346
  11.3 4.4 %shard_map.119 = (f32[2,640]{1,0:T(2,128)S(1)}, bf16[3,34,32,640]{3,2,1,0:T(8,128)(2,1)S(1)}, bf16[640,1024]{1,0:T(8,128)(2,1)S(1)}) custom-call(s32[1]{0:T(128)} %bitcast.dev, s32[32,24]{1,0:T(8,128)S(1)} %copy-done.5, bf16[16,32,640]{2,1,0:T(8,128)(2,1)S(1)} %bitcast.13, bf16[16,32,640]{2,1,0:T(8,128)(2,1)S(1)} %collective-permute-done.2.lat_far, ...), custom_call_target="tpu_custom_call" | custom-call | flops 3858759680 | tf_op jit(solution)/shard_map/pallas_call | solution.py:457
  15.6 1.1 %collective-permute-done.1.mine = bf16[40,2944]{1,0:T(8,128)(2,1)S(1)} collective-permute-done((bf16[40,2944]{1,0:T(8,128)(2,1)S(1)}, bf16[40,2944]{1,0:T(8,128)(2,1)S(1)}, u32[]{:S(2)}, u32[]{:S(2)}) %collective-permute-start.1) | collective-permute-done | bytes 235552 | tf_op jit(solution)/shard_map/ppermute | solution.py:346
  16.8 4.6 %shard_map.120 = (bf16[320,2944]{1,0:T(8,128)(2,1)S(1)}, bf16[80,2944]{1,0:T(8,128)(2,1)S(1)}, bf16[120,2944]{1,0:T(8,128)(2,1)S(1)}, bf16[80,2944]{1,0:T(8,128)(2,1)S(1)}, bf16[80,2944]{1,0:T(8,128)(2,1)S(1)}) custom-call(s32[1]{0:T(128)} %bitcast.dev, bf16[3,34,32,640]{3,2,1,0:T(8,128)(2,1)S(1)} %get-tuple-element.72.acts, ...), custom_call_target="tpu_custom_call" | custom-call | flops 7717519360 | tf_op jit(solution)/shard_map/pallas_call | solution.py:467
  21.8 1.6 %collective-permute-start.6 = (bf16[80,2944]{1,0:T(8,128)(2,1)S(1)}, bf16[80,2944]{1,0:T(8,128)(2,1)S(1)}, u32[]{:S(2)}, u32[]{:S(2)}) collective-permute-start(bf16[80,2944]{1,0:T(8,128)(2,1)S(1)} %collective-permute-done.4.refs_1_), channel_id=1, source_target_pairs={{0,4},{4,8},{8,12},{12,14},{14,10},{10,6},{6,2},{2,0},{1,5},{5,9},... | collective-permute-start | bytes 1413128 | tf_op jit(solution)/shard_map/ppermute | solution.py:371
  23.4 0.4 collective-permute-start.7
  23.9 1.5 %collective-permute-start.10 = (bf16[80,2944]{1,0:T(8,128)(2,1)S(1)}, bf16[80,2944]{1,0:T(8,128)(2,1)S(1)}, u32[]{:S(2)}, u32[]{:S(2)}) collective-permute-start(bf16[80,2944]{1,0:T(8,128)(2,1)S(1)} %get-tuple-element.76), channel_id=1, source_target_pairs={{0,16},{16,0},{1,17},{17,1},{2,18},{18,2},{3,19},{19,3},{4,20},{20... | collective-permute-start | bytes 1413128 | tf_op jit(solution)/shard_map/ppermute | solution.py:346
  25.3 0.5 collective-permute-start.16
  25.9 4.5 %shard_map.121 = (bf16[3,34,32,768]{3,2,1,0:T(8,128)(2,1)S(1)}, bf16[32,32,640]{2,1,0:T(8,128)(2,1)S(1)}, bf16[32,32,640]{2,1,0:T(8,128)(2,1)S(1)}, bf16[640,768]{1,0:T(8,128)(2,1)S(1)}) custom-call(s32[1]{0:T(128)} %bitcast.dev, s32[32,24]{1,0:T(8,128)S(1)} %copy-done.5, f32[2,640]{1,0:T(2,128)S(1)} %get-tuple-element.81.stats, f32[1,640]{1,0:T(1,128)S(1)} %copy-done.1, ...), custom_call_target="tpu_custom_call" | custom-call | flops 3858759680 | tf_op jit(solution)/shard_map/pallas_call | solution.py:479
  30.4 3.1 %collective-permute-done.6.refs_3_ = bf16[80,2944]{1,0:T(8,128)(2,1)S(1)} collective-permute-done((bf16[80,2944]{1,0:T(8,128)(2,1)S(1)}, bf16[80,2944]{1,0:T(8,128)(2,1)S(1)}, u32[]{:S(2)}, u32[]{:S(2)}) %collective-permute-start.6) | collective-permute-done | bytes 471072 | tf_op jit(solution)/shard_map/ppermute | solution.py:371
  33.5 1.3 %collective-permute-done.7.refs_4_ = bf16[80,2944]{1,0:T(8,128)(2,1)S(1)} collective-permute-done((bf16[80,2944]{1,0:T(8,128)(2,1)S(1)}, bf16[80,2944]{1,0:T(8,128)(2,1)S(1)}, u32[]{:S(2)}, u32[]{:S(2)}) %collective-permute-start.7) | collective-permute-done | bytes 471072 | tf_op jit(solution)/shard_map/ppermute | solution.py:374
  34.8 1.6 %collective-permute-start.8 = (bf16[80,2944]{1,0:T(8,128)(2,1)S(1)}, bf16[80,2944]{1,0:T(8,128)(2,1)S(1)}, u32[]{:S(2)}, u32[]{:S(2)}) collective-permute-start(bf16[80,2944]{1,0:T(8,128)(2,1)S(1)} %collective-permute-done.6.refs_3_), channel_id=1, source_target_pairs={{0,4},{4,8},{8,12},{12,14},{14,10},{10,6},{6,2},{2,0},{1,5},{5,9},... | collective-permute-start | bytes 1413128 | tf_op jit(solution)/shard_map/ppermute | solution.py:371
  36.4 0.4 collective-permute-start.9
  36.8 4.0 %shard_map.122 = (f32[512,512]{1,0:T(8,128)S(1)}, bf16[512,512]{1,0:T(8,128)(2,1)S(1)}) custom-call(s32[1]{0:T(128)} %bitcast.dev, bf16[3,34,32,640]{3,2,1,0:T(8,128)(2,1)S(1)} %get-tuple-element.72.acts, bf16[80,2944]{1,0:T(8,128)(2,1)S(1)} %maximum_select_fusion.refs_0_, bf16[80,2944]{1,0:T(8,128)(2,1)S(1)} %collective-permute-done.4.refs_1_, ...), custom_call_target="tpu_custom_call" | custom-call | flops 3858759680 | tf_op jit(solution)/shard_map/pallas_call | solution.py:497
  40.9 1.6 %collective-permute-start.17 = (bf16[40,2944]{1,0:T(8,128)(2,1)S(1)}, bf16[40,2944]{1,0:T(8,128)(2,1)S(1)}, u32[]{:S(2)}, u32[]{:S(2)}) collective-permute-start(bf16[40,2944]{1,0:T(8,128)(2,1)S(1)} %get-tuple-element.134), channel_id=1, source_target_pairs={{0,4},{4,8},{8,12},{12,14},{14,10},{10,6},{6,2},{2,0},{1,5},{5,9},... | collective-permute-start | bytes 706568 | tf_op jit(solution)/shard_map/ppermute | solution.py:371
  43.0 5.4 %shard_map.123 = f32[2,640]{1,0:T(2,128)S(1)} custom-call(s32[1]{0:T(128)} %bitcast.dev, bf16[3,34,32,768]{3,2,1,0:T(8,128)(2,1)S(1)} %get-tuple-element.101.cots, bf16[32,32,640]{2,1,0:T(8,128)(2,1)S(1)} %get-tuple-element.92.slope, bf16[32,32,640]{2,1,0:T(8,128)(2,1)S(1)} %get-tuple-element.93.slope_x, bf16[80,2944]{1,0:T(8,128)(2,1)S(1)} %maximum_select_fusion.refs_0_, ...), custom_call_target="tpu_custom_call" | custom-call | flops 3858759680 | tf_op jit(solution)/shard_map/pallas_call | solution.py:489
  48.4 1.6 %collective-permute-start.15 = (bf16[80,2944]{1,0:T(8,128)(2,1)S(1)}, bf16[80,2944]{1,0:T(8,128)(2,1)S(1)}, u32[]{:S(2)}, u32[]{:S(2)}) collective-permute-start(bf16[80,2944]{1,0:T(8,128)(2,1)S(1)} %get-tuple-element.100), channel_id=1, source_target_pairs={{0,16},{16,0},{1,17},{17,1},{2,18},{18,2},{3,19},{19,3},{4,20},{20... | collective-permute-start | bytes 1413128 | tf_op jit(solution)/shard_map/ppermute | solution.py:346
  50.0 1.6 %collective-permute-start.12 = (bf16[40,2944]{1,0:T(8,128)(2,1)S(1)}, bf16[40,2944]{1,0:T(8,128)(2,1)S(1)}, u32[]{:S(2)}, u32[]{:S(2)}) collective-permute-start(bf16[40,2944]{1,0:T(8,128)(2,1)S(1)} %slice.67), channel_id=1, source_target_pairs={{0,4},{4,8},{8,12},{12,14},{14,10},{10,6},{6,2},{2,0},{1,5},{5,9},... | collective-permute-start | bytes 706568 | tf_op jit(solution)/shard_map/ppermute | solution.py:371
  51.7 0.7 collective-permute-done.16.carried
  52.4 1.6 %collective-permute-start.13 = (bf16[40,2944]{1,0:T(8,128)(2,1)S(1)}, bf16[40,2944]{1,0:T(8,128)(2,1)S(1)}, u32[]{:S(2)}, u32[]{:S(2)}) collective-permute-start(bf16[40,2944]{1,0:T(8,128)(2,1)S(1)} %slice.68), channel_id=1, source_target_pairs={{4,0},{8,4},{12,8},{14,12},{10,14},{6,10},{2,6},{0,2},{5,1},{9,5},... | collective-permute-start | bytes 706568 | tf_op jit(solution)/shard_map/ppermute | solution.py:374
  54.1 0.5 collective-permute-start.18
  54.6 1.6 %collective-permute-start.20 = (bf16[40,2944]{1,0:T(8,128)(2,1)S(1)}, bf16[40,2944]{1,0:T(8,128)(2,1)S(1)}, u32[]{:S(2)}, u32[]{:S(2)}) collective-permute-start(bf16[40,2944]{1,0:T(8,128)(2,1)S(1)} %get-tuple-element.129), channel_id=1, source_target_pairs={{4,0},{8,4},{12,8},{14,12},{10,14},{6,10},{2,6},{0,2},{5,1},{9,5},... | collective-permute-start | bytes 706568 | tf_op jit(solution)/shard_map/ppermute | solution.py:374
  56.2 1.7 %collective-permute-done.12.refs_2_.refs_5_ = bf16[40,2944]{1,0:T(8,128)(2,1)S(1)} collective-permute-done((bf16[40,2944]{1,0:T(8,128)(2,1)S(1)}, bf16[40,2944]{1,0:T(8,128)(2,1)S(1)}, u32[]{:S(2)}, u32[]{:S(2)}) %collective-permute-start.12) | collective-permute-done | bytes 235552 | tf_op jit(solution)/shard_map/ppermute | solution.py:371
  57.9 1.4 %collective-permute-start.11 = (bf16[80,2944]{1,0:T(8,128)(2,1)S(1)}, bf16[80,2944]{1,0:T(8,128)(2,1)S(1)}, u32[]{:S(2)}, u32[]{:S(2)}) collective-permute-start(bf16[80,2944]{1,0:T(8,128)(2,1)S(1)} %get-tuple-element.95), channel_id=1, source_target_pairs={{0,16},{16,0},{1,17},{17,1},{2,18},{18,2},{3,19},{19,3},{4,20},{20... | collective-permute-start | bytes 1413128 | tf_op jit(solution)/shard_map/ppermute | solution.py:346
  59.3 1.4 %shard_map.124 = bf16[512,256]{1,0:T(8,128)(2,1)S(1)} custom-call(s32[1]{0:T(128)} %bitcast.dev, bf16[3,34,32,640]{3,2,1,0:T(8,128)(2,1)S(1)} %get-tuple-element.72.acts, bf16[80,2944]{1,0:T(8,128)(2,1)S(1)} %collective-permute-done.8.refs_0_.refs_3_, bf16[80,2944]{1,0:T(8,128)(2,1)S(1)} %collective-permute-done.9.refs_1_.refs_4_, ...), custom_call_target="tpu_custom_call" | custom-call | flops 1929379840 | tf_op jit(solution)/shard_map/pallas_call | solution.py:506
  60.8 3.2 %shard_map.125 = f32[2,640]{1,0:T(2,128)S(1)} custom-call(s32[1]{0:T(128)} %bitcast.dev, bf16[3,34,32,768]{3,2,1,0:T(8,128)(2,1)S(1)} %get-tuple-element.101.cots, bf16[32,32,640]{2,1,0:T(8,128)(2,1)S(1)} %get-tuple-element.92.slope, bf16[32,32,640]{2,1,0:T(8,128)(2,1)S(1)} %get-tuple-element.93.slope_x, ...), custom_call_target="tpu_custom_call" | custom-call | flops 3858759680 | tf_op jit(solution)/shard_map/pallas_call | solution.py:489
  64.2 0.5 collective-permute-start.14
  64.9 1.6 %collective-permute-start.24 = (bf16[40,2944]{1,0:T(8,128)(2,1)S(1)}, bf16[40,2944]{1,0:T(8,128)(2,1)S(1)}, u32[]{:S(2)}, u32[]{:S(2)}) collective-permute-start(bf16[40,2944]{1,0:T(8,128)(2,1)S(1)} %get-tuple-element.132), channel_id=1, source_target_pairs={{0,4},{4,8},{8,12},{12,14},{14,10},{10,6},{6,2},{2,0},{1,5},{5,9},... | collective-permute-start | bytes 706568 | tf_op jit(solution)/shard_map/ppermute | solution.py:371
  66.4 0.5 collective-permute-start.25
  67.0 1.4 %collective-permute-start.22 = (f32[3,640]{1,0:T(4,128)S(1)}, f32[3,640]{1,0:T(4,128)S(1)}, u32[]{:S(2)}, u32[]{:S(2)}) collective-permute-start(f32[3,640]{1,0:T(4,128)S(1)} %fusion.4), channel_id=1, source_target_pairs={{0,16},{16,0},{1,17},{17,1},{2,18},{18,2},{3,19},{19,3},{4,20},{20... | collective-permute-start | bytes 23048 | tf_op jit(solution)/shard_map/ppermute | solution.py:395
  68.4 2.3 %collective-permute-done.22 = f32[3,640]{1,0:T(4,128)S(1)} collective-permute-done((f32[3,640]{1,0:T(4,128)S(1)}, f32[3,640]{1,0:T(4,128)S(1)}, u32[]{:S(2)}, u32[]{:S(2)}) %collective-permute-start.22) | collective-permute-done | bytes 7712 | tf_op jit(solution)/shard_map/ppermute | solution.py:395
  70.7 1.5 %collective-permute-start.23 = (f32[3,640]{1,0:T(4,128)S(1)}, f32[3,640]{1,0:T(4,128)S(1)}, u32[]{:S(2)}, u32[]{:S(2)}) collective-permute-start(f32[3,640]{1,0:T(4,128)S(1)} %add.91), channel_id=1, source_target_pairs={{0,4},{4,0},{8,12},{12,8},{1,5},{5,1},{9,13},{13,9},{2,6},{6,2},{1... | collective-permute-start | bytes 23048 | tf_op jit(solution)/shard_map/ppermute | solution.py:395
  72.2 2.1 %collective-permute-done.23 = f32[3,640]{1,0:T(4,128)S(1)} collective-permute-done((f32[3,640]{1,0:T(4,128)S(1)}, f32[3,640]{1,0:T(4,128)S(1)}, u32[]{:S(2)}, u32[]{:S(2)}) %collective-permute-start.23) | collective-permute-done | bytes 7712 | tf_op jit(solution)/shard_map/ppermute | solution.py:395
  74.5 1.6 %collective-permute-start.26 = (bf16[40,2944]{1,0:T(8,128)(2,1)S(1)}, bf16[40,2944]{1,0:T(8,128)(2,1)S(1)}, u32[]{:S(2)}, u32[]{:S(2)}) collective-permute-start(bf16[40,2944]{1,0:T(8,128)(2,1)S(1)} %add_convert_fusion.1), channel_id=1, source_target_pairs={{0,4},{4,8},{8,12},{12,14},{14,10},{10,6},{6,2},{2,0},{1,5},{5,9},... | collective-permute-start | bytes 706568 | tf_op jit(solution)/shard_map/ppermute | solution.py:371
  76.3 3.7 %shard_map.126 = bf16[16,32,640]{2,1,0:T(8,128)(2,1)} custom-call(s32[1]{0:T(128)} %bitcast.dev, bf16[3,34,32,640]{3,2,1,0:T(8,128)(2,1)S(1)} %get-tuple-element.72.acts, bf16[512,256]{1,0:T(8,128)(2,1)S(1)} %collective-permute-done.14.got, bf16[16,32,640]{2,1,0:T(8,128)(2,1)S(1)} %bitcast.15, f32[1,640]{1,0:T(1,128)S(1)} %copy-done.3, ...), custom_call_target="tpu_custom_call" | custom-call | flops 3858759680 | tf_op jit(solution)/shard_map/pallas_call | solution.py:514
  80.0 0.8 collective-permute-start.28
  80.8 2.8 %collective-permute-done.28 = f32[3,640]{1,0:T(4,128)S(1)} collective-permute-done((f32[3,640]{1,0:T(4,128)S(1)}, f32[3,640]{1,0:T(4,128)S(1)}, u32[]{:S(2)}, u32[]{:S(2)}) %collective-permute-start.28) | collective-permute-done | bytes 7712 | tf_op jit(solution)/shard_map/ppermute | solution.py:395
  83.8 1.4 %collective-permute-start.29 = (bf16[40,2944]{1,0:T(8,128)(2,1)S(1)}, bf16[40,2944]{1,0:T(8,128)(2,1)S(1)}, u32[]{:S(2)}, u32[]{:S(2)}) collective-permute-start(bf16[40,2944]{1,0:T(8,128)(2,1)S(1)} %add_convert_fusion), channel_id=1, source_target_pairs={{0,16},{16,0},{1,17},{17,1},{2,18},{18,2},{3,19},{19,3},{4,20},{20... | collective-permute-start | bytes 706568 | tf_op jit(solution)/shard_map/ppermute | solution.py:346
  85.2 2.5 %collective-permute-start.30 = (f32[3,640]{1,0:T(4,128)S(1)}, f32[3,640]{1,0:T(4,128)S(1)}, u32[]{:S(2)}, u32[]{:S(2)}) collective-permute-start(f32[3,640]{1,0:T(4,128)S(1)} %add.99), channel_id=1, source_target_pairs={{0,8},{4,12},{8,0},{12,4},{1,9},{5,13},{9,1},{13,5},{2,10},{6,14},... | collective-permute-start | bytes 23048 | tf_op jit(solution)/shard_map/ppermute | solution.py:395
  87.8 2.0 %collective-permute-done.30 = f32[3,640]{1,0:T(4,128)S(1)} collective-permute-done((f32[3,640]{1,0:T(4,128)S(1)}, f32[3,640]{1,0:T(4,128)S(1)}, u32[]{:S(2)}, u32[]{:S(2)}) %collective-permute-start.30) | collective-permute-done | bytes 7712 | tf_op jit(solution)/shard_map/ppermute | solution.py:395
  89.8 0.9 collective-permute-done.29
  91.4 0.8 collective-permute-done.31.aside
  92.3 1.2 %shard_map.127 = (f32[40,5760]{1,0:T(8,128)}, f32[1,640]{1,0:T(1,128)}, f32[1,640]{1,0:T(1,128)}, f32[1,640]{1,0:T(1,128)}) custom-call(s32[1]{0:T(128)} %bitcast.dev, s32[1]{0:T(128)S(6)} %copy.13.step, f32[40,5760]{1,0:T(8,128)S(1)} %bitcast.11, bf16[40,2944]{1,0:T(8,128)(2,1)S(1)} %collective-permute-done.1.mine, ...), custom_call_target="tpu_custom_call" | custom-call | flops 964689920 | tf_op jit(solution)/shard_map/pallas_call | solution.py:586
  (56 shorter events, 2.4 us)
Async XLA Ops:
  0.6 2.6 %copy-start.4 = (bf16[1,16,32,640]{3,2,1,0:T(8,128)(2,1)S(1)}, bf16[1,16,32,640]{3,2,1,0:T(8,128)(2,1)}, u32[]{:S(2)}) copy-start(bf16[1,16,32,640]{3,2,1,0:T(8,128)(2,1)} %param.8) | copy-start | bytes 1966084
  0.6 2.6 %copy-start = (f32[1,40,5760]{2,1,0:T(8,128)S(1)}, f32[1,40,5760]{2,1,0:T(8,128)}, u32[]{:S(2)}) copy-start(f32[1,40,5760]{2,1,0:T(8,128)} %param.10) | copy-start | bytes 2764804
  0.7 10.6 %copy-start.1 = (f32[1,640]{1,0:T(1,128)S(1)}, f32[1,640]{1,0:T(1,128)}, u32[]{:S(2)}) copy-start(f32[1,640]{1,0:T(1,128)} %gain.3) | copy-start | bytes 7684
  0.7 10.6 %copy-start.2 = (f32[1,640]{1,0:T(1,128)S(1)}, f32[1,640]{1,0:T(1,128)}, u32[]{:S(2)}) copy-start(f32[1,640]{1,0:T(1,128)} %shift.3) | copy-start | bytes 7684
  2.7 8.5 %collective-permute-start.3 = (bf16[16,32,640]{2,1,0:T(8,128)(2,1)S(1)}, bf16[16,32,640]{2,1,0:T(8,128)(2,1)S(1)}, u32[]{:S(2)}, u32[]{:S(2)}) collective-permute-start(bf16[16,32,640]{2,1,0:T(8,128)(2,1)S(1)} %get-tuple-element.136.cot_own), channel_id=1, source_target_pairs={{0,1},{1,0},{2,3},{3,2},{4,5},{5,4},{6,7},{7,6},{8,9},{9,8},{10,11... | collective-permute-start | bytes 1966088 | tf_op jit(solution)/shard_map/ppermute | solution.py:346
  3.2 8.0 %collective-permute-start.2 = (bf16[16,32,640]{2,1,0:T(8,128)(2,1)S(1)}, bf16[16,32,640]{2,1,0:T(8,128)(2,1)S(1)}, u32[]{:S(2)}, u32[]{:S(2)}) collective-permute-start(bf16[16,32,640]{2,1,0:T(8,128)(2,1)S(1)} %bitcast.12), channel_id=1, source_target_pairs={{0,1},{1,0},{2,3},{3,2},{4,5},{5,4},{6,7},{7,6},{8,9},{9,8},{10,11... | collective-permute-start | bytes 1966088 | tf_op jit(solution)/shard_map/ppermute | solution.py:346
  3.3 8.0 %copy-start.5 = (s32[32,24]{1,0:T(8,128)S(1)}, s32[32,24]{1,0:T(8,128)}, u32[]{:S(2)}) copy-start(s32[32,24]{1,0:T(8,128)} %constant.38.clone.table) | copy-start | bytes 9220
  3.4 2.8 %collective-permute-start = (bf16[40,2944]{1,0:T(8,128)(2,1)S(1)}, bf16[40,2944]{1,0:T(8,128)(2,1)S(1)}, u32[]{:S(2)}, u32[]{:S(2)}) collective-permute-start(bf16[40,2944]{1,0:T(8,128)(2,1)S(1)} %get-tuple-element.138.theirs), channel_id=1, source_target_pairs={{0,1},{1,0},{2,3},{3,2},{4,5},{5,4},{6,7},{7,6},{8,9},{9,8},{10,11... | collective-permute-start | bytes 706568 | tf_op jit(solution)/shard_map/ppermute | solution.py:346
  6.3 15.1 %collective-permute-start.4 = (bf16[80,2944]{1,0:T(8,128)(2,1)S(1)}, bf16[80,2944]{1,0:T(8,128)(2,1)S(1)}, u32[]{:S(2)}, u32[]{:S(2)}) collective-permute-start(bf16[80,2944]{1,0:T(8,128)(2,1)S(1)} %maximum_select_fusion.refs_0_), channel_id=1, source_target_pairs={{0,4},{4,8},{8,12},{12,14},{14,10},{10,6},{6,2},{2,0},{1,5},{5,9},... | collective-permute-start | bytes 1413128 | tf_op jit(solution)/shard_map/ppermute | solution.py:371
  9.3 12.5 %collective-permute-start.5 = (bf16[80,2944]{1,0:T(8,128)(2,1)S(1)}, bf16[80,2944]{1,0:T(8,128)(2,1)S(1)}, u32[]{:S(2)}, u32[]{:S(2)}) collective-permute-start(bf16[80,2944]{1,0:T(8,128)(2,1)S(1)} %maximum_select_fusion.refs_0_), channel_id=1, source_target_pairs={{4,0},{8,4},{12,8},{14,12},{10,14},{6,10},{2,6},{0,2},{5,1},{9,5},... | collective-permute-start | bytes 1413128 | tf_op jit(solution)/shard_map/ppermute | solution.py:374
  9.3 7.5 %collective-permute-start.1 = (bf16[40,2944]{1,0:T(8,128)(2,1)S(1)}, bf16[40,2944]{1,0:T(8,128)(2,1)S(1)}, u32[]{:S(2)}, u32[]{:S(2)}) collective-permute-start(bf16[40,2944]{1,0:T(8,128)(2,1)S(1)} %get-tuple-element.70), channel_id=1, source_target_pairs={{0,16},{16,0},{1,17},{17,1},{2,18},{18,2},{3,19},{19,3},{4,20},{20... | collective-permute-start | bytes 706568 | tf_op jit(solution)/shard_map/ppermute | solution.py:346
  21.8 11.7 %collective-permute-start.6 = (bf16[80,2944]{1,0:T(8,128)(2,1)S(1)}, bf16[80,2944]{1,0:T(8,128)(2,1)S(1)}, u32[]{:S(2)}, u32[]{:S(2)}) collective-permute-start(bf16[80,2944]{1,0:T(8,128)(2,1)S(1)} %collective-permute-done.4.refs_1_), channel_id=1, source_target_pairs={{0,4},{4,8},{8,12},{12,14},{14,10},{10,6},{6,2},{2,0},{1,5},{5,9},... | collective-permute-start | bytes 1413128 | tf_op jit(solution)/shard_map/ppermute | solution.py:371
  23.4 11.4 %collective-permute-start.7 = (bf16[80,2944]{1,0:T(8,128)(2,1)S(1)}, bf16[80,2944]{1,0:T(8,128)(2,1)S(1)}, u32[]{:S(2)}, u32[]{:S(2)}) collective-permute-start(bf16[80,2944]{1,0:T(8,128)(2,1)S(1)} %collective-permute-done.5.refs_2_), channel_id=1, source_target_pairs={{4,0},{8,4},{12,8},{14,12},{10,14},{6,10},{2,6},{0,2},{5,1},{9,5},... | collective-permute-start | bytes 1413128 | tf_op jit(solution)/shard_map/ppermute | solution.py:374
  23.9 17.0 %collective-permute-start.10 = (bf16[80,2944]{1,0:T(8,128)(2,1)S(1)}, bf16[80,2944]{1,0:T(8,128)(2,1)S(1)}, u32[]{:S(2)}, u32[]{:S(2)}) collective-permute-start(bf16[80,2944]{1,0:T(8,128)(2,1)S(1)} %get-tuple-element.76), channel_id=1, source_target_pairs={{0,16},{16,0},{1,17},{17,1},{2,18},{18,2},{3,19},{19,3},{4,20},{20... | collective-permute-start | bytes 1413128 | tf_op jit(solution)/shard_map/ppermute | solution.py:346
  25.3 27.0 %collective-permute-start.16 = (bf16[120,2944]{1,0:T(8,128)(2,1)S(1)}, bf16[120,2944]{1,0:T(8,128)(2,1)S(1)}, u32[]{:S(2)}, u32[]{:S(2)}) collective-permute-start(bf16[120,2944]{1,0:T(8,128)(2,1)S(1)} %get-tuple-element.102), channel_id=1, source_target_pairs={{0,16},{16,0},{1,17},{17,1},{2,18},{18,2},{3,19},{19,3},{4,20},{20... | collective-permute-start | bytes 2119688 | tf_op jit(solution)/shard_map/ppermute | solution.py:346
  34.8 13.6 %collective-permute-start.8 = (bf16[80,2944]{1,0:T(8,128)(2,1)S(1)}, bf16[80,2944]{1,0:T(8,128)(2,1)S(1)}, u32[]{:S(2)}, u32[]{:S(2)}) collective-permute-start(bf16[80,2944]{1,0:T(8,128)(2,1)S(1)} %collective-permute-done.6.refs_3_), channel_id=1, source_target_pairs={{0,4},{4,8},{8,12},{12,14},{14,10},{10,6},{6,2},{2,0},{1,5},{5,9},... | collective-permute-start | bytes 1413128 | tf_op jit(solution)/shard_map/ppermute | solution.py:371
  36.4 13.6 %collective-permute-start.9 = (bf16[80,2944]{1,0:T(8,128)(2,1)S(1)}, bf16[80,2944]{1,0:T(8,128)(2,1)S(1)}, u32[]{:S(2)}, u32[]{:S(2)}) collective-permute-start(bf16[80,2944]{1,0:T(8,128)(2,1)S(1)} %collective-permute-done.7.refs_4_), channel_id=1, source_target_pairs={{4,0},{8,4},{12,8},{14,12},{10,14},{6,10},{2,6},{0,2},{5,1},{9,5},... | collective-permute-start | bytes 1413128 | tf_op jit(solution)/shard_map/ppermute | solution.py:374
  40.9 13.0 %collective-permute-start.17 = (bf16[40,2944]{1,0:T(8,128)(2,1)S(1)}, bf16[40,2944]{1,0:T(8,128)(2,1)S(1)}, u32[]{:S(2)}, u32[]{:S(2)}) collective-permute-start(bf16[40,2944]{1,0:T(8,128)(2,1)S(1)} %get-tuple-element.134), channel_id=1, source_target_pairs={{0,4},{4,8},{8,12},{12,14},{14,10},{10,6},{6,2},{2,0},{1,5},{5,9},... | collective-permute-start | bytes 706568 | tf_op jit(solution)/shard_map/ppermute | solution.py:371
  42.6 11.4 %collective-permute-start.19 = (bf16[40,2944]{1,0:T(8,128)(2,1)S(1)}, bf16[40,2944]{1,0:T(8,128)(2,1)S(1)}, u32[]{:S(2)}, u32[]{:S(2)}) collective-permute-start(bf16[40,2944]{1,0:T(8,128)(2,1)S(1)} %get-tuple-element.133), channel_id=1, source_target_pairs={{4,0},{8,4},{12,8},{14,12},{10,14},{6,10},{2,6},{0,2},{5,1},{9,5},... | collective-permute-start | bytes 706568 | tf_op jit(solution)/shard_map/ppermute | solution.py:374
  48.4 15.6 %collective-permute-start.15 = (bf16[80,2944]{1,0:T(8,128)(2,1)S(1)}, bf16[80,2944]{1,0:T(8,128)(2,1)S(1)}, u32[]{:S(2)}, u32[]{:S(2)}) collective-permute-start(bf16[80,2944]{1,0:T(8,128)(2,1)S(1)} %get-tuple-element.100), channel_id=1, source_target_pairs={{0,16},{16,0},{1,17},{17,1},{2,18},{18,2},{3,19},{19,3},{4,20},{20... | collective-permute-start | bytes 1413128 | tf_op jit(solution)/shard_map/ppermute | solution.py:346
  50.0 7.9 %collective-permute-start.12 = (bf16[40,2944]{1,0:T(8,128)(2,1)S(1)}, bf16[40,2944]{1,0:T(8,128)(2,1)S(1)}, u32[]{:S(2)}, u32[]{:S(2)}) collective-permute-start(bf16[40,2944]{1,0:T(8,128)(2,1)S(1)} %slice.67), channel_id=1, source_target_pairs={{0,4},{4,8},{8,12},{12,14},{14,10},{10,6},{6,2},{2,0},{1,5},{5,9},... | collective-permute-start | bytes 706568 | tf_op jit(solution)/shard_map/ppermute | solution.py:371
  52.4 7.0 %collective-permute-start.13 = (bf16[40,2944]{1,0:T(8,128)(2,1)S(1)}, bf16[40,2944]{1,0:T(8,128)(2,1)S(1)}, u32[]{:S(2)}, u32[]{:S(2)}) collective-permute-start(bf16[40,2944]{1,0:T(8,128)(2,1)S(1)} %slice.68), channel_id=1, source_target_pairs={{4,0},{8,4},{12,8},{14,12},{10,14},{6,10},{2,6},{0,2},{5,1},{9,5},... | collective-permute-start | bytes 706568 | tf_op jit(solution)/shard_map/ppermute | solution.py:374
  54.1 9.9 %collective-permute-start.18 = (bf16[40,2944]{1,0:T(8,128)(2,1)S(1)}, bf16[40,2944]{1,0:T(8,128)(2,1)S(1)}, u32[]{:S(2)}, u32[]{:S(2)}) collective-permute-start(bf16[40,2944]{1,0:T(8,128)(2,1)S(1)} %get-tuple-element.130), channel_id=1, source_target_pairs={{0,4},{4,8},{8,12},{12,14},{14,10},{10,6},{6,2},{2,0},{1,5},{5,9},... | collective-permute-start | bytes 706568 | tf_op jit(solution)/shard_map/ppermute | solution.py:371
  54.6 9.4 %collective-permute-start.20 = (bf16[40,2944]{1,0:T(8,128)(2,1)S(1)}, bf16[40,2944]{1,0:T(8,128)(2,1)S(1)}, u32[]{:S(2)}, u32[]{:S(2)}) collective-permute-start(bf16[40,2944]{1,0:T(8,128)(2,1)S(1)} %get-tuple-element.129), channel_id=1, source_target_pairs={{4,0},{8,4},{12,8},{14,12},{10,14},{6,10},{2,6},{0,2},{5,1},{9,5},... | collective-permute-start | bytes 706568 | tf_op jit(solution)/shard_map/ppermute | solution.py:374
  57.9 16.5 %collective-permute-start.11 = (bf16[80,2944]{1,0:T(8,128)(2,1)S(1)}, bf16[80,2944]{1,0:T(8,128)(2,1)S(1)}, u32[]{:S(2)}, u32[]{:S(2)}) collective-permute-start(bf16[80,2944]{1,0:T(8,128)(2,1)S(1)} %get-tuple-element.95), channel_id=1, source_target_pairs={{0,16},{16,0},{1,17},{17,1},{2,18},{18,2},{3,19},{19,3},{4,20},{20... | collective-permute-start | bytes 1413128 | tf_op jit(solution)/shard_map/ppermute | solution.py:346
  60.8 3.3 %copy-start.3 = (f32[1,640]{1,0:T(1,128)S(1)}, f32[1,640]{1,0:T(1,128)}, u32[]{:S(2)}) copy-start(f32[1,640]{1,0:T(1,128)} %bias.1) | copy-start | bytes 7684
  64.1 2.9 %collective-permute-start.21 = (f32[3,640]{1,0:T(4,128)S(1)}, f32[3,640]{1,0:T(4,128)S(1)}, u32[]{:S(2)}, u32[]{:S(2)}) collective-permute-start(f32[3,640]{1,0:T(4,128)S(1)} %fusion.2), channel_id=1, source_target_pairs={{0,1},{1,0},{2,3},{3,2},{4,5},{5,4},{6,7},{7,6},{8,9},{9,8},{10,11... | collective-permute-start | bytes 23048 | tf_op jit(solution)/shard_map/ppermute | solution.py:346
  64.2 10.3 %collective-permute-start.14 = (bf16[512,256]{1,0:T(8,128)(2,1)S(1)}, bf16[512,256]{1,0:T(8,128)(2,1)S(1)}, u32[]{:S(2)}, u32[]{:S(2)}) collective-permute-start(bf16[512,256]{1,0:T(8,128)(2,1)S(1)} %shard_map.124), channel_id=1, source_target_pairs={{0,1},{1,0},{2,3},{3,2},{4,5},{5,4},{6,7},{7,6},{8,9},{9,8},{10,11... | collective-permute-start | bytes 786440 | tf_op jit(solution)/shard_map/ppermute | solution.py:346
  64.9 9.5 %collective-permute-start.24 = (bf16[40,2944]{1,0:T(8,128)(2,1)S(1)}, bf16[40,2944]{1,0:T(8,128)(2,1)S(1)}, u32[]{:S(2)}, u32[]{:S(2)}) collective-permute-start(bf16[40,2944]{1,0:T(8,128)(2,1)S(1)} %get-tuple-element.132), channel_id=1, source_target_pairs={{0,4},{4,8},{8,12},{12,14},{14,10},{10,6},{6,2},{2,0},{1,5},{5,9},... | collective-permute-start | bytes 706568 | tf_op jit(solution)/shard_map/ppermute | solution.py:371
  66.4 8.0 %collective-permute-start.25 = (bf16[40,2944]{1,0:T(8,128)(2,1)S(1)}, bf16[40,2944]{1,0:T(8,128)(2,1)S(1)}, u32[]{:S(2)}, u32[]{:S(2)}) collective-permute-start(bf16[40,2944]{1,0:T(8,128)(2,1)S(1)} %get-tuple-element.131), channel_id=1, source_target_pairs={{4,0},{8,4},{12,8},{14,12},{10,14},{6,10},{2,6},{0,2},{5,1},{9,5},... | collective-permute-start | bytes 706568 | tf_op jit(solution)/shard_map/ppermute | solution.py:374
  67.0 3.7 %collective-permute-start.22 = (f32[3,640]{1,0:T(4,128)S(1)}, f32[3,640]{1,0:T(4,128)S(1)}, u32[]{:S(2)}, u32[]{:S(2)}) collective-permute-start(f32[3,640]{1,0:T(4,128)S(1)} %fusion.4), channel_id=1, source_target_pairs={{0,16},{16,0},{1,17},{17,1},{2,18},{18,2},{3,19},{19,3},{4,20},{20... | collective-permute-start | bytes 23048 | tf_op jit(solution)/shard_map/ppermute | solution.py:395
  70.7 3.7 %collective-permute-start.23 = (f32[3,640]{1,0:T(4,128)S(1)}, f32[3,640]{1,0:T(4,128)S(1)}, u32[]{:S(2)}, u32[]{:S(2)}) collective-permute-start(f32[3,640]{1,0:T(4,128)S(1)} %add.91), channel_id=1, source_target_pairs={{0,4},{4,0},{8,12},{12,8},{1,5},{5,1},{9,13},{13,9},{2,6},{6,2},{1... | collective-permute-start | bytes 23048 | tf_op jit(solution)/shard_map/ppermute | solution.py:395
  74.4 1.9 %collective-permute-start.27 = (bf16[512,512]{1,0:T(8,128)(2,1)S(1)}, bf16[512,512]{1,0:T(8,128)(2,1)S(1)}, u32[]{:S(2)}, u32[]{:S(2)}) collective-permute-start(bf16[512,512]{1,0:T(8,128)(2,1)S(1)} %get-tuple-element.112), channel_id=1, source_target_pairs={{0,1},{1,0},{2,3},{3,2},{4,5},{5,4},{6,7},{7,6},{8,9},{9,8},{10,11... | collective-permute-start | bytes 1572872 | tf_op jit(solution)/shard_map/ppermute | solution.py:346
  74.5 9.1 %collective-permute-start.26 = (bf16[40,2944]{1,0:T(8,128)(2,1)S(1)}, bf16[40,2944]{1,0:T(8,128)(2,1)S(1)}, u32[]{:S(2)}, u32[]{:S(2)}) collective-permute-start(bf16[40,2944]{1,0:T(8,128)(2,1)S(1)} %add_convert_fusion.1), channel_id=1, source_target_pairs={{0,4},{4,8},{8,12},{12,14},{14,10},{10,6},{6,2},{2,0},{1,5},{5,9},... | collective-permute-start | bytes 706568 | tf_op jit(solution)/shard_map/ppermute | solution.py:371
  80.0 3.7 %collective-permute-start.28 = (f32[3,640]{1,0:T(4,128)S(1)}, f32[3,640]{1,0:T(4,128)S(1)}, u32[]{:S(2)}, u32[]{:S(2)}) collective-permute-start(f32[3,640]{1,0:T(4,128)S(1)} %add.92), channel_id=1, source_target_pairs={{0,2},{2,0},{1,3},{3,1},{4,6},{6,4},{5,7},{7,5},{8,10},{10,8},{9,1... | collective-permute-start | bytes 23048 | tf_op jit(solution)/shard_map/ppermute | solution.py:395
  83.8 6.9 %collective-permute-start.29 = (bf16[40,2944]{1,0:T(8,128)(2,1)S(1)}, bf16[40,2944]{1,0:T(8,128)(2,1)S(1)}, u32[]{:S(2)}, u32[]{:S(2)}) collective-permute-start(bf16[40,2944]{1,0:T(8,128)(2,1)S(1)} %add_convert_fusion), channel_id=1, source_target_pairs={{0,16},{16,0},{1,17},{17,1},{2,18},{18,2},{3,19},{19,3},{4,20},{20... | collective-permute-start | bytes 706568 | tf_op jit(solution)/shard_map/ppermute | solution.py:346
  85.2 4.6 %collective-permute-start.30 = (f32[3,640]{1,0:T(4,128)S(1)}, f32[3,640]{1,0:T(4,128)S(1)}, u32[]{:S(2)}, u32[]{:S(2)}) collective-permute-start(f32[3,640]{1,0:T(4,128)S(1)} %add.99), channel_id=1, source_target_pairs={{0,8},{4,12},{8,0},{12,4},{1,9},{5,13},{9,1},{13,5},{2,10},{6,14},... | collective-permute-start | bytes 23048 | tf_op jit(solution)/shard_map/ppermute | solution.py:395
  90.7 1.6 %collective-permute-start.31 = (bf16[40,2944]{1,0:T(8,128)(2,1)S(1)}, bf16[40,2944]{1,0:T(8,128)(2,1)S(1)}, u32[]{:S(2)}, u32[]{:S(2)}) collective-permute-start(bf16[40,2944]{1,0:T(8,128)(2,1)S(1)} %get-tuple-element.139), channel_id=1, source_target_pairs={{0,1},{1,0},{2,3},{3,2},{4,5},{5,4},{6,7},{7,6},{8,9},{9,8},{10,11... | collective-permute-start | bytes 706568 | tf_op jit(solution)/shard_map/ppermute | solution.py:346

commit v17 on v14

--- a/solution.py
+++ b/solution.py
@@ -425,6 +425,7 @@
 
     mine = lax.dynamic_slice_in_dim(shard, core * cols.start, cols.lead, 1).astype(BF16)
     theirs = lax.dynamic_slice_in_dim(shard, (1 - core) * cols.start, cols.lead, 1).astype(BF16)
+    theirs, cotan = tied(theirs, cotan)
     got = swap(theirs, "core")
     unit = jnp.where(lower, jnp.concatenate([mine, got]), jnp.concatenate([got, mine]))
     lat_far = swap(latent, "core")
@@ -435,7 +436,7 @@
         table = jnp.asarray(ring.table(part))
         order = (ring.count, part, 2 * ring.count)
         up1, down1 = ring.up(unit), ring.down(unit)
-        peer = swap(mine, "replica")
+        peer = swap(tied(mine, unit)[0], "replica")
     else:
         table = jnp.zeros((replicas * zs * 4, 1), jnp.int32)
         order = None
@@ -524,7 +525,9 @@
 
     if paired:
         kept, *sent = pieces
-        crossed = [swap(piece, "replica") for piece in sent]
+        crossed = [swap(sent[0], "replica")]
+        up, down, stats, *sent[:3] = tied(up1, down1, stats, *sent[:3])
+        crossed += [swap(piece, "replica") for piece in sent[1:3]]
         theirs = crossed[1]
 
         def ring_sums(j, *received):
@@ -537,7 +540,6 @@
         def ring_step(ahead, behind):
             return ring.up(ahead), ring.down(behind)
 
-        up, down, stats, _ = tied(up1, down1, stats, sent[0])
         blocks = [unit, up, down]
         up, down = ring.up(up), ring.down(down)
         up, down, cots, *slopes, order = tied(up, down, *slopes_of(stats))
@@ -549,7 +551,8 @@
         conv_first_own, conv_send = conv_first(blocks)
         cots, conv_send = tied(cots, conv_send)
         first_sums = back(0, cots, slopes, blocks)
-        up, down, first_sums, crossed[1] = tied(up, down, first_sums, crossed[1])
+        up, down, first_sums, crossed[1], sent[3] = tied(up, down, first_sums, crossed[1], sent[3])
+        crossed.append(swap(sent[3], "replica"))
         late = [up, down]
         received = up[2 * part:], down[2 * part:]
 
@@ -564,7 +567,7 @@
         conv_got = swap(conv_send, "core")
         received = ring_step(*ring_sums(zs - 2, *received))
         sums = back(1, cots, slopes, late)
-        crossed[3], conv_got, sums, *received = tied(crossed[3], conv_got, sums, *received)
+        crossed[3], conv_got, *received = tied(crossed[3], conv_got, *received)
         ahead, behind = ring_sums(zs - 1, *received)
         last = ring.up(ahead)
         block = conv_own(conv_got, [conv_first_own, conv_first_got, order], late)

time: 93.9 us -> 97.5 us (1.038)
  starting transfers between devices: 30.9 us -> 32.2 us
  local copies, waits for them, and re-layouts: 0.13 us -> 1.36 us
  waiting for transfers between devices: 25.8 us -> 26.8 us
    ppermute x6, waiting for transfers between devices: 7.14 us -> 0.65 us  [down(): return lax.ppermute(value, NODE, self.behind)]
    ppermute x13, waiting for transfers between devices: 5.21 us -> 11.5 us  [swap(): return lax.ppermute(value, axis, [(0, 1), (1, 0)])]
    ppermute x6, starting transfers between devices: 2.38 us -> 5.36 us  [down(): return lax.ppermute(value, NODE, self.behind)]
    ppermute x4, waiting for transfers between devices: 6.32 us -> 9.05 us  [hop(): lax.ppermute(value, axis, [(s, s ^ mask) for s in range(count)])]
    ppermute x7, starting transfers between devices: 12.4 us -> 10.4 us  [up(): return lax.ppermute(value, NODE, self.ahead)]
    ppermute x7, waiting for transfers between devices: 7.14 us -> 5.6 us  [up(): return lax.ppermute(value, NODE, self.ahead)]
    convert_element_type x1, local copies, waits for them, and re-layouts: 0.07 us -> 1.29 us  [per_device(): lax.dynamic_slice_in_dim(shard, (1 - core) * cols.start, cols.lead, 1)]
    ppermute x4, starting transfers between devices: 5.61 us -> 6.61 us  [hop(): lax.ppermute(value, axis, [(s, s ^ mask) for s in range(count)])]
  transfers between devices with their start and end apart: 30 -> 30, of which waited for: 16 -> 15; matrix products, arithmetic and copies ran while one was open for 1% -> 1% of each run, Pallas kernels for 33% -> 32%
where the time goes in v17:
time: 97.5 us; the launch traced here: 97.3 us
  Pallas kernels  32.3 us (33%)
  starting transfers between devices  32.2 us (33%)
  waiting for transfers between devices  26.8 us (27%)
  other arithmetic  2.98 us (3%)
  between operations  1.58 us (2%)
  local copies, waits for them, and re-layouts  1.36 us (1%)
    ppermute x13, waiting for transfers between devices, swap(): return lax.ppermute(value, axis, [(0, 1), (1, 0)])  11.5 us
    ppermute x7, starting transfers between devices, up(): return lax.ppermute(value, NODE, self.ahead)  10.4 us
    ppermute x13, starting transfers between devices, swap(): return lax.ppermute(value, axis, [(0, 1), (1, 0)])  9.89 us
    ppermute x4, waiting for transfers between devices, hop(): lax.ppermute(value, axis, [(s, s ^ mask) for s in range(count)])  9.05 us
    pallas_call x2, Pallas kernels, back(): call(partial(back_kernel, cols, stages, stage), jax.ShapeDtypeStruct((2,...  8.56 us
    ppermute x4, starting transfers between devices, hop(): lax.ppermute(value, axis, [(s, s ^ mask) for s in range(count)])  6.61 us
    ppermute x7, waiting for transfers between devices, up(): return lax.ppermute(value, NODE, self.ahead)  5.6 us
    ppermute x6, starting transfers between devices, down(): return lax.ppermute(value, NODE, self.behind)  5.36 us
  transfers between devices with their start and end apart: 30, of which 15 were waited for; matrix products, arithmetic and copies ran while one was open for 1% of the time, Pallas kernels for 32%

profile of v17, /device:TPU:0, one launch (start us, length us, event | category | flops | bytes accessed | tf_op | source)
XLA Modules:
  0.0 97.3 jit_solution(3231280424384726503)
XLA Ops:
  0.7 1.3 %fusion.1 = (bf16[40,2944]{1,0:T(8,128)(2,1)S(1)}, bf16[40,2944]{1,0:T(8,128)(2,1)S(1)}) fusion(f32[1,40,5760]{2,1,0:T(8,128)} %param.10, s32[]{:T(128)S(6)} %select_n.28, s32[]{:T(128)S(6)} %select_n.26), kind=kLoop, calls=%fused_computation.14 | loop fusion | bytes 942088 | tf_op jit(solution)/shard_map/convert_element_type | solution.py:427
  2.0 2.0 %fusion.3 = (f32[640]{0:T(1024)S(1)}, bf16[16,32,640]{2,1,0:T(8,128)(2,1)S(1)}) fusion(f32[16,32,640]{2,1,0:T(8,128)} %bitcast.15), kind=kLoop, calls=%fused_computation.20 | loop fusion | flops 654720 | bytes 1968640 | tf_op jit(solution)/shard_map/reduce_sum | solution.py:522
  4.0 0.5 collective-permute-start.3
  4.6 0.4 collective-permute-start
  5.0 2.5 %collective-permute-done = bf16[40,2944]{1,0:T(8,128)(2,1)S(1)} collective-permute-done((bf16[40,2944]{1,0:T(8,128)(2,1)S(1)}, bf16[40,2944]{1,0:T(8,128)(2,1)S(1)}, u32[]{:S(2)}, u32[]{:S(2)}) %collective-permute-start) | collective-permute-done | bytes 235552 | tf_op jit(solution)/shard_map/ppermute | solution.py:346
  7.6 3.0 %collective-permute-start.4 = (bf16[80,2944]{1,0:T(8,128)(2,1)S(1)}, bf16[80,2944]{1,0:T(8,128)(2,1)S(1)}, u32[]{:S(2)}, u32[]{:S(2)}) collective-permute-start(bf16[80,2944]{1,0:T(8,128)(2,1)S(1)} %maximum_select_fusion.refs_0_), channel_id=1, source_target_pairs={{0,4},{4,8},{8,12},{12,14},{14,10},{10,6},{6,2},{2,0},{1,5},{5,9},... | collective-permute-start | bytes 1413128 | tf_op jit(solution)/shard_map/ppermute | solution.py:371
  10.6 1.9 %collective-permute-start.1 = (bf16[40,2944]{1,0:T(8,128)(2,1)S(1)}, bf16[40,2944]{1,0:T(8,128)(2,1)S(1)}, u32[]{:S(2)}, u32[]{:S(2)}) collective-permute-start(bf16[40,2944]{1,0:T(8,128)(2,1)S(1)} %get-tuple-element.66), channel_id=1, source_target_pairs={{0,16},{16,0},{1,17},{17,1},{2,18},{18,2},{3,19},{19,3},{4,20},{20... | collective-permute-start | bytes 706568 | tf_op jit(solution)/shard_map/ppermute | solution.py:346
  12.5 4.4 %shard_map.119 = (f32[2,640]{1,0:T(2,128)S(1)}, bf16[3,34,32,640]{3,2,1,0:T(8,128)(2,1)S(1)}, bf16[640,1024]{1,0:T(8,128)(2,1)S(1)}) custom-call(s32[1]{0:T(128)} %bitcast.dev, s32[32,24]{1,0:T(8,128)S(1)} %copy-done.5, bf16[16,32,640]{2,1,0:T(8,128)(2,1)S(1)} %bitcast.12, bf16[16,32,640]{2,1,0:T(8,128)(2,1)S(1)} %collective-permute-done.2.lat_far, ...), custom_call_target="tpu_custom_call" | custom-call | flops 3858759680 | tf_op jit(solution)/shard_map/pallas_call | solution.py:458
  16.9 1.1 %collective-permute-done.1.mine = bf16[40,2944]{1,0:T(8,128)(2,1)S(1)} collective-permute-done((bf16[40,2944]{1,0:T(8,128)(2,1)S(1)}, bf16[40,2944]{1,0:T(8,128)(2,1)S(1)}, u32[]{:S(2)}, u32[]{:S(2)}) %collective-permute-start.1) | collective-permute-done | bytes 235552 | tf_op jit(solution)/shard_map/ppermute | solution.py:346
  18.1 4.6 %shard_map.120 = (bf16[320,2944]{1,0:T(8,128)(2,1)S(1)}, bf16[80,2944]{1,0:T(8,128)(2,1)S(1)}, bf16[120,2944]{1,0:T(8,128)(2,1)S(1)}, bf16[80,2944]{1,0:T(8,128)(2,1)S(1)}, bf16[80,2944]{1,0:T(8,128)(2,1)S(1)}) custom-call(s32[1]{0:T(128)} %bitcast.dev, bf16[3,34,32,640]{3,2,1,0:T(8,128)(2,1)S(1)} %get-tuple-element.69.acts, ...), custom_call_target="tpu_custom_call" | custom-call | flops 7717519360 | tf_op jit(solution)/shard_map/pallas_call | solution.py:468
  22.7 1.7 %collective-permute-start.8 = (bf16[80,2944]{1,0:T(8,128)(2,1)S(1)}, bf16[80,2944]{1,0:T(8,128)(2,1)S(1)}, u32[]{:S(2)}, u32[]{:S(2)}) collective-permute-start(bf16[80,2944]{1,0:T(8,128)(2,1)S(1)} %get-tuple-element.73), channel_id=1, source_target_pairs={{0,16},{16,0},{1,17},{17,1},{2,18},{18,2},{3,19},{19,3},{4,20},{20... | collective-permute-start | bytes 1413128 | tf_op jit(solution)/shard_map/ppermute | solution.py:346
  24.4 1.6 %collective-permute-start.6 = (bf16[80,2944]{1,0:T(8,128)(2,1)S(1)}, bf16[80,2944]{1,0:T(8,128)(2,1)S(1)}, u32[]{:S(2)}, u32[]{:S(2)}) collective-permute-start(bf16[80,2944]{1,0:T(8,128)(2,1)S(1)} %collective-permute-done.4.refs_1_), channel_id=1, source_target_pairs={{0,4},{4,8},{8,12},{12,14},{14,10},{10,6},{6,2},{2,0},{1,5},{5,9},... | collective-permute-start | bytes 1413128 | tf_op jit(solution)/shard_map/ppermute | solution.py:371
  26.0 0.4 collective-permute-start.7
  26.8 1.6 %collective-permute-start.13 = (bf16[80,2944]{1,0:T(8,128)(2,1)S(1)}, bf16[80,2944]{1,0:T(8,128)(2,1)S(1)}, u32[]{:S(2)}, u32[]{:S(2)}) collective-permute-start(bf16[80,2944]{1,0:T(8,128)(2,1)S(1)} %get-tuple-element.93), channel_id=1, source_target_pairs={{0,16},{16,0},{1,17},{17,1},{2,18},{18,2},{3,19},{19,3},{4,20},{20... | collective-permute-start | bytes 1413128 | tf_op jit(solution)/shard_map/ppermute | solution.py:346
  28.5 4.5 %shard_map.121 = (bf16[3,34,32,768]{3,2,1,0:T(8,128)(2,1)S(1)}, bf16[32,32,640]{2,1,0:T(8,128)(2,1)S(1)}, bf16[32,32,640]{2,1,0:T(8,128)(2,1)S(1)}, bf16[640,768]{1,0:T(8,128)(2,1)S(1)}) custom-call(s32[1]{0:T(128)} %bitcast.dev, s32[32,24]{1,0:T(8,128)S(1)} %copy-done.5, f32[2,640]{1,0:T(2,128)S(1)} %get-tuple-element.78.stats, f32[1,640]{1,0:T(1,128)S(1)} %copy-done.1, ...), custom_call_target="tpu_custom_call" | custom-call | flops 3858759680 | tf_op jit(solution)/shard_map/pallas_call | solution.py:480
  33.0 3.4 %collective-permute-done.8 = bf16[80,2944]{1,0:T(8,128)(2,1)S(1)} collective-permute-done((bf16[80,2944]{1,0:T(8,128)(2,1)S(1)}, bf16[80,2944]{1,0:T(8,128)(2,1)S(1)}, u32[]{:S(2)}, u32[]{:S(2)}) %collective-permute-start.8) | collective-permute-done | bytes 471072 | tf_op jit(solution)/shard_map/ppermute | solution.py:346
  36.9 1.5 %collective-permute-start.10 = (bf16[120,2944]{1,0:T(8,128)(2,1)S(1)}, bf16[120,2944]{1,0:T(8,128)(2,1)S(1)}, u32[]{:S(2)}, u32[]{:S(2)}) collective-permute-start(bf16[120,2944]{1,0:T(8,128)(2,1)S(1)} %pad_maximum_fusion.1), channel_id=1, source_target_pairs={{4,0},{8,4},{12,8},{14,12},{10,14},{6,10},{2,6},{0,2},{5,1},{9,5},... | collective-permute-start | bytes 2119688 | tf_op jit(solution)/shard_map/ppermute | solution.py:374
  38.4 0.7 collective-permute-start.9
  39.1 4.0 %shard_map.122 = (f32[512,512]{1,0:T(8,128)S(1)}, bf16[512,512]{1,0:T(8,128)(2,1)S(1)}) custom-call(s32[1]{0:T(128)} %bitcast.dev, bf16[3,34,32,640]{3,2,1,0:T(8,128)(2,1)S(1)} %get-tuple-element.69.acts, bf16[80,2944]{1,0:T(8,128)(2,1)S(1)} %maximum_select_fusion.refs_0_, bf16[80,2944]{1,0:T(8,128)(2,1)S(1)} %collective-permute-done.4.refs_1_, ...), custom_call_target="tpu_custom_call" | custom-call | flops 3858759680 | tf_op jit(solution)/shard_map/pallas_call | solution.py:498
  43.1 5.3 %shard_map.123 = f32[2,640]{1,0:T(2,128)S(1)} custom-call(s32[1]{0:T(128)} %bitcast.dev, bf16[3,34,32,768]{3,2,1,0:T(8,128)(2,1)S(1)} %get-tuple-element.106.cots, bf16[32,32,640]{2,1,0:T(8,128)(2,1)S(1)} %get-tuple-element.88.slope, bf16[32,32,640]{2,1,0:T(8,128)(2,1)S(1)} %get-tuple-element.89.slope_x, bf16[80,2944]{1,0:T(8,128)(2,1)S(1)} %maximum_select_fusion.refs_0_, ...), custom_call_target="tpu_custom_call" | custom-call | flops 3858759680 | tf_op jit(solution)/shard_map/pallas_call | solution.py:490
  48.4 3.2 %collective-permute-done.11.carried = bf16[120,2944]{1,0:T(8,128)(2,1)S(1)} collective-permute-done((bf16[120,2944]{1,0:T(8,128)(2,1)S(1)}, bf16[120,2944]{1,0:T(8,128)(2,1)S(1)}, u32[]{:S(2)}, u32[]{:S(2)}) %collective-permute-start.11) | collective-permute-done | bytes 706592 | tf_op jit(solution)/shard_map/ppermute | solution.py:346
  51.9 1.4 %collective-permute-done.9.refs_0_.refs_3_ = bf16[120,2944]{1,0:T(8,128)(2,1)S(1)} collective-permute-done((bf16[120,2944]{1,0:T(8,128)(2,1)S(1)}, bf16[120,2944]{1,0:T(8,128)(2,1)S(1)}, u32[]{:S(2)}, u32[]{:S(2)}) %collective-permute-start.9) | collective-permute-done | bytes 706592 | tf_op jit(solution)/shard_map/ppermute | solution.py:371
  53.3 1.5 %collective-permute-start.14 = (bf16[40,2944]{1,0:T(8,128)(2,1)S(1)}, bf16[40,2944]{1,0:T(8,128)(2,1)S(1)}, u32[]{:S(2)}, u32[]{:S(2)}) collective-permute-start(bf16[40,2944]{1,0:T(8,128)(2,1)S(1)} %slice.77), channel_id=1, source_target_pairs={{0,4},{4,8},{8,12},{12,14},{14,10},{10,6},{6,2},{2,0},{1,5},{5,9},... | collective-permute-start | bytes 706568 | tf_op jit(solution)/shard_map/ppermute | solution.py:371
  54.9 1.3 %collective-permute-start.15 = (bf16[40,2944]{1,0:T(8,128)(2,1)S(1)}, bf16[40,2944]{1,0:T(8,128)(2,1)S(1)}, u32[]{:S(2)}, u32[]{:S(2)}) collective-permute-start(bf16[40,2944]{1,0:T(8,128)(2,1)S(1)} %slice.78), channel_id=1, source_target_pairs={{4,0},{8,4},{12,8},{14,12},{10,14},{6,10},{2,6},{0,2},{5,1},{9,5},... | collective-permute-start | bytes 706568 | tf_op jit(solution)/shard_map/ppermute | solution.py:374
  56.3 0.9 collective-permute-start.17
  57.2 1.4 %collective-permute-start.19 = (bf16[40,2944]{1,0:T(8,128)(2,1)S(1)}, bf16[40,2944]{1,0:T(8,128)(2,1)S(1)}, u32[]{:S(2)}, u32[]{:S(2)}) collective-permute-start(bf16[40,2944]{1,0:T(8,128)(2,1)S(1)} %get-tuple-element.119), channel_id=1, source_target_pairs={{4,0},{8,4},{12,8},{14,12},{10,14},{6,10},{2,6},{0,2},{5,1},{9,5},... | collective-permute-start | bytes 706568 | tf_op jit(solution)/shard_map/ppermute | solution.py:374
  58.6 1.5 %collective-permute-done.14.refs_2_.refs_5_ = bf16[40,2944]{1,0:T(8,128)(2,1)S(1)} collective-permute-done((bf16[40,2944]{1,0:T(8,128)(2,1)S(1)}, bf16[40,2944]{1,0:T(8,128)(2,1)S(1)}, u32[]{:S(2)}, u32[]{:S(2)}) %collective-permute-start.14) | collective-permute-done | bytes 235552 | tf_op jit(solution)/shard_map/ppermute | solution.py:371
  60.1 1.2 %collective-permute-start.12 = (bf16[80,2944]{1,0:T(8,128)(2,1)S(1)}, bf16[80,2944]{1,0:T(8,128)(2,1)S(1)}, u32[]{:S(2)}, u32[]{:S(2)}) collective-permute-start(bf16[80,2944]{1,0:T(8,128)(2,1)S(1)} %get-tuple-element.92), channel_id=1, source_target_pairs={{0,16},{16,0},{1,17},{17,1},{2,18},{18,2},{3,19},{19,3},{4,20},{20... | collective-permute-start | bytes 1413128 | tf_op jit(solution)/shard_map/ppermute | solution.py:346
  61.3 1.4 %shard_map.124 = bf16[512,256]{1,0:T(8,128)(2,1)S(1)} custom-call(s32[1]{0:T(128)} %bitcast.dev, bf16[3,34,32,640]{3,2,1,0:T(8,128)(2,1)S(1)} %get-tuple-element.69.acts, bf16[120,2944]{1,0:T(8,128)(2,1)S(1)} %collective-permute-done.9.refs_0_.refs_3_, bf16[120,2944]{1,0:T(8,128)(2,1)S(1)} %collective-permute-done.10.refs_1_.refs_4_, ...), custom_call_target="tpu_custom_call" | custom-call | flops 1929379840 | tf_op jit(solution)/shard_map/pallas_call | solution.py:507
  62.7 3.2 %shard_map.126 = f32[2,640]{1,0:T(2,128)S(1)} custom-call(s32[1]{0:T(128)} %bitcast.dev, bf16[3,34,32,768]{3,2,1,0:T(8,128)(2,1)S(1)} %get-tuple-element.106.cots, bf16[32,32,640]{2,1,0:T(8,128)(2,1)S(1)} %get-tuple-element.88.slope, bf16[32,32,640]{2,1,0:T(8,128)(2,1)S(1)} %get-tuple-element.89.slope_x, ...), custom_call_target="tpu_custom_call" | custom-call | flops 3858759680 | tf_op jit(solution)/shard_map/pallas_call | solution.py:490
  66.1 0.5 collective-permute-start.16
  66.8 1.4 %collective-permute-start.18 = (bf16[40,2944]{1,0:T(8,128)(2,1)S(1)}, bf16[40,2944]{1,0:T(8,128)(2,1)S(1)}, u32[]{:S(2)}, u32[]{:S(2)}) collective-permute-start(bf16[40,2944]{1,0:T(8,128)(2,1)S(1)} %get-tuple-element.122), channel_id=1, source_target_pairs={{0,4},{4,8},{8,12},{12,14},{14,10},{10,6},{6,2},{2,0},{1,5},{5,9},... | collective-permute-start | bytes 706568 | tf_op jit(solution)/shard_map/ppermute | solution.py:371
  68.1 0.7 collective-permute-start.20
  68.9 1.4 %collective-permute-start.24 = (f32[3,640]{1,0:T(4,128)S(1)}, f32[3,640]{1,0:T(4,128)S(1)}, u32[]{:S(2)}, u32[]{:S(2)}) collective-permute-start(f32[3,640]{1,0:T(4,128)S(1)} %fusion.4), channel_id=1, source_target_pairs={{0,16},{16,0},{1,17},{17,1},{2,18},{18,2},{3,19},{19,3},{4,20},{20... | collective-permute-start | bytes 23048 | tf_op jit(solution)/shard_map/ppermute | solution.py:395
  70.3 2.3 %collective-permute-done.24 = f32[3,640]{1,0:T(4,128)S(1)} collective-permute-done((f32[3,640]{1,0:T(4,128)S(1)}, f32[3,640]{1,0:T(4,128)S(1)}, u32[]{:S(2)}, u32[]{:S(2)}) %collective-permute-start.24) | collective-permute-done | bytes 7712 | tf_op jit(solution)/shard_map/ppermute | solution.py:395
  72.6 1.3 %collective-permute-start.25 = (f32[3,640]{1,0:T(4,128)S(1)}, f32[3,640]{1,0:T(4,128)S(1)}, u32[]{:S(2)}, u32[]{:S(2)}) collective-permute-start(f32[3,640]{1,0:T(4,128)S(1)} %add.97), channel_id=1, source_target_pairs={{0,4},{4,0},{8,12},{12,8},{1,5},{5,1},{9,13},{13,9},{2,6},{6,2},{1... | collective-permute-start | bytes 23048 | tf_op jit(solution)/shard_map/ppermute | solution.py:395
  73.9 2.4 %collective-permute-done.25 = f32[3,640]{1,0:T(4,128)S(1)} collective-permute-done((f32[3,640]{1,0:T(4,128)S(1)}, f32[3,640]{1,0:T(4,128)S(1)}, u32[]{:S(2)}, u32[]{:S(2)}) %collective-permute-start.25) | collective-permute-done | bytes 7712 | tf_op jit(solution)/shard_map/ppermute | solution.py:395
  76.5 1.4 %collective-permute-start.21 = (bf16[40,2944]{1,0:T(8,128)(2,1)S(1)}, bf16[40,2944]{1,0:T(8,128)(2,1)S(1)}, u32[]{:S(2)}, u32[]{:S(2)}) collective-permute-start(bf16[40,2944]{1,0:T(8,128)(2,1)S(1)} %add_convert_fusion.1), channel_id=1, source_target_pairs={{0,4},{4,8},{8,12},{12,14},{14,10},{10,6},{6,2},{2,0},{1,5},{5,9},... | collective-permute-start | bytes 706568 | tf_op jit(solution)/shard_map/ppermute | solution.py:371
  77.8 0.4 collective-permute-done.22.refs_1_
  78.2 3.7 %shard_map.125 = bf16[16,32,640]{2,1,0:T(8,128)(2,1)} custom-call(s32[1]{0:T(128)} %bitcast.dev, bf16[3,34,32,640]{3,2,1,0:T(8,128)(2,1)S(1)} %get-tuple-element.69.acts, bf16[512,256]{1,0:T(8,128)(2,1)S(1)} %collective-permute-done.16.got, bf16[16,32,640]{2,1,0:T(8,128)(2,1)S(1)} %bitcast.14, f32[1,640]{1,0:T(1,128)S(1)} %copy-done.3, ...), custom_call_target="tpu_custom_call" | custom-call | flops 3858759680 | tf_op jit(solution)/shard_map/pallas_call | solution.py:515
  81.9 2.8 %collective-permute-done.21 = bf16[40,2944]{1,0:T(8,128)(2,1)S(1)} collective-permute-done((bf16[40,2944]{1,0:T(8,128)(2,1)S(1)}, bf16[40,2944]{1,0:T(8,128)(2,1)S(1)}, u32[]{:S(2)}, u32[]{:S(2)}) %collective-permute-start.21) | collective-permute-done | bytes 235552 | tf_op jit(solution)/shard_map/ppermute | solution.py:371
  84.8 1.4 %collective-permute-start.26 = (bf16[40,2944]{1,0:T(8,128)(2,1)S(1)}, bf16[40,2944]{1,0:T(8,128)(2,1)S(1)}, u32[]{:S(2)}, u32[]{:S(2)}) collective-permute-start(bf16[40,2944]{1,0:T(8,128)(2,1)S(1)} %add_convert_fusion), channel_id=1, source_target_pairs={{0,16},{16,0},{1,17},{17,1},{2,18},{18,2},{3,19},{19,3},{4,20},{20... | collective-permute-start | bytes 706568 | tf_op jit(solution)/shard_map/ppermute | solution.py:346
  86.2 1.5 %collective-permute-start.27 = (f32[3,640]{1,0:T(4,128)S(1)}, f32[3,640]{1,0:T(4,128)S(1)}, u32[]{:S(2)}, u32[]{:S(2)}) collective-permute-start(f32[3,640]{1,0:T(4,128)S(1)} %add.98), channel_id=1, source_target_pairs={{0,2},{2,0},{1,3},{3,1},{4,6},{6,4},{5,7},{7,5},{8,10},{10,8},{9,1... | collective-permute-start | bytes 23048 | tf_op jit(solution)/shard_map/ppermute | solution.py:395
  87.7 2.1 %collective-permute-done.27 = f32[3,640]{1,0:T(4,128)S(1)} collective-permute-done((f32[3,640]{1,0:T(4,128)S(1)}, f32[3,640]{1,0:T(4,128)S(1)}, u32[]{:S(2)}, u32[]{:S(2)}) %collective-permute-start.27) | collective-permute-done | bytes 7712 | tf_op jit(solution)/shard_map/ppermute | solution.py:395
  89.9 2.4 %collective-permute-start.28 = (f32[3,640]{1,0:T(4,128)S(1)}, f32[3,640]{1,0:T(4,128)S(1)}, u32[]{:S(2)}, u32[]{:S(2)}) collective-permute-start(f32[3,640]{1,0:T(4,128)S(1)} %add.102), channel_id=1, source_target_pairs={{0,8},{4,12},{8,0},{12,4},{1,9},{5,13},{9,1},{13,5},{2,10},{6,14},... | collective-permute-start | bytes 23048 | tf_op jit(solution)/shard_map/ppermute | solution.py:395
  92.2 2.2 %collective-permute-done.28 = f32[3,640]{1,0:T(4,128)S(1)} collective-permute-done((f32[3,640]{1,0:T(4,128)S(1)}, f32[3,640]{1,0:T(4,128)S(1)}, u32[]{:S(2)}, u32[]{:S(2)}) %collective-permute-start.28) | collective-permute-done | bytes 7712 | tf_op jit(solution)/shard_map/ppermute | solution.py:395
  95.2 0.8 collective-permute-done.29.aside
  96.1 1.2 %shard_map.127 = (f32[40,5760]{1,0:T(8,128)}, f32[1,640]{1,0:T(1,128)}, f32[1,640]{1,0:T(1,128)}, f32[1,640]{1,0:T(1,128)}) custom-call(s32[1]{0:T(128)} %bitcast.dev, s32[1]{0:T(128)S(6)} %copy.13.step, f32[40,5760]{1,0:T(8,128)S(1)} %bitcast.10, bf16[40,2944]{1,0:T(8,128)(2,1)S(1)} %collective-permute-done.1.mine, ...), custom_call_target="tpu_custom_call" | custom-call | flops 964689920 | tf_op jit(solution)/shard_map/pallas_call | solution.py:586
  (54 shorter events, 2.4 us)
Async XLA Ops:
  0.6 3.8 %copy-start.4 = (bf16[1,16,32,640]{3,2,1,0:T(8,128)(2,1)S(1)}, bf16[1,16,32,640]{3,2,1,0:T(8,128)(2,1)}, u32[]{:S(2)}) copy-start(bf16[1,16,32,640]{3,2,1,0:T(8,128)(2,1)} %param.8) | copy-start | bytes 1966084
  1.9 10.6 %copy-start.1 = (f32[1,640]{1,0:T(1,128)S(1)}, f32[1,640]{1,0:T(1,128)}, u32[]{:S(2)}) copy-start(f32[1,640]{1,0:T(1,128)} %gain.3) | copy-start | bytes 7684
  2.0 10.5 %copy-start.2 = (f32[1,640]{1,0:T(1,128)S(1)}, f32[1,640]{1,0:T(1,128)}, u32[]{:S(2)}) copy-start(f32[1,640]{1,0:T(1,128)} %shift.3) | copy-start | bytes 7684
  2.0 10.5 %copy-start.5 = (s32[32,24]{1,0:T(8,128)S(1)}, s32[32,24]{1,0:T(8,128)}, u32[]{:S(2)}) copy-start(s32[32,24]{1,0:T(8,128)} %constant.38.clone.table) | copy-start | bytes 9220
  4.0 8.5 %collective-permute-start.3 = (bf16[16,32,640]{2,1,0:T(8,128)(2,1)S(1)}, bf16[16,32,640]{2,1,0:T(8,128)(2,1)S(1)}, u32[]{:S(2)}, u32[]{:S(2)}) collective-permute-start(bf16[16,32,640]{2,1,0:T(8,128)(2,1)S(1)} %get-tuple-element.126.cot_own), channel_id=1, source_target_pairs={{0,1},{1,0},{2,3},{3,2},{4,5},{5,4},{6,7},{7,6},{8,9},{9,8},{10,11... | collective-permute-start | bytes 1966088 | tf_op jit(solution)/shard_map/ppermute | solution.py:346
  4.5 8.0 %collective-permute-start.2 = (bf16[16,32,640]{2,1,0:T(8,128)(2,1)S(1)}, bf16[16,32,640]{2,1,0:T(8,128)(2,1)S(1)}, u32[]{:S(2)}, u32[]{:S(2)}) collective-permute-start(bf16[16,32,640]{2,1,0:T(8,128)(2,1)S(1)} %bitcast.11), channel_id=1, source_target_pairs={{0,1},{1,0},{2,3},{3,2},{4,5},{5,4},{6,7},{7,6},{8,9},{9,8},{10,11... | collective-permute-start | bytes 1966088 | tf_op jit(solution)/shard_map/ppermute | solution.py:346
  4.6 2.9 %collective-permute-start = (bf16[40,2944]{1,0:T(8,128)(2,1)S(1)}, bf16[40,2944]{1,0:T(8,128)(2,1)S(1)}, u32[]{:S(2)}, u32[]{:S(2)}) collective-permute-start(bf16[40,2944]{1,0:T(8,128)(2,1)S(1)} %get-tuple-element.65.theirs), channel_id=1, source_target_pairs={{0,1},{1,0},{2,3},{3,2},{4,5},{5,4},{6,7},{7,6},{8,9},{9,8},{10,11... | collective-permute-start | bytes 706568 | tf_op jit(solution)/shard_map/ppermute | solution.py:346
  7.6 16.8 %collective-permute-start.4 = (bf16[80,2944]{1,0:T(8,128)(2,1)S(1)}, bf16[80,2944]{1,0:T(8,128)(2,1)S(1)}, u32[]{:S(2)}, u32[]{:S(2)}) collective-permute-start(bf16[80,2944]{1,0:T(8,128)(2,1)S(1)} %maximum_select_fusion.refs_0_), channel_id=1, source_target_pairs={{0,4},{4,8},{8,12},{12,14},{14,10},{10,6},{6,2},{2,0},{1,5},{5,9},... | collective-permute-start | bytes 1413128 | tf_op jit(solution)/shard_map/ppermute | solution.py:371
  10.6 13.8 %collective-permute-start.5 = (bf16[80,2944]{1,0:T(8,128)(2,1)S(1)}, bf16[80,2944]{1,0:T(8,128)(2,1)S(1)}, u32[]{:S(2)}, u32[]{:S(2)}) collective-permute-start(bf16[80,2944]{1,0:T(8,128)(2,1)S(1)} %maximum_select_fusion.refs_0_), channel_id=1, source_target_pairs={{4,0},{8,4},{12,8},{14,12},{10,14},{6,10},{2,6},{0,2},{5,1},{9,5},... | collective-permute-start | bytes 1413128 | tf_op jit(solution)/shard_map/ppermute | solution.py:374
  10.6 7.5 %collective-permute-start.1 = (bf16[40,2944]{1,0:T(8,128)(2,1)S(1)}, bf16[40,2944]{1,0:T(8,128)(2,1)S(1)}, u32[]{:S(2)}, u32[]{:S(2)}) collective-permute-start(bf16[40,2944]{1,0:T(8,128)(2,1)S(1)} %get-tuple-element.66), channel_id=1, source_target_pairs={{0,16},{16,0},{1,17},{17,1},{2,18},{18,2},{3,19},{19,3},{4,20},{20... | collective-permute-start | bytes 706568 | tf_op jit(solution)/shard_map/ppermute | solution.py:346
  22.7 13.8 %collective-permute-start.8 = (bf16[80,2944]{1,0:T(8,128)(2,1)S(1)}, bf16[80,2944]{1,0:T(8,128)(2,1)S(1)}, u32[]{:S(2)}, u32[]{:S(2)}) collective-permute-start(bf16[80,2944]{1,0:T(8,128)(2,1)S(1)} %get-tuple-element.73), channel_id=1, source_target_pairs={{0,16},{16,0},{1,17},{17,1},{2,18},{18,2},{3,19},{19,3},{4,20},{20... | collective-permute-start | bytes 1413128 | tf_op jit(solution)/shard_map/ppermute | solution.py:346
  24.4 12.2 %collective-permute-start.6 = (bf16[80,2944]{1,0:T(8,128)(2,1)S(1)}, bf16[80,2944]{1,0:T(8,128)(2,1)S(1)}, u32[]{:S(2)}, u32[]{:S(2)}) collective-permute-start(bf16[80,2944]{1,0:T(8,128)(2,1)S(1)} %collective-permute-done.4.refs_1_), channel_id=1, source_target_pairs={{0,4},{4,8},{8,12},{12,14},{14,10},{10,6},{6,2},{2,0},{1,5},{5,9},... | collective-permute-start | bytes 1413128 | tf_op jit(solution)/shard_map/ppermute | solution.py:371
  26.0 10.8 %collective-permute-start.7 = (bf16[80,2944]{1,0:T(8,128)(2,1)S(1)}, bf16[80,2944]{1,0:T(8,128)(2,1)S(1)}, u32[]{:S(2)}, u32[]{:S(2)}) collective-permute-start(bf16[80,2944]{1,0:T(8,128)(2,1)S(1)} %collective-permute-done.5.refs_2_), channel_id=1, source_target_pairs={{4,0},{8,4},{12,8},{14,12},{10,14},{6,10},{2,6},{0,2},{5,1},{9,5},... | collective-permute-start | bytes 1413128 | tf_op jit(solution)/shard_map/ppermute | solution.py:374
  26.5 25.1 %collective-permute-start.11 = (bf16[120,2944]{1,0:T(8,128)(2,1)S(1)}, bf16[120,2944]{1,0:T(8,128)(2,1)S(1)}, u32[]{:S(2)}, u32[]{:S(2)}) collective-permute-start(bf16[120,2944]{1,0:T(8,128)(2,1)S(1)} %get-tuple-element.90), channel_id=1, source_target_pairs={{0,16},{16,0},{1,17},{17,1},{2,18},{18,2},{3,19},{19,3},{4,20},{20... | collective-permute-start | bytes 2119688 | tf_op jit(solution)/shard_map/ppermute | solution.py:346
  26.8 35.9 %collective-permute-start.13 = (bf16[80,2944]{1,0:T(8,128)(2,1)S(1)}, bf16[80,2944]{1,0:T(8,128)(2,1)S(1)}, u32[]{:S(2)}, u32[]{:S(2)}) collective-permute-start(bf16[80,2944]{1,0:T(8,128)(2,1)S(1)} %get-tuple-element.93), channel_id=1, source_target_pairs={{0,16},{16,0},{1,17},{17,1},{2,18},{18,2},{3,19},{19,3},{4,20},{20... | collective-permute-start | bytes 1413128 | tf_op jit(solution)/shard_map/ppermute | solution.py:346
  36.9 15.0 %collective-permute-start.10 = (bf16[120,2944]{1,0:T(8,128)(2,1)S(1)}, bf16[120,2944]{1,0:T(8,128)(2,1)S(1)}, u32[]{:S(2)}, u32[]{:S(2)}) collective-permute-start(bf16[120,2944]{1,0:T(8,128)(2,1)S(1)} %pad_maximum_fusion.1), channel_id=1, source_target_pairs={{4,0},{8,4},{12,8},{14,12},{10,14},{6,10},{2,6},{0,2},{5,1},{9,5},... | collective-permute-start | bytes 2119688 | tf_op jit(solution)/shard_map/ppermute | solution.py:374
  38.4 14.9 %collective-permute-start.9 = (bf16[120,2944]{1,0:T(8,128)(2,1)S(1)}, bf16[120,2944]{1,0:T(8,128)(2,1)S(1)}, u32[]{:S(2)}, u32[]{:S(2)}) collective-permute-start(bf16[120,2944]{1,0:T(8,128)(2,1)S(1)} %pad_maximum_fusion), channel_id=1, source_target_pairs={{0,4},{4,8},{8,12},{12,14},{14,10},{10,6},{6,2},{2,0},{1,5},{5,9},... | collective-permute-start | bytes 2119688 | tf_op jit(solution)/shard_map/ppermute | solution.py:371
  53.3 6.8 %collective-permute-start.14 = (bf16[40,2944]{1,0:T(8,128)(2,1)S(1)}, bf16[40,2944]{1,0:T(8,128)(2,1)S(1)}, u32[]{:S(2)}, u32[]{:S(2)}) collective-permute-start(bf16[40,2944]{1,0:T(8,128)(2,1)S(1)} %slice.77), channel_id=1, source_target_pairs={{0,4},{4,8},{8,12},{12,14},{14,10},{10,6},{6,2},{2,0},{1,5},{5,9},... | collective-permute-start | bytes 706568 | tf_op jit(solution)/shard_map/ppermute | solution.py:371
  54.9 6.4 %collective-permute-start.15 = (bf16[40,2944]{1,0:T(8,128)(2,1)S(1)}, bf16[40,2944]{1,0:T(8,128)(2,1)S(1)}, u32[]{:S(2)}, u32[]{:S(2)}) collective-permute-start(bf16[40,2944]{1,0:T(8,128)(2,1)S(1)} %slice.78), channel_id=1, source_target_pairs={{4,0},{8,4},{12,8},{14,12},{10,14},{6,10},{2,6},{0,2},{5,1},{9,5},... | collective-permute-start | bytes 706568 | tf_op jit(solution)/shard_map/ppermute | solution.py:374
  56.3 10.2 %collective-permute-start.17 = (bf16[40,2944]{1,0:T(8,128)(2,1)S(1)}, bf16[40,2944]{1,0:T(8,128)(2,1)S(1)}, u32[]{:S(2)}, u32[]{:S(2)}) collective-permute-start(bf16[40,2944]{1,0:T(8,128)(2,1)S(1)} %get-tuple-element.120), channel_id=1, source_target_pairs={{0,4},{4,8},{8,12},{12,14},{14,10},{10,6},{6,2},{2,0},{1,5},{5,9},... | collective-permute-start | bytes 706568 | tf_op jit(solution)/shard_map/ppermute | solution.py:371
  57.2 9.4 %collective-permute-start.19 = (bf16[40,2944]{1,0:T(8,128)(2,1)S(1)}, bf16[40,2944]{1,0:T(8,128)(2,1)S(1)}, u32[]{:S(2)}, u32[]{:S(2)}) collective-permute-start(bf16[40,2944]{1,0:T(8,128)(2,1)S(1)} %get-tuple-element.119), channel_id=1, source_target_pairs={{4,0},{8,4},{12,8},{14,12},{10,14},{6,10},{2,6},{0,2},{5,1},{9,5},... | collective-permute-start | bytes 706568 | tf_op jit(solution)/shard_map/ppermute | solution.py:374
  60.1 16.2 %collective-permute-start.12 = (bf16[80,2944]{1,0:T(8,128)(2,1)S(1)}, bf16[80,2944]{1,0:T(8,128)(2,1)S(1)}, u32[]{:S(2)}, u32[]{:S(2)}) collective-permute-start(bf16[80,2944]{1,0:T(8,128)(2,1)S(1)} %get-tuple-element.92), channel_id=1, source_target_pairs={{0,16},{16,0},{1,17},{17,1},{2,18},{18,2},{3,19},{19,3},{4,20},{20... | collective-permute-start | bytes 1413128 | tf_op jit(solution)/shard_map/ppermute | solution.py:346
  62.7 3.3 %copy-start.3 = (f32[1,640]{1,0:T(1,128)S(1)}, f32[1,640]{1,0:T(1,128)}, u32[]{:S(2)}) copy-start(f32[1,640]{1,0:T(1,128)} %bias.1) | copy-start | bytes 7684
  66.0 2.9 %collective-permute-start.23 = (f32[3,640]{1,0:T(4,128)S(1)}, f32[3,640]{1,0:T(4,128)S(1)}, u32[]{:S(2)}, u32[]{:S(2)}) collective-permute-start(f32[3,640]{1,0:T(4,128)S(1)} %fusion.2), channel_id=1, source_target_pairs={{0,1},{1,0},{2,3},{3,2},{4,5},{5,4},{6,7},{7,6},{8,9},{9,8},{10,11... | collective-permute-start | bytes 23048 | tf_op jit(solution)/shard_map/ppermute | solution.py:346
  66.1 10.3 %collective-permute-start.16 = (bf16[512,256]{1,0:T(8,128)(2,1)S(1)}, bf16[512,256]{1,0:T(8,128)(2,1)S(1)}, u32[]{:S(2)}, u32[]{:S(2)}) collective-permute-start(bf16[512,256]{1,0:T(8,128)(2,1)S(1)} %shard_map.124), channel_id=1, source_target_pairs={{0,1},{1,0},{2,3},{3,2},{4,5},{5,4},{6,7},{7,6},{8,9},{9,8},{10,11... | collective-permute-start | bytes 786440 | tf_op jit(solution)/shard_map/ppermute | solution.py:346
  66.8 9.5 %collective-permute-start.18 = (bf16[40,2944]{1,0:T(8,128)(2,1)S(1)}, bf16[40,2944]{1,0:T(8,128)(2,1)S(1)}, u32[]{:S(2)}, u32[]{:S(2)}) collective-permute-start(bf16[40,2944]{1,0:T(8,128)(2,1)S(1)} %get-tuple-element.122), channel_id=1, source_target_pairs={{0,4},{4,8},{8,12},{12,14},{14,10},{10,6},{6,2},{2,0},{1,5},{5,9},... | collective-permute-start | bytes 706568 | tf_op jit(solution)/shard_map/ppermute | solution.py:371
  68.1 8.2 %collective-permute-start.20 = (bf16[40,2944]{1,0:T(8,128)(2,1)S(1)}, bf16[40,2944]{1,0:T(8,128)(2,1)S(1)}, u32[]{:S(2)}, u32[]{:S(2)}) collective-permute-start(bf16[40,2944]{1,0:T(8,128)(2,1)S(1)} %get-tuple-element.121), channel_id=1, source_target_pairs={{4,0},{8,4},{12,8},{14,12},{10,14},{6,10},{2,6},{0,2},{5,1},{9,5},... | collective-permute-start | bytes 706568 | tf_op jit(solution)/shard_map/ppermute | solution.py:374
  68.9 3.7 %collective-permute-start.24 = (f32[3,640]{1,0:T(4,128)S(1)}, f32[3,640]{1,0:T(4,128)S(1)}, u32[]{:S(2)}, u32[]{:S(2)}) collective-permute-start(f32[3,640]{1,0:T(4,128)S(1)} %fusion.4), channel_id=1, source_target_pairs={{0,16},{16,0},{1,17},{17,1},{2,18},{18,2},{3,19},{19,3},{4,20},{20... | collective-permute-start | bytes 23048 | tf_op jit(solution)/shard_map/ppermute | solution.py:395
  72.6 3.7 %collective-permute-start.25 = (f32[3,640]{1,0:T(4,128)S(1)}, f32[3,640]{1,0:T(4,128)S(1)}, u32[]{:S(2)}, u32[]{:S(2)}) collective-permute-start(f32[3,640]{1,0:T(4,128)S(1)} %add.97), channel_id=1, source_target_pairs={{0,4},{4,0},{8,12},{12,8},{1,5},{5,1},{9,13},{13,9},{2,6},{6,2},{1... | collective-permute-start | bytes 23048 | tf_op jit(solution)/shard_map/ppermute | solution.py:395
  76.3 1.9 %collective-permute-start.22 = (bf16[512,512]{1,0:T(8,128)(2,1)S(1)}, bf16[512,512]{1,0:T(8,128)(2,1)S(1)}, u32[]{:S(2)}, u32[]{:S(2)}) collective-permute-start(bf16[512,512]{1,0:T(8,128)(2,1)S(1)} %get-tuple-element.103), channel_id=1, source_target_pairs={{0,1},{1,0},{2,3},{3,2},{4,5},{5,4},{6,7},{7,6},{8,9},{9,8},{10,11... | collective-permute-start | bytes 1572872 | tf_op jit(solution)/shard_map/ppermute | solution.py:346
  76.5 8.2 %collective-permute-start.21 = (bf16[40,2944]{1,0:T(8,128)(2,1)S(1)}, bf16[40,2944]{1,0:T(8,128)(2,1)S(1)}, u32[]{:S(2)}, u32[]{:S(2)}) collective-permute-start(bf16[40,2944]{1,0:T(8,128)(2,1)S(1)} %add_convert_fusion.1), channel_id=1, source_target_pairs={{0,4},{4,8},{8,12},{12,14},{14,10},{10,6},{6,2},{2,0},{1,5},{5,9},... | collective-permute-start | bytes 706568 | tf_op jit(solution)/shard_map/ppermute | solution.py:371
  81.9 14.2 %copy-start = (f32[1,40,5760]{2,1,0:T(8,128)S(1)}, f32[1,40,5760]{2,1,0:T(8,128)}, u32[]{:S(2)}) copy-start(f32[1,40,5760]{2,1,0:T(8,128)} %param.10) | copy-start | bytes 2764804
  84.8 9.7 %collective-permute-start.26 = (bf16[40,2944]{1,0:T(8,128)(2,1)S(1)}, bf16[40,2944]{1,0:T(8,128)(2,1)S(1)}, u32[]{:S(2)}, u32[]{:S(2)}) collective-permute-start(bf16[40,2944]{1,0:T(8,128)(2,1)S(1)} %add_convert_fusion), channel_id=1, source_target_pairs={{0,16},{16,0},{1,17},{17,1},{2,18},{18,2},{3,19},{19,3},{4,20},{20... | collective-permute-start | bytes 706568 | tf_op jit(solution)/shard_map/ppermute | solution.py:346
  86.2 3.7 %collective-permute-start.27 = (f32[3,640]{1,0:T(4,128)S(1)}, f32[3,640]{1,0:T(4,128)S(1)}, u32[]{:S(2)}, u32[]{:S(2)}) collective-permute-start(f32[3,640]{1,0:T(4,128)S(1)} %add.98), channel_id=1, source_target_pairs={{0,2},{2,0},{1,3},{3,1},{4,6},{6,4},{5,7},{7,5},{8,10},{10,8},{9,1... | collective-permute-start | bytes 23048 | tf_op jit(solution)/shard_map/ppermute | solution.py:395
  89.9 4.6 %collective-permute-start.28 = (f32[3,640]{1,0:T(4,128)S(1)}, f32[3,640]{1,0:T(4,128)S(1)}, u32[]{:S(2)}, u32[]{:S(2)}) collective-permute-start(f32[3,640]{1,0:T(4,128)S(1)} %add.102), channel_id=1, source_target_pairs={{0,8},{4,12},{8,0},{12,4},{1,9},{5,13},{9,1},{13,5},{2,10},{6,14},... | collective-permute-start | bytes 23048 | tf_op jit(solution)/shard_map/ppermute | solution.py:395
  94.5 1.6 %collective-permute-start.29 = (bf16[40,2944]{1,0:T(8,128)(2,1)S(1)}, bf16[40,2944]{1,0:T(8,128)(2,1)S(1)}, u32[]{:S(2)}, u32[]{:S(2)}) collective-permute-start(bf16[40,2944]{1,0:T(8,128)(2,1)S(1)} %get-tuple-element.129), channel_id=1, source_target_pairs={{0,1},{1,0},{2,3},{3,2},{4,5},{5,4},{6,7},{7,6},{8,9},{9,8},{10,11... | collective-permute-start | bytes 706568 | tf_op jit(solution)/shard_map/ppermute | solution.py:346

commit v18 on v10

--- a/solution.py
+++ b/solution.py
@@ -120,7 +120,7 @@
             cot_t[2 * q * part:(2 * q + 2) * part] = jnp.concatenate(pair).astype(BF16)
 
 
-def grad_kernel(cols, dev, acts, cot_t, *pieces):
+def grad_kernel(cols, carrier, dev, acts, cot_t, theirs, *pieces):
     core = dev[0] % 2
     rows, width, chans = acts.shape[1] - 2, acts.shape[2], acts.shape[3]
     cells = rows * width
@@ -128,9 +128,10 @@
     def emit(window, place, wide):
         value = jnp.dot(cot_t[...], window, preferred_element_type=F32)
         at = 0
-        for piece in pieces:
-            piece[:, pl.ds(place, wide)] = value[at:at + piece.shape[0]].astype(BF16)
-            at += piece.shape[0]
+        for i, piece in enumerate(pieces):
+            count = piece.shape[0] - (theirs.shape[0] if i == carrier else 0)
+            piece[:count, pl.ds(place, wide)] = value[at:at + count].astype(BF16)
+            at += count
 
     def two_taps(k, _):
         taps, place = cols.pair(core, k, chans)
@@ -141,6 +142,8 @@
     lax.fori_loop(0, 2, two_taps, 0)
     place, channel = cols.middle(core, chans)
     emit(acts[1, 1:rows + 1, :, pl.ds(channel, cols.mid)].reshape(cells, cols.mid), place, cols.mid)
+    if carrier is not None:
+        pieces[carrier][-theirs.shape[0]:] = theirs[...]
 
 
 class Stages:
@@ -321,12 +324,13 @@
     sums[1:2] = scale * jnp.sum(shifts, axis=0, keepdims=True)
 
 
-def finish_kernel(cols, dev, step, shard, mine, theirs, ours, aside, out):
+def finish_kernel(cols, dev, step, shard, mine, carried, ours, aside, out):
     lower = dev[0] % 2 == 0
     rate = LR_KERNEL * (1.0 - (step[0] % 1000).astype(F32) / 2000.0)
     factor = 0.5 * cols.total ** (-0.5) * rate
     here = 0.5 * mine[...].astype(F32) - factor * ours[...].astype(F32)
-    there = 0.5 * theirs[...].astype(F32) - factor * aside[...].astype(F32)
+    theirs = carried[-shard.shape[0]:].astype(F32)
+    there = 0.5 * theirs - factor * aside[...].astype(F32)
     left, right = jnp.where(lower, here, there), jnp.where(lower, there, here)
     out[:, :cols.lead] = 0.5 * shard[:, :cols.lead] + left
     out[:, cols.lead:] = 0.5 * shard[:, cols.lead:] + right[:, cols.both:]
@@ -428,7 +432,7 @@
         table = jnp.asarray(ring.table(part))
         order = (ring.count, part, 2 * ring.count)
         up1, down1 = ring.up(unit), ring.down(unit)
-        peer = swap(mine, "replica"), swap(theirs, "replica")
+        peer = swap(mine, "replica")
     else:
         table = jnp.zeros((replicas * zs * 4, 1), jnp.int32)
         order = None
@@ -454,14 +458,14 @@
         [pltpu.VMEM((chans, 2 * cells), F32)],
         8, flops // 4,
     )(dev, table, latent, lat_far, cot_b, cot_far, gn_gain, gn_shift)
-    counts = [zs] + [1] * zs if paired else [2 * zs]
+    counts = [2 * zs, 2, 3] + [2] * (zs - 2) if paired else [4 * zs]
     pieces = call(
-        partial(grad_kernel, cols),
-        [jax.ShapeDtypeStruct((n * 2 * part, cols.lead), BF16) for n in counts],
-        [SMEM_SPEC] + [VMEM_SPEC] * 2,
+        partial(grad_kernel, cols, 2 if paired else None),
+        [jax.ShapeDtypeStruct((n * part, cols.lead), BF16) for n in counts],
+        [SMEM_SPEC] + [VMEM_SPEC] * 3,
         [],
         4, flops // 2,
-    )(dev, acts, cot_t)
+    )(dev, acts, cot_t, theirs)
     stages = Stages([2 * zs - 3, 3] if paired else [1], 2 * part if paired else chans)
     staged = paired
 
@@ -515,7 +519,7 @@
 
     if paired:
         kept, *sent = pieces
-        up, down, sent[0], mine, theirs = tied(up1, down1, sent[0], *peer)
+        up, down, sent[0], mine = tied(up1, down1, sent[0], peer)
         blocks = [unit, up, down]
         crossed = [swap(piece, "replica") for piece in sent]
         up, down = ring.up(up), ring.down(down)
@@ -524,7 +528,7 @@
 
         def ring_step(j, *received):
             parts = kept[2 * j * part:(2 * j + 2) * part], crossed[j]
-            ahead, behind = (tuple(x[half] for x in parts) for half in (slice(part), slice(part, None)))
+            ahead, behind = (tuple(x[at:at + part] for x in parts) for at in (0, part))
             up_sum = ring.up(add(*ahead, *received[:1]))
             if j < zs - 1:
                 return up_sum, ring.down(add(*behind, *received[1:]))
@@ -564,7 +568,7 @@
         new_kernel = call(
             partial(finish_kernel, cols), jax.ShapeDtypeStruct(shard.shape, F32),
             [SMEM_SPEC] * 2 + [VMEM_SPEC] * 5, [], 8, flops // 16,
-        )(dev, step, shard, mine, theirs, ours, aside)
+        )(dev, step, shard, mine, crossed[1], ours, aside)
         vectors = hop(vectors, "y", 1)
         reach = 2
         while reach < zs:

time: 92.5 us -> 93.5 us (1.011)
  waiting for transfers between devices: 20.1 us -> 22 us
  starting transfers between devices: 33.5 us -> 32.5 us
    ppermute x8, starting transfers between devices: 9.16 us -> 13.9 us  [up(): return lax.ppermute(value, NODE, self.ahead)]
    ppermute x7, starting transfers between devices: 7.41 us -> 2.76 us  [down(): return lax.ppermute(value, NODE, self.behind)]
    ppermute x8, waiting for transfers between devices: 7.34 us -> 10.8 us  [up(): return lax.ppermute(value, NODE, self.ahead)]
    ppermute x14 -> x13, waiting for transfers between devices: 2.59 us -> 0.14 us  [swap(): return lax.ppermute(value, axis, [(0, 1), (1, 0)])]
    ppermute x4, starting transfers between devices: 7 us -> 5.4 us  [hop(): lax.ppermute(value, axis, [(s, s ^ mask) for s in range(count)])]
    ppermute x4, waiting for transfers between devices: 5.57 us -> 6.92 us  [hop(): lax.ppermute(value, axis, [(s, s ^ mask) for s in range(count)])]
    ppermute x14 -> x13, starting transfers between devices: 9.92 us -> 10.4 us  [swap(): return lax.ppermute(value, axis, [(0, 1), (1, 0)])]
  transfers between devices with their start and end apart: 33 -> 32, of which waited for: 13 -> 14; matrix products, arithmetic and copies ran while one was open for 4% -> 4% of each run, Pallas kernels for 34% -> 33%
where the time goes in v18:
time: 93.5 us; the launch traced here: 93.3 us
  starting transfers between devices  32.5 us (35%)
  Pallas kernels  32.4 us (35%)
  waiting for transfers between devices  22 us (24%)
  other arithmetic  2.87 us (3%)
  local copies, waits for them, and re-layouts  1.94 us (2%)
  between operations  1.56 us (2%)
    ppermute x8, starting transfers between devices, up(): return lax.ppermute(value, NODE, self.ahead)  13.9 us
    ppermute x8, waiting for transfers between devices, up(): return lax.ppermute(value, NODE, self.ahead)  10.8 us
    ppermute x13, starting transfers between devices, swap(): return lax.ppermute(value, axis, [(0, 1), (1, 0)])  10.4 us
    pallas_call x2, Pallas kernels, back(): call(partial(back_kernel, cols, stages, stage), jax.ShapeDtypeStruct((2,...  8.61 us
    ppermute x4, waiting for transfers between devices, hop(): lax.ppermute(value, axis, [(s, s ^ mask) for s in range(count)])  6.92 us
    ppermute x4, starting transfers between devices, hop(): lax.ppermute(value, axis, [(s, s ^ mask) for s in range(count)])  5.4 us
    pallas_call x1, Pallas kernels, per_device(): call(partial(grad_kernel, cols, 2 if paired else None), [jax.ShapeDtypeSt...  4.63 us
    pallas_call x1, Pallas kernels, slopes_of(): call(partial(slope_kernel, stages), (jax.ShapeDtypeStruct((3, 2 * half +...  4.48 us
  transfers between devices with their start and end apart: 32, of which 14 were waited for; matrix products, arithmetic and copies ran while one was open for 4% of the time, Pallas kernels for 33%

profile of v18, /device:TPU:0, one launch (start us, length us, event | category | flops | bytes accessed | tf_op | source)
XLA Modules:
  0.0 93.3 jit_solution(13398865141887128860)
XLA Ops:
  0.7 1.3 %fusion.1 = (bf16[40,2944]{1,0:T(8,128)(2,1)S(1)}, bf16[40,2944]{1,0:T(8,128)(2,1)S(1)}) fusion(f32[1,40,5760]{2,1,0:T(8,128)} %param.10, s32[]{:T(128)S(6)} %select_n.28, s32[]{:T(128)S(6)} %select_n.26), kind=kLoop, calls=%fused_computation.13 | loop fusion | bytes 942088 | tf_op jit(solution)/shard_map/convert_element_type | solution.py:423
  2.0 0.5 collective-permute-start.4
  2.5 2.0 %fusion.3 = (f32[640]{0:T(1024)S(1)}, bf16[16,32,640]{2,1,0:T(8,128)(2,1)S(1)}) fusion(f32[1,16,32,640]{3,2,1,0:T(8,128)} %param.9), kind=kLoop, calls=%fused_computation.20 | loop fusion | flops 654720 | bytes 1968640 | tf_op jit(solution)/shard_map/reduce_sum | solution.py:516
  4.6 0.5 collective-permute-start
  5.1 2.7 %collective-permute-start.5 = (bf16[80,2944]{1,0:T(8,128)(2,1)S(1)}, bf16[80,2944]{1,0:T(8,128)(2,1)S(1)}, u32[]{:S(2)}, u32[]{:S(2)}) collective-permute-start(bf16[80,2944]{1,0:T(8,128)(2,1)S(1)} %maximum_select_fusion.refs_0_), channel_id=1, source_target_pairs={{0,4},{4,8},{8,12},{12,14},{14,10},{10,6},{6,2},{2,0},{1,5},{5,9},... | collective-permute-start | bytes 1413128 | tf_op jit(solution)/shard_map/ppermute | solution.py:368
  7.8 1.9 %collective-permute-start.7 = (bf16[40,2944]{1,0:T(8,128)(2,1)S(1)}, bf16[40,2944]{1,0:T(8,128)(2,1)S(1)}, u32[]{:S(2)}, u32[]{:S(2)}) collective-permute-start(bf16[40,2944]{1,0:T(8,128)(2,1)S(1)} %get-tuple-element.117), channel_id=1, source_target_pairs={{0,16},{16,0},{1,17},{17,1},{2,18},{18,2},{3,19},{19,3},{4,20},{20... | collective-permute-start | bytes 706568 | tf_op jit(solution)/shard_map/ppermute | solution.py:343
  9.8 4.4 %shard_map.119 = (f32[2,640]{1,0:T(2,128)S(1)}, bf16[3,34,32,640]{3,2,1,0:T(8,128)(2,1)S(1)}, bf16[640,1024]{1,0:T(8,128)(2,1)S(1)}) custom-call(s32[1]{0:T(128)} %bitcast.dev, s32[32,24]{1,0:T(8,128)S(1)} %copy-done.5, bf16[16,32,640]{2,1,0:T(8,128)(2,1)S(1)} %bitcast.13, bf16[16,32,640]{2,1,0:T(8,128)(2,1)S(1)} %collective-permute-done.lat_far, ...), custom_call_target="tpu_custom_call" | custom-call | flops 964689920 | tf_op jit(solution)/shard_map/pallas_call | solution.py:454
  14.2 4.6 %shard_map.120 = (bf16[320,2944]{1,0:T(8,128)(2,1)S(1)}, bf16[80,2944]{1,0:T(8,128)(2,1)S(1)}, bf16[120,2944]{1,0:T(8,128)(2,1)S(1)}, bf16[80,2944]{1,0:T(8,128)(2,1)S(1)}, bf16[80,2944]{1,0:T(8,128)(2,1)S(1)}) custom-call(s32[1]{0:T(128)} %bitcast.dev, bf16[3,34,32,640]{3,2,1,0:T(8,128)(2,1)S(1)} %get-tuple-element.93.acts, ...), custom_call_target="tpu_custom_call" | custom-call | flops 1929379840 | tf_op jit(solution)/shard_map/pallas_call | solution.py:462
  19.1 1.5 %collective-permute-done.6.refs_2_ = bf16[80,2944]{1,0:T(8,128)(2,1)S(1)} collective-permute-done((bf16[80,2944]{1,0:T(8,128)(2,1)S(1)}, bf16[80,2944]{1,0:T(8,128)(2,1)S(1)}, u32[]{:S(2)}, u32[]{:S(2)}) %collective-permute-start.6) | collective-permute-done | bytes 471072 | tf_op jit(solution)/shard_map/ppermute | solution.py:371
  20.7 1.6 %collective-permute-start.8 = (bf16[80,2944]{1,0:T(8,128)(2,1)S(1)}, bf16[80,2944]{1,0:T(8,128)(2,1)S(1)}, u32[]{:S(2)}, u32[]{:S(2)}) collective-permute-start(bf16[80,2944]{1,0:T(8,128)(2,1)S(1)} %collective-permute-done.5.refs_1_), channel_id=1, source_target_pairs={{0,4},{4,8},{8,12},{12,14},{14,10},{10,6},{6,2},{2,0},{1,5},{5,9},... | collective-permute-start | bytes 1413128 | tf_op jit(solution)/shard_map/ppermute | solution.py:368
  22.7 1.5 %collective-permute-start.10 = (bf16[80,2944]{1,0:T(8,128)(2,1)S(1)}, bf16[80,2944]{1,0:T(8,128)(2,1)S(1)}, u32[]{:S(2)}, u32[]{:S(2)}) collective-permute-start(bf16[80,2944]{1,0:T(8,128)(2,1)S(1)} %get-tuple-element.74), channel_id=1, source_target_pairs={{0,16},{16,0},{1,17},{17,1},{2,18},{18,2},{3,19},{19,3},{4,20},{20... | collective-permute-start | bytes 1413128 | tf_op jit(solution)/shard_map/ppermute | solution.py:343
  24.2 0.5 collective-permute-start.13
  24.7 4.5 %shard_map.121 = (bf16[3,34,32,768]{3,2,1,0:T(8,128)(2,1)S(1)}, bf16[32,32,640]{2,1,0:T(8,128)(2,1)S(1)}, bf16[32,32,640]{2,1,0:T(8,128)(2,1)S(1)}, bf16[640,768]{1,0:T(8,128)(2,1)S(1)}) custom-call(s32[1]{0:T(128)} %bitcast.dev, s32[32,24]{1,0:T(8,128)S(1)} %copy-done.5, f32[2,640]{1,0:T(2,128)S(1)} %get-tuple-element.68.stats, f32[1,640]{1,0:T(1,128)S(1)} %copy-done.3, ...), custom_call_target="tpu_custom_call" | custom-call | flops 964689920 | tf_op jit(solution)/shard_map/pallas_call | solution.py:474
  29.2 3.5 %collective-permute-done.8.refs_3_ = bf16[80,2944]{1,0:T(8,128)(2,1)S(1)} collective-permute-done((bf16[80,2944]{1,0:T(8,128)(2,1)S(1)}, bf16[80,2944]{1,0:T(8,128)(2,1)S(1)}, u32[]{:S(2)}, u32[]{:S(2)}) %collective-permute-start.8) | collective-permute-done | bytes 471072 | tf_op jit(solution)/shard_map/ppermute | solution.py:368
  32.7 1.3 %collective-permute-done.9.refs_4_ = bf16[80,2944]{1,0:T(8,128)(2,1)S(1)} collective-permute-done((bf16[80,2944]{1,0:T(8,128)(2,1)S(1)}, bf16[80,2944]{1,0:T(8,128)(2,1)S(1)}, u32[]{:S(2)}, u32[]{:S(2)}) %collective-permute-start.9) | collective-permute-done | bytes 471072 | tf_op jit(solution)/shard_map/ppermute | solution.py:371
  34.0 1.6 %collective-permute-start.11 = (bf16[80,2944]{1,0:T(8,128)(2,1)S(1)}, bf16[80,2944]{1,0:T(8,128)(2,1)S(1)}, u32[]{:S(2)}, u32[]{:S(2)}) collective-permute-start(bf16[80,2944]{1,0:T(8,128)(2,1)S(1)} %collective-permute-done.8.refs_3_), channel_id=1, source_target_pairs={{0,4},{4,8},{8,12},{12,14},{14,10},{10,6},{6,2},{2,0},{1,5},{5,9},... | collective-permute-start | bytes 1413128 | tf_op jit(solution)/shard_map/ppermute | solution.py:368
  35.6 0.4 collective-permute-start.12
  36.0 4.0 %shard_map.122 = (f32[512,512]{1,0:T(8,128)S(1)}, bf16[512,512]{1,0:T(8,128)(2,1)S(1)}) custom-call(s32[1]{0:T(128)} %bitcast.dev, bf16[3,34,32,640]{3,2,1,0:T(8,128)(2,1)S(1)} %get-tuple-element.93.acts, bf16[80,2944]{1,0:T(8,128)(2,1)S(1)} %maximum_select_fusion.refs_0_, bf16[80,2944]{1,0:T(8,128)(2,1)S(1)} %collective-permute-done.5.refs_1_, ...), custom_call_target="tpu_custom_call" | custom-call | flops 964689920 | tf_op jit(solution)/shard_map/pallas_call | solution.py:492
  40.1 1.6 %collective-permute-start.16 = (bf16[40,2944]{1,0:T(8,128)(2,1)S(1)}, bf16[40,2944]{1,0:T(8,128)(2,1)S(1)}, u32[]{:S(2)}, u32[]{:S(2)}) collective-permute-start(bf16[40,2944]{1,0:T(8,128)(2,1)S(1)} %get-tuple-element.114), channel_id=1, source_target_pairs={{0,4},{4,8},{8,12},{12,14},{14,10},{10,6},{6,2},{2,0},{1,5},{5,9},... | collective-permute-start | bytes 706568 | tf_op jit(solution)/shard_map/ppermute | solution.py:368
  41.8 0.5 collective-permute-start.17
  42.2 5.4 %shard_map.123 = f32[2,640]{1,0:T(2,128)S(1)} custom-call(s32[1]{0:T(128)} %bitcast.dev, bf16[3,34,32,768]{3,2,1,0:T(8,128)(2,1)S(1)} %get-tuple-element.79.cots, bf16[32,32,640]{2,1,0:T(8,128)(2,1)S(1)} %get-tuple-element.80.slope, bf16[32,32,640]{2,1,0:T(8,128)(2,1)S(1)} %get-tuple-element.81.slope_x, bf16[80,2944]{1,0:T(8,128)(2,1)S(1)} %maximum_select_fusion.refs_0_, ...), custom_call_target="tpu_custom_call" | custom-call | flops 964689920 | tf_op jit(solution)/shard_map/pallas_call | solution.py:484
  47.6 2.2 %collective-permute-done.16 = bf16[40,2944]{1,0:T(8,128)(2,1)S(1)} collective-permute-done((bf16[40,2944]{1,0:T(8,128)(2,1)S(1)}, bf16[40,2944]{1,0:T(8,128)(2,1)S(1)}, u32[]{:S(2)}, u32[]{:S(2)}) %collective-permute-start.16) | collective-permute-done | bytes 235552 | tf_op jit(solution)/shard_map/ppermute | solution.py:368
  49.9 1.5 %collective-permute-start.3 = (bf16[80,2944]{1,0:T(8,128)(2,1)S(1)}, bf16[80,2944]{1,0:T(8,128)(2,1)S(1)}, u32[]{:S(2)}, u32[]{:S(2)}) collective-permute-start(bf16[80,2944]{1,0:T(8,128)(2,1)S(1)} %get-tuple-element.63), channel_id=1, source_target_pairs={{0,16},{16,0},{1,17},{17,1},{2,18},{18,2},{3,19},{19,3},{4,20},{20... | collective-permute-start | bytes 1413128 | tf_op jit(solution)/shard_map/ppermute | solution.py:343
  51.4 1.6 %collective-permute-start.14 = (bf16[40,2944]{1,0:T(8,128)(2,1)S(1)}, bf16[40,2944]{1,0:T(8,128)(2,1)S(1)}, u32[]{:S(2)}, u32[]{:S(2)}) collective-permute-start(bf16[40,2944]{1,0:T(8,128)(2,1)S(1)} %slice.76), channel_id=1, source_target_pairs={{0,4},{4,8},{8,12},{12,14},{14,10},{10,6},{6,2},{2,0},{1,5},{5,9},... | collective-permute-start | bytes 706568 | tf_op jit(solution)/shard_map/ppermute | solution.py:368
  53.0 0.5 collective-permute-start.15
  53.7 1.6 %collective-permute-start.18 = (bf16[40,2944]{1,0:T(8,128)(2,1)S(1)}, bf16[40,2944]{1,0:T(8,128)(2,1)S(1)}, u32[]{:S(2)}, u32[]{:S(2)}) collective-permute-start(bf16[40,2944]{1,0:T(8,128)(2,1)S(1)} %get-tuple-element.110), channel_id=1, source_target_pairs={{0,4},{4,8},{8,12},{12,14},{14,10},{10,6},{6,2},{2,0},{1,5},{5,9},... | collective-permute-start | bytes 706568 | tf_op jit(solution)/shard_map/ppermute | solution.py:368
  55.4 0.5 collective-permute-start.19
  55.8 2.7 %collective-permute-done.14.refs_2_.refs_5_ = bf16[40,2944]{1,0:T(8,128)(2,1)S(1)} collective-permute-done((bf16[40,2944]{1,0:T(8,128)(2,1)S(1)}, bf16[40,2944]{1,0:T(8,128)(2,1)S(1)}, u32[]{:S(2)}, u32[]{:S(2)}) %collective-permute-start.14) | collective-permute-done | bytes 235552 | tf_op jit(solution)/shard_map/ppermute | solution.py:368
  58.5 1.3 %collective-permute-start.2 = (bf16[80,2944]{1,0:T(8,128)(2,1)S(1)}, bf16[80,2944]{1,0:T(8,128)(2,1)S(1)}, u32[]{:S(2)}, u32[]{:S(2)}) collective-permute-start(bf16[80,2944]{1,0:T(8,128)(2,1)S(1)} %get-tuple-element.62), channel_id=1, source_target_pairs={{0,16},{16,0},{1,17},{17,1},{2,18},{18,2},{3,19},{19,3},{4,20},{20... | collective-permute-start | bytes 1413128 | tf_op jit(solution)/shard_map/ppermute | solution.py:343
  59.9 3.2 %shard_map.124 = f32[2,640]{1,0:T(2,128)S(1)} custom-call(s32[1]{0:T(128)} %bitcast.dev, bf16[3,34,32,768]{3,2,1,0:T(8,128)(2,1)S(1)} %get-tuple-element.79.cots, bf16[32,32,640]{2,1,0:T(8,128)(2,1)S(1)} %get-tuple-element.80.slope, bf16[32,32,640]{2,1,0:T(8,128)(2,1)S(1)} %get-tuple-element.81.slope_x, ...), custom_call_target="tpu_custom_call" | custom-call | flops 964689920 | tf_op jit(solution)/shard_map/pallas_call | solution.py:484
  63.4 1.4 %shard_map.125 = bf16[512,256]{1,0:T(8,128)(2,1)S(1)} custom-call(s32[1]{0:T(128)} %bitcast.dev, bf16[3,34,32,640]{3,2,1,0:T(8,128)(2,1)S(1)} %get-tuple-element.93.acts, bf16[80,2944]{1,0:T(8,128)(2,1)S(1)} %collective-permute-done.11.refs_0_.refs_3_, bf16[80,2944]{1,0:T(8,128)(2,1)S(1)} %collective-permute-done.12.refs_1_.refs_4_, ...), custom_call_target="tpu_custom_call" | custom-call | flops 482344960 | tf_op jit(solution)/shard_map/pallas_call | solution.py:501
  64.8 0.6 collective-permute-start.20
  65.6 1.6 %collective-permute-start.23 = (bf16[40,2944]{1,0:T(8,128)(2,1)S(1)}, bf16[40,2944]{1,0:T(8,128)(2,1)S(1)}, u32[]{:S(2)}, u32[]{:S(2)}) collective-permute-start(bf16[40,2944]{1,0:T(8,128)(2,1)S(1)} %get-tuple-element.112), channel_id=1, source_target_pairs={{0,4},{4,8},{8,12},{12,14},{14,10},{10,6},{6,2},{2,0},{1,5},{5,9},... | collective-permute-start | bytes 706568 | tf_op jit(solution)/shard_map/ppermute | solution.py:368
  67.2 0.4 collective-permute-start.24
  67.7 1.9 %collective-permute-start.22 = (f32[3,640]{1,0:T(4,128)S(1)}, f32[3,640]{1,0:T(4,128)S(1)}, u32[]{:S(2)}, u32[]{:S(2)}) collective-permute-start(f32[3,640]{1,0:T(4,128)S(1)} %fusion.5), channel_id=1, source_target_pairs={{0,16},{16,0},{1,17},{17,1},{2,18},{18,2},{3,19},{19,3},{4,20},{20... | collective-permute-start | bytes 23048 | tf_op jit(solution)/shard_map/ppermute | solution.py:392
  69.6 1.8 %collective-permute-done.22 = f32[3,640]{1,0:T(4,128)S(1)} collective-permute-done((f32[3,640]{1,0:T(4,128)S(1)}, f32[3,640]{1,0:T(4,128)S(1)}, u32[]{:S(2)}, u32[]{:S(2)}) %collective-permute-start.22) | collective-permute-done | bytes 7712 | tf_op jit(solution)/shard_map/ppermute | solution.py:392
  71.4 1.8 %collective-permute-done.23 = bf16[40,2944]{1,0:T(8,128)(2,1)S(1)} collective-permute-done((bf16[40,2944]{1,0:T(8,128)(2,1)S(1)}, bf16[40,2944]{1,0:T(8,128)(2,1)S(1)}, u32[]{:S(2)}, u32[]{:S(2)}) %collective-permute-start.23) | collective-permute-done | bytes 235552 | tf_op jit(solution)/shard_map/ppermute | solution.py:368
  73.3 1.3 %collective-permute-done.24 = bf16[40,2944]{1,0:T(8,128)(2,1)S(1)} collective-permute-done((bf16[40,2944]{1,0:T(8,128)(2,1)S(1)}, bf16[40,2944]{1,0:T(8,128)(2,1)S(1)}, u32[]{:S(2)}, u32[]{:S(2)}) %collective-permute-start.24) | collective-permute-done | bytes 235552 | tf_op jit(solution)/shard_map/ppermute | solution.py:371
  74.7 1.6 %collective-permute-start.25 = (bf16[40,2944]{1,0:T(8,128)(2,1)S(1)}, bf16[40,2944]{1,0:T(8,128)(2,1)S(1)}, u32[]{:S(2)}, u32[]{:S(2)}) collective-permute-start(bf16[40,2944]{1,0:T(8,128)(2,1)S(1)} %add_convert_fusion.1), channel_id=1, source_target_pairs={{0,4},{4,8},{8,12},{12,14},{14,10},{10,6},{6,2},{2,0},{1,5},{5,9},... | collective-permute-start | bytes 706568 | tf_op jit(solution)/shard_map/ppermute | solution.py:368
  76.2 1.1 %collective-permute-start.27 = (f32[3,640]{1,0:T(4,128)S(1)}, f32[3,640]{1,0:T(4,128)S(1)}, u32[]{:S(2)}, u32[]{:S(2)}) collective-permute-start(f32[3,640]{1,0:T(4,128)S(1)} %add.91), channel_id=1, source_target_pairs={{0,4},{4,0},{8,12},{12,8},{1,5},{5,1},{9,13},{13,9},{2,6},{6,2},{1... | collective-permute-start | bytes 23048 | tf_op jit(solution)/shard_map/ppermute | solution.py:392
  77.4 3.7 %shard_map.126 = bf16[16,32,640]{2,1,0:T(8,128)(2,1)} custom-call(s32[1]{0:T(128)} %bitcast.dev, bf16[3,34,32,640]{3,2,1,0:T(8,128)(2,1)S(1)} %get-tuple-element.93.acts, bf16[512,256]{1,0:T(8,128)(2,1)S(1)} %collective-permute-done.20.got, bf16[16,32,640]{2,1,0:T(8,128)(2,1)S(1)} %bitcast.15, f32[1,640]{1,0:T(1,128)S(1)} %copy-done.2, ...), custom_call_target="tpu_custom_call" | custom-call | flops 964689920 | tf_op jit(solution)/shard_map/pallas_call | solution.py:509
  81.3 1.9 %collective-permute-start.28 = (bf16[40,2944]{1,0:T(8,128)(2,1)S(1)}, bf16[40,2944]{1,0:T(8,128)(2,1)S(1)}, u32[]{:S(2)}, u32[]{:S(2)}) collective-permute-start(bf16[40,2944]{1,0:T(8,128)(2,1)S(1)} %add_convert_fusion), channel_id=1, source_target_pairs={{0,16},{16,0},{1,17},{17,1},{2,18},{18,2},{3,19},{19,3},{4,20},{20... | collective-permute-start | bytes 706568 | tf_op jit(solution)/shard_map/ppermute | solution.py:343
  83.3 0.7 collective-permute-start.30
  84.6 2.3 %collective-permute-done.30 = f32[3,640]{1,0:T(4,128)S(1)} collective-permute-done((f32[3,640]{1,0:T(4,128)S(1)}, f32[3,640]{1,0:T(4,128)S(1)}, u32[]{:S(2)}, u32[]{:S(2)}) %collective-permute-start.30) | collective-permute-done | bytes 7712 | tf_op jit(solution)/shard_map/ppermute | solution.py:392
  86.9 1.7 %collective-permute-start.31 = (f32[3,640]{1,0:T(4,128)S(1)}, f32[3,640]{1,0:T(4,128)S(1)}, u32[]{:S(2)}, u32[]{:S(2)}) collective-permute-start(f32[3,640]{1,0:T(4,128)S(1)} %add.102), channel_id=1, source_target_pairs={{0,8},{4,12},{8,0},{12,4},{1,9},{5,13},{9,1},{13,5},{2,10},{6,14},... | collective-permute-start | bytes 23048 | tf_op jit(solution)/shard_map/ppermute | solution.py:392
  88.8 2.7 %collective-permute-done.31 = f32[3,640]{1,0:T(4,128)S(1)} collective-permute-done((f32[3,640]{1,0:T(4,128)S(1)}, f32[3,640]{1,0:T(4,128)S(1)}, u32[]{:S(2)}, u32[]{:S(2)}) %collective-permute-start.31) | collective-permute-done | bytes 7712 | tf_op jit(solution)/shard_map/ppermute | solution.py:392
  91.5 0.6 fusion.4
  92.1 1.2 %shard_map.127 = f32[40,5760]{1,0:T(8,128)} custom-call(s32[1]{0:T(128)} %bitcast.dev, s32[1]{0:T(128)S(6)} %copy.13.step, f32[40,5760]{1,0:T(8,128)S(1)} %bitcast.11, bf16[40,2944]{1,0:T(8,128)(2,1)S(1)} %collective-permute-done.7.mine, bf16[120,2944]{1,0:T(8,128)(2,1)S(1)} %collective-permute-done.13.carried, ...), custom_call_target="tpu_custom_call" | custom-call | flops 241172480 | tf_op jit(solution)/shard_map/pallas_call | solution.py:568
  (57 shorter events, 2.4 us)
Async XLA Ops:
  0.6 3.9 %copy-start.1 = (bf16[1,16,32,640]{3,2,1,0:T(8,128)(2,1)S(1)}, bf16[1,16,32,640]{3,2,1,0:T(8,128)(2,1)}, u32[]{:S(2)}) copy-start(bf16[1,16,32,640]{3,2,1,0:T(8,128)(2,1)} %param.8) | copy-start | bytes 1966084
  0.7 9.1 %copy-start.3 = (f32[1,640]{1,0:T(1,128)S(1)}, f32[1,640]{1,0:T(1,128)}, u32[]{:S(2)}) copy-start(f32[1,640]{1,0:T(1,128)} %gain.3) | copy-start | bytes 7684
  0.7 9.1 %copy-start.4 = (f32[1,640]{1,0:T(1,128)S(1)}, f32[1,640]{1,0:T(1,128)}, u32[]{:S(2)}) copy-start(f32[1,640]{1,0:T(1,128)} %shift.3) | copy-start | bytes 7684
  0.7 9.1 %copy-start.5 = (s32[32,24]{1,0:T(8,128)S(1)}, s32[32,24]{1,0:T(8,128)}, u32[]{:S(2)}) copy-start(s32[32,24]{1,0:T(8,128)} %constant.40.clone.table) | copy-start | bytes 9220
  2.0 3.1 %collective-permute-start.4 = (bf16[40,2944]{1,0:T(8,128)(2,1)S(1)}, bf16[40,2944]{1,0:T(8,128)(2,1)S(1)}, u32[]{:S(2)}, u32[]{:S(2)}) collective-permute-start(bf16[40,2944]{1,0:T(8,128)(2,1)S(1)} %get-tuple-element.118.theirs), channel_id=1, source_target_pairs={{0,1},{1,0},{2,3},{3,2},{4,5},{5,4},{6,7},{7,6},{8,9},{9,8},{10,11... | collective-permute-start | bytes 706568 | tf_op jit(solution)/shard_map/ppermute | solution.py:343
  4.5 5.3 %collective-permute-start.1 = (bf16[16,32,640]{2,1,0:T(8,128)(2,1)S(1)}, bf16[16,32,640]{2,1,0:T(8,128)(2,1)S(1)}, u32[]{:S(2)}, u32[]{:S(2)}) collective-permute-start(bf16[16,32,640]{2,1,0:T(8,128)(2,1)S(1)} %get-tuple-element.116.cot_own), channel_id=1, source_target_pairs={{0,1},{1,0},{2,3},{3,2},{4,5},{5,4},{6,7},{7,6},{8,9},{9,8},{10,11... | collective-permute-start | bytes 1966088 | tf_op jit(solution)/shard_map/ppermute | solution.py:343
  4.6 5.2 %collective-permute-start = (bf16[16,32,640]{2,1,0:T(8,128)(2,1)S(1)}, bf16[16,32,640]{2,1,0:T(8,128)(2,1)S(1)}, u32[]{:S(2)}, u32[]{:S(2)}) collective-permute-start(bf16[16,32,640]{2,1,0:T(8,128)(2,1)S(1)} %bitcast.12), channel_id=1, source_target_pairs={{0,1},{1,0},{2,3},{3,2},{4,5},{5,4},{6,7},{7,6},{8,9},{9,8},{10,11... | collective-permute-start | bytes 1966088 | tf_op jit(solution)/shard_map/ppermute | solution.py:343
  5.1 14.0 %collective-permute-start.5 = (bf16[80,2944]{1,0:T(8,128)(2,1)S(1)}, bf16[80,2944]{1,0:T(8,128)(2,1)S(1)}, u32[]{:S(2)}, u32[]{:S(2)}) collective-permute-start(bf16[80,2944]{1,0:T(8,128)(2,1)S(1)} %maximum_select_fusion.refs_0_), channel_id=1, source_target_pairs={{0,4},{4,8},{8,12},{12,14},{14,10},{10,6},{6,2},{2,0},{1,5},{5,9},... | collective-permute-start | bytes 1413128 | tf_op jit(solution)/shard_map/ppermute | solution.py:368
  7.8 12.8 %collective-permute-start.6 = (bf16[80,2944]{1,0:T(8,128)(2,1)S(1)}, bf16[80,2944]{1,0:T(8,128)(2,1)S(1)}, u32[]{:S(2)}, u32[]{:S(2)}) collective-permute-start(bf16[80,2944]{1,0:T(8,128)(2,1)S(1)} %maximum_select_fusion.refs_0_), channel_id=1, source_target_pairs={{4,0},{8,4},{12,8},{14,12},{10,14},{6,10},{2,6},{0,2},{5,1},{9,5},... | collective-permute-start | bytes 1413128 | tf_op jit(solution)/shard_map/ppermute | solution.py:371
  7.8 11.0 %collective-permute-start.7 = (bf16[40,2944]{1,0:T(8,128)(2,1)S(1)}, bf16[40,2944]{1,0:T(8,128)(2,1)S(1)}, u32[]{:S(2)}, u32[]{:S(2)}) collective-permute-start(bf16[40,2944]{1,0:T(8,128)(2,1)S(1)} %get-tuple-element.117), channel_id=1, source_target_pairs={{0,16},{16,0},{1,17},{17,1},{2,18},{18,2},{3,19},{19,3},{4,20},{20... | collective-permute-start | bytes 706568 | tf_op jit(solution)/shard_map/ppermute | solution.py:343
  20.7 12.0 %collective-permute-start.8 = (bf16[80,2944]{1,0:T(8,128)(2,1)S(1)}, bf16[80,2944]{1,0:T(8,128)(2,1)S(1)}, u32[]{:S(2)}, u32[]{:S(2)}) collective-permute-start(bf16[80,2944]{1,0:T(8,128)(2,1)S(1)} %collective-permute-done.5.refs_1_), channel_id=1, source_target_pairs={{0,4},{4,8},{8,12},{12,14},{14,10},{10,6},{6,2},{2,0},{1,5},{5,9},... | collective-permute-start | bytes 1413128 | tf_op jit(solution)/shard_map/ppermute | solution.py:368
  22.3 11.7 %collective-permute-start.9 = (bf16[80,2944]{1,0:T(8,128)(2,1)S(1)}, bf16[80,2944]{1,0:T(8,128)(2,1)S(1)}, u32[]{:S(2)}, u32[]{:S(2)}) collective-permute-start(bf16[80,2944]{1,0:T(8,128)(2,1)S(1)} %collective-permute-done.6.refs_2_), channel_id=1, source_target_pairs={{4,0},{8,4},{12,8},{14,12},{10,14},{6,10},{2,6},{0,2},{5,1},{9,5},... | collective-permute-start | bytes 1413128 | tf_op jit(solution)/shard_map/ppermute | solution.py:371
  22.7 17.3 %collective-permute-start.10 = (bf16[80,2944]{1,0:T(8,128)(2,1)S(1)}, bf16[80,2944]{1,0:T(8,128)(2,1)S(1)}, u32[]{:S(2)}, u32[]{:S(2)}) collective-permute-start(bf16[80,2944]{1,0:T(8,128)(2,1)S(1)} %get-tuple-element.74), channel_id=1, source_target_pairs={{0,16},{16,0},{1,17},{17,1},{2,18},{18,2},{3,19},{19,3},{4,20},{20... | collective-permute-start | bytes 1413128 | tf_op jit(solution)/shard_map/ppermute | solution.py:343
  24.2 27.2 %collective-permute-start.13 = (bf16[120,2944]{1,0:T(8,128)(2,1)S(1)}, bf16[120,2944]{1,0:T(8,128)(2,1)S(1)}, u32[]{:S(2)}, u32[]{:S(2)}) collective-permute-start(bf16[120,2944]{1,0:T(8,128)(2,1)S(1)} %get-tuple-element.82), channel_id=1, source_target_pairs={{0,16},{16,0},{1,17},{17,1},{2,18},{18,2},{3,19},{19,3},{4,20},{20... | collective-permute-start | bytes 2119688 | tf_op jit(solution)/shard_map/ppermute | solution.py:343
  34.0 17.4 %collective-permute-start.11 = (bf16[80,2944]{1,0:T(8,128)(2,1)S(1)}, bf16[80,2944]{1,0:T(8,128)(2,1)S(1)}, u32[]{:S(2)}, u32[]{:S(2)}) collective-permute-start(bf16[80,2944]{1,0:T(8,128)(2,1)S(1)} %collective-permute-done.8.refs_3_), channel_id=1, source_target_pairs={{0,4},{4,8},{8,12},{12,14},{14,10},{10,6},{6,2},{2,0},{1,5},{5,9},... | collective-permute-start | bytes 1413128 | tf_op jit(solution)/shard_map/ppermute | solution.py:368
  35.6 15.8 %collective-permute-start.12 = (bf16[80,2944]{1,0:T(8,128)(2,1)S(1)}, bf16[80,2944]{1,0:T(8,128)(2,1)S(1)}, u32[]{:S(2)}, u32[]{:S(2)}) collective-permute-start(bf16[80,2944]{1,0:T(8,128)(2,1)S(1)} %collective-permute-done.9.refs_4_), channel_id=1, source_target_pairs={{4,0},{8,4},{12,8},{14,12},{10,14},{6,10},{2,6},{0,2},{5,1},{9,5},... | collective-permute-start | bytes 1413128 | tf_op jit(solution)/shard_map/ppermute | solution.py:371
  40.1 9.7 %collective-permute-start.16 = (bf16[40,2944]{1,0:T(8,128)(2,1)S(1)}, bf16[40,2944]{1,0:T(8,128)(2,1)S(1)}, u32[]{:S(2)}, u32[]{:S(2)}) collective-permute-start(bf16[40,2944]{1,0:T(8,128)(2,1)S(1)} %get-tuple-element.114), channel_id=1, source_target_pairs={{0,4},{4,8},{8,12},{12,14},{14,10},{10,6},{6,2},{2,0},{1,5},{5,9},... | collective-permute-start | bytes 706568 | tf_op jit(solution)/shard_map/ppermute | solution.py:368
  41.8 9.6 %collective-permute-start.17 = (bf16[40,2944]{1,0:T(8,128)(2,1)S(1)}, bf16[40,2944]{1,0:T(8,128)(2,1)S(1)}, u32[]{:S(2)}, u32[]{:S(2)}) collective-permute-start(bf16[40,2944]{1,0:T(8,128)(2,1)S(1)} %get-tuple-element.113), channel_id=1, source_target_pairs={{4,0},{8,4},{12,8},{14,12},{10,14},{6,10},{2,6},{0,2},{5,1},{9,5},... | collective-permute-start | bytes 706568 | tf_op jit(solution)/shard_map/ppermute | solution.py:371
  49.9 13.4 %collective-permute-start.3 = (bf16[80,2944]{1,0:T(8,128)(2,1)S(1)}, bf16[80,2944]{1,0:T(8,128)(2,1)S(1)}, u32[]{:S(2)}, u32[]{:S(2)}) collective-permute-start(bf16[80,2944]{1,0:T(8,128)(2,1)S(1)} %get-tuple-element.63), channel_id=1, source_target_pairs={{0,16},{16,0},{1,17},{17,1},{2,18},{18,2},{3,19},{19,3},{4,20},{20... | collective-permute-start | bytes 1413128 | tf_op jit(solution)/shard_map/ppermute | solution.py:343
  51.4 7.1 %collective-permute-start.14 = (bf16[40,2944]{1,0:T(8,128)(2,1)S(1)}, bf16[40,2944]{1,0:T(8,128)(2,1)S(1)}, u32[]{:S(2)}, u32[]{:S(2)}) collective-permute-start(bf16[40,2944]{1,0:T(8,128)(2,1)S(1)} %slice.76), channel_id=1, source_target_pairs={{0,4},{4,8},{8,12},{12,14},{14,10},{10,6},{6,2},{2,0},{1,5},{5,9},... | collective-permute-start | bytes 706568 | tf_op jit(solution)/shard_map/ppermute | solution.py:368
  53.0 6.9 %collective-permute-start.15 = (bf16[40,2944]{1,0:T(8,128)(2,1)S(1)}, bf16[40,2944]{1,0:T(8,128)(2,1)S(1)}, u32[]{:S(2)}, u32[]{:S(2)}) collective-permute-start(bf16[40,2944]{1,0:T(8,128)(2,1)S(1)} %slice.77), channel_id=1, source_target_pairs={{4,0},{8,4},{12,8},{14,12},{10,14},{6,10},{2,6},{0,2},{5,1},{9,5},... | collective-permute-start | bytes 706568 | tf_op jit(solution)/shard_map/ppermute | solution.py:371
  53.7 9.5 %collective-permute-start.18 = (bf16[40,2944]{1,0:T(8,128)(2,1)S(1)}, bf16[40,2944]{1,0:T(8,128)(2,1)S(1)}, u32[]{:S(2)}, u32[]{:S(2)}) collective-permute-start(bf16[40,2944]{1,0:T(8,128)(2,1)S(1)} %get-tuple-element.110), channel_id=1, source_target_pairs={{0,4},{4,8},{8,12},{12,14},{14,10},{10,6},{6,2},{2,0},{1,5},{5,9},... | collective-permute-start | bytes 706568 | tf_op jit(solution)/shard_map/ppermute | solution.py:368
  55.4 7.9 %collective-permute-start.19 = (bf16[40,2944]{1,0:T(8,128)(2,1)S(1)}, bf16[40,2944]{1,0:T(8,128)(2,1)S(1)}, u32[]{:S(2)}, u32[]{:S(2)}) collective-permute-start(bf16[40,2944]{1,0:T(8,128)(2,1)S(1)} %get-tuple-element.109), channel_id=1, source_target_pairs={{4,0},{8,4},{12,8},{14,12},{10,14},{6,10},{2,6},{0,2},{5,1},{9,5},... | collective-permute-start | bytes 706568 | tf_op jit(solution)/shard_map/ppermute | solution.py:371
  58.5 4.7 %copy-start.2 = (f32[1,640]{1,0:T(1,128)S(1)}, f32[1,640]{1,0:T(1,128)}, u32[]{:S(2)}) copy-start(f32[1,640]{1,0:T(1,128)} %bias.1) | copy-start | bytes 7684
  58.5 12.9 %collective-permute-start.2 = (bf16[80,2944]{1,0:T(8,128)(2,1)S(1)}, bf16[80,2944]{1,0:T(8,128)(2,1)S(1)}, u32[]{:S(2)}, u32[]{:S(2)}) collective-permute-start(bf16[80,2944]{1,0:T(8,128)(2,1)S(1)} %get-tuple-element.62), channel_id=1, source_target_pairs={{0,16},{16,0},{1,17},{17,1},{2,18},{18,2},{3,19},{19,3},{4,20},{20... | collective-permute-start | bytes 1413128 | tf_op jit(solution)/shard_map/ppermute | solution.py:343
  63.3 4.3 %collective-permute-start.21 = (f32[3,640]{1,0:T(4,128)S(1)}, f32[3,640]{1,0:T(4,128)S(1)}, u32[]{:S(2)}, u32[]{:S(2)}) collective-permute-start(f32[3,640]{1,0:T(4,128)S(1)} %fusion.2), channel_id=1, source_target_pairs={{0,1},{1,0},{2,3},{3,2},{4,5},{5,4},{6,7},{7,6},{8,9},{9,8},{10,11... | collective-permute-start | bytes 23048 | tf_op jit(solution)/shard_map/ppermute | solution.py:343
  64.8 9.8 %collective-permute-start.20 = (bf16[512,256]{1,0:T(8,128)(2,1)S(1)}, bf16[512,256]{1,0:T(8,128)(2,1)S(1)}, u32[]{:S(2)}, u32[]{:S(2)}) collective-permute-start(bf16[512,256]{1,0:T(8,128)(2,1)S(1)} %shard_map.125), channel_id=1, source_target_pairs={{0,1},{1,0},{2,3},{3,2},{4,5},{5,4},{6,7},{7,6},{8,9},{9,8},{10,11... | collective-permute-start | bytes 786440 | tf_op jit(solution)/shard_map/ppermute | solution.py:343
  65.6 7.7 %collective-permute-start.23 = (bf16[40,2944]{1,0:T(8,128)(2,1)S(1)}, bf16[40,2944]{1,0:T(8,128)(2,1)S(1)}, u32[]{:S(2)}, u32[]{:S(2)}) collective-permute-start(bf16[40,2944]{1,0:T(8,128)(2,1)S(1)} %get-tuple-element.112), channel_id=1, source_target_pairs={{0,4},{4,8},{8,12},{12,14},{14,10},{10,6},{6,2},{2,0},{1,5},{5,9},... | collective-permute-start | bytes 706568 | tf_op jit(solution)/shard_map/ppermute | solution.py:368
  67.2 7.4 %collective-permute-start.24 = (bf16[40,2944]{1,0:T(8,128)(2,1)S(1)}, bf16[40,2944]{1,0:T(8,128)(2,1)S(1)}, u32[]{:S(2)}, u32[]{:S(2)}) collective-permute-start(bf16[40,2944]{1,0:T(8,128)(2,1)S(1)} %get-tuple-element.111), channel_id=1, source_target_pairs={{4,0},{8,4},{12,8},{14,12},{10,14},{6,10},{2,6},{0,2},{5,1},{9,5},... | collective-permute-start | bytes 706568 | tf_op jit(solution)/shard_map/ppermute | solution.py:371
  67.7 3.7 %collective-permute-start.22 = (f32[3,640]{1,0:T(4,128)S(1)}, f32[3,640]{1,0:T(4,128)S(1)}, u32[]{:S(2)}, u32[]{:S(2)}) collective-permute-start(f32[3,640]{1,0:T(4,128)S(1)} %fusion.5), channel_id=1, source_target_pairs={{0,16},{16,0},{1,17},{17,1},{2,18},{18,2},{3,19},{19,3},{4,20},{20... | collective-permute-start | bytes 23048 | tf_op jit(solution)/shard_map/ppermute | solution.py:392
  71.4 6.0 %collective-permute-start.26 = (bf16[512,512]{1,0:T(8,128)(2,1)S(1)}, bf16[512,512]{1,0:T(8,128)(2,1)S(1)}, u32[]{:S(2)}, u32[]{:S(2)}) collective-permute-start(bf16[512,512]{1,0:T(8,128)(2,1)S(1)} %get-tuple-element.100), channel_id=1, source_target_pairs={{0,1},{1,0},{2,3},{3,2},{4,5},{5,4},{6,7},{7,6},{8,9},{9,8},{10,11... | collective-permute-start | bytes 1572872 | tf_op jit(solution)/shard_map/ppermute | solution.py:343
  74.7 6.5 %collective-permute-start.25 = (bf16[40,2944]{1,0:T(8,128)(2,1)S(1)}, bf16[40,2944]{1,0:T(8,128)(2,1)S(1)}, u32[]{:S(2)}, u32[]{:S(2)}) collective-permute-start(bf16[40,2944]{1,0:T(8,128)(2,1)S(1)} %add_convert_fusion.1), channel_id=1, source_target_pairs={{0,4},{4,8},{8,12},{12,14},{14,10},{10,6},{6,2},{2,0},{1,5},{5,9},... | collective-permute-start | bytes 706568 | tf_op jit(solution)/shard_map/ppermute | solution.py:368
  76.2 4.8 %collective-permute-start.27 = (f32[3,640]{1,0:T(4,128)S(1)}, f32[3,640]{1,0:T(4,128)S(1)}, u32[]{:S(2)}, u32[]{:S(2)}) collective-permute-start(f32[3,640]{1,0:T(4,128)S(1)} %add.91), channel_id=1, source_target_pairs={{0,4},{4,0},{8,12},{12,8},{1,5},{5,1},{9,13},{13,9},{2,6},{6,2},{1... | collective-permute-start | bytes 23048 | tf_op jit(solution)/shard_map/ppermute | solution.py:392
  81.0 11.1 %copy-start = (f32[1,40,5760]{2,1,0:T(8,128)S(1)}, f32[1,40,5760]{2,1,0:T(8,128)}, u32[]{:S(2)}) copy-start(f32[1,40,5760]{2,1,0:T(8,128)} %param.10) | copy-start | bytes 2764804
  81.3 7.3 %collective-permute-start.28 = (bf16[40,2944]{1,0:T(8,128)(2,1)S(1)}, bf16[40,2944]{1,0:T(8,128)(2,1)S(1)}, u32[]{:S(2)}, u32[]{:S(2)}) collective-permute-start(bf16[40,2944]{1,0:T(8,128)(2,1)S(1)} %add_convert_fusion), channel_id=1, source_target_pairs={{0,16},{16,0},{1,17},{17,1},{2,18},{18,2},{3,19},{19,3},{4,20},{20... | collective-permute-start | bytes 706568 | tf_op jit(solution)/shard_map/ppermute | solution.py:343
  83.3 3.7 %collective-permute-start.30 = (f32[3,640]{1,0:T(4,128)S(1)}, f32[3,640]{1,0:T(4,128)S(1)}, u32[]{:S(2)}, u32[]{:S(2)}) collective-permute-start(f32[3,640]{1,0:T(4,128)S(1)} %add.98), channel_id=1, source_target_pairs={{0,2},{2,0},{1,3},{3,1},{4,6},{6,4},{5,7},{7,5},{8,10},{10,8},{9,1... | collective-permute-start | bytes 23048 | tf_op jit(solution)/shard_map/ppermute | solution.py:392
  86.9 4.6 %collective-permute-start.31 = (f32[3,640]{1,0:T(4,128)S(1)}, f32[3,640]{1,0:T(4,128)S(1)}, u32[]{:S(2)}, u32[]{:S(2)}) collective-permute-start(f32[3,640]{1,0:T(4,128)S(1)} %add.102), channel_id=1, source_target_pairs={{0,8},{4,12},{8,0},{12,4},{1,9},{5,13},{9,1},{13,5},{2,10},{6,14},... | collective-permute-start | bytes 23048 | tf_op jit(solution)/shard_map/ppermute | solution.py:392
  88.7 3.4 %collective-permute-start.29 = (bf16[40,2944]{1,0:T(8,128)(2,1)S(1)}, bf16[40,2944]{1,0:T(8,128)(2,1)S(1)}, u32[]{:S(2)}, u32[]{:S(2)}) collective-permute-start(bf16[40,2944]{1,0:T(8,128)(2,1)S(1)} %get-tuple-element.119), channel_id=1, source_target_pairs={{0,1},{1,0},{2,3},{3,2},{4,5},{5,4},{6,7},{7,6},{8,9},{9,8},{10,11... | collective-permute-start | bytes 706568 | tf_op jit(solution)/shard_map/ppermute | solution.py:343

commit v19 on v10

--- a/solution.py
+++ b/solution.py
@@ -550,9 +550,10 @@
         crossed[-2], sums, *received = tied(crossed[-2], sums, *received)
         acts_last, *_ = tied(acts, sums, *received)
         received = ring_step(zs - 2, *received)
-        conv_got = swap(conv_far(acts_last, late), "core")
+        conv_send = conv_far(acts_last, late)
         vectors = hop(chip_sum(first_sums + sums), "replica", 1)
-        crossed[-1], conv_got, vectors, *received = tied(crossed[-1], conv_got, vectors, *received)
+        crossed[-1], conv_send, vectors, *received = tied(crossed[-1], conv_send, vectors, *received)
+        conv_got = swap(conv_send, "core")
         last, behind = ring_step(zs - 1, *received)
         block = conv_own(conv_got, [conv_first_own, conv_first_got, order], late)
         vectors = hop(vectors, "z", 1)

time: 92.5 us -> 95.5 us (1.032)
  waiting for transfers between devices: 20.1 us -> 22.6 us
    ppermute x4, waiting for transfers between devices: 5.57 us -> 8.03 us  [hop(): lax.ppermute(value, axis, [(s, s ^ mask) for s in range(count)])]
    ppermute x4, starting transfers between devices: 7 us -> 8 us  [hop(): lax.ppermute(value, axis, [(s, s ^ mask) for s in range(count)])]
  transfers between devices with their start and end apart: 33 -> 33, of which waited for: 13 -> 13; matrix products, arithmetic and copies ran while one was open for 4% -> 4% of each run, Pallas kernels for 34% -> 33%
where the time goes in v19:
time: 95.5 us; the launch traced here: 95.3 us
  starting transfers between devices  33.9 us (35%)
  Pallas kernels  32.4 us (34%)
  waiting for transfers between devices  22.6 us (24%)
  other arithmetic  2.88 us (3%)
  local copies, waits for them, and re-layouts  1.94 us (2%)
  between operations  1.54 us (2%)
    ppermute x14, starting transfers between devices, swap(): return lax.ppermute(value, axis, [(0, 1), (1, 0)])  9.31 us
    ppermute x8, starting transfers between devices, up(): return lax.ppermute(value, NODE, self.ahead)  9.16 us
    pallas_call x2, Pallas kernels, back(): call(partial(back_kernel, cols, stages, stage), jax.ShapeDtypeStruct((2,...  8.6 us
    ppermute x4, waiting for transfers between devices, hop(): lax.ppermute(value, axis, [(s, s ^ mask) for s in range(count)])  8.03 us
    ppermute x4, starting transfers between devices, hop(): lax.ppermute(value, axis, [(s, s ^ mask) for s in range(count)])  8 us
    ppermute x7, starting transfers between devices, down(): return lax.ppermute(value, NODE, self.behind)  7.4 us
    ppermute x8, waiting for transfers between devices, up(): return lax.ppermute(value, NODE, self.ahead)  7.38 us
    pallas_call x1, Pallas kernels, per_device(): call(partial(grad_kernel, cols), [jax.ShapeDtypeStruct((n * 2 * part, col...  4.64 us
  transfers between devices with their start and end apart: 33, of which 13 were waited for; matrix products, arithmetic and copies ran while one was open for 4% of the time, Pallas kernels for 33%

profile of v19, /device:TPU:0, one launch (start us, length us, event | category | flops | bytes accessed | tf_op | source)
XLA Modules:
  0.0 95.3 jit_solution(17329534205705552080)
XLA Ops:
  0.7 1.3 %fusion = (bf16[40,2944]{1,0:T(8,128)(2,1)S(1)}, bf16[40,2944]{1,0:T(8,128)(2,1)S(1)}) fusion(f32[1,40,5760]{2,1,0:T(8,128)} %param.10, s32[]{:T(128)S(6)} %select_n.27, s32[]{:T(128)S(6)} %select_n.28), kind=kLoop, calls=%fused_computation.12 | loop fusion | bytes 942088 | tf_op jit(solution)/shard_map/convert_element_type | solution.py:419
  2.0 0.5 collective-permute-start.4
  2.5 2.0 %fusion.3 = (f32[640]{0:T(1024)S(1)}, bf16[16,32,640]{2,1,0:T(8,128)(2,1)S(1)}) fusion(f32[1,16,32,640]{3,2,1,0:T(8,128)} %param.9), kind=kLoop, calls=%fused_computation.20 | loop fusion | flops 654720 | bytes 1968640 | tf_op jit(solution)/shard_map/reduce_sum | solution.py:512
  4.6 0.5 collective-permute-start
  5.1 2.7 %collective-permute-start.5 = (bf16[80,2944]{1,0:T(8,128)(2,1)S(1)}, bf16[80,2944]{1,0:T(8,128)(2,1)S(1)}, u32[]{:S(2)}, u32[]{:S(2)}) collective-permute-start(bf16[80,2944]{1,0:T(8,128)(2,1)S(1)} %maximum_select_fusion.refs_0_), channel_id=1, source_target_pairs={{0,4},{4,8},{8,12},{12,14},{14,10},{10,6},{6,2},{2,0},{1,5},{5,9},... | collective-permute-start | bytes 1413128 | tf_op jit(solution)/shard_map/ppermute | solution.py:364
  7.8 1.9 %collective-permute-start.7 = (bf16[40,2944]{1,0:T(8,128)(2,1)S(1)}, bf16[40,2944]{1,0:T(8,128)(2,1)S(1)}, u32[]{:S(2)}, u32[]{:S(2)}) collective-permute-start(bf16[40,2944]{1,0:T(8,128)(2,1)S(1)} %get-tuple-element.119), channel_id=1, source_target_pairs={{0,16},{16,0},{1,17},{17,1},{2,18},{18,2},{3,19},{19,3},{4,20},{20... | collective-permute-start | bytes 706568 | tf_op jit(solution)/shard_map/ppermute | solution.py:339
  9.9 4.4 %shard_map.119 = (f32[2,640]{1,0:T(2,128)S(1)}, bf16[3,34,32,640]{3,2,1,0:T(8,128)(2,1)S(1)}, bf16[640,1024]{1,0:T(8,128)(2,1)S(1)}) custom-call(s32[1]{0:T(128)} %bitcast.dev, s32[32,24]{1,0:T(8,128)S(1)} %copy-done.5, bf16[16,32,640]{2,1,0:T(8,128)(2,1)S(1)} %bitcast.13, bf16[16,32,640]{2,1,0:T(8,128)(2,1)S(1)} %collective-permute-done.lat_far, ...), custom_call_target="tpu_custom_call" | custom-call | flops 964689920 | tf_op jit(solution)/shard_map/pallas_call | solution.py:450
  14.3 4.6 %shard_map.120 = (bf16[320,2944]{1,0:T(8,128)(2,1)S(1)}, bf16[80,2944]{1,0:T(8,128)(2,1)S(1)}, bf16[80,2944]{1,0:T(8,128)(2,1)S(1)}, bf16[80,2944]{1,0:T(8,128)(2,1)S(1)}, bf16[80,2944]{1,0:T(8,128)(2,1)S(1)}) custom-call(s32[1]{0:T(128)} %bitcast.dev, bf16[3,34,32,640]{3,2,1,0:T(8,128)(2,1)S(1)} %get-tuple-element.94.acts, ...), custom_call_target="tpu_custom_call" | custom-call | flops 1929379840 | tf_op jit(solution)/shard_map/pallas_call | solution.py:458
  19.0 1.7 %collective-permute-done.8.theirs = bf16[40,2944]{1,0:T(8,128)(2,1)S(1)} collective-permute-done((bf16[40,2944]{1,0:T(8,128)(2,1)S(1)}, bf16[40,2944]{1,0:T(8,128)(2,1)S(1)}, u32[]{:S(2)}, u32[]{:S(2)}) %collective-permute-start.8) | collective-permute-done | bytes 235552 | tf_op jit(solution)/shard_map/ppermute | solution.py:339
  20.7 1.7 %collective-permute-start.10 = (bf16[80,2944]{1,0:T(8,128)(2,1)S(1)}, bf16[80,2944]{1,0:T(8,128)(2,1)S(1)}, u32[]{:S(2)}, u32[]{:S(2)}) collective-permute-start(bf16[80,2944]{1,0:T(8,128)(2,1)S(1)} %collective-permute-done.6.refs_2_), channel_id=1, source_target_pairs={{4,0},{8,4},{12,8},{14,12},{10,14},{6,10},{2,6},{0,2},{5,1},{9,5},... | collective-permute-start | bytes 1413128 | tf_op jit(solution)/shard_map/ppermute | solution.py:367
  22.7 1.7 %collective-permute-start.11 = (bf16[80,2944]{1,0:T(8,128)(2,1)S(1)}, bf16[80,2944]{1,0:T(8,128)(2,1)S(1)}, u32[]{:S(2)}, u32[]{:S(2)}) collective-permute-start(bf16[80,2944]{1,0:T(8,128)(2,1)S(1)} %get-tuple-element.75), channel_id=1, source_target_pairs={{0,16},{16,0},{1,17},{17,1},{2,18},{18,2},{3,19},{19,3},{4,20},{20... | collective-permute-start | bytes 1413128 | tf_op jit(solution)/shard_map/ppermute | solution.py:339
  24.7 4.5 %shard_map.121 = (bf16[3,34,32,768]{3,2,1,0:T(8,128)(2,1)S(1)}, bf16[32,32,640]{2,1,0:T(8,128)(2,1)S(1)}, bf16[32,32,640]{2,1,0:T(8,128)(2,1)S(1)}, bf16[640,768]{1,0:T(8,128)(2,1)S(1)}) custom-call(s32[1]{0:T(128)} %bitcast.dev, s32[32,24]{1,0:T(8,128)S(1)} %copy-done.5, f32[2,640]{1,0:T(2,128)S(1)} %get-tuple-element.69.stats, f32[1,640]{1,0:T(1,128)S(1)} %copy-done.3, ...), custom_call_target="tpu_custom_call" | custom-call | flops 964689920 | tf_op jit(solution)/shard_map/pallas_call | solution.py:470
  29.2 3.5 %collective-permute-done.10.refs_4_ = bf16[80,2944]{1,0:T(8,128)(2,1)S(1)} collective-permute-done((bf16[80,2944]{1,0:T(8,128)(2,1)S(1)}, bf16[80,2944]{1,0:T(8,128)(2,1)S(1)}, u32[]{:S(2)}, u32[]{:S(2)}) %collective-permute-start.10) | collective-permute-done | bytes 471072 | tf_op jit(solution)/shard_map/ppermute | solution.py:367
  32.7 1.1 %collective-permute-done.9.refs_3_ = bf16[80,2944]{1,0:T(8,128)(2,1)S(1)} collective-permute-done((bf16[80,2944]{1,0:T(8,128)(2,1)S(1)}, bf16[80,2944]{1,0:T(8,128)(2,1)S(1)}, u32[]{:S(2)}, u32[]{:S(2)}) %collective-permute-start.9) | collective-permute-done | bytes 471072 | tf_op jit(solution)/shard_map/ppermute | solution.py:364
  33.8 0.7 collective-permute-start.12
  34.5 1.4 %collective-permute-start.13 = (bf16[80,2944]{1,0:T(8,128)(2,1)S(1)}, bf16[80,2944]{1,0:T(8,128)(2,1)S(1)}, u32[]{:S(2)}, u32[]{:S(2)}) collective-permute-start(bf16[80,2944]{1,0:T(8,128)(2,1)S(1)} %collective-permute-done.10.refs_4_), channel_id=1, source_target_pairs={{4,0},{8,4},{12,8},{14,12},{10,14},{6,10},{2,6},{0,2},{5,1},{9,5},... | collective-permute-start | bytes 1413128 | tf_op jit(solution)/shard_map/ppermute | solution.py:367
  35.8 4.0 %shard_map.122 = (f32[512,512]{1,0:T(8,128)S(1)}, bf16[512,512]{1,0:T(8,128)(2,1)S(1)}) custom-call(s32[1]{0:T(128)} %bitcast.dev, bf16[3,34,32,640]{3,2,1,0:T(8,128)(2,1)S(1)} %get-tuple-element.94.acts, bf16[80,2944]{1,0:T(8,128)(2,1)S(1)} %maximum_select_fusion.refs_0_, bf16[80,2944]{1,0:T(8,128)(2,1)S(1)} %collective-permute-done.5.refs_1_, ...), custom_call_target="tpu_custom_call" | custom-call | flops 964689920 | tf_op jit(solution)/shard_map/pallas_call | solution.py:488
  39.9 0.7 collective-permute-start.17
  40.7 1.4 %collective-permute-start.18 = (bf16[40,2944]{1,0:T(8,128)(2,1)S(1)}, bf16[40,2944]{1,0:T(8,128)(2,1)S(1)}, u32[]{:S(2)}, u32[]{:S(2)}) collective-permute-start(bf16[40,2944]{1,0:T(8,128)(2,1)S(1)} %get-tuple-element.115), channel_id=1, source_target_pairs={{4,0},{8,4},{12,8},{14,12},{10,14},{6,10},{2,6},{0,2},{5,1},{9,5},... | collective-permute-start | bytes 706568 | tf_op jit(solution)/shard_map/ppermute | solution.py:367
  42.0 5.4 %shard_map.123 = f32[2,640]{1,0:T(2,128)S(1)} custom-call(s32[1]{0:T(128)} %bitcast.dev, bf16[3,34,32,768]{3,2,1,0:T(8,128)(2,1)S(1)} %get-tuple-element.80.cots, bf16[32,32,640]{2,1,0:T(8,128)(2,1)S(1)} %get-tuple-element.81.slope, bf16[32,32,640]{2,1,0:T(8,128)(2,1)S(1)} %get-tuple-element.82.slope_x, bf16[80,2944]{1,0:T(8,128)(2,1)S(1)} %maximum_select_fusion.refs_0_, ...), custom_call_target="tpu_custom_call" | custom-call | flops 964689920 | tf_op jit(solution)/shard_map/pallas_call | solution.py:480
  47.4 1.9 %collective-permute-done.17 = bf16[40,2944]{1,0:T(8,128)(2,1)S(1)} collective-permute-done((bf16[40,2944]{1,0:T(8,128)(2,1)S(1)}, bf16[40,2944]{1,0:T(8,128)(2,1)S(1)}, u32[]{:S(2)}, u32[]{:S(2)}) %collective-permute-start.17) | collective-permute-done | bytes 235552 | tf_op jit(solution)/shard_map/ppermute | solution.py:364
  49.3 1.5 %collective-permute-start.3 = (bf16[80,2944]{1,0:T(8,128)(2,1)S(1)}, bf16[80,2944]{1,0:T(8,128)(2,1)S(1)}, u32[]{:S(2)}, u32[]{:S(2)}) collective-permute-start(bf16[80,2944]{1,0:T(8,128)(2,1)S(1)} %get-tuple-element.63), channel_id=1, source_target_pairs={{0,16},{16,0},{1,17},{17,1},{2,18},{18,2},{3,19},{19,3},{4,20},{20... | collective-permute-start | bytes 1413128 | tf_op jit(solution)/shard_map/ppermute | solution.py:339
  50.9 0.9 collective-permute-start.15
  51.9 1.2 %collective-permute-start.16 = (bf16[40,2944]{1,0:T(8,128)(2,1)S(1)}, bf16[40,2944]{1,0:T(8,128)(2,1)S(1)}, u32[]{:S(2)}, u32[]{:S(2)}) collective-permute-start(bf16[40,2944]{1,0:T(8,128)(2,1)S(1)} %slice.77), channel_id=1, source_target_pairs={{4,0},{8,4},{12,8},{14,12},{10,14},{6,10},{2,6},{0,2},{5,1},{9,5},... | collective-permute-start | bytes 706568 | tf_op jit(solution)/shard_map/ppermute | solution.py:367
  53.2 0.9 collective-permute-start.19
  54.2 1.1 %collective-permute-start.20 = (bf16[40,2944]{1,0:T(8,128)(2,1)S(1)}, bf16[40,2944]{1,0:T(8,128)(2,1)S(1)}, u32[]{:S(2)}, u32[]{:S(2)}) collective-permute-start(bf16[40,2944]{1,0:T(8,128)(2,1)S(1)} %get-tuple-element.113), channel_id=1, source_target_pairs={{4,0},{8,4},{12,8},{14,12},{10,14},{6,10},{2,6},{0,2},{5,1},{9,5},... | collective-permute-start | bytes 706568 | tf_op jit(solution)/shard_map/ppermute | solution.py:367
  55.3 2.4 %collective-permute-done.15.refs_2_.refs_5_ = bf16[40,2944]{1,0:T(8,128)(2,1)S(1)} collective-permute-done((bf16[40,2944]{1,0:T(8,128)(2,1)S(1)}, bf16[40,2944]{1,0:T(8,128)(2,1)S(1)}, u32[]{:S(2)}, u32[]{:S(2)}) %collective-permute-start.15) | collective-permute-done | bytes 235552 | tf_op jit(solution)/shard_map/ppermute | solution.py:364
  57.7 0.9 collective-permute-start.2
  58.7 3.2 %shard_map.124 = f32[2,640]{1,0:T(2,128)S(1)} custom-call(s32[1]{0:T(128)} %bitcast.dev, bf16[3,34,32,768]{3,2,1,0:T(8,128)(2,1)S(1)} %get-tuple-element.80.cots, bf16[32,32,640]{2,1,0:T(8,128)(2,1)S(1)} %get-tuple-element.81.slope, bf16[32,32,640]{2,1,0:T(8,128)(2,1)S(1)} %get-tuple-element.82.slope_x, ...), custom_call_target="tpu_custom_call" | custom-call | flops 964689920 | tf_op jit(solution)/shard_map/pallas_call | solution.py:480
  61.9 0.8 collective-permute-done.3
  63.0 1.4 %collective-permute-start.23 = (bf16[40,2944]{1,0:T(8,128)(2,1)S(1)}, bf16[40,2944]{1,0:T(8,128)(2,1)S(1)}, u32[]{:S(2)}, u32[]{:S(2)}) collective-permute-start(bf16[40,2944]{1,0:T(8,128)(2,1)S(1)} %get-tuple-element.112), channel_id=1, source_target_pairs={{0,4},{4,8},{8,12},{12,14},{14,10},{10,6},{6,2},{2,0},{1,5},{5,9},... | collective-permute-start | bytes 706568 | tf_op jit(solution)/shard_map/ppermute | solution.py:364
  64.4 0.7 collective-permute-start.24
  65.1 1.9 %collective-permute-start.22 = (f32[3,640]{1,0:T(4,128)S(1)}, f32[3,640]{1,0:T(4,128)S(1)}, u32[]{:S(2)}, u32[]{:S(2)}) collective-permute-start(f32[3,640]{1,0:T(4,128)S(1)} %fusion.5), channel_id=1, source_target_pairs={{0,16},{16,0},{1,17},{17,1},{2,18},{18,2},{3,19},{19,3},{4,20},{20... | collective-permute-start | bytes 23048 | tf_op jit(solution)/shard_map/ppermute | solution.py:388
  67.1 1.4 %shard_map.125 = bf16[512,256]{1,0:T(8,128)(2,1)S(1)} custom-call(s32[1]{0:T(128)} %bitcast.dev, bf16[3,34,32,640]{3,2,1,0:T(8,128)(2,1)S(1)} %get-tuple-element.94.acts, bf16[80,2944]{1,0:T(8,128)(2,1)S(1)} %collective-permute-done.12.refs_0_.refs_3_, bf16[80,2944]{1,0:T(8,128)(2,1)S(1)} %collective-permute-done.13.refs_1_.refs_4_, ...), custom_call_target="tpu_custom_call" | custom-call | flops 482344960 | tf_op jit(solution)/shard_map/pallas_call | solution.py:497
  68.5 0.7 collective-permute-done.22
  69.2 2.0 %collective-permute-done.23 = bf16[40,2944]{1,0:T(8,128)(2,1)S(1)} collective-permute-done((bf16[40,2944]{1,0:T(8,128)(2,1)S(1)}, bf16[40,2944]{1,0:T(8,128)(2,1)S(1)}, u32[]{:S(2)}, u32[]{:S(2)}) %collective-permute-start.23) | collective-permute-done | bytes 235552 | tf_op jit(solution)/shard_map/ppermute | solution.py:364
  71.2 1.1 %collective-permute-done.24 = bf16[40,2944]{1,0:T(8,128)(2,1)S(1)} collective-permute-done((bf16[40,2944]{1,0:T(8,128)(2,1)S(1)}, bf16[40,2944]{1,0:T(8,128)(2,1)S(1)}, u32[]{:S(2)}, u32[]{:S(2)}) %collective-permute-start.24) | collective-permute-done | bytes 235552 | tf_op jit(solution)/shard_map/ppermute | solution.py:367
  72.4 1.4 %collective-permute-start.25 = (bf16[40,2944]{1,0:T(8,128)(2,1)S(1)}, bf16[40,2944]{1,0:T(8,128)(2,1)S(1)}, u32[]{:S(2)}, u32[]{:S(2)}) collective-permute-start(bf16[40,2944]{1,0:T(8,128)(2,1)S(1)} %add_convert_fusion.1), channel_id=1, source_target_pairs={{0,4},{4,8},{8,12},{12,14},{14,10},{10,6},{6,2},{2,0},{1,5},{5,9},... | collective-permute-start | bytes 706568 | tf_op jit(solution)/shard_map/ppermute | solution.py:364
  73.8 1.4 %collective-permute-start.28 = (f32[3,640]{1,0:T(4,128)S(1)}, f32[3,640]{1,0:T(4,128)S(1)}, u32[]{:S(2)}, u32[]{:S(2)}) collective-permute-start(f32[3,640]{1,0:T(4,128)S(1)} %add.91), channel_id=1, source_target_pairs={{0,4},{4,0},{8,12},{12,8},{1,5},{5,1},{9,13},{13,9},{2,6},{6,2},{1... | collective-permute-start | bytes 23048 | tf_op jit(solution)/shard_map/ppermute | solution.py:388
  75.2 4.5 %collective-permute-done.28 = f32[3,640]{1,0:T(4,128)S(1)} collective-permute-done((f32[3,640]{1,0:T(4,128)S(1)}, f32[3,640]{1,0:T(4,128)S(1)}, u32[]{:S(2)}, u32[]{:S(2)}) %collective-permute-start.28) | collective-permute-done | bytes 7712 | tf_op jit(solution)/shard_map/ppermute | solution.py:388
  79.7 3.7 %shard_map.126 = bf16[16,32,640]{2,1,0:T(8,128)(2,1)} custom-call(s32[1]{0:T(128)} %bitcast.dev, bf16[3,34,32,640]{3,2,1,0:T(8,128)(2,1)S(1)} %get-tuple-element.94.acts, bf16[512,256]{1,0:T(8,128)(2,1)S(1)} %collective-permute-done.26.got, bf16[16,32,640]{2,1,0:T(8,128)(2,1)S(1)} %bitcast.15, f32[1,640]{1,0:T(1,128)S(1)} %copy-done.2, ...), custom_call_target="tpu_custom_call" | custom-call | flops 964689920 | tf_op jit(solution)/shard_map/pallas_call | solution.py:505
  83.5 1.7 %collective-permute-start.29 = (bf16[40,2944]{1,0:T(8,128)(2,1)S(1)}, bf16[40,2944]{1,0:T(8,128)(2,1)S(1)}, u32[]{:S(2)}, u32[]{:S(2)}) collective-permute-start(bf16[40,2944]{1,0:T(8,128)(2,1)S(1)} %add_convert_fusion), channel_id=1, source_target_pairs={{0,16},{16,0},{1,17},{17,1},{2,18},{18,2},{3,19},{19,3},{4,20},{20... | collective-permute-start | bytes 706568 | tf_op jit(solution)/shard_map/ppermute | solution.py:339
  85.2 2.0 %collective-permute-start.31 = (f32[3,640]{1,0:T(4,128)S(1)}, f32[3,640]{1,0:T(4,128)S(1)}, u32[]{:S(2)}, u32[]{:S(2)}) collective-permute-start(f32[3,640]{1,0:T(4,128)S(1)} %add.98), channel_id=1, source_target_pairs={{0,2},{2,0},{1,3},{3,1},{4,6},{6,4},{5,7},{7,5},{8,10},{10,8},{9,1... | collective-permute-start | bytes 23048 | tf_op jit(solution)/shard_map/ppermute | solution.py:388
  87.9 1.0 %collective-permute-done.31 = f32[3,640]{1,0:T(4,128)S(1)} collective-permute-done((f32[3,640]{1,0:T(4,128)S(1)}, f32[3,640]{1,0:T(4,128)S(1)}, u32[]{:S(2)}, u32[]{:S(2)}) %collective-permute-start.31) | collective-permute-done | bytes 7712 | tf_op jit(solution)/shard_map/ppermute | solution.py:388
  88.9 2.7 %collective-permute-start.32 = (f32[3,640]{1,0:T(4,128)S(1)}, f32[3,640]{1,0:T(4,128)S(1)}, u32[]{:S(2)}, u32[]{:S(2)}) collective-permute-start(f32[3,640]{1,0:T(4,128)S(1)} %add.102), channel_id=1, source_target_pairs={{0,8},{4,12},{8,0},{12,4},{1,9},{5,13},{9,1},{13,5},{2,10},{6,14},... | collective-permute-start | bytes 23048 | tf_op jit(solution)/shard_map/ppermute | solution.py:388
  91.7 1.8 %collective-permute-done.32 = f32[3,640]{1,0:T(4,128)S(1)} collective-permute-done((f32[3,640]{1,0:T(4,128)S(1)}, f32[3,640]{1,0:T(4,128)S(1)}, u32[]{:S(2)}, u32[]{:S(2)}) %collective-permute-start.32) | collective-permute-done | bytes 7712 | tf_op jit(solution)/shard_map/ppermute | solution.py:388
  93.5 0.6 fusion.4
  94.1 1.2 %shard_map.127 = f32[40,5760]{1,0:T(8,128)} custom-call(s32[1]{0:T(128)} %bitcast.dev, s32[1]{0:T(128)S(6)} %copy.13.step, f32[40,5760]{1,0:T(8,128)S(1)} %bitcast.11, bf16[40,2944]{1,0:T(8,128)(2,1)S(1)} %collective-permute-done.7.mine, bf16[40,2944]{1,0:T(8,128)(2,1)S(1)} %collective-permute-done.8.theirs, bf16[40,2944]{1,0:T(8,128)(2,1)S(1)} %get-tuple-element.122.ours, ...), custom_call_target="tpu_custom_call" | custom-call | flops 241172480 | tf_op jit(solution)/shard_map/pallas_call | solution.py:565
  (59 shorter events, 2.2 us)
Async XLA Ops:
  0.6 3.9 %copy-start.1 = (bf16[1,16,32,640]{3,2,1,0:T(8,128)(2,1)S(1)}, bf16[1,16,32,640]{3,2,1,0:T(8,128)(2,1)}, u32[]{:S(2)}) copy-start(bf16[1,16,32,640]{3,2,1,0:T(8,128)(2,1)} %param.8) | copy-start | bytes 1966084
  0.7 9.2 %copy-start.3 = (f32[1,640]{1,0:T(1,128)S(1)}, f32[1,640]{1,0:T(1,128)}, u32[]{:S(2)}) copy-start(f32[1,640]{1,0:T(1,128)} %gain.3) | copy-start | bytes 7684
  0.7 9.2 %copy-start.4 = (f32[1,640]{1,0:T(1,128)S(1)}, f32[1,640]{1,0:T(1,128)}, u32[]{:S(2)}) copy-start(f32[1,640]{1,0:T(1,128)} %shift.3) | copy-start | bytes 7684
  0.7 9.2 %copy-start.5 = (s32[32,24]{1,0:T(8,128)S(1)}, s32[32,24]{1,0:T(8,128)}, u32[]{:S(2)}) copy-start(s32[32,24]{1,0:T(8,128)} %constant.40.clone.table) | copy-start | bytes 9220
  2.0 3.1 %collective-permute-start.4 = (bf16[40,2944]{1,0:T(8,128)(2,1)S(1)}, bf16[40,2944]{1,0:T(8,128)(2,1)S(1)}, u32[]{:S(2)}, u32[]{:S(2)}) collective-permute-start(bf16[40,2944]{1,0:T(8,128)(2,1)S(1)} %get-tuple-element.120), channel_id=1, source_target_pairs={{0,1},{1,0},{2,3},{3,2},{4,5},{5,4},{6,7},{7,6},{8,9},{9,8},{10,11... | collective-permute-start | bytes 706568 | tf_op jit(solution)/shard_map/ppermute | solution.py:339
  4.5 5.3 %collective-permute-start.1 = (bf16[16,32,640]{2,1,0:T(8,128)(2,1)S(1)}, bf16[16,32,640]{2,1,0:T(8,128)(2,1)S(1)}, u32[]{:S(2)}, u32[]{:S(2)}) collective-permute-start(bf16[16,32,640]{2,1,0:T(8,128)(2,1)S(1)} %get-tuple-element.118.cot_own), channel_id=1, source_target_pairs={{0,1},{1,0},{2,3},{3,2},{4,5},{5,4},{6,7},{7,6},{8,9},{9,8},{10,11... | collective-permute-start | bytes 1966088 | tf_op jit(solution)/shard_map/ppermute | solution.py:339
  4.6 5.3 %collective-permute-start = (bf16[16,32,640]{2,1,0:T(8,128)(2,1)S(1)}, bf16[16,32,640]{2,1,0:T(8,128)(2,1)S(1)}, u32[]{:S(2)}, u32[]{:S(2)}) collective-permute-start(bf16[16,32,640]{2,1,0:T(8,128)(2,1)S(1)} %bitcast.12), channel_id=1, source_target_pairs={{0,1},{1,0},{2,3},{3,2},{4,5},{5,4},{6,7},{7,6},{8,9},{9,8},{10,11... | collective-permute-start | bytes 1966088 | tf_op jit(solution)/shard_map/ppermute | solution.py:339
  5.1 15.6 %collective-permute-start.5 = (bf16[80,2944]{1,0:T(8,128)(2,1)S(1)}, bf16[80,2944]{1,0:T(8,128)(2,1)S(1)}, u32[]{:S(2)}, u32[]{:S(2)}) collective-permute-start(bf16[80,2944]{1,0:T(8,128)(2,1)S(1)} %maximum_select_fusion.refs_0_), channel_id=1, source_target_pairs={{0,4},{4,8},{8,12},{12,14},{14,10},{10,6},{6,2},{2,0},{1,5},{5,9},... | collective-permute-start | bytes 1413128 | tf_op jit(solution)/shard_map/ppermute | solution.py:364
  7.8 12.9 %collective-permute-start.6 = (bf16[80,2944]{1,0:T(8,128)(2,1)S(1)}, bf16[80,2944]{1,0:T(8,128)(2,1)S(1)}, u32[]{:S(2)}, u32[]{:S(2)}) collective-permute-start(bf16[80,2944]{1,0:T(8,128)(2,1)S(1)} %maximum_select_fusion.refs_0_), channel_id=1, source_target_pairs={{4,0},{8,4},{12,8},{14,12},{10,14},{6,10},{2,6},{0,2},{5,1},{9,5},... | collective-permute-start | bytes 1413128 | tf_op jit(solution)/shard_map/ppermute | solution.py:367
  7.8 11.1 %collective-permute-start.7 = (bf16[40,2944]{1,0:T(8,128)(2,1)S(1)}, bf16[40,2944]{1,0:T(8,128)(2,1)S(1)}, u32[]{:S(2)}, u32[]{:S(2)}) collective-permute-start(bf16[40,2944]{1,0:T(8,128)(2,1)S(1)} %get-tuple-element.119), channel_id=1, source_target_pairs={{0,16},{16,0},{1,17},{17,1},{2,18},{18,2},{3,19},{19,3},{4,20},{20... | collective-permute-start | bytes 706568 | tf_op jit(solution)/shard_map/ppermute | solution.py:339
  9.8 10.9 %collective-permute-start.8 = (bf16[40,2944]{1,0:T(8,128)(2,1)S(1)}, bf16[40,2944]{1,0:T(8,128)(2,1)S(1)}, u32[]{:S(2)}, u32[]{:S(2)}) collective-permute-start(bf16[40,2944]{1,0:T(8,128)(2,1)S(1)} %get-tuple-element.120), channel_id=1, source_target_pairs={{0,16},{16,0},{1,17},{17,1},{2,18},{18,2},{3,19},{19,3},{4,20},{20... | collective-permute-start | bytes 706568 | tf_op jit(solution)/shard_map/ppermute | solution.py:339
  20.7 12.0 %collective-permute-start.10 = (bf16[80,2944]{1,0:T(8,128)(2,1)S(1)}, bf16[80,2944]{1,0:T(8,128)(2,1)S(1)}, u32[]{:S(2)}, u32[]{:S(2)}) collective-permute-start(bf16[80,2944]{1,0:T(8,128)(2,1)S(1)} %collective-permute-done.6.refs_2_), channel_id=1, source_target_pairs={{4,0},{8,4},{12,8},{14,12},{10,14},{6,10},{2,6},{0,2},{5,1},{9,5},... | collective-permute-start | bytes 1413128 | tf_op jit(solution)/shard_map/ppermute | solution.py:367
  22.4 11.4 %collective-permute-start.9 = (bf16[80,2944]{1,0:T(8,128)(2,1)S(1)}, bf16[80,2944]{1,0:T(8,128)(2,1)S(1)}, u32[]{:S(2)}, u32[]{:S(2)}) collective-permute-start(bf16[80,2944]{1,0:T(8,128)(2,1)S(1)} %collective-permute-done.5.refs_1_), channel_id=1, source_target_pairs={{0,4},{4,8},{8,12},{12,14},{14,10},{10,6},{6,2},{2,0},{1,5},{5,9},... | collective-permute-start | bytes 1413128 | tf_op jit(solution)/shard_map/ppermute | solution.py:364
  22.7 17.1 %collective-permute-start.11 = (bf16[80,2944]{1,0:T(8,128)(2,1)S(1)}, bf16[80,2944]{1,0:T(8,128)(2,1)S(1)}, u32[]{:S(2)}, u32[]{:S(2)}) collective-permute-start(bf16[80,2944]{1,0:T(8,128)(2,1)S(1)} %get-tuple-element.75), channel_id=1, source_target_pairs={{0,16},{16,0},{1,17},{17,1},{2,18},{18,2},{3,19},{19,3},{4,20},{20... | collective-permute-start | bytes 1413128 | tf_op jit(solution)/shard_map/ppermute | solution.py:339
  24.4 26.5 %collective-permute-start.14 = (bf16[80,2944]{1,0:T(8,128)(2,1)S(1)}, bf16[80,2944]{1,0:T(8,128)(2,1)S(1)}, u32[]{:S(2)}, u32[]{:S(2)}) collective-permute-start(bf16[80,2944]{1,0:T(8,128)(2,1)S(1)} %get-tuple-element.83), channel_id=1, source_target_pairs={{0,16},{16,0},{1,17},{17,1},{2,18},{18,2},{3,19},{19,3},{4,20},{20... | collective-permute-start | bytes 1413128 | tf_op jit(solution)/shard_map/ppermute | solution.py:339
  33.8 17.0 %collective-permute-start.12 = (bf16[80,2944]{1,0:T(8,128)(2,1)S(1)}, bf16[80,2944]{1,0:T(8,128)(2,1)S(1)}, u32[]{:S(2)}, u32[]{:S(2)}) collective-permute-start(bf16[80,2944]{1,0:T(8,128)(2,1)S(1)} %collective-permute-done.9.refs_3_), channel_id=1, source_target_pairs={{0,4},{4,8},{8,12},{12,14},{14,10},{10,6},{6,2},{2,0},{1,5},{5,9},... | collective-permute-start | bytes 1413128 | tf_op jit(solution)/shard_map/ppermute | solution.py:364
  34.5 16.4 %collective-permute-start.13 = (bf16[80,2944]{1,0:T(8,128)(2,1)S(1)}, bf16[80,2944]{1,0:T(8,128)(2,1)S(1)}, u32[]{:S(2)}, u32[]{:S(2)}) collective-permute-start(bf16[80,2944]{1,0:T(8,128)(2,1)S(1)} %collective-permute-done.10.refs_4_), channel_id=1, source_target_pairs={{4,0},{8,4},{12,8},{14,12},{10,14},{6,10},{2,6},{0,2},{5,1},{9,5},... | collective-permute-start | bytes 1413128 | tf_op jit(solution)/shard_map/ppermute | solution.py:367
  39.9 9.4 %collective-permute-start.17 = (bf16[40,2944]{1,0:T(8,128)(2,1)S(1)}, bf16[40,2944]{1,0:T(8,128)(2,1)S(1)}, u32[]{:S(2)}, u32[]{:S(2)}) collective-permute-start(bf16[40,2944]{1,0:T(8,128)(2,1)S(1)} %get-tuple-element.116), channel_id=1, source_target_pairs={{0,4},{4,8},{8,12},{12,14},{14,10},{10,6},{6,2},{2,0},{1,5},{5,9},... | collective-permute-start | bytes 706568 | tf_op jit(solution)/shard_map/ppermute | solution.py:364
  40.7 10.2 %collective-permute-start.18 = (bf16[40,2944]{1,0:T(8,128)(2,1)S(1)}, bf16[40,2944]{1,0:T(8,128)(2,1)S(1)}, u32[]{:S(2)}, u32[]{:S(2)}) collective-permute-start(bf16[40,2944]{1,0:T(8,128)(2,1)S(1)} %get-tuple-element.115), channel_id=1, source_target_pairs={{4,0},{8,4},{12,8},{14,12},{10,14},{6,10},{2,6},{0,2},{5,1},{9,5},... | collective-permute-start | bytes 706568 | tf_op jit(solution)/shard_map/ppermute | solution.py:367
  49.3 13.4 %collective-permute-start.3 = (bf16[80,2944]{1,0:T(8,128)(2,1)S(1)}, bf16[80,2944]{1,0:T(8,128)(2,1)S(1)}, u32[]{:S(2)}, u32[]{:S(2)}) collective-permute-start(bf16[80,2944]{1,0:T(8,128)(2,1)S(1)} %get-tuple-element.63), channel_id=1, source_target_pairs={{0,16},{16,0},{1,17},{17,1},{2,18},{18,2},{3,19},{19,3},{4,20},{20... | collective-permute-start | bytes 1413128 | tf_op jit(solution)/shard_map/ppermute | solution.py:339
  50.9 6.8 %collective-permute-start.15 = (bf16[40,2944]{1,0:T(8,128)(2,1)S(1)}, bf16[40,2944]{1,0:T(8,128)(2,1)S(1)}, u32[]{:S(2)}, u32[]{:S(2)}) collective-permute-start(bf16[40,2944]{1,0:T(8,128)(2,1)S(1)} %slice.76), channel_id=1, source_target_pairs={{0,4},{4,8},{8,12},{12,14},{14,10},{10,6},{6,2},{2,0},{1,5},{5,9},... | collective-permute-start | bytes 706568 | tf_op jit(solution)/shard_map/ppermute | solution.py:364
  51.9 6.8 %collective-permute-start.16 = (bf16[40,2944]{1,0:T(8,128)(2,1)S(1)}, bf16[40,2944]{1,0:T(8,128)(2,1)S(1)}, u32[]{:S(2)}, u32[]{:S(2)}) collective-permute-start(bf16[40,2944]{1,0:T(8,128)(2,1)S(1)} %slice.77), channel_id=1, source_target_pairs={{4,0},{8,4},{12,8},{14,12},{10,14},{6,10},{2,6},{0,2},{5,1},{9,5},... | collective-permute-start | bytes 706568 | tf_op jit(solution)/shard_map/ppermute | solution.py:367
  53.2 9.5 %collective-permute-start.19 = (bf16[40,2944]{1,0:T(8,128)(2,1)S(1)}, bf16[40,2944]{1,0:T(8,128)(2,1)S(1)}, u32[]{:S(2)}, u32[]{:S(2)}) collective-permute-start(bf16[40,2944]{1,0:T(8,128)(2,1)S(1)} %get-tuple-element.114), channel_id=1, source_target_pairs={{0,4},{4,8},{8,12},{12,14},{14,10},{10,6},{6,2},{2,0},{1,5},{5,9},... | collective-permute-start | bytes 706568 | tf_op jit(solution)/shard_map/ppermute | solution.py:364
  54.2 8.5 %collective-permute-start.20 = (bf16[40,2944]{1,0:T(8,128)(2,1)S(1)}, bf16[40,2944]{1,0:T(8,128)(2,1)S(1)}, u32[]{:S(2)}, u32[]{:S(2)}) collective-permute-start(bf16[40,2944]{1,0:T(8,128)(2,1)S(1)} %get-tuple-element.113), channel_id=1, source_target_pairs={{4,0},{8,4},{12,8},{14,12},{10,14},{6,10},{2,6},{0,2},{5,1},{9,5},... | collective-permute-start | bytes 706568 | tf_op jit(solution)/shard_map/ppermute | solution.py:367
  57.7 5.0 %copy-start.2 = (f32[1,640]{1,0:T(1,128)S(1)}, f32[1,640]{1,0:T(1,128)}, u32[]{:S(2)}) copy-start(f32[1,640]{1,0:T(1,128)} %bias.1) | copy-start | bytes 7684
  57.7 11.5 %collective-permute-start.2 = (bf16[80,2944]{1,0:T(8,128)(2,1)S(1)}, bf16[80,2944]{1,0:T(8,128)(2,1)S(1)}, u32[]{:S(2)}, u32[]{:S(2)}) collective-permute-start(bf16[80,2944]{1,0:T(8,128)(2,1)S(1)} %get-tuple-element.62), channel_id=1, source_target_pairs={{0,16},{16,0},{1,17},{17,1},{2,18},{18,2},{3,19},{19,3},{4,20},{20... | collective-permute-start | bytes 1413128 | tf_op jit(solution)/shard_map/ppermute | solution.py:339
  58.7 21.0 %collective-permute-start.27 = (bf16[512,512]{1,0:T(8,128)(2,1)S(1)}, bf16[512,512]{1,0:T(8,128)(2,1)S(1)}, u32[]{:S(2)}, u32[]{:S(2)}) collective-permute-start(bf16[512,512]{1,0:T(8,128)(2,1)S(1)} %get-tuple-element.101), channel_id=1, source_target_pairs={{0,1},{1,0},{2,3},{3,2},{4,5},{5,4},{6,7},{7,6},{8,9},{9,8},{10,11... | collective-permute-start | bytes 1572872 | tf_op jit(solution)/shard_map/ppermute | solution.py:339
  62.7 2.4 %collective-permute-start.21 = (f32[3,640]{1,0:T(4,128)S(1)}, f32[3,640]{1,0:T(4,128)S(1)}, u32[]{:S(2)}, u32[]{:S(2)}) collective-permute-start(f32[3,640]{1,0:T(4,128)S(1)} %fusion.2), channel_id=1, source_target_pairs={{0,1},{1,0},{2,3},{3,2},{4,5},{5,4},{6,7},{7,6},{8,9},{9,8},{10,11... | collective-permute-start | bytes 23048 | tf_op jit(solution)/shard_map/ppermute | solution.py:339
  63.0 8.2 %collective-permute-start.23 = (bf16[40,2944]{1,0:T(8,128)(2,1)S(1)}, bf16[40,2944]{1,0:T(8,128)(2,1)S(1)}, u32[]{:S(2)}, u32[]{:S(2)}) collective-permute-start(bf16[40,2944]{1,0:T(8,128)(2,1)S(1)} %get-tuple-element.112), channel_id=1, source_target_pairs={{0,4},{4,8},{8,12},{12,14},{14,10},{10,6},{6,2},{2,0},{1,5},{5,9},... | collective-permute-start | bytes 706568 | tf_op jit(solution)/shard_map/ppermute | solution.py:364
  64.4 7.9 %collective-permute-start.24 = (bf16[40,2944]{1,0:T(8,128)(2,1)S(1)}, bf16[40,2944]{1,0:T(8,128)(2,1)S(1)}, u32[]{:S(2)}, u32[]{:S(2)}) collective-permute-start(bf16[40,2944]{1,0:T(8,128)(2,1)S(1)} %get-tuple-element.111), channel_id=1, source_target_pairs={{4,0},{8,4},{12,8},{14,12},{10,14},{6,10},{2,6},{0,2},{5,1},{9,5},... | collective-permute-start | bytes 706568 | tf_op jit(solution)/shard_map/ppermute | solution.py:367
  65.1 4.1 %collective-permute-start.22 = (f32[3,640]{1,0:T(4,128)S(1)}, f32[3,640]{1,0:T(4,128)S(1)}, u32[]{:S(2)}, u32[]{:S(2)}) collective-permute-start(f32[3,640]{1,0:T(4,128)S(1)} %fusion.5), channel_id=1, source_target_pairs={{0,16},{16,0},{1,17},{17,1},{2,18},{18,2},{3,19},{19,3},{4,20},{20... | collective-permute-start | bytes 23048 | tf_op jit(solution)/shard_map/ppermute | solution.py:388
  72.3 7.4 %collective-permute-start.26 = (bf16[512,256]{1,0:T(8,128)(2,1)S(1)}, bf16[512,256]{1,0:T(8,128)(2,1)S(1)}, u32[]{:S(2)}, u32[]{:S(2)}) collective-permute-start(bf16[512,256]{1,0:T(8,128)(2,1)S(1)} %shard_map.125), channel_id=1, source_target_pairs={{0,1},{1,0},{2,3},{3,2},{4,5},{5,4},{6,7},{7,6},{8,9},{9,8},{10,11... | collective-permute-start | bytes 786440 | tf_op jit(solution)/shard_map/ppermute | solution.py:339
  72.4 11.0 %collective-permute-start.25 = (bf16[40,2944]{1,0:T(8,128)(2,1)S(1)}, bf16[40,2944]{1,0:T(8,128)(2,1)S(1)}, u32[]{:S(2)}, u32[]{:S(2)}) collective-permute-start(bf16[40,2944]{1,0:T(8,128)(2,1)S(1)} %add_convert_fusion.1), channel_id=1, source_target_pairs={{0,4},{4,8},{8,12},{12,14},{14,10},{10,6},{6,2},{2,0},{1,5},{5,9},... | collective-permute-start | bytes 706568 | tf_op jit(solution)/shard_map/ppermute | solution.py:364
  73.8 5.9 %collective-permute-start.28 = (f32[3,640]{1,0:T(4,128)S(1)}, f32[3,640]{1,0:T(4,128)S(1)}, u32[]{:S(2)}, u32[]{:S(2)}) collective-permute-start(f32[3,640]{1,0:T(4,128)S(1)} %add.91), channel_id=1, source_target_pairs={{0,4},{4,0},{8,12},{12,8},{1,5},{5,1},{9,13},{13,9},{2,6},{6,2},{1... | collective-permute-start | bytes 23048 | tf_op jit(solution)/shard_map/ppermute | solution.py:388
  83.4 10.7 %copy-start = (f32[1,40,5760]{2,1,0:T(8,128)S(1)}, f32[1,40,5760]{2,1,0:T(8,128)}, u32[]{:S(2)}) copy-start(f32[1,40,5760]{2,1,0:T(8,128)} %param.10) | copy-start | bytes 2764804
  83.5 8.1 %collective-permute-start.29 = (bf16[40,2944]{1,0:T(8,128)(2,1)S(1)}, bf16[40,2944]{1,0:T(8,128)(2,1)S(1)}, u32[]{:S(2)}, u32[]{:S(2)}) collective-permute-start(bf16[40,2944]{1,0:T(8,128)(2,1)S(1)} %add_convert_fusion), channel_id=1, source_target_pairs={{0,16},{16,0},{1,17},{17,1},{2,18},{18,2},{3,19},{19,3},{4,20},{20... | collective-permute-start | bytes 706568 | tf_op jit(solution)/shard_map/ppermute | solution.py:339
  85.2 3.7 %collective-permute-start.31 = (f32[3,640]{1,0:T(4,128)S(1)}, f32[3,640]{1,0:T(4,128)S(1)}, u32[]{:S(2)}, u32[]{:S(2)}) collective-permute-start(f32[3,640]{1,0:T(4,128)S(1)} %add.98), channel_id=1, source_target_pairs={{0,2},{2,0},{1,3},{3,1},{4,6},{6,4},{5,7},{7,5},{8,10},{10,8},{9,1... | collective-permute-start | bytes 23048 | tf_op jit(solution)/shard_map/ppermute | solution.py:388
  88.9 4.6 %collective-permute-start.32 = (f32[3,640]{1,0:T(4,128)S(1)}, f32[3,640]{1,0:T(4,128)S(1)}, u32[]{:S(2)}, u32[]{:S(2)}) collective-permute-start(f32[3,640]{1,0:T(4,128)S(1)} %add.102), channel_id=1, source_target_pairs={{0,8},{4,12},{8,0},{12,4},{1,9},{5,13},{9,1},{13,5},{2,10},{6,14},... | collective-permute-start | bytes 23048 | tf_op jit(solution)/shard_map/ppermute | solution.py:388
  91.6 2.4 %collective-permute-start.30 = (bf16[40,2944]{1,0:T(8,128)(2,1)S(1)}, bf16[40,2944]{1,0:T(8,128)(2,1)S(1)}, u32[]{:S(2)}, u32[]{:S(2)}) collective-permute-start(bf16[40,2944]{1,0:T(8,128)(2,1)S(1)} %get-tuple-element.121), channel_id=1, source_target_pairs={{0,1},{1,0},{2,3},{3,2},{4,5},{5,4},{6,7},{7,6},{8,9},{9,8},{10,11... | collective-permute-start | bytes 706568 | tf_op jit(solution)/shard_map/ppermute | solution.py:339

commit v20 on v10

--- a/solution.py
+++ b/solution.py
@@ -546,11 +546,12 @@
             received = ring_step(j, *received)
         late += halves
 
+        conv_send = conv_far(acts, late)
+        cots, conv_send = tied(cots, conv_send)
+        conv_got = swap(conv_send, "core")
         sums = back(1, cots, slopes, late)
         crossed[-2], sums, *received = tied(crossed[-2], sums, *received)
-        acts_last, *_ = tied(acts, sums, *received)
         received = ring_step(zs - 2, *received)
-        conv_got = swap(conv_far(acts_last, late), "core")
         vectors = hop(chip_sum(first_sums + sums), "replica", 1)
         crossed[-1], conv_got, vectors, *received = tied(crossed[-1], conv_got, vectors, *received)
         last, behind = ring_step(zs - 1, *received)

time: 92.5 us -> 92.1 us (level)
  starting transfers between devices: 33.5 us -> 31.3 us
  waiting for transfers between devices: 20.1 us -> 21.8 us
    ppermute x7, starting transfers between devices: 7.41 us -> 2.77 us  [down(): return lax.ppermute(value, NODE, self.behind)]
    ppermute x8, starting transfers between devices: 9.16 us -> 13.7 us  [up(): return lax.ppermute(value, NODE, self.ahead)]
    ppermute x8, waiting for transfers between devices: 7.34 us -> 10.7 us  [up(): return lax.ppermute(value, NODE, self.ahead)]
    ppermute x7, waiting for transfers between devices: 4.63 us -> 2.49 us  [down(): return lax.ppermute(value, NODE, self.behind)]
    ppermute x4, starting transfers between devices: 7 us -> 5.22 us  [hop(): lax.ppermute(value, axis, [(s, s ^ mask) for s in range(count)])]
    ppermute x4, waiting for transfers between devices: 5.57 us -> 6.88 us  [hop(): lax.ppermute(value, axis, [(s, s ^ mask) for s in range(count)])]
  transfers between devices with their start and end apart: 33 -> 33, of which waited for: 13 -> 12; matrix products, arithmetic and copies ran while one was open for 4% -> 4% of each run, Pallas kernels for 34% -> 34%
where the time goes in v20:
time: 92.1 us; the launch traced here: 91.9 us
  Pallas kernels  32.4 us (35%)
  starting transfers between devices  31.3 us (34%)
  waiting for transfers between devices  21.8 us (24%)
  other arithmetic  2.88 us (3%)
  local copies, waits for them, and re-layouts  1.94 us (2%)
  between operations  1.58 us (2%)
    ppermute x8, starting transfers between devices, up(): return lax.ppermute(value, NODE, self.ahead)  13.7 us
    ppermute x8, waiting for transfers between devices, up(): return lax.ppermute(value, NODE, self.ahead)  10.7 us
    ppermute x14, starting transfers between devices, swap(): return lax.ppermute(value, axis, [(0, 1), (1, 0)])  9.61 us
    pallas_call x2, Pallas kernels, back(): call(partial(back_kernel, cols, stages, stage), jax.ShapeDtypeStruct((2,...  8.62 us
    ppermute x4, waiting for transfers between devices, hop(): lax.ppermute(value, axis, [(s, s ^ mask) for s in range(count)])  6.88 us
    ppermute x4, starting transfers between devices, hop(): lax.ppermute(value, axis, [(s, s ^ mask) for s in range(count)])  5.22 us
    pallas_call x1, Pallas kernels, per_device(): call(partial(grad_kernel, cols), [jax.ShapeDtypeStruct((n * 2 * part, col...  4.64 us
    pallas_call x1, Pallas kernels, slopes_of(): call(partial(slope_kernel, stages), (jax.ShapeDtypeStruct((3, 2 * half +...  4.48 us
  transfers between devices with their start and end apart: 33, of which 12 were waited for; matrix products, arithmetic and copies ran while one was open for 4% of the time, Pallas kernels for 34%

profile of v20, /device:TPU:0, one launch (start us, length us, event | category | flops | bytes accessed | tf_op | source)
XLA Modules:
  0.0 91.9 jit_solution(164387837003840947)
XLA Ops:
  0.7 1.3 %fusion = (bf16[40,2944]{1,0:T(8,128)(2,1)S(1)}, bf16[40,2944]{1,0:T(8,128)(2,1)S(1)}) fusion(f32[1,40,5760]{2,1,0:T(8,128)} %param.10, s32[]{:T(128)S(6)} %select_n.27, s32[]{:T(128)S(6)} %select_n.28), kind=kLoop, calls=%fused_computation.12 | loop fusion | bytes 942088 | tf_op jit(solution)/shard_map/convert_element_type | solution.py:419
  2.0 0.5 collective-permute-start.3
  2.5 2.0 %fusion.3 = (f32[640]{0:T(1024)S(1)}, bf16[16,32,640]{2,1,0:T(8,128)(2,1)S(1)}) fusion(f32[1,16,32,640]{3,2,1,0:T(8,128)} %param.9), kind=kLoop, calls=%fused_computation.20 | loop fusion | flops 654720 | bytes 1968640 | tf_op jit(solution)/shard_map/reduce_sum | solution.py:512
  4.6 0.5 collective-permute-start
  5.1 2.7 %collective-permute-start.4 = (bf16[80,2944]{1,0:T(8,128)(2,1)S(1)}, bf16[80,2944]{1,0:T(8,128)(2,1)S(1)}, u32[]{:S(2)}, u32[]{:S(2)}) collective-permute-start(bf16[80,2944]{1,0:T(8,128)(2,1)S(1)} %maximum_select_fusion.refs_0_), channel_id=1, source_target_pairs={{0,4},{4,8},{8,12},{12,14},{14,10},{10,6},{6,2},{2,0},{1,5},{5,9},... | collective-permute-start | bytes 1413128 | tf_op jit(solution)/shard_map/ppermute | solution.py:364
  7.8 1.9 %collective-permute-start.6 = (bf16[40,2944]{1,0:T(8,128)(2,1)S(1)}, bf16[40,2944]{1,0:T(8,128)(2,1)S(1)}, u32[]{:S(2)}, u32[]{:S(2)}) collective-permute-start(bf16[40,2944]{1,0:T(8,128)(2,1)S(1)} %get-tuple-element.121), channel_id=1, source_target_pairs={{0,16},{16,0},{1,17},{17,1},{2,18},{18,2},{3,19},{19,3},{4,20},{20... | collective-permute-start | bytes 706568 | tf_op jit(solution)/shard_map/ppermute | solution.py:339
  9.9 4.4 %shard_map.119 = (f32[2,640]{1,0:T(2,128)S(1)}, bf16[3,34,32,640]{3,2,1,0:T(8,128)(2,1)S(1)}, bf16[640,1024]{1,0:T(8,128)(2,1)S(1)}) custom-call(s32[1]{0:T(128)} %bitcast.dev, s32[32,24]{1,0:T(8,128)S(1)} %copy-done.5, bf16[16,32,640]{2,1,0:T(8,128)(2,1)S(1)} %bitcast.13, bf16[16,32,640]{2,1,0:T(8,128)(2,1)S(1)} %collective-permute-done.lat_far, ...), custom_call_target="tpu_custom_call" | custom-call | flops 964689920 | tf_op jit(solution)/shard_map/pallas_call | solution.py:450
  14.3 4.6 %shard_map.120 = (bf16[320,2944]{1,0:T(8,128)(2,1)S(1)}, bf16[80,2944]{1,0:T(8,128)(2,1)S(1)}, bf16[80,2944]{1,0:T(8,128)(2,1)S(1)}, bf16[80,2944]{1,0:T(8,128)(2,1)S(1)}, bf16[80,2944]{1,0:T(8,128)(2,1)S(1)}) custom-call(s32[1]{0:T(128)} %bitcast.dev, bf16[3,34,32,640]{3,2,1,0:T(8,128)(2,1)S(1)} %get-tuple-element.60.acts, ...), custom_call_target="tpu_custom_call" | custom-call | flops 1929379840 | tf_op jit(solution)/shard_map/pallas_call | solution.py:458
  19.0 1.7 %collective-permute-done.7.theirs = bf16[40,2944]{1,0:T(8,128)(2,1)S(1)} collective-permute-done((bf16[40,2944]{1,0:T(8,128)(2,1)S(1)}, bf16[40,2944]{1,0:T(8,128)(2,1)S(1)}, u32[]{:S(2)}, u32[]{:S(2)}) %collective-permute-start.7) | collective-permute-done | bytes 235552 | tf_op jit(solution)/shard_map/ppermute | solution.py:339
  20.7 1.7 %collective-permute-start.8 = (bf16[80,2944]{1,0:T(8,128)(2,1)S(1)}, bf16[80,2944]{1,0:T(8,128)(2,1)S(1)}, u32[]{:S(2)}, u32[]{:S(2)}) collective-permute-start(bf16[80,2944]{1,0:T(8,128)(2,1)S(1)} %collective-permute-done.4.refs_1_), channel_id=1, source_target_pairs={{0,4},{4,8},{8,12},{12,14},{14,10},{10,6},{6,2},{2,0},{1,5},{5,9},... | collective-permute-start | bytes 1413128 | tf_op jit(solution)/shard_map/ppermute | solution.py:364
  22.7 1.7 %collective-permute-start.10 = (bf16[80,2944]{1,0:T(8,128)(2,1)S(1)}, bf16[80,2944]{1,0:T(8,128)(2,1)S(1)}, u32[]{:S(2)}, u32[]{:S(2)}) collective-permute-start(bf16[80,2944]{1,0:T(8,128)(2,1)S(1)} %get-tuple-element.75), channel_id=1, source_target_pairs={{0,16},{16,0},{1,17},{17,1},{2,18},{18,2},{3,19},{19,3},{4,20},{20... | collective-permute-start | bytes 1413128 | tf_op jit(solution)/shard_map/ppermute | solution.py:339
  24.7 4.5 %shard_map.121 = (bf16[3,34,32,768]{3,2,1,0:T(8,128)(2,1)S(1)}, bf16[32,32,640]{2,1,0:T(8,128)(2,1)S(1)}, bf16[32,32,640]{2,1,0:T(8,128)(2,1)S(1)}, bf16[640,768]{1,0:T(8,128)(2,1)S(1)}) custom-call(s32[1]{0:T(128)} %bitcast.dev, s32[32,24]{1,0:T(8,128)S(1)} %copy-done.5, f32[2,640]{1,0:T(2,128)S(1)} %get-tuple-element.69.stats, f32[1,640]{1,0:T(1,128)S(1)} %copy-done.3, ...), custom_call_target="tpu_custom_call" | custom-call | flops 964689920 | tf_op jit(solution)/shard_map/pallas_call | solution.py:470
  29.2 3.5 %collective-permute-done.8.refs_3_ = bf16[80,2944]{1,0:T(8,128)(2,1)S(1)} collective-permute-done((bf16[80,2944]{1,0:T(8,128)(2,1)S(1)}, bf16[80,2944]{1,0:T(8,128)(2,1)S(1)}, u32[]{:S(2)}, u32[]{:S(2)}) %collective-permute-start.8) | collective-permute-done | bytes 471072 | tf_op jit(solution)/shard_map/ppermute | solution.py:364
  32.7 1.3 %collective-permute-done.9.refs_4_ = bf16[80,2944]{1,0:T(8,128)(2,1)S(1)} collective-permute-done((bf16[80,2944]{1,0:T(8,128)(2,1)S(1)}, bf16[80,2944]{1,0:T(8,128)(2,1)S(1)}, u32[]{:S(2)}, u32[]{:S(2)}) %collective-permute-start.9) | collective-permute-done | bytes 471072 | tf_op jit(solution)/shard_map/ppermute | solution.py:367
  34.0 1.6 %collective-permute-start.11 = (bf16[80,2944]{1,0:T(8,128)(2,1)S(1)}, bf16[80,2944]{1,0:T(8,128)(2,1)S(1)}, u32[]{:S(2)}, u32[]{:S(2)}) collective-permute-start(bf16[80,2944]{1,0:T(8,128)(2,1)S(1)} %collective-permute-done.8.refs_3_), channel_id=1, source_target_pairs={{0,4},{4,8},{8,12},{12,14},{14,10},{10,6},{6,2},{2,0},{1,5},{5,9},... | collective-permute-start | bytes 1413128 | tf_op jit(solution)/shard_map/ppermute | solution.py:364
  35.6 0.4 collective-permute-start.12
  36.0 4.0 %shard_map.122 = (f32[512,512]{1,0:T(8,128)S(1)}, bf16[512,512]{1,0:T(8,128)(2,1)S(1)}) custom-call(s32[1]{0:T(128)} %bitcast.dev, bf16[3,34,32,640]{3,2,1,0:T(8,128)(2,1)S(1)} %get-tuple-element.60.acts, bf16[80,2944]{1,0:T(8,128)(2,1)S(1)} %maximum_select_fusion.refs_0_, bf16[80,2944]{1,0:T(8,128)(2,1)S(1)} %collective-permute-done.4.refs_1_, ...), custom_call_target="tpu_custom_call" | custom-call | flops 964689920 | tf_op jit(solution)/shard_map/pallas_call | solution.py:488
  40.1 1.6 %collective-permute-start.18 = (bf16[40,2944]{1,0:T(8,128)(2,1)S(1)}, bf16[40,2944]{1,0:T(8,128)(2,1)S(1)}, u32[]{:S(2)}, u32[]{:S(2)}) collective-permute-start(bf16[40,2944]{1,0:T(8,128)(2,1)S(1)} %get-tuple-element.118), channel_id=1, source_target_pairs={{0,4},{4,8},{8,12},{12,14},{14,10},{10,6},{6,2},{2,0},{1,5},{5,9},... | collective-permute-start | bytes 706568 | tf_op jit(solution)/shard_map/ppermute | solution.py:364
  41.8 0.5 collective-permute-start.19
  42.2 5.4 %shard_map.123 = f32[2,640]{1,0:T(2,128)S(1)} custom-call(s32[1]{0:T(128)} %bitcast.dev, bf16[3,34,32,768]{3,2,1,0:T(8,128)(2,1)S(1)} %get-tuple-element.89.cots, bf16[32,32,640]{2,1,0:T(8,128)(2,1)S(1)} %get-tuple-element.81.slope, bf16[32,32,640]{2,1,0:T(8,128)(2,1)S(1)} %get-tuple-element.82.slope_x, bf16[80,2944]{1,0:T(8,128)(2,1)S(1)} %maximum_select_fusion.refs_0_, ...), custom_call_target="tpu_custom_call" | custom-call | flops 964689920 | tf_op jit(solution)/shard_map/pallas_call | solution.py:480
  47.6 2.0 %collective-permute-done.18 = bf16[40,2944]{1,0:T(8,128)(2,1)S(1)} collective-permute-done((bf16[40,2944]{1,0:T(8,128)(2,1)S(1)}, bf16[40,2944]{1,0:T(8,128)(2,1)S(1)}, u32[]{:S(2)}, u32[]{:S(2)}) %collective-permute-start.18) | collective-permute-done | bytes 235552 | tf_op jit(solution)/shard_map/ppermute | solution.py:364
  49.7 1.5 %collective-permute-start.17 = (bf16[80,2944]{1,0:T(8,128)(2,1)S(1)}, bf16[80,2944]{1,0:T(8,128)(2,1)S(1)}, u32[]{:S(2)}, u32[]{:S(2)}) collective-permute-start(bf16[80,2944]{1,0:T(8,128)(2,1)S(1)} %get-tuple-element.88), channel_id=1, source_target_pairs={{0,16},{16,0},{1,17},{17,1},{2,18},{18,2},{3,19},{19,3},{4,20},{20... | collective-permute-start | bytes 1413128 | tf_op jit(solution)/shard_map/ppermute | solution.py:339
  51.2 1.6 %collective-permute-start.14 = (bf16[40,2944]{1,0:T(8,128)(2,1)S(1)}, bf16[40,2944]{1,0:T(8,128)(2,1)S(1)}, u32[]{:S(2)}, u32[]{:S(2)}) collective-permute-start(bf16[40,2944]{1,0:T(8,128)(2,1)S(1)} %slice.76), channel_id=1, source_target_pairs={{0,4},{4,8},{8,12},{12,14},{14,10},{10,6},{6,2},{2,0},{1,5},{5,9},... | collective-permute-start | bytes 706568 | tf_op jit(solution)/shard_map/ppermute | solution.py:364
  52.9 0.5 collective-permute-start.15
  53.6 1.6 %collective-permute-start.20 = (bf16[40,2944]{1,0:T(8,128)(2,1)S(1)}, bf16[40,2944]{1,0:T(8,128)(2,1)S(1)}, u32[]{:S(2)}, u32[]{:S(2)}) collective-permute-start(bf16[40,2944]{1,0:T(8,128)(2,1)S(1)} %get-tuple-element.116), channel_id=1, source_target_pairs={{0,4},{4,8},{8,12},{12,14},{14,10},{10,6},{6,2},{2,0},{1,5},{5,9},... | collective-permute-start | bytes 706568 | tf_op jit(solution)/shard_map/ppermute | solution.py:364
  55.2 0.5 collective-permute-start.21
  55.6 2.5 %collective-permute-done.14.refs_2_.refs_5_ = bf16[40,2944]{1,0:T(8,128)(2,1)S(1)} collective-permute-done((bf16[40,2944]{1,0:T(8,128)(2,1)S(1)}, bf16[40,2944]{1,0:T(8,128)(2,1)S(1)}, u32[]{:S(2)}, u32[]{:S(2)}) %collective-permute-start.14) | collective-permute-done | bytes 235552 | tf_op jit(solution)/shard_map/ppermute | solution.py:364
  58.2 1.3 %collective-permute-start.2 = (bf16[80,2944]{1,0:T(8,128)(2,1)S(1)}, bf16[80,2944]{1,0:T(8,128)(2,1)S(1)}, u32[]{:S(2)}, u32[]{:S(2)}) collective-permute-start(bf16[80,2944]{1,0:T(8,128)(2,1)S(1)} %get-tuple-element.63), channel_id=1, source_target_pairs={{0,16},{16,0},{1,17},{17,1},{2,18},{18,2},{3,19},{19,3},{4,20},{20... | collective-permute-start | bytes 1413128 | tf_op jit(solution)/shard_map/ppermute | solution.py:339
  59.6 1.4 %shard_map.124 = bf16[512,256]{1,0:T(8,128)(2,1)S(1)} custom-call(s32[1]{0:T(128)} %bitcast.dev, bf16[3,34,32,640]{3,2,1,0:T(8,128)(2,1)S(1)} %get-tuple-element.60.acts, bf16[80,2944]{1,0:T(8,128)(2,1)S(1)} %collective-permute-done.11.refs_0_.refs_3_, bf16[80,2944]{1,0:T(8,128)(2,1)S(1)} %collective-permute-done.12.refs_1_.refs_4_, ...), custom_call_target="tpu_custom_call" | custom-call | flops 482344960 | tf_op jit(solution)/shard_map/pallas_call | solution.py:497
  61.0 3.2 %shard_map.125 = f32[2,640]{1,0:T(2,128)S(1)} custom-call(s32[1]{0:T(128)} %bitcast.dev, bf16[3,34,32,768]{3,2,1,0:T(8,128)(2,1)S(1)} %get-tuple-element.89.cots, bf16[32,32,640]{2,1,0:T(8,128)(2,1)S(1)} %get-tuple-element.81.slope, bf16[32,32,640]{2,1,0:T(8,128)(2,1)S(1)} %get-tuple-element.82.slope_x, ...), custom_call_target="tpu_custom_call" | custom-call | flops 964689920 | tf_op jit(solution)/shard_map/pallas_call | solution.py:480
  64.4 0.5 collective-permute-start.16
  65.1 1.5 %collective-permute-start.24 = (bf16[40,2944]{1,0:T(8,128)(2,1)S(1)}, bf16[40,2944]{1,0:T(8,128)(2,1)S(1)}, u32[]{:S(2)}, u32[]{:S(2)}) collective-permute-start(bf16[40,2944]{1,0:T(8,128)(2,1)S(1)} %get-tuple-element.114), channel_id=1, source_target_pairs={{0,4},{4,8},{8,12},{12,14},{14,10},{10,6},{6,2},{2,0},{1,5},{5,9},... | collective-permute-start | bytes 706568 | tf_op jit(solution)/shard_map/ppermute | solution.py:364
  66.5 0.6 collective-permute-start.25
  67.2 1.2 %collective-permute-start.23 = (f32[3,640]{1,0:T(4,128)S(1)}, f32[3,640]{1,0:T(4,128)S(1)}, u32[]{:S(2)}, u32[]{:S(2)}) collective-permute-start(f32[3,640]{1,0:T(4,128)S(1)} %fusion.5), channel_id=1, source_target_pairs={{0,16},{16,0},{1,17},{17,1},{2,18},{18,2},{3,19},{19,3},{4,20},{20... | collective-permute-start | bytes 23048 | tf_op jit(solution)/shard_map/ppermute | solution.py:388
  68.4 2.6 %collective-permute-done.23 = f32[3,640]{1,0:T(4,128)S(1)} collective-permute-done((f32[3,640]{1,0:T(4,128)S(1)}, f32[3,640]{1,0:T(4,128)S(1)}, u32[]{:S(2)}, u32[]{:S(2)}) %collective-permute-start.23) | collective-permute-done | bytes 7712 | tf_op jit(solution)/shard_map/ppermute | solution.py:388
  70.9 1.9 %collective-permute-done.24 = bf16[40,2944]{1,0:T(8,128)(2,1)S(1)} collective-permute-done((bf16[40,2944]{1,0:T(8,128)(2,1)S(1)}, bf16[40,2944]{1,0:T(8,128)(2,1)S(1)}, u32[]{:S(2)}, u32[]{:S(2)}) %collective-permute-start.24) | collective-permute-done | bytes 235552 | tf_op jit(solution)/shard_map/ppermute | solution.py:364
  72.9 1.1 %collective-permute-done.25 = bf16[40,2944]{1,0:T(8,128)(2,1)S(1)} collective-permute-done((bf16[40,2944]{1,0:T(8,128)(2,1)S(1)}, bf16[40,2944]{1,0:T(8,128)(2,1)S(1)}, u32[]{:S(2)}, u32[]{:S(2)}) %collective-permute-start.25) | collective-permute-done | bytes 235552 | tf_op jit(solution)/shard_map/ppermute | solution.py:367
  74.1 1.3 %collective-permute-start.26 = (bf16[40,2944]{1,0:T(8,128)(2,1)S(1)}, bf16[40,2944]{1,0:T(8,128)(2,1)S(1)}, u32[]{:S(2)}, u32[]{:S(2)}) collective-permute-start(bf16[40,2944]{1,0:T(8,128)(2,1)S(1)} %add_convert_fusion.1), channel_id=1, source_target_pairs={{0,4},{4,8},{8,12},{12,14},{14,10},{10,6},{6,2},{2,0},{1,5},{5,9},... | collective-permute-start | bytes 706568 | tf_op jit(solution)/shard_map/ppermute | solution.py:364
  75.4 0.9 collective-permute-start.28
  76.3 3.7 %shard_map.126 = bf16[16,32,640]{2,1,0:T(8,128)(2,1)} custom-call(s32[1]{0:T(128)} %bitcast.dev, bf16[3,34,32,640]{3,2,1,0:T(8,128)(2,1)S(1)} %get-tuple-element.60.acts, bf16[512,256]{1,0:T(8,128)(2,1)S(1)} %collective-permute-done.16.got, bf16[16,32,640]{2,1,0:T(8,128)(2,1)S(1)} %bitcast.15, f32[1,640]{1,0:T(1,128)S(1)} %copy-done.2, ...), custom_call_target="tpu_custom_call" | custom-call | flops 964689920 | tf_op jit(solution)/shard_map/pallas_call | solution.py:505
  80.0 0.7 collective-permute-done.26
  80.8 1.0 %collective-permute-start.29 = (bf16[40,2944]{1,0:T(8,128)(2,1)S(1)}, bf16[40,2944]{1,0:T(8,128)(2,1)S(1)}, u32[]{:S(2)}, u32[]{:S(2)}) collective-permute-start(bf16[40,2944]{1,0:T(8,128)(2,1)S(1)} %add_convert_fusion), channel_id=1, source_target_pairs={{0,16},{16,0},{1,17},{17,1},{2,18},{18,2},{3,19},{19,3},{4,20},{20... | collective-permute-start | bytes 706568 | tf_op jit(solution)/shard_map/ppermute | solution.py:339
  81.9 1.0 %collective-permute-start.31 = (f32[3,640]{1,0:T(4,128)S(1)}, f32[3,640]{1,0:T(4,128)S(1)}, u32[]{:S(2)}, u32[]{:S(2)}) collective-permute-start(f32[3,640]{1,0:T(4,128)S(1)} %add.98), channel_id=1, source_target_pairs={{0,2},{2,0},{1,3},{3,1},{4,6},{6,4},{5,7},{7,5},{8,10},{10,8},{9,1... | collective-permute-start | bytes 23048 | tf_op jit(solution)/shard_map/ppermute | solution.py:388
  83.5 2.0 %collective-permute-done.31 = f32[3,640]{1,0:T(4,128)S(1)} collective-permute-done((f32[3,640]{1,0:T(4,128)S(1)}, f32[3,640]{1,0:T(4,128)S(1)}, u32[]{:S(2)}, u32[]{:S(2)}) %collective-permute-start.31) | collective-permute-done | bytes 7712 | tf_op jit(solution)/shard_map/ppermute | solution.py:388
  85.6 2.2 %collective-permute-start.32 = (f32[3,640]{1,0:T(4,128)S(1)}, f32[3,640]{1,0:T(4,128)S(1)}, u32[]{:S(2)}, u32[]{:S(2)}) collective-permute-start(f32[3,640]{1,0:T(4,128)S(1)} %add.102), channel_id=1, source_target_pairs={{0,8},{4,12},{8,0},{12,4},{1,9},{5,13},{9,1},{13,5},{2,10},{6,14},... | collective-permute-start | bytes 23048 | tf_op jit(solution)/shard_map/ppermute | solution.py:388
  87.8 2.3 %collective-permute-done.32 = f32[3,640]{1,0:T(4,128)S(1)} collective-permute-done((f32[3,640]{1,0:T(4,128)S(1)}, f32[3,640]{1,0:T(4,128)S(1)}, u32[]{:S(2)}, u32[]{:S(2)}) %collective-permute-start.32) | collective-permute-done | bytes 7712 | tf_op jit(solution)/shard_map/ppermute | solution.py:388
  90.1 0.6 fusion.4
  90.7 1.2 %shard_map.127 = f32[40,5760]{1,0:T(8,128)} custom-call(s32[1]{0:T(128)} %bitcast.dev, s32[1]{0:T(128)S(6)} %copy.13.step, f32[40,5760]{1,0:T(8,128)S(1)} %bitcast.11, bf16[40,2944]{1,0:T(8,128)(2,1)S(1)} %collective-permute-done.6.mine, bf16[40,2944]{1,0:T(8,128)(2,1)S(1)} %collective-permute-done.7.theirs, bf16[40,2944]{1,0:T(8,128)(2,1)S(1)} %get-tuple-element.124.ours, ...), custom_call_target="tpu_custom_call" | custom-call | flops 241172480 | tf_op jit(solution)/shard_map/pallas_call | solution.py:565
  (59 shorter events, 2.1 us)
Async XLA Ops:
  0.6 3.9 %copy-start.1 = (bf16[1,16,32,640]{3,2,1,0:T(8,128)(2,1)S(1)}, bf16[1,16,32,640]{3,2,1,0:T(8,128)(2,1)}, u32[]{:S(2)}) copy-start(bf16[1,16,32,640]{3,2,1,0:T(8,128)(2,1)} %param.8) | copy-start | bytes 1966084
  0.7 9.2 %copy-start.3 = (f32[1,640]{1,0:T(1,128)S(1)}, f32[1,640]{1,0:T(1,128)}, u32[]{:S(2)}) copy-start(f32[1,640]{1,0:T(1,128)} %gain.3) | copy-start | bytes 7684
  0.7 9.2 %copy-start.4 = (f32[1,640]{1,0:T(1,128)S(1)}, f32[1,640]{1,0:T(1,128)}, u32[]{:S(2)}) copy-start(f32[1,640]{1,0:T(1,128)} %shift.3) | copy-start | bytes 7684
  0.7 9.2 %copy-start.5 = (s32[32,24]{1,0:T(8,128)S(1)}, s32[32,24]{1,0:T(8,128)}, u32[]{:S(2)}) copy-start(s32[32,24]{1,0:T(8,128)} %constant.40.clone.table) | copy-start | bytes 9220
  2.0 3.1 %collective-permute-start.3 = (bf16[40,2944]{1,0:T(8,128)(2,1)S(1)}, bf16[40,2944]{1,0:T(8,128)(2,1)S(1)}, u32[]{:S(2)}, u32[]{:S(2)}) collective-permute-start(bf16[40,2944]{1,0:T(8,128)(2,1)S(1)} %get-tuple-element.122), channel_id=1, source_target_pairs={{0,1},{1,0},{2,3},{3,2},{4,5},{5,4},{6,7},{7,6},{8,9},{9,8},{10,11... | collective-permute-start | bytes 706568 | tf_op jit(solution)/shard_map/ppermute | solution.py:339
  4.5 5.3 %collective-permute-start.1 = (bf16[16,32,640]{2,1,0:T(8,128)(2,1)S(1)}, bf16[16,32,640]{2,1,0:T(8,128)(2,1)S(1)}, u32[]{:S(2)}, u32[]{:S(2)}) collective-permute-start(bf16[16,32,640]{2,1,0:T(8,128)(2,1)S(1)} %get-tuple-element.120.cot_own), channel_id=1, source_target_pairs={{0,1},{1,0},{2,3},{3,2},{4,5},{5,4},{6,7},{7,6},{8,9},{9,8},{10,11... | collective-permute-start | bytes 1966088 | tf_op jit(solution)/shard_map/ppermute | solution.py:339
  4.6 5.3 %collective-permute-start = (bf16[16,32,640]{2,1,0:T(8,128)(2,1)S(1)}, bf16[16,32,640]{2,1,0:T(8,128)(2,1)S(1)}, u32[]{:S(2)}, u32[]{:S(2)}) collective-permute-start(bf16[16,32,640]{2,1,0:T(8,128)(2,1)S(1)} %bitcast.12), channel_id=1, source_target_pairs={{0,1},{1,0},{2,3},{3,2},{4,5},{5,4},{6,7},{7,6},{8,9},{9,8},{10,11... | collective-permute-start | bytes 1966088 | tf_op jit(solution)/shard_map/ppermute | solution.py:339
  5.1 15.6 %collective-permute-start.4 = (bf16[80,2944]{1,0:T(8,128)(2,1)S(1)}, bf16[80,2944]{1,0:T(8,128)(2,1)S(1)}, u32[]{:S(2)}, u32[]{:S(2)}) collective-permute-start(bf16[80,2944]{1,0:T(8,128)(2,1)S(1)} %maximum_select_fusion.refs_0_), channel_id=1, source_target_pairs={{0,4},{4,8},{8,12},{12,14},{14,10},{10,6},{6,2},{2,0},{1,5},{5,9},... | collective-permute-start | bytes 1413128 | tf_op jit(solution)/shard_map/ppermute | solution.py:364
  7.8 12.9 %collective-permute-start.5 = (bf16[80,2944]{1,0:T(8,128)(2,1)S(1)}, bf16[80,2944]{1,0:T(8,128)(2,1)S(1)}, u32[]{:S(2)}, u32[]{:S(2)}) collective-permute-start(bf16[80,2944]{1,0:T(8,128)(2,1)S(1)} %maximum_select_fusion.refs_0_), channel_id=1, source_target_pairs={{4,0},{8,4},{12,8},{14,12},{10,14},{6,10},{2,6},{0,2},{5,1},{9,5},... | collective-permute-start | bytes 1413128 | tf_op jit(solution)/shard_map/ppermute | solution.py:367
  7.8 11.1 %collective-permute-start.6 = (bf16[40,2944]{1,0:T(8,128)(2,1)S(1)}, bf16[40,2944]{1,0:T(8,128)(2,1)S(1)}, u32[]{:S(2)}, u32[]{:S(2)}) collective-permute-start(bf16[40,2944]{1,0:T(8,128)(2,1)S(1)} %get-tuple-element.121), channel_id=1, source_target_pairs={{0,16},{16,0},{1,17},{17,1},{2,18},{18,2},{3,19},{19,3},{4,20},{20... | collective-permute-start | bytes 706568 | tf_op jit(solution)/shard_map/ppermute | solution.py:339
  9.8 10.9 %collective-permute-start.7 = (bf16[40,2944]{1,0:T(8,128)(2,1)S(1)}, bf16[40,2944]{1,0:T(8,128)(2,1)S(1)}, u32[]{:S(2)}, u32[]{:S(2)}) collective-permute-start(bf16[40,2944]{1,0:T(8,128)(2,1)S(1)} %get-tuple-element.122), channel_id=1, source_target_pairs={{0,16},{16,0},{1,17},{17,1},{2,18},{18,2},{3,19},{19,3},{4,20},{20... | collective-permute-start | bytes 706568 | tf_op jit(solution)/shard_map/ppermute | solution.py:339
  20.7 12.0 %collective-permute-start.8 = (bf16[80,2944]{1,0:T(8,128)(2,1)S(1)}, bf16[80,2944]{1,0:T(8,128)(2,1)S(1)}, u32[]{:S(2)}, u32[]{:S(2)}) collective-permute-start(bf16[80,2944]{1,0:T(8,128)(2,1)S(1)} %collective-permute-done.4.refs_1_), channel_id=1, source_target_pairs={{0,4},{4,8},{8,12},{12,14},{14,10},{10,6},{6,2},{2,0},{1,5},{5,9},... | collective-permute-start | bytes 1413128 | tf_op jit(solution)/shard_map/ppermute | solution.py:364
  22.4 11.6 %collective-permute-start.9 = (bf16[80,2944]{1,0:T(8,128)(2,1)S(1)}, bf16[80,2944]{1,0:T(8,128)(2,1)S(1)}, u32[]{:S(2)}, u32[]{:S(2)}) collective-permute-start(bf16[80,2944]{1,0:T(8,128)(2,1)S(1)} %collective-permute-done.5.refs_2_), channel_id=1, source_target_pairs={{4,0},{8,4},{12,8},{14,12},{10,14},{6,10},{2,6},{0,2},{5,1},{9,5},... | collective-permute-start | bytes 1413128 | tf_op jit(solution)/shard_map/ppermute | solution.py:367
  22.7 17.3 %collective-permute-start.10 = (bf16[80,2944]{1,0:T(8,128)(2,1)S(1)}, bf16[80,2944]{1,0:T(8,128)(2,1)S(1)}, u32[]{:S(2)}, u32[]{:S(2)}) collective-permute-start(bf16[80,2944]{1,0:T(8,128)(2,1)S(1)} %get-tuple-element.75), channel_id=1, source_target_pairs={{0,16},{16,0},{1,17},{17,1},{2,18},{18,2},{3,19},{19,3},{4,20},{20... | collective-permute-start | bytes 1413128 | tf_op jit(solution)/shard_map/ppermute | solution.py:339
  24.4 26.8 %collective-permute-start.13 = (bf16[80,2944]{1,0:T(8,128)(2,1)S(1)}, bf16[80,2944]{1,0:T(8,128)(2,1)S(1)}, u32[]{:S(2)}, u32[]{:S(2)}) collective-permute-start(bf16[80,2944]{1,0:T(8,128)(2,1)S(1)} %get-tuple-element.83), channel_id=1, source_target_pairs={{0,16},{16,0},{1,17},{17,1},{2,18},{18,2},{3,19},{19,3},{4,20},{20... | collective-permute-start | bytes 1413128 | tf_op jit(solution)/shard_map/ppermute | solution.py:339
  34.0 17.2 %collective-permute-start.11 = (bf16[80,2944]{1,0:T(8,128)(2,1)S(1)}, bf16[80,2944]{1,0:T(8,128)(2,1)S(1)}, u32[]{:S(2)}, u32[]{:S(2)}) collective-permute-start(bf16[80,2944]{1,0:T(8,128)(2,1)S(1)} %collective-permute-done.8.refs_3_), channel_id=1, source_target_pairs={{0,4},{4,8},{8,12},{12,14},{14,10},{10,6},{6,2},{2,0},{1,5},{5,9},... | collective-permute-start | bytes 1413128 | tf_op jit(solution)/shard_map/ppermute | solution.py:364
  35.6 15.6 %collective-permute-start.12 = (bf16[80,2944]{1,0:T(8,128)(2,1)S(1)}, bf16[80,2944]{1,0:T(8,128)(2,1)S(1)}, u32[]{:S(2)}, u32[]{:S(2)}) collective-permute-start(bf16[80,2944]{1,0:T(8,128)(2,1)S(1)} %collective-permute-done.9.refs_4_), channel_id=1, source_target_pairs={{4,0},{8,4},{12,8},{14,12},{10,14},{6,10},{2,6},{0,2},{5,1},{9,5},... | collective-permute-start | bytes 1413128 | tf_op jit(solution)/shard_map/ppermute | solution.py:367
  40.1 9.5 %collective-permute-start.18 = (bf16[40,2944]{1,0:T(8,128)(2,1)S(1)}, bf16[40,2944]{1,0:T(8,128)(2,1)S(1)}, u32[]{:S(2)}, u32[]{:S(2)}) collective-permute-start(bf16[40,2944]{1,0:T(8,128)(2,1)S(1)} %get-tuple-element.118), channel_id=1, source_target_pairs={{0,4},{4,8},{8,12},{12,14},{14,10},{10,6},{6,2},{2,0},{1,5},{5,9},... | collective-permute-start | bytes 706568 | tf_op jit(solution)/shard_map/ppermute | solution.py:364
  41.8 9.4 %collective-permute-start.19 = (bf16[40,2944]{1,0:T(8,128)(2,1)S(1)}, bf16[40,2944]{1,0:T(8,128)(2,1)S(1)}, u32[]{:S(2)}, u32[]{:S(2)}) collective-permute-start(bf16[40,2944]{1,0:T(8,128)(2,1)S(1)} %get-tuple-element.117), channel_id=1, source_target_pairs={{4,0},{8,4},{12,8},{14,12},{10,14},{6,10},{2,6},{0,2},{5,1},{9,5},... | collective-permute-start | bytes 706568 | tf_op jit(solution)/shard_map/ppermute | solution.py:367
  49.7 14.6 %collective-permute-start.17 = (bf16[80,2944]{1,0:T(8,128)(2,1)S(1)}, bf16[80,2944]{1,0:T(8,128)(2,1)S(1)}, u32[]{:S(2)}, u32[]{:S(2)}) collective-permute-start(bf16[80,2944]{1,0:T(8,128)(2,1)S(1)} %get-tuple-element.88), channel_id=1, source_target_pairs={{0,16},{16,0},{1,17},{17,1},{2,18},{18,2},{3,19},{19,3},{4,20},{20... | collective-permute-start | bytes 1413128 | tf_op jit(solution)/shard_map/ppermute | solution.py:339
  51.2 7.0 %collective-permute-start.14 = (bf16[40,2944]{1,0:T(8,128)(2,1)S(1)}, bf16[40,2944]{1,0:T(8,128)(2,1)S(1)}, u32[]{:S(2)}, u32[]{:S(2)}) collective-permute-start(bf16[40,2944]{1,0:T(8,128)(2,1)S(1)} %slice.76), channel_id=1, source_target_pairs={{0,4},{4,8},{8,12},{12,14},{14,10},{10,6},{6,2},{2,0},{1,5},{5,9},... | collective-permute-start | bytes 706568 | tf_op jit(solution)/shard_map/ppermute | solution.py:364
  52.9 6.7 %collective-permute-start.15 = (bf16[40,2944]{1,0:T(8,128)(2,1)S(1)}, bf16[40,2944]{1,0:T(8,128)(2,1)S(1)}, u32[]{:S(2)}, u32[]{:S(2)}) collective-permute-start(bf16[40,2944]{1,0:T(8,128)(2,1)S(1)} %slice.77), channel_id=1, source_target_pairs={{4,0},{8,4},{12,8},{14,12},{10,14},{6,10},{2,6},{0,2},{5,1},{9,5},... | collective-permute-start | bytes 706568 | tf_op jit(solution)/shard_map/ppermute | solution.py:367
  53.6 10.7 %collective-permute-start.20 = (bf16[40,2944]{1,0:T(8,128)(2,1)S(1)}, bf16[40,2944]{1,0:T(8,128)(2,1)S(1)}, u32[]{:S(2)}, u32[]{:S(2)}) collective-permute-start(bf16[40,2944]{1,0:T(8,128)(2,1)S(1)} %get-tuple-element.116), channel_id=1, source_target_pairs={{0,4},{4,8},{8,12},{12,14},{14,10},{10,6},{6,2},{2,0},{1,5},{5,9},... | collective-permute-start | bytes 706568 | tf_op jit(solution)/shard_map/ppermute | solution.py:364
  55.2 9.1 %collective-permute-start.21 = (bf16[40,2944]{1,0:T(8,128)(2,1)S(1)}, bf16[40,2944]{1,0:T(8,128)(2,1)S(1)}, u32[]{:S(2)}, u32[]{:S(2)}) collective-permute-start(bf16[40,2944]{1,0:T(8,128)(2,1)S(1)} %get-tuple-element.115), channel_id=1, source_target_pairs={{4,0},{8,4},{12,8},{14,12},{10,14},{6,10},{2,6},{0,2},{5,1},{9,5},... | collective-permute-start | bytes 706568 | tf_op jit(solution)/shard_map/ppermute | solution.py:367
  58.2 12.8 %collective-permute-start.2 = (bf16[80,2944]{1,0:T(8,128)(2,1)S(1)}, bf16[80,2944]{1,0:T(8,128)(2,1)S(1)}, u32[]{:S(2)}, u32[]{:S(2)}) collective-permute-start(bf16[80,2944]{1,0:T(8,128)(2,1)S(1)} %get-tuple-element.63), channel_id=1, source_target_pairs={{0,16},{16,0},{1,17},{17,1},{2,18},{18,2},{3,19},{19,3},{4,20},{20... | collective-permute-start | bytes 1413128 | tf_op jit(solution)/shard_map/ppermute | solution.py:339
  61.0 3.3 %copy-start.2 = (f32[1,640]{1,0:T(1,128)S(1)}, f32[1,640]{1,0:T(1,128)}, u32[]{:S(2)}) copy-start(f32[1,640]{1,0:T(1,128)} %bias.1) | copy-start | bytes 7684
  64.3 2.9 %collective-permute-start.22 = (f32[3,640]{1,0:T(4,128)S(1)}, f32[3,640]{1,0:T(4,128)S(1)}, u32[]{:S(2)}, u32[]{:S(2)}) collective-permute-start(f32[3,640]{1,0:T(4,128)S(1)} %fusion.2), channel_id=1, source_target_pairs={{0,1},{1,0},{2,3},{3,2},{4,5},{5,4},{6,7},{7,6},{8,9},{9,8},{10,11... | collective-permute-start | bytes 23048 | tf_op jit(solution)/shard_map/ppermute | solution.py:339
  64.4 9.6 %collective-permute-start.16 = (bf16[512,256]{1,0:T(8,128)(2,1)S(1)}, bf16[512,256]{1,0:T(8,128)(2,1)S(1)}, u32[]{:S(2)}, u32[]{:S(2)}) collective-permute-start(bf16[512,256]{1,0:T(8,128)(2,1)S(1)} %shard_map.124), channel_id=1, source_target_pairs={{0,1},{1,0},{2,3},{3,2},{4,5},{5,4},{6,7},{7,6},{8,9},{9,8},{10,11... | collective-permute-start | bytes 786440 | tf_op jit(solution)/shard_map/ppermute | solution.py:339
  65.1 7.8 %collective-permute-start.24 = (bf16[40,2944]{1,0:T(8,128)(2,1)S(1)}, bf16[40,2944]{1,0:T(8,128)(2,1)S(1)}, u32[]{:S(2)}, u32[]{:S(2)}) collective-permute-start(bf16[40,2944]{1,0:T(8,128)(2,1)S(1)} %get-tuple-element.114), channel_id=1, source_target_pairs={{0,4},{4,8},{8,12},{12,14},{14,10},{10,6},{6,2},{2,0},{1,5},{5,9},... | collective-permute-start | bytes 706568 | tf_op jit(solution)/shard_map/ppermute | solution.py:364
  66.5 7.4 %collective-permute-start.25 = (bf16[40,2944]{1,0:T(8,128)(2,1)S(1)}, bf16[40,2944]{1,0:T(8,128)(2,1)S(1)}, u32[]{:S(2)}, u32[]{:S(2)}) collective-permute-start(bf16[40,2944]{1,0:T(8,128)(2,1)S(1)} %get-tuple-element.113), channel_id=1, source_target_pairs={{4,0},{8,4},{12,8},{14,12},{10,14},{6,10},{2,6},{0,2},{5,1},{9,5},... | collective-permute-start | bytes 706568 | tf_op jit(solution)/shard_map/ppermute | solution.py:367
  67.2 3.7 %collective-permute-start.23 = (f32[3,640]{1,0:T(4,128)S(1)}, f32[3,640]{1,0:T(4,128)S(1)}, u32[]{:S(2)}, u32[]{:S(2)}) collective-permute-start(f32[3,640]{1,0:T(4,128)S(1)} %fusion.5), channel_id=1, source_target_pairs={{0,16},{16,0},{1,17},{17,1},{2,18},{18,2},{3,19},{19,3},{4,20},{20... | collective-permute-start | bytes 23048 | tf_op jit(solution)/shard_map/ppermute | solution.py:388
  70.9 5.4 %collective-permute-start.27 = (bf16[512,512]{1,0:T(8,128)(2,1)S(1)}, bf16[512,512]{1,0:T(8,128)(2,1)S(1)}, u32[]{:S(2)}, u32[]{:S(2)}) collective-permute-start(bf16[512,512]{1,0:T(8,128)(2,1)S(1)} %get-tuple-element.103), channel_id=1, source_target_pairs={{0,1},{1,0},{2,3},{3,2},{4,5},{5,4},{6,7},{7,6},{8,9},{9,8},{10,11... | collective-permute-start | bytes 1572872 | tf_op jit(solution)/shard_map/ppermute | solution.py:339
  74.1 6.6 %collective-permute-start.26 = (bf16[40,2944]{1,0:T(8,128)(2,1)S(1)}, bf16[40,2944]{1,0:T(8,128)(2,1)S(1)}, u32[]{:S(2)}, u32[]{:S(2)}) collective-permute-start(bf16[40,2944]{1,0:T(8,128)(2,1)S(1)} %add_convert_fusion.1), channel_id=1, source_target_pairs={{0,4},{4,8},{8,12},{12,14},{14,10},{10,6},{6,2},{2,0},{1,5},{5,9},... | collective-permute-start | bytes 706568 | tf_op jit(solution)/shard_map/ppermute | solution.py:364
  75.4 4.6 %collective-permute-start.28 = (f32[3,640]{1,0:T(4,128)S(1)}, f32[3,640]{1,0:T(4,128)S(1)}, u32[]{:S(2)}, u32[]{:S(2)}) collective-permute-start(f32[3,640]{1,0:T(4,128)S(1)} %add.91), channel_id=1, source_target_pairs={{0,4},{4,0},{8,12},{12,8},{1,5},{5,1},{9,13},{13,9},{2,6},{6,2},{1... | collective-permute-start | bytes 23048 | tf_op jit(solution)/shard_map/ppermute | solution.py:388
  80.0 10.7 %copy-start = (f32[1,40,5760]{2,1,0:T(8,128)S(1)}, f32[1,40,5760]{2,1,0:T(8,128)}, u32[]{:S(2)}) copy-start(f32[1,40,5760]{2,1,0:T(8,128)} %param.10) | copy-start | bytes 2764804
  80.8 6.9 %collective-permute-start.29 = (bf16[40,2944]{1,0:T(8,128)(2,1)S(1)}, bf16[40,2944]{1,0:T(8,128)(2,1)S(1)}, u32[]{:S(2)}, u32[]{:S(2)}) collective-permute-start(bf16[40,2944]{1,0:T(8,128)(2,1)S(1)} %add_convert_fusion), channel_id=1, source_target_pairs={{0,16},{16,0},{1,17},{17,1},{2,18},{18,2},{3,19},{19,3},{4,20},{20... | collective-permute-start | bytes 706568 | tf_op jit(solution)/shard_map/ppermute | solution.py:339
  81.9 3.7 %collective-permute-start.31 = (f32[3,640]{1,0:T(4,128)S(1)}, f32[3,640]{1,0:T(4,128)S(1)}, u32[]{:S(2)}, u32[]{:S(2)}) collective-permute-start(f32[3,640]{1,0:T(4,128)S(1)} %add.98), channel_id=1, source_target_pairs={{0,2},{2,0},{1,3},{3,1},{4,6},{6,4},{5,7},{7,5},{8,10},{10,8},{9,1... | collective-permute-start | bytes 23048 | tf_op jit(solution)/shard_map/ppermute | solution.py:388
  85.6 4.6 %collective-permute-start.32 = (f32[3,640]{1,0:T(4,128)S(1)}, f32[3,640]{1,0:T(4,128)S(1)}, u32[]{:S(2)}, u32[]{:S(2)}) collective-permute-start(f32[3,640]{1,0:T(4,128)S(1)} %add.102), channel_id=1, source_target_pairs={{0,8},{4,12},{8,0},{12,4},{1,9},{5,13},{9,1},{13,5},{2,10},{6,14},... | collective-permute-start | bytes 23048 | tf_op jit(solution)/shard_map/ppermute | solution.py:388
  87.8 3.0 %collective-permute-start.30 = (bf16[40,2944]{1,0:T(8,128)(2,1)S(1)}, bf16[40,2944]{1,0:T(8,128)(2,1)S(1)}, u32[]{:S(2)}, u32[]{:S(2)}) collective-permute-start(bf16[40,2944]{1,0:T(8,128)(2,1)S(1)} %get-tuple-element.123), channel_id=1, source_target_pairs={{0,1},{1,0},{2,3},{3,2},{4,5},{5,4},{6,7},{7,6},{8,9},{9,8},{10,11... | collective-permute-start | bytes 706568 | tf_op jit(solution)/shard_map/ppermute | solution.py:339

commit v21 on v20

--- a/solution.py
+++ b/solution.py
@@ -566,11 +566,11 @@
             partial(finish_kernel, cols), jax.ShapeDtypeStruct(shard.shape, F32),
             [SMEM_SPEC] * 2 + [VMEM_SPEC] * 5, [], 8, flops // 16,
         )(dev, step, shard, mine, theirs, ours, aside)
-        vectors = hop(vectors, "y", 1)
         reach = 2
         while reach < zs:
             vectors = hop(vectors, "z", reach)
             reach *= 2
+        vectors = hop(vectors, "y", 1)
         new_v = 0.5 * vectors
     else:
         late = [lax.all_gather(unit, NODE, axis=0, tiled=True)]

time: 92.1 us -> 92.1 us (level)
  no operation moved by 1% of the time
where the time goes in v21:
time: 92.1 us; the launch traced here: 91.9 us
  Pallas kernels  32.4 us (35%)
  starting transfers between devices  31.3 us (34%)
  waiting for transfers between devices  21.8 us (24%)
  other arithmetic  2.88 us (3%)
  local copies, waits for them, and re-layouts  1.94 us (2%)
  between operations  1.58 us (2%)
    ppermute x8, starting transfers between devices, up(): return lax.ppermute(value, NODE, self.ahead)  13.7 us
    ppermute x8, waiting for transfers between devices, up(): return lax.ppermute(value, NODE, self.ahead)  10.7 us
    ppermute x14, starting transfers between devices, swap(): return lax.ppermute(value, axis, [(0, 1), (1, 0)])  9.61 us
    pallas_call x2, Pallas kernels, back(): call(partial(back_kernel, cols, stages, stage), jax.ShapeDtypeStruct((2,...  8.62 us
    ppermute x4, waiting for transfers between devices, hop(): lax.ppermute(value, axis, [(s, s ^ mask) for s in range(count)])  6.88 us
    ppermute x4, starting transfers between devices, hop(): lax.ppermute(value, axis, [(s, s ^ mask) for s in range(count)])  5.22 us
    pallas_call x1, Pallas kernels, per_device(): call(partial(grad_kernel, cols), [jax.ShapeDtypeStruct((n * 2 * part, col...  4.64 us
    pallas_call x1, Pallas kernels, slopes_of(): call(partial(slope_kernel, stages), (jax.ShapeDtypeStruct((3, 2 * half +...  4.48 us
  transfers between devices with their start and end apart: 33, of which 12 were waited for; matrix products, arithmetic and copies ran while one was open for 4% of the time, Pallas kernels for 34%

profile of v21, /device:TPU:0, one launch (start us, length us, event | category | flops | bytes accessed | tf_op | source)
XLA Modules:
  0.0 91.9 jit_solution(346062053013616299)
XLA Ops:
  0.7 1.3 %fusion = (bf16[40,2944]{1,0:T(8,128)(2,1)S(1)}, bf16[40,2944]{1,0:T(8,128)(2,1)S(1)}) fusion(f32[1,40,5760]{2,1,0:T(8,128)} %param.10, s32[]{:T(128)S(6)} %select_n.27, s32[]{:T(128)S(6)} %select_n.28), kind=kLoop, calls=%fused_computation.12 | loop fusion | bytes 942088 | tf_op jit(solution)/shard_map/convert_element_type | solution.py:419
  2.0 0.5 collective-permute-start.3
  2.5 2.0 %fusion.3 = (f32[640]{0:T(1024)S(1)}, bf16[16,32,640]{2,1,0:T(8,128)(2,1)S(1)}) fusion(f32[1,16,32,640]{3,2,1,0:T(8,128)} %param.9), kind=kLoop, calls=%fused_computation.20 | loop fusion | flops 654720 | bytes 1968640 | tf_op jit(solution)/shard_map/reduce_sum | solution.py:512
  4.6 0.5 collective-permute-start
  5.1 2.7 %collective-permute-start.4 = (bf16[80,2944]{1,0:T(8,128)(2,1)S(1)}, bf16[80,2944]{1,0:T(8,128)(2,1)S(1)}, u32[]{:S(2)}, u32[]{:S(2)}) collective-permute-start(bf16[80,2944]{1,0:T(8,128)(2,1)S(1)} %maximum_select_fusion.refs_0_), channel_id=1, source_target_pairs={{0,4},{4,8},{8,12},{12,14},{14,10},{10,6},{6,2},{2,0},{1,5},{5,9},... | collective-permute-start | bytes 1413128 | tf_op jit(solution)/shard_map/ppermute | solution.py:364
  7.8 1.9 %collective-permute-start.6 = (bf16[40,2944]{1,0:T(8,128)(2,1)S(1)}, bf16[40,2944]{1,0:T(8,128)(2,1)S(1)}, u32[]{:S(2)}, u32[]{:S(2)}) collective-permute-start(bf16[40,2944]{1,0:T(8,128)(2,1)S(1)} %get-tuple-element.121), channel_id=1, source_target_pairs={{0,16},{16,0},{1,17},{17,1},{2,18},{18,2},{3,19},{19,3},{4,20},{20... | collective-permute-start | bytes 706568 | tf_op jit(solution)/shard_map/ppermute | solution.py:339
  9.9 4.4 %shard_map.119 = (f32[2,640]{1,0:T(2,128)S(1)}, bf16[3,34,32,640]{3,2,1,0:T(8,128)(2,1)S(1)}, bf16[640,1024]{1,0:T(8,128)(2,1)S(1)}) custom-call(s32[1]{0:T(128)} %bitcast.dev, s32[32,24]{1,0:T(8,128)S(1)} %copy-done.5, bf16[16,32,640]{2,1,0:T(8,128)(2,1)S(1)} %bitcast.13, bf16[16,32,640]{2,1,0:T(8,128)(2,1)S(1)} %collective-permute-done.lat_far, ...), custom_call_target="tpu_custom_call" | custom-call | flops 964689920 | tf_op jit(solution)/shard_map/pallas_call | solution.py:450
  14.3 4.6 %shard_map.120 = (bf16[320,2944]{1,0:T(8,128)(2,1)S(1)}, bf16[80,2944]{1,0:T(8,128)(2,1)S(1)}, bf16[80,2944]{1,0:T(8,128)(2,1)S(1)}, bf16[80,2944]{1,0:T(8,128)(2,1)S(1)}, bf16[80,2944]{1,0:T(8,128)(2,1)S(1)}) custom-call(s32[1]{0:T(128)} %bitcast.dev, bf16[3,34,32,640]{3,2,1,0:T(8,128)(2,1)S(1)} %get-tuple-element.60.acts, ...), custom_call_target="tpu_custom_call" | custom-call | flops 1929379840 | tf_op jit(solution)/shard_map/pallas_call | solution.py:458
  19.0 1.7 %collective-permute-done.7.theirs = bf16[40,2944]{1,0:T(8,128)(2,1)S(1)} collective-permute-done((bf16[40,2944]{1,0:T(8,128)(2,1)S(1)}, bf16[40,2944]{1,0:T(8,128)(2,1)S(1)}, u32[]{:S(2)}, u32[]{:S(2)}) %collective-permute-start.7) | collective-permute-done | bytes 235552 | tf_op jit(solution)/shard_map/ppermute | solution.py:339
  20.7 1.7 %collective-permute-start.8 = (bf16[80,2944]{1,0:T(8,128)(2,1)S(1)}, bf16[80,2944]{1,0:T(8,128)(2,1)S(1)}, u32[]{:S(2)}, u32[]{:S(2)}) collective-permute-start(bf16[80,2944]{1,0:T(8,128)(2,1)S(1)} %collective-permute-done.4.refs_1_), channel_id=1, source_target_pairs={{0,4},{4,8},{8,12},{12,14},{14,10},{10,6},{6,2},{2,0},{1,5},{5,9},... | collective-permute-start | bytes 1413128 | tf_op jit(solution)/shard_map/ppermute | solution.py:364
  22.7 1.7 %collective-permute-start.10 = (bf16[80,2944]{1,0:T(8,128)(2,1)S(1)}, bf16[80,2944]{1,0:T(8,128)(2,1)S(1)}, u32[]{:S(2)}, u32[]{:S(2)}) collective-permute-start(bf16[80,2944]{1,0:T(8,128)(2,1)S(1)} %get-tuple-element.75), channel_id=1, source_target_pairs={{0,16},{16,0},{1,17},{17,1},{2,18},{18,2},{3,19},{19,3},{4,20},{20... | collective-permute-start | bytes 1413128 | tf_op jit(solution)/shard_map/ppermute | solution.py:339
  24.7 4.5 %shard_map.121 = (bf16[3,34,32,768]{3,2,1,0:T(8,128)(2,1)S(1)}, bf16[32,32,640]{2,1,0:T(8,128)(2,1)S(1)}, bf16[32,32,640]{2,1,0:T(8,128)(2,1)S(1)}, bf16[640,768]{1,0:T(8,128)(2,1)S(1)}) custom-call(s32[1]{0:T(128)} %bitcast.dev, s32[32,24]{1,0:T(8,128)S(1)} %copy-done.5, f32[2,640]{1,0:T(2,128)S(1)} %get-tuple-element.69.stats, f32[1,640]{1,0:T(1,128)S(1)} %copy-done.3, ...), custom_call_target="tpu_custom_call" | custom-call | flops 964689920 | tf_op jit(solution)/shard_map/pallas_call | solution.py:470
  29.2 3.5 %collective-permute-done.8.refs_3_ = bf16[80,2944]{1,0:T(8,128)(2,1)S(1)} collective-permute-done((bf16[80,2944]{1,0:T(8,128)(2,1)S(1)}, bf16[80,2944]{1,0:T(8,128)(2,1)S(1)}, u32[]{:S(2)}, u32[]{:S(2)}) %collective-permute-start.8) | collective-permute-done | bytes 471072 | tf_op jit(solution)/shard_map/ppermute | solution.py:364
  32.7 1.3 %collective-permute-done.9.refs_4_ = bf16[80,2944]{1,0:T(8,128)(2,1)S(1)} collective-permute-done((bf16[80,2944]{1,0:T(8,128)(2,1)S(1)}, bf16[80,2944]{1,0:T(8,128)(2,1)S(1)}, u32[]{:S(2)}, u32[]{:S(2)}) %collective-permute-start.9) | collective-permute-done | bytes 471072 | tf_op jit(solution)/shard_map/ppermute | solution.py:367
  34.0 1.6 %collective-permute-start.11 = (bf16[80,2944]{1,0:T(8,128)(2,1)S(1)}, bf16[80,2944]{1,0:T(8,128)(2,1)S(1)}, u32[]{:S(2)}, u32[]{:S(2)}) collective-permute-start(bf16[80,2944]{1,0:T(8,128)(2,1)S(1)} %collective-permute-done.8.refs_3_), channel_id=1, source_target_pairs={{0,4},{4,8},{8,12},{12,14},{14,10},{10,6},{6,2},{2,0},{1,5},{5,9},... | collective-permute-start | bytes 1413128 | tf_op jit(solution)/shard_map/ppermute | solution.py:364
  35.6 0.4 collective-permute-start.12
  36.0 4.0 %shard_map.122 = (f32[512,512]{1,0:T(8,128)S(1)}, bf16[512,512]{1,0:T(8,128)(2,1)S(1)}) custom-call(s32[1]{0:T(128)} %bitcast.dev, bf16[3,34,32,640]{3,2,1,0:T(8,128)(2,1)S(1)} %get-tuple-element.60.acts, bf16[80,2944]{1,0:T(8,128)(2,1)S(1)} %maximum_select_fusion.refs_0_, bf16[80,2944]{1,0:T(8,128)(2,1)S(1)} %collective-permute-done.4.refs_1_, ...), custom_call_target="tpu_custom_call" | custom-call | flops 964689920 | tf_op jit(solution)/shard_map/pallas_call | solution.py:488
  40.1 1.6 %collective-permute-start.18 = (bf16[40,2944]{1,0:T(8,128)(2,1)S(1)}, bf16[40,2944]{1,0:T(8,128)(2,1)S(1)}, u32[]{:S(2)}, u32[]{:S(2)}) collective-permute-start(bf16[40,2944]{1,0:T(8,128)(2,1)S(1)} %get-tuple-element.118), channel_id=1, source_target_pairs={{0,4},{4,8},{8,12},{12,14},{14,10},{10,6},{6,2},{2,0},{1,5},{5,9},... | collective-permute-start | bytes 706568 | tf_op jit(solution)/shard_map/ppermute | solution.py:364
  41.8 0.5 collective-permute-start.19
  42.2 5.4 %shard_map.123 = f32[2,640]{1,0:T(2,128)S(1)} custom-call(s32[1]{0:T(128)} %bitcast.dev, bf16[3,34,32,768]{3,2,1,0:T(8,128)(2,1)S(1)} %get-tuple-element.89.cots, bf16[32,32,640]{2,1,0:T(8,128)(2,1)S(1)} %get-tuple-element.81.slope, bf16[32,32,640]{2,1,0:T(8,128)(2,1)S(1)} %get-tuple-element.82.slope_x, bf16[80,2944]{1,0:T(8,128)(2,1)S(1)} %maximum_select_fusion.refs_0_, ...), custom_call_target="tpu_custom_call" | custom-call | flops 964689920 | tf_op jit(solution)/shard_map/pallas_call | solution.py:480
  47.6 2.0 %collective-permute-done.18 = bf16[40,2944]{1,0:T(8,128)(2,1)S(1)} collective-permute-done((bf16[40,2944]{1,0:T(8,128)(2,1)S(1)}, bf16[40,2944]{1,0:T(8,128)(2,1)S(1)}, u32[]{:S(2)}, u32[]{:S(2)}) %collective-permute-start.18) | collective-permute-done | bytes 235552 | tf_op jit(solution)/shard_map/ppermute | solution.py:364
  49.7 1.5 %collective-permute-start.17 = (bf16[80,2944]{1,0:T(8,128)(2,1)S(1)}, bf16[80,2944]{1,0:T(8,128)(2,1)S(1)}, u32[]{:S(2)}, u32[]{:S(2)}) collective-permute-start(bf16[80,2944]{1,0:T(8,128)(2,1)S(1)} %get-tuple-element.88), channel_id=1, source_target_pairs={{0,16},{16,0},{1,17},{17,1},{2,18},{18,2},{3,19},{19,3},{4,20},{20... | collective-permute-start | bytes 1413128 | tf_op jit(solution)/shard_map/ppermute | solution.py:339
  51.2 1.6 %collective-permute-start.14 = (bf16[40,2944]{1,0:T(8,128)(2,1)S(1)}, bf16[40,2944]{1,0:T(8,128)(2,1)S(1)}, u32[]{:S(2)}, u32[]{:S(2)}) collective-permute-start(bf16[40,2944]{1,0:T(8,128)(2,1)S(1)} %slice.76), channel_id=1, source_target_pairs={{0,4},{4,8},{8,12},{12,14},{14,10},{10,6},{6,2},{2,0},{1,5},{5,9},... | collective-permute-start | bytes 706568 | tf_op jit(solution)/shard_map/ppermute | solution.py:364
  52.9 0.5 collective-permute-start.15
  53.6 1.6 %collective-permute-start.20 = (bf16[40,2944]{1,0:T(8,128)(2,1)S(1)}, bf16[40,2944]{1,0:T(8,128)(2,1)S(1)}, u32[]{:S(2)}, u32[]{:S(2)}) collective-permute-start(bf16[40,2944]{1,0:T(8,128)(2,1)S(1)} %get-tuple-element.116), channel_id=1, source_target_pairs={{0,4},{4,8},{8,12},{12,14},{14,10},{10,6},{6,2},{2,0},{1,5},{5,9},... | collective-permute-start | bytes 706568 | tf_op jit(solution)/shard_map/ppermute | solution.py:364
  55.2 0.5 collective-permute-start.21
  55.6 2.5 %collective-permute-done.14.refs_2_.refs_5_ = bf16[40,2944]{1,0:T(8,128)(2,1)S(1)} collective-permute-done((bf16[40,2944]{1,0:T(8,128)(2,1)S(1)}, bf16[40,2944]{1,0:T(8,128)(2,1)S(1)}, u32[]{:S(2)}, u32[]{:S(2)}) %collective-permute-start.14) | collective-permute-done | bytes 235552 | tf_op jit(solution)/shard_map/ppermute | solution.py:364
  58.2 1.3 %collective-permute-start.2 = (bf16[80,2944]{1,0:T(8,128)(2,1)S(1)}, bf16[80,2944]{1,0:T(8,128)(2,1)S(1)}, u32[]{:S(2)}, u32[]{:S(2)}) collective-permute-start(bf16[80,2944]{1,0:T(8,128)(2,1)S(1)} %get-tuple-element.63), channel_id=1, source_target_pairs={{0,16},{16,0},{1,17},{17,1},{2,18},{18,2},{3,19},{19,3},{4,20},{20... | collective-permute-start | bytes 1413128 | tf_op jit(solution)/shard_map/ppermute | solution.py:339
  59.6 1.4 %shard_map.124 = bf16[512,256]{1,0:T(8,128)(2,1)S(1)} custom-call(s32[1]{0:T(128)} %bitcast.dev, bf16[3,34,32,640]{3,2,1,0:T(8,128)(2,1)S(1)} %get-tuple-element.60.acts, bf16[80,2944]{1,0:T(8,128)(2,1)S(1)} %collective-permute-done.11.refs_0_.refs_3_, bf16[80,2944]{1,0:T(8,128)(2,1)S(1)} %collective-permute-done.12.refs_1_.refs_4_, ...), custom_call_target="tpu_custom_call" | custom-call | flops 482344960 | tf_op jit(solution)/shard_map/pallas_call | solution.py:497
  61.0 3.2 %shard_map.125 = f32[2,640]{1,0:T(2,128)S(1)} custom-call(s32[1]{0:T(128)} %bitcast.dev, bf16[3,34,32,768]{3,2,1,0:T(8,128)(2,1)S(1)} %get-tuple-element.89.cots, bf16[32,32,640]{2,1,0:T(8,128)(2,1)S(1)} %get-tuple-element.81.slope, bf16[32,32,640]{2,1,0:T(8,128)(2,1)S(1)} %get-tuple-element.82.slope_x, ...), custom_call_target="tpu_custom_call" | custom-call | flops 964689920 | tf_op jit(solution)/shard_map/pallas_call | solution.py:480
  64.4 0.5 collective-permute-start.16
  65.1 1.5 %collective-permute-start.24 = (bf16[40,2944]{1,0:T(8,128)(2,1)S(1)}, bf16[40,2944]{1,0:T(8,128)(2,1)S(1)}, u32[]{:S(2)}, u32[]{:S(2)}) collective-permute-start(bf16[40,2944]{1,0:T(8,128)(2,1)S(1)} %get-tuple-element.114), channel_id=1, source_target_pairs={{0,4},{4,8},{8,12},{12,14},{14,10},{10,6},{6,2},{2,0},{1,5},{5,9},... | collective-permute-start | bytes 706568 | tf_op jit(solution)/shard_map/ppermute | solution.py:364
  66.5 0.6 collective-permute-start.25
  67.2 1.2 %collective-permute-start.23 = (f32[3,640]{1,0:T(4,128)S(1)}, f32[3,640]{1,0:T(4,128)S(1)}, u32[]{:S(2)}, u32[]{:S(2)}) collective-permute-start(f32[3,640]{1,0:T(4,128)S(1)} %fusion.5), channel_id=1, source_target_pairs={{0,16},{16,0},{1,17},{17,1},{2,18},{18,2},{3,19},{19,3},{4,20},{20... | collective-permute-start | bytes 23048 | tf_op jit(solution)/shard_map/ppermute | solution.py:388
  68.4 2.6 %collective-permute-done.23 = f32[3,640]{1,0:T(4,128)S(1)} collective-permute-done((f32[3,640]{1,0:T(4,128)S(1)}, f32[3,640]{1,0:T(4,128)S(1)}, u32[]{:S(2)}, u32[]{:S(2)}) %collective-permute-start.23) | collective-permute-done | bytes 7712 | tf_op jit(solution)/shard_map/ppermute | solution.py:388
  70.9 1.9 %collective-permute-done.24 = bf16[40,2944]{1,0:T(8,128)(2,1)S(1)} collective-permute-done((bf16[40,2944]{1,0:T(8,128)(2,1)S(1)}, bf16[40,2944]{1,0:T(8,128)(2,1)S(1)}, u32[]{:S(2)}, u32[]{:S(2)}) %collective-permute-start.24) | collective-permute-done | bytes 235552 | tf_op jit(solution)/shard_map/ppermute | solution.py:364
  72.9 1.1 %collective-permute-done.25 = bf16[40,2944]{1,0:T(8,128)(2,1)S(1)} collective-permute-done((bf16[40,2944]{1,0:T(8,128)(2,1)S(1)}, bf16[40,2944]{1,0:T(8,128)(2,1)S(1)}, u32[]{:S(2)}, u32[]{:S(2)}) %collective-permute-start.25) | collective-permute-done | bytes 235552 | tf_op jit(solution)/shard_map/ppermute | solution.py:367
  74.1 1.3 %collective-permute-start.26 = (bf16[40,2944]{1,0:T(8,128)(2,1)S(1)}, bf16[40,2944]{1,0:T(8,128)(2,1)S(1)}, u32[]{:S(2)}, u32[]{:S(2)}) collective-permute-start(bf16[40,2944]{1,0:T(8,128)(2,1)S(1)} %add_convert_fusion.1), channel_id=1, source_target_pairs={{0,4},{4,8},{8,12},{12,14},{14,10},{10,6},{6,2},{2,0},{1,5},{5,9},... | collective-permute-start | bytes 706568 | tf_op jit(solution)/shard_map/ppermute | solution.py:364
  75.4 0.9 collective-permute-start.28
  76.3 3.7 %shard_map.126 = bf16[16,32,640]{2,1,0:T(8,128)(2,1)} custom-call(s32[1]{0:T(128)} %bitcast.dev, bf16[3,34,32,640]{3,2,1,0:T(8,128)(2,1)S(1)} %get-tuple-element.60.acts, bf16[512,256]{1,0:T(8,128)(2,1)S(1)} %collective-permute-done.16.got, bf16[16,32,640]{2,1,0:T(8,128)(2,1)S(1)} %bitcast.15, f32[1,640]{1,0:T(1,128)S(1)} %copy-done.2, ...), custom_call_target="tpu_custom_call" | custom-call | flops 964689920 | tf_op jit(solution)/shard_map/pallas_call | solution.py:505
  80.0 0.7 collective-permute-done.26
  80.8 1.0 %collective-permute-start.29 = (bf16[40,2944]{1,0:T(8,128)(2,1)S(1)}, bf16[40,2944]{1,0:T(8,128)(2,1)S(1)}, u32[]{:S(2)}, u32[]{:S(2)}) collective-permute-start(bf16[40,2944]{1,0:T(8,128)(2,1)S(1)} %add_convert_fusion), channel_id=1, source_target_pairs={{0,16},{16,0},{1,17},{17,1},{2,18},{18,2},{3,19},{19,3},{4,20},{20... | collective-permute-start | bytes 706568 | tf_op jit(solution)/shard_map/ppermute | solution.py:339
  81.9 2.2 %collective-permute-start.31 = (f32[3,640]{1,0:T(4,128)S(1)}, f32[3,640]{1,0:T(4,128)S(1)}, u32[]{:S(2)}, u32[]{:S(2)}) collective-permute-start(f32[3,640]{1,0:T(4,128)S(1)} %add.98), channel_id=1, source_target_pairs={{0,8},{4,12},{8,0},{12,4},{1,9},{5,13},{9,1},{13,5},{2,10},{6,14},... | collective-permute-start | bytes 23048 | tf_op jit(solution)/shard_map/ppermute | solution.py:388
  84.7 1.8 %collective-permute-done.31 = f32[3,640]{1,0:T(4,128)S(1)} collective-permute-done((f32[3,640]{1,0:T(4,128)S(1)}, f32[3,640]{1,0:T(4,128)S(1)}, u32[]{:S(2)}, u32[]{:S(2)}) %collective-permute-start.31) | collective-permute-done | bytes 7712 | tf_op jit(solution)/shard_map/ppermute | solution.py:388
  86.5 1.0 %collective-permute-start.32 = (f32[3,640]{1,0:T(4,128)S(1)}, f32[3,640]{1,0:T(4,128)S(1)}, u32[]{:S(2)}, u32[]{:S(2)}) collective-permute-start(f32[3,640]{1,0:T(4,128)S(1)} %add.102), channel_id=1, source_target_pairs={{0,2},{2,0},{1,3},{3,1},{4,6},{6,4},{5,7},{7,5},{8,10},{10,8},{9,1... | collective-permute-start | bytes 23048 | tf_op jit(solution)/shard_map/ppermute | solution.py:388
  87.6 2.6 %collective-permute-done.32 = f32[3,640]{1,0:T(4,128)S(1)} collective-permute-done((f32[3,640]{1,0:T(4,128)S(1)}, f32[3,640]{1,0:T(4,128)S(1)}, u32[]{:S(2)}, u32[]{:S(2)}) %collective-permute-start.32) | collective-permute-done | bytes 7712 | tf_op jit(solution)/shard_map/ppermute | solution.py:388
  90.1 0.6 fusion.4
  90.7 1.2 %shard_map.127 = f32[40,5760]{1,0:T(8,128)} custom-call(s32[1]{0:T(128)} %bitcast.dev, s32[1]{0:T(128)S(6)} %copy.13.step, f32[40,5760]{1,0:T(8,128)S(1)} %bitcast.11, bf16[40,2944]{1,0:T(8,128)(2,1)S(1)} %collective-permute-done.6.mine, bf16[40,2944]{1,0:T(8,128)(2,1)S(1)} %collective-permute-done.7.theirs, bf16[40,2944]{1,0:T(8,128)(2,1)S(1)} %get-tuple-element.124.ours, ...), custom_call_target="tpu_custom_call" | custom-call | flops 241172480 | tf_op jit(solution)/shard_map/pallas_call | solution.py:565
  (59 shorter events, 2.1 us)
Async XLA Ops:
  0.6 3.9 %copy-start.1 = (bf16[1,16,32,640]{3,2,1,0:T(8,128)(2,1)S(1)}, bf16[1,16,32,640]{3,2,1,0:T(8,128)(2,1)}, u32[]{:S(2)}) copy-start(bf16[1,16,32,640]{3,2,1,0:T(8,128)(2,1)} %param.8) | copy-start | bytes 1966084
  0.7 9.2 %copy-start.3 = (f32[1,640]{1,0:T(1,128)S(1)}, f32[1,640]{1,0:T(1,128)}, u32[]{:S(2)}) copy-start(f32[1,640]{1,0:T(1,128)} %gain.3) | copy-start | bytes 7684
  0.7 9.2 %copy-start.4 = (f32[1,640]{1,0:T(1,128)S(1)}, f32[1,640]{1,0:T(1,128)}, u32[]{:S(2)}) copy-start(f32[1,640]{1,0:T(1,128)} %shift.3) | copy-start | bytes 7684
  0.7 9.2 %copy-start.5 = (s32[32,24]{1,0:T(8,128)S(1)}, s32[32,24]{1,0:T(8,128)}, u32[]{:S(2)}) copy-start(s32[32,24]{1,0:T(8,128)} %constant.40.clone.table) | copy-start | bytes 9220
  2.0 3.1 %collective-permute-start.3 = (bf16[40,2944]{1,0:T(8,128)(2,1)S(1)}, bf16[40,2944]{1,0:T(8,128)(2,1)S(1)}, u32[]{:S(2)}, u32[]{:S(2)}) collective-permute-start(bf16[40,2944]{1,0:T(8,128)(2,1)S(1)} %get-tuple-element.122), channel_id=1, source_target_pairs={{0,1},{1,0},{2,3},{3,2},{4,5},{5,4},{6,7},{7,6},{8,9},{9,8},{10,11... | collective-permute-start | bytes 706568 | tf_op jit(solution)/shard_map/ppermute | solution.py:339
  4.5 5.3 %collective-permute-start.1 = (bf16[16,32,640]{2,1,0:T(8,128)(2,1)S(1)}, bf16[16,32,640]{2,1,0:T(8,128)(2,1)S(1)}, u32[]{:S(2)}, u32[]{:S(2)}) collective-permute-start(bf16[16,32,640]{2,1,0:T(8,128)(2,1)S(1)} %get-tuple-element.120.cot_own), channel_id=1, source_target_pairs={{0,1},{1,0},{2,3},{3,2},{4,5},{5,4},{6,7},{7,6},{8,9},{9,8},{10,11... | collective-permute-start | bytes 1966088 | tf_op jit(solution)/shard_map/ppermute | solution.py:339
  4.6 5.3 %collective-permute-start = (bf16[16,32,640]{2,1,0:T(8,128)(2,1)S(1)}, bf16[16,32,640]{2,1,0:T(8,128)(2,1)S(1)}, u32[]{:S(2)}, u32[]{:S(2)}) collective-permute-start(bf16[16,32,640]{2,1,0:T(8,128)(2,1)S(1)} %bitcast.12), channel_id=1, source_target_pairs={{0,1},{1,0},{2,3},{3,2},{4,5},{5,4},{6,7},{7,6},{8,9},{9,8},{10,11... | collective-permute-start | bytes 1966088 | tf_op jit(solution)/shard_map/ppermute | solution.py:339
  5.1 15.6 %collective-permute-start.4 = (bf16[80,2944]{1,0:T(8,128)(2,1)S(1)}, bf16[80,2944]{1,0:T(8,128)(2,1)S(1)}, u32[]{:S(2)}, u32[]{:S(2)}) collective-permute-start(bf16[80,2944]{1,0:T(8,128)(2,1)S(1)} %maximum_select_fusion.refs_0_), channel_id=1, source_target_pairs={{0,4},{4,8},{8,12},{12,14},{14,10},{10,6},{6,2},{2,0},{1,5},{5,9},... | collective-permute-start | bytes 1413128 | tf_op jit(solution)/shard_map/ppermute | solution.py:364
  7.8 12.9 %collective-permute-start.5 = (bf16[80,2944]{1,0:T(8,128)(2,1)S(1)}, bf16[80,2944]{1,0:T(8,128)(2,1)S(1)}, u32[]{:S(2)}, u32[]{:S(2)}) collective-permute-start(bf16[80,2944]{1,0:T(8,128)(2,1)S(1)} %maximum_select_fusion.refs_0_), channel_id=1, source_target_pairs={{4,0},{8,4},{12,8},{14,12},{10,14},{6,10},{2,6},{0,2},{5,1},{9,5},... | collective-permute-start | bytes 1413128 | tf_op jit(solution)/shard_map/ppermute | solution.py:367
  7.8 11.1 %collective-permute-start.6 = (bf16[40,2944]{1,0:T(8,128)(2,1)S(1)}, bf16[40,2944]{1,0:T(8,128)(2,1)S(1)}, u32[]{:S(2)}, u32[]{:S(2)}) collective-permute-start(bf16[40,2944]{1,0:T(8,128)(2,1)S(1)} %get-tuple-element.121), channel_id=1, source_target_pairs={{0,16},{16,0},{1,17},{17,1},{2,18},{18,2},{3,19},{19,3},{4,20},{20... | collective-permute-start | bytes 706568 | tf_op jit(solution)/shard_map/ppermute | solution.py:339
  9.8 10.9 %collective-permute-start.7 = (bf16[40,2944]{1,0:T(8,128)(2,1)S(1)}, bf16[40,2944]{1,0:T(8,128)(2,1)S(1)}, u32[]{:S(2)}, u32[]{:S(2)}) collective-permute-start(bf16[40,2944]{1,0:T(8,128)(2,1)S(1)} %get-tuple-element.122), channel_id=1, source_target_pairs={{0,16},{16,0},{1,17},{17,1},{2,18},{18,2},{3,19},{19,3},{4,20},{20... | collective-permute-start | bytes 706568 | tf_op jit(solution)/shard_map/ppermute | solution.py:339
  20.7 12.0 %collective-permute-start.8 = (bf16[80,2944]{1,0:T(8,128)(2,1)S(1)}, bf16[80,2944]{1,0:T(8,128)(2,1)S(1)}, u32[]{:S(2)}, u32[]{:S(2)}) collective-permute-start(bf16[80,2944]{1,0:T(8,128)(2,1)S(1)} %collective-permute-done.4.refs_1_), channel_id=1, source_target_pairs={{0,4},{4,8},{8,12},{12,14},{14,10},{10,6},{6,2},{2,0},{1,5},{5,9},... | collective-permute-start | bytes 1413128 | tf_op jit(solution)/shard_map/ppermute | solution.py:364
  22.4 11.6 %collective-permute-start.9 = (bf16[80,2944]{1,0:T(8,128)(2,1)S(1)}, bf16[80,2944]{1,0:T(8,128)(2,1)S(1)}, u32[]{:S(2)}, u32[]{:S(2)}) collective-permute-start(bf16[80,2944]{1,0:T(8,128)(2,1)S(1)} %collective-permute-done.5.refs_2_), channel_id=1, source_target_pairs={{4,0},{8,4},{12,8},{14,12},{10,14},{6,10},{2,6},{0,2},{5,1},{9,5},... | collective-permute-start | bytes 1413128 | tf_op jit(solution)/shard_map/ppermute | solution.py:367
  22.7 17.3 %collective-permute-start.10 = (bf16[80,2944]{1,0:T(8,128)(2,1)S(1)}, bf16[80,2944]{1,0:T(8,128)(2,1)S(1)}, u32[]{:S(2)}, u32[]{:S(2)}) collective-permute-start(bf16[80,2944]{1,0:T(8,128)(2,1)S(1)} %get-tuple-element.75), channel_id=1, source_target_pairs={{0,16},{16,0},{1,17},{17,1},{2,18},{18,2},{3,19},{19,3},{4,20},{20... | collective-permute-start | bytes 1413128 | tf_op jit(solution)/shard_map/ppermute | solution.py:339
  24.4 26.8 %collective-permute-start.13 = (bf16[80,2944]{1,0:T(8,128)(2,1)S(1)}, bf16[80,2944]{1,0:T(8,128)(2,1)S(1)}, u32[]{:S(2)}, u32[]{:S(2)}) collective-permute-start(bf16[80,2944]{1,0:T(8,128)(2,1)S(1)} %get-tuple-element.83), channel_id=1, source_target_pairs={{0,16},{16,0},{1,17},{17,1},{2,18},{18,2},{3,19},{19,3},{4,20},{20... | collective-permute-start | bytes 1413128 | tf_op jit(solution)/shard_map/ppermute | solution.py:339
  34.0 17.2 %collective-permute-start.11 = (bf16[80,2944]{1,0:T(8,128)(2,1)S(1)}, bf16[80,2944]{1,0:T(8,128)(2,1)S(1)}, u32[]{:S(2)}, u32[]{:S(2)}) collective-permute-start(bf16[80,2944]{1,0:T(8,128)(2,1)S(1)} %collective-permute-done.8.refs_3_), channel_id=1, source_target_pairs={{0,4},{4,8},{8,12},{12,14},{14,10},{10,6},{6,2},{2,0},{1,5},{5,9},... | collective-permute-start | bytes 1413128 | tf_op jit(solution)/shard_map/ppermute | solution.py:364
  35.6 15.6 %collective-permute-start.12 = (bf16[80,2944]{1,0:T(8,128)(2,1)S(1)}, bf16[80,2944]{1,0:T(8,128)(2,1)S(1)}, u32[]{:S(2)}, u32[]{:S(2)}) collective-permute-start(bf16[80,2944]{1,0:T(8,128)(2,1)S(1)} %collective-permute-done.9.refs_4_), channel_id=1, source_target_pairs={{4,0},{8,4},{12,8},{14,12},{10,14},{6,10},{2,6},{0,2},{5,1},{9,5},... | collective-permute-start | bytes 1413128 | tf_op jit(solution)/shard_map/ppermute | solution.py:367
  40.1 9.5 %collective-permute-start.18 = (bf16[40,2944]{1,0:T(8,128)(2,1)S(1)}, bf16[40,2944]{1,0:T(8,128)(2,1)S(1)}, u32[]{:S(2)}, u32[]{:S(2)}) collective-permute-start(bf16[40,2944]{1,0:T(8,128)(2,1)S(1)} %get-tuple-element.118), channel_id=1, source_target_pairs={{0,4},{4,8},{8,12},{12,14},{14,10},{10,6},{6,2},{2,0},{1,5},{5,9},... | collective-permute-start | bytes 706568 | tf_op jit(solution)/shard_map/ppermute | solution.py:364
  41.8 9.4 %collective-permute-start.19 = (bf16[40,2944]{1,0:T(8,128)(2,1)S(1)}, bf16[40,2944]{1,0:T(8,128)(2,1)S(1)}, u32[]{:S(2)}, u32[]{:S(2)}) collective-permute-start(bf16[40,2944]{1,0:T(8,128)(2,1)S(1)} %get-tuple-element.117), channel_id=1, source_target_pairs={{4,0},{8,4},{12,8},{14,12},{10,14},{6,10},{2,6},{0,2},{5,1},{9,5},... | collective-permute-start | bytes 706568 | tf_op jit(solution)/shard_map/ppermute | solution.py:367
  49.7 14.6 %collective-permute-start.17 = (bf16[80,2944]{1,0:T(8,128)(2,1)S(1)}, bf16[80,2944]{1,0:T(8,128)(2,1)S(1)}, u32[]{:S(2)}, u32[]{:S(2)}) collective-permute-start(bf16[80,2944]{1,0:T(8,128)(2,1)S(1)} %get-tuple-element.88), channel_id=1, source_target_pairs={{0,16},{16,0},{1,17},{17,1},{2,18},{18,2},{3,19},{19,3},{4,20},{20... | collective-permute-start | bytes 1413128 | tf_op jit(solution)/shard_map/ppermute | solution.py:339
  51.2 7.0 %collective-permute-start.14 = (bf16[40,2944]{1,0:T(8,128)(2,1)S(1)}, bf16[40,2944]{1,0:T(8,128)(2,1)S(1)}, u32[]{:S(2)}, u32[]{:S(2)}) collective-permute-start(bf16[40,2944]{1,0:T(8,128)(2,1)S(1)} %slice.76), channel_id=1, source_target_pairs={{0,4},{4,8},{8,12},{12,14},{14,10},{10,6},{6,2},{2,0},{1,5},{5,9},... | collective-permute-start | bytes 706568 | tf_op jit(solution)/shard_map/ppermute | solution.py:364
  52.9 6.7 %collective-permute-start.15 = (bf16[40,2944]{1,0:T(8,128)(2,1)S(1)}, bf16[40,2944]{1,0:T(8,128)(2,1)S(1)}, u32[]{:S(2)}, u32[]{:S(2)}) collective-permute-start(bf16[40,2944]{1,0:T(8,128)(2,1)S(1)} %slice.77), channel_id=1, source_target_pairs={{4,0},{8,4},{12,8},{14,12},{10,14},{6,10},{2,6},{0,2},{5,1},{9,5},... | collective-permute-start | bytes 706568 | tf_op jit(solution)/shard_map/ppermute | solution.py:367
  53.6 10.7 %collective-permute-start.20 = (bf16[40,2944]{1,0:T(8,128)(2,1)S(1)}, bf16[40,2944]{1,0:T(8,128)(2,1)S(1)}, u32[]{:S(2)}, u32[]{:S(2)}) collective-permute-start(bf16[40,2944]{1,0:T(8,128)(2,1)S(1)} %get-tuple-element.116), channel_id=1, source_target_pairs={{0,4},{4,8},{8,12},{12,14},{14,10},{10,6},{6,2},{2,0},{1,5},{5,9},... | collective-permute-start | bytes 706568 | tf_op jit(solution)/shard_map/ppermute | solution.py:364
  55.2 9.1 %collective-permute-start.21 = (bf16[40,2944]{1,0:T(8,128)(2,1)S(1)}, bf16[40,2944]{1,0:T(8,128)(2,1)S(1)}, u32[]{:S(2)}, u32[]{:S(2)}) collective-permute-start(bf16[40,2944]{1,0:T(8,128)(2,1)S(1)} %get-tuple-element.115), channel_id=1, source_target_pairs={{4,0},{8,4},{12,8},{14,12},{10,14},{6,10},{2,6},{0,2},{5,1},{9,5},... | collective-permute-start | bytes 706568 | tf_op jit(solution)/shard_map/ppermute | solution.py:367
  58.2 12.8 %collective-permute-start.2 = (bf16[80,2944]{1,0:T(8,128)(2,1)S(1)}, bf16[80,2944]{1,0:T(8,128)(2,1)S(1)}, u32[]{:S(2)}, u32[]{:S(2)}) collective-permute-start(bf16[80,2944]{1,0:T(8,128)(2,1)S(1)} %get-tuple-element.63), channel_id=1, source_target_pairs={{0,16},{16,0},{1,17},{17,1},{2,18},{18,2},{3,19},{19,3},{4,20},{20... | collective-permute-start | bytes 1413128 | tf_op jit(solution)/shard_map/ppermute | solution.py:339
  61.0 3.3 %copy-start.2 = (f32[1,640]{1,0:T(1,128)S(1)}, f32[1,640]{1,0:T(1,128)}, u32[]{:S(2)}) copy-start(f32[1,640]{1,0:T(1,128)} %bias.1) | copy-start | bytes 7684
  64.3 2.9 %collective-permute-start.22 = (f32[3,640]{1,0:T(4,128)S(1)}, f32[3,640]{1,0:T(4,128)S(1)}, u32[]{:S(2)}, u32[]{:S(2)}) collective-permute-start(f32[3,640]{1,0:T(4,128)S(1)} %fusion.2), channel_id=1, source_target_pairs={{0,1},{1,0},{2,3},{3,2},{4,5},{5,4},{6,7},{7,6},{8,9},{9,8},{10,11... | collective-permute-start | bytes 23048 | tf_op jit(solution)/shard_map/ppermute | solution.py:339
  64.4 9.6 %collective-permute-start.16 = (bf16[512,256]{1,0:T(8,128)(2,1)S(1)}, bf16[512,256]{1,0:T(8,128)(2,1)S(1)}, u32[]{:S(2)}, u32[]{:S(2)}) collective-permute-start(bf16[512,256]{1,0:T(8,128)(2,1)S(1)} %shard_map.124), channel_id=1, source_target_pairs={{0,1},{1,0},{2,3},{3,2},{4,5},{5,4},{6,7},{7,6},{8,9},{9,8},{10,11... | collective-permute-start | bytes 786440 | tf_op jit(solution)/shard_map/ppermute | solution.py:339
  65.1 7.8 %collective-permute-start.24 = (bf16[40,2944]{1,0:T(8,128)(2,1)S(1)}, bf16[40,2944]{1,0:T(8,128)(2,1)S(1)}, u32[]{:S(2)}, u32[]{:S(2)}) collective-permute-start(bf16[40,2944]{1,0:T(8,128)(2,1)S(1)} %get-tuple-element.114), channel_id=1, source_target_pairs={{0,4},{4,8},{8,12},{12,14},{14,10},{10,6},{6,2},{2,0},{1,5},{5,9},... | collective-permute-start | bytes 706568 | tf_op jit(solution)/shard_map/ppermute | solution.py:364
  66.5 7.4 %collective-permute-start.25 = (bf16[40,2944]{1,0:T(8,128)(2,1)S(1)}, bf16[40,2944]{1,0:T(8,128)(2,1)S(1)}, u32[]{:S(2)}, u32[]{:S(2)}) collective-permute-start(bf16[40,2944]{1,0:T(8,128)(2,1)S(1)} %get-tuple-element.113), channel_id=1, source_target_pairs={{4,0},{8,4},{12,8},{14,12},{10,14},{6,10},{2,6},{0,2},{5,1},{9,5},... | collective-permute-start | bytes 706568 | tf_op jit(solution)/shard_map/ppermute | solution.py:367
  67.2 3.7 %collective-permute-start.23 = (f32[3,640]{1,0:T(4,128)S(1)}, f32[3,640]{1,0:T(4,128)S(1)}, u32[]{:S(2)}, u32[]{:S(2)}) collective-permute-start(f32[3,640]{1,0:T(4,128)S(1)} %fusion.5), channel_id=1, source_target_pairs={{0,16},{16,0},{1,17},{17,1},{2,18},{18,2},{3,19},{19,3},{4,20},{20... | collective-permute-start | bytes 23048 | tf_op jit(solution)/shard_map/ppermute | solution.py:388
  70.9 5.4 %collective-permute-start.27 = (bf16[512,512]{1,0:T(8,128)(2,1)S(1)}, bf16[512,512]{1,0:T(8,128)(2,1)S(1)}, u32[]{:S(2)}, u32[]{:S(2)}) collective-permute-start(bf16[512,512]{1,0:T(8,128)(2,1)S(1)} %get-tuple-element.103), channel_id=1, source_target_pairs={{0,1},{1,0},{2,3},{3,2},{4,5},{5,4},{6,7},{7,6},{8,9},{9,8},{10,11... | collective-permute-start | bytes 1572872 | tf_op jit(solution)/shard_map/ppermute | solution.py:339
  74.1 6.6 %collective-permute-start.26 = (bf16[40,2944]{1,0:T(8,128)(2,1)S(1)}, bf16[40,2944]{1,0:T(8,128)(2,1)S(1)}, u32[]{:S(2)}, u32[]{:S(2)}) collective-permute-start(bf16[40,2944]{1,0:T(8,128)(2,1)S(1)} %add_convert_fusion.1), channel_id=1, source_target_pairs={{0,4},{4,8},{8,12},{12,14},{14,10},{10,6},{6,2},{2,0},{1,5},{5,9},... | collective-permute-start | bytes 706568 | tf_op jit(solution)/shard_map/ppermute | solution.py:364
  75.4 4.6 %collective-permute-start.28 = (f32[3,640]{1,0:T(4,128)S(1)}, f32[3,640]{1,0:T(4,128)S(1)}, u32[]{:S(2)}, u32[]{:S(2)}) collective-permute-start(f32[3,640]{1,0:T(4,128)S(1)} %add.91), channel_id=1, source_target_pairs={{0,4},{4,0},{8,12},{12,8},{1,5},{5,1},{9,13},{13,9},{2,6},{6,2},{1... | collective-permute-start | bytes 23048 | tf_op jit(solution)/shard_map/ppermute | solution.py:388
  80.0 10.7 %copy-start = (f32[1,40,5760]{2,1,0:T(8,128)S(1)}, f32[1,40,5760]{2,1,0:T(8,128)}, u32[]{:S(2)}) copy-start(f32[1,40,5760]{2,1,0:T(8,128)} %param.10) | copy-start | bytes 2764804
  80.8 6.6 %collective-permute-start.29 = (bf16[40,2944]{1,0:T(8,128)(2,1)S(1)}, bf16[40,2944]{1,0:T(8,128)(2,1)S(1)}, u32[]{:S(2)}, u32[]{:S(2)}) collective-permute-start(bf16[40,2944]{1,0:T(8,128)(2,1)S(1)} %add_convert_fusion), channel_id=1, source_target_pairs={{0,16},{16,0},{1,17},{17,1},{2,18},{18,2},{3,19},{19,3},{4,20},{20... | collective-permute-start | bytes 706568 | tf_op jit(solution)/shard_map/ppermute | solution.py:339
  81.9 4.6 %collective-permute-start.31 = (f32[3,640]{1,0:T(4,128)S(1)}, f32[3,640]{1,0:T(4,128)S(1)}, u32[]{:S(2)}, u32[]{:S(2)}) collective-permute-start(f32[3,640]{1,0:T(4,128)S(1)} %add.98), channel_id=1, source_target_pairs={{0,8},{4,12},{8,0},{12,4},{1,9},{5,13},{9,1},{13,5},{2,10},{6,14},... | collective-permute-start | bytes 23048 | tf_op jit(solution)/shard_map/ppermute | solution.py:388
  86.5 3.7 %collective-permute-start.32 = (f32[3,640]{1,0:T(4,128)S(1)}, f32[3,640]{1,0:T(4,128)S(1)}, u32[]{:S(2)}, u32[]{:S(2)}) collective-permute-start(f32[3,640]{1,0:T(4,128)S(1)} %add.102), channel_id=1, source_target_pairs={{0,2},{2,0},{1,3},{3,1},{4,6},{6,4},{5,7},{7,5},{8,10},{10,8},{9,1... | collective-permute-start | bytes 23048 | tf_op jit(solution)/shard_map/ppermute | solution.py:388
  87.5 3.2 %collective-permute-start.30 = (bf16[40,2944]{1,0:T(8,128)(2,1)S(1)}, bf16[40,2944]{1,0:T(8,128)(2,1)S(1)}, u32[]{:S(2)}, u32[]{:S(2)}) collective-permute-start(bf16[40,2944]{1,0:T(8,128)(2,1)S(1)} %get-tuple-element.123), channel_id=1, source_target_pairs={{0,1},{1,0},{2,3},{3,2},{4,5},{5,4},{6,7},{7,6},{8,9},{9,8},{10,11... | collective-permute-start | bytes 706568 | tf_op jit(solution)/shard_map/ppermute | solution.py:339
